TPU v7x, 32 devices: a whole 2x2x4 slice. The times are simulated.
32 devices in a mesh: rep: 2 (over y), tp: 16 (over z, x, core).
Axes of the slice: x: 2, y: 2, z: 4, core: 2. Of those that a mesh axis runs over, the one named last changes fastest.
Arguments:
- hidden: bfloat16 [192, 28672], P('rep', 'tp'), parts along dimension 0, may hold values from -6 to 6
- down_matrix: bfloat16 [28672, 8192], P('tp'), may hold values from -0.046875 to 0.046875
- shrink_matrices: bfloat16 [32, 28672, 64], P(('rep', 'tp')), parts along dimension 0, may hold values from -0.03125 to 0.03125
- expand_matrices: bfloat16 [32, 8192, 64], P(('rep', 'tp')), parts along dimension 0, may hold values from -0.75 to 0.75
- adapter_of_row: int32 [192], P('rep'), parts along dimension 0, may hold values from 0 to 15, as said below
- adapter_holder_slot: int32 [32], P('rep'), parts along dimension 0, may hold values from 0 to 15, each once
Outputs:
- projected: bfloat16 [192, 8192], P('rep', 'tp'), parts along dimension 0
There are 2 independent parts, one for each index of `rep`. A program takes and returns all parts, laid end to end along the dimension named above; an argument that names none is the same for every part. Nothing has to cross between parts.
Inputs may be any that keep to these rules, and one draw needn't show every extreme that they name: `adapter_of_row`: rows come in aligned blocks of 4 rows that share one adapter; adapter numbers never fall along the rows; every adapter has rows, no adapter has more than 20, and some adapter has exactly 20. `adapter_holder_slot`: each device of tp holds exactly one adapter.
All inputs are finite; a program needn't handle non-finite values.
Results may differ from a plain program's by a relative error of at most 0.0027.
Values may be sent and summed in bfloat16 or wider, within the bound.
No kernel may reach another device: no remote copies, remote signals or barrier semaphores. Data moves between devices by JAX's collectives and lax.ppermute only.
A program may use at most 128 MiB of HBM per device.

v0:
```python
import jax
import jax.numpy as jnp
from jax import lax
from jax.sharding import PartitionSpec as P

ADAPTER_SCALE = 0.5


def sum_partials(partial_value):
    return lax.psum_scatter(partial_value, "tp", scatter_dimension=1, tiled=True)


def shards(
    hidden, down_matrix, shrink_matrices, expand_matrices, adapter_of_row, adapter_holder_slot
):
    total_rows = hidden.shape[0]
    partial_value = jnp.dot(hidden, down_matrix, preferred_element_type=jnp.float32)
    adapter_count = adapter_holder_slot.shape[0]
    adapter_ids = jnp.arange(adapter_count, dtype=jnp.int32)
    shrink_result, expand_result = (
        lax.all_to_all(shrink_matrices, "tp", split_axis=1, concat_axis=0, tiled=True),
        lax.all_to_all(expand_matrices, "tp", split_axis=1, concat_axis=0, tiled=True),
    )
    base_partial_sum = sum_partials(partial_value)
    row_match = adapter_of_row[:, None] == adapter_ids[None, :]
    row_slot = jnp.sum(jnp.where(row_match, adapter_holder_slot[None, :], 0), axis=1)
    slot_mask = row_slot[:, None] == adapter_ids[None, :]
    rank_every = jnp.einsum(
        "rf,afk->rak", hidden, shrink_result, preferred_element_type=jnp.float32
    )
    rank_terms = jnp.sum(jnp.where(slot_mask[:, :, None], rank_every, 0.0), axis=1)
    rank_rows = lax.psum(rank_terms, "tp").astype(jnp.bfloat16)
    spread_rows = jnp.where(
        slot_mask[:, :, None], rank_rows[:, None, :], jnp.zeros((), jnp.bfloat16)
    )
    spread_rows = spread_rows.reshape(total_rows, -1)
    expand_table = jnp.transpose(expand_result, (0, 2, 1)).reshape(-1, expand_result.shape[1])
    adapter_result = jnp.dot(spread_rows, expand_table, preferred_element_type=jnp.float32)
    reduced_output = base_partial_sum + ADAPTER_SCALE * adapter_result
    return reduced_output.astype(jnp.bfloat16)


def solution(mesh):
    in_specs = (
        P("rep", "tp"),
        P("tp", None),
        P(("rep", "tp"), None, None),
        P(("rep", "tp"), None, None),
        P("rep"),
        P("rep"),
    )
    out_specs = P("rep", "tp")
    return jax.shard_map(shards, mesh=mesh, in_specs=in_specs, out_specs=out_specs, check_vma=False)
```

profile of v0, /device:TPU:0, one launch (start us, length us, event | category | flops | bytes accessed | tf_op | source)
XLA Modules:
  0.0 481.4 jit_solution(9588605567448455301)
XLA Ops:
  6.5 0.0 copy-start
  6.5 9.2 %copy.21 = bf16[1,8192,64]{2,0,1:T(2,128)(2,1)} copy(bf16[1,8192,64]{1,2,0:T(8,128)(2,1)} %param.9) | data formatting | bytes 2097152 | tf_op args[3]
  15.8 0.5 broadcast.17
  16.3 45.2 %reduce = bf16[8192,64]{1,0:T(8,128)(2,1)S(1)} reduce(bf16[8192,1,64]{2,1,0:T(2,128)(2,1)} %bitcast.28, bf16[]{:T(256)} %broadcast.17), dimensions={1}, to_apply=%bitcast.17.reduce_sub_computation | reduce | bytes 2097154
  61.5 2.3 reshape.37
  63.8 7.4 %all-to-all-start.1 = ((bf16[16,2,16384]{2,1,0:T(2,128)(2,1)}), bf16[16,2,16384]{2,1,0:T(2,128)(2,1)S(1)}, u32[]{:S(2)}, u32[]{:S(2)}) async-start(bf16[16,2,16384]{2,1,0:T(2,128)(2,1)} %reshape.37), calls=%async_computation.2 | async-start | bytes 2097152 | tf_op jit(solution)/shard_map/all_to_all | solution.py:22
  71.1 29.0 %copy.18 = bf16[1,28672,64]{2,0,1:T(2,128)(2,1)} copy(bf16[1,28672,64]{1,2,0:T(8,128)(2,1)} %param.8) | data formatting | bytes 7340032 | tf_op args[2]
  100.1 157.1 %reduce.1 = bf16[28672,64]{1,0:T(8,128)(2,1)} reduce(bf16[28672,1,64]{2,1,0:T(2,128)(2,1)} %bitcast.25, bf16[]{:T(256)} %broadcast.17), dimensions={1}, to_apply=%bitcast.19.reduce_sub_computation | reduce | bytes 7340034
  257.2 13.3 %reshape.39 = bf16[16,2,57344]{2,1,0:T(2,128)(2,1)} reshape(bf16[28672,64]{1,0:T(8,128)(2,1)} %reduce.1) | data formatting | bytes 7340032
  270.4 0.0 all-to-all-done.1
  270.5 6.0 %all-to-all-start = ((bf16[16,2,57344]{2,1,0:T(2,128)(2,1)}), bf16[16,2,57344]{2,1,0:T(2,128)(2,1)}, u32[]{:S(2)}, u32[]{:S(2)}) async-start(bf16[16,2,57344]{2,1,0:T(2,128)(2,1)} %reshape.39), calls=%async_computation.1 | async-start | bytes 7340032 | tf_op jit(solution)/shard_map/all_to_all | solution.py:21
  276.5 0.0 copy-start.1
  276.5 0.0 copy-start.2
  276.5 0.3 reduce-scatter.2.cloned.1.call-start
  276.8 0.0 copy-done
  276.8 15.7 %fusion.9 = f32[96,8192]{1,0:T(8,128)} fusion(bf16[96,1792]{1,0:T(8,128)(2,1)S(1)} %copy-done, bf16[1792,8192]{1,0:T(8,128)(2,1)} %param.7), kind=kOutput, calls=%fused_computation.14 | convolution fusion | flops 2818572288 | bytes 32849920 | tf_op jit(solution)/shard_map/dot_general | solution.py:17
  292.6 0.0 reduce-scatter.2.cloned.1.call-update
  292.6 0.0 copy-done.1
  292.6 0.0 copy-done.2
  292.6 0.1 select_reduce_fusion.1
  292.7 7.0 %reshape.38 = bf16[8192,1,64]{2,1,0:T(2,128)(2,1)} reshape(bf16[16,2,16384]{2,1,0:T(2,128)(2,1)S(1)} %all-to-all-done.1) | data formatting | bytes 2097152
  299.7 2.6 copy.29
  302.3 0.8 copy.23
  303.2 54.5 %all-to-all-done = bf16[16,2,57344]{2,1,0:T(2,128)(2,1)} async-done(((bf16[16,2,57344]{2,1,0:T(2,128)(2,1)}), bf16[16,2,57344]{2,1,0:T(2,128)(2,1)}, u32[]{:S(2)}, u32[]{:S(2)}) %all-to-all-start) | async-done | bytes 3670048 | tf_op jit(solution)/shard_map/all_to_all | solution.py:21
  357.7 14.2 %reshape.40 = bf16[28672,1,64]{2,1,0:T(2,128)(2,1)} reshape(bf16[16,2,57344]{2,1,0:T(2,128)(2,1)} %all-to-all-done) | data formatting | bytes 7340032
  371.9 9.7 %copy.28 = bf16[1,28672,64]{2,1,0:T(8,128)(2,1)} copy(bf16[1,28672,64]{2,0,1:T(2,128)(2,1)} %bitcast.26) | data formatting | bytes 7340032
  381.6 8.0 %copy.20 = bf16[16,1792,64]{1,2,0:T(8,128)(2,1)} copy(bf16[16,1792,64]{2,1,0:T(8,128)(2,1)} %bitcast.27) | data formatting | bytes 7340032 | tf_op jit(solution)/shard_map/all_to_all | solution.py:21
  389.6 3.1 fusion.10
  392.7 0.1 select_reduce_fusion
  392.8 79.9 %psum.7 = bf16[96,64]{0,1:T(8,128)(2,1)S(1)} all-reduce(f32[96,64]{0,1:T(8,128)S(1)} %select_reduce_fusion), channel_id=1, replica_groups=mesh['rep'=2,'tp'=16] {'tp'}, use_global_device_ids=true, to_apply=%region_3.4 | all-reduce | flops 6144 | bytes 36864 | tf_op jit(solution)/shard_map/psum | solution.py:32
  472.7 0.0 reduce-scatter.2.cloned.1.call-done
  472.7 1.9 fusion.2
  (1 shorter events, 0.0 us)
Async XLA Ops:
  6.5 270.3 %copy-start = (bf16[96,1792]{1,0:T(8,128)(2,1)S(1)}, bf16[96,1792]{1,0:T(8,128)(2,1)}, u32[]{:S(2)}) copy-start(bf16[96,1792]{1,0:T(8,128)(2,1)} %param.6) | copy-start | bytes 1032196
  63.8 206.7 %all-to-all-start.1 = ((bf16[16,2,16384]{2,1,0:T(2,128)(2,1)}), bf16[16,2,16384]{2,1,0:T(2,128)(2,1)S(1)}, u32[]{:S(2)}, u32[]{:S(2)}) async-start(bf16[16,2,16384]{2,1,0:T(2,128)(2,1)} %reshape.37), calls=%async_computation.2 | async-start | bytes 2097152 | tf_op jit(solution)/shard_map/all_to_all | solution.py:22
  270.5 87.2 %all-to-all-start = ((bf16[16,2,57344]{2,1,0:T(2,128)(2,1)}), bf16[16,2,57344]{2,1,0:T(2,128)(2,1)}, u32[]{:S(2)}, u32[]{:S(2)}) async-start(bf16[16,2,57344]{2,1,0:T(2,128)(2,1)} %reshape.39), calls=%async_computation.1 | async-start | bytes 7340032 | tf_op jit(solution)/shard_map/all_to_all | solution.py:21
  276.5 16.1 %copy-start.1 = (s32[16]{0:T(128)S(1)}, s32[16]{0:T(128)}, u32[]{:S(2)}) copy-start(s32[16]{0:T(128)} %param.11) | copy-start | bytes 196
  276.5 16.1 %copy-start.2 = (s32[96]{0:T(128)S(1)}, s32[96]{0:T(128)}, u32[]{:S(2)}) copy-start(s32[96]{0:T(128)} %param.10) | copy-start | bytes 1156
  276.5 196.1 %reduce-scatter.2.cloned.1.call-start = ((), (), s32[]{:S(2)}) async-start(), calls=%async_computation.3 | async-start | bytes 3342336 | tf_op jit(solution)/shard_map/reduce_scatter | solution.py:10
Sparse Core Ops, SparseCore 0:
  292.7 85.7 reduce-scatter.1
where the time goes:
time: 485 us; the launch traced here: 481 us
  other arithmetic  202 us (42%)
  local copies, waits for them, and re-layouts  96.6 us (20%)
  blocking collectives  79.9 us (16%)
  waiting for transfers between devices  54.5 us (11%)
  matrix products  20.8 us (4%)
  starting transfers between devices  13.7 us (3%)
  between operations  13.5 us (3%)
    unnamed x2, other arithmetic  202 us
    unnamed x15, local copies, waits for them, and re-layouts  87.8 us
    psum x1, blocking collectives, shards(): rank_rows = lax.psum(rank_terms, 'tp').astype(jnp.bfloat16)  79.9 us
    all_to_all x1, waiting for transfers between devices, shards(): lax.all_to_all(shrink_matrices, 'tp', split_axis=1, concat_axis=0, tiled=...  54.5 us
    dot_general x1, matrix products, shards(): jnp.dot(hidden, down_matrix, preferred_element_type=jnp.float32)  15.7 us
  transfers between devices with their start and end apart: 3, of which 1 were waited for; matrix products, arithmetic and copies ran while one was open for 54% of the time, Pallas kernels for 0%

commit v1 on v0

v1 whole, which is shorter than its diff:
```python
import functools

import jax
import jax.numpy as jnp
from jax import lax
from jax.experimental import pallas as pl
from jax.experimental.pallas import tpu as pltpu
from jax.sharding import PartitionSpec as P

ADAPTER_SCALE = 0.5
BLOCK = 4
MOST = 20
LANES = 128
F16_TOP = 14.0


def xor_permute(value, group, offset):
    return lax.ppermute(value, "tp", [(i, i ^ offset) for i in range(group)])


def column_blocks_kernel(order_ref, hidden_ref, down_ref, out_ref):
    product = jnp.dot(hidden_ref[...], down_ref[...], preferred_element_type=jnp.float32)
    for lane in range(out_ref.shape[0]):
        out_ref[lane] = product[:, lane * LANES : (lane + 1) * LANES]


def column_blocks(hidden, down_matrix, order, width):
    rows, depth = hidden.shape
    count = order.shape[0]
    parts = width // LANES
    return pl.pallas_call(
        column_blocks_kernel,
        out_shape=jax.ShapeDtypeStruct((count * parts, rows, LANES), jnp.float32),
        grid_spec=pltpu.PrefetchScalarGridSpec(
            num_scalar_prefetch=1,
            grid=(count,),
            in_specs=[
                pl.BlockSpec((rows, depth), lambda j, order_ref: (0, 0)),
                pl.BlockSpec((depth, width), lambda j, order_ref: (0, order_ref[j])),
            ],
            out_specs=pl.BlockSpec((parts, rows, LANES), lambda j, order_ref: (j, 0, 0)),
        ),
        compiler_params=pltpu.CompilerParams(vmem_limit_bytes=40 * 2**20),
        cost_estimate=pl.CostEstimate(
            flops=2 * rows * depth * width * count,
            bytes_accessed=2 * depth * width * count + 4 * rows * width * count,
            transcendentals=0,
        ),
    )(order, hidden, down_matrix)


def pack_scaled(value):
    peak = jnp.max(jnp.abs(value), axis=(0, 2), keepdims=True)
    exponent = jnp.ceil(jnp.log2(jnp.maximum(peak, 2.0**-100)))
    scaled = (value * jnp.exp2(F16_TOP - exponent)).astype(jnp.float16)
    marks = jnp.broadcast_to(exponent, (1,) + value.shape[1:]).astype(jnp.float16)
    return jnp.concatenate([scaled, marks], axis=0)


def unpack_scaled(packed):
    exponent = packed[-1:].astype(jnp.float32)
    return packed[:-1].astype(jnp.float32) * jnp.exp2(exponent - F16_TOP)


def base_blocks(hidden, down_matrix, group, me, width):
    rows = hidden.shape[0]
    parts = width // LANES
    quads = list(range(0, group, 4))
    odd_order = [q + 1 for q in quads] + [q + 3 for q in quads]
    even_order = quads + [q + 2 for q in quads]
    odd = column_blocks(hidden, down_matrix, me ^ jnp.array(odd_order, jnp.int32), width)
    odd_in = xor_permute(odd, group, 1)
    even = column_blocks(hidden, down_matrix, me ^ jnp.array(even_order, jnp.int32), width)
    chip = even + odd_in
    half = len(quads) * parts
    pair_in = xor_permute(pack_scaled(chip[half:]), group, 2)
    pair = chip[:half] + unpack_scaled(pair_in)
    total = pair[:parts]
    arrived = [
        xor_permute(pack_scaled(pair[i * parts : (i + 1) * parts]), group, quads[i])
        for i in range(1, len(quads))
    ]
    for packed in arrived:
        total = total + unpack_scaled(packed)
    return jnp.transpose(total, (1, 0, 2)).reshape(rows, width)


def shards(
    hidden, down_matrix, shrink_matrices, expand_matrices, adapter_of_row, adapter_holder_slot
):
    group = lax.axis_size("tp")
    me = lax.axis_index("tp")
    rows, depth = hidden.shape
    model_width = down_matrix.shape[1]
    width = model_width // group
    rank = shrink_matrices.shape[2]
    blocks = MOST // BLOCK
    adapter_ids = jnp.arange(group, dtype=jnp.int32)

    row_match = adapter_of_row[:, None] == adapter_ids[None, :]
    row_slot = jnp.sum(jnp.where(row_match, adapter_holder_slot[None, :], 0), axis=1)
    slot_mask = row_slot[None, :] == adapter_ids[:, None]
    before = jnp.cumsum(slot_mask.astype(jnp.int32), axis=1) - 1
    place = jnp.where(slot_mask, before, -1)
    pick = place[:, None, :] == jnp.arange(MOST, dtype=jnp.int32)[None, :, None]
    pick = pick.reshape(group * MOST, rows)
    pick16 = pick.astype(jnp.bfloat16)

    packed = jnp.dot(pick16, hidden, preferred_element_type=jnp.float32).astype(jnp.bfloat16)
    packed = packed.reshape(group * blocks, BLOCK, depth)
    gathered = lax.all_to_all(packed, "tp", split_axis=0, concat_axis=0, tiled=True)

    if width % LANES == 0 and depth % LANES == 0:
        base = base_blocks(hidden, down_matrix, group, me, width)
    else:
        partial_value = jnp.dot(hidden, down_matrix, preferred_element_type=jnp.float32)
        base = lax.psum_scatter(partial_value, "tp", scatter_dimension=1, tiled=True)

    gathered = gathered.reshape(group, MOST, depth)
    shrink_parts = shrink_matrices.reshape(group, depth, rank)
    rank_rows = lax.dot_general(
        jnp.transpose(gathered, (1, 0, 2)).reshape(MOST, group * depth),
        shrink_matrices[0],
        (((1,), (0,)), ((), ())),
        preferred_element_type=jnp.float32,
    ).astype(jnp.bfloat16)
    adapter_out = lax.dot_general(
        rank_rows, expand_matrices[0], (((1,), (1,)), ((), ())), preferred_element_type=jnp.float32
    ).astype(jnp.bfloat16)
    adapter_out = jnp.transpose(adapter_out.reshape(blocks, BLOCK, group, width), (2, 0, 1, 3))
    adapter_in = lax.all_to_all(
        adapter_out.reshape(group * blocks, BLOCK, width), "tp", split_axis=0, concat_axis=0, tiled=True
    )
    adapter_rows = lax.dot_general(
        pick16,
        adapter_in.reshape(group * MOST, width),
        (((0,), (0,)), ((), ())),
        preferred_element_type=jnp.float32,
    )
    return (base + ADAPTER_SCALE * adapter_rows).astype(jnp.bfloat16)


def solution(mesh):
    in_specs = (
        P("rep", "tp"),
        P("tp", None),
        P(("rep", "tp"), None, None),
        P(("rep", "tp"), None, None),
        P("rep"),
        P("rep"),
    )
    out_specs = P("rep", "tp")
    return jax.shard_map(shards, mesh=mesh, in_specs=in_specs, out_specs=out_specs, check_vma=False)
```

time: 485 us -> 88.9 us (0.18)
  other arithmetic: 202 us -> 8.9 us
  local copies, waits for them, and re-layouts: 96.6 us -> 9.77 us
  blocking collectives: 79.9 us -> 0 us
  waiting for transfers between devices: 54.5 us -> 23.5 us
  Pallas kernels: 0 us -> 18.5 us
  between operations: 13.5 us -> 0.27 us
  matrix products: 20.8 us -> 7.77 us
  starting transfers between devices: 13.7 us -> 19.2 us
    unnamed x2 -> x0, other arithmetic: 202 us -> none
    unnamed x15 -> x16, local copies, waits for them, and re-layouts: 87.8 us -> 2.63 us
    psum x1 -> x0, blocking collectives: 79.9 us -> none  [shards(): rank_rows = lax.psum(rank_terms, 'tp').astype(jnp.bfloat16)]
    all_to_all x2, waiting for transfers between devices: 54.5 us -> 9.53 us  [the longest x1 9.52 us: shards(): lax.all_to_all(adapter_out.reshape(group * blocks, BLOCK, width), 'tp', s...]
    pallas_call x0 -> x2, Pallas kernels: none -> 18.5 us  [column_blocks(): pl.pallas_call(column_blocks_kernel, out_shape=jax.ShapeDtypeStruct((coun...]
    ppermute x0 -> x5, waiting for transfers between devices: none -> 14 us  [xor_permute(): return lax.ppermute(value, 'tp', [(i, i ^ offset) for i in range(group)])]
    dot_general x2 -> x3, matrix products: 17.6 us -> 7.77 us  [the longest x1 4.39 us: shards(): lax.dot_general(rank_rows, expand_matrices[0], (((1,), (1,)), ((), ())),...]
    all_to_all x2 -> x0, local copies, waits for them, and re-layouts: 8.81 us -> none  [the longest x1 7.98 us: shards(): lax.all_to_all(shrink_matrices, 'tp', split_axis=1, concat_axis=0, tiled=...]
  transfers between devices with their start and end apart: 3 -> 7, of which waited for: 1 -> 2; matrix products, arithmetic and copies ran while one was open for 54% -> 26% of each run, Pallas kernels for 0% -> 11%
where the time goes in v1:
time: 88.9 us; the launch traced here: 87.9 us
  waiting for transfers between devices  23.5 us (26%)
  starting transfers between devices  19.2 us (22%)
  Pallas kernels  18.5 us (21%)
  local copies, waits for them, and re-layouts  9.77 us (11%)
  other arithmetic  8.9 us (10%)
  matrix products  7.77 us (9%)
    pallas_call x2, Pallas kernels, column_blocks(): pl.pallas_call(column_blocks_kernel, out_shape=jax.ShapeDtypeStruct((coun...  18.5 us
    ppermute x5, waiting for transfers between devices, xor_permute(): return lax.ppermute(value, 'tp', [(i, i ^ offset) for i in range(group)])  14 us
    all_to_all x1, waiting for transfers between devices, shards(): lax.all_to_all(adapter_out.reshape(group * blocks, BLOCK, width), 'tp', s...  9.52 us
    ppermute x5, starting transfers between devices, xor_permute(): return lax.ppermute(value, 'tp', [(i, i ^ offset) for i in range(group)])  7.83 us
    all_to_all x1, starting transfers between devices, shards(): lax.all_to_all(packed, 'tp', split_axis=0, concat_axis=0, tiled=True)  7.19 us
    dot_general x1, matrix products, shards(): lax.dot_general(rank_rows, expand_matrices[0], (((1,), (1,)), ((), ())),...  4.39 us
    all_to_all x1, starting transfers between devices, shards(): lax.all_to_all(adapter_out.reshape(group * blocks, BLOCK, width), 'tp', s...  4.22 us
    reshape x1, local copies, waits for them, and re-layouts, shards(): packed = packed.reshape(group * blocks, BLOCK, depth)  3.04 us
  transfers between devices with their start and end apart: 7, of which 2 were waited for; matrix products, arithmetic and copies ran while one was open for 26% of the time, Pallas kernels for 11%

profile of v1, /device:TPU:0, one launch (start us, length us, event | category | flops | bytes accessed | tf_op | source)
XLA Modules:
  0.0 87.9 jit_solution(9759836400378593235)
XLA Ops:
  0.0 0.0 copy-start
  0.0 0.7 broadcast_xor_fusion.order_ref
  0.8 0.0 copy-start.1
  0.8 1.0 %copy-done.1 = bf16[96,1792]{1,0:T(8,128)(2,1)S(1)} copy-done((bf16[96,1792]{1,0:T(8,128)(2,1)S(1)}, bf16[96,1792]{1,0:T(8,128)(2,1)}, u32[]{:S(2)}) %copy-start.1) | copy-done | bytes 344088
  1.7 0.0 copy-start.3
  1.7 0.0 copy-start.4
  1.7 0.0 copy-start.2
  1.7 9.2 %shard_map.83 = f32[32,96,128]{2,1,0:T(8,128)S(1)} custom-call(s32[8]{0:T(128)S(1)} %broadcast_xor_fusion.order_ref, bf16[96,1792]{1,0:T(8,128)(2,1)S(1)} %copy-done.1, bf16[1792,8192]{1,0:T(8,128)(2,1)} %down_ref.3), custom_call_target="tpu_custom_call" | custom-call | flops 1409286144 | bytes 16252928 | tf_op jit(solution)/shard_map/pallas_call | solution.py:31
  11.0 0.5 collective-permute-start
  11.5 0.0 copy-done.3
  11.5 0.0 copy-done.4
  11.5 0.1 select_reduce_fusion
  11.6 0.3 reduce_window_sum.11
  11.9 0.1 eq.79
  12.0 0.0 copy-done.2
  12.0 1.5 %convolution_convert_fusion.1 = bf16[320,1792]{1,0:T(8,128)(2,1)} fusion(bf16[96,1792]{1,0:T(8,128)(2,1)S(1)} %copy-done.2, s32[320,96]{1,0:T(8,128)S(1)} %eq.77, s32[320]{0:T(512)S(1)} %eq.79), kind=kOutput, calls=%fused_computation.3 | convolution fusion | flops 110704640 | bytes 1615104 | tf_op jit(solution)/shard_map/dot_general | solution.py:109
  13.6 3.0 %reshape.195 = bf16[80,4,1792]{2,1,0:T(4,128)(2,1)} reshape(bf16[320,1792]{1,0:T(8,128)(2,1)} %convolution_convert_fusion.1) | data formatting | bytes 2293760 | tf_op jit(solution)/shard_map/reshape | solution.py:110
  16.6 0.0 copy-start.5
  16.6 7.2 %all-to-all-start = ((bf16[80,4,1792]{2,1,0:T(4,128)(2,1)}), bf16[80,4,1792]{2,1,0:T(4,128)(2,1)}, u32[]{:S(2)}, u32[]{:S(2)}) async-start(bf16[80,4,1792]{2,1,0:T(4,128)(2,1)} %reshape.195), calls=%async_computation | async-start | bytes 2293760 | tf_op jit(solution)/shard_map/all_to_all | solution.py:111
  23.8 0.0 copy-done.5
  23.8 9.3 %shard_map.82 = f32[32,96,128]{2,1,0:T(8,128)S(1)} custom-call(s32[8]{0:T(128)S(1)} %broadcast_xor_fusion.1.order_ref, bf16[96,1792]{1,0:T(8,128)(2,1)S(1)} %copy-done.2, bf16[1792,8192]{1,0:T(8,128)(2,1)} %down_ref.3), custom_call_target="tpu_custom_call" | custom-call | flops 1409286144 | bytes 16252928 | tf_op jit(solution)/shard_map/pallas_call | solution.py:31
  33.1 0.0 collective-permute-done
  33.1 1.6 %add.27 = f32[32,96,128]{2,1,0:T(8,128)S(1)} add(f32[32,96,128]{2,1,0:T(8,128)S(1)} %shard_map.82, f32[32,96,128]{2,1,0:T(8,128)} %collective-permute-done) | non-fusion elementwise | flops 393216 | bytes 4718592 | tf_op jit(solution)/shard_map/add | solution.py:74
  34.7 0.1 abs_reduce_fusion
  34.9 0.2 multiply_convert_fusion
  35.0 0.1 broadcast_in_dim.22
  35.1 0.1 pad_maximum_fusion
  35.2 1.9 %collective-permute-start.1 = (f16[17,96,128]{2,1,0:T(8,128)(2,1)S(1)}, f16[17,96,128]{2,1,0:T(8,128)(2,1)}, u32[]{:S(2)}, u32[]{:S(2)}) collective-permute-start(f16[17,96,128]{2,1,0:T(8,128)(2,1)S(1)} %pad_maximum_fusion), channel_id=1, source_target_pairs={{0,2},{1,3},{2,0},{3,1},{4,6},{5,7},{6,4},{7,5},{8,10},{9,11},{10,... | collective-permute-start | bytes 1253384 | tf_op jit(solution)/shard_map/ppermute | solution.py:18
  37.2 14.0 %collective-permute-done.1 = f16[17,96,128]{2,1,0:T(8,128)(2,1)} collective-permute-done((f16[17,96,128]{2,1,0:T(8,128)(2,1)S(1)}, f16[17,96,128]{2,1,0:T(8,128)(2,1)}, u32[]{:S(2)}, u32[]{:S(2)}) %collective-permute-start.1) | collective-permute-done | bytes 417824 | tf_op jit(solution)/shard_map/ppermute | solution.py:18
  51.2 0.8 exponential_bitcast_fusion.3
  52.0 1.1 %slice_add_fusion = f32[16,96,128]{2,1,0:T(8,128)S(1)} fusion(f32[32,96,128]{2,1,0:T(8,128)S(1)} %add.27, f16[17,96,128]{2,1,0:T(8,128)(2,1)} %collective-permute-done.1, f32[96,128]{1,0:T(8,128)S(1)} %exponential_bitcast_fusion.3), kind=kLoop, calls=%fused_computation.9 | loop fusion | flops 589824 | bytes 2015232 | tf_op jit(solution)/shard_map/add | solution.py:77
  53.0 0.2 abs_reduce_fusion.3
  53.2 0.1 multiply_convert_fusion.3
  53.4 0.1 broadcast_in_dim.23
  53.5 0.7 pad_maximum_fusion.1
  54.2 2.9 %collective-permute-start.2 = (f16[5,96,128]{2,1,0:T(8,128)(2,1)}, f16[5,96,128]{2,1,0:T(8,128)(2,1)S(1)}, u32[]{:S(2)}, u32[]{:S(2)}) collective-permute-start(f16[5,96,128]{2,1,0:T(8,128)(2,1)} %pad_maximum_fusion.1), channel_id=1, source_target_pairs={{0,4},{1,5},{2,6},{3,7},{4,0},{5,1},{6,2},{7,3},{8,12},{9,13},{10,... | collective-permute-start | bytes 368648 | tf_op jit(solution)/shard_map/ppermute | solution.py:18
  57.1 0.1 broadcast_in_dim.24
  57.1 0.7 pad_maximum_fusion.2
  57.8 1.0 %collective-permute-start.3 = (f16[5,96,128]{2,1,0:T(8,128)(2,1)}, f16[5,96,128]{2,1,0:T(8,128)(2,1)}, u32[]{:S(2)}, u32[]{:S(2)}) collective-permute-start(f16[5,96,128]{2,1,0:T(8,128)(2,1)} %pad_maximum_fusion.2), channel_id=1, source_target_pairs={{0,8},{1,9},{2,10},{3,11},{4,12},{5,13},{6,14},{7,15},{8,0},{9,1},... | collective-permute-start | bytes 368648 | tf_op jit(solution)/shard_map/ppermute | solution.py:18
  58.8 0.1 broadcast_in_dim.25
  58.9 0.7 pad_maximum_fusion.3
  59.6 1.5 %collective-permute-start.4 = (f16[5,96,128]{2,1,0:T(8,128)(2,1)}, f16[5,96,128]{2,1,0:T(8,128)(2,1)}, u32[]{:S(2)}, u32[]{:S(2)}) collective-permute-start(f16[5,96,128]{2,1,0:T(8,128)(2,1)} %pad_maximum_fusion.3), channel_id=1, source_target_pairs={{0,12},{1,13},{2,14},{3,15},{4,8},{5,9},{6,10},{7,11},{8,4},{9,5},... | collective-permute-start | bytes 368648 | tf_op jit(solution)/shard_map/ppermute | solution.py:18
  61.1 0.0 all-to-all-done
  61.1 2.4 %reshape.196 = bf16[16,20,1792]{2,1,0:T(8,128)(2,1)S(1)} reshape(bf16[80,4,1792]{2,1,0:T(4,128)(2,1)} %all-to-all-done) | data formatting | bytes 2293760 | tf_op jit(solution)/shard_map/reshape | solution.py:119
  63.4 0.2 copy.13
  63.6 0.1 pad.8
  63.7 0.4 copy.16
  64.2 0.0 copy-done
  64.2 4.4 %convolution_convert_fusion = bf16[20,8192]{1,0:T(8,128)(2,1)} fusion(bf16[20,28672]{1,0:T(8,128)(2,1)S(1)} %bitcast.41, bf16[1,28672,64]{1,2,0:T(8,128)(2,1)} %param.10, bf16[1,8192,64]{1,2,0:T(8,128)(2,1)S(1)} %copy-done), kind=kOutput, calls=%fused_computation | convolution fusion | flops 94536960 | bytes 6193152 | tf_op jit(solution)/shard_map/dot_general | solution.py:127
  68.6 1.1 %copy.17 = bf16[3,8,16,512]{3,2,1,0:T(8,128)(2,1)S(1)} copy(bf16[3,8,16,512]{3,1,2,0:T(8,128)(2,1)} %bitcast.42) | data formatting | bytes 786432
  69.7 1.0 %copy.14 = bf16[5,4,16,512]{3,1,0,2:T(4,128)(2,1)} copy(bf16[5,4,16,512]{3,2,1,0:T(8,128)(2,1)S(1)} %bitcast.44) | data formatting | bytes 655360 | tf_op jit(solution)/shard_map/reshape | solution.py:130
  70.7 4.2 %all-to-all-start.1 = ((bf16[80,4,512]{2,1,0:T(4,128)(2,1)}), bf16[80,4,512]{2,1,0:T(4,128)(2,1)S(1)}, u32[]{:S(2)}, u32[]{:S(2)}) async-start(bf16[80,4,512]{2,1,0:T(4,128)(2,1)} %bitcast.9), calls=%async_computation.1 | async-start | bytes 655360 | tf_op jit(solution)/shard_map/all_to_all | solution.py:131
  74.9 0.0 collective-permute-done.2
  74.9 0.0 collective-permute-done.3
  75.0 0.8 exponential_bitcast_fusion.1
  75.7 0.0 collective-permute-done.4
  75.7 0.8 exponential_bitcast_fusion
  76.5 9.5 %all-to-all-done.1 = bf16[80,4,512]{2,1,0:T(4,128)(2,1)S(1)} async-done(((bf16[80,4,512]{2,1,0:T(4,128)(2,1)}), bf16[80,4,512]{2,1,0:T(4,128)(2,1)S(1)}, u32[]{:S(2)}, u32[]{:S(2)}) %all-to-all-start.1) | async-done | bytes 327712 | tf_op jit(solution)/shard_map/all_to_all | solution.py:131
  86.0 0.1 reshape.200
  86.1 1.8 %fusion.3 = bf16[96,512]{1,0:T(8,128)(2,1)} fusion(pred[320,96]{1,0:T(32,128)(4,1)S(1)} %eq.76, bf16[320,512]{1,0:T(8,128)(2,1)S(1)} %reshape.200, f32[16,96,128]{2,1,0:T(8,128)S(1)} %slice_add_fusion, f16[5,96,128]{2,1,0:T(8,128)(2,1)} %collective-permute-done.4, f16[5,96,128]{2,1,0:T(8,128)(2,1)} %collective-permute-done.3, ...), kind=kOutput, calls=%fused_computation.6 | convolution fusion | flops 32047104 | bytes 1105920 | tf_op jit(solution)/shard_map/dot_general | solution.py:134
  (13 shorter events, 0.2 us)
Async XLA Ops:
  0.0 64.2 %copy-start = (bf16[1,8192,64]{1,2,0:T(8,128)(2,1)S(1)}, bf16[1,8192,64]{1,2,0:T(8,128)(2,1)}, u32[]{:S(2)}) copy-start(bf16[1,8192,64]{1,2,0:T(8,128)(2,1)} %param.11) | copy-start | bytes 3145732
  0.8 1.0 %copy-start.1 = (bf16[96,1792]{1,0:T(8,128)(2,1)S(1)}, bf16[96,1792]{1,0:T(8,128)(2,1)}, u32[]{:S(2)}) copy-start(bf16[96,1792]{1,0:T(8,128)(2,1)} %hidden_ref.3) | copy-start | bytes 1032196
  1.7 9.8 %copy-start.3 = (s32[16]{0:T(128)S(1)}, s32[16]{0:T(128)}, u32[]{:S(2)}) copy-start(s32[16]{0:T(128)} %param.13) | copy-start | bytes 196
  1.7 9.8 %copy-start.4 = (s32[96]{0:T(128)S(1)}, s32[96]{0:T(128)}, u32[]{:S(2)}) copy-start(s32[96]{0:T(128)} %param.12) | copy-start | bytes 1156
  1.7 10.3 %copy-start.2 = (bf16[96,1792]{1,0:T(8,128)(2,1)S(1)}, bf16[96,1792]{1,0:T(8,128)(2,1)}, u32[]{:S(2)}) copy-start(bf16[96,1792]{1,0:T(8,128)(2,1)} %hidden_ref.3) | copy-start | bytes 1032196
  11.0 22.1 %collective-permute-start = (f32[32,96,128]{2,1,0:T(8,128)S(1)}, f32[32,96,128]{2,1,0:T(8,128)}, u32[]{:S(2)}, u32[]{:S(2)}) collective-permute-start(f32[32,96,128]{2,1,0:T(8,128)S(1)} %shard_map.83), channel_id=1, source_target_pairs={{0,1},{1,0},{2,3},{3,2},{4,5},{5,4},{6,7},{7,6},{8,9},{9,8},{10,11... | collective-permute-start | bytes 4718600 | tf_op jit(solution)/shard_map/ppermute | solution.py:18
  16.6 7.2 %copy-start.5 = (s32[8]{0:T(128)S(1)}, s32[8]{0:T(128)}, u32[]{:S(2)}) copy-start(s32[8]{0:T(128)} %constant.37.clone) | copy-start | bytes 100
  16.6 44.4 %all-to-all-start = ((bf16[80,4,1792]{2,1,0:T(4,128)(2,1)}), bf16[80,4,1792]{2,1,0:T(4,128)(2,1)}, u32[]{:S(2)}, u32[]{:S(2)}) async-start(bf16[80,4,1792]{2,1,0:T(4,128)(2,1)} %reshape.195), calls=%async_computation | async-start | bytes 2293760 | tf_op jit(solution)/shard_map/all_to_all | solution.py:111
  35.2 16.0 %collective-permute-start.1 = (f16[17,96,128]{2,1,0:T(8,128)(2,1)S(1)}, f16[17,96,128]{2,1,0:T(8,128)(2,1)}, u32[]{:S(2)}, u32[]{:S(2)}) collective-permute-start(f16[17,96,128]{2,1,0:T(8,128)(2,1)S(1)} %pad_maximum_fusion), channel_id=1, source_target_pairs={{0,2},{1,3},{2,0},{3,1},{4,6},{5,7},{6,4},{7,5},{8,10},{9,11},{10,... | collective-permute-start | bytes 1253384 | tf_op jit(solution)/shard_map/ppermute | solution.py:18
  54.2 20.8 %collective-permute-start.2 = (f16[5,96,128]{2,1,0:T(8,128)(2,1)}, f16[5,96,128]{2,1,0:T(8,128)(2,1)S(1)}, u32[]{:S(2)}, u32[]{:S(2)}) collective-permute-start(f16[5,96,128]{2,1,0:T(8,128)(2,1)} %pad_maximum_fusion.1), channel_id=1, source_target_pairs={{0,4},{1,5},{2,6},{3,7},{4,0},{5,1},{6,2},{7,3},{8,12},{9,13},{10,... | collective-permute-start | bytes 368648 | tf_op jit(solution)/shard_map/ppermute | solution.py:18
  57.8 17.1 %collective-permute-start.3 = (f16[5,96,128]{2,1,0:T(8,128)(2,1)}, f16[5,96,128]{2,1,0:T(8,128)(2,1)}, u32[]{:S(2)}, u32[]{:S(2)}) collective-permute-start(f16[5,96,128]{2,1,0:T(8,128)(2,1)} %pad_maximum_fusion.2), channel_id=1, source_target_pairs={{0,8},{1,9},{2,10},{3,11},{4,12},{5,13},{6,14},{7,15},{8,0},{9,1},... | collective-permute-start | bytes 368648 | tf_op jit(solution)/shard_map/ppermute | solution.py:18
  59.6 16.1 %collective-permute-start.4 = (f16[5,96,128]{2,1,0:T(8,128)(2,1)}, f16[5,96,128]{2,1,0:T(8,128)(2,1)}, u32[]{:S(2)}, u32[]{:S(2)}) collective-permute-start(f16[5,96,128]{2,1,0:T(8,128)(2,1)} %pad_maximum_fusion.3), channel_id=1, source_target_pairs={{0,12},{1,13},{2,14},{3,15},{4,8},{5,9},{6,10},{7,11},{8,4},{9,5},... | collective-permute-start | bytes 368648 | tf_op jit(solution)/shard_map/ppermute | solution.py:18
  70.7 15.3 %all-to-all-start.1 = ((bf16[80,4,512]{2,1,0:T(4,128)(2,1)}), bf16[80,4,512]{2,1,0:T(4,128)(2,1)S(1)}, u32[]{:S(2)}, u32[]{:S(2)}) async-start(bf16[80,4,512]{2,1,0:T(4,128)(2,1)} %bitcast.9), calls=%async_computation.1 | async-start | bytes 655360 | tf_op jit(solution)/shard_map/all_to_all | solution.py:131

commit v2 on v1

--- a/solution.py
+++ b/solution.py
@@ -62,15 +62,13 @@
     return packed[:-1].astype(jnp.float32) * jnp.exp2(exponent - F16_TOP)
 
 
-def base_blocks(hidden, down_matrix, group, me, width):
+def base_blocks(hidden, down_matrix, group, order, width):
     rows = hidden.shape[0]
     parts = width // LANES
     quads = list(range(0, group, 4))
-    odd_order = [q + 1 for q in quads] + [q + 3 for q in quads]
-    even_order = quads + [q + 2 for q in quads]
-    odd = column_blocks(hidden, down_matrix, me ^ jnp.array(odd_order, jnp.int32), width)
+    odd = column_blocks(hidden, down_matrix, order[: group // 2], width)
     odd_in = xor_permute(odd, group, 1)
-    even = column_blocks(hidden, down_matrix, me ^ jnp.array(even_order, jnp.int32), width)
+    even = column_blocks(hidden, down_matrix, order[group // 2 :], width)
     chip = even + odd_in
     half = len(quads) * parts
     pair_in = xor_permute(pack_scaled(chip[half:]), group, 2)
@@ -85,44 +83,163 @@
     return jnp.transpose(total, (1, 0, 2)).reshape(rows, width)
 
 
+def pack_kernel(blocks, orders, me_ref, slot_ref, adapter_ref, hidden_ref, packed_ref, pick_ref, order_ref):
+    rows = hidden_ref.shape[0]
+    group = slot_ref.shape[0]
+    for i, offset in enumerate(orders):
+        order_ref[i] = me_ref[0] ^ offset
+    ids = lax.broadcasted_iota(jnp.int32, (group, 1), 0)
+    slots = jnp.zeros((group, 1), jnp.int32)
+    for adapter in range(group):
+        slots = jnp.where(ids == adapter, slot_ref[adapter], slots)
+    adapter = adapter_ref[...]
+    first = jnp.sum((adapter < ids).astype(jnp.int32), axis=1, keepdims=True)
+    shift = jnp.where(adapter == ids, slots * (blocks * BLOCK) - first, 0)
+    place = jnp.sum(shift, axis=0, keepdims=True) + lax.broadcasted_iota(jnp.int32, (1, rows), 1)
+    spots = lax.broadcasted_iota(jnp.int32, (group * blocks * BLOCK, rows), 0)
+    pick = jnp.where(spots == place, 1.0, 0.0).astype(jnp.bfloat16)
+    pick_ref[...] = pick
+    packed = jnp.dot(pick, hidden_ref[...], preferred_element_type=jnp.float32)
+    packed_ref[...] = packed.astype(jnp.bfloat16).reshape(packed_ref.shape)
+
+
+def pack_rows(hidden, adapter_of_row, adapter_holder_slot, me, orders):
+    rows, depth = hidden.shape
+    group = adapter_holder_slot.shape[0]
+    blocks = MOST // BLOCK
+    vmem = pl.BlockSpec(memory_space=pltpu.VMEM)
+    smem = pl.BlockSpec(memory_space=pltpu.SMEM)
+    return pl.pallas_call(
+        functools.partial(pack_kernel, blocks, orders),
+        out_shape=(
+            jax.ShapeDtypeStruct((group * blocks, BLOCK, depth), jnp.bfloat16),
+            jax.ShapeDtypeStruct((group * MOST, rows), jnp.bfloat16),
+            jax.ShapeDtypeStruct((len(orders),), jnp.int32),
+        ),
+        in_specs=[smem, smem, vmem, vmem],
+        out_specs=(vmem, vmem, smem),
+        compiler_params=pltpu.CompilerParams(vmem_limit_bytes=24 * 2**20),
+    )(me.reshape(1), adapter_holder_slot, adapter_of_row.reshape(1, rows), hidden)
+
+
+def adapter_kernel(rows_ref, shrink_ref, expand_ref, out_ref, total_ref):
+    step = pl.program_id(0)
+    block, depth = rows_ref.shape[1:]
+    blocks = MOST // BLOCK
+    sources = rows_ref.shape[0] // blocks
+    total = jnp.zeros(total_ref.shape, jnp.float32)
+    for source in range(sources):
+        own = rows_ref[source * blocks : (source + 1) * blocks].reshape(MOST, depth)
+        total += lax.dot_general(
+            own,
+            shrink_ref[:, source * depth : (source + 1) * depth],
+            (((1,), (1,)), ((), ())),
+            preferred_element_type=jnp.float32,
+        )
+
+    @pl.when(step == 0)
+    def _():
+        total_ref[...] = total
+
+    @pl.when(step > 0)
+    def _():
+        total_ref[...] += total
+
+    @pl.when(step == pl.num_programs(0) - 1)
+    def _():
+        rank_rows = total_ref[...].astype(jnp.bfloat16)
+        width = out_ref.shape[2]
+        for target in range(out_ref.shape[0] // blocks):
+            piece = jnp.dot(
+                rank_rows,
+                expand_ref[:, target * width : (target + 1) * width],
+                preferred_element_type=jnp.float32,
+            )
+            out_ref[target * blocks : (target + 1) * blocks] = piece.astype(jnp.bfloat16).reshape(
+                blocks, BLOCK, width
+            )
+
+
+def adapter_output(gathered, shrink, expand, group):
+    rank, hidden_width = shrink.shape
+    model_width = expand.shape[1]
+    depth = gathered.shape[2]
+    blocks = MOST // BLOCK
+    width = model_width // group
+    steps = 4
+    sources = group // steps
+    return pl.pallas_call(
+        adapter_kernel,
+        out_shape=jax.ShapeDtypeStruct((group * blocks, BLOCK, width), jnp.bfloat16),
+        grid=(steps,),
+        in_specs=[
+            pl.BlockSpec((sources * blocks, BLOCK, depth), lambda i: (i, 0, 0)),
+            pl.BlockSpec((rank, sources * depth), lambda i: (0, i)),
+            pl.BlockSpec((rank, model_width), lambda i: (0, 0)),
+        ],
+        out_specs=pl.BlockSpec((group * blocks, BLOCK, width), lambda i: (0, 0, 0)),
+        scratch_shapes=[pltpu.VMEM((MOST, rank), jnp.float32)],
+        compiler_params=pltpu.CompilerParams(vmem_limit_bytes=32 * 2**20),
+        cost_estimate=pl.CostEstimate(
+            flops=2 * MOST * rank * (hidden_width + model_width),
+            bytes_accessed=2 * rank * (hidden_width + model_width) + 2 * MOST * hidden_width,
+            transcendentals=0,
+        ),
+    )(gathered, shrink, expand)
+
+
+def shards_by_blocks(
+    hidden, down_matrix, shrink_matrices, expand_matrices, adapter_of_row, adapter_holder_slot
+):
+    group = lax.axis_size("tp")
+    me = lax.axis_index("tp")
+    rows, depth = hidden.shape
+    width = down_matrix.shape[1] // group
+    quads = list(range(0, group, 4))
+    orders = [q + k for k in (1, 3, 0, 2) for q in quads]
+    packed, pick, order = pack_rows(hidden, adapter_of_row, adapter_holder_slot, me, orders)
+    gathered = lax.all_to_all(packed, "tp", split_axis=0, concat_axis=0, tiled=True)
+    base = base_blocks(hidden, down_matrix, group, order, width)
+    shrink = jnp.swapaxes(shrink_matrices, 1, 2)[0]
+    expand = jnp.swapaxes(expand_matrices, 1, 2)[0]
+    adapter_out = adapter_output(gathered, shrink, expand, group)
+    adapter_in = lax.all_to_all(adapter_out, "tp", split_axis=0, concat_axis=0, tiled=True)
+    adapter_rows = lax.dot_general(
+        pick,
+        adapter_in.reshape(group * MOST, width),
+        (((0,), (0,)), ((), ())),
+        preferred_element_type=jnp.float32,
+    )
+    return (base + ADAPTER_SCALE * adapter_rows).astype(jnp.bfloat16)
+
+
 def shards(
     hidden, down_matrix, shrink_matrices, expand_matrices, adapter_of_row, adapter_holder_slot
 ):
     group = lax.axis_size("tp")
-    me = lax.axis_index("tp")
-    rows, depth = hidden.shape
-    model_width = down_matrix.shape[1]
-    width = model_width // group
-    rank = shrink_matrices.shape[2]
+    rows, depth = hidden.shape
+    width = down_matrix.shape[1] // group
+    if width % LANES == 0 and depth % LANES == 0 and group % 4 == 0:
+        return shards_by_blocks(
+            hidden, down_matrix, shrink_matrices, expand_matrices, adapter_of_row, adapter_holder_slot
+        )
     blocks = MOST // BLOCK
     adapter_ids = jnp.arange(group, dtype=jnp.int32)
-
     row_match = adapter_of_row[:, None] == adapter_ids[None, :]
     row_slot = jnp.sum(jnp.where(row_match, adapter_holder_slot[None, :], 0), axis=1)
     slot_mask = row_slot[None, :] == adapter_ids[:, None]
     before = jnp.cumsum(slot_mask.astype(jnp.int32), axis=1) - 1
     place = jnp.where(slot_mask, before, -1)
     pick = place[:, None, :] == jnp.arange(MOST, dtype=jnp.int32)[None, :, None]
-    pick = pick.reshape(group * MOST, rows)
-    pick16 = pick.astype(jnp.bfloat16)
-
-    packed = jnp.dot(pick16, hidden, preferred_element_type=jnp.float32).astype(jnp.bfloat16)
+    pick = pick.reshape(group * MOST, rows).astype(jnp.bfloat16)
+    packed = jnp.dot(pick, hidden, preferred_element_type=jnp.float32).astype(jnp.bfloat16)
     packed = packed.reshape(group * blocks, BLOCK, depth)
     gathered = lax.all_to_all(packed, "tp", split_axis=0, concat_axis=0, tiled=True)
-
-    if width % LANES == 0 and depth % LANES == 0:
-        base = base_blocks(hidden, down_matrix, group, me, width)
-    else:
-        partial_value = jnp.dot(hidden, down_matrix, preferred_element_type=jnp.float32)
-        base = lax.psum_scatter(partial_value, "tp", scatter_dimension=1, tiled=True)
-
-    gathered = gathered.reshape(group, MOST, depth)
-    shrink_parts = shrink_matrices.reshape(group, depth, rank)
-    rank_rows = lax.dot_general(
-        jnp.transpose(gathered, (1, 0, 2)).reshape(MOST, group * depth),
-        shrink_matrices[0],
-        (((1,), (0,)), ((), ())),
-        preferred_element_type=jnp.float32,
+    partial_value = jnp.dot(hidden, down_matrix, preferred_element_type=jnp.float32)
+    base = lax.psum_scatter(partial_value, "tp", scatter_dimension=1, tiled=True)
+    own_rows = jnp.transpose(gathered.reshape(group, MOST, depth), (1, 0, 2))
+    rank_rows = jnp.dot(
+        own_rows.reshape(MOST, group * depth), shrink_matrices[0], preferred_element_type=jnp.float32
     ).astype(jnp.bfloat16)
     adapter_out = lax.dot_general(
         rank_rows, expand_matrices[0], (((1,), (1,)), ((), ())), preferred_element_type=jnp.float32
@@ -132,7 +249,7 @@
         adapter_out.reshape(group * blocks, BLOCK, width), "tp", split_axis=0, concat_axis=0, tiled=True
     )
     adapter_rows = lax.dot_general(
-        pick16,
+        pick,
         adapter_in.reshape(group * MOST, width),
         (((0,), (0,)), ((), ())),
         preferred_element_type=jnp.float32,

time: 88.9 us -> 79.7 us (0.90)
  matrix products: 7.77 us -> 0.88 us
  other arithmetic: 8.9 us -> 4.59 us
  Pallas kernels: 18.5 us -> 22.5 us
  local copies, waits for them, and re-layouts: 9.77 us -> 6.79 us
  waiting for transfers between devices: 23.5 us -> 24.9 us
    dot_general x3 -> x1, matrix products: 7.77 us -> 0.88 us  [shards_by_blocks(): lax.dot_general(pick, adapter_in.reshape(group * MOST, width), (((0,), (0...]
    reshape x4 -> x1, local copies, waits for them, and re-layouts: 6.48 us -> 0.08 us  [shards_by_blocks(): adapter_in.reshape(group * MOST, width)]
    pallas_call x0 -> x2, Pallas kernels: none -> 4.03 us  [the longest x1 2.77 us: adapter_output(): pl.pallas_call(adapter_kernel, out_shape=jax.ShapeDtypeStruct((group * bl...]
    unnamed x16, local copies, waits for them, and re-layouts: 2.63 us -> 6.33 us
    mul x4, other arithmetic: 2.28 us -> 0.07 us  [unpack_scaled(): return packed[:-1].astype(jnp.float32) * jnp.exp2(exponent - F16_TOP)]
    all_to_all x2, waiting for transfers between devices: 9.53 us -> 11 us  [the longest x1 11 us: shards_by_blocks(): lax.all_to_all(adapter_out, 'tp', split_axis=0, concat_axis=0, tiled=True)]
    add x1, other arithmetic: 1.09 us -> 0.12 us  [base_blocks(): pair = chip[:half] + unpack_scaled(pair_in)]
  transfers between devices with their start and end apart: 7 -> 7, of which waited for: 2 -> 2; matrix products, arithmetic and copies ran while one was open for 26% -> 6% of each run, Pallas kernels for 11% -> 15%
where the time goes in v2:
time: 79.7 us; the launch traced here: 79.1 us
  waiting for transfers between devices  24.9 us (31%)
  Pallas kernels  22.5 us (28%)
  starting transfers between devices  19.2 us (24%)
  local copies, waits for them, and re-layouts  6.79 us (9%)
  other arithmetic  4.59 us (6%)
  matrix products  0.88 us (1%)
    pallas_call x2, Pallas kernels, column_blocks(): pl.pallas_call(column_blocks_kernel, out_shape=jax.ShapeDtypeStruct((coun...  18.5 us
    ppermute x5, waiting for transfers between devices, xor_permute(): return lax.ppermute(value, 'tp', [(i, i ^ offset) for i in range(group)])  13.9 us
    all_to_all x1, waiting for transfers between devices, shards_by_blocks(): lax.all_to_all(adapter_out, 'tp', split_axis=0, concat_axis=0, tiled=True)  11 us
    ppermute x5, starting transfers between devices, xor_permute(): return lax.ppermute(value, 'tp', [(i, i ^ offset) for i in range(group)])  7.87 us
    all_to_all x1, starting transfers between devices, shards_by_blocks(): lax.all_to_all(packed, 'tp', split_axis=0, concat_axis=0, tiled=True)  7.06 us
    unnamed x16, local copies, waits for them, and re-layouts  6.33 us
    all_to_all x1, starting transfers between devices, shards_by_blocks(): lax.all_to_all(adapter_out, 'tp', split_axis=0, concat_axis=0, tiled=True)  4.22 us
    pallas_call x1, Pallas kernels, adapter_output(): pl.pallas_call(adapter_kernel, out_shape=jax.ShapeDtypeStruct((group * bl...  2.77 us
  transfers between devices with their start and end apart: 7, of which 2 were waited for; matrix products, arithmetic and copies ran while one was open for 6% of the time, Pallas kernels for 15%

profile of v2, /device:TPU:0, one launch (start us, length us, event | category | flops | bytes accessed | tf_op | source)
XLA Modules:
  0.0 79.1 jit_solution(7517820922937523582)
XLA Ops:
  0.0 0.0 copy-start.1
  0.0 1.0 %copy-done.1 = bf16[96,1792]{1,0:T(8,128)(2,1)S(1)} copy-done((bf16[96,1792]{1,0:T(8,128)(2,1)S(1)}, bf16[96,1792]{1,0:T(8,128)(2,1)}, u32[]{:S(2)}) %copy-start.1) | copy-done | bytes 344088
  1.0 0.0 copy-start.6
  1.0 0.7 copy-done.6
  1.6 0.0 copy-start.7
  1.6 0.7 copy-done.7
  2.3 1.3 %shard_map.64 = (bf16[80,4,1792]{2,1,0:T(4,128)(2,1)S(1)}, bf16[320,96]{1,0:T(8,128)(2,1)S(1)}, s32[16]{0:T(128)S(1)}) custom-call(s32[1]{0:T(128)} %bitcast.me_ref, s32[16]{0:T(128)S(1)} %copy-done.6, s32[1,96]{1,0:T(1,128)S(1)} %bitcast.26, bf16[96,1792]{1,0:T(8,128)(2,1)S(1)} %copy-done.1), custom_call_target="tpu_custom_call" | custom-call | tf_op jit(solution)/shard_map/pallas_call | solution.py:112
  3.6 0.0 copy-start.4
  3.6 1.0 %copy-done.4 = bf16[80,4,1792]{2,1,0:T(4,128)(2,1)} copy-done((bf16[80,4,1792]{2,1,0:T(4,128)(2,1)}, bf16[80,4,1792]{2,1,0:T(4,128)(2,1)S(1)}, u32[]{:S(2)}) %copy-start.4) | copy-done | bytes 1146904
  4.6 0.1 fusion.9
  4.7 0.0 copy-start.2
  4.7 1.0 %copy-done.2 = bf16[96,1792]{1,0:T(8,128)(2,1)S(1)} copy-done((bf16[96,1792]{1,0:T(8,128)(2,1)S(1)}, bf16[96,1792]{1,0:T(8,128)(2,1)}, u32[]{:S(2)}) %copy-start.2) | copy-done | bytes 344088
  5.6 9.2 %shard_map.66 = f32[32,96,128]{2,1,0:T(8,128)S(1)} custom-call(s32[8]{0:T(128)S(1)} %get-tuple-element.25.order_ref, bf16[96,1792]{1,0:T(8,128)(2,1)S(1)} %copy-done.2, bf16[1792,8192]{1,0:T(8,128)(2,1)} %down_ref.3), custom_call_target="tpu_custom_call" | custom-call | flops 1409286144 | bytes 16252928 | tf_op jit(solution)/shard_map/pallas_call | solution.py:31
  14.9 0.0 copy-start.3
  14.9 0.5 collective-permute-start
  15.4 7.1 %all-to-all-start = ((bf16[80,4,1792]{2,1,0:T(4,128)(2,1)}), bf16[80,4,1792]{2,1,0:T(4,128)(2,1)S(1)}, u32[]{:S(2)}, u32[]{:S(2)}) async-start(bf16[80,4,1792]{2,1,0:T(4,128)(2,1)} %copy-done.4), calls=%async_computation | async-start | bytes 2293760 | tf_op jit(solution)/shard_map/all_to_all | solution.py:201
  22.5 0.0 copy-done.3
  22.5 9.2 %shard_map.65 = f32[32,96,128]{2,1,0:T(8,128)S(1)} custom-call(s32[8]{0:T(128)S(1)} %get-tuple-element.26.order_ref, bf16[96,1792]{1,0:T(8,128)(2,1)S(1)} %copy-done.3, bf16[1792,8192]{1,0:T(8,128)(2,1)} %down_ref.3), custom_call_target="tpu_custom_call" | custom-call | flops 1409286144 | bytes 16252928 | tf_op jit(solution)/shard_map/pallas_call | solution.py:31
  31.8 0.0 collective-permute-done
  31.8 1.6 %add.22 = f32[32,96,128]{2,1,0:T(8,128)S(1)} add(f32[32,96,128]{2,1,0:T(8,128)S(1)} %shard_map.65, f32[32,96,128]{2,1,0:T(8,128)} %collective-permute-done) | non-fusion elementwise | flops 393216 | bytes 4718592 | tf_op jit(solution)/shard_map/add | solution.py:72
  33.4 0.1 abs_reduce_fusion
  33.5 0.2 multiply_convert_fusion
  33.7 0.1 broadcast_in_dim.8
  33.8 0.1 pad_maximum_fusion
  33.9 2.0 %collective-permute-start.1 = (f16[17,96,128]{2,1,0:T(8,128)(2,1)S(1)}, f16[17,96,128]{2,1,0:T(8,128)(2,1)S(1)}, u32[]{:S(2)}, u32[]{:S(2)}) collective-permute-start(f16[17,96,128]{2,1,0:T(8,128)(2,1)S(1)} %pad_maximum_fusion), channel_id=1, source_target_pairs={{0,2},{1,3},{2,0},{3,1},{4,6},{5,7},{6,4},{7,5},{8,10},{9,11},{10,... | collective-permute-start | bytes 1253384 | tf_op jit(solution)/shard_map/ppermute | solution.py:18
  35.9 13.9 %collective-permute-done.1 = f16[17,96,128]{2,1,0:T(8,128)(2,1)S(1)} collective-permute-done((f16[17,96,128]{2,1,0:T(8,128)(2,1)S(1)}, f16[17,96,128]{2,1,0:T(8,128)(2,1)S(1)}, u32[]{:S(2)}, u32[]{:S(2)}) %collective-permute-start.1) | collective-permute-done | bytes 417824 | tf_op jit(solution)/shard_map/ppermute | solution.py:18
  49.8 0.1 slice_add_fusion
  50.0 0.0 copy-start.5
  50.0 0.2 abs_reduce_fusion.3
  50.2 0.1 multiply_convert_fusion.3
  50.3 0.1 broadcast_in_dim.9
  50.4 0.7 pad_maximum_fusion.1
  51.1 2.9 %collective-permute-start.2 = (f16[5,96,128]{2,1,0:T(8,128)(2,1)}, f16[5,96,128]{2,1,0:T(8,128)(2,1)S(1)}, u32[]{:S(2)}, u32[]{:S(2)}) collective-permute-start(f16[5,96,128]{2,1,0:T(8,128)(2,1)} %pad_maximum_fusion.1), channel_id=1, source_target_pairs={{0,4},{1,5},{2,6},{3,7},{4,0},{5,1},{6,2},{7,3},{8,12},{9,13},{10,... | collective-permute-start | bytes 368648 | tf_op jit(solution)/shard_map/ppermute | solution.py:18
  54.0 0.1 broadcast_in_dim.10
  54.1 0.7 pad_maximum_fusion.2
  54.8 1.0 %collective-permute-start.3 = (f16[5,96,128]{2,1,0:T(8,128)(2,1)}, f16[5,96,128]{2,1,0:T(8,128)(2,1)S(1)}, u32[]{:S(2)}, u32[]{:S(2)}) collective-permute-start(f16[5,96,128]{2,1,0:T(8,128)(2,1)} %pad_maximum_fusion.2), channel_id=1, source_target_pairs={{0,8},{1,9},{2,10},{3,11},{4,12},{5,13},{6,14},{7,15},{8,0},{9,1},... | collective-permute-start | bytes 368648 | tf_op jit(solution)/shard_map/ppermute | solution.py:18
  55.8 0.1 broadcast_in_dim.11
  55.8 0.7 pad_maximum_fusion.3
  56.5 1.5 %collective-permute-start.4 = (f16[5,96,128]{2,1,0:T(8,128)(2,1)}, f16[5,96,128]{2,1,0:T(8,128)(2,1)S(1)}, u32[]{:S(2)}, u32[]{:S(2)}) collective-permute-start(f16[5,96,128]{2,1,0:T(8,128)(2,1)} %pad_maximum_fusion.3), channel_id=1, source_target_pairs={{0,12},{1,13},{2,14},{3,15},{4,8},{5,9},{6,10},{7,11},{8,4},{9,5},... | collective-permute-start | bytes 368648 | tf_op jit(solution)/shard_map/ppermute | solution.py:18
  58.0 0.0 all-to-all-done.rows_ref
  58.0 0.0 copy-done.5
  58.0 0.0 copy-start
  58.0 2.0 %copy-done = bf16[1,28672,64]{1,2,0:T(8,128)(2,1)S(1)} copy-done((bf16[1,28672,64]{1,2,0:T(8,128)(2,1)S(1)}, bf16[1,28672,64]{1,2,0:T(8,128)(2,1)}, u32[]{:S(2)}) %copy-start) | copy-done | bytes 3670040
  60.0 2.8 %shard_map.67 = bf16[80,4,512]{2,1,0:T(4,128)(2,1)} custom-call(bf16[80,4,1792]{2,1,0:T(4,128)(2,1)S(1)} %all-to-all-done.rows_ref, bf16[64,28672]{1,0:T(8,128)(2,1)S(1)} %bitcast.24, bf16[64,8192]{1,0:T(8,128)(2,1)S(1)} %bitcast.25), custom_call_target="tpu_custom_call" | custom-call | flops 94371840 | bytes 5865472 | tf_op jit(solution)/shard_map/pallas_call | solution.py:171
  62.8 4.2 %all-to-all-start.1 = ((bf16[80,4,512]{2,1,0:T(4,128)(2,1)}), bf16[80,4,512]{2,1,0:T(4,128)(2,1)S(1)}, u32[]{:S(2)}, u32[]{:S(2)}) async-start(bf16[80,4,512]{2,1,0:T(4,128)(2,1)} %shard_map.67), calls=%async_computation.1 | async-start | bytes 655360 | tf_op jit(solution)/shard_map/all_to_all | solution.py:206
  67.0 0.0 collective-permute-done.2
  67.1 0.0 collective-permute-done.3
  67.1 0.0 collective-permute-done.4
  67.1 11.0 %all-to-all-done.1 = bf16[80,4,512]{2,1,0:T(4,128)(2,1)S(1)} async-done(((bf16[80,4,512]{2,1,0:T(4,128)(2,1)}), bf16[80,4,512]{2,1,0:T(4,128)(2,1)S(1)}, u32[]{:S(2)}, u32[]{:S(2)}) %all-to-all-start.1) | async-done | bytes 327712 | tf_op jit(solution)/shard_map/all_to_all | solution.py:206
  78.1 0.1 reshape.115
  78.2 0.9 %fusion.1 = bf16[96,512]{1,0:T(8,128)(2,1)} fusion(bf16[320,96]{1,0:T(8,128)(2,1)S(1)} %get-tuple-element.9, bf16[320,512]{1,0:T(8,128)(2,1)S(1)} %reshape.115, f32[16,96,128]{2,1,0:T(8,128)S(1)} %slice_add_fusion, f16[5,96,128]{2,1,0:T(8,128)(2,1)S(1)} %collective-permute-done.4, f16[5,96,128]{2,1,0:T(8,128)(2,1)S(1)} %collective-permute-done.3, ...), kind=kOutput, calls=%fused_computation.2 | convolution fusion | flops 32047104 | bytes 1146880 | tf_op jit(solution)/shard_map/dot_general | solution.py:207
  (7 shorter events, 0.1 us)
Async XLA Ops:
  0.0 1.0 %copy-start.1 = (bf16[96,1792]{1,0:T(8,128)(2,1)S(1)}, bf16[96,1792]{1,0:T(8,128)(2,1)}, u32[]{:S(2)}) copy-start(bf16[96,1792]{1,0:T(8,128)(2,1)} %hidden_ref.5) | copy-start | bytes 1032196
  1.0 0.7 copy-start.6
  1.6 0.7 copy-start.7
  3.6 1.0 %copy-start.4 = (bf16[80,4,1792]{2,1,0:T(4,128)(2,1)}, bf16[80,4,1792]{2,1,0:T(4,128)(2,1)S(1)}, u32[]{:S(2)}) copy-start(bf16[80,4,1792]{2,1,0:T(4,128)(2,1)S(1)} %get-tuple-element.10) | copy-start | bytes 3440644
  4.7 1.0 %copy-start.2 = (bf16[96,1792]{1,0:T(8,128)(2,1)S(1)}, bf16[96,1792]{1,0:T(8,128)(2,1)}, u32[]{:S(2)}) copy-start(bf16[96,1792]{1,0:T(8,128)(2,1)} %hidden_ref.5) | copy-start | bytes 1032196
  14.9 7.6 %copy-start.3 = (bf16[96,1792]{1,0:T(8,128)(2,1)S(1)}, bf16[96,1792]{1,0:T(8,128)(2,1)}, u32[]{:S(2)}) copy-start(bf16[96,1792]{1,0:T(8,128)(2,1)} %hidden_ref.5) | copy-start | bytes 1032196
  14.9 16.9 %collective-permute-start = (f32[32,96,128]{2,1,0:T(8,128)S(1)}, f32[32,96,128]{2,1,0:T(8,128)}, u32[]{:S(2)}, u32[]{:S(2)}) collective-permute-start(f32[32,96,128]{2,1,0:T(8,128)S(1)} %shard_map.66), channel_id=1, source_target_pairs={{0,1},{1,0},{2,3},{3,2},{4,5},{5,4},{6,7},{7,6},{8,9},{9,8},{10,11... | collective-permute-start | bytes 4718600 | tf_op jit(solution)/shard_map/ppermute | solution.py:18
  15.4 42.6 %all-to-all-start = ((bf16[80,4,1792]{2,1,0:T(4,128)(2,1)}), bf16[80,4,1792]{2,1,0:T(4,128)(2,1)S(1)}, u32[]{:S(2)}, u32[]{:S(2)}) async-start(bf16[80,4,1792]{2,1,0:T(4,128)(2,1)} %copy-done.4), calls=%async_computation | async-start | bytes 2293760 | tf_op jit(solution)/shard_map/all_to_all | solution.py:201
  33.9 15.9 %collective-permute-start.1 = (f16[17,96,128]{2,1,0:T(8,128)(2,1)S(1)}, f16[17,96,128]{2,1,0:T(8,128)(2,1)S(1)}, u32[]{:S(2)}, u32[]{:S(2)}) collective-permute-start(f16[17,96,128]{2,1,0:T(8,128)(2,1)S(1)} %pad_maximum_fusion), channel_id=1, source_target_pairs={{0,2},{1,3},{2,0},{3,1},{4,6},{5,7},{6,4},{7,5},{8,10},{9,11},{10,... | collective-permute-start | bytes 1253384 | tf_op jit(solution)/shard_map/ppermute | solution.py:18
  50.0 8.0 %copy-start.5 = (bf16[1,8192,64]{1,2,0:T(8,128)(2,1)S(1)}, bf16[1,8192,64]{1,2,0:T(8,128)(2,1)}, u32[]{:S(2)}) copy-start(bf16[1,8192,64]{1,2,0:T(8,128)(2,1)} %param.9) | copy-start | bytes 3145732
  51.1 15.9 %collective-permute-start.2 = (f16[5,96,128]{2,1,0:T(8,128)(2,1)}, f16[5,96,128]{2,1,0:T(8,128)(2,1)S(1)}, u32[]{:S(2)}, u32[]{:S(2)}) collective-permute-start(f16[5,96,128]{2,1,0:T(8,128)(2,1)} %pad_maximum_fusion.1), channel_id=1, source_target_pairs={{0,4},{1,5},{2,6},{3,7},{4,0},{5,1},{6,2},{7,3},{8,12},{9,13},{10,... | collective-permute-start | bytes 368648 | tf_op jit(solution)/shard_map/ppermute | solution.py:18
  54.8 12.3 %collective-permute-start.3 = (f16[5,96,128]{2,1,0:T(8,128)(2,1)}, f16[5,96,128]{2,1,0:T(8,128)(2,1)S(1)}, u32[]{:S(2)}, u32[]{:S(2)}) collective-permute-start(f16[5,96,128]{2,1,0:T(8,128)(2,1)} %pad_maximum_fusion.2), channel_id=1, source_target_pairs={{0,8},{1,9},{2,10},{3,11},{4,12},{5,13},{6,14},{7,15},{8,0},{9,1},... | collective-permute-start | bytes 368648 | tf_op jit(solution)/shard_map/ppermute | solution.py:18
  56.5 10.6 %collective-permute-start.4 = (f16[5,96,128]{2,1,0:T(8,128)(2,1)}, f16[5,96,128]{2,1,0:T(8,128)(2,1)S(1)}, u32[]{:S(2)}, u32[]{:S(2)}) collective-permute-start(f16[5,96,128]{2,1,0:T(8,128)(2,1)} %pad_maximum_fusion.3), channel_id=1, source_target_pairs={{0,12},{1,13},{2,14},{3,15},{4,8},{5,9},{6,10},{7,11},{8,4},{9,5},... | collective-permute-start | bytes 368648 | tf_op jit(solution)/shard_map/ppermute | solution.py:18
  58.0 2.0 %copy-start = (bf16[1,28672,64]{1,2,0:T(8,128)(2,1)S(1)}, bf16[1,28672,64]{1,2,0:T(8,128)(2,1)}, u32[]{:S(2)}) copy-start(bf16[1,28672,64]{1,2,0:T(8,128)(2,1)} %param.8) | copy-start | bytes 11010052
  62.8 15.3 %all-to-all-start.1 = ((bf16[80,4,512]{2,1,0:T(4,128)(2,1)}), bf16[80,4,512]{2,1,0:T(4,128)(2,1)S(1)}, u32[]{:S(2)}, u32[]{:S(2)}) async-start(bf16[80,4,512]{2,1,0:T(4,128)(2,1)} %shard_map.67), calls=%async_computation.1 | async-start | bytes 655360 | tf_op jit(solution)/shard_map/all_to_all | solution.py:206

commit v3 on v2

--- a/solution.py
+++ b/solution.py
@@ -18,34 +18,49 @@
     return lax.ppermute(value, "tp", [(i, i ^ offset) for i in range(group)])
 
 
-def column_blocks_kernel(order_ref, hidden_ref, down_ref, out_ref):
-    product = jnp.dot(hidden_ref[...], down_ref[...], preferred_element_type=jnp.float32)
-    for lane in range(out_ref.shape[0]):
-        out_ref[lane] = product[:, lane * LANES : (lane + 1) * LANES]
+def column_blocks_kernel(order_ref, hidden_ref, down_ref, out_ref, held_ref, sems):
+    count, depth, width = held_ref.shape
+    parts = width // LANES
+    pieces = sems.shape[1]
+    cut = depth // pieces
+
+    def copy(block, piece):
+        start = pl.multiple_of(order_ref[block] * width, LANES)
+        lines = pl.ds(piece * cut, cut)
+        return pltpu.make_async_copy(
+            down_ref.at[lines, pl.ds(start, width)], held_ref.at[block, lines], sems.at[block, piece]
+        )
+
+    for block in range(count):
+        for piece in range(pieces):
+            copy(block, piece).start()
+    for block in range(count):
+        for piece in range(pieces):
+            copy(block, piece).wait()
+        product = jnp.dot(hidden_ref[...], held_ref[block], preferred_element_type=jnp.float32)
+        for lane in range(parts):
+            out_ref[block * parts + lane] = product[:, lane * LANES : (lane + 1) * LANES]
 
 
 def column_blocks(hidden, down_matrix, order, width):
     rows, depth = hidden.shape
     count = order.shape[0]
-    parts = width // LANES
+    pieces = 2 if depth % 32 == 0 else 1
+    vmem = pl.BlockSpec(memory_space=pltpu.VMEM)
     return pl.pallas_call(
         column_blocks_kernel,
-        out_shape=jax.ShapeDtypeStruct((count * parts, rows, LANES), jnp.float32),
-        grid_spec=pltpu.PrefetchScalarGridSpec(
-            num_scalar_prefetch=1,
-            grid=(count,),
-            in_specs=[
-                pl.BlockSpec((rows, depth), lambda j, order_ref: (0, 0)),
-                pl.BlockSpec((depth, width), lambda j, order_ref: (0, order_ref[j])),
-            ],
-            out_specs=pl.BlockSpec((parts, rows, LANES), lambda j, order_ref: (j, 0, 0)),
-        ),
+        out_shape=jax.ShapeDtypeStruct((count * width // LANES, rows, LANES), jnp.float32),
+        in_specs=[
+            pl.BlockSpec(memory_space=pltpu.SMEM),
+            vmem,
+            pl.BlockSpec(memory_space=pl.ANY),
+        ],
+        out_specs=vmem,
+        scratch_shapes=[
+            pltpu.VMEM((count, depth, width), jnp.bfloat16),
+            pltpu.SemaphoreType.DMA((count, pieces)),
+        ],
         compiler_params=pltpu.CompilerParams(vmem_limit_bytes=40 * 2**20),
-        cost_estimate=pl.CostEstimate(
-            flops=2 * rows * depth * width * count,
-            bytes_accessed=2 * depth * width * count + 4 * rows * width * count,
-            transcendentals=0,
-        ),
     )(order, hidden, down_matrix)
 
 

time: 79.7 us -> 74.5 us (0.935)
  Pallas kernels: 22.5 us -> 16.8 us
  waiting for transfers between devices: 24.9 us -> 26.2 us
    pallas_call x2, Pallas kernels: 18.5 us -> 12.8 us  [column_blocks(): pl.pallas_call(column_blocks_kernel, out_shape=jax.ShapeDtypeStruct((coun...]
    ppermute x5, waiting for transfers between devices: 13.9 us -> 15.2 us  [xor_permute(): return lax.ppermute(value, 'tp', [(i, i ^ offset) for i in range(group)])]
  transfers between devices with their start and end apart: 7 -> 7, of which waited for: 2 -> 2; matrix products, arithmetic and copies ran while one was open for 6% -> 7% of each run, Pallas kernels for 15% -> 12%
where the time goes in v3:
time: 74.5 us; the launch traced here: 74.1 us
  waiting for transfers between devices  26.2 us (35%)
  starting transfers between devices  18.6 us (25%)
  Pallas kernels  16.8 us (23%)
  local copies, waits for them, and re-layouts  6.79 us (9%)
  other arithmetic  4.59 us (6%)
  matrix products  0.88 us (1%)
    ppermute x5, waiting for transfers between devices, xor_permute(): return lax.ppermute(value, 'tp', [(i, i ^ offset) for i in range(group)])  15.2 us
    pallas_call x2, Pallas kernels, column_blocks(): pl.pallas_call(column_blocks_kernel, out_shape=jax.ShapeDtypeStruct((coun...  12.8 us
    all_to_all x1, waiting for transfers between devices, shards_by_blocks(): lax.all_to_all(adapter_out, 'tp', split_axis=0, concat_axis=0, tiled=True)  11 us
    ppermute x5, starting transfers between devices, xor_permute(): return lax.ppermute(value, 'tp', [(i, i ^ offset) for i in range(group)])  7.97 us
    all_to_all x1, starting transfers between devices, shards_by_blocks(): lax.all_to_all(packed, 'tp', split_axis=0, concat_axis=0, tiled=True)  7.06 us
    unnamed x16, local copies, waits for them, and re-layouts  6.33 us
    all_to_all x1, starting transfers between devices, shards_by_blocks(): lax.all_to_all(adapter_out, 'tp', split_axis=0, concat_axis=0, tiled=True)  3.54 us
    pallas_call x1, Pallas kernels, adapter_output(): pl.pallas_call(adapter_kernel, out_shape=jax.ShapeDtypeStruct((group * bl...  2.77 us
  transfers between devices with their start and end apart: 7, of which 2 were waited for; matrix products, arithmetic and copies ran while one was open for 7% of the time, Pallas kernels for 12%

profile of v3, /device:TPU:0, one launch (start us, length us, event | category | flops | bytes accessed | tf_op | source)
XLA Modules:
  0.0 74.1 jit_solution(7894529000692239055)
XLA Ops:
  0.0 0.0 copy-start.1
  0.0 1.0 %copy-done.1 = bf16[96,1792]{1,0:T(8,128)(2,1)S(1)} copy-done((bf16[96,1792]{1,0:T(8,128)(2,1)S(1)}, bf16[96,1792]{1,0:T(8,128)(2,1)}, u32[]{:S(2)}) %copy-start.1) | copy-done | bytes 344088
  1.0 0.0 copy-start.6
  1.0 0.7 copy-done.6
  1.6 0.0 copy-start.7
  1.6 0.7 copy-done.7
  2.3 1.3 %shard_map.64 = (bf16[80,4,1792]{2,1,0:T(4,128)(2,1)S(1)}, bf16[320,96]{1,0:T(8,128)(2,1)S(1)}, s32[16]{0:T(128)S(1)}) custom-call(s32[1]{0:T(128)} %bitcast.me_ref, s32[16]{0:T(128)S(1)} %copy-done.6, s32[1,96]{1,0:T(1,128)S(1)} %bitcast.26, bf16[96,1792]{1,0:T(8,128)(2,1)S(1)} %copy-done.1), custom_call_target="tpu_custom_call" | custom-call | tf_op jit(solution)/shard_map/pallas_call | solution.py:127
  3.6 0.0 copy-start.4
  3.6 1.0 %copy-done.4 = bf16[80,4,1792]{2,1,0:T(4,128)(2,1)} copy-done((bf16[80,4,1792]{2,1,0:T(4,128)(2,1)}, bf16[80,4,1792]{2,1,0:T(4,128)(2,1)S(1)}, u32[]{:S(2)}) %copy-start.4) | copy-done | bytes 1146904
  4.6 0.1 fusion.9
  4.7 0.0 copy-start.2
  4.7 1.0 %copy-done.2 = bf16[96,1792]{1,0:T(8,128)(2,1)S(1)} copy-done((bf16[96,1792]{1,0:T(8,128)(2,1)S(1)}, bf16[96,1792]{1,0:T(8,128)(2,1)}, u32[]{:S(2)}) %copy-start.2) | copy-done | bytes 344088
  5.6 6.4 %shard_map.66 = f32[32,96,128]{2,1,0:T(8,128)S(1)} custom-call(s32[8]{0:T(128)S(1)} %get-tuple-element.25.order_ref, bf16[96,1792]{1,0:T(8,128)(2,1)S(1)} %copy-done.2, bf16[1792,8192]{1,0:T(8,128)(2,1)} %down_ref.3), custom_call_target="tpu_custom_call" | custom-call | tf_op jit(solution)/shard_map/pallas_call | solution.py:50
  12.1 0.0 copy-start.3
  12.1 0.5 collective-permute-start
  12.6 7.1 %all-to-all-start = ((bf16[80,4,1792]{2,1,0:T(4,128)(2,1)}), bf16[80,4,1792]{2,1,0:T(4,128)(2,1)S(1)}, u32[]{:S(2)}, u32[]{:S(2)}) async-start(bf16[80,4,1792]{2,1,0:T(4,128)(2,1)} %copy-done.4), calls=%async_computation | async-start | bytes 2293760 | tf_op jit(solution)/shard_map/all_to_all | solution.py:216
  19.7 0.0 copy-done.3
  19.7 6.4 %shard_map.65 = f32[32,96,128]{2,1,0:T(8,128)S(1)} custom-call(s32[8]{0:T(128)S(1)} %get-tuple-element.26.order_ref, bf16[96,1792]{1,0:T(8,128)(2,1)S(1)} %copy-done.3, bf16[1792,8192]{1,0:T(8,128)(2,1)} %down_ref.3), custom_call_target="tpu_custom_call" | custom-call | tf_op jit(solution)/shard_map/pallas_call | solution.py:50
  26.1 0.0 collective-permute-done
  26.1 1.6 %add.22 = f32[32,96,128]{2,1,0:T(8,128)S(1)} add(f32[32,96,128]{2,1,0:T(8,128)S(1)} %shard_map.65, f32[32,96,128]{2,1,0:T(8,128)} %collective-permute-done) | non-fusion elementwise | flops 393216 | bytes 4718592 | tf_op jit(solution)/shard_map/add | solution.py:87
  27.7 0.1 abs_reduce_fusion
  27.8 0.2 multiply_convert_fusion
  28.0 0.1 broadcast_in_dim.8
  28.1 0.1 pad_maximum_fusion
  28.2 2.0 %collective-permute-start.1 = (f16[17,96,128]{2,1,0:T(8,128)(2,1)S(1)}, f16[17,96,128]{2,1,0:T(8,128)(2,1)S(1)}, u32[]{:S(2)}, u32[]{:S(2)}) collective-permute-start(f16[17,96,128]{2,1,0:T(8,128)(2,1)S(1)} %pad_maximum_fusion), channel_id=1, source_target_pairs={{0,2},{1,3},{2,0},{3,1},{4,6},{5,7},{6,4},{7,5},{8,10},{9,11},{10,... | collective-permute-start | bytes 1253384 | tf_op jit(solution)/shard_map/ppermute | solution.py:18
  30.2 15.2 %collective-permute-done.1 = f16[17,96,128]{2,1,0:T(8,128)(2,1)S(1)} collective-permute-done((f16[17,96,128]{2,1,0:T(8,128)(2,1)S(1)}, f16[17,96,128]{2,1,0:T(8,128)(2,1)S(1)}, u32[]{:S(2)}, u32[]{:S(2)}) %collective-permute-start.1) | collective-permute-done | bytes 417824 | tf_op jit(solution)/shard_map/ppermute | solution.py:18
  45.4 0.1 slice_add_fusion
  45.5 0.0 copy-start.5
  45.6 0.2 abs_reduce_fusion.3
  45.7 0.1 multiply_convert_fusion.3
  45.9 0.1 broadcast_in_dim.9
  46.0 0.7 pad_maximum_fusion.1
  46.7 3.1 %collective-permute-start.2 = (f16[5,96,128]{2,1,0:T(8,128)(2,1)}, f16[5,96,128]{2,1,0:T(8,128)(2,1)S(1)}, u32[]{:S(2)}, u32[]{:S(2)}) collective-permute-start(f16[5,96,128]{2,1,0:T(8,128)(2,1)} %pad_maximum_fusion.1), channel_id=1, source_target_pairs={{0,4},{1,5},{2,6},{3,7},{4,0},{5,1},{6,2},{7,3},{8,12},{9,13},{10,... | collective-permute-start | bytes 368648 | tf_op jit(solution)/shard_map/ppermute | solution.py:18
  49.8 0.1 broadcast_in_dim.10
  49.8 0.7 pad_maximum_fusion.2
  50.5 0.7 collective-permute-start.3
  51.2 0.1 broadcast_in_dim.11
  51.3 0.7 pad_maximum_fusion.3
  52.0 1.7 %collective-permute-start.4 = (f16[5,96,128]{2,1,0:T(8,128)(2,1)}, f16[5,96,128]{2,1,0:T(8,128)(2,1)S(1)}, u32[]{:S(2)}, u32[]{:S(2)}) collective-permute-start(f16[5,96,128]{2,1,0:T(8,128)(2,1)} %pad_maximum_fusion.3), channel_id=1, source_target_pairs={{0,12},{1,13},{2,14},{3,15},{4,8},{5,9},{6,10},{7,11},{8,4},{9,5},... | collective-permute-start | bytes 368648 | tf_op jit(solution)/shard_map/ppermute | solution.py:18
  53.7 0.0 all-to-all-done.rows_ref
  53.7 0.0 copy-done.5
  53.7 0.0 copy-start
  53.7 2.0 %copy-done = bf16[1,28672,64]{1,2,0:T(8,128)(2,1)S(1)} copy-done((bf16[1,28672,64]{1,2,0:T(8,128)(2,1)S(1)}, bf16[1,28672,64]{1,2,0:T(8,128)(2,1)}, u32[]{:S(2)}) %copy-start) | copy-done | bytes 3670040
  55.7 2.8 %shard_map.67 = bf16[80,4,512]{2,1,0:T(4,128)(2,1)} custom-call(bf16[80,4,1792]{2,1,0:T(4,128)(2,1)S(1)} %all-to-all-done.rows_ref, bf16[64,28672]{1,0:T(8,128)(2,1)S(1)} %bitcast.24, bf16[64,8192]{1,0:T(8,128)(2,1)S(1)} %bitcast.25), custom_call_target="tpu_custom_call" | custom-call | flops 94371840 | bytes 5865472 | tf_op jit(solution)/shard_map/pallas_call | solution.py:186
  58.5 3.5 %all-to-all-start.1 = ((bf16[80,4,512]{2,1,0:T(4,128)(2,1)}), bf16[80,4,512]{2,1,0:T(4,128)(2,1)S(1)}, u32[]{:S(2)}, u32[]{:S(2)}) async-start(bf16[80,4,512]{2,1,0:T(4,128)(2,1)} %shard_map.67), calls=%async_computation.1 | async-start | bytes 655360 | tf_op jit(solution)/shard_map/all_to_all | solution.py:221
  62.0 0.0 collective-permute-done.2
  62.1 0.0 collective-permute-done.3
  62.1 0.0 collective-permute-done.4
  62.1 11.0 %all-to-all-done.1 = bf16[80,4,512]{2,1,0:T(4,128)(2,1)S(1)} async-done(((bf16[80,4,512]{2,1,0:T(4,128)(2,1)}), bf16[80,4,512]{2,1,0:T(4,128)(2,1)S(1)}, u32[]{:S(2)}, u32[]{:S(2)}) %all-to-all-start.1) | async-done | bytes 327712 | tf_op jit(solution)/shard_map/all_to_all | solution.py:221
  73.1 0.1 reshape.115
  73.2 0.9 %fusion.1 = bf16[96,512]{1,0:T(8,128)(2,1)} fusion(bf16[320,96]{1,0:T(8,128)(2,1)S(1)} %get-tuple-element.9, bf16[320,512]{1,0:T(8,128)(2,1)S(1)} %reshape.115, f32[16,96,128]{2,1,0:T(8,128)S(1)} %slice_add_fusion, f16[5,96,128]{2,1,0:T(8,128)(2,1)S(1)} %collective-permute-done.4, f16[5,96,128]{2,1,0:T(8,128)(2,1)S(1)} %collective-permute-done.3, ...), kind=kOutput, calls=%fused_computation.2 | convolution fusion | flops 32047104 | bytes 1146880 | tf_op jit(solution)/shard_map/dot_general | solution.py:222
  (7 shorter events, 0.1 us)
Async XLA Ops:
  0.0 1.0 %copy-start.1 = (bf16[96,1792]{1,0:T(8,128)(2,1)S(1)}, bf16[96,1792]{1,0:T(8,128)(2,1)}, u32[]{:S(2)}) copy-start(bf16[96,1792]{1,0:T(8,128)(2,1)} %hidden_ref.5) | copy-start | bytes 1032196
  1.0 0.7 copy-start.6
  1.6 0.7 copy-start.7
  3.6 1.0 %copy-start.4 = (bf16[80,4,1792]{2,1,0:T(4,128)(2,1)}, bf16[80,4,1792]{2,1,0:T(4,128)(2,1)S(1)}, u32[]{:S(2)}) copy-start(bf16[80,4,1792]{2,1,0:T(4,128)(2,1)S(1)} %get-tuple-element.10) | copy-start | bytes 3440644
  4.7 1.0 %copy-start.2 = (bf16[96,1792]{1,0:T(8,128)(2,1)S(1)}, bf16[96,1792]{1,0:T(8,128)(2,1)}, u32[]{:S(2)}) copy-start(bf16[96,1792]{1,0:T(8,128)(2,1)} %hidden_ref.5) | copy-start | bytes 1032196
  12.1 7.6 %copy-start.3 = (bf16[96,1792]{1,0:T(8,128)(2,1)S(1)}, bf16[96,1792]{1,0:T(8,128)(2,1)}, u32[]{:S(2)}) copy-start(bf16[96,1792]{1,0:T(8,128)(2,1)} %hidden_ref.5) | copy-start | bytes 1032196
  12.1 14.0 %collective-permute-start = (f32[32,96,128]{2,1,0:T(8,128)S(1)}, f32[32,96,128]{2,1,0:T(8,128)}, u32[]{:S(2)}, u32[]{:S(2)}) collective-permute-start(f32[32,96,128]{2,1,0:T(8,128)S(1)} %shard_map.66), channel_id=1, source_target_pairs={{0,1},{1,0},{2,3},{3,2},{4,5},{5,4},{6,7},{7,6},{8,9},{9,8},{10,11... | collective-permute-start | bytes 4718600 | tf_op jit(solution)/shard_map/ppermute | solution.py:18
  12.6 41.1 %all-to-all-start = ((bf16[80,4,1792]{2,1,0:T(4,128)(2,1)}), bf16[80,4,1792]{2,1,0:T(4,128)(2,1)S(1)}, u32[]{:S(2)}, u32[]{:S(2)}) async-start(bf16[80,4,1792]{2,1,0:T(4,128)(2,1)} %copy-done.4), calls=%async_computation | async-start | bytes 2293760 | tf_op jit(solution)/shard_map/all_to_all | solution.py:216
  28.2 17.2 %collective-permute-start.1 = (f16[17,96,128]{2,1,0:T(8,128)(2,1)S(1)}, f16[17,96,128]{2,1,0:T(8,128)(2,1)S(1)}, u32[]{:S(2)}, u32[]{:S(2)}) collective-permute-start(f16[17,96,128]{2,1,0:T(8,128)(2,1)S(1)} %pad_maximum_fusion), channel_id=1, source_target_pairs={{0,2},{1,3},{2,0},{3,1},{4,6},{5,7},{6,4},{7,5},{8,10},{9,11},{10,... | collective-permute-start | bytes 1253384 | tf_op jit(solution)/shard_map/ppermute | solution.py:18
  45.5 8.1 %copy-start.5 = (bf16[1,8192,64]{1,2,0:T(8,128)(2,1)S(1)}, bf16[1,8192,64]{1,2,0:T(8,128)(2,1)}, u32[]{:S(2)}) copy-start(bf16[1,8192,64]{1,2,0:T(8,128)(2,1)} %param.9) | copy-start | bytes 3145732
  46.7 15.4 %collective-permute-start.2 = (f16[5,96,128]{2,1,0:T(8,128)(2,1)}, f16[5,96,128]{2,1,0:T(8,128)(2,1)S(1)}, u32[]{:S(2)}, u32[]{:S(2)}) collective-permute-start(f16[5,96,128]{2,1,0:T(8,128)(2,1)} %pad_maximum_fusion.1), channel_id=1, source_target_pairs={{0,4},{1,5},{2,6},{3,7},{4,0},{5,1},{6,2},{7,3},{8,12},{9,13},{10,... | collective-permute-start | bytes 368648 | tf_op jit(solution)/shard_map/ppermute | solution.py:18
  50.5 11.5 %collective-permute-start.3 = (f16[5,96,128]{2,1,0:T(8,128)(2,1)}, f16[5,96,128]{2,1,0:T(8,128)(2,1)S(1)}, u32[]{:S(2)}, u32[]{:S(2)}) collective-permute-start(f16[5,96,128]{2,1,0:T(8,128)(2,1)} %pad_maximum_fusion.2), channel_id=1, source_target_pairs={{0,8},{1,9},{2,10},{3,11},{4,12},{5,13},{6,14},{7,15},{8,0},{9,1},... | collective-permute-start | bytes 368648 | tf_op jit(solution)/shard_map/ppermute | solution.py:18
  52.0 10.1 %collective-permute-start.4 = (f16[5,96,128]{2,1,0:T(8,128)(2,1)}, f16[5,96,128]{2,1,0:T(8,128)(2,1)S(1)}, u32[]{:S(2)}, u32[]{:S(2)}) collective-permute-start(f16[5,96,128]{2,1,0:T(8,128)(2,1)} %pad_maximum_fusion.3), channel_id=1, source_target_pairs={{0,12},{1,13},{2,14},{3,15},{4,8},{5,9},{6,10},{7,11},{8,4},{9,5},... | collective-permute-start | bytes 368648 | tf_op jit(solution)/shard_map/ppermute | solution.py:18
  53.7 2.0 %copy-start = (bf16[1,28672,64]{1,2,0:T(8,128)(2,1)S(1)}, bf16[1,28672,64]{1,2,0:T(8,128)(2,1)}, u32[]{:S(2)}) copy-start(bf16[1,28672,64]{1,2,0:T(8,128)(2,1)} %param.8) | copy-start | bytes 11010052
  58.5 14.6 %all-to-all-start.1 = ((bf16[80,4,512]{2,1,0:T(4,128)(2,1)}), bf16[80,4,512]{2,1,0:T(4,128)(2,1)S(1)}, u32[]{:S(2)}, u32[]{:S(2)}) async-start(bf16[80,4,512]{2,1,0:T(4,128)(2,1)} %shard_map.67), calls=%async_computation.1 | async-start | bytes 655360 | tf_op jit(solution)/shard_map/all_to_all | solution.py:221

commit v4 on v3

--- a/solution.py
+++ b/solution.py
@@ -14,11 +14,15 @@
 F16_TOP = 14.0
 
 
+def in_hbm(value):
+    return pltpu.with_memory_space_constraint(value, pltpu.HBM)
+
+
 def xor_permute(value, group, offset):
     return lax.ppermute(value, "tp", [(i, i ^ offset) for i in range(group)])
 
 
-def column_blocks_kernel(order_ref, hidden_ref, down_ref, out_ref, held_ref, sems):
+def column_blocks_kernel(order_ref, hidden_hbm, down_ref, out_ref, hidden_ref, held_ref, hidden_sem, sems):
     count, depth, width = held_ref.shape
     parts = width // LANES
     pieces = sems.shape[1]
@@ -31,9 +35,12 @@
             down_ref.at[lines, pl.ds(start, width)], held_ref.at[block, lines], sems.at[block, piece]
         )
 
+    hidden_copy = pltpu.make_async_copy(hidden_hbm, hidden_ref, hidden_sem)
+    hidden_copy.start()
     for block in range(count):
         for piece in range(pieces):
             copy(block, piece).start()
+    hidden_copy.wait()
     for block in range(count):
         for piece in range(pieces):
             copy(block, piece).wait()
@@ -46,22 +53,24 @@
     rows, depth = hidden.shape
     count = order.shape[0]
     pieces = 2 if depth % 32 == 0 else 1
-    vmem = pl.BlockSpec(memory_space=pltpu.VMEM)
     return pl.pallas_call(
         column_blocks_kernel,
         out_shape=jax.ShapeDtypeStruct((count * width // LANES, rows, LANES), jnp.float32),
         in_specs=[
             pl.BlockSpec(memory_space=pltpu.SMEM),
-            vmem,
-            pl.BlockSpec(memory_space=pl.ANY),
+            pl.BlockSpec(memory_space=pltpu.HBM),
+            pl.BlockSpec(memory_space=pltpu.HBM),
         ],
-        out_specs=vmem,
+        out_specs=pl.BlockSpec(memory_space=pltpu.VMEM),
         scratch_shapes=[
+            pltpu.VMEM((rows, depth), jnp.bfloat16),
             pltpu.VMEM((count, depth, width), jnp.bfloat16),
+            pltpu.SemaphoreType.DMA,
             pltpu.SemaphoreType.DMA((count, pieces)),
         ],
         compiler_params=pltpu.CompilerParams(vmem_limit_bytes=40 * 2**20),
-    )(order, hidden, down_matrix)
+        cost_estimate=pl.CostEstimate(flops=1000, bytes_accessed=1000, transcendentals=0),
+    )(order, in_hbm(hidden), in_hbm(down_matrix))
 
 
 def pack_scaled(value):
@@ -98,15 +107,38 @@
     return jnp.transpose(total, (1, 0, 2)).reshape(rows, width)
 
 
-def pack_kernel(blocks, orders, me_ref, slot_ref, adapter_ref, hidden_ref, packed_ref, pick_ref, order_ref):
+def pack_kernel(
+    blocks,
+    orders,
+    me_ref,
+    slot_hbm,
+    adapter_hbm,
+    hidden_hbm,
+    packed_ref,
+    pick_ref,
+    order_ref,
+    slot_ref,
+    adapter_ref,
+    hidden_ref,
+    sems,
+):
     rows = hidden_ref.shape[0]
     group = slot_ref.shape[0]
+    copies = [
+        pltpu.make_async_copy(slot_hbm, slot_ref, sems.at[0]),
+        pltpu.make_async_copy(adapter_hbm, adapter_ref, sems.at[1]),
+        pltpu.make_async_copy(hidden_hbm, hidden_ref, sems.at[2]),
+    ]
+    for copy in copies:
+        copy.start()
     for i, offset in enumerate(orders):
         order_ref[i] = me_ref[0] ^ offset
     ids = lax.broadcasted_iota(jnp.int32, (group, 1), 0)
     slots = jnp.zeros((group, 1), jnp.int32)
+    copies[0].wait()
     for adapter in range(group):
         slots = jnp.where(ids == adapter, slot_ref[adapter], slots)
+    copies[1].wait()
     adapter = adapter_ref[...]
     first = jnp.sum((adapter < ids).astype(jnp.int32), axis=1, keepdims=True)
     shift = jnp.where(adapter == ids, slots * (blocks * BLOCK) - first, 0)
@@ -114,6 +146,7 @@
     spots = lax.broadcasted_iota(jnp.int32, (group * blocks * BLOCK, rows), 0)
     pick = jnp.where(spots == place, 1.0, 0.0).astype(jnp.bfloat16)
     pick_ref[...] = pick
+    copies[2].wait()
     packed = jnp.dot(pick, hidden_ref[...], preferred_element_type=jnp.float32)
     packed_ref[...] = packed.astype(jnp.bfloat16).reshape(packed_ref.shape)
 
@@ -124,6 +157,7 @@
     blocks = MOST // BLOCK
     vmem = pl.BlockSpec(memory_space=pltpu.VMEM)
     smem = pl.BlockSpec(memory_space=pltpu.SMEM)
+    anywhere = pl.BlockSpec(memory_space=pltpu.HBM)
     return pl.pallas_call(
         functools.partial(pack_kernel, blocks, orders),
         out_shape=(
@@ -131,10 +165,16 @@
             jax.ShapeDtypeStruct((group * MOST, rows), jnp.bfloat16),
             jax.ShapeDtypeStruct((len(orders),), jnp.int32),
         ),
-        in_specs=[smem, smem, vmem, vmem],
+        in_specs=[smem, anywhere, anywhere, anywhere],
         out_specs=(vmem, vmem, smem),
+        scratch_shapes=[
+            pltpu.SMEM((group,), jnp.int32),
+            pltpu.VMEM((1, rows), jnp.int32),
+            pltpu.VMEM((rows, depth), jnp.bfloat16),
+            pltpu.SemaphoreType.DMA((3,)),
+        ],
         compiler_params=pltpu.CompilerParams(vmem_limit_bytes=24 * 2**20),
-    )(me.reshape(1), adapter_holder_slot, adapter_of_row.reshape(1, rows), hidden)
+    )(me.reshape(1), in_hbm(adapter_holder_slot), in_hbm(adapter_of_row.reshape(1, rows)), in_hbm(hidden))
 
 
 def adapter_kernel(rows_ref, shrink_ref, expand_ref, out_ref, total_ref):
@@ -200,7 +240,7 @@
             bytes_accessed=2 * rank * (hidden_width + model_width) + 2 * MOST * hidden_width,
             transcendentals=0,
         ),
-    )(gathered, shrink, expand)
+    )(gathered, in_hbm(shrink), in_hbm(expand))
 
 
 def shards_by_blocks(

time: 74.5 us -> 74.8 us (level)
  Pallas kernels: 16.8 us -> 25.1 us
  local copies, waits for them, and re-layouts: 6.79 us -> 1.45 us
  other arithmetic: 4.59 us -> 2.61 us
  waiting for transfers between devices: 26.2 us -> 25 us
    pallas_call x2, Pallas kernels: 12.8 us -> 18.6 us  [column_blocks(): pl.pallas_call(column_blocks_kernel, out_shape=jax.ShapeDtypeStruct((coun...]
    unnamed x16 -> x2, local copies, waits for them, and re-layouts: 6.33 us -> 1 us
    pallas_call x1, Pallas kernels: 2.77 us -> 4.9 us  [adapter_output(): pl.pallas_call(adapter_kernel, out_shape=jax.ShapeDtypeStruct((group * bl...]
    concatenate x4, other arithmetic: 2.18 us -> 0.23 us  [pack_scaled(): return jnp.concatenate([scaled, marks], axis=0)]
    ppermute x5, waiting for transfers between devices: 15.2 us -> 14.3 us  [xor_permute(): return lax.ppermute(value, 'tp', [(i, i ^ offset) for i in range(group)])]
  transfers between devices with their start and end apart: 7 -> 7, of which waited for: 2 -> 3; matrix products, arithmetic and copies ran while one was open for 7% -> 4% of each run, Pallas kernels for 12% -> 19%
where the time goes in v4:
time: 74.8 us; the launch traced here: 74.4 us
  Pallas kernels  25.1 us (34%)
  waiting for transfers between devices  25 us (33%)
  starting transfers between devices  19.2 us (26%)
  other arithmetic  2.61 us (3%)
  local copies, waits for them, and re-layouts  1.45 us (2%)
  matrix products  0.88 us (1%)
    pallas_call x2, Pallas kernels, column_blocks(): pl.pallas_call(column_blocks_kernel, out_shape=jax.ShapeDtypeStruct((coun...  18.6 us
    ppermute x5, waiting for transfers between devices, xor_permute(): return lax.ppermute(value, 'tp', [(i, i ^ offset) for i in range(group)])  14.3 us
    all_to_all x1, waiting for transfers between devices, shards_by_blocks(): lax.all_to_all(adapter_out, 'tp', split_axis=0, concat_axis=0, tiled=True)  10.6 us
    ppermute x5, starting transfers between devices, xor_permute(): return lax.ppermute(value, 'tp', [(i, i ^ offset) for i in range(group)])  8.08 us
    all_to_all x1, starting transfers between devices, shards_by_blocks(): lax.all_to_all(packed, 'tp', split_axis=0, concat_axis=0, tiled=True)  6.89 us
    pallas_call x1, Pallas kernels, adapter_output(): pl.pallas_call(adapter_kernel, out_shape=jax.ShapeDtypeStruct((group * bl...  4.9 us
    all_to_all x1, starting transfers between devices, shards_by_blocks(): lax.all_to_all(adapter_out, 'tp', split_axis=0, concat_axis=0, tiled=True)  4.2 us
    pallas_call x1, Pallas kernels, pack_rows(): pl.pallas_call(functools.partial(pack_kernel, blocks, orders), out_shape=...  1.62 us
  transfers between devices with their start and end apart: 7, of which 3 were waited for; matrix products, arithmetic and copies ran while one was open for 4% of the time, Pallas kernels for 19%

profile of v4, /device:TPU:0, one launch (start us, length us, event | category | flops | bytes accessed | tf_op | source)
XLA Modules:
  0.0 74.4 jit_solution(14138370504859212892)
XLA Ops:
  0.0 1.6 %shard_map.64 = (bf16[80,4,1792]{2,1,0:T(4,128)(2,1)S(1)}, bf16[320,96]{1,0:T(8,128)(2,1)S(1)}, s32[16]{0:T(128)S(1)}) custom-call(s32[1]{0:T(128)} %bitcast.me_ref, s32[16]{0:T(128)} %slot_hbm.1, s32[1,96]{1,0:T(1,128)} %bitcast.26, bf16[96,1792]{1,0:T(8,128)(2,1)} %hidden_hbm.5), custom_call_target="tpu_custom_call" | custom-call | tf_op jit(solution)/shard_map/pallas_call | solution.py:161
  1.6 0.0 copy-start
  1.6 1.0 %copy-done = bf16[80,4,1792]{2,1,0:T(4,128)(2,1)} copy-done((bf16[80,4,1792]{2,1,0:T(4,128)(2,1)}, bf16[80,4,1792]{2,1,0:T(4,128)(2,1)S(1)}, u32[]{:S(2)}) %copy-start) | copy-done | bytes 1146904
  2.6 0.1 fusion.9
  2.7 9.2 %shard_map.66 = f32[32,96,128]{2,1,0:T(8,128)S(1)} custom-call(s32[8]{0:T(128)S(1)} %get-tuple-element.25.order_ref, bf16[96,1792]{1,0:T(8,128)(2,1)} %hidden_hbm.5, bf16[1792,8192]{1,0:T(8,128)(2,1)} %down_ref.3), custom_call_target="tpu_custom_call" | custom-call | flops 1000 | bytes 1000 | tf_op jit(solution)/shard_map/pallas_call | solution.py:56
  11.9 0.6 collective-permute-start
  12.6 6.9 %all-to-all-start = ((bf16[80,4,1792]{2,1,0:T(4,128)(2,1)}), bf16[80,4,1792]{2,1,0:T(4,128)(2,1)S(1)}, u32[]{:S(2)}, u32[]{:S(2)}) async-start(bf16[80,4,1792]{2,1,0:T(4,128)(2,1)} %copy-done), calls=%async_computation | async-start | bytes 2293760 | tf_op jit(solution)/shard_map/all_to_all | solution.py:256
  19.5 9.4 %shard_map.65 = f32[32,96,128]{2,1,0:T(8,128)S(1)} custom-call(s32[8]{0:T(128)S(1)} %get-tuple-element.26.order_ref, bf16[96,1792]{1,0:T(8,128)(2,1)} %hidden_hbm.5, bf16[1792,8192]{1,0:T(8,128)(2,1)} %down_ref.3), custom_call_target="tpu_custom_call" | custom-call | flops 1000 | bytes 1000 | tf_op jit(solution)/shard_map/pallas_call | solution.py:56
  28.9 0.0 collective-permute-done
  28.9 1.6 %add.22 = f32[32,96,128]{2,1,0:T(8,128)S(1)} add(f32[32,96,128]{2,1,0:T(8,128)S(1)} %shard_map.65, f32[32,96,128]{2,1,0:T(8,128)} %collective-permute-done) | non-fusion elementwise | flops 393216 | bytes 4718592 | tf_op jit(solution)/shard_map/add | solution.py:96
  30.5 0.1 abs_reduce_fusion
  30.6 0.2 multiply_convert_fusion
  30.8 0.1 broadcast_in_dim.8
  30.9 0.1 pad_maximum_fusion
  31.0 1.9 %collective-permute-start.1 = (f16[17,96,128]{2,1,0:T(8,128)(2,1)S(1)}, f16[17,96,128]{2,1,0:T(8,128)(2,1)S(1)}, u32[]{:S(2)}, u32[]{:S(2)}) collective-permute-start(f16[17,96,128]{2,1,0:T(8,128)(2,1)S(1)} %pad_maximum_fusion), channel_id=1, source_target_pairs={{0,2},{1,3},{2,0},{3,1},{4,6},{5,7},{6,4},{7,5},{8,10},{9,11},{10,... | collective-permute-start | bytes 1253384 | tf_op jit(solution)/shard_map/ppermute | solution.py:22
  32.9 14.0 %collective-permute-done.1 = f16[17,96,128]{2,1,0:T(8,128)(2,1)S(1)} collective-permute-done((f16[17,96,128]{2,1,0:T(8,128)(2,1)S(1)}, f16[17,96,128]{2,1,0:T(8,128)(2,1)S(1)}, u32[]{:S(2)}, u32[]{:S(2)}) %collective-permute-start.1) | collective-permute-done | bytes 417824 | tf_op jit(solution)/shard_map/ppermute | solution.py:22
  46.8 0.1 slice_add_fusion
  46.9 0.2 abs_reduce_fusion.3
  47.1 0.1 multiply_convert_fusion.3
  47.3 0.1 broadcast_in_dim.9
  47.4 2.9 %collective-permute-start.2 = (f16[5,96,128]{2,1,0:T(8,128)(2,1)S(1)}, f16[5,96,128]{2,1,0:T(8,128)(2,1)S(1)}, u32[]{:S(2)}, u32[]{:S(2)}) collective-permute-start(f16[5,96,128]{2,1,0:T(8,128)(2,1)S(1)} %pad_maximum_fusion.1), channel_id=1, source_target_pairs={{0,4},{1,5},{2,6},{3,7},{4,0},{5,1},{6,2},{7,3},{8,12},{9,13},{10,... | collective-permute-start | bytes 368648 | tf_op jit(solution)/shard_map/ppermute | solution.py:22
  50.4 0.1 broadcast_in_dim.10
  50.5 1.1 %collective-permute-start.3 = (f16[5,96,128]{2,1,0:T(8,128)(2,1)S(1)}, f16[5,96,128]{2,1,0:T(8,128)(2,1)S(1)}, u32[]{:S(2)}, u32[]{:S(2)}) collective-permute-start(f16[5,96,128]{2,1,0:T(8,128)(2,1)S(1)} %pad_maximum_fusion.2), channel_id=1, source_target_pairs={{0,8},{1,9},{2,10},{3,11},{4,12},{5,13},{6,14},{7,15},{8,0},{9,1},... | collective-permute-start | bytes 368648 | tf_op jit(solution)/shard_map/ppermute | solution.py:22
  51.6 0.1 broadcast_in_dim.11
  51.7 1.5 %collective-permute-start.4 = (f16[5,96,128]{2,1,0:T(8,128)(2,1)S(1)}, f16[5,96,128]{2,1,0:T(8,128)(2,1)S(1)}, u32[]{:S(2)}, u32[]{:S(2)}) collective-permute-start(f16[5,96,128]{2,1,0:T(8,128)(2,1)S(1)} %pad_maximum_fusion.3), channel_id=1, source_target_pairs={{0,12},{1,13},{2,14},{3,15},{4,8},{5,9},{6,10},{7,11},{8,4},{9,5},... | collective-permute-start | bytes 368648 | tf_op jit(solution)/shard_map/ppermute | solution.py:22
  53.2 0.0 all-to-all-done.rows_ref
  53.2 4.9 %shard_map.67 = bf16[80,4,512]{2,1,0:T(4,128)(2,1)} custom-call(bf16[80,4,1792]{2,1,0:T(4,128)(2,1)S(1)} %all-to-all-done.rows_ref, bf16[64,28672]{1,0:T(8,128)(2,1)} %bitcast.24, bf16[64,8192]{1,0:T(8,128)(2,1)} %bitcast.25), custom_call_target="tpu_custom_call" | custom-call | flops 94371840 | bytes 5865472 | tf_op jit(solution)/shard_map/pallas_call | solution.py:226
  58.1 4.2 %all-to-all-start.1 = ((bf16[80,4,512]{2,1,0:T(4,128)(2,1)}), bf16[80,4,512]{2,1,0:T(4,128)(2,1)S(1)}, u32[]{:S(2)}, u32[]{:S(2)}) async-start(bf16[80,4,512]{2,1,0:T(4,128)(2,1)} %shard_map.67), calls=%async_computation.1 | async-start | bytes 655360 | tf_op jit(solution)/shard_map/all_to_all | solution.py:261
  62.3 0.0 collective-permute-done.2
  62.4 0.4 collective-permute-done.3
  62.8 0.0 collective-permute-done.4
  62.8 10.6 %all-to-all-done.1 = bf16[80,4,512]{2,1,0:T(4,128)(2,1)S(1)} async-done(((bf16[80,4,512]{2,1,0:T(4,128)(2,1)}), bf16[80,4,512]{2,1,0:T(4,128)(2,1)S(1)}, u32[]{:S(2)}, u32[]{:S(2)}) %all-to-all-start.1) | async-done | bytes 327712 | tf_op jit(solution)/shard_map/all_to_all | solution.py:261
  73.4 0.1 reshape.115
  73.5 0.9 %fusion.1 = bf16[96,512]{1,0:T(8,128)(2,1)} fusion(bf16[320,96]{1,0:T(8,128)(2,1)S(1)} %get-tuple-element.9, bf16[320,512]{1,0:T(8,128)(2,1)S(1)} %reshape.115, f32[16,96,128]{2,1,0:T(8,128)S(1)} %slice_add_fusion, f16[5,96,128]{2,1,0:T(8,128)(2,1)S(1)} %collective-permute-done.4, f16[5,96,128]{2,1,0:T(8,128)(2,1)S(1)} %collective-permute-done.3, ...), kind=kOutput, calls=%fused_computation.2 | convolution fusion | flops 32047104 | bytes 1146880 | tf_op jit(solution)/shard_map/dot_general | solution.py:262
  (10 shorter events, 0.2 us)
Async XLA Ops:
  1.6 1.0 %copy-start = (bf16[80,4,1792]{2,1,0:T(4,128)(2,1)}, bf16[80,4,1792]{2,1,0:T(4,128)(2,1)S(1)}, u32[]{:S(2)}) copy-start(bf16[80,4,1792]{2,1,0:T(4,128)(2,1)S(1)} %get-tuple-element.10) | copy-start | bytes 3440644
  11.9 16.9 %collective-permute-start = (f32[32,96,128]{2,1,0:T(8,128)S(1)}, f32[32,96,128]{2,1,0:T(8,128)}, u32[]{:S(2)}, u32[]{:S(2)}) collective-permute-start(f32[32,96,128]{2,1,0:T(8,128)S(1)} %shard_map.66), channel_id=1, source_target_pairs={{0,1},{1,0},{2,3},{3,2},{4,5},{5,4},{6,7},{7,6},{8,9},{9,8},{10,11... | collective-permute-start | bytes 4718600 | tf_op jit(solution)/shard_map/ppermute | solution.py:22
  12.6 40.6 %all-to-all-start = ((bf16[80,4,1792]{2,1,0:T(4,128)(2,1)}), bf16[80,4,1792]{2,1,0:T(4,128)(2,1)S(1)}, u32[]{:S(2)}, u32[]{:S(2)}) async-start(bf16[80,4,1792]{2,1,0:T(4,128)(2,1)} %copy-done), calls=%async_computation | async-start | bytes 2293760 | tf_op jit(solution)/shard_map/all_to_all | solution.py:256
  31.0 15.8 %collective-permute-start.1 = (f16[17,96,128]{2,1,0:T(8,128)(2,1)S(1)}, f16[17,96,128]{2,1,0:T(8,128)(2,1)S(1)}, u32[]{:S(2)}, u32[]{:S(2)}) collective-permute-start(f16[17,96,128]{2,1,0:T(8,128)(2,1)S(1)} %pad_maximum_fusion), channel_id=1, source_target_pairs={{0,2},{1,3},{2,0},{3,1},{4,6},{5,7},{6,4},{7,5},{8,10},{9,11},{10,... | collective-permute-start | bytes 1253384 | tf_op jit(solution)/shard_map/ppermute | solution.py:22
  47.4 14.9 %collective-permute-start.2 = (f16[5,96,128]{2,1,0:T(8,128)(2,1)S(1)}, f16[5,96,128]{2,1,0:T(8,128)(2,1)S(1)}, u32[]{:S(2)}, u32[]{:S(2)}) collective-permute-start(f16[5,96,128]{2,1,0:T(8,128)(2,1)S(1)} %pad_maximum_fusion.1), channel_id=1, source_target_pairs={{0,4},{1,5},{2,6},{3,7},{4,0},{5,1},{6,2},{7,3},{8,12},{9,13},{10,... | collective-permute-start | bytes 368648 | tf_op jit(solution)/shard_map/ppermute | solution.py:22
  50.5 12.3 %collective-permute-start.3 = (f16[5,96,128]{2,1,0:T(8,128)(2,1)S(1)}, f16[5,96,128]{2,1,0:T(8,128)(2,1)S(1)}, u32[]{:S(2)}, u32[]{:S(2)}) collective-permute-start(f16[5,96,128]{2,1,0:T(8,128)(2,1)S(1)} %pad_maximum_fusion.2), channel_id=1, source_target_pairs={{0,8},{1,9},{2,10},{3,11},{4,12},{5,13},{6,14},{7,15},{8,0},{9,1},... | collective-permute-start | bytes 368648 | tf_op jit(solution)/shard_map/ppermute | solution.py:22
  51.7 11.1 %collective-permute-start.4 = (f16[5,96,128]{2,1,0:T(8,128)(2,1)S(1)}, f16[5,96,128]{2,1,0:T(8,128)(2,1)S(1)}, u32[]{:S(2)}, u32[]{:S(2)}) collective-permute-start(f16[5,96,128]{2,1,0:T(8,128)(2,1)S(1)} %pad_maximum_fusion.3), channel_id=1, source_target_pairs={{0,12},{1,13},{2,14},{3,15},{4,8},{5,9},{6,10},{7,11},{8,4},{9,5},... | collective-permute-start | bytes 368648 | tf_op jit(solution)/shard_map/ppermute | solution.py:22
  58.1 15.3 %all-to-all-start.1 = ((bf16[80,4,512]{2,1,0:T(4,128)(2,1)}), bf16[80,4,512]{2,1,0:T(4,128)(2,1)S(1)}, u32[]{:S(2)}, u32[]{:S(2)}) async-start(bf16[80,4,512]{2,1,0:T(4,128)(2,1)} %shard_map.67), calls=%async_computation.1 | async-start | bytes 655360 | tf_op jit(solution)/shard_map/all_to_all | solution.py:261

commit v5 on v4

--- a/solution.py
+++ b/solution.py
@@ -12,6 +12,7 @@
 MOST = 20
 LANES = 128
 F16_TOP = 14.0
+IN_FLIGHT = 3
 
 
 def in_hbm(value):
@@ -37,13 +38,16 @@
 
     hidden_copy = pltpu.make_async_copy(hidden_hbm, hidden_ref, hidden_sem)
     hidden_copy.start()
-    for block in range(count):
+    for block in range(min(IN_FLIGHT, count)):
         for piece in range(pieces):
             copy(block, piece).start()
     hidden_copy.wait()
     for block in range(count):
         for piece in range(pieces):
             copy(block, piece).wait()
+        if block + IN_FLIGHT < count:
+            for piece in range(pieces):
+                copy(block + IN_FLIGHT, piece).start()
         product = jnp.dot(hidden_ref[...], held_ref[block], preferred_element_type=jnp.float32)
         for lane in range(parts):
             out_ref[block * parts + lane] = product[:, lane * LANES : (lane + 1) * LANES]
@@ -86,21 +90,35 @@
     return packed[:-1].astype(jnp.float32) * jnp.exp2(exponent - F16_TOP)
 
 
+def chip_sums(hidden, down_matrix, group, order, width):
+    def work():
+        odd = column_blocks(hidden, down_matrix, order[: group // 2], width)
+        odd_in = xor_permute(odd, group, 1)
+        even = column_blocks(hidden, down_matrix, order[group // 2 :], width)
+        chip = even + odd_in
+        half = chip.shape[0] // 2
+        return chip[:half], pack_scaled(chip[half:])
+
+    def idle():
+        rows = hidden.shape[0]
+        half = group * width // LANES // 4
+        return (
+            jnp.zeros((half, rows, LANES), jnp.float32),
+            jnp.zeros((half + 1, rows, LANES), jnp.float16),
+        )
+
+    return lax.cond(order[0] >= 0, work, idle)
+
+
 def base_blocks(hidden, down_matrix, group, order, width):
     rows = hidden.shape[0]
     parts = width // LANES
-    quads = list(range(0, group, 4))
-    odd = column_blocks(hidden, down_matrix, order[: group // 2], width)
-    odd_in = xor_permute(odd, group, 1)
-    even = column_blocks(hidden, down_matrix, order[group // 2 :], width)
-    chip = even + odd_in
-    half = len(quads) * parts
-    pair_in = xor_permute(pack_scaled(chip[half:]), group, 2)
-    pair = chip[:half] + unpack_scaled(pair_in)
+    kept, sent = chip_sums(hidden, down_matrix, group, order, width)
+    pair = kept + unpack_scaled(xor_permute(sent, group, 2))
     total = pair[:parts]
     arrived = [
-        xor_permute(pack_scaled(pair[i * parts : (i + 1) * parts]), group, quads[i])
-        for i in range(1, len(quads))
+        xor_permute(pack_scaled(pair[i * parts : (i + 1) * parts]), group, 4 * i)
+        for i in range(1, group // 4)
     ]
     for packed in arrived:
         total = total + unpack_scaled(packed)

time: 74.8 us -> 69.7 us (0.932)
  Pallas kernels: 25.1 us -> 22.2 us
  other arithmetic: 2.61 us -> 1.27 us
  local copies, waits for them, and re-layouts: 1.45 us -> 0.46 us
  waiting for transfers between devices: 25 us -> 24.2 us
    pallas_call x2, Pallas kernels: 18.6 us -> 14.9 us  [column_blocks(): pl.pallas_call(column_blocks_kernel, out_shape=jax.ShapeDtypeStruct((coun...]
    all_to_all x1, starting transfers between devices: 4.2 us -> 5.71 us  [shards_by_blocks(): lax.all_to_all(adapter_out, 'tp', split_axis=0, concat_axis=0, tiled=True)]
    add x2, other arithmetic: 1.7 us -> 0.29 us  [the longest x1 0.19 us: work(): chip = even + odd_in]
    ppermute x5, starting transfers between devices: 8.08 us -> 6.8 us  [xor_permute(): return lax.ppermute(value, 'tp', [(i, i ^ offset) for i in range(group)])]
    ppermute x5, waiting for transfers between devices: 14.3 us -> 13.2 us  [xor_permute(): return lax.ppermute(value, 'tp', [(i, i ^ offset) for i in range(group)])]
    unnamed x2 -> x0, local copies, waits for them, and re-layouts: 1 us -> none
    pallas_call x1, Pallas kernels: 1.62 us -> 2.47 us  [pack_rows(): pl.pallas_call(functools.partial(pack_kernel, blocks, orders), out_shape=...]
  transfers between devices with their start and end apart: 7 -> 7, of which waited for: 3 -> 2; matrix products, arithmetic and copies ran while one was open for 4% -> 2% of each run, Pallas kernels for 19% -> 29%
where the time goes in v5:
time: 69.7 us; the launch traced here: 69.2 us
  waiting for transfers between devices  24.2 us (35%)
  Pallas kernels  22.2 us (32%)
  starting transfers between devices  19.9 us (29%)
  other arithmetic  1.27 us (2%)
  matrix products  0.88 us (1%)
    pallas_call x2, Pallas kernels, column_blocks(): pl.pallas_call(column_blocks_kernel, out_shape=jax.ShapeDtypeStruct((coun...  14.9 us
    ppermute x5, waiting for transfers between devices, xor_permute(): return lax.ppermute(value, 'tp', [(i, i ^ offset) for i in range(group)])  13.2 us
    all_to_all x1, waiting for transfers between devices, shards_by_blocks(): lax.all_to_all(adapter_out, 'tp', split_axis=0, concat_axis=0, tiled=True)  11 us
    all_to_all x1, starting transfers between devices, shards_by_blocks(): lax.all_to_all(packed, 'tp', split_axis=0, concat_axis=0, tiled=True)  7.37 us
    ppermute x5, starting transfers between devices, xor_permute(): return lax.ppermute(value, 'tp', [(i, i ^ offset) for i in range(group)])  6.8 us
    all_to_all x1, starting transfers between devices, shards_by_blocks(): lax.all_to_all(adapter_out, 'tp', split_axis=0, concat_axis=0, tiled=True)  5.71 us
    pallas_call x1, Pallas kernels, adapter_output(): pl.pallas_call(adapter_kernel, out_shape=jax.ShapeDtypeStruct((group * bl...  4.9 us
    pallas_call x1, Pallas kernels, pack_rows(): pl.pallas_call(functools.partial(pack_kernel, blocks, orders), out_shape=...  2.47 us
  transfers between devices with their start and end apart: 7, of which 2 were waited for; matrix products, arithmetic and copies ran while one was open for 2% of the time, Pallas kernels for 29%

profile of v5, /device:TPU:0, one launch (start us, length us, event | category | flops | bytes accessed | tf_op | source)
XLA Modules:
  0.0 69.2 jit_solution(16594268585452255108)
XLA Ops:
  0.0 2.5 %shard_map.65 = (bf16[80,4,1792]{2,1,0:T(4,128)(2,1)}, bf16[320,96]{1,0:T(8,128)(2,1)S(1)}, s32[16]{0:T(128)S(1)}) custom-call(s32[1]{0:T(128)} %bitcast.me_ref, s32[16]{0:T(128)} %slot_hbm.1, s32[1,96]{1,0:T(1,128)} %bitcast.29, bf16[96,1792]{1,0:T(8,128)(2,1)} %hidden_hbm.1), custom_call_target="tpu_custom_call" | custom-call | tf_op jit(solution)/shard_map/pallas_call | solution.py:179
  2.5 7.4 %all-to-all-start = ((bf16[80,4,1792]{2,1,0:T(4,128)(2,1)}), bf16[80,4,1792]{2,1,0:T(4,128)(2,1)S(1)}, u32[]{:S(2)}, u32[]{:S(2)}) async-start(bf16[80,4,1792]{2,1,0:T(4,128)(2,1)} %get-tuple-element.23), calls=%async_computation | async-start | bytes 2293760 | tf_op jit(solution)/shard_map/all_to_all | solution.py:274
  9.9 16.2 %conditional.1 = (f32[16,96,128]{2,1,0:T(8,128)S(1)}, f16[17,96,128]{2,1,0:T(8,128)(2,1)S(1)}) conditional(s32[]{:T(128)} %bitcast.2, () %tuple.13, (s32[16]{0:T(128)S(1)}, bf16[96,1792]{1,0:T(8,128)(2,1)}, bf16[1792,8192]{1,0:T(8,128)(2,1)}) %tuple.14), branch_computations={%region_0.0_spmd, %region_1.0_spmd} | conditional | flops 1391024 | bytes 15413256 | solution.py:110
  9.9 0.1 fusion.9
  10.0 7.4 %branch_1_fun.3 = f32[32,96,128]{2,1,0:T(8,128)S(1)} custom-call(s32[8]{0:T(128)S(1)} %get-tuple-element.33.order_ref, bf16[96,1792]{1,0:T(8,128)(2,1)} %get-tuple-element.12.hidden_hbm, bf16[1792,8192]{1,0:T(8,128)(2,1)} %get-tuple-element.25.down_ref), custom_call_target="tpu_custom_call" | custom-call | flops 1000 | bytes 1000 | tf_op jit(solution)/shard_map/cond/branch_1_fun/pallas_call | solution.py:60
  17.4 0.5 collective-permute-start
  17.9 7.4 %branch_1_fun.2 = f32[32,96,128]{2,1,0:T(8,128)S(1)} custom-call(s32[8]{0:T(128)S(1)} %get-tuple-element.34.order_ref, bf16[96,1792]{1,0:T(8,128)(2,1)} %get-tuple-element.12.hidden_hbm, bf16[1792,8192]{1,0:T(8,128)(2,1)} %get-tuple-element.25.down_ref), custom_call_target="tpu_custom_call" | custom-call | flops 1000 | bytes 1000 | tf_op jit(solution)/shard_map/cond/branch_1_fun/pallas_call | solution.py:60
  25.3 0.0 collective-permute-done
  25.4 0.2 add.16
  25.6 0.1 abs_reduce_fusion
  25.7 0.2 multiply_convert_fusion
  25.9 0.1 broadcast_in_dim.8
  26.0 0.1 pad_maximum_fusion
  26.1 1.7 %collective-permute-start.1 = (f16[17,96,128]{2,1,0:T(8,128)(2,1)S(1)}, f16[17,96,128]{2,1,0:T(8,128)(2,1)S(1)}, u32[]{:S(2)}, u32[]{:S(2)}) collective-permute-start(f16[17,96,128]{2,1,0:T(8,128)(2,1)S(1)} %get-tuple-element.21), channel_id=1, source_target_pairs={{0,2},{1,3},{2,0},{3,1},{4,6},{5,7},{6,4},{7,5},{8,10},{9,11},{10,... | collective-permute-start | bytes 1253384 | tf_op jit(solution)/shard_map/ppermute | solution.py:23
  27.9 13.2 %collective-permute-done.1 = f16[17,96,128]{2,1,0:T(8,128)(2,1)S(1)} collective-permute-done((f16[17,96,128]{2,1,0:T(8,128)(2,1)S(1)}, f16[17,96,128]{2,1,0:T(8,128)(2,1)S(1)}, u32[]{:S(2)}, u32[]{:S(2)}) %collective-permute-start.1) | collective-permute-done | bytes 417824 | tf_op jit(solution)/shard_map/ppermute | solution.py:23
  41.1 0.1 multiply_add_fusion
  41.2 0.2 abs_reduce_fusion.3
  41.4 0.1 multiply_convert_fusion.3
  41.6 0.1 broadcast_in_dim.12
  41.7 2.1 %collective-permute-start.2 = (f16[5,96,128]{2,1,0:T(8,128)(2,1)S(1)}, f16[5,96,128]{2,1,0:T(8,128)(2,1)S(1)}, u32[]{:S(2)}, u32[]{:S(2)}) collective-permute-start(f16[5,96,128]{2,1,0:T(8,128)(2,1)S(1)} %pad_maximum_fusion.1), channel_id=1, source_target_pairs={{0,4},{1,5},{2,6},{3,7},{4,0},{5,1},{6,2},{7,3},{8,12},{9,13},{10,... | collective-permute-start | bytes 368648 | tf_op jit(solution)/shard_map/ppermute | solution.py:23
  43.8 0.1 broadcast_in_dim.13
  43.9 1.1 %collective-permute-start.3 = (f16[5,96,128]{2,1,0:T(8,128)(2,1)S(1)}, f16[5,96,128]{2,1,0:T(8,128)(2,1)S(1)}, u32[]{:S(2)}, u32[]{:S(2)}) collective-permute-start(f16[5,96,128]{2,1,0:T(8,128)(2,1)S(1)} %pad_maximum_fusion.2), channel_id=1, source_target_pairs={{0,8},{1,9},{2,10},{3,11},{4,12},{5,13},{6,14},{7,15},{8,0},{9,1},... | collective-permute-start | bytes 368648 | tf_op jit(solution)/shard_map/ppermute | solution.py:23
  45.0 0.1 broadcast_in_dim.14
  45.1 1.5 %collective-permute-start.4 = (f16[5,96,128]{2,1,0:T(8,128)(2,1)S(1)}, f16[5,96,128]{2,1,0:T(8,128)(2,1)S(1)}, u32[]{:S(2)}, u32[]{:S(2)}) collective-permute-start(f16[5,96,128]{2,1,0:T(8,128)(2,1)S(1)} %pad_maximum_fusion.3), channel_id=1, source_target_pairs={{0,12},{1,13},{2,14},{3,15},{4,8},{5,9},{6,10},{7,11},{8,4},{9,5},... | collective-permute-start | bytes 368648 | tf_op jit(solution)/shard_map/ppermute | solution.py:23
  46.5 0.0 all-to-all-done.rows_ref
  46.5 4.9 %shard_map.66 = bf16[80,4,512]{2,1,0:T(4,128)(2,1)} custom-call(bf16[80,4,1792]{2,1,0:T(4,128)(2,1)S(1)} %all-to-all-done.rows_ref, bf16[64,28672]{1,0:T(8,128)(2,1)} %bitcast.26, bf16[64,8192]{1,0:T(8,128)(2,1)} %bitcast.27), custom_call_target="tpu_custom_call" | custom-call | flops 94371840 | bytes 5865472 | tf_op jit(solution)/shard_map/pallas_call | solution.py:244
  51.4 5.7 %all-to-all-start.1 = ((bf16[80,4,512]{2,1,0:T(4,128)(2,1)}), bf16[80,4,512]{2,1,0:T(4,128)(2,1)S(1)}, u32[]{:S(2)}, u32[]{:S(2)}) async-start(bf16[80,4,512]{2,1,0:T(4,128)(2,1)} %shard_map.66), calls=%async_computation.1 | async-start | bytes 655360 | tf_op jit(solution)/shard_map/all_to_all | solution.py:279
  57.2 0.0 collective-permute-done.2
  57.2 0.0 collective-permute-done.3
  57.2 0.0 collective-permute-done.4
  57.3 11.0 %all-to-all-done.1 = bf16[80,4,512]{2,1,0:T(4,128)(2,1)S(1)} async-done(((bf16[80,4,512]{2,1,0:T(4,128)(2,1)}), bf16[80,4,512]{2,1,0:T(4,128)(2,1)S(1)}, u32[]{:S(2)}, u32[]{:S(2)}) %all-to-all-start.1) | async-done | bytes 327712 | tf_op jit(solution)/shard_map/all_to_all | solution.py:279
  68.3 0.1 reshape.119
  68.3 0.9 %fusion.2 = bf16[96,512]{1,0:T(8,128)(2,1)} fusion(bf16[320,96]{1,0:T(8,128)(2,1)S(1)} %get-tuple-element.22, bf16[320,512]{1,0:T(8,128)(2,1)S(1)} %reshape.119, f32[16,96,128]{2,1,0:T(8,128)S(1)} %multiply_add_fusion, f16[5,96,128]{2,1,0:T(8,128)(2,1)S(1)} %collective-permute-done.4, f16[5,96,128]{2,1,0:T(8,128)(2,1)S(1)} %collective-permute-done.3, ...), kind=kOutput, calls=%fused_computation.8 | convolution fusion | flops 32047104 | bytes 1146880 | tf_op jit(solution)/shard_map/dot_general | solution.py:280
  (10 shorter events, 0.2 us)
Async XLA Ops:
  2.5 44.1 %all-to-all-start = ((bf16[80,4,1792]{2,1,0:T(4,128)(2,1)}), bf16[80,4,1792]{2,1,0:T(4,128)(2,1)S(1)}, u32[]{:S(2)}, u32[]{:S(2)}) async-start(bf16[80,4,1792]{2,1,0:T(4,128)(2,1)} %get-tuple-element.23), calls=%async_computation | async-start | bytes 2293760 | tf_op jit(solution)/shard_map/all_to_all | solution.py:274
  17.4 7.9 %collective-permute-start = (f32[32,96,128]{2,1,0:T(8,128)S(1)}, f32[32,96,128]{2,1,0:T(8,128)S(1)}, u32[]{:S(2)}, u32[]{:S(2)}) collective-permute-start(f32[32,96,128]{2,1,0:T(8,128)S(1)} %branch_1_fun.3), channel_id=1, source_target_pairs={{0,1},{1,0},{2,3},{3,2},{4,5},{5,4},{6,7},{7,6},{8,9},{9,8},{10,11... | collective-permute-start | bytes 4718600 | tf_op jit(solution)/shard_map/cond/branch_1_fun/ppermute | solution.py:23
  26.1 15.0 %collective-permute-start.1 = (f16[17,96,128]{2,1,0:T(8,128)(2,1)S(1)}, f16[17,96,128]{2,1,0:T(8,128)(2,1)S(1)}, u32[]{:S(2)}, u32[]{:S(2)}) collective-permute-start(f16[17,96,128]{2,1,0:T(8,128)(2,1)S(1)} %get-tuple-element.21), channel_id=1, source_target_pairs={{0,2},{1,3},{2,0},{3,1},{4,6},{5,7},{6,4},{7,5},{8,10},{9,11},{10,... | collective-permute-start | bytes 1253384 | tf_op jit(solution)/shard_map/ppermute | solution.py:23
  41.7 15.5 %collective-permute-start.2 = (f16[5,96,128]{2,1,0:T(8,128)(2,1)S(1)}, f16[5,96,128]{2,1,0:T(8,128)(2,1)S(1)}, u32[]{:S(2)}, u32[]{:S(2)}) collective-permute-start(f16[5,96,128]{2,1,0:T(8,128)(2,1)S(1)} %pad_maximum_fusion.1), channel_id=1, source_target_pairs={{0,4},{1,5},{2,6},{3,7},{4,0},{5,1},{6,2},{7,3},{8,12},{9,13},{10,... | collective-permute-start | bytes 368648 | tf_op jit(solution)/shard_map/ppermute | solution.py:23
  43.9 13.3 %collective-permute-start.3 = (f16[5,96,128]{2,1,0:T(8,128)(2,1)S(1)}, f16[5,96,128]{2,1,0:T(8,128)(2,1)S(1)}, u32[]{:S(2)}, u32[]{:S(2)}) collective-permute-start(f16[5,96,128]{2,1,0:T(8,128)(2,1)S(1)} %pad_maximum_fusion.2), channel_id=1, source_target_pairs={{0,8},{1,9},{2,10},{3,11},{4,12},{5,13},{6,14},{7,15},{8,0},{9,1},... | collective-permute-start | bytes 368648 | tf_op jit(solution)/shard_map/ppermute | solution.py:23
  45.1 12.2 %collective-permute-start.4 = (f16[5,96,128]{2,1,0:T(8,128)(2,1)S(1)}, f16[5,96,128]{2,1,0:T(8,128)(2,1)S(1)}, u32[]{:S(2)}, u32[]{:S(2)}) collective-permute-start(f16[5,96,128]{2,1,0:T(8,128)(2,1)S(1)} %pad_maximum_fusion.3), channel_id=1, source_target_pairs={{0,12},{1,13},{2,14},{3,15},{4,8},{5,9},{6,10},{7,11},{8,4},{9,5},... | collective-permute-start | bytes 368648 | tf_op jit(solution)/shard_map/ppermute | solution.py:23
  51.4 16.8 %all-to-all-start.1 = ((bf16[80,4,512]{2,1,0:T(4,128)(2,1)}), bf16[80,4,512]{2,1,0:T(4,128)(2,1)S(1)}, u32[]{:S(2)}, u32[]{:S(2)}) async-start(bf16[80,4,512]{2,1,0:T(4,128)(2,1)} %shard_map.66), calls=%async_computation.1 | async-start | bytes 655360 | tf_op jit(solution)/shard_map/all_to_all | solution.py:279

commit v6 on v5

--- a/solution.py
+++ b/solution.py
@@ -12,7 +12,6 @@
 MOST = 20
 LANES = 128
 F16_TOP = 14.0
-IN_FLIGHT = 3
 
 
 def in_hbm(value):
@@ -23,7 +22,7 @@
     return lax.ppermute(value, "tp", [(i, i ^ offset) for i in range(group)])
 
 
-def column_blocks_kernel(order_ref, hidden_hbm, down_ref, out_ref, hidden_ref, held_ref, hidden_sem, sems):
+def column_blocks_kernel(order_ref, hidden_ref, down_ref, out_ref, held_ref, sems):
     count, depth, width = held_ref.shape
     parts = width // LANES
     pieces = sems.shape[1]
@@ -36,18 +35,12 @@
             down_ref.at[lines, pl.ds(start, width)], held_ref.at[block, lines], sems.at[block, piece]
         )
 
-    hidden_copy = pltpu.make_async_copy(hidden_hbm, hidden_ref, hidden_sem)
-    hidden_copy.start()
-    for block in range(min(IN_FLIGHT, count)):
+    for block in range(count):
         for piece in range(pieces):
             copy(block, piece).start()
-    hidden_copy.wait()
     for block in range(count):
         for piece in range(pieces):
             copy(block, piece).wait()
-        if block + IN_FLIGHT < count:
-            for piece in range(pieces):
-                copy(block + IN_FLIGHT, piece).start()
         product = jnp.dot(hidden_ref[...], held_ref[block], preferred_element_type=jnp.float32)
         for lane in range(parts):
             out_ref[block * parts + lane] = product[:, lane * LANES : (lane + 1) * LANES]
@@ -57,24 +50,23 @@
     rows, depth = hidden.shape
     count = order.shape[0]
     pieces = 2 if depth % 32 == 0 else 1
+    vmem = pl.BlockSpec(memory_space=pltpu.VMEM)
     return pl.pallas_call(
         column_blocks_kernel,
         out_shape=jax.ShapeDtypeStruct((count * width // LANES, rows, LANES), jnp.float32),
         in_specs=[
             pl.BlockSpec(memory_space=pltpu.SMEM),
-            pl.BlockSpec(memory_space=pltpu.HBM),
-            pl.BlockSpec(memory_space=pltpu.HBM),
+            vmem,
+            pl.BlockSpec(memory_space=pl.ANY),
         ],
-        out_specs=pl.BlockSpec(memory_space=pltpu.VMEM),
+        out_specs=vmem,
         scratch_shapes=[
-            pltpu.VMEM((rows, depth), jnp.bfloat16),
             pltpu.VMEM((count, depth, width), jnp.bfloat16),
-            pltpu.SemaphoreType.DMA,
             pltpu.SemaphoreType.DMA((count, pieces)),
         ],
         compiler_params=pltpu.CompilerParams(vmem_limit_bytes=40 * 2**20),
         cost_estimate=pl.CostEstimate(flops=1000, bytes_accessed=1000, transcendentals=0),
-    )(order, in_hbm(hidden), in_hbm(down_matrix))
+    )(order, hidden, in_hbm(down_matrix))
 
 
 def pack_scaled(value):
@@ -110,19 +102,25 @@
     return lax.cond(order[0] >= 0, work, idle)
 
 
-def base_blocks(hidden, down_matrix, group, order, width):
-    rows = hidden.shape[0]
+def line_sums(kept, pair_in, flag, group, width):
+    rows = kept.shape[1]
     parts = width // LANES
-    kept, sent = chip_sums(hidden, down_matrix, group, order, width)
-    pair = kept + unpack_scaled(xor_permute(sent, group, 2))
-    total = pair[:parts]
-    arrived = [
-        xor_permute(pack_scaled(pair[i * parts : (i + 1) * parts]), group, 4 * i)
-        for i in range(1, group // 4)
-    ]
-    for packed in arrived:
-        total = total + unpack_scaled(packed)
-    return jnp.transpose(total, (1, 0, 2)).reshape(rows, width)
+
+    def work():
+        pair = kept + unpack_scaled(pair_in)
+        total = pair[:parts]
+        arrived = [
+            xor_permute(pack_scaled(pair[i * parts : (i + 1) * parts]), group, 4 * i)
+            for i in range(1, group // 4)
+        ]
+        for packed in arrived:
+            total = total + unpack_scaled(packed)
+        return total
+
+    def idle():
+        return jnp.zeros((parts, rows, LANES), jnp.float32)
+
+    return lax.cond(flag >= 0, work, idle)
 
 
 def pack_kernel(
@@ -135,6 +133,7 @@
     packed_ref,
     pick_ref,
     order_ref,
+    kept_ref,
     slot_ref,
     adapter_ref,
     hidden_ref,
@@ -167,6 +166,7 @@
     copies[2].wait()
     packed = jnp.dot(pick, hidden_ref[...], preferred_element_type=jnp.float32)
     packed_ref[...] = packed.astype(jnp.bfloat16).reshape(packed_ref.shape)
+    kept_ref[...] = hidden_ref[...]
 
 
 def pack_rows(hidden, adapter_of_row, adapter_holder_slot, me, orders):
@@ -182,9 +182,10 @@
             jax.ShapeDtypeStruct((group * blocks, BLOCK, depth), jnp.bfloat16),
             jax.ShapeDtypeStruct((group * MOST, rows), jnp.bfloat16),
             jax.ShapeDtypeStruct((len(orders),), jnp.int32),
+            jax.ShapeDtypeStruct((rows, depth), jnp.bfloat16),
         ),
         in_specs=[smem, anywhere, anywhere, anywhere],
-        out_specs=(vmem, vmem, smem),
+        out_specs=(vmem, vmem, smem, vmem),
         scratch_shapes=[
             pltpu.SMEM((group,), jnp.int32),
             pltpu.VMEM((1, rows), jnp.int32),
@@ -195,8 +196,9 @@
     )(me.reshape(1), in_hbm(adapter_holder_slot), in_hbm(adapter_of_row.reshape(1, rows)), in_hbm(hidden))
 
 
-def adapter_kernel(rows_ref, shrink_ref, expand_ref, out_ref, total_ref):
+def adapter_kernel(rows_ref, shrink_ref, expand_ref, out_ref, flag_ref, total_ref):
     step = pl.program_id(0)
+    flag_ref[0] = step
     block, depth = rows_ref.shape[1:]
     blocks = MOST // BLOCK
     sources = rows_ref.shape[0] // blocks
@@ -243,14 +245,20 @@
     sources = group // steps
     return pl.pallas_call(
         adapter_kernel,
-        out_shape=jax.ShapeDtypeStruct((group * blocks, BLOCK, width), jnp.bfloat16),
+        out_shape=(
+            jax.ShapeDtypeStruct((group * blocks, BLOCK, width), jnp.bfloat16),
+            jax.ShapeDtypeStruct((1,), jnp.int32),
+        ),
         grid=(steps,),
         in_specs=[
             pl.BlockSpec((sources * blocks, BLOCK, depth), lambda i: (i, 0, 0)),
             pl.BlockSpec((rank, sources * depth), lambda i: (0, i)),
             pl.BlockSpec((rank, model_width), lambda i: (0, 0)),
         ],
-        out_specs=pl.BlockSpec((group * blocks, BLOCK, width), lambda i: (0, 0, 0)),
+        out_specs=(
+            pl.BlockSpec((group * blocks, BLOCK, width), lambda i: (0, 0, 0)),
+            pl.BlockSpec(memory_space=pltpu.SMEM),
+        ),
         scratch_shapes=[pltpu.VMEM((MOST, rank), jnp.float32)],
         compiler_params=pltpu.CompilerParams(vmem_limit_bytes=32 * 2**20),
         cost_estimate=pl.CostEstimate(
@@ -258,7 +266,7 @@
             bytes_accessed=2 * rank * (hidden_width + model_width) + 2 * MOST * hidden_width,
             transcendentals=0,
         ),
-    )(gathered, in_hbm(shrink), in_hbm(expand))
+    )(gathered, shrink, expand)
 
 
 def shards_by_blocks(
@@ -270,13 +278,18 @@
     width = down_matrix.shape[1] // group
     quads = list(range(0, group, 4))
     orders = [q + k for k in (1, 3, 0, 2) for q in quads]
-    packed, pick, order = pack_rows(hidden, adapter_of_row, adapter_holder_slot, me, orders)
+    packed, pick, order, kept_hidden = pack_rows(
+        hidden, adapter_of_row, adapter_holder_slot, me, orders
+    )
     gathered = lax.all_to_all(packed, "tp", split_axis=0, concat_axis=0, tiled=True)
-    base = base_blocks(hidden, down_matrix, group, order, width)
+    kept, sent = chip_sums(kept_hidden, down_matrix, group, order, width)
+    pair_in = xor_permute(sent, group, 2)
     shrink = jnp.swapaxes(shrink_matrices, 1, 2)[0]
     expand = jnp.swapaxes(expand_matrices, 1, 2)[0]
-    adapter_out = adapter_output(gathered, shrink, expand, group)
+    adapter_out, flag = adapter_output(gathered, shrink, expand, group)
     adapter_in = lax.all_to_all(adapter_out, "tp", split_axis=0, concat_axis=0, tiled=True)
+    total = line_sums(kept, pair_in, flag[0], group, width)
+    base = jnp.transpose(total, (1, 0, 2)).reshape(rows, width)
     adapter_rows = lax.dot_general(
         pick,
         adapter_in.reshape(group * MOST, width),

time: 69.7 us -> 89.1 us (1.28)
  blocking collectives: 0 us -> 36.2 us
  starting transfers between devices: 19.9 us -> 10.2 us
  waiting for transfers between devices: 24.2 us -> 19.2 us
  Pallas kernels: 22.2 us -> 17.4 us
  local copies, waits for them, and re-layouts: 0.46 us -> 2.5 us
    all_to_all x0 -> x1, blocking collectives: none -> 36.2 us  [shards_by_blocks(): lax.all_to_all(packed, 'tp', split_axis=0, concat_axis=0, tiled=True)]
    all_to_all x1, waiting for transfers between devices: 11 us -> 0.01 us  [shards_by_blocks(): lax.all_to_all(adapter_out, 'tp', split_axis=0, concat_axis=0, tiled=True)]
    all_to_all x1 -> x0, starting transfers between devices: 7.37 us -> none  [shards_by_blocks(): lax.all_to_all(packed, 'tp', split_axis=0, concat_axis=0, tiled=True)]
    ppermute x5, waiting for transfers between devices: 13.2 us -> 19.2 us  [xor_permute(): return lax.ppermute(value, 'tp', [(i, i ^ offset) for i in range(group)])]
    all_to_all x1, starting transfers between devices: 5.71 us -> 3.55 us  [shards_by_blocks(): lax.all_to_all(adapter_out, 'tp', split_axis=0, concat_axis=0, tiled=True)]
    pallas_call x2, Pallas kernels: 14.9 us -> 12.8 us  [column_blocks(): pl.pallas_call(column_blocks_kernel, out_shape=jax.ShapeDtypeStruct((coun...]
    unnamed x0 -> x4, local copies, waits for them, and re-layouts: none -> 2.04 us
    pallas_call x1, Pallas kernels: 4.9 us -> 2.86 us  [adapter_output(): pl.pallas_call(adapter_kernel, out_shape=(jax.ShapeDtypeStruct((group * b...]
  transfers between devices with their start and end apart: 7 -> 6, of which waited for: 2 -> 3; matrix products, arithmetic and copies ran while one was open for 2% -> 2% of each run, Pallas kernels for 29% -> 14%
where the time goes in v6:
time: 89.1 us; the launch traced here: 88.8 us
  blocking collectives  36.2 us (41%)
  waiting for transfers between devices  19.2 us (22%)
  Pallas kernels  17.4 us (20%)
  starting transfers between devices  10.2 us (11%)
  local copies, waits for them, and re-layouts  2.5 us (3%)
  other arithmetic  1.38 us (2%)
    all_to_all x1, blocking collectives, shards_by_blocks(): lax.all_to_all(packed, 'tp', split_axis=0, concat_axis=0, tiled=True)  36.2 us
    ppermute x5, waiting for transfers between devices, xor_permute(): return lax.ppermute(value, 'tp', [(i, i ^ offset) for i in range(group)])  19.2 us
    pallas_call x2, Pallas kernels, column_blocks(): pl.pallas_call(column_blocks_kernel, out_shape=jax.ShapeDtypeStruct((coun...  12.8 us
    ppermute x5, starting transfers between devices, xor_permute(): return lax.ppermute(value, 'tp', [(i, i ^ offset) for i in range(group)])  6.69 us
    all_to_all x1, starting transfers between devices, shards_by_blocks(): lax.all_to_all(adapter_out, 'tp', split_axis=0, concat_axis=0, tiled=True)  3.55 us
    pallas_call x1, Pallas kernels, adapter_output(): pl.pallas_call(adapter_kernel, out_shape=(jax.ShapeDtypeStruct((group * b...  2.86 us
    unnamed x4, local copies, waits for them, and re-layouts  2.04 us
  transfers between devices with their start and end apart: 6, of which 3 were waited for; matrix products, arithmetic and copies ran while one was open for 2% of the time, Pallas kernels for 14%

profile of v6, /device:TPU:0, one launch (start us, length us, event | category | flops | bytes accessed | tf_op | source)
XLA Modules:
  0.0 88.8 jit_solution(7839868142855723480)
XLA Ops:
  0.0 0.0 copy-start.1
  0.0 1.7 %shard_map.65 = (bf16[80,4,1792]{2,1,0:T(4,128)(2,1)S(1)}, bf16[320,96]{1,0:T(8,128)(2,1)S(1)}, s32[16]{0:T(128)S(1)}, bf16[96,1792]{1,0:T(8,128)(2,1)S(1)}) custom-call(s32[1]{0:T(128)} %bitcast.4.me_ref, s32[16]{0:T(128)} %slot_hbm.1, s32[1,96]{1,0:T(1,128)} %bitcast.32, bf16[96,1792]{1,0:T(8,128)(2,1)} %hidden_hbm.1), custom_call_target="tpu_custom_call" | custom-call | tf_op jit(solution)/shard_map/pallas_call | solution.py:179
  1.7 36.2 %all_to_all.10.rows_ref = bf16[80,4,1792]{2,1,0:T(4,128)(2,1)S(1)} all-to-all(bf16[80,4,1792]{2,1,0:T(4,128)(2,1)S(1)} %get-tuple-element.31), channel_id=1, replica_groups=mesh['rep'=2,'tp'=16] {'tp'}, dimensions={0} | all-to-all | bytes 2293760 | tf_op jit(solution)/shard_map/all_to_all | solution.py:284
  37.9 0.0 copy-done.1
  38.0 0.0 copy-start
  38.0 2.0 %copy-done = bf16[1,28672,64]{1,2,0:T(8,128)(2,1)S(1)} copy-done((bf16[1,28672,64]{1,2,0:T(8,128)(2,1)S(1)}, bf16[1,28672,64]{1,2,0:T(8,128)(2,1)}, u32[]{:S(2)}) %copy-start) | copy-done | bytes 3670040
  40.0 2.9 %shard_map.66 = (bf16[80,4,512]{2,1,0:T(4,128)(2,1)}, s32[1]{0:T(128)}) custom-call(bf16[80,4,1792]{2,1,0:T(4,128)(2,1)S(1)} %all_to_all.10.rows_ref, bf16[64,28672]{1,0:T(8,128)(2,1)S(1)} %bitcast.29, bf16[64,8192]{1,0:T(8,128)(2,1)S(1)} %bitcast.30), custom_call_target="tpu_custom_call" | custom-call | flops 94371840 | bytes 5865472 | tf_op jit(solution)/shard_map/pallas_call | solution.py:246
  42.9 3.6 %all-to-all-start.1 = ((bf16[80,4,512]{2,1,0:T(4,128)(2,1)}), bf16[80,4,512]{2,1,0:T(4,128)(2,1)S(1)}, u32[]{:S(2)}, u32[]{:S(2)}) async-start(bf16[80,4,512]{2,1,0:T(4,128)(2,1)} %get-tuple-element.38), calls=%async_computation.1 | async-start | bytes 655360 | tf_op jit(solution)/shard_map/all_to_all | solution.py:290
  46.5 14.1 %conditional.2 = (f32[16,96,128]{2,1,0:T(8,128)S(1)}, f16[17,96,128]{2,1,0:T(8,128)(2,1)S(1)}) conditional(s32[]{:T(128)} %bitcast.11, () %tuple.20, (s32[16]{0:T(128)S(1)}, bf16[96,1792]{1,0:T(8,128)(2,1)S(1)}, bf16[1792,8192]{1,0:T(8,128)(2,1)}) %tuple.21), branch_computations={%region_0.0_spmd, %region_1.0_spmd} | conditional | flops 1391024 | bytes 15413256 | solution.py:102
  46.5 0.1 fusion.7
  46.6 6.4 %branch_1_fun.3 = f32[32,96,128]{2,1,0:T(8,128)S(1)} custom-call(s32[8]{0:T(128)S(1)} %get-tuple-element.48.order_ref, bf16[96,1792]{1,0:T(8,128)(2,1)S(1)} %get-tuple-element.19.hidden_ref, bf16[1792,8192]{1,0:T(8,128)(2,1)} %get-tuple-element.40.down_ref), custom_call_target="tpu_custom_call" | custom-call | flops 1000 | bytes 1000 | tf_op jit(solution)/shard_map/cond/branch_1_fun/pallas_call | solution.py:54
  53.0 0.4 collective-permute-start.3
  53.3 6.4 %branch_1_fun.2 = f32[32,96,128]{2,1,0:T(8,128)S(1)} custom-call(s32[8]{0:T(128)S(1)} %get-tuple-element.49.order_ref, bf16[96,1792]{1,0:T(8,128)(2,1)S(1)} %get-tuple-element.19.hidden_ref, bf16[1792,8192]{1,0:T(8,128)(2,1)} %get-tuple-element.40.down_ref), custom_call_target="tpu_custom_call" | custom-call | flops 1000 | bytes 1000 | tf_op jit(solution)/shard_map/cond/branch_1_fun/pallas_call | solution.py:54
  59.8 0.0 collective-permute-done.3
  59.8 0.2 add.16
  60.0 0.1 abs_reduce_fusion
  60.1 0.2 multiply_convert_fusion
  60.3 0.1 broadcast_in_dim.8
  60.4 0.1 pad_maximum_fusion
  60.5 1.7 %collective-permute-start.4 = (f16[17,96,128]{2,1,0:T(8,128)(2,1)S(1)}, f16[17,96,128]{2,1,0:T(8,128)(2,1)S(1)}, u32[]{:S(2)}, u32[]{:S(2)}) collective-permute-start(f16[17,96,128]{2,1,0:T(8,128)(2,1)S(1)} %get-tuple-element.35), channel_id=1, source_target_pairs={{0,2},{1,3},{2,0},{3,1},{4,6},{5,7},{6,4},{7,5},{8,10},{9,11},{10,... | collective-permute-start | bytes 1253384 | tf_op jit(solution)/shard_map/ppermute | solution.py:22
  62.3 10.2 %collective-permute-done.4 = f16[17,96,128]{2,1,0:T(8,128)(2,1)S(1)} collective-permute-done((f16[17,96,128]{2,1,0:T(8,128)(2,1)S(1)}, f16[17,96,128]{2,1,0:T(8,128)(2,1)S(1)}, u32[]{:S(2)}, u32[]{:S(2)}) %collective-permute-start.4) | collective-permute-done | bytes 417824 | tf_op jit(solution)/shard_map/ppermute | solution.py:22
  73.1 14.7 %conditional.3 = (f32[4,96,128]{2,1,0:T(8,128)S(1)}) conditional(s32[]{:T(128)} %bitcast.10, () %tuple.19, (f16[17,96,128]{2,1,0:T(8,128)(2,1)S(1)}, f32[16,96,128]{2,1,0:T(8,128)S(1)}) %tuple.22), branch_computations={%region_3.0_spmd, %region_4.0_spmd} | conditional | flops 1955232 | bytes 6911744 | solution.py:123
  73.1 0.1 multiply_add_fusion
  73.3 0.2 abs_reduce_fusion.3
  73.5 0.1 multiply_convert_fusion.3
  73.6 0.1 broadcast_in_dim.9
  73.7 1.8 %collective-permute-start = (f16[5,96,128]{2,1,0:T(8,128)(2,1)S(1)}, f16[5,96,128]{2,1,0:T(8,128)(2,1)S(1)}, u32[]{:S(2)}, u32[]{:S(2)}) collective-permute-start(f16[5,96,128]{2,1,0:T(8,128)(2,1)S(1)} %pad_maximum_fusion.1), channel_id=1, source_target_pairs={{0,4},{1,5},{2,6},{3,7},{4,0},{5,1},{6,2},{7,3},{8,12},{9,13},{10,... | collective-permute-start | bytes 368648 | tf_op jit(solution)/shard_map/cond/branch_1_fun/ppermute | solution.py:22
  75.6 0.1 broadcast_in_dim.10
  75.7 2.5 %collective-permute-start.1 = (f16[5,96,128]{2,1,0:T(8,128)(2,1)S(1)}, f16[5,96,128]{2,1,0:T(8,128)(2,1)S(1)}, u32[]{:S(2)}, u32[]{:S(2)}) collective-permute-start(f16[5,96,128]{2,1,0:T(8,128)(2,1)S(1)} %pad_maximum_fusion.2), channel_id=1, source_target_pairs={{0,8},{1,9},{2,10},{3,11},{4,12},{5,13},{6,14},{7,15},{8,0},{9,1},... | collective-permute-start | bytes 368648 | tf_op jit(solution)/shard_map/cond/branch_1_fun/ppermute | solution.py:22
  78.2 0.1 broadcast_in_dim.11
  78.3 0.3 collective-permute-start.2
  78.6 1.1 %collective-permute-done = f16[5,96,128]{2,1,0:T(8,128)(2,1)S(1)} collective-permute-done((f16[5,96,128]{2,1,0:T(8,128)(2,1)S(1)}, f16[5,96,128]{2,1,0:T(8,128)(2,1)S(1)}, u32[]{:S(2)}, u32[]{:S(2)}) %collective-permute-start) | collective-permute-done | bytes 122912 | tf_op jit(solution)/shard_map/cond/branch_1_fun/ppermute | solution.py:22
  79.7 8.0 %collective-permute-done.1 = f16[5,96,128]{2,1,0:T(8,128)(2,1)S(1)} collective-permute-done((f16[5,96,128]{2,1,0:T(8,128)(2,1)S(1)}, f16[5,96,128]{2,1,0:T(8,128)(2,1)S(1)}, u32[]{:S(2)}, u32[]{:S(2)}) %collective-permute-start.1) | collective-permute-done | bytes 122912 | tf_op jit(solution)/shard_map/cond/branch_1_fun/ppermute | solution.py:22
  87.7 0.0 collective-permute-done.2
  87.7 0.1 fusion.2
  87.8 0.0 all-to-all-done.1
  87.8 0.1 reshape.123
  87.9 0.9 fusion.6
  (10 shorter events, 0.2 us)
Async XLA Ops:
  0.0 37.9 %copy-start.1 = (bf16[1,8192,64]{1,2,0:T(8,128)(2,1)S(1)}, bf16[1,8192,64]{1,2,0:T(8,128)(2,1)}, u32[]{:S(2)}) copy-start(bf16[1,8192,64]{1,2,0:T(8,128)(2,1)} %param.13) | copy-start | bytes 3145732
  38.0 2.0 %copy-start = (bf16[1,28672,64]{1,2,0:T(8,128)(2,1)S(1)}, bf16[1,28672,64]{1,2,0:T(8,128)(2,1)}, u32[]{:S(2)}) copy-start(bf16[1,28672,64]{1,2,0:T(8,128)(2,1)} %param.12) | copy-start | bytes 11010052
  42.9 45.0 %all-to-all-start.1 = ((bf16[80,4,512]{2,1,0:T(4,128)(2,1)}), bf16[80,4,512]{2,1,0:T(4,128)(2,1)S(1)}, u32[]{:S(2)}, u32[]{:S(2)}) async-start(bf16[80,4,512]{2,1,0:T(4,128)(2,1)} %get-tuple-element.38), calls=%async_computation.1 | async-start | bytes 655360 | tf_op jit(solution)/shard_map/all_to_all | solution.py:290
  53.0 6.8 %collective-permute-start.3 = (f32[32,96,128]{2,1,0:T(8,128)S(1)}, f32[32,96,128]{2,1,0:T(8,128)S(1)}, u32[]{:S(2)}, u32[]{:S(2)}) collective-permute-start(f32[32,96,128]{2,1,0:T(8,128)S(1)} %branch_1_fun.3), channel_id=1, source_target_pairs={{0,1},{1,0},{2,3},{3,2},{4,5},{5,4},{6,7},{7,6},{8,9},{9,8},{10,11... | collective-permute-start | bytes 4718600 | tf_op jit(solution)/shard_map/cond/branch_1_fun/ppermute | solution.py:22
  60.5 11.9 %collective-permute-start.4 = (f16[17,96,128]{2,1,0:T(8,128)(2,1)S(1)}, f16[17,96,128]{2,1,0:T(8,128)(2,1)S(1)}, u32[]{:S(2)}, u32[]{:S(2)}) collective-permute-start(f16[17,96,128]{2,1,0:T(8,128)(2,1)S(1)} %get-tuple-element.35), channel_id=1, source_target_pairs={{0,2},{1,3},{2,0},{3,1},{4,6},{5,7},{6,4},{7,5},{8,10},{9,11},{10,... | collective-permute-start | bytes 1253384 | tf_op jit(solution)/shard_map/ppermute | solution.py:22
  73.7 5.9 %collective-permute-start = (f16[5,96,128]{2,1,0:T(8,128)(2,1)S(1)}, f16[5,96,128]{2,1,0:T(8,128)(2,1)S(1)}, u32[]{:S(2)}, u32[]{:S(2)}) collective-permute-start(f16[5,96,128]{2,1,0:T(8,128)(2,1)S(1)} %pad_maximum_fusion.1), channel_id=1, source_target_pairs={{0,4},{1,5},{2,6},{3,7},{4,0},{5,1},{6,2},{7,3},{8,12},{9,13},{10,... | collective-permute-start | bytes 368648 | tf_op jit(solution)/shard_map/cond/branch_1_fun/ppermute | solution.py:22
  75.7 12.0 %collective-permute-start.1 = (f16[5,96,128]{2,1,0:T(8,128)(2,1)S(1)}, f16[5,96,128]{2,1,0:T(8,128)(2,1)S(1)}, u32[]{:S(2)}, u32[]{:S(2)}) collective-permute-start(f16[5,96,128]{2,1,0:T(8,128)(2,1)S(1)} %pad_maximum_fusion.2), channel_id=1, source_target_pairs={{0,8},{1,9},{2,10},{3,11},{4,12},{5,13},{6,14},{7,15},{8,0},{9,1},... | collective-permute-start | bytes 368648 | tf_op jit(solution)/shard_map/cond/branch_1_fun/ppermute | solution.py:22
  78.3 9.4 %collective-permute-start.2 = (f16[5,96,128]{2,1,0:T(8,128)(2,1)S(1)}, f16[5,96,128]{2,1,0:T(8,128)(2,1)S(1)}, u32[]{:S(2)}, u32[]{:S(2)}) collective-permute-start(f16[5,96,128]{2,1,0:T(8,128)(2,1)S(1)} %pad_maximum_fusion.3), channel_id=1, source_target_pairs={{0,12},{1,13},{2,14},{3,15},{4,8},{5,9},{6,10},{7,11},{8,4},{9,5},... | collective-permute-start | bytes 368648 | tf_op jit(solution)/shard_map/cond/branch_1_fun/ppermute | solution.py:22

commit v7 on v6

--- a/solution.py
+++ b/solution.py
@@ -283,6 +283,7 @@
     )
     gathered = lax.all_to_all(packed, "tp", split_axis=0, concat_axis=0, tiled=True)
     kept, sent = chip_sums(kept_hidden, down_matrix, group, order, width)
+    gathered, _ = lax.optimization_barrier((gathered, sent))
     pair_in = xor_permute(sent, group, 2)
     shrink = jnp.swapaxes(shrink_matrices, 1, 2)[0]
     expand = jnp.swapaxes(expand_matrices, 1, 2)[0]

time: 89.1 us -> 78.9 us (0.89)
  blocking collectives: 36.2 us -> 0 us
  waiting for transfers between devices: 19.2 us -> 32.2 us
  starting transfers between devices: 10.2 us -> 21.7 us
    all_to_all x1 -> x0, blocking collectives: 36.2 us -> none  [shards_by_blocks(): lax.all_to_all(packed, 'tp', split_axis=0, concat_axis=0, tiled=True)]
    all_to_all x0 -> x1, waiting for transfers between devices: none -> 9.55 us  [shards_by_blocks(): lax.all_to_all(packed, 'tp', split_axis=0, concat_axis=0, tiled=True)]
    all_to_all x0 -> x1, starting transfers between devices: none -> 7.37 us  [shards_by_blocks(): lax.all_to_all(packed, 'tp', split_axis=0, concat_axis=0, tiled=True)]
    all_to_all x1, starting transfers between devices: 3.55 us -> 7.36 us  [shards_by_blocks(): lax.all_to_all(adapter_out, 'tp', split_axis=0, concat_axis=0, tiled=True)]
    ppermute x5, waiting for transfers between devices: 19.2 us -> 22.6 us  [xor_permute(): return lax.ppermute(value, 'tp', [(i, i ^ offset) for i in range(group)])]
  transfers between devices with their start and end apart: 6 -> 7, of which waited for: 3 -> 4; matrix products, arithmetic and copies ran while one was open for 2% -> 3% of each run, Pallas kernels for 14% -> 16%
where the time goes in v7:
time: 78.9 us; the launch traced here: 78.5 us
  waiting for transfers between devices  32.2 us (41%)
  starting transfers between devices  21.7 us (28%)
  Pallas kernels  18.2 us (23%)
  local copies, waits for them, and re-layouts  2.51 us (3%)
  other arithmetic  2.13 us (3%)
  matrix products  0.87 us (1%)
    ppermute x5, waiting for transfers between devices, xor_permute(): return lax.ppermute(value, 'tp', [(i, i ^ offset) for i in range(group)])  22.6 us
    pallas_call x2, Pallas kernels, column_blocks(): pl.pallas_call(column_blocks_kernel, out_shape=jax.ShapeDtypeStruct((coun...  12.8 us
    all_to_all x1, waiting for transfers between devices, shards_by_blocks(): lax.all_to_all(packed, 'tp', split_axis=0, concat_axis=0, tiled=True)  9.55 us
    all_to_all x1, starting transfers between devices, shards_by_blocks(): lax.all_to_all(packed, 'tp', split_axis=0, concat_axis=0, tiled=True)  7.37 us
    all_to_all x1, starting transfers between devices, shards_by_blocks(): lax.all_to_all(adapter_out, 'tp', split_axis=0, concat_axis=0, tiled=True)  7.36 us
    ppermute x5, starting transfers between devices, xor_permute(): return lax.ppermute(value, 'tp', [(i, i ^ offset) for i in range(group)])  6.99 us
    pallas_call x1, Pallas kernels, adapter_output(): pl.pallas_call(adapter_kernel, out_shape=(jax.ShapeDtypeStruct((group * b...  2.86 us
    pallas_call x1, Pallas kernels, pack_rows(): pl.pallas_call(functools.partial(pack_kernel, blocks, orders), out_shape=...  2.49 us
  transfers between devices with their start and end apart: 7, of which 4 were waited for; matrix products, arithmetic and copies ran while one was open for 3% of the time, Pallas kernels for 16%

profile of v7, /device:TPU:0, one launch (start us, length us, event | category | flops | bytes accessed | tf_op | source)
XLA Modules:
  0.0 78.5 jit_solution(15737734372023603642)
XLA Ops:
  0.0 2.5 %shard_map.65 = (bf16[80,4,1792]{2,1,0:T(4,128)(2,1)}, bf16[320,96]{1,0:T(8,128)(2,1)S(1)}, s32[16]{0:T(128)S(1)}, bf16[96,1792]{1,0:T(8,128)(2,1)S(1)}) custom-call(s32[1]{0:T(128)} %bitcast.4.me_ref, s32[16]{0:T(128)} %slot_hbm.1, s32[1,96]{1,0:T(1,128)} %bitcast.32, bf16[96,1792]{1,0:T(8,128)(2,1)} %hidden_hbm.1), custom_call_target="tpu_custom_call" | custom-call | tf_op jit(solution)/shard_map/pallas_call | solution.py:179
  2.5 7.4 %all-to-all-start = ((bf16[80,4,1792]{2,1,0:T(4,128)(2,1)}), bf16[80,4,1792]{2,1,0:T(4,128)(2,1)S(1)}, u32[]{:S(2)}, u32[]{:S(2)}) async-start(bf16[80,4,1792]{2,1,0:T(4,128)(2,1)} %get-tuple-element.32), calls=%async_computation | async-start | bytes 2293760 | tf_op jit(solution)/shard_map/all_to_all | solution.py:284
  9.9 0.0 copy-start.1
  9.9 15.0 %conditional.2 = (f32[16,96,128]{2,1,0:T(8,128)S(1)}, f16[17,96,128]{2,1,0:T(8,128)(2,1)}) conditional(s32[]{:T(128)} %bitcast.6, () %tuple.20, (s32[16]{0:T(128)S(1)}, bf16[96,1792]{1,0:T(8,128)(2,1)S(1)}, bf16[1792,8192]{1,0:T(8,128)(2,1)}) %tuple.21), branch_computations={%region_0.0_spmd, %region_1.0_spmd} | conditional | flops 1391024 | bytes 15413256 | solution.py:102
  9.9 0.1 fusion.7
  10.0 6.4 %branch_1_fun.3 = f32[32,96,128]{2,1,0:T(8,128)S(1)} custom-call(s32[8]{0:T(128)S(1)} %get-tuple-element.50.order_ref, bf16[96,1792]{1,0:T(8,128)(2,1)S(1)} %get-tuple-element.19.hidden_ref, bf16[1792,8192]{1,0:T(8,128)(2,1)} %get-tuple-element.42.down_ref), custom_call_target="tpu_custom_call" | custom-call | flops 1000 | bytes 1000 | tf_op jit(solution)/shard_map/cond/branch_1_fun/pallas_call | solution.py:54
  16.4 0.5 collective-permute-start.3
  16.9 6.4 %branch_1_fun.2 = f32[32,96,128]{2,1,0:T(8,128)S(1)} custom-call(s32[8]{0:T(128)S(1)} %get-tuple-element.51.order_ref, bf16[96,1792]{1,0:T(8,128)(2,1)S(1)} %get-tuple-element.19.hidden_ref, bf16[1792,8192]{1,0:T(8,128)(2,1)} %get-tuple-element.42.down_ref), custom_call_target="tpu_custom_call" | custom-call | flops 1000 | bytes 1000 | tf_op jit(solution)/shard_map/cond/branch_1_fun/pallas_call | solution.py:54
  23.3 0.0 collective-permute-done.3
  23.3 0.2 add.16
  23.5 0.1 abs_reduce_fusion
  23.7 0.2 multiply_convert_fusion
  23.9 0.1 broadcast_in_dim.8
  24.0 0.9 %pad_maximum_fusion = f16[17,96,128]{2,1,0:T(8,128)(2,1)} fusion(f16[1,96,128]{2,1,0:T(8,128)(2,1)S(1)} %broadcast_in_dim.8, f16[16,96,128]{2,1,0:T(8,128)(2,1)S(1)} %get-tuple-element.46), kind=kLoop, calls=%fused_computation.2 | loop fusion | flops 208896 | bytes 835584 | tf_op jit(solution)/shard_map/cond/branch_1_fun/concatenate | solution.py:77
  24.9 9.6 %all-to-all-done.rows_ref = bf16[80,4,1792]{2,1,0:T(4,128)(2,1)S(1)} async-done(((bf16[80,4,1792]{2,1,0:T(4,128)(2,1)}), bf16[80,4,1792]{2,1,0:T(4,128)(2,1)S(1)}, u32[]{:S(2)}, u32[]{:S(2)}) %all-to-all-start) | async-done | bytes 1146912 | tf_op jit(solution)/shard_map/all_to_all | solution.py:284
  34.4 0.0 copy-done.1
  34.4 0.0 copy-start
  34.4 2.0 %copy-done = bf16[1,28672,64]{1,2,0:T(8,128)(2,1)S(1)} copy-done((bf16[1,28672,64]{1,2,0:T(8,128)(2,1)S(1)}, bf16[1,28672,64]{1,2,0:T(8,128)(2,1)}, u32[]{:S(2)}) %copy-start) | copy-done | bytes 3670040
  36.5 2.9 %shard_map.66 = (bf16[80,4,512]{2,1,0:T(4,128)(2,1)}, s32[1]{0:T(128)}) custom-call(bf16[80,4,1792]{2,1,0:T(4,128)(2,1)S(1)} %all-to-all-done.rows_ref, bf16[64,28672]{1,0:T(8,128)(2,1)S(1)} %bitcast.29, bf16[64,8192]{1,0:T(8,128)(2,1)S(1)} %bitcast.30), custom_call_target="tpu_custom_call" | custom-call | flops 94371840 | bytes 5865472 | tf_op jit(solution)/shard_map/pallas_call | solution.py:246
  39.4 7.4 %all-to-all-start.1 = ((bf16[80,4,512]{2,1,0:T(4,128)(2,1)}), bf16[80,4,512]{2,1,0:T(4,128)(2,1)S(1)}, u32[]{:S(2)}, u32[]{:S(2)}) async-start(bf16[80,4,512]{2,1,0:T(4,128)(2,1)} %get-tuple-element.40), calls=%async_computation.1 | async-start | bytes 655360 | tf_op jit(solution)/shard_map/all_to_all | solution.py:291
  46.7 1.9 %collective-permute-start.4 = (f16[17,96,128]{2,1,0:T(8,128)(2,1)}, f16[17,96,128]{2,1,0:T(8,128)(2,1)S(1)}, u32[]{:S(2)}, u32[]{:S(2)}) collective-permute-start(f16[17,96,128]{2,1,0:T(8,128)(2,1)} %get-tuple-element.35), channel_id=1, source_target_pairs={{0,2},{1,3},{2,0},{3,1},{4,6},{5,7},{6,4},{7,5},{8,10},{9,11},{10,... | collective-permute-start | bytes 1253384 | tf_op jit(solution)/shard_map/ppermute | solution.py:22
  48.7 13.7 %collective-permute-done.4 = f16[17,96,128]{2,1,0:T(8,128)(2,1)S(1)} collective-permute-done((f16[17,96,128]{2,1,0:T(8,128)(2,1)}, f16[17,96,128]{2,1,0:T(8,128)(2,1)S(1)}, u32[]{:S(2)}, u32[]{:S(2)}) %collective-permute-start.4) | collective-permute-done | bytes 417824 | tf_op jit(solution)/shard_map/ppermute | solution.py:22
  63.0 14.6 %conditional.3 = (f32[4,96,128]{2,1,0:T(8,128)S(1)}) conditional(s32[]{:T(128)} %bitcast.11, () %tuple.23, (f16[17,96,128]{2,1,0:T(8,128)(2,1)S(1)}, f32[16,96,128]{2,1,0:T(8,128)S(1)}) %tuple.24), branch_computations={%region_3.0_spmd, %region_4.0_spmd} | conditional | flops 1955232 | bytes 6911744 | solution.py:123
  63.0 0.1 multiply_add_fusion
  63.1 0.2 abs_reduce_fusion.3
  63.3 0.1 multiply_convert_fusion.3
  63.5 0.1 broadcast_in_dim.9
  63.6 1.5 %collective-permute-start = (f16[5,96,128]{2,1,0:T(8,128)(2,1)S(1)}, f16[5,96,128]{2,1,0:T(8,128)(2,1)S(1)}, u32[]{:S(2)}, u32[]{:S(2)}) collective-permute-start(f16[5,96,128]{2,1,0:T(8,128)(2,1)S(1)} %pad_maximum_fusion.1), channel_id=1, source_target_pairs={{0,4},{1,5},{2,6},{3,7},{4,0},{5,1},{6,2},{7,3},{8,12},{9,13},{10,... | collective-permute-start | bytes 368648 | tf_op jit(solution)/shard_map/cond/branch_1_fun/ppermute | solution.py:22
  65.1 0.1 broadcast_in_dim.10
  65.2 2.4 %collective-permute-start.1 = (f16[5,96,128]{2,1,0:T(8,128)(2,1)S(1)}, f16[5,96,128]{2,1,0:T(8,128)(2,1)S(1)}, u32[]{:S(2)}, u32[]{:S(2)}) collective-permute-start(f16[5,96,128]{2,1,0:T(8,128)(2,1)S(1)} %pad_maximum_fusion.2), channel_id=1, source_target_pairs={{0,8},{1,9},{2,10},{3,11},{4,12},{5,13},{6,14},{7,15},{8,0},{9,1},... | collective-permute-start | bytes 368648 | tf_op jit(solution)/shard_map/cond/branch_1_fun/ppermute | solution.py:22
  67.7 0.1 broadcast_in_dim.11
  67.8 0.6 collective-permute-start.2
  68.4 1.4 %collective-permute-done = f16[5,96,128]{2,1,0:T(8,128)(2,1)S(1)} collective-permute-done((f16[5,96,128]{2,1,0:T(8,128)(2,1)S(1)}, f16[5,96,128]{2,1,0:T(8,128)(2,1)S(1)}, u32[]{:S(2)}, u32[]{:S(2)}) %collective-permute-start) | collective-permute-done | bytes 122912 | tf_op jit(solution)/shard_map/cond/branch_1_fun/ppermute | solution.py:22
  69.9 7.6 %collective-permute-done.1 = f16[5,96,128]{2,1,0:T(8,128)(2,1)S(1)} collective-permute-done((f16[5,96,128]{2,1,0:T(8,128)(2,1)S(1)}, f16[5,96,128]{2,1,0:T(8,128)(2,1)S(1)}, u32[]{:S(2)}, u32[]{:S(2)}) %collective-permute-start.1) | collective-permute-done | bytes 122912 | tf_op jit(solution)/shard_map/cond/branch_1_fun/ppermute | solution.py:22
  77.4 0.0 collective-permute-done.2
  77.5 0.1 fusion.2
  77.6 0.0 all-to-all-done.1
  77.6 0.1 reshape.123
  77.7 0.9 %fusion.6 = bf16[96,512]{1,0:T(8,128)(2,1)} fusion(bf16[320,96]{1,0:T(8,128)(2,1)S(1)} %get-tuple-element.39, bf16[320,512]{1,0:T(8,128)(2,1)S(1)} %reshape.123, f32[4,96,128]{2,1,0:T(8,128)S(1)} %get-tuple-element.67), kind=kOutput, calls=%fused_computation.34 | convolution fusion | flops 31604736 | bytes 684032 | tf_op jit(solution)/shard_map/dot_general | solution.py:294
  (10 shorter events, 0.2 us)
Async XLA Ops:
  2.5 31.9 %all-to-all-start = ((bf16[80,4,1792]{2,1,0:T(4,128)(2,1)}), bf16[80,4,1792]{2,1,0:T(4,128)(2,1)S(1)}, u32[]{:S(2)}, u32[]{:S(2)}) async-start(bf16[80,4,1792]{2,1,0:T(4,128)(2,1)} %get-tuple-element.32), calls=%async_computation | async-start | bytes 2293760 | tf_op jit(solution)/shard_map/all_to_all | solution.py:284
  9.9 24.5 %copy-start.1 = (bf16[1,8192,64]{1,2,0:T(8,128)(2,1)S(1)}, bf16[1,8192,64]{1,2,0:T(8,128)(2,1)}, u32[]{:S(2)}) copy-start(bf16[1,8192,64]{1,2,0:T(8,128)(2,1)} %param.13) | copy-start | bytes 3145732
  16.4 6.9 %collective-permute-start.3 = (f32[32,96,128]{2,1,0:T(8,128)S(1)}, f32[32,96,128]{2,1,0:T(8,128)S(1)}, u32[]{:S(2)}, u32[]{:S(2)}) collective-permute-start(f32[32,96,128]{2,1,0:T(8,128)S(1)} %branch_1_fun.3), channel_id=1, source_target_pairs={{0,1},{1,0},{2,3},{3,2},{4,5},{5,4},{6,7},{7,6},{8,9},{9,8},{10,11... | collective-permute-start | bytes 4718600 | tf_op jit(solution)/shard_map/cond/branch_1_fun/ppermute | solution.py:22
  34.4 2.0 %copy-start = (bf16[1,28672,64]{1,2,0:T(8,128)(2,1)S(1)}, bf16[1,28672,64]{1,2,0:T(8,128)(2,1)}, u32[]{:S(2)}) copy-start(bf16[1,28672,64]{1,2,0:T(8,128)(2,1)} %param.12) | copy-start | bytes 11010052
  39.4 38.2 %all-to-all-start.1 = ((bf16[80,4,512]{2,1,0:T(4,128)(2,1)}), bf16[80,4,512]{2,1,0:T(4,128)(2,1)S(1)}, u32[]{:S(2)}, u32[]{:S(2)}) async-start(bf16[80,4,512]{2,1,0:T(4,128)(2,1)} %get-tuple-element.40), calls=%async_computation.1 | async-start | bytes 655360 | tf_op jit(solution)/shard_map/all_to_all | solution.py:291
  46.7 15.6 %collective-permute-start.4 = (f16[17,96,128]{2,1,0:T(8,128)(2,1)}, f16[17,96,128]{2,1,0:T(8,128)(2,1)S(1)}, u32[]{:S(2)}, u32[]{:S(2)}) collective-permute-start(f16[17,96,128]{2,1,0:T(8,128)(2,1)} %get-tuple-element.35), channel_id=1, source_target_pairs={{0,2},{1,3},{2,0},{3,1},{4,6},{5,7},{6,4},{7,5},{8,10},{9,11},{10,... | collective-permute-start | bytes 1253384 | tf_op jit(solution)/shard_map/ppermute | solution.py:22
  63.6 6.3 %collective-permute-start = (f16[5,96,128]{2,1,0:T(8,128)(2,1)S(1)}, f16[5,96,128]{2,1,0:T(8,128)(2,1)S(1)}, u32[]{:S(2)}, u32[]{:S(2)}) collective-permute-start(f16[5,96,128]{2,1,0:T(8,128)(2,1)S(1)} %pad_maximum_fusion.1), channel_id=1, source_target_pairs={{0,4},{1,5},{2,6},{3,7},{4,0},{5,1},{6,2},{7,3},{8,12},{9,13},{10,... | collective-permute-start | bytes 368648 | tf_op jit(solution)/shard_map/cond/branch_1_fun/ppermute | solution.py:22
  65.2 12.2 %collective-permute-start.1 = (f16[5,96,128]{2,1,0:T(8,128)(2,1)S(1)}, f16[5,96,128]{2,1,0:T(8,128)(2,1)S(1)}, u32[]{:S(2)}, u32[]{:S(2)}) collective-permute-start(f16[5,96,128]{2,1,0:T(8,128)(2,1)S(1)} %pad_maximum_fusion.2), channel_id=1, source_target_pairs={{0,8},{1,9},{2,10},{3,11},{4,12},{5,13},{6,14},{7,15},{8,0},{9,1},... | collective-permute-start | bytes 368648 | tf_op jit(solution)/shard_map/cond/branch_1_fun/ppermute | solution.py:22
  67.8 9.6 %collective-permute-start.2 = (f16[5,96,128]{2,1,0:T(8,128)(2,1)S(1)}, f16[5,96,128]{2,1,0:T(8,128)(2,1)S(1)}, u32[]{:S(2)}, u32[]{:S(2)}) collective-permute-start(f16[5,96,128]{2,1,0:T(8,128)(2,1)S(1)} %pad_maximum_fusion.3), channel_id=1, source_target_pairs={{0,12},{1,13},{2,14},{3,15},{4,8},{5,9},{6,10},{7,11},{8,4},{9,5},... | collective-permute-start | bytes 368648 | tf_op jit(solution)/shard_map/cond/branch_1_fun/ppermute | solution.py:22

commit v8 on v6

--- a/solution.py
+++ b/solution.py
@@ -12,6 +12,8 @@
 MOST = 20
 LANES = 128
 F16_TOP = 14.0
+PLANE = 4
+HELD = 24
 
 
 def in_hbm(value):
@@ -64,7 +66,7 @@
             pltpu.VMEM((count, depth, width), jnp.bfloat16),
             pltpu.SemaphoreType.DMA((count, pieces)),
         ],
-        compiler_params=pltpu.CompilerParams(vmem_limit_bytes=40 * 2**20),
+        compiler_params=pltpu.CompilerParams(vmem_limit_bytes=20 * 2**20),
         cost_estimate=pl.CostEstimate(flops=1000, bytes_accessed=1000, transcendentals=0),
     )(order, hidden, in_hbm(down_matrix))
 
@@ -82,45 +84,35 @@
     return packed[:-1].astype(jnp.float32) * jnp.exp2(exponent - F16_TOP)
 
 
-def chip_sums(hidden, down_matrix, group, order, width):
+def pair_sums(hidden, down_matrix, group, order, width):
+    half = group * width // LANES // 4
+    rows = hidden.shape[0]
+
     def work():
         odd = column_blocks(hidden, down_matrix, order[: group // 2], width)
         odd_in = xor_permute(odd, group, 1)
         even = column_blocks(hidden, down_matrix, order[group // 2 :], width)
         chip = even + odd_in
-        half = chip.shape[0] // 2
-        return chip[:half], pack_scaled(chip[half:])
+        pair_in = xor_permute(pack_scaled(chip[half:]), group, 2)
+        return chip[:half] + unpack_scaled(pair_in)
 
     def idle():
-        rows = hidden.shape[0]
-        half = group * width // LANES // 4
-        return (
-            jnp.zeros((half, rows, LANES), jnp.float32),
-            jnp.zeros((half + 1, rows, LANES), jnp.float16),
-        )
+        return jnp.zeros((half, rows, LANES), jnp.float32)
 
     return lax.cond(order[0] >= 0, work, idle)
 
 
-def line_sums(kept, pair_in, flag, group, width):
-    rows = kept.shape[1]
+def line_sums(pair, group, width):
+    rows = pair.shape[1]
     parts = width // LANES
-
-    def work():
-        pair = kept + unpack_scaled(pair_in)
-        total = pair[:parts]
-        arrived = [
-            xor_permute(pack_scaled(pair[i * parts : (i + 1) * parts]), group, 4 * i)
-            for i in range(1, group // 4)
-        ]
-        for packed in arrived:
-            total = total + unpack_scaled(packed)
-        return total
-
-    def idle():
-        return jnp.zeros((parts, rows, LANES), jnp.float32)
-
-    return lax.cond(flag >= 0, work, idle)
+    arrived = [
+        xor_permute(pack_scaled(pair[i * parts : (i + 1) * parts]), group, 4 * i)
+        for i in range(1, group // 4)
+    ]
+    total = pair[:parts]
+    for packed in arrived:
+        total = total + unpack_scaled(packed)
+    return jnp.transpose(total, (1, 0, 2)).reshape(rows, width)
 
 
 def pack_kernel(
@@ -162,7 +154,10 @@
     place = jnp.sum(shift, axis=0, keepdims=True) + lax.broadcasted_iota(jnp.int32, (1, rows), 1)
     spots = lax.broadcasted_iota(jnp.int32, (group * blocks * BLOCK, rows), 0)
     pick = jnp.where(spots == place, 1.0, 0.0).astype(jnp.bfloat16)
-    pick_ref[...] = pick
+    for k in range(PLANE):
+        line = lax.broadcasted_iota(jnp.int32, (HELD, rows), 0)
+        mine = (line + (me_ref[0] ^ k) * (blocks * BLOCK) == place) & (line < blocks * BLOCK)
+        pick_ref[k * HELD : (k + 1) * HELD] = jnp.where(mine, 1.0, 0.0).astype(jnp.bfloat16)
     copies[2].wait()
     packed = jnp.dot(pick, hidden_ref[...], preferred_element_type=jnp.float32)
     packed_ref[...] = packed.astype(jnp.bfloat16).reshape(packed_ref.shape)
@@ -180,7 +175,7 @@
         functools.partial(pack_kernel, blocks, orders),
         out_shape=(
             jax.ShapeDtypeStruct((group * blocks, BLOCK, depth), jnp.bfloat16),
-            jax.ShapeDtypeStruct((group * MOST, rows), jnp.bfloat16),
+            jax.ShapeDtypeStruct((PLANE * HELD, rows), jnp.bfloat16),
             jax.ShapeDtypeStruct((len(orders),), jnp.int32),
             jax.ShapeDtypeStruct((rows, depth), jnp.bfloat16),
         ),
@@ -196,13 +191,13 @@
     )(me.reshape(1), in_hbm(adapter_holder_slot), in_hbm(adapter_of_row.reshape(1, rows)), in_hbm(hidden))
 
 
-def adapter_kernel(rows_ref, shrink_ref, expand_ref, out_ref, flag_ref, total_ref):
+def adapter_kernel(parts, me_ref, rows_ref, shrink_ref, expand_ref, *refs):
+    out_refs, total_ref = refs[:PLANE], refs[PLANE]
     step = pl.program_id(0)
-    flag_ref[0] = step
     block, depth = rows_ref.shape[1:]
     blocks = MOST // BLOCK
     sources = rows_ref.shape[0] // blocks
-    total = jnp.zeros(total_ref.shape, jnp.float32)
+    total = jnp.zeros((MOST, total_ref.shape[1]), jnp.float32)
     for source in range(sources):
         own = rows_ref[source * blocks : (source + 1) * blocks].reshape(MOST, depth)
         total += lax.dot_general(
@@ -214,59 +209,71 @@
 
     @pl.when(step == 0)
     def _():
-        total_ref[...] = total
-
-    @pl.when(step > 0)
-    def _():
-        total_ref[...] += total
+        total_ref[...] = jnp.zeros_like(total_ref)
+
+    total_ref[:MOST] += total
 
     @pl.when(step == pl.num_programs(0) - 1)
     def _():
         rank_rows = total_ref[...].astype(jnp.bfloat16)
-        width = out_ref.shape[2]
-        for target in range(out_ref.shape[0] // blocks):
-            piece = jnp.dot(
-                rank_rows,
-                expand_ref[:, target * width : (target + 1) * width],
-                preferred_element_type=jnp.float32,
-            )
-            out_ref[target * blocks : (target + 1) * blocks] = piece.astype(jnp.bfloat16).reshape(
-                blocks, BLOCK, width
-            )
-
-
-def adapter_output(gathered, shrink, expand, group):
+        width = parts * LANES
+        for k in range(PLANE):
+            for line in range(out_refs[k].shape[0] // parts):
+                target = me_ref[0] ^ (PLANE * line + k)
+                columns = pl.ds(pl.multiple_of(target * width, LANES), width)
+                piece = jnp.dot(rank_rows, expand_ref[:, columns], preferred_element_type=jnp.float32)
+                piece = piece.astype(jnp.bfloat16)
+                for part in range(parts):
+                    out_refs[k][line * parts + part] = piece[:, part * LANES : (part + 1) * LANES]
+
+
+def adapter_output(gathered, shrink, expand, group, me):
     rank, hidden_width = shrink.shape
     model_width = expand.shape[1]
     depth = gathered.shape[2]
     blocks = MOST // BLOCK
-    width = model_width // group
+    parts = model_width // group // LANES
+    held = (model_width // PLANE // LANES, HELD, LANES)
     steps = 4
     sources = group // steps
     return pl.pallas_call(
-        adapter_kernel,
-        out_shape=(
-            jax.ShapeDtypeStruct((group * blocks, BLOCK, width), jnp.bfloat16),
-            jax.ShapeDtypeStruct((1,), jnp.int32),
-        ),
+        functools.partial(adapter_kernel, parts),
+        out_shape=[jax.ShapeDtypeStruct(held, jnp.bfloat16)] * PLANE,
         grid=(steps,),
         in_specs=[
+            pl.BlockSpec(memory_space=pltpu.SMEM),
             pl.BlockSpec((sources * blocks, BLOCK, depth), lambda i: (i, 0, 0)),
             pl.BlockSpec((rank, sources * depth), lambda i: (0, i)),
             pl.BlockSpec((rank, model_width), lambda i: (0, 0)),
         ],
-        out_specs=(
-            pl.BlockSpec((group * blocks, BLOCK, width), lambda i: (0, 0, 0)),
-            pl.BlockSpec(memory_space=pltpu.SMEM),
-        ),
-        scratch_shapes=[pltpu.VMEM((MOST, rank), jnp.float32)],
-        compiler_params=pltpu.CompilerParams(vmem_limit_bytes=32 * 2**20),
-        cost_estimate=pl.CostEstimate(
-            flops=2 * MOST * rank * (hidden_width + model_width),
-            bytes_accessed=2 * rank * (hidden_width + model_width) + 2 * MOST * hidden_width,
-            transcendentals=0,
-        ),
-    )(gathered, shrink, expand)
+        out_specs=[pl.BlockSpec(held, lambda i: (0, 0, 0))] * PLANE,
+        scratch_shapes=[pltpu.VMEM((HELD, rank), jnp.float32)],
+        compiler_params=pltpu.CompilerParams(vmem_limit_bytes=24 * 2**20),
+    )(me.reshape(1), gathered, shrink, expand)
+
+
+def merge_kernel(pair_ref, pick_ref, *refs):
+    in_refs, out_ref, held_ref = refs[:PLANE], refs[PLANE], refs[PLANE + 1]
+    for k in range(PLANE):
+        held_ref[:, k * HELD : (k + 1) * HELD] = in_refs[k][...]
+    pick = pick_ref[...]
+    for part in range(pair_ref.shape[0]):
+        adapter_rows = lax.dot_general(
+            pick, held_ref[part], (((0,), (0,)), ((), ())), preferred_element_type=jnp.float32
+        )
+        out_ref[part] = pair_ref[part] + ADAPTER_SCALE * adapter_rows
+
+
+def merge_adapters(pair, pick, arrived):
+    vmem = pl.BlockSpec(memory_space=pltpu.VMEM)
+    return pl.pallas_call(
+        merge_kernel,
+        out_shape=jax.ShapeDtypeStruct(pair.shape, jnp.float32),
+        in_specs=[vmem] * (2 + PLANE),
+        out_specs=vmem,
+        scratch_shapes=[pltpu.VMEM((pair.shape[0], PLANE * HELD, LANES), jnp.bfloat16)],
+        compiler_params=pltpu.CompilerParams(vmem_limit_bytes=24 * 2**20),
+    )(pair, pick, *arrived)
 
 
 def shards_by_blocks(
@@ -282,21 +289,14 @@
         hidden, adapter_of_row, adapter_holder_slot, me, orders
     )
     gathered = lax.all_to_all(packed, "tp", split_axis=0, concat_axis=0, tiled=True)
-    kept, sent = chip_sums(kept_hidden, down_matrix, group, order, width)
-    pair_in = xor_permute(sent, group, 2)
+    pair = pair_sums(kept_hidden, down_matrix, group, order, width)
+    gathered, _ = lax.optimization_barrier((gathered, pair))
     shrink = jnp.swapaxes(shrink_matrices, 1, 2)[0]
     expand = jnp.swapaxes(expand_matrices, 1, 2)[0]
-    adapter_out, flag = adapter_output(gathered, shrink, expand, group)
-    adapter_in = lax.all_to_all(adapter_out, "tp", split_axis=0, concat_axis=0, tiled=True)
-    total = line_sums(kept, pair_in, flag[0], group, width)
-    base = jnp.transpose(total, (1, 0, 2)).reshape(rows, width)
-    adapter_rows = lax.dot_general(
-        pick,
-        adapter_in.reshape(group * MOST, width),
-        (((0,), (0,)), ((), ())),
-        preferred_element_type=jnp.float32,
-    )
-    return (base + ADAPTER_SCALE * adapter_rows).astype(jnp.bfloat16)
+    outs = adapter_output(gathered, shrink, expand, group, me)
+    arrived = [outs[0]] + [xor_permute(outs[k], group, k) for k in range(1, PLANE)]
+    merged = merge_adapters(pair, pick, arrived)
+    return line_sums(merged, group, width).astype(jnp.bfloat16)
 
 
 def shards(
@@ -305,7 +305,7 @@
     group = lax.axis_size("tp")
     rows, depth = hidden.shape
     width = down_matrix.shape[1] // group
-    if width % LANES == 0 and depth % LANES == 0 and group % 4 == 0:
+    if width % LANES == 0 and depth % LANES == 0 and group >= PLANE and group & (group - 1) == 0:
         return shards_by_blocks(
             hidden, down_matrix, shrink_matrices, expand_matrices, adapter_of_row, adapter_holder_slot
         )

time: 89.1 us -> 67.9 us (0.76)
  blocking collectives: 36.2 us -> 0 us
  waiting for transfers between devices: 19.2 us -> 28 us
  starting transfers between devices: 10.2 us -> 17.3 us
    all_to_all x1 -> x0, blocking collectives: 36.2 us -> none  [shards_by_blocks(): lax.all_to_all(packed, 'tp', split_axis=0, concat_axis=0, tiled=True)]
    ppermute x5 -> x8, waiting for transfers between devices: 19.2 us -> 28 us  [xor_permute(): return lax.ppermute(value, 'tp', [(i, i ^ offset) for i in range(group)])]
    all_to_all x1, starting transfers between devices: 3.55 us -> 7.37 us  [shards_by_blocks(): lax.all_to_all(packed, 'tp', split_axis=0, concat_axis=0, tiled=True)]
    ppermute x5 -> x8, starting transfers between devices: 6.69 us -> 9.91 us  [xor_permute(): return lax.ppermute(value, 'tp', [(i, i ^ offset) for i in range(group)])]
    pallas_call x1 -> x2, Pallas kernels: 2.86 us -> 2.37 us  [the longest x1 2.07 us: adapter_output(): pl.pallas_call(functools.partial(adapter_kernel, parts), out_shape=[jax.S...]
  transfers between devices with their start and end apart: 6 -> 9, of which waited for: 3 -> 5; matrix products, arithmetic and copies ran while one was open for 2% -> 2% of each run, Pallas kernels for 14% -> 19%
where the time goes in v8:
time: 67.9 us; the launch traced here: 67.7 us
  waiting for transfers between devices  28 us (41%)
  Pallas kernels  17.7 us (26%)
  starting transfers between devices  17.3 us (25%)
  local copies, waits for them, and re-layouts  2.42 us (4%)
  other arithmetic  1.97 us (3%)
    ppermute x8, waiting for transfers between devices, xor_permute(): return lax.ppermute(value, 'tp', [(i, i ^ offset) for i in range(group)])  28 us
    pallas_call x2, Pallas kernels, column_blocks(): pl.pallas_call(column_blocks_kernel, out_shape=jax.ShapeDtypeStruct((coun...  12.8 us
    ppermute x8, starting transfers between devices, xor_permute(): return lax.ppermute(value, 'tp', [(i, i ^ offset) for i in range(group)])  9.91 us
    all_to_all x1, starting transfers between devices, shards_by_blocks(): lax.all_to_all(packed, 'tp', split_axis=0, concat_axis=0, tiled=True)  7.37 us
    pallas_call x1, Pallas kernels, pack_rows(): pl.pallas_call(functools.partial(pack_kernel, blocks, orders), out_shape=...  2.5 us
    pallas_call x1, Pallas kernels, adapter_output(): pl.pallas_call(functools.partial(adapter_kernel, parts), out_shape=[jax.S...  2.07 us
    unnamed x4, local copies, waits for them, and re-layouts  2.04 us
  transfers between devices with their start and end apart: 9, of which 5 were waited for; matrix products, arithmetic and copies ran while one was open for 2% of the time, Pallas kernels for 19%

profile of v8, /device:TPU:0, one launch (start us, length us, event | category | flops | bytes accessed | tf_op | source)
XLA Modules:
  0.0 67.7 jit_solution(17437031177204603293)
XLA Ops:
  0.0 2.5 %shard_map.65 = (bf16[80,4,1792]{2,1,0:T(4,128)(2,1)}, bf16[96,96]{1,0:T(8,128)(2,1)S(1)}, s32[16]{0:T(128)S(1)}, bf16[96,1792]{1,0:T(8,128)(2,1)S(1)}) custom-call(s32[1]{0:T(128)} %bitcast.1.me_ref, s32[16]{0:T(128)} %slot_hbm.1, s32[1,96]{1,0:T(1,128)} %bitcast.27, bf16[96,1792]{1,0:T(8,128)(2,1)} %hidden_hbm.1), custom_call_target="tpu_custom_call" | custom-call | tf_op jit(solution)/shard_map/pallas_call | solution.py:174
  2.5 7.4 %all-to-all-start = ((bf16[80,4,1792]{2,1,0:T(4,128)(2,1)}), bf16[80,4,1792]{2,1,0:T(4,128)(2,1)S(1)}, u32[]{:S(2)}, u32[]{:S(2)}) async-start(bf16[80,4,1792]{2,1,0:T(4,128)(2,1)} %get-tuple-element.29), calls=%async_computation | async-start | bytes 2293760 | tf_op jit(solution)/shard_map/all_to_all | solution.py:291
  9.9 0.0 copy-start.1
  9.9 29.3 %conditional.1 = (f32[16,96,128]{2,1,0:T(8,128)S(1)}) conditional(s32[]{:T(128)} %bitcast.3, () %tuple.12, (s32[16]{0:T(128)S(1)}, bf16[96,1792]{1,0:T(8,128)(2,1)S(1)}, bf16[1792,8192]{1,0:T(8,128)(2,1)}) %tuple.13), branch_computations={%region_0.0_spmd, %region_1.0_spmd} | conditional | flops 2017712 | bytes 17600552 | solution.py:102
  10.0 0.1 fusion.8
  10.0 6.4 %branch_1_fun.3 = f32[32,96,128]{2,1,0:T(8,128)S(1)} custom-call(s32[8]{0:T(128)S(1)} %get-tuple-element.42.order_ref, bf16[96,1792]{1,0:T(8,128)(2,1)S(1)} %get-tuple-element.15.hidden_ref, bf16[1792,8192]{1,0:T(8,128)(2,1)} %get-tuple-element.36.down_ref), custom_call_target="tpu_custom_call" | custom-call | flops 1000 | bytes 1000 | tf_op jit(solution)/shard_map/cond/branch_1_fun/pallas_call | solution.py:56
  16.4 0.5 collective-permute-start
  16.9 6.4 %branch_1_fun.2 = f32[32,96,128]{2,1,0:T(8,128)S(1)} custom-call(s32[8]{0:T(128)S(1)} %get-tuple-element.43.order_ref, bf16[96,1792]{1,0:T(8,128)(2,1)S(1)} %get-tuple-element.15.hidden_ref, bf16[1792,8192]{1,0:T(8,128)(2,1)} %get-tuple-element.36.down_ref), custom_call_target="tpu_custom_call" | custom-call | flops 1000 | bytes 1000 | tf_op jit(solution)/shard_map/cond/branch_1_fun/pallas_call | solution.py:56
  23.4 0.0 collective-permute-done
  23.4 0.2 add.14
  23.6 0.1 abs_reduce_fusion
  23.7 0.2 multiply_convert_fusion
  23.9 0.1 broadcast_in_dim.8
  24.0 0.1 pad_maximum_fusion
  24.1 1.7 %collective-permute-start.1 = (f16[17,96,128]{2,1,0:T(8,128)(2,1)S(1)}, f16[17,96,128]{2,1,0:T(8,128)(2,1)S(1)}, u32[]{:S(2)}, u32[]{:S(2)}) collective-permute-start(f16[17,96,128]{2,1,0:T(8,128)(2,1)S(1)} %pad_maximum_fusion), channel_id=1, source_target_pairs={{0,2},{1,3},{2,0},{3,1},{4,6},{5,7},{6,4},{7,5},{8,10},{9,11},{10,... | collective-permute-start | bytes 1253384 | tf_op jit(solution)/shard_map/cond/branch_1_fun/ppermute | solution.py:24
  25.8 13.2 %collective-permute-done.1 = f16[17,96,128]{2,1,0:T(8,128)(2,1)S(1)} collective-permute-done((f16[17,96,128]{2,1,0:T(8,128)(2,1)S(1)}, f16[17,96,128]{2,1,0:T(8,128)(2,1)S(1)}, u32[]{:S(2)}, u32[]{:S(2)}) %collective-permute-start.1) | collective-permute-done | bytes 417824 | tf_op jit(solution)/shard_map/cond/branch_1_fun/ppermute | solution.py:24
  39.1 0.1 slice_add_fusion
  39.2 0.0 all-to-all-done.rows_ref
  39.2 0.0 copy-done.1
  39.2 0.0 copy-start
  39.2 2.0 %copy-done = bf16[1,28672,64]{1,2,0:T(8,128)(2,1)S(1)} copy-done((bf16[1,28672,64]{1,2,0:T(8,128)(2,1)S(1)}, bf16[1,28672,64]{1,2,0:T(8,128)(2,1)}, u32[]{:S(2)}) %copy-start) | copy-done | bytes 3670040
  41.3 2.1 %shard_map.66 = (bf16[16,24,128]{2,1,0:T(8,128)(2,1)S(1)}, bf16[16,24,128]{2,1,0:T(8,128)(2,1)S(1)}, bf16[16,24,128]{2,1,0:T(8,128)(2,1)S(1)}, bf16[16,24,128]{2,1,0:T(8,128)(2,1)S(1)}) custom-call(s32[1]{0:T(128)} %bitcast.1.me_ref, bf16[80,4,1792]{2,1,0:T(4,128)(2,1)S(1)} %all-to-all-done.rows_ref, bf16[64,28672]{1,0:T(8,128)(2,1)S(1)} %bitcast.24, ...), custom_call_target="tpu_custom_call" | custom-call | tf_op jit(solution)/shard_map/pallas_call | solution.py:239
  43.3 0.1 collective-permute-start.2
  43.4 1.4 %collective-permute-start.3 = (bf16[16,24,128]{2,1,0:T(8,128)(2,1)S(1)}, bf16[16,24,128]{2,1,0:T(8,128)(2,1)S(1)}, u32[]{:S(2)}, u32[]{:S(2)}) collective-permute-start(bf16[16,24,128]{2,1,0:T(8,128)(2,1)S(1)} %get-tuple-element.33), channel_id=1, source_target_pairs={{0,2},{1,3},{2,0},{3,1},{4,6},{5,7},{6,4},{7,5},{8,10},{9,11},{10,... | collective-permute-start | bytes 294920 | tf_op jit(solution)/shard_map/ppermute | solution.py:24
  44.8 0.5 collective-permute-start.4
  45.3 0.0 collective-permute-done.2.refs_1_
  45.3 3.8 %collective-permute-done.3.refs_2_ = bf16[16,24,128]{2,1,0:T(8,128)(2,1)S(1)} collective-permute-done((bf16[16,24,128]{2,1,0:T(8,128)(2,1)S(1)}, bf16[16,24,128]{2,1,0:T(8,128)(2,1)S(1)}, u32[]{:S(2)}, u32[]{:S(2)}) %collective-permute-start.3) | collective-permute-done | bytes 98336 | tf_op jit(solution)/shard_map/ppermute | solution.py:24
  49.1 1.2 %collective-permute-done.4.refs_3_ = bf16[16,24,128]{2,1,0:T(8,128)(2,1)S(1)} collective-permute-done((bf16[16,24,128]{2,1,0:T(8,128)(2,1)S(1)}, bf16[16,24,128]{2,1,0:T(8,128)(2,1)S(1)}, u32[]{:S(2)}, u32[]{:S(2)}) %collective-permute-start.4) | collective-permute-done | bytes 98336 | tf_op jit(solution)/shard_map/ppermute | solution.py:24
  50.3 0.3 shard_map.67
  50.6 0.2 abs_reduce_fusion.3
  50.8 0.1 multiply_convert_fusion.3
  50.9 0.1 broadcast_in_dim.12
  51.1 3.2 %collective-permute-start.5 = (f16[5,96,128]{2,1,0:T(8,128)(2,1)S(1)}, f16[5,96,128]{2,1,0:T(8,128)(2,1)S(1)}, u32[]{:S(2)}, u32[]{:S(2)}) collective-permute-start(f16[5,96,128]{2,1,0:T(8,128)(2,1)S(1)} %pad_maximum_fusion.1), channel_id=1, source_target_pairs={{0,4},{1,5},{2,6},{3,7},{4,0},{5,1},{6,2},{7,3},{8,12},{9,13},{10,... | collective-permute-start | bytes 368648 | tf_op jit(solution)/shard_map/ppermute | solution.py:24
  54.3 0.1 broadcast_in_dim.13
  54.4 1.1 %collective-permute-start.6 = (f16[5,96,128]{2,1,0:T(8,128)(2,1)S(1)}, f16[5,96,128]{2,1,0:T(8,128)(2,1)S(1)}, u32[]{:S(2)}, u32[]{:S(2)}) collective-permute-start(f16[5,96,128]{2,1,0:T(8,128)(2,1)S(1)} %pad_maximum_fusion.2), channel_id=1, source_target_pairs={{0,8},{1,9},{2,10},{3,11},{4,12},{5,13},{6,14},{7,15},{8,0},{9,1},... | collective-permute-start | bytes 368648 | tf_op jit(solution)/shard_map/ppermute | solution.py:24
  55.6 0.1 broadcast_in_dim.14
  55.7 1.4 %collective-permute-start.7 = (f16[5,96,128]{2,1,0:T(8,128)(2,1)S(1)}, f16[5,96,128]{2,1,0:T(8,128)(2,1)S(1)}, u32[]{:S(2)}, u32[]{:S(2)}) collective-permute-start(f16[5,96,128]{2,1,0:T(8,128)(2,1)S(1)} %pad_maximum_fusion.3), channel_id=1, source_target_pairs={{0,12},{1,13},{2,14},{3,15},{4,8},{5,9},{6,10},{7,11},{8,4},{9,5},... | collective-permute-start | bytes 368648 | tf_op jit(solution)/shard_map/ppermute | solution.py:24
  57.1 0.9 %collective-permute-done.5 = f16[5,96,128]{2,1,0:T(8,128)(2,1)S(1)} collective-permute-done((f16[5,96,128]{2,1,0:T(8,128)(2,1)S(1)}, f16[5,96,128]{2,1,0:T(8,128)(2,1)S(1)}, u32[]{:S(2)}, u32[]{:S(2)}) %collective-permute-start.5) | collective-permute-done | bytes 122912 | tf_op jit(solution)/shard_map/ppermute | solution.py:24
  58.0 8.9 %collective-permute-done.6 = f16[5,96,128]{2,1,0:T(8,128)(2,1)S(1)} collective-permute-done((f16[5,96,128]{2,1,0:T(8,128)(2,1)S(1)}, f16[5,96,128]{2,1,0:T(8,128)(2,1)S(1)}, u32[]{:S(2)}, u32[]{:S(2)}) %collective-permute-start.6) | collective-permute-done | bytes 122912 | tf_op jit(solution)/shard_map/ppermute | solution.py:24
  66.9 0.0 collective-permute-done.7
  66.9 0.7 %copy_bitcast_fusion = bf16[96,512]{1,0:T(8,128)(2,1)} fusion(f32[16,96,128]{2,1,0:T(8,128)S(1)} %shard_map.67, f16[5,96,128]{2,1,0:T(8,128)(2,1)S(1)} %collective-permute-done.7, f16[5,96,128]{2,1,0:T(8,128)(2,1)S(1)} %collective-permute-done.6, f16[5,96,128]{2,1,0:T(8,128)(2,1)S(1)} %collective-permute-done.5, f32[96,128]{1,0:T(8,128)S(1)} %exponential_bitcast_fusion.1, ...), kind=kLoop, calls=%fused_computation.22 | loop fusion | flops 491520 | bytes 737280 | tf_op jit(solution)/shard_map/convert_element_type | solution.py:299
  (10 shorter events, 0.2 us)
Async XLA Ops:
  2.5 36.7 %all-to-all-start = ((bf16[80,4,1792]{2,1,0:T(4,128)(2,1)}), bf16[80,4,1792]{2,1,0:T(4,128)(2,1)S(1)}, u32[]{:S(2)}, u32[]{:S(2)}) async-start(bf16[80,4,1792]{2,1,0:T(4,128)(2,1)} %get-tuple-element.29), calls=%async_computation | async-start | bytes 2293760 | tf_op jit(solution)/shard_map/all_to_all | solution.py:291
  9.9 29.3 %copy-start.1 = (bf16[1,8192,64]{1,2,0:T(8,128)(2,1)S(1)}, bf16[1,8192,64]{1,2,0:T(8,128)(2,1)}, u32[]{:S(2)}) copy-start(bf16[1,8192,64]{1,2,0:T(8,128)(2,1)} %param.11) | copy-start | bytes 3145732
  16.4 6.9 %collective-permute-start = (f32[32,96,128]{2,1,0:T(8,128)S(1)}, f32[32,96,128]{2,1,0:T(8,128)S(1)}, u32[]{:S(2)}, u32[]{:S(2)}) collective-permute-start(f32[32,96,128]{2,1,0:T(8,128)S(1)} %branch_1_fun.3), channel_id=1, source_target_pairs={{0,1},{1,0},{2,3},{3,2},{4,5},{5,4},{6,7},{7,6},{8,9},{9,8},{10,11... | collective-permute-start | bytes 4718600 | tf_op jit(solution)/shard_map/cond/branch_1_fun/ppermute | solution.py:24
  24.1 15.0 %collective-permute-start.1 = (f16[17,96,128]{2,1,0:T(8,128)(2,1)S(1)}, f16[17,96,128]{2,1,0:T(8,128)(2,1)S(1)}, u32[]{:S(2)}, u32[]{:S(2)}) collective-permute-start(f16[17,96,128]{2,1,0:T(8,128)(2,1)S(1)} %pad_maximum_fusion), channel_id=1, source_target_pairs={{0,2},{1,3},{2,0},{3,1},{4,6},{5,7},{6,4},{7,5},{8,10},{9,11},{10,... | collective-permute-start | bytes 1253384 | tf_op jit(solution)/shard_map/cond/branch_1_fun/ppermute | solution.py:24
  39.2 2.0 %copy-start = (bf16[1,28672,64]{1,2,0:T(8,128)(2,1)S(1)}, bf16[1,28672,64]{1,2,0:T(8,128)(2,1)}, u32[]{:S(2)}) copy-start(bf16[1,28672,64]{1,2,0:T(8,128)(2,1)} %param.10) | copy-start | bytes 11010052
  43.3 1.9 %collective-permute-start.2 = (bf16[16,24,128]{2,1,0:T(8,128)(2,1)S(1)}, bf16[16,24,128]{2,1,0:T(8,128)(2,1)S(1)}, u32[]{:S(2)}, u32[]{:S(2)}) collective-permute-start(bf16[16,24,128]{2,1,0:T(8,128)(2,1)S(1)} %get-tuple-element.32), channel_id=1, source_target_pairs={{0,1},{1,0},{2,3},{3,2},{4,5},{5,4},{6,7},{7,6},{8,9},{9,8},{10,11... | collective-permute-start | bytes 294920 | tf_op jit(solution)/shard_map/ppermute | solution.py:24
  43.4 5.7 %collective-permute-start.3 = (bf16[16,24,128]{2,1,0:T(8,128)(2,1)S(1)}, bf16[16,24,128]{2,1,0:T(8,128)(2,1)S(1)}, u32[]{:S(2)}, u32[]{:S(2)}) collective-permute-start(bf16[16,24,128]{2,1,0:T(8,128)(2,1)S(1)} %get-tuple-element.33), channel_id=1, source_target_pairs={{0,2},{1,3},{2,0},{3,1},{4,6},{5,7},{6,4},{7,5},{8,10},{9,11},{10,... | collective-permute-start | bytes 294920 | tf_op jit(solution)/shard_map/ppermute | solution.py:24
  44.8 5.5 %collective-permute-start.4 = (bf16[16,24,128]{2,1,0:T(8,128)(2,1)S(1)}, bf16[16,24,128]{2,1,0:T(8,128)(2,1)S(1)}, u32[]{:S(2)}, u32[]{:S(2)}) collective-permute-start(bf16[16,24,128]{2,1,0:T(8,128)(2,1)S(1)} %get-tuple-element.34), channel_id=1, source_target_pairs={{0,3},{1,2},{2,1},{3,0},{4,7},{5,6},{6,5},{7,4},{8,11},{9,10},{10,... | collective-permute-start | bytes 294920 | tf_op jit(solution)/shard_map/ppermute | solution.py:24
  51.1 6.9 %collective-permute-start.5 = (f16[5,96,128]{2,1,0:T(8,128)(2,1)S(1)}, f16[5,96,128]{2,1,0:T(8,128)(2,1)S(1)}, u32[]{:S(2)}, u32[]{:S(2)}) collective-permute-start(f16[5,96,128]{2,1,0:T(8,128)(2,1)S(1)} %pad_maximum_fusion.1), channel_id=1, source_target_pairs={{0,4},{1,5},{2,6},{3,7},{4,0},{5,1},{6,2},{7,3},{8,12},{9,13},{10,... | collective-permute-start | bytes 368648 | tf_op jit(solution)/shard_map/ppermute | solution.py:24
  54.4 12.4 %collective-permute-start.6 = (f16[5,96,128]{2,1,0:T(8,128)(2,1)S(1)}, f16[5,96,128]{2,1,0:T(8,128)(2,1)S(1)}, u32[]{:S(2)}, u32[]{:S(2)}) collective-permute-start(f16[5,96,128]{2,1,0:T(8,128)(2,1)S(1)} %pad_maximum_fusion.2), channel_id=1, source_target_pairs={{0,8},{1,9},{2,10},{3,11},{4,12},{5,13},{6,14},{7,15},{8,0},{9,1},... | collective-permute-start | bytes 368648 | tf_op jit(solution)/shard_map/ppermute | solution.py:24
  55.7 11.2 %collective-permute-start.7 = (f16[5,96,128]{2,1,0:T(8,128)(2,1)S(1)}, f16[5,96,128]{2,1,0:T(8,128)(2,1)S(1)}, u32[]{:S(2)}, u32[]{:S(2)}) collective-permute-start(f16[5,96,128]{2,1,0:T(8,128)(2,1)S(1)} %pad_maximum_fusion.3), channel_id=1, source_target_pairs={{0,12},{1,13},{2,14},{3,15},{4,8},{5,9},{6,10},{7,11},{8,4},{9,5},... | collective-permute-start | bytes 368648 | tf_op jit(solution)/shard_map/ppermute | solution.py:24

commit v9 on v8

--- a/solution.py
+++ b/solution.py
@@ -24,7 +24,13 @@
     return lax.ppermute(value, "tp", [(i, i ^ offset) for i in range(group)])
 
 
-def column_blocks_kernel(order_ref, hidden_ref, down_ref, out_ref, held_ref, sems):
+def column_blocks_kernel(groups, order_ref, hidden_ref, down_ref, *refs):
+    carried = len(refs) > groups + 2
+    if carried:
+        carry_in, refs = refs[0], refs[1:]
+        carry = pltpu.make_async_copy(carry_in, refs[groups], refs[-1])
+        refs = refs[:groups] + refs[groups + 1 : -1]
+    out_refs, held_ref, sems = refs[:groups], refs[groups], refs[groups + 1]
     count, depth, width = held_ref.shape
     parts = width // LANES
     pieces = sems.shape[1]
@@ -40,35 +46,50 @@
     for block in range(count):
         for piece in range(pieces):
             copy(block, piece).start()
+    if carried:
+        carry.start()
+    share = count // groups
     for block in range(count):
         for piece in range(pieces):
             copy(block, piece).wait()
         product = jnp.dot(hidden_ref[...], held_ref[block], preferred_element_type=jnp.float32)
         for lane in range(parts):
-            out_ref[block * parts + lane] = product[:, lane * LANES : (lane + 1) * LANES]
-
-
-def column_blocks(hidden, down_matrix, order, width):
+            out_refs[block // share][block % share * parts + lane] = product[
+                :, lane * LANES : (lane + 1) * LANES
+            ]
+    if carried:
+        carry.wait()
+
+
+def column_blocks(hidden, down_matrix, order, width, groups=1, carry=None):
     rows, depth = hidden.shape
     count = order.shape[0]
     pieces = 2 if depth % 32 == 0 else 1
     vmem = pl.BlockSpec(memory_space=pltpu.VMEM)
+    hbm = pl.BlockSpec(memory_space=pl.ANY)
+    out_shape = [
+        jax.ShapeDtypeStruct((count // groups * width // LANES, rows, LANES), jnp.float32)
+    ] * groups
+    operands = [order, hidden, in_hbm(down_matrix)]
+    in_specs = [pl.BlockSpec(memory_space=pltpu.SMEM), vmem, hbm]
+    scratch = [
+        pltpu.VMEM((count, depth, width), jnp.bfloat16),
+        pltpu.SemaphoreType.DMA((count, pieces)),
+    ]
+    if carry is not None:
+        out_shape.append(jax.ShapeDtypeStruct(carry.shape, carry.dtype))
+        operands.append(in_hbm(carry))
+        in_specs.append(hbm)
+        scratch.append(pltpu.SemaphoreType.DMA)
     return pl.pallas_call(
-        column_blocks_kernel,
-        out_shape=jax.ShapeDtypeStruct((count * width // LANES, rows, LANES), jnp.float32),
-        in_specs=[
-            pl.BlockSpec(memory_space=pltpu.SMEM),
-            vmem,
-            pl.BlockSpec(memory_space=pl.ANY),
-        ],
-        out_specs=vmem,
-        scratch_shapes=[
-            pltpu.VMEM((count, depth, width), jnp.bfloat16),
-            pltpu.SemaphoreType.DMA((count, pieces)),
-        ],
-        compiler_params=pltpu.CompilerParams(vmem_limit_bytes=20 * 2**20),
+        functools.partial(column_blocks_kernel, groups),
+        out_shape=out_shape,
+        in_specs=in_specs,
+        out_specs=[vmem] * len(out_shape),
+        scratch_shapes=scratch,
+        compiler_params=pltpu.CompilerParams(vmem_limit_bytes=(12 + 12 * groups) * 2**20),
         cost_estimate=pl.CostEstimate(flops=1000, bytes_accessed=1000, transcendentals=0),
-    )(order, hidden, in_hbm(down_matrix))
+    )(*operands)
 
 
 def pack_scaled(value):
@@ -84,22 +105,35 @@
     return packed[:-1].astype(jnp.float32) * jnp.exp2(exponent - F16_TOP)
 
 
-def pair_sums(hidden, down_matrix, group, order, width):
+def pair_sums(hidden, down_matrix, shrink, group, order, width):
     half = group * width // LANES // 4
     rows = hidden.shape[0]
-
-    def work():
-        odd = column_blocks(hidden, down_matrix, order[: group // 2], width)
-        odd_in = xor_permute(odd, group, 1)
-        even = column_blocks(hidden, down_matrix, order[group // 2 :], width)
-        chip = even + odd_in
-        pair_in = xor_permute(pack_scaled(chip[half:]), group, 2)
-        return chip[:half] + unpack_scaled(pair_in)
-
-    def idle():
-        return jnp.zeros((half, rows, LANES), jnp.float32)
-
-    return lax.cond(order[0] >= 0, work, idle)
+    share = group // 4
+
+    def first():
+        (far,) = column_blocks(hidden, down_matrix, order[:share], width)
+        far_in = xor_permute(far, group, 1)
+        (near,) = column_blocks(hidden, down_matrix, order[share : 2 * share], width)
+        return pack_scaled(near + far_in)
+
+    def first_idle():
+        return jnp.zeros((half + 1, rows, LANES), jnp.float16)
+
+    sent = lax.cond(order[0] >= 0, first, first_idle)
+    pair_in = xor_permute(sent, group, 2)
+    order, _ = lax.optimization_barrier((order, sent))
+
+    def second():
+        far, near, held = column_blocks(
+            hidden, down_matrix, order[2 * share :], width, groups=2, carry=shrink
+        )
+        return near + xor_permute(far, group, 1), held
+
+    def second_idle():
+        return jnp.zeros((half, rows, LANES), jnp.float32), jnp.zeros(shrink.shape, shrink.dtype)
+
+    kept, held = lax.cond(order[1] >= 0, second, second_idle)
+    return kept + unpack_scaled(pair_in), held
 
 
 def line_sums(pair, group, width):
@@ -284,14 +318,14 @@
     rows, depth = hidden.shape
     width = down_matrix.shape[1] // group
     quads = list(range(0, group, 4))
-    orders = [q + k for k in (1, 3, 0, 2) for q in quads]
+    orders = [q + k for k in (3, 2, 1, 0) for q in quads]
     packed, pick, order, kept_hidden = pack_rows(
         hidden, adapter_of_row, adapter_holder_slot, me, orders
     )
     gathered = lax.all_to_all(packed, "tp", split_axis=0, concat_axis=0, tiled=True)
-    pair = pair_sums(kept_hidden, down_matrix, group, order, width)
+    shrink = jnp.swapaxes(shrink_matrices, 1, 2)[0]
+    pair, shrink = pair_sums(kept_hidden, down_matrix, shrink, group, order, width)
     gathered, _ = lax.optimization_barrier((gathered, pair))
-    shrink = jnp.swapaxes(shrink_matrices, 1, 2)[0]
     expand = jnp.swapaxes(expand_matrices, 1, 2)[0]
     outs = adapter_output(gathered, shrink, expand, group, me)
     arrived = [outs[0]] + [xor_permute(outs[k], group, k) for k in range(1, PLANE)]

time: 67.9 us -> 64 us (0.943)
  waiting for transfers between devices: 28 us -> 18.7 us
  Pallas kernels: 17.7 us -> 24 us
  local copies, waits for them, and re-layouts: 2.42 us -> 1.07 us
    ppermute x8 -> x9, waiting for transfers between devices: 28 us -> 18.7 us  [xor_permute(): return lax.ppermute(value, 'tp', [(i, i ^ offset) for i in range(group)])]
    pallas_call x2 -> x3, Pallas kernels: 12.8 us -> 17.3 us  [column_blocks(): pl.pallas_call(functools.partial(column_blocks_kernel, groups), out_shape...]
    unnamed x4 -> x2, local copies, waits for them, and re-layouts: 2.04 us -> 0.01 us
    pallas_call x1, Pallas kernels: 2.07 us -> 3.89 us  [adapter_output(): pl.pallas_call(functools.partial(adapter_kernel, parts), out_shape=[jax.S...]
    slice x1 -> x3, local copies, waits for them, and re-layouts: 0.07 us -> 0.76 us  [the longest x1 0.61 us: pair_sums(): kept, held = lax.cond(order[1] >= 0, second, second_idle)]
    ppermute x8 -> x9, starting transfers between devices: 9.91 us -> 9.62 us  [xor_permute(): return lax.ppermute(value, 'tp', [(i, i ^ offset) for i in range(group)])]
  transfers between devices with their start and end apart: 9 -> 10, of which waited for: 5 -> 6; matrix products, arithmetic and copies ran while one was open for 2% -> 3% of each run, Pallas kernels for 19% -> 27%
where the time goes in v9:
time: 64 us; the launch traced here: 63.7 us
  Pallas kernels  24 us (38%)
  waiting for transfers between devices  18.7 us (29%)
  starting transfers between devices  17 us (27%)
  other arithmetic  1.97 us (3%)
  local copies, waits for them, and re-layouts  1.07 us (2%)
  between operations  0.85 us (1%)
    ppermute x9, waiting for transfers between devices, xor_permute(): return lax.ppermute(value, 'tp', [(i, i ^ offset) for i in range(group)])  18.7 us
    pallas_call x3, Pallas kernels, column_blocks(): pl.pallas_call(functools.partial(column_blocks_kernel, groups), out_shape...  17.3 us
    ppermute x9, starting transfers between devices, xor_permute(): return lax.ppermute(value, 'tp', [(i, i ^ offset) for i in range(group)])  9.62 us
    all_to_all x1, starting transfers between devices, shards_by_blocks(): lax.all_to_all(packed, 'tp', split_axis=0, concat_axis=0, tiled=True)  7.37 us
    pallas_call x1, Pallas kernels, adapter_output(): pl.pallas_call(functools.partial(adapter_kernel, parts), out_shape=[jax.S...  3.89 us
    pallas_call x1, Pallas kernels, pack_rows(): pl.pallas_call(functools.partial(pack_kernel, blocks, orders), out_shape=...  2.48 us
  transfers between devices with their start and end apart: 10, of which 6 were waited for; matrix products, arithmetic and copies ran while one was open for 3% of the time, Pallas kernels for 27%

profile of v9, /device:TPU:0, one launch (start us, length us, event | category | flops | bytes accessed | tf_op | source)
XLA Modules:
  0.0 63.7 jit_solution(3931161642826935898)
XLA Ops:
  0.0 2.5 %shard_map.64 = (bf16[80,4,1792]{2,1,0:T(4,128)(2,1)}, bf16[96,96]{1,0:T(8,128)(2,1)S(1)}, s32[16]{0:T(128)S(1)}, bf16[96,1792]{1,0:T(8,128)(2,1)S(1)}) custom-call(s32[1]{0:T(128)} %bitcast.1.me_ref, s32[16]{0:T(128)} %slot_hbm.1, s32[1,96]{1,0:T(1,128)} %bitcast.28, bf16[96,1792]{1,0:T(8,128)(2,1)} %hidden_hbm.1), custom_call_target="tpu_custom_call" | custom-call | tf_op jit(solution)/shard_map/pallas_call | solution.py:208
  2.5 7.4 %all-to-all-start = ((bf16[80,4,1792]{2,1,0:T(4,128)(2,1)}), bf16[80,4,1792]{2,1,0:T(4,128)(2,1)S(1)}, u32[]{:S(2)}, u32[]{:S(2)}) async-start(bf16[80,4,1792]{2,1,0:T(4,128)(2,1)} %get-tuple-element.50), calls=%async_computation | async-start | bytes 2293760 | tf_op jit(solution)/shard_map/all_to_all | solution.py:325
  9.9 9.6 %conditional.2 = (f16[17,96,128]{2,1,0:T(8,128)(2,1)S(1)}) conditional(s32[]{:T(128)} %bitcast.3, () %tuple.21, (s32[16]{0:T(128)S(1)}, bf16[96,1792]{1,0:T(8,128)(2,1)S(1)}, bf16[1792,8192]{1,0:T(8,128)(2,1)}) %tuple.22), branch_computations={%region_0.0_spmd, %region_1.0_spmd} | conditional | flops 1194416 | bytes 7548864 | solution.py:122
  9.9 0.1 fusion.8
  10.0 4.2 %branch_1_fun.4 = f32[16,96,128]{2,1,0:T(8,128)S(1)} custom-call(s32[4]{0:T(128)S(1)} %get-tuple-element.64.order_ref, bf16[96,1792]{1,0:T(8,128)(2,1)S(1)} %get-tuple-element.24.hidden_ref, bf16[1792,8192]{1,0:T(8,128)(2,1)} %get-tuple-element.25.down_ref), custom_call_target="tpu_custom_call" | custom-call | flops 1000 | bytes 1000 | tf_op jit(solution)/shard_map/cond/branch_1_fun/pallas_call | solution.py:84
  14.2 0.5 collective-permute-start.1
  14.7 4.2 %branch_1_fun.3 = f32[16,96,128]{2,1,0:T(8,128)S(1)} custom-call(s32[4]{0:T(128)S(1)} %get-tuple-element.65.order_ref, bf16[96,1792]{1,0:T(8,128)(2,1)S(1)} %get-tuple-element.24.hidden_ref, bf16[1792,8192]{1,0:T(8,128)(2,1)} %get-tuple-element.25.down_ref), custom_call_target="tpu_custom_call" | custom-call | flops 1000 | bytes 1000 | tf_op jit(solution)/shard_map/cond/branch_1_fun/pallas_call | solution.py:84
  18.9 0.0 collective-permute-done.1
  18.9 0.2 abs_reduce_fusion
  19.1 0.2 multiply_convert_fusion
  19.3 0.1 broadcast_in_dim.8
  19.4 0.1 pad_maximum_fusion
  19.5 1.7 %collective-permute-start.2 = (f16[17,96,128]{2,1,0:T(8,128)(2,1)S(1)}, f16[17,96,128]{2,1,0:T(8,128)(2,1)S(1)}, u32[]{:S(2)}, u32[]{:S(2)}) collective-permute-start(f16[17,96,128]{2,1,0:T(8,128)(2,1)S(1)} %get-tuple-element.81), channel_id=1, source_target_pairs={{0,2},{1,3},{2,0},{3,1},{4,6},{5,7},{6,4},{7,5},{8,10},{9,11},{10,... | collective-permute-start | bytes 1253384 | tf_op jit(solution)/shard_map/ppermute | solution.py:24
  21.2 0.6 slice.52
  22.5 0.0 copy-start
  22.5 11.5 %conditional.3 = (f32[16,96,128]{2,1,0:T(8,128)S(1)}, bf16[64,28672]{1,0:T(8,128)(2,1)}) conditional(s32[]{:T(128)} %bitcast.4, () %tuple.24, (s32[16]{0:T(128)S(1)}, bf16[1,64,28672]{2,1,0:T(8,128)(2,1)}, bf16[96,1792]{1,0:T(8,128)(2,1)S(1)}, bf16[1792,8192]{1,0:T(8,128)(2,1)}) %tuple.43), branch_computations={%region_3.0_spmd, %region_4.0_spmd} | conditional | flops 197608 | bytes 5506144 | solution.py:135
  22.5 0.1 slice.36.order_ref
  22.6 8.9 %branch_1_fun.5 = (f32[16,96,128]{2,1,0:T(8,128)S(1)}, f32[16,96,128]{2,1,0:T(8,128)S(1)}, bf16[64,28672]{1,0:T(8,128)(2,1)}) custom-call(s32[8]{0:T(128)S(1)} %slice.36.order_ref, bf16[96,1792]{1,0:T(8,128)(2,1)S(1)} %get-tuple-element.27.hidden_ref, bf16[1792,8192]{1,0:T(8,128)(2,1)} %get-tuple-element.28.down_ref, bf16[64,28672]{1,0:T(8,128)(2,1)} %bitcast.26), custom_call_target="tpu_custom_call" | custom-call | flops 1000 | bytes 1000 | tf_op jit(solution)/shard_map/cond/branch_1_fun/pallas_call | solution.py:84
  31.5 0.1 collective-permute-start
  31.7 2.2 %collective-permute-done = f32[16,96,128]{2,1,0:T(8,128)S(1)} collective-permute-done((f32[16,96,128]{2,1,0:T(8,128)S(1)}, f32[16,96,128]{2,1,0:T(8,128)S(1)}, u32[]{:S(2)}, u32[]{:S(2)}) %collective-permute-start) | collective-permute-done | bytes 786464 | tf_op jit(solution)/shard_map/cond/branch_1_fun/ppermute | solution.py:24
  33.9 0.1 add.17
  34.0 2.4 %collective-permute-done.2 = f16[17,96,128]{2,1,0:T(8,128)(2,1)S(1)} collective-permute-done((f16[17,96,128]{2,1,0:T(8,128)(2,1)S(1)}, f16[17,96,128]{2,1,0:T(8,128)(2,1)S(1)}, u32[]{:S(2)}, u32[]{:S(2)}) %collective-permute-start.2) | collective-permute-done | bytes 417824 | tf_op jit(solution)/shard_map/ppermute | solution.py:24
  36.5 0.1 multiply_add_fusion.pair_ref
  36.6 0.0 all-to-all-done.rows_ref
  36.6 0.0 copy-done
  36.6 3.9 %shard_map.65 = (bf16[16,24,128]{2,1,0:T(8,128)(2,1)S(1)}, bf16[16,24,128]{2,1,0:T(8,128)(2,1)S(1)}, bf16[16,24,128]{2,1,0:T(8,128)(2,1)S(1)}, bf16[16,24,128]{2,1,0:T(8,128)(2,1)S(1)}) custom-call(s32[1]{0:T(128)} %bitcast.1.me_ref, bf16[80,4,1792]{2,1,0:T(4,128)(2,1)S(1)} %all-to-all-done.rows_ref, bf16[64,28672]{1,0:T(8,128)(2,1)} %get-tuple-element.52.shrink_ref, ...), custom_call_target="tpu_custom_call" | custom-call | tf_op jit(solution)/shard_map/pallas_call | solution.py:273
  40.5 0.1 collective-permute-start.3
  40.6 1.9 %collective-permute-start.4 = (bf16[16,24,128]{2,1,0:T(8,128)(2,1)S(1)}, bf16[16,24,128]{2,1,0:T(8,128)(2,1)S(1)}, u32[]{:S(2)}, u32[]{:S(2)}) collective-permute-start(bf16[16,24,128]{2,1,0:T(8,128)(2,1)S(1)} %get-tuple-element.55), channel_id=1, source_target_pairs={{0,2},{1,3},{2,0},{3,1},{4,6},{5,7},{6,4},{7,5},{8,10},{9,11},{10,... | collective-permute-start | bytes 294920 | tf_op jit(solution)/shard_map/ppermute | solution.py:24
  42.5 0.1 collective-permute-start.5
  42.6 0.0 collective-permute-done.3.refs_1_
  42.6 3.6 %collective-permute-done.4.refs_2_ = bf16[16,24,128]{2,1,0:T(8,128)(2,1)S(1)} collective-permute-done((bf16[16,24,128]{2,1,0:T(8,128)(2,1)S(1)}, bf16[16,24,128]{2,1,0:T(8,128)(2,1)S(1)}, u32[]{:S(2)}, u32[]{:S(2)}) %collective-permute-start.4) | collective-permute-done | bytes 98336 | tf_op jit(solution)/shard_map/ppermute | solution.py:24
  46.2 1.4 %collective-permute-done.5.refs_3_ = bf16[16,24,128]{2,1,0:T(8,128)(2,1)S(1)} collective-permute-done((bf16[16,24,128]{2,1,0:T(8,128)(2,1)S(1)}, bf16[16,24,128]{2,1,0:T(8,128)(2,1)S(1)}, u32[]{:S(2)}, u32[]{:S(2)}) %collective-permute-start.5) | collective-permute-done | bytes 98336 | tf_op jit(solution)/shard_map/ppermute | solution.py:24
  47.7 0.3 shard_map.66
  48.0 0.2 abs_reduce_fusion.3
  48.2 0.1 multiply_convert_fusion.3
  48.3 0.1 broadcast_in_dim.12
  48.4 2.1 %collective-permute-start.6 = (f16[5,96,128]{2,1,0:T(8,128)(2,1)S(1)}, f16[5,96,128]{2,1,0:T(8,128)(2,1)S(1)}, u32[]{:S(2)}, u32[]{:S(2)}) collective-permute-start(f16[5,96,128]{2,1,0:T(8,128)(2,1)S(1)} %pad_maximum_fusion.1), channel_id=1, source_target_pairs={{0,4},{1,5},{2,6},{3,7},{4,0},{5,1},{6,2},{7,3},{8,12},{9,13},{10,... | collective-permute-start | bytes 368648 | tf_op jit(solution)/shard_map/ppermute | solution.py:24
  50.6 0.1 broadcast_in_dim.13
  50.7 1.5 %collective-permute-start.7 = (f16[5,96,128]{2,1,0:T(8,128)(2,1)S(1)}, f16[5,96,128]{2,1,0:T(8,128)(2,1)S(1)}, u32[]{:S(2)}, u32[]{:S(2)}) collective-permute-start(f16[5,96,128]{2,1,0:T(8,128)(2,1)S(1)} %pad_maximum_fusion.2), channel_id=1, source_target_pairs={{0,8},{1,9},{2,10},{3,11},{4,12},{5,13},{6,14},{7,15},{8,0},{9,1},... | collective-permute-start | bytes 368648 | tf_op jit(solution)/shard_map/ppermute | solution.py:24
  52.2 0.1 broadcast_in_dim.14
  52.4 1.5 %collective-permute-start.8 = (f16[5,96,128]{2,1,0:T(8,128)(2,1)S(1)}, f16[5,96,128]{2,1,0:T(8,128)(2,1)S(1)}, u32[]{:S(2)}, u32[]{:S(2)}) collective-permute-start(f16[5,96,128]{2,1,0:T(8,128)(2,1)S(1)} %pad_maximum_fusion.3), channel_id=1, source_target_pairs={{0,12},{1,13},{2,14},{3,15},{4,8},{5,9},{6,10},{7,11},{8,4},{9,5},... | collective-permute-start | bytes 368648 | tf_op jit(solution)/shard_map/ppermute | solution.py:24
  53.9 0.5 collective-permute-done.6
  54.4 8.5 %collective-permute-done.7 = f16[5,96,128]{2,1,0:T(8,128)(2,1)S(1)} collective-permute-done((f16[5,96,128]{2,1,0:T(8,128)(2,1)S(1)}, f16[5,96,128]{2,1,0:T(8,128)(2,1)S(1)}, u32[]{:S(2)}, u32[]{:S(2)}) %collective-permute-start.7) | collective-permute-done | bytes 122912 | tf_op jit(solution)/shard_map/ppermute | solution.py:24
  62.9 0.0 collective-permute-done.8
  63.0 0.7 %copy_bitcast_fusion = bf16[96,512]{1,0:T(8,128)(2,1)} fusion(f32[16,96,128]{2,1,0:T(8,128)S(1)} %shard_map.66, f16[5,96,128]{2,1,0:T(8,128)(2,1)S(1)} %collective-permute-done.8, f16[5,96,128]{2,1,0:T(8,128)(2,1)S(1)} %collective-permute-done.7, f16[5,96,128]{2,1,0:T(8,128)(2,1)S(1)} %collective-permute-done.6, f32[96,128]{1,0:T(8,128)S(1)} %exponential_bitcast_fusion, ...), kind=kLoop, calls=%fused_computation.21 | loop fusion | flops 491520 | bytes 737280 | tf_op jit(solution)/shard_map/convert_element_type | solution.py:333
  (10 shorter events, 0.2 us)
Async XLA Ops:
  2.5 34.1 %all-to-all-start = ((bf16[80,4,1792]{2,1,0:T(4,128)(2,1)}), bf16[80,4,1792]{2,1,0:T(4,128)(2,1)S(1)}, u32[]{:S(2)}, u32[]{:S(2)}) async-start(bf16[80,4,1792]{2,1,0:T(4,128)(2,1)} %get-tuple-element.50), calls=%async_computation | async-start | bytes 2293760 | tf_op jit(solution)/shard_map/all_to_all | solution.py:325
  14.2 4.7 %collective-permute-start.1 = (f32[16,96,128]{2,1,0:T(8,128)S(1)}, f32[16,96,128]{2,1,0:T(8,128)S(1)}, u32[]{:S(2)}, u32[]{:S(2)}) collective-permute-start(f32[16,96,128]{2,1,0:T(8,128)S(1)} %branch_1_fun.4), channel_id=1, source_target_pairs={{0,1},{1,0},{2,3},{3,2},{4,5},{5,4},{6,7},{7,6},{8,9},{9,8},{10,11... | collective-permute-start | bytes 2359304 | tf_op jit(solution)/shard_map/cond/branch_1_fun/ppermute | solution.py:24
  19.5 16.9 %collective-permute-start.2 = (f16[17,96,128]{2,1,0:T(8,128)(2,1)S(1)}, f16[17,96,128]{2,1,0:T(8,128)(2,1)S(1)}, u32[]{:S(2)}, u32[]{:S(2)}) collective-permute-start(f16[17,96,128]{2,1,0:T(8,128)(2,1)S(1)} %get-tuple-element.81), channel_id=1, source_target_pairs={{0,2},{1,3},{2,0},{3,1},{4,6},{5,7},{6,4},{7,5},{8,10},{9,11},{10,... | collective-permute-start | bytes 1253384 | tf_op jit(solution)/shard_map/ppermute | solution.py:24
  22.5 14.1 %copy-start = (bf16[1,8192,64]{1,2,0:T(8,128)(2,1)S(1)}, bf16[1,8192,64]{1,2,0:T(8,128)(2,1)}, u32[]{:S(2)}) copy-start(bf16[1,8192,64]{1,2,0:T(8,128)(2,1)} %param.13) | copy-start | bytes 3145732
  31.5 2.4 %collective-permute-start = (f32[16,96,128]{2,1,0:T(8,128)S(1)}, f32[16,96,128]{2,1,0:T(8,128)S(1)}, u32[]{:S(2)}, u32[]{:S(2)}) collective-permute-start(f32[16,96,128]{2,1,0:T(8,128)S(1)} %get-tuple-element.31), channel_id=1, source_target_pairs={{0,1},{1,0},{2,3},{3,2},{4,5},{5,4},{6,7},{7,6},{8,9},{9,8},{10,11... | collective-permute-start | bytes 2359304 | tf_op jit(solution)/shard_map/cond/branch_1_fun/ppermute | solution.py:24
  40.5 2.1 %collective-permute-start.3 = (bf16[16,24,128]{2,1,0:T(8,128)(2,1)S(1)}, bf16[16,24,128]{2,1,0:T(8,128)(2,1)S(1)}, u32[]{:S(2)}, u32[]{:S(2)}) collective-permute-start(bf16[16,24,128]{2,1,0:T(8,128)(2,1)S(1)} %get-tuple-element.54), channel_id=1, source_target_pairs={{0,1},{1,0},{2,3},{3,2},{4,5},{5,4},{6,7},{7,6},{8,9},{9,8},{10,11... | collective-permute-start | bytes 294920 | tf_op jit(solution)/shard_map/ppermute | solution.py:24
  40.6 5.7 %collective-permute-start.4 = (bf16[16,24,128]{2,1,0:T(8,128)(2,1)S(1)}, bf16[16,24,128]{2,1,0:T(8,128)(2,1)S(1)}, u32[]{:S(2)}, u32[]{:S(2)}) collective-permute-start(bf16[16,24,128]{2,1,0:T(8,128)(2,1)S(1)} %get-tuple-element.55), channel_id=1, source_target_pairs={{0,2},{1,3},{2,0},{3,1},{4,6},{5,7},{6,4},{7,5},{8,10},{9,11},{10,... | collective-permute-start | bytes 294920 | tf_op jit(solution)/shard_map/ppermute | solution.py:24
  42.5 5.2 %collective-permute-start.5 = (bf16[16,24,128]{2,1,0:T(8,128)(2,1)S(1)}, bf16[16,24,128]{2,1,0:T(8,128)(2,1)S(1)}, u32[]{:S(2)}, u32[]{:S(2)}) collective-permute-start(bf16[16,24,128]{2,1,0:T(8,128)(2,1)S(1)} %get-tuple-element.56), channel_id=1, source_target_pairs={{0,3},{1,2},{2,1},{3,0},{4,7},{5,6},{6,5},{7,4},{8,11},{9,10},{10,... | collective-permute-start | bytes 294920 | tf_op jit(solution)/shard_map/ppermute | solution.py:24
  48.4 5.9 %collective-permute-start.6 = (f16[5,96,128]{2,1,0:T(8,128)(2,1)S(1)}, f16[5,96,128]{2,1,0:T(8,128)(2,1)S(1)}, u32[]{:S(2)}, u32[]{:S(2)}) collective-permute-start(f16[5,96,128]{2,1,0:T(8,128)(2,1)S(1)} %pad_maximum_fusion.1), channel_id=1, source_target_pairs={{0,4},{1,5},{2,6},{3,7},{4,0},{5,1},{6,2},{7,3},{8,12},{9,13},{10,... | collective-permute-start | bytes 368648 | tf_op jit(solution)/shard_map/ppermute | solution.py:24
  50.7 12.2 %collective-permute-start.7 = (f16[5,96,128]{2,1,0:T(8,128)(2,1)S(1)}, f16[5,96,128]{2,1,0:T(8,128)(2,1)S(1)}, u32[]{:S(2)}, u32[]{:S(2)}) collective-permute-start(f16[5,96,128]{2,1,0:T(8,128)(2,1)S(1)} %pad_maximum_fusion.2), channel_id=1, source_target_pairs={{0,8},{1,9},{2,10},{3,11},{4,12},{5,13},{6,14},{7,15},{8,0},{9,1},... | collective-permute-start | bytes 368648 | tf_op jit(solution)/shard_map/ppermute | solution.py:24
  52.4 10.6 %collective-permute-start.8 = (f16[5,96,128]{2,1,0:T(8,128)(2,1)S(1)}, f16[5,96,128]{2,1,0:T(8,128)(2,1)S(1)}, u32[]{:S(2)}, u32[]{:S(2)}) collective-permute-start(f16[5,96,128]{2,1,0:T(8,128)(2,1)S(1)} %pad_maximum_fusion.3), channel_id=1, source_target_pairs={{0,12},{1,13},{2,14},{3,15},{4,8},{5,9},{6,10},{7,11},{8,4},{9,5},... | collective-permute-start | bytes 368648 | tf_op jit(solution)/shard_map/ppermute | solution.py:24

commit v10 on v8

--- a/solution.py
+++ b/solution.py
@@ -24,7 +24,8 @@
     return lax.ppermute(value, "tp", [(i, i ^ offset) for i in range(group)])
 
 
-def column_blocks_kernel(order_ref, hidden_ref, down_ref, out_ref, held_ref, sems):
+def column_blocks_kernel(groups, order_ref, hidden_ref, down_ref, *refs):
+    out_refs, held_ref, sems = refs[:groups], refs[groups], refs[groups + 1]
     count, depth, width = held_ref.shape
     parts = width // LANES
     pieces = sems.shape[1]
@@ -40,33 +41,37 @@
     for block in range(count):
         for piece in range(pieces):
             copy(block, piece).start()
+    share = count // groups
     for block in range(count):
         for piece in range(pieces):
             copy(block, piece).wait()
         product = jnp.dot(hidden_ref[...], held_ref[block], preferred_element_type=jnp.float32)
         for lane in range(parts):
-            out_ref[block * parts + lane] = product[:, lane * LANES : (lane + 1) * LANES]
-
-
-def column_blocks(hidden, down_matrix, order, width):
+            out_refs[block // share][block % share * parts + lane] = product[
+                :, lane * LANES : (lane + 1) * LANES
+            ]
+
+
+def column_blocks(hidden, down_matrix, order, width, groups=1):
     rows, depth = hidden.shape
     count = order.shape[0]
     pieces = 2 if depth % 32 == 0 else 1
     vmem = pl.BlockSpec(memory_space=pltpu.VMEM)
+    out = jax.ShapeDtypeStruct((count // groups * width // LANES, rows, LANES), jnp.float32)
     return pl.pallas_call(
-        column_blocks_kernel,
-        out_shape=jax.ShapeDtypeStruct((count * width // LANES, rows, LANES), jnp.float32),
+        functools.partial(column_blocks_kernel, groups),
+        out_shape=[out] * groups,
         in_specs=[
             pl.BlockSpec(memory_space=pltpu.SMEM),
             vmem,
             pl.BlockSpec(memory_space=pl.ANY),
         ],
-        out_specs=vmem,
+        out_specs=[vmem] * groups,
         scratch_shapes=[
             pltpu.VMEM((count, depth, width), jnp.bfloat16),
             pltpu.SemaphoreType.DMA((count, pieces)),
         ],
-        compiler_params=pltpu.CompilerParams(vmem_limit_bytes=20 * 2**20),
+        compiler_params=pltpu.CompilerParams(vmem_limit_bytes=(12 + 12 * groups) * 2**20),
         cost_estimate=pl.CostEstimate(flops=1000, bytes_accessed=1000, transcendentals=0),
     )(order, hidden, in_hbm(down_matrix))
 
@@ -87,19 +92,33 @@
 def pair_sums(hidden, down_matrix, group, order, width):
     half = group * width // LANES // 4
     rows = hidden.shape[0]
-
-    def work():
-        odd = column_blocks(hidden, down_matrix, order[: group // 2], width)
-        odd_in = xor_permute(odd, group, 1)
-        even = column_blocks(hidden, down_matrix, order[group // 2 :], width)
-        chip = even + odd_in
-        pair_in = xor_permute(pack_scaled(chip[half:]), group, 2)
-        return chip[:half] + unpack_scaled(pair_in)
+    share = group // 4
+
+    def first():
+        (far,) = column_blocks(hidden, down_matrix, order[:share], width)
+        far_in = xor_permute(far, group, 1)
+        (near,) = column_blocks(hidden, down_matrix, order[share : 2 * share], width)
+        return pack_scaled(near + far_in)
+
+    def first_idle():
+        return jnp.zeros((half + 1, rows, LANES), jnp.float16)
+
+    def whole():
+        sent = lax.cond(order[1] >= 0, first, first_idle)
+        pair_in = xor_permute(sent, group, 2)
+        later, _ = lax.optimization_barrier((order, sent))
+
+        def second():
+            far, near = column_blocks(hidden, down_matrix, later[2 * share :], width, groups=2)
+            return near + xor_permute(far, group, 1)
+
+        kept = lax.cond(later[2] >= 0, second, idle)
+        return kept + unpack_scaled(pair_in)
 
     def idle():
         return jnp.zeros((half, rows, LANES), jnp.float32)
 
-    return lax.cond(order[0] >= 0, work, idle)
+    return lax.cond(order[0] >= 0, whole, idle)
 
 
 def line_sums(pair, group, width):
@@ -116,32 +135,24 @@
 
 
 def pack_kernel(
-    blocks,
-    orders,
-    me_ref,
-    slot_hbm,
-    adapter_hbm,
-    hidden_hbm,
-    packed_ref,
-    pick_ref,
-    order_ref,
-    kept_ref,
-    slot_ref,
-    adapter_ref,
-    hidden_ref,
-    sems,
+    blocks, orders, me_ref, slot_hbm, adapter_hbm, hidden_hbm, other_hbm, *refs
 ):
+    chips = len(refs) - 8
+    packed_refs = refs[:chips]
+    pick_ref, order_ref, kept_ref, slot_ref, adapter_ref, hidden_ref, other_ref, sems = refs[chips:]
     rows = hidden_ref.shape[0]
     group = slot_ref.shape[0]
+    me = me_ref[0]
     copies = [
         pltpu.make_async_copy(slot_hbm, slot_ref, sems.at[0]),
         pltpu.make_async_copy(adapter_hbm, adapter_ref, sems.at[1]),
         pltpu.make_async_copy(hidden_hbm, hidden_ref, sems.at[2]),
+        pltpu.make_async_copy(other_hbm, other_ref, sems.at[3]),
     ]
     for copy in copies:
         copy.start()
     for i, offset in enumerate(orders):
-        order_ref[i] = me_ref[0] ^ offset
+        order_ref[i] = me ^ offset
     ids = lax.broadcasted_iota(jnp.int32, (group, 1), 0)
     slots = jnp.zeros((group, 1), jnp.int32)
     copies[0].wait()
@@ -150,106 +161,128 @@
     copies[1].wait()
     adapter = adapter_ref[...]
     first = jnp.sum((adapter < ids).astype(jnp.int32), axis=1, keepdims=True)
-    shift = jnp.where(adapter == ids, slots * (blocks * BLOCK) - first, 0)
-    place = jnp.sum(shift, axis=0, keepdims=True) + lax.broadcasted_iota(jnp.int32, (1, rows), 1)
-    spots = lax.broadcasted_iota(jnp.int32, (group * blocks * BLOCK, rows), 0)
-    pick = jnp.where(spots == place, 1.0, 0.0).astype(jnp.bfloat16)
+    offset = jnp.sum(jnp.where(adapter == ids, slots ^ me, 0), axis=0, keepdims=True)
+    first = jnp.sum(jnp.where(adapter == ids, first, 0), axis=0, keepdims=True)
+    index = lax.broadcasted_iota(jnp.int32, (1, rows), 1) - first
     for k in range(PLANE):
         line = lax.broadcasted_iota(jnp.int32, (HELD, rows), 0)
-        mine = (line + (me_ref[0] ^ k) * (blocks * BLOCK) == place) & (line < blocks * BLOCK)
+        mine = (offset == k) & (index == line)
         pick_ref[k * HELD : (k + 1) * HELD] = jnp.where(mine, 1.0, 0.0).astype(jnp.bfloat16)
-    copies[2].wait()
-    packed = jnp.dot(pick, hidden_ref[...], preferred_element_type=jnp.float32)
-    packed_ref[...] = packed.astype(jnp.bfloat16).reshape(packed_ref.shape)
+    held = blocks * BLOCK
+    place = jnp.where((offset & 1) == 0, (offset >> 1) * held + index, -1)
+    spots = lax.broadcasted_iota(jnp.int32, (chips * held, rows), 0)
+    pick = jnp.where(spots == place, 1.0, 0.0).astype(jnp.bfloat16)
+    for source, source_ref in enumerate((hidden_ref, other_ref)):
+        copies[2 + source].wait()
+        packed = jnp.dot(pick, source_ref[...], preferred_element_type=jnp.float32)
+        packed = packed.astype(jnp.bfloat16).reshape(chips * blocks, BLOCK, packed.shape[1])
+        for chip in range(chips):
+            packed_refs[chip][source * blocks : (source + 1) * blocks] = packed[
+                chip * blocks : (chip + 1) * blocks
+            ]
     kept_ref[...] = hidden_ref[...]
 
 
-def pack_rows(hidden, adapter_of_row, adapter_holder_slot, me, orders):
+def pack_rows(hidden, other, adapter_of_row, adapter_holder_slot, me, orders):
     rows, depth = hidden.shape
     group = adapter_holder_slot.shape[0]
     blocks = MOST // BLOCK
+    chips = group // 2
     vmem = pl.BlockSpec(memory_space=pltpu.VMEM)
     smem = pl.BlockSpec(memory_space=pltpu.SMEM)
-    anywhere = pl.BlockSpec(memory_space=pltpu.HBM)
+    anywhere = pl.BlockSpec(memory_space=pl.ANY)
     return pl.pallas_call(
         functools.partial(pack_kernel, blocks, orders),
-        out_shape=(
-            jax.ShapeDtypeStruct((group * blocks, BLOCK, depth), jnp.bfloat16),
+        out_shape=[jax.ShapeDtypeStruct((2 * blocks, BLOCK, depth), jnp.bfloat16)] * chips
+        + [
             jax.ShapeDtypeStruct((PLANE * HELD, rows), jnp.bfloat16),
             jax.ShapeDtypeStruct((len(orders),), jnp.int32),
             jax.ShapeDtypeStruct((rows, depth), jnp.bfloat16),
-        ),
-        in_specs=[smem, anywhere, anywhere, anywhere],
-        out_specs=(vmem, vmem, smem, vmem),
+        ],
+        in_specs=[smem] + [anywhere] * 4,
+        out_specs=[vmem] * (chips + 1) + [smem, vmem],
         scratch_shapes=[
             pltpu.SMEM((group,), jnp.int32),
             pltpu.VMEM((1, rows), jnp.int32),
             pltpu.VMEM((rows, depth), jnp.bfloat16),
-            pltpu.SemaphoreType.DMA((3,)),
+            pltpu.VMEM((rows, depth), jnp.bfloat16),
+            pltpu.SemaphoreType.DMA((4,)),
         ],
         compiler_params=pltpu.CompilerParams(vmem_limit_bytes=24 * 2**20),
-    )(me.reshape(1), in_hbm(adapter_holder_slot), in_hbm(adapter_of_row.reshape(1, rows)), in_hbm(hidden))
-
-
-def adapter_kernel(parts, me_ref, rows_ref, shrink_ref, expand_ref, *refs):
-    out_refs, total_ref = refs[:PLANE], refs[PLANE]
-    step = pl.program_id(0)
-    block, depth = rows_ref.shape[1:]
+    )(
+        me.reshape(1),
+        in_hbm(adapter_holder_slot),
+        in_hbm(adapter_of_row.reshape(1, rows)),
+        in_hbm(hidden),
+        other,
+    )
+
+
+def adapter_kernel(parts, chips, me_ref, *refs):
+    row_refs, (shrink_hbm, expand_hbm) = refs[:chips], refs[chips : chips + 2]
+    out_refs = refs[chips + 2 : chips + 2 + PLANE]
+    shrink_ref, expand_ref, total_ref, sems, expand_sem = refs[chips + 2 + PLANE :]
+    me = me_ref[0]
+    block, depth = row_refs[0].shape[1:]
     blocks = MOST // BLOCK
-    sources = rows_ref.shape[0] // blocks
+
+    def copy(source):
+        start = pl.multiple_of((me ^ source) * depth, LANES)
+        return pltpu.make_async_copy(
+            shrink_hbm.at[:, pl.ds(start, depth)], shrink_ref.at[source], sems.at[source]
+        )
+
+    for source in range(2 * chips):
+        copy(source).start()
+    expand_copy = pltpu.make_async_copy(expand_hbm, expand_ref, expand_sem)
+    expand_copy.start()
     total = jnp.zeros((MOST, total_ref.shape[1]), jnp.float32)
-    for source in range(sources):
-        own = rows_ref[source * blocks : (source + 1) * blocks].reshape(MOST, depth)
+    for source in range(2 * chips):
+        copy(source).wait()
+        part = source % 2
+        own = row_refs[source // 2][part * blocks : (part + 1) * blocks].reshape(MOST, depth)
         total += lax.dot_general(
-            own,
-            shrink_ref[:, source * depth : (source + 1) * depth],
-            (((1,), (1,)), ((), ())),
-            preferred_element_type=jnp.float32,
-        )
-
-    @pl.when(step == 0)
-    def _():
-        total_ref[...] = jnp.zeros_like(total_ref)
-
-    total_ref[:MOST] += total
-
-    @pl.when(step == pl.num_programs(0) - 1)
-    def _():
-        rank_rows = total_ref[...].astype(jnp.bfloat16)
-        width = parts * LANES
-        for k in range(PLANE):
-            for line in range(out_refs[k].shape[0] // parts):
-                target = me_ref[0] ^ (PLANE * line + k)
-                columns = pl.ds(pl.multiple_of(target * width, LANES), width)
-                piece = jnp.dot(rank_rows, expand_ref[:, columns], preferred_element_type=jnp.float32)
-                piece = piece.astype(jnp.bfloat16)
-                for part in range(parts):
-                    out_refs[k][line * parts + part] = piece[:, part * LANES : (part + 1) * LANES]
+            own, shrink_ref[source], (((1,), (1,)), ((), ())), preferred_element_type=jnp.float32
+        )
+    total_ref[...] = jnp.zeros_like(total_ref)
+    total_ref[:MOST] = total
+    rank_rows = total_ref[...].astype(jnp.bfloat16)
+    expand_copy.wait()
+    width = parts * LANES
+    for k in range(PLANE):
+        for line in range(out_refs[k].shape[0] // parts):
+            target = me ^ (PLANE * line + k)
+            columns = pl.ds(pl.multiple_of(target * width, LANES), width)
+            piece = jnp.dot(rank_rows, expand_ref[:, columns], preferred_element_type=jnp.float32)
+            piece = piece.astype(jnp.bfloat16)
+            for part in range(parts):
+                out_refs[k][line * parts + part] = piece[:, part * LANES : (part + 1) * LANES]
 
 
 def adapter_output(gathered, shrink, expand, group, me):
-    rank, hidden_width = shrink.shape
+    rank = shrink.shape[0]
     model_width = expand.shape[1]
-    depth = gathered.shape[2]
-    blocks = MOST // BLOCK
+    depth = gathered[0].shape[2]
     parts = model_width // group // LANES
     held = (model_width // PLANE // LANES, HELD, LANES)
-    steps = 4
-    sources = group // steps
+    vmem = pl.BlockSpec(memory_space=pltpu.VMEM)
+    anywhere = pl.BlockSpec(memory_space=pl.ANY)
     return pl.pallas_call(
-        functools.partial(adapter_kernel, parts),
+        functools.partial(adapter_kernel, parts, group // 2),
         out_shape=[jax.ShapeDtypeStruct(held, jnp.bfloat16)] * PLANE,
-        grid=(steps,),
-        in_specs=[
-            pl.BlockSpec(memory_space=pltpu.SMEM),
-            pl.BlockSpec((sources * blocks, BLOCK, depth), lambda i: (i, 0, 0)),
-            pl.BlockSpec((rank, sources * depth), lambda i: (0, i)),
-            pl.BlockSpec((rank, model_width), lambda i: (0, 0)),
-        ],
-        out_specs=[pl.BlockSpec(held, lambda i: (0, 0, 0))] * PLANE,
-        scratch_shapes=[pltpu.VMEM((HELD, rank), jnp.float32)],
+        in_specs=[pl.BlockSpec(memory_space=pltpu.SMEM)]
+        + [vmem] * len(gathered)
+        + [anywhere] * 2,
+        out_specs=[vmem] * PLANE,
+        scratch_shapes=[
+            pltpu.VMEM((group, rank, depth), jnp.bfloat16),
+            pltpu.VMEM((rank, model_width), jnp.bfloat16),
+            pltpu.VMEM((HELD, rank), jnp.float32),
+            pltpu.SemaphoreType.DMA((group,)),
+            pltpu.SemaphoreType.DMA,
+        ],
         compiler_params=pltpu.CompilerParams(vmem_limit_bytes=24 * 2**20),
-    )(me.reshape(1), gathered, shrink, expand)
+    )(me.reshape(1), *gathered, in_hbm(shrink), in_hbm(expand))
 
 
 def merge_kernel(pair_ref, pick_ref, *refs):
@@ -284,11 +317,13 @@
     rows, depth = hidden.shape
     width = down_matrix.shape[1] // group
     quads = list(range(0, group, 4))
-    orders = [q + k for k in (1, 3, 0, 2) for q in quads]
-    packed, pick, order, kept_hidden = pack_rows(
-        hidden, adapter_of_row, adapter_holder_slot, me, orders
-    )
-    gathered = lax.all_to_all(packed, "tp", split_axis=0, concat_axis=0, tiled=True)
+    orders = [q + k for k in (3, 2, 1, 0) for q in quads]
+    chips = group // 2
+    other = xor_permute(hidden, group, 1)
+    *packed, pick, order, kept_hidden = pack_rows(
+        hidden, other, adapter_of_row, adapter_holder_slot, me, orders
+    )
+    gathered = [packed[0]] + [xor_permute(packed[q], group, 2 * q) for q in range(1, chips)]
     pair = pair_sums(kept_hidden, down_matrix, group, order, width)
     gathered, _ = lax.optimization_barrier((gathered, pair))
     shrink = jnp.swapaxes(shrink_matrices, 1, 2)[0]

time: 67.9 us -> 86.6 us (1.28)
  starting transfers between devices: 17.3 us -> 25.4 us
  waiting for transfers between devices: 28 us -> 33.2 us
  Pallas kernels: 17.7 us -> 20.9 us
  other arithmetic: 1.97 us -> 3.65 us
  loops' own time: 0.08 us -> 1.38 us
    ppermute x8 -> x17, starting transfers between devices: 9.91 us -> 25.4 us  [xor_permute(): return lax.ppermute(value, 'tp', [(i, i ^ offset) for i in range(group)])]
    all_to_all x1 -> x0, starting transfers between devices: 7.37 us -> none  [shards_by_blocks(): lax.all_to_all(packed, 'tp', split_axis=0, concat_axis=0, tiled=True)]
    ppermute x8 -> x17, waiting for transfers between devices: 28 us -> 33.2 us  [xor_permute(): return lax.ppermute(value, 'tp', [(i, i ^ offset) for i in range(group)])]
    pallas_call x3 -> x4, Pallas kernels: 14.9 us -> 18.6 us  [the longest x3 14.8 us: column_blocks(): pl.pallas_call(functools.partial(column_blocks_kernel, groups), out_shape...]
    unnamed x4 -> x0, local copies, waits for them, and re-layouts: 2.04 us -> none
    another operation x1 -> x3, loops' own time: 0.08 us -> 1.38 us  [the longest x1 1.29 us: pair_sums(): return lax.cond(order[0] >= 0, whole, idle)]
    slice x1 -> x4, local copies, waits for them, and re-layouts: 0.07 us -> 1.35 us  [the longest x1 0.66 us: whole(): sent = lax.cond(order[1] >= 0, first, first_idle)]
    add x2, other arithmetic: 0.33 us -> 1.22 us  [the longest x1 1.13 us: whole(): return kept + unpack_scaled(pair_in)]
  transfers between devices with their start and end apart: 9 -> 17, of which waited for: 5 -> 8; matrix products, arithmetic and copies ran while one was open for 2% -> 5% of each run, Pallas kernels for 19% -> 17%
where the time goes in v10:
time: 86.6 us; the launch traced here: 86.3 us
  waiting for transfers between devices  33.2 us (38%)
  starting transfers between devices  25.4 us (29%)
  Pallas kernels  20.9 us (24%)
  other arithmetic  3.65 us (4%)
  local copies, waits for them, and re-layouts  1.66 us (2%)
  loops' own time  1.38 us (2%)
    ppermute x17, waiting for transfers between devices, xor_permute(): return lax.ppermute(value, 'tp', [(i, i ^ offset) for i in range(group)])  33.2 us
    ppermute x17, starting transfers between devices, xor_permute(): return lax.ppermute(value, 'tp', [(i, i ^ offset) for i in range(group)])  25.4 us
    pallas_call x3, Pallas kernels, column_blocks(): pl.pallas_call(functools.partial(column_blocks_kernel, groups), out_shape...  14.8 us
    pallas_call x1, Pallas kernels, adapter_output(): pl.pallas_call(functools.partial(adapter_kernel, parts, group // 2), out_...  3.83 us
    pallas_call x1, Pallas kernels, pack_rows(): pl.pallas_call(functools.partial(pack_kernel, blocks, orders), out_shape=...  1.94 us
  transfers between devices with their start and end apart: 17, of which 8 were waited for; matrix products, arithmetic and copies ran while one was open for 5% of the time, Pallas kernels for 17%

profile of v10, /device:TPU:0, one launch (start us, length us, event | category | flops | bytes accessed | tf_op | source)
XLA Modules:
  0.0 86.3 jit_solution(2457318879551964475)
XLA Ops:
  0.0 0.5 collective-permute-start.3
  0.5 1.5 %collective-permute-done.3.other_hbm = bf16[96,1792]{1,0:T(8,128)(2,1)S(1)} collective-permute-done((bf16[96,1792]{1,0:T(8,128)(2,1)}, bf16[96,1792]{1,0:T(8,128)(2,1)S(1)}, u32[]{:S(2)}, u32[]{:S(2)}) %collective-permute-start.3) | collective-permute-done | bytes 344096 | tf_op jit(solution)/shard_map/ppermute | solution.py:24
  1.9 1.9 %shard_map.65 = (bf16[10,4,1792]{2,1,0:T(4,128)(2,1)S(1)}, bf16[10,4,1792]{2,1,0:T(4,128)(2,1)S(1)}, bf16[10,4,1792]{2,1,0:T(4,128)(2,1)S(1)}, bf16[10,4,1792]{2...) custom-call(s32[1]{0:T(128)} %bitcast.3.me_ref, ...), custom_call_target="tpu_custom_call" | custom-call | tf_op jit(solution)/shard_map/pallas_call | solution.py:194
  3.9 2.9 %collective-permute-start.4 = (bf16[10,4,1792]{2,1,0:T(4,128)(2,1)S(1)}, bf16[10,4,1792]{2,1,0:T(4,128)(2,1)S(1)}, u32[]{:S(2)}, u32[]{:S(2)}) collective-permute-start(bf16[10,4,1792]{2,1,0:T(4,128)(2,1)S(1)} %get-tuple-element.71), channel_id=1, source_target_pairs={{0,2},{1,3},{2,0},{3,1},{4,6},{5,7},{6,4},{7,5},{8,10},{9,11},{10,... | collective-permute-start | bytes 430088 | tf_op jit(solution)/shard_map/ppermute | solution.py:24
  6.8 1.6 %collective-permute-start.5 = (bf16[10,4,1792]{2,1,0:T(4,128)(2,1)S(1)}, bf16[10,4,1792]{2,1,0:T(4,128)(2,1)S(1)}, u32[]{:S(2)}, u32[]{:S(2)}) collective-permute-start(bf16[10,4,1792]{2,1,0:T(4,128)(2,1)S(1)} %get-tuple-element.72), channel_id=1, source_target_pairs={{0,4},{1,5},{2,6},{3,7},{4,0},{5,1},{6,2},{7,3},{8,12},{9,13},{10,... | collective-permute-start | bytes 430088 | tf_op jit(solution)/shard_map/ppermute | solution.py:24
  8.4 0.1 collective-permute-start.6
  8.5 24.8 %conditional.3 = (f32[16,96,128]{2,1,0:T(8,128)S(1)}) conditional(s32[]{:T(128)} %bitcast.5, () %tuple.24, (s32[16]{0:T(128)S(1)}, bf16[96,1792]{1,0:T(8,128)(2,1)S(1)}, bf16[1792,8192]{1,0:T(8,128)(2,1)}) %tuple.25), branch_computations={%region_0.0_spmd, %region_1.0_spmd} | conditional | flops 2018716 | bytes 16815220 | solution.py:121
  8.5 0.7 slice.39
  9.9 9.1 %conditional = (f16[17,96,128]{2,1,0:T(8,128)(2,1)S(1)}) conditional(s32[]{:T(128)} %bitcast, () %tuple.17, (s32[16]{0:T(128)S(1)}, bf16[96,1792]{1,0:T(8,128)(2,1)S(1)}, bf16[1792,8192]{1,0:T(8,128)(2,1)}) %param.5), branch_computations={%region_2.0_spmd, %region_3.0_spmd} | conditional | flops 1194416 | bytes 7548864 | solution.py:107
  9.9 0.1 fusion.8
  10.0 4.2 %branch_1_fun.4 = f32[16,96,128]{2,1,0:T(8,128)S(1)} custom-call(s32[4]{0:T(128)S(1)} %get-tuple-element.99.order_ref, bf16[96,1792]{1,0:T(8,128)(2,1)S(1)} %get-tuple-element.32.hidden_ref, bf16[1792,8192]{1,0:T(8,128)(2,1)} %get-tuple-element.34.down_ref), custom_call_target="tpu_custom_call" | custom-call | flops 1000 | bytes 1000 | tf_op jit(solution)/shard_map/cond/branch_1_fun/cond/branch_1_fun/pallas_call | solution.py:61
  14.2 0.1 collective-permute-start.1
  14.3 4.2 %branch_1_fun.3 = f32[16,96,128]{2,1,0:T(8,128)S(1)} custom-call(s32[4]{0:T(128)S(1)} %get-tuple-element.100.order_ref, bf16[96,1792]{1,0:T(8,128)(2,1)S(1)} %get-tuple-element.32.hidden_ref, bf16[1792,8192]{1,0:T(8,128)(2,1)} %get-tuple-element.34.down_ref), custom_call_target="tpu_custom_call" | custom-call | flops 1000 | bytes 1000 | tf_op jit(solution)/shard_map/cond/branch_1_fun/cond/branch_1_fun/pallas_call | solution.py:61
  18.5 0.0 collective-permute-done.1
  18.5 0.2 abs_reduce_fusion
  18.7 0.2 multiply_convert_fusion
  18.8 0.1 broadcast_in_dim.8
  18.9 0.1 pad_maximum_fusion
  19.0 1.9 %collective-permute-start.2 = (f16[17,96,128]{2,1,0:T(8,128)(2,1)S(1)}, f16[17,96,128]{2,1,0:T(8,128)(2,1)}, u32[]{:S(2)}, u32[]{:S(2)}) collective-permute-start(f16[17,96,128]{2,1,0:T(8,128)(2,1)S(1)} %get-tuple-element.112), channel_id=1, source_target_pairs={{0,2},{1,3},{2,0},{3,1},{4,6},{5,7},{6,4},{7,5},{8,10},{9,11},{10,... | collective-permute-start | bytes 1253384 | tf_op jit(solution)/shard_map/cond/branch_1_fun/ppermute | solution.py:24
  21.0 0.6 slice.40
  22.1 8.9 %conditional.1 = (f32[16,96,128]{2,1,0:T(8,128)S(1)}) conditional(s32[]{:T(128)} %bitcast.1, () %tuple.19, (s32[16]{0:T(128)S(1)}, bf16[96,1792]{1,0:T(8,128)(2,1)S(1)}, bf16[1792,8192]{1,0:T(8,128)(2,1)}) %param.5), branch_computations={%region_5.0_spmd, %region_6.0_spmd} | conditional | flops 197608 | bytes 5506136 | solution.py:115
  22.1 0.1 slice.38.order_ref
  22.2 6.4 %branch_1_fun.5 = (f32[16,96,128]{2,1,0:T(8,128)S(1)}, f32[16,96,128]{2,1,0:T(8,128)S(1)}) custom-call(s32[8]{0:T(128)S(1)} %slice.38.order_ref, bf16[96,1792]{1,0:T(8,128)(2,1)S(1)} %get-tuple-element.36.hidden_ref, bf16[1792,8192]{1,0:T(8,128)(2,1)} %get-tuple-element.37.down_ref), custom_call_target="tpu_custom_call" | custom-call | flops 1000 | bytes 1000 | tf_op jit(solution)/shard_map/cond/branch_1_fun/cond/branch_1_fun/pallas_call | solution.py:61
  28.6 0.3 collective-permute-start
  28.9 2.1 %collective-permute-done = f32[16,96,128]{2,1,0:T(8,128)S(1)} collective-permute-done((f32[16,96,128]{2,1,0:T(8,128)S(1)}, f32[16,96,128]{2,1,0:T(8,128)S(1)}, u32[]{:S(2)}, u32[]{:S(2)}) %collective-permute-start) | collective-permute-done | bytes 786464 | tf_op jit(solution)/shard_map/cond/branch_1_fun/cond/branch_1_fun/ppermute | solution.py:24
  30.9 0.1 add.17
  31.0 0.3 collective-permute-done.2
  31.4 0.8 exponential_bitcast_fusion
  32.1 1.1 %multiply_add_fusion = f32[16,96,128]{2,1,0:T(8,128)S(1)} fusion(f32[16,96,128]{2,1,0:T(8,128)S(1)} %get-tuple-element.113, f16[17,96,128]{2,1,0:T(8,128)(2,1)} %collective-permute-done.2, f32[96,128]{1,0:T(8,128)S(1)} %exponential_bitcast_fusion), kind=kLoop, calls=%fused_computation.6 | loop fusion | flops 589824 | bytes 2015232 | tf_op jit(solution)/shard_map/cond/branch_1_fun/add | solution.py:116
  33.3 2.9 %collective-permute-start.7 = (bf16[10,4,1792]{2,1,0:T(4,128)(2,1)S(1)}, bf16[10,4,1792]{2,1,0:T(4,128)(2,1)S(1)}, u32[]{:S(2)}, u32[]{:S(2)}) collective-permute-start(bf16[10,4,1792]{2,1,0:T(4,128)(2,1)S(1)} %get-tuple-element.74), channel_id=1, source_target_pairs={{0,8},{1,9},{2,10},{3,11},{4,12},{5,13},{6,14},{7,15},{8,0},{9,1},... | collective-permute-start | bytes 430088 | tf_op jit(solution)/shard_map/ppermute | solution.py:24
  36.2 1.3 %collective-permute-start.8 = (bf16[10,4,1792]{2,1,0:T(4,128)(2,1)S(1)}, bf16[10,4,1792]{2,1,0:T(4,128)(2,1)S(1)}, u32[]{:S(2)}, u32[]{:S(2)}) collective-permute-start(bf16[10,4,1792]{2,1,0:T(4,128)(2,1)S(1)} %get-tuple-element.75), channel_id=1, source_target_pairs={{0,10},{1,11},{2,8},{3,9},{4,14},{5,15},{6,12},{7,13},{8,2},{9,3},... | collective-permute-start | bytes 430088 | tf_op jit(solution)/shard_map/ppermute | solution.py:24
  37.4 0.0 collective-permute-done.4.refs_1_
  37.4 3.6 %collective-permute-start.9 = (bf16[10,4,1792]{2,1,0:T(4,128)(2,1)S(1)}, bf16[10,4,1792]{2,1,0:T(4,128)(2,1)S(1)}, u32[]{:S(2)}, u32[]{:S(2)}) collective-permute-start(bf16[10,4,1792]{2,1,0:T(4,128)(2,1)S(1)} %get-tuple-element.76), channel_id=1, source_target_pairs={{0,12},{1,13},{2,14},{3,15},{4,8},{5,9},{6,10},{7,11},{8,4},{9,5},... | collective-permute-start | bytes 430088 | tf_op jit(solution)/shard_map/ppermute | solution.py:24
  41.1 0.0 collective-permute-done.5.refs_2_
  41.1 0.0 collective-permute-start.10
  41.1 0.0 collective-permute-done.6.refs_3_
  41.1 12.1 %collective-permute-done.7.refs_4_ = bf16[10,4,1792]{2,1,0:T(4,128)(2,1)S(1)} collective-permute-done((bf16[10,4,1792]{2,1,0:T(4,128)(2,1)S(1)}, bf16[10,4,1792]{2,1,0:T(4,128)(2,1)S(1)}, u32[]{:S(2)}, u32[]{:S(2)}) %collective-permute-start.7) | collective-permute-done | bytes 143392 | tf_op jit(solution)/shard_map/ppermute | solution.py:24
  53.2 4.1 %collective-permute-done.8.refs_5_ = bf16[10,4,1792]{2,1,0:T(4,128)(2,1)S(1)} collective-permute-done((bf16[10,4,1792]{2,1,0:T(4,128)(2,1)S(1)}, bf16[10,4,1792]{2,1,0:T(4,128)(2,1)S(1)}, u32[]{:S(2)}, u32[]{:S(2)}) %collective-permute-start.8) | collective-permute-done | bytes 143392 | tf_op jit(solution)/shard_map/ppermute | solution.py:24
  57.3 0.0 collective-permute-done.9.refs_6_
  57.3 0.0 collective-permute-done.10.refs_7_
  57.3 3.8 %shard_map.66 = (bf16[16,24,128]{2,1,0:T(8,128)(2,1)S(1)}, bf16[16,24,128]{2,1,0:T(8,128)(2,1)S(1)}, bf16[16,24,128]{2,1,0:T(8,128)(2,1)S(1)}, bf16[16,24,128]{2,1,0:T(8,128)(2,1)S(1)}) custom-call(s32[1]{0:T(128)} %bitcast.3.me_ref, bf16[10,4,1792]{2,1,0:T(4,128)(2,1)S(1)} %get-tuple-element.78.refs_0_, ...), custom_call_target="tpu_custom_call" | custom-call | tf_op jit(solution)/shard_map/pallas_call | solution.py:270
  61.1 0.1 collective-permute-start.11
  61.2 0.5 collective-permute-start.12
  61.7 1.4 %collective-permute-start.13 = (bf16[16,24,128]{2,1,0:T(8,128)(2,1)S(1)}, bf16[16,24,128]{2,1,0:T(8,128)(2,1)S(1)}, u32[]{:S(2)}, u32[]{:S(2)}) collective-permute-start(bf16[16,24,128]{2,1,0:T(8,128)(2,1)S(1)} %get-tuple-element.89), channel_id=1, source_target_pairs={{0,3},{1,2},{2,1},{3,0},{4,7},{5,6},{6,5},{7,4},{8,11},{9,10},{10,... | collective-permute-start | bytes 294920 | tf_op jit(solution)/shard_map/ppermute | solution.py:24
  63.1 0.0 collective-permute-done.11.refs_1_
  63.1 3.8 %collective-permute-done.12.refs_2_ = bf16[16,24,128]{2,1,0:T(8,128)(2,1)S(1)} collective-permute-done((bf16[16,24,128]{2,1,0:T(8,128)(2,1)S(1)}, bf16[16,24,128]{2,1,0:T(8,128)(2,1)S(1)}, u32[]{:S(2)}, u32[]{:S(2)}) %collective-permute-start.12) | collective-permute-done | bytes 98336 | tf_op jit(solution)/shard_map/ppermute | solution.py:24
  66.9 1.2 %collective-permute-done.13.refs_3_ = bf16[16,24,128]{2,1,0:T(8,128)(2,1)S(1)} collective-permute-done((bf16[16,24,128]{2,1,0:T(8,128)(2,1)S(1)}, bf16[16,24,128]{2,1,0:T(8,128)(2,1)S(1)}, u32[]{:S(2)}, u32[]{:S(2)}) %collective-permute-start.13) | collective-permute-done | bytes 98336 | tf_op jit(solution)/shard_map/ppermute | solution.py:24
  68.1 0.3 shard_map.67
  68.4 0.2 abs_reduce_fusion.3
  68.6 0.1 multiply_convert_fusion.3
  68.7 0.1 broadcast_in_dim.14
  68.9 2.5 %collective-permute-start.16 = (f16[5,96,128]{2,1,0:T(8,128)(2,1)S(1)}, f16[5,96,128]{2,1,0:T(8,128)(2,1)S(1)}, u32[]{:S(2)}, u32[]{:S(2)}) collective-permute-start(f16[5,96,128]{2,1,0:T(8,128)(2,1)S(1)} %pad_maximum_fusion.3), channel_id=1, source_target_pairs={{0,12},{1,13},{2,14},{3,15},{4,8},{5,9},{6,10},{7,11},{8,4},{9,5},... | collective-permute-start | bytes 368648 | tf_op jit(solution)/shard_map/ppermute | solution.py:24
  71.4 0.1 broadcast_in_dim.13
  71.5 5.2 %collective-permute-start.15 = (f16[5,96,128]{2,1,0:T(8,128)(2,1)S(1)}, f16[5,96,128]{2,1,0:T(8,128)(2,1)S(1)}, u32[]{:S(2)}, u32[]{:S(2)}) collective-permute-start(f16[5,96,128]{2,1,0:T(8,128)(2,1)S(1)} %pad_maximum_fusion.2), channel_id=1, source_target_pairs={{0,8},{1,9},{2,10},{3,11},{4,12},{5,13},{6,14},{7,15},{8,0},{9,1},... | collective-permute-start | bytes 368648 | tf_op jit(solution)/shard_map/ppermute | solution.py:24
  76.7 0.1 broadcast_in_dim.12
  76.8 0.6 collective-permute-start.14
  77.5 0.0 collective-permute-done.16
  77.5 8.0 %collective-permute-done.15 = f16[5,96,128]{2,1,0:T(8,128)(2,1)S(1)} collective-permute-done((f16[5,96,128]{2,1,0:T(8,128)(2,1)S(1)}, f16[5,96,128]{2,1,0:T(8,128)(2,1)S(1)}, u32[]{:S(2)}, u32[]{:S(2)}) %collective-permute-start.15) | collective-permute-done | bytes 122912 | tf_op jit(solution)/shard_map/ppermute | solution.py:24
  85.6 0.0 collective-permute-done.14
  85.6 0.7 copy_bitcast_fusion
  (9 shorter events, 0.2 us)
Async XLA Ops:
  0.0 1.9 %collective-permute-start.3 = (bf16[96,1792]{1,0:T(8,128)(2,1)}, bf16[96,1792]{1,0:T(8,128)(2,1)S(1)}, u32[]{:S(2)}, u32[]{:S(2)}) collective-permute-start(bf16[96,1792]{1,0:T(8,128)(2,1)} %hidden_hbm.1), channel_id=1, source_target_pairs={{0,1},{1,0},{2,3},{3,2},{4,5},{5,4},{6,7},{7,6},{8,9},{9,8},{10,11... | collective-permute-start | bytes 1032200 | tf_op jit(solution)/shard_map/ppermute | solution.py:24
  3.9 33.6 %collective-permute-start.4 = (bf16[10,4,1792]{2,1,0:T(4,128)(2,1)S(1)}, bf16[10,4,1792]{2,1,0:T(4,128)(2,1)S(1)}, u32[]{:S(2)}, u32[]{:S(2)}) collective-permute-start(bf16[10,4,1792]{2,1,0:T(4,128)(2,1)S(1)} %get-tuple-element.71), channel_id=1, source_target_pairs={{0,2},{1,3},{2,0},{3,1},{4,6},{5,7},{6,4},{7,5},{8,10},{9,11},{10,... | collective-permute-start | bytes 430088 | tf_op jit(solution)/shard_map/ppermute | solution.py:24
  6.8 34.2 %collective-permute-start.5 = (bf16[10,4,1792]{2,1,0:T(4,128)(2,1)S(1)}, bf16[10,4,1792]{2,1,0:T(4,128)(2,1)S(1)}, u32[]{:S(2)}, u32[]{:S(2)}) collective-permute-start(bf16[10,4,1792]{2,1,0:T(4,128)(2,1)S(1)} %get-tuple-element.72), channel_id=1, source_target_pairs={{0,4},{1,5},{2,6},{3,7},{4,0},{5,1},{6,2},{7,3},{8,12},{9,13},{10,... | collective-permute-start | bytes 430088 | tf_op jit(solution)/shard_map/ppermute | solution.py:24
  8.4 32.7 %collective-permute-start.6 = (bf16[10,4,1792]{2,1,0:T(4,128)(2,1)S(1)}, bf16[10,4,1792]{2,1,0:T(4,128)(2,1)S(1)}, u32[]{:S(2)}, u32[]{:S(2)}) collective-permute-start(bf16[10,4,1792]{2,1,0:T(4,128)(2,1)S(1)} %get-tuple-element.73), channel_id=1, source_target_pairs={{0,6},{1,7},{2,4},{3,5},{4,2},{5,3},{6,0},{7,1},{8,14},{9,15},{10,... | collective-permute-start | bytes 430088 | tf_op jit(solution)/shard_map/ppermute | solution.py:24
  14.2 4.3 %collective-permute-start.1 = (f32[16,96,128]{2,1,0:T(8,128)S(1)}, f32[16,96,128]{2,1,0:T(8,128)S(1)}, u32[]{:S(2)}, u32[]{:S(2)}) collective-permute-start(f32[16,96,128]{2,1,0:T(8,128)S(1)} %branch_1_fun.4), channel_id=1, source_target_pairs={{0,1},{1,0},{2,3},{3,2},{4,5},{5,4},{6,7},{7,6},{8,9},{9,8},{10,11... | collective-permute-start | bytes 2359304 | tf_op jit(solution)/shard_map/cond/branch_1_fun/cond/branch_1_fun/ppermute | solution.py:24
  19.0 12.4 %collective-permute-start.2 = (f16[17,96,128]{2,1,0:T(8,128)(2,1)S(1)}, f16[17,96,128]{2,1,0:T(8,128)(2,1)}, u32[]{:S(2)}, u32[]{:S(2)}) collective-permute-start(f16[17,96,128]{2,1,0:T(8,128)(2,1)S(1)} %get-tuple-element.112), channel_id=1, source_target_pairs={{0,2},{1,3},{2,0},{3,1},{4,6},{5,7},{6,4},{7,5},{8,10},{9,11},{10,... | collective-permute-start | bytes 1253384 | tf_op jit(solution)/shard_map/cond/branch_1_fun/ppermute | solution.py:24
  28.6 2.4 %collective-permute-start = (f32[16,96,128]{2,1,0:T(8,128)S(1)}, f32[16,96,128]{2,1,0:T(8,128)S(1)}, u32[]{:S(2)}, u32[]{:S(2)}) collective-permute-start(f32[16,96,128]{2,1,0:T(8,128)S(1)} %get-tuple-element.39), channel_id=1, source_target_pairs={{0,1},{1,0},{2,3},{3,2},{4,5},{5,4},{6,7},{7,6},{8,9},{9,8},{10,11... | collective-permute-start | bytes 2359304 | tf_op jit(solution)/shard_map/cond/branch_1_fun/cond/branch_1_fun/ppermute | solution.py:24
  33.3 19.9 %collective-permute-start.7 = (bf16[10,4,1792]{2,1,0:T(4,128)(2,1)S(1)}, bf16[10,4,1792]{2,1,0:T(4,128)(2,1)S(1)}, u32[]{:S(2)}, u32[]{:S(2)}) collective-permute-start(bf16[10,4,1792]{2,1,0:T(4,128)(2,1)S(1)} %get-tuple-element.74), channel_id=1, source_target_pairs={{0,8},{1,9},{2,10},{3,11},{4,12},{5,13},{6,14},{7,15},{8,0},{9,1},... | collective-permute-start | bytes 430088 | tf_op jit(solution)/shard_map/ppermute | solution.py:24
  36.2 21.1 %collective-permute-start.8 = (bf16[10,4,1792]{2,1,0:T(4,128)(2,1)S(1)}, bf16[10,4,1792]{2,1,0:T(4,128)(2,1)S(1)}, u32[]{:S(2)}, u32[]{:S(2)}) collective-permute-start(bf16[10,4,1792]{2,1,0:T(4,128)(2,1)S(1)} %get-tuple-element.75), channel_id=1, source_target_pairs={{0,10},{1,11},{2,8},{3,9},{4,14},{5,15},{6,12},{7,13},{8,2},{9,3},... | collective-permute-start | bytes 430088 | tf_op jit(solution)/shard_map/ppermute | solution.py:24
  37.4 19.9 %collective-permute-start.9 = (bf16[10,4,1792]{2,1,0:T(4,128)(2,1)S(1)}, bf16[10,4,1792]{2,1,0:T(4,128)(2,1)S(1)}, u32[]{:S(2)}, u32[]{:S(2)}) collective-permute-start(bf16[10,4,1792]{2,1,0:T(4,128)(2,1)S(1)} %get-tuple-element.76), channel_id=1, source_target_pairs={{0,12},{1,13},{2,14},{3,15},{4,8},{5,9},{6,10},{7,11},{8,4},{9,5},... | collective-permute-start | bytes 430088 | tf_op jit(solution)/shard_map/ppermute | solution.py:24
  41.1 16.3 %collective-permute-start.10 = (bf16[10,4,1792]{2,1,0:T(4,128)(2,1)S(1)}, bf16[10,4,1792]{2,1,0:T(4,128)(2,1)S(1)}, u32[]{:S(2)}, u32[]{:S(2)}) collective-permute-start(bf16[10,4,1792]{2,1,0:T(4,128)(2,1)S(1)} %get-tuple-element.77), channel_id=1, source_target_pairs={{0,14},{1,15},{2,12},{3,13},{4,10},{5,11},{6,8},{7,9},{8,6},{9,7},... | collective-permute-start | bytes 430088 | tf_op jit(solution)/shard_map/ppermute | solution.py:24
  61.1 1.9 %collective-permute-start.11 = (bf16[16,24,128]{2,1,0:T(8,128)(2,1)S(1)}, bf16[16,24,128]{2,1,0:T(8,128)(2,1)S(1)}, u32[]{:S(2)}, u32[]{:S(2)}) collective-permute-start(bf16[16,24,128]{2,1,0:T(8,128)(2,1)S(1)} %get-tuple-element.87), channel_id=1, source_target_pairs={{0,1},{1,0},{2,3},{3,2},{4,5},{5,4},{6,7},{7,6},{8,9},{9,8},{10,11... | collective-permute-start | bytes 294920 | tf_op jit(solution)/shard_map/ppermute | solution.py:24
  61.2 5.7 %collective-permute-start.12 = (bf16[16,24,128]{2,1,0:T(8,128)(2,1)S(1)}, bf16[16,24,128]{2,1,0:T(8,128)(2,1)S(1)}, u32[]{:S(2)}, u32[]{:S(2)}) collective-permute-start(bf16[16,24,128]{2,1,0:T(8,128)(2,1)S(1)} %get-tuple-element.88), channel_id=1, source_target_pairs={{0,2},{1,3},{2,0},{3,1},{4,6},{5,7},{6,4},{7,5},{8,10},{9,11},{10,... | collective-permute-start | bytes 294920 | tf_op jit(solution)/shard_map/ppermute | solution.py:24
  61.7 6.4 %collective-permute-start.13 = (bf16[16,24,128]{2,1,0:T(8,128)(2,1)S(1)}, bf16[16,24,128]{2,1,0:T(8,128)(2,1)S(1)}, u32[]{:S(2)}, u32[]{:S(2)}) collective-permute-start(bf16[16,24,128]{2,1,0:T(8,128)(2,1)S(1)} %get-tuple-element.89), channel_id=1, source_target_pairs={{0,3},{1,2},{2,1},{3,0},{4,7},{5,6},{6,5},{7,4},{8,11},{9,10},{10,... | collective-permute-start | bytes 294920 | tf_op jit(solution)/shard_map/ppermute | solution.py:24
  68.9 8.6 %collective-permute-start.16 = (f16[5,96,128]{2,1,0:T(8,128)(2,1)S(1)}, f16[5,96,128]{2,1,0:T(8,128)(2,1)S(1)}, u32[]{:S(2)}, u32[]{:S(2)}) collective-permute-start(f16[5,96,128]{2,1,0:T(8,128)(2,1)S(1)} %pad_maximum_fusion.3), channel_id=1, source_target_pairs={{0,12},{1,13},{2,14},{3,15},{4,8},{5,9},{6,10},{7,11},{8,4},{9,5},... | collective-permute-start | bytes 368648 | tf_op jit(solution)/shard_map/ppermute | solution.py:24
  71.5 14.0 %collective-permute-start.15 = (f16[5,96,128]{2,1,0:T(8,128)(2,1)S(1)}, f16[5,96,128]{2,1,0:T(8,128)(2,1)S(1)}, u32[]{:S(2)}, u32[]{:S(2)}) collective-permute-start(f16[5,96,128]{2,1,0:T(8,128)(2,1)S(1)} %pad_maximum_fusion.2), channel_id=1, source_target_pairs={{0,8},{1,9},{2,10},{3,11},{4,12},{5,13},{6,14},{7,15},{8,0},{9,1},... | collective-permute-start | bytes 368648 | tf_op jit(solution)/shard_map/ppermute | solution.py:24
  76.8 8.7 %collective-permute-start.14 = (f16[5,96,128]{2,1,0:T(8,128)(2,1)S(1)}, f16[5,96,128]{2,1,0:T(8,128)(2,1)S(1)}, u32[]{:S(2)}, u32[]{:S(2)}) collective-permute-start(f16[5,96,128]{2,1,0:T(8,128)(2,1)S(1)} %pad_maximum_fusion.1), channel_id=1, source_target_pairs={{0,4},{1,5},{2,6},{3,7},{4,0},{5,1},{6,2},{7,3},{8,12},{9,13},{10,... | collective-permute-start | bytes 368648 | tf_op jit(solution)/shard_map/ppermute | solution.py:24

commit v11 on v10

--- a/solution.py
+++ b/solution.py
@@ -14,6 +14,7 @@
 F16_TOP = 14.0
 PLANE = 4
 HELD = 24
+IN_FLIGHT = 4
 
 
 def in_hbm(value):
@@ -135,13 +136,26 @@
 
 
 def pack_kernel(
-    blocks, orders, me_ref, slot_hbm, adapter_hbm, hidden_hbm, other_hbm, *refs
+    blocks,
+    orders,
+    me_ref,
+    slot_hbm,
+    adapter_hbm,
+    hidden_hbm,
+    other_hbm,
+    packed_ref,
+    pick_ref,
+    order_ref,
+    kept_ref,
+    slot_ref,
+    adapter_ref,
+    hidden_ref,
+    other_ref,
+    sems,
 ):
-    chips = len(refs) - 8
-    packed_refs = refs[:chips]
-    pick_ref, order_ref, kept_ref, slot_ref, adapter_ref, hidden_ref, other_ref, sems = refs[chips:]
     rows = hidden_ref.shape[0]
     group = slot_ref.shape[0]
+    chips = group // 2
     me = me_ref[0]
     copies = [
         pltpu.make_async_copy(slot_hbm, slot_ref, sems.at[0]),
@@ -161,7 +175,8 @@
     copies[1].wait()
     adapter = adapter_ref[...]
     first = jnp.sum((adapter < ids).astype(jnp.int32), axis=1, keepdims=True)
-    offset = jnp.sum(jnp.where(adapter == ids, slots ^ me, 0), axis=0, keepdims=True)
+    slot = jnp.sum(jnp.where(adapter == ids, slots, 0), axis=0, keepdims=True)
+    offset = slot ^ me
     first = jnp.sum(jnp.where(adapter == ids, first, 0), axis=0, keepdims=True)
     index = lax.broadcasted_iota(jnp.int32, (1, rows), 1) - first
     for k in range(PLANE):
@@ -169,7 +184,7 @@
         mine = (offset == k) & (index == line)
         pick_ref[k * HELD : (k + 1) * HELD] = jnp.where(mine, 1.0, 0.0).astype(jnp.bfloat16)
     held = blocks * BLOCK
-    place = jnp.where((offset & 1) == 0, (offset >> 1) * held + index, -1)
+    place = jnp.where((offset & 1) == 0, (slot >> 1) * held + index, -1)
     spots = lax.broadcasted_iota(jnp.int32, (chips * held, rows), 0)
     pick = jnp.where(spots == place, 1.0, 0.0).astype(jnp.bfloat16)
     for source, source_ref in enumerate((hidden_ref, other_ref)):
@@ -177,9 +192,8 @@
         packed = jnp.dot(pick, source_ref[...], preferred_element_type=jnp.float32)
         packed = packed.astype(jnp.bfloat16).reshape(chips * blocks, BLOCK, packed.shape[1])
         for chip in range(chips):
-            packed_refs[chip][source * blocks : (source + 1) * blocks] = packed[
-                chip * blocks : (chip + 1) * blocks
-            ]
+            start = (2 * chip + source) * blocks
+            packed_ref[start : start + blocks] = packed[chip * blocks : (chip + 1) * blocks]
     kept_ref[...] = hidden_ref[...]
 
 
@@ -187,20 +201,19 @@
     rows, depth = hidden.shape
     group = adapter_holder_slot.shape[0]
     blocks = MOST // BLOCK
-    chips = group // 2
     vmem = pl.BlockSpec(memory_space=pltpu.VMEM)
     smem = pl.BlockSpec(memory_space=pltpu.SMEM)
     anywhere = pl.BlockSpec(memory_space=pl.ANY)
     return pl.pallas_call(
         functools.partial(pack_kernel, blocks, orders),
-        out_shape=[jax.ShapeDtypeStruct((2 * blocks, BLOCK, depth), jnp.bfloat16)] * chips
-        + [
+        out_shape=[
+            jax.ShapeDtypeStruct((group * blocks, BLOCK, depth), jnp.bfloat16),
             jax.ShapeDtypeStruct((PLANE * HELD, rows), jnp.bfloat16),
             jax.ShapeDtypeStruct((len(orders),), jnp.int32),
             jax.ShapeDtypeStruct((rows, depth), jnp.bfloat16),
         ],
         in_specs=[smem] + [anywhere] * 4,
-        out_specs=[vmem] * (chips + 1) + [smem, vmem],
+        out_specs=[vmem, vmem, smem, vmem],
         scratch_shapes=[
             pltpu.SMEM((group,), jnp.int32),
             pltpu.VMEM((1, rows), jnp.int32),
@@ -218,29 +231,31 @@
     )
 
 
-def adapter_kernel(parts, chips, me_ref, *refs):
-    row_refs, (shrink_hbm, expand_hbm) = refs[:chips], refs[chips : chips + 2]
-    out_refs = refs[chips + 2 : chips + 2 + PLANE]
-    shrink_ref, expand_ref, total_ref, sems, expand_sem = refs[chips + 2 + PLANE :]
+def adapter_kernel(parts, me_ref, rows_ref, shrink_hbm, expand_hbm, *refs):
+    out_refs = refs[:PLANE]
+    shrink_ref, expand_ref, total_ref, sems, expand_sem = refs[PLANE:]
     me = me_ref[0]
-    block, depth = row_refs[0].shape[1:]
+    group, _, depth = shrink_ref.shape
     blocks = MOST // BLOCK
 
     def copy(source):
-        start = pl.multiple_of((me ^ source) * depth, LANES)
+        device = source // 2 * 2 + ((me & 1) ^ (source % 2))
+        start = pl.multiple_of(device * depth, LANES)
         return pltpu.make_async_copy(
             shrink_hbm.at[:, pl.ds(start, depth)], shrink_ref.at[source], sems.at[source]
         )
 
-    for source in range(2 * chips):
+    for source in range(IN_FLIGHT):
         copy(source).start()
     expand_copy = pltpu.make_async_copy(expand_hbm, expand_ref, expand_sem)
-    expand_copy.start()
     total = jnp.zeros((MOST, total_ref.shape[1]), jnp.float32)
-    for source in range(2 * chips):
+    for source in range(group):
         copy(source).wait()
-        part = source % 2
-        own = row_refs[source // 2][part * blocks : (part + 1) * blocks].reshape(MOST, depth)
+        if source + IN_FLIGHT < group:
+            copy(source + IN_FLIGHT).start()
+        elif source + IN_FLIGHT == group:
+            expand_copy.start()
+        own = rows_ref[source * blocks : (source + 1) * blocks].reshape(MOST, depth)
         total += lax.dot_general(
             own, shrink_ref[source], (((1,), (1,)), ((), ())), preferred_element_type=jnp.float32
         )
@@ -262,17 +277,15 @@
 def adapter_output(gathered, shrink, expand, group, me):
     rank = shrink.shape[0]
     model_width = expand.shape[1]
-    depth = gathered[0].shape[2]
+    depth = gathered.shape[2]
     parts = model_width // group // LANES
     held = (model_width // PLANE // LANES, HELD, LANES)
     vmem = pl.BlockSpec(memory_space=pltpu.VMEM)
     anywhere = pl.BlockSpec(memory_space=pl.ANY)
     return pl.pallas_call(
-        functools.partial(adapter_kernel, parts, group // 2),
+        functools.partial(adapter_kernel, parts),
         out_shape=[jax.ShapeDtypeStruct(held, jnp.bfloat16)] * PLANE,
-        in_specs=[pl.BlockSpec(memory_space=pltpu.SMEM)]
-        + [vmem] * len(gathered)
-        + [anywhere] * 2,
+        in_specs=[pl.BlockSpec(memory_space=pltpu.SMEM), vmem, anywhere, anywhere],
         out_specs=[vmem] * PLANE,
         scratch_shapes=[
             pltpu.VMEM((group, rank, depth), jnp.bfloat16),
@@ -282,7 +295,7 @@
             pltpu.SemaphoreType.DMA,
         ],
         compiler_params=pltpu.CompilerParams(vmem_limit_bytes=24 * 2**20),
-    )(me.reshape(1), *gathered, in_hbm(shrink), in_hbm(expand))
+    )(me.reshape(1), gathered, in_hbm(shrink), in_hbm(expand))
 
 
 def merge_kernel(pair_ref, pick_ref, *refs):
@@ -318,12 +331,14 @@
     width = down_matrix.shape[1] // group
     quads = list(range(0, group, 4))
     orders = [q + k for k in (3, 2, 1, 0) for q in quads]
-    chips = group // 2
     other = xor_permute(hidden, group, 1)
-    *packed, pick, order, kept_hidden = pack_rows(
+    packed, pick, order, kept_hidden = pack_rows(
         hidden, other, adapter_of_row, adapter_holder_slot, me, orders
     )
-    gathered = [packed[0]] + [xor_permute(packed[q], group, 2 * q) for q in range(1, chips)]
+    same_core = [list(range(core, group, 2)) for core in range(2)]
+    gathered = lax.all_to_all(
+        packed, "tp", split_axis=0, concat_axis=0, axis_index_groups=same_core, tiled=True
+    )
     pair = pair_sums(kept_hidden, down_matrix, group, order, width)
     gathered, _ = lax.optimization_barrier((gathered, pair))
     shrink = jnp.swapaxes(shrink_matrices, 1, 2)[0]

time: 86.6 us -> 70.8 us (0.82)
  waiting for transfers between devices: 33.2 us -> 22.6 us
  starting transfers between devices: 25.4 us -> 17.3 us
  Pallas kernels: 20.9 us -> 23.6 us
    ppermute x17 -> x10, starting transfers between devices: 25.4 us -> 10.1 us  [xor_permute(): return lax.ppermute(value, 'tp', [(i, i ^ offset) for i in range(group)])]
    ppermute x17 -> x10, waiting for transfers between devices: 33.2 us -> 22.6 us  [xor_permute(): return lax.ppermute(value, 'tp', [(i, i ^ offset) for i in range(group)])]
    all_to_all x0 -> x1, starting transfers between devices: none -> 7.19 us  [shards_by_blocks(): lax.all_to_all(packed, 'tp', split_axis=0, concat_axis=0, axis_index_grou...]
    pallas_call x1, Pallas kernels: 3.83 us -> 5.78 us  [adapter_output(): pl.pallas_call(functools.partial(adapter_kernel, parts), out_shape=[jax.S...]
  transfers between devices with their start and end apart: 17 -> 11, of which waited for: 8 -> 7; matrix products, arithmetic and copies ran while one was open for 5% -> 6% of each run, Pallas kernels for 17% -> 21%
where the time goes in v11:
time: 70.8 us; the launch traced here: 70.4 us
  Pallas kernels  23.6 us (33%)
  waiting for transfers between devices  22.6 us (32%)
  starting transfers between devices  17.3 us (24%)
  other arithmetic  3.68 us (5%)
  local copies, waits for them, and re-layouts  1.69 us (2%)
  loops' own time  1.36 us (2%)
    ppermute x10, waiting for transfers between devices, xor_permute(): return lax.ppermute(value, 'tp', [(i, i ^ offset) for i in range(group)])  22.6 us
    pallas_call x3, Pallas kernels, column_blocks(): pl.pallas_call(functools.partial(column_blocks_kernel, groups), out_shape...  14.8 us
    ppermute x10, starting transfers between devices, xor_permute(): return lax.ppermute(value, 'tp', [(i, i ^ offset) for i in range(group)])  10.1 us
    all_to_all x1, starting transfers between devices, shards_by_blocks(): lax.all_to_all(packed, 'tp', split_axis=0, concat_axis=0, axis_index_grou...  7.19 us
    pallas_call x1, Pallas kernels, adapter_output(): pl.pallas_call(functools.partial(adapter_kernel, parts), out_shape=[jax.S...  5.78 us
    pallas_call x1, Pallas kernels, pack_rows(): pl.pallas_call(functools.partial(pack_kernel, blocks, orders), out_shape=...  2.71 us
  transfers between devices with their start and end apart: 11, of which 7 were waited for; matrix products, arithmetic and copies ran while one was open for 6% of the time, Pallas kernels for 21%

profile of v11, /device:TPU:0, one launch (start us, length us, event | category | flops | bytes accessed | tf_op | source)
XLA Modules:
  0.0 70.4 jit_solution(14572241455929840388)
XLA Ops:
  0.0 0.5 collective-permute-start.3
  0.5 1.5 %collective-permute-done.3.other_hbm = bf16[96,1792]{1,0:T(8,128)(2,1)S(1)} collective-permute-done((bf16[96,1792]{1,0:T(8,128)(2,1)}, bf16[96,1792]{1,0:T(8,128)(2,1)S(1)}, u32[]{:S(2)}, u32[]{:S(2)}) %collective-permute-start.3) | collective-permute-done | bytes 344096 | tf_op jit(solution)/shard_map/ppermute | solution.py:25
  1.9 2.7 %shard_map.65 = (bf16[80,4,1792]{2,1,0:T(4,128)(2,1)}, bf16[96,96]{1,0:T(8,128)(2,1)S(1)}, s32[16]{0:T(128)S(1)}, bf16[96,1792]{1,0:T(8,128)(2,1)S(1)}) custom-call(s32[1]{0:T(128)} %bitcast.3.me_ref, s32[16]{0:T(128)} %slot_hbm.1, s32[1,96]{1,0:T(1,128)} %bitcast.29, bf16[96,1792]{1,0:T(8,128)(2,1)} %hidden_hbm.1, ...), custom_call_target="tpu_custom_call" | custom-call | tf_op jit(solution)/shard_map/pallas_call | solution.py:207
  4.7 7.2 %all-to-all-start = ((bf16[80,4,1792]{2,1,0:T(4,128)(2,1)}), bf16[80,4,1792]{2,1,0:T(4,128)(2,1)S(1)}, u32[]{:S(2)}, u32[]{:S(2)}) async-start(bf16[80,4,1792]{2,1,0:T(4,128)(2,1)} %get-tuple-element.56), calls=%async_computation | async-start | bytes 2293760 | tf_op jit(solution)/shard_map/all_to_all | solution.py:339
  11.9 28.9 %conditional.3 = (f32[16,96,128]{2,1,0:T(8,128)S(1)}) conditional(s32[]{:T(128)} %bitcast.5, () %tuple.24, (s32[16]{0:T(128)S(1)}, bf16[96,1792]{1,0:T(8,128)(2,1)S(1)}, bf16[1792,8192]{1,0:T(8,128)(2,1)}) %tuple.25), branch_computations={%region_0.0_spmd, %region_1.0_spmd} | conditional | flops 2018716 | bytes 16815220 | solution.py:122
  11.9 0.6 slice.39
  13.2 9.2 %conditional = (f16[17,96,128]{2,1,0:T(8,128)(2,1)S(1)}) conditional(s32[]{:T(128)} %bitcast, () %tuple.17, (s32[16]{0:T(128)S(1)}, bf16[96,1792]{1,0:T(8,128)(2,1)S(1)}, bf16[1792,8192]{1,0:T(8,128)(2,1)}) %param.5), branch_computations={%region_2.0_spmd, %region_3.0_spmd} | conditional | flops 1194416 | bytes 7548864 | solution.py:108
  13.2 0.1 fusion.8
  13.3 4.2 %branch_1_fun.4 = f32[16,96,128]{2,1,0:T(8,128)S(1)} custom-call(s32[4]{0:T(128)S(1)} %get-tuple-element.71.order_ref, bf16[96,1792]{1,0:T(8,128)(2,1)S(1)} %get-tuple-element.32.hidden_ref, bf16[1792,8192]{1,0:T(8,128)(2,1)} %get-tuple-element.34.down_ref), custom_call_target="tpu_custom_call" | custom-call | flops 1000 | bytes 1000 | tf_op jit(solution)/shard_map/cond/branch_1_fun/cond/branch_1_fun/pallas_call | solution.py:62
  17.5 0.1 collective-permute-start.1
  17.6 4.2 %branch_1_fun.3 = f32[16,96,128]{2,1,0:T(8,128)S(1)} custom-call(s32[4]{0:T(128)S(1)} %get-tuple-element.72.order_ref, bf16[96,1792]{1,0:T(8,128)(2,1)S(1)} %get-tuple-element.32.hidden_ref, bf16[1792,8192]{1,0:T(8,128)(2,1)} %get-tuple-element.34.down_ref), custom_call_target="tpu_custom_call" | custom-call | flops 1000 | bytes 1000 | tf_op jit(solution)/shard_map/cond/branch_1_fun/cond/branch_1_fun/pallas_call | solution.py:62
  21.8 0.0 collective-permute-done.1
  21.8 0.2 abs_reduce_fusion
  22.0 0.2 multiply_convert_fusion
  22.2 0.1 broadcast_in_dim.8
  22.3 0.1 pad_maximum_fusion
  22.4 2.1 %collective-permute-start.2 = (f16[17,96,128]{2,1,0:T(8,128)(2,1)S(1)}, f16[17,96,128]{2,1,0:T(8,128)(2,1)}, u32[]{:S(2)}, u32[]{:S(2)}) collective-permute-start(f16[17,96,128]{2,1,0:T(8,128)(2,1)S(1)} %get-tuple-element.84), channel_id=1, source_target_pairs={{0,2},{1,3},{2,0},{3,1},{4,6},{5,7},{6,4},{7,5},{8,10},{9,11},{10,... | collective-permute-start | bytes 1253384 | tf_op jit(solution)/shard_map/cond/branch_1_fun/ppermute | solution.py:25
  24.5 0.6 slice.40
  25.6 9.0 %conditional.1 = (f32[16,96,128]{2,1,0:T(8,128)S(1)}) conditional(s32[]{:T(128)} %bitcast.1, () %tuple.19, (s32[16]{0:T(128)S(1)}, bf16[96,1792]{1,0:T(8,128)(2,1)S(1)}, bf16[1792,8192]{1,0:T(8,128)(2,1)}) %param.5), branch_computations={%region_5.0_spmd, %region_6.0_spmd} | conditional | flops 197608 | bytes 5506136 | solution.py:116
  25.6 0.1 slice.38.order_ref
  25.7 6.4 %branch_1_fun.5 = (f32[16,96,128]{2,1,0:T(8,128)S(1)}, f32[16,96,128]{2,1,0:T(8,128)S(1)}) custom-call(s32[8]{0:T(128)S(1)} %slice.38.order_ref, bf16[96,1792]{1,0:T(8,128)(2,1)S(1)} %get-tuple-element.36.hidden_ref, bf16[1792,8192]{1,0:T(8,128)(2,1)} %get-tuple-element.37.down_ref), custom_call_target="tpu_custom_call" | custom-call | flops 1000 | bytes 1000 | tf_op jit(solution)/shard_map/cond/branch_1_fun/cond/branch_1_fun/pallas_call | solution.py:62
  32.1 0.3 collective-permute-start
  32.4 2.1 %collective-permute-done = f32[16,96,128]{2,1,0:T(8,128)S(1)} collective-permute-done((f32[16,96,128]{2,1,0:T(8,128)S(1)}, f32[16,96,128]{2,1,0:T(8,128)S(1)}, u32[]{:S(2)}, u32[]{:S(2)}) %collective-permute-start) | collective-permute-done | bytes 786464 | tf_op jit(solution)/shard_map/cond/branch_1_fun/cond/branch_1_fun/ppermute | solution.py:25
  34.5 0.1 add.17
  34.6 4.3 %collective-permute-done.2 = f16[17,96,128]{2,1,0:T(8,128)(2,1)} collective-permute-done((f16[17,96,128]{2,1,0:T(8,128)(2,1)S(1)}, f16[17,96,128]{2,1,0:T(8,128)(2,1)}, u32[]{:S(2)}, u32[]{:S(2)}) %collective-permute-start.2) | collective-permute-done | bytes 417824 | tf_op jit(solution)/shard_map/cond/branch_1_fun/ppermute | solution.py:25
  39.0 0.8 %exponential_bitcast_fusion = f32[96,128]{1,0:T(8,128)S(1)} fusion(f16[17,96,128]{2,1,0:T(8,128)(2,1)} %collective-permute-done.2), kind=kLoop, calls=%fused_computation.7 | loop fusion | flops 36864 | bytes 73728 | tf_op jit(solution)/shard_map/cond/branch_1_fun/mul | solution.py:90
  39.7 1.1 %multiply_add_fusion = f32[16,96,128]{2,1,0:T(8,128)S(1)} fusion(f32[16,96,128]{2,1,0:T(8,128)S(1)} %get-tuple-element.85, f16[17,96,128]{2,1,0:T(8,128)(2,1)} %collective-permute-done.2, f32[96,128]{1,0:T(8,128)S(1)} %exponential_bitcast_fusion), kind=kLoop, calls=%fused_computation.6 | loop fusion | flops 589824 | bytes 2015232 | tf_op jit(solution)/shard_map/cond/branch_1_fun/add | solution.py:117
  40.8 0.0 all-to-all-done.rows_ref
  40.8 5.8 %shard_map.66 = (bf16[16,24,128]{2,1,0:T(8,128)(2,1)S(1)}, bf16[16,24,128]{2,1,0:T(8,128)(2,1)S(1)}, bf16[16,24,128]{2,1,0:T(8,128)(2,1)S(1)}, bf16[16,24,128]{2,1,0:T(8,128)(2,1)S(1)}) custom-call(s32[1]{0:T(128)} %bitcast.3.me_ref, bf16[80,4,1792]{2,1,0:T(4,128)(2,1)S(1)} %all-to-all-done.rows_ref, bf16[64,28672]{1,0:T(8,128)(2,1)} %bitcast.26, ...), custom_call_target="tpu_custom_call" | custom-call | tf_op jit(solution)/shard_map/pallas_call | solution.py:285
  46.6 0.1 collective-permute-start.4
  46.7 0.7 %collective-permute-start.5 = (bf16[16,24,128]{2,1,0:T(8,128)(2,1)S(1)}, bf16[16,24,128]{2,1,0:T(8,128)(2,1)S(1)}, u32[]{:S(2)}, u32[]{:S(2)}) collective-permute-start(bf16[16,24,128]{2,1,0:T(8,128)(2,1)S(1)} %get-tuple-element.60), channel_id=1, source_target_pairs={{0,2},{1,3},{2,0},{3,1},{4,6},{5,7},{6,4},{7,5},{8,10},{9,11},{10,... | collective-permute-start | bytes 294920 | tf_op jit(solution)/shard_map/ppermute | solution.py:25
  47.4 1.2 %collective-permute-start.6 = (bf16[16,24,128]{2,1,0:T(8,128)(2,1)S(1)}, bf16[16,24,128]{2,1,0:T(8,128)(2,1)S(1)}, u32[]{:S(2)}, u32[]{:S(2)}) collective-permute-start(bf16[16,24,128]{2,1,0:T(8,128)(2,1)S(1)} %get-tuple-element.61), channel_id=1, source_target_pairs={{0,3},{1,2},{2,1},{3,0},{4,7},{5,6},{6,5},{7,4},{8,11},{9,10},{10,... | collective-permute-start | bytes 294920 | tf_op jit(solution)/shard_map/ppermute | solution.py:25
  48.6 0.0 collective-permute-done.4.refs_1_
  48.6 3.8 %collective-permute-done.5.refs_2_ = bf16[16,24,128]{2,1,0:T(8,128)(2,1)S(1)} collective-permute-done((bf16[16,24,128]{2,1,0:T(8,128)(2,1)S(1)}, bf16[16,24,128]{2,1,0:T(8,128)(2,1)S(1)}, u32[]{:S(2)}, u32[]{:S(2)}) %collective-permute-start.5) | collective-permute-done | bytes 98336 | tf_op jit(solution)/shard_map/ppermute | solution.py:25
  52.4 1.2 %collective-permute-done.6.refs_3_ = bf16[16,24,128]{2,1,0:T(8,128)(2,1)S(1)} collective-permute-done((bf16[16,24,128]{2,1,0:T(8,128)(2,1)S(1)}, bf16[16,24,128]{2,1,0:T(8,128)(2,1)S(1)}, u32[]{:S(2)}, u32[]{:S(2)}) %collective-permute-start.6) | collective-permute-done | bytes 98336 | tf_op jit(solution)/shard_map/ppermute | solution.py:25
  53.6 0.3 shard_map.67
  53.9 0.2 abs_reduce_fusion.3
  54.1 0.1 multiply_convert_fusion.3
  54.2 0.1 broadcast_in_dim.14
  54.3 2.9 %collective-permute-start.9 = (f16[5,96,128]{2,1,0:T(8,128)(2,1)S(1)}, f16[5,96,128]{2,1,0:T(8,128)(2,1)S(1)}, u32[]{:S(2)}, u32[]{:S(2)}) collective-permute-start(f16[5,96,128]{2,1,0:T(8,128)(2,1)S(1)} %pad_maximum_fusion.3), channel_id=1, source_target_pairs={{0,12},{1,13},{2,14},{3,15},{4,8},{5,9},{6,10},{7,11},{8,4},{9,5},... | collective-permute-start | bytes 368648 | tf_op jit(solution)/shard_map/ppermute | solution.py:25
  57.2 0.1 broadcast_in_dim.13
  57.4 2.3 %collective-permute-start.8 = (f16[5,96,128]{2,1,0:T(8,128)(2,1)S(1)}, f16[5,96,128]{2,1,0:T(8,128)(2,1)S(1)}, u32[]{:S(2)}, u32[]{:S(2)}) collective-permute-start(f16[5,96,128]{2,1,0:T(8,128)(2,1)S(1)} %pad_maximum_fusion.2), channel_id=1, source_target_pairs={{0,8},{1,9},{2,10},{3,11},{4,12},{5,13},{6,14},{7,15},{8,0},{9,1},... | collective-permute-start | bytes 368648 | tf_op jit(solution)/shard_map/ppermute | solution.py:25
  59.7 0.1 broadcast_in_dim.12
  59.8 0.1 collective-permute-start.7
  59.9 2.1 %collective-permute-done.9 = f16[5,96,128]{2,1,0:T(8,128)(2,1)S(1)} collective-permute-done((f16[5,96,128]{2,1,0:T(8,128)(2,1)S(1)}, f16[5,96,128]{2,1,0:T(8,128)(2,1)S(1)}, u32[]{:S(2)}, u32[]{:S(2)}) %collective-permute-start.9) | collective-permute-done | bytes 122912 | tf_op jit(solution)/shard_map/ppermute | solution.py:25
  62.0 7.6 %collective-permute-done.8 = f16[5,96,128]{2,1,0:T(8,128)(2,1)S(1)} collective-permute-done((f16[5,96,128]{2,1,0:T(8,128)(2,1)S(1)}, f16[5,96,128]{2,1,0:T(8,128)(2,1)S(1)}, u32[]{:S(2)}, u32[]{:S(2)}) %collective-permute-start.8) | collective-permute-done | bytes 122912 | tf_op jit(solution)/shard_map/ppermute | solution.py:25
  69.6 0.0 collective-permute-done.7
  69.7 0.7 %copy_bitcast_fusion = bf16[96,512]{1,0:T(8,128)(2,1)} fusion(f32[16,96,128]{2,1,0:T(8,128)S(1)} %shard_map.67, f16[5,96,128]{2,1,0:T(8,128)(2,1)S(1)} %collective-permute-done.9, f16[5,96,128]{2,1,0:T(8,128)(2,1)S(1)} %collective-permute-done.8, f16[5,96,128]{2,1,0:T(8,128)(2,1)S(1)} %collective-permute-done.7, f32[96,128]{1,0:T(8,128)S(1)} %exponential_bitcast_fusion.1, ...), kind=kLoop, calls=%fused_computation.22 | loop fusion | flops 491520 | bytes 737280 | tf_op jit(solution)/shard_map/convert_element_type | solution.py:349
  (9 shorter events, 0.2 us)
Async XLA Ops:
  0.0 1.9 %collective-permute-start.3 = (bf16[96,1792]{1,0:T(8,128)(2,1)}, bf16[96,1792]{1,0:T(8,128)(2,1)S(1)}, u32[]{:S(2)}, u32[]{:S(2)}) collective-permute-start(bf16[96,1792]{1,0:T(8,128)(2,1)} %hidden_hbm.1), channel_id=1, source_target_pairs={{0,1},{1,0},{2,3},{3,2},{4,5},{5,4},{6,7},{7,6},{8,9},{9,8},{10,11... | collective-permute-start | bytes 1032200 | tf_op jit(solution)/shard_map/ppermute | solution.py:25
  4.7 36.2 %all-to-all-start = ((bf16[80,4,1792]{2,1,0:T(4,128)(2,1)}), bf16[80,4,1792]{2,1,0:T(4,128)(2,1)S(1)}, u32[]{:S(2)}, u32[]{:S(2)}) async-start(bf16[80,4,1792]{2,1,0:T(4,128)(2,1)} %get-tuple-element.56), calls=%async_computation | async-start | bytes 2293760 | tf_op jit(solution)/shard_map/all_to_all | solution.py:339
  17.5 4.3 %collective-permute-start.1 = (f32[16,96,128]{2,1,0:T(8,128)S(1)}, f32[16,96,128]{2,1,0:T(8,128)S(1)}, u32[]{:S(2)}, u32[]{:S(2)}) collective-permute-start(f32[16,96,128]{2,1,0:T(8,128)S(1)} %branch_1_fun.4), channel_id=1, source_target_pairs={{0,1},{1,0},{2,3},{3,2},{4,5},{5,4},{6,7},{7,6},{8,9},{9,8},{10,11... | collective-permute-start | bytes 2359304 | tf_op jit(solution)/shard_map/cond/branch_1_fun/cond/branch_1_fun/ppermute | solution.py:25
  22.4 16.6 %collective-permute-start.2 = (f16[17,96,128]{2,1,0:T(8,128)(2,1)S(1)}, f16[17,96,128]{2,1,0:T(8,128)(2,1)}, u32[]{:S(2)}, u32[]{:S(2)}) collective-permute-start(f16[17,96,128]{2,1,0:T(8,128)(2,1)S(1)} %get-tuple-element.84), channel_id=1, source_target_pairs={{0,2},{1,3},{2,0},{3,1},{4,6},{5,7},{6,4},{7,5},{8,10},{9,11},{10,... | collective-permute-start | bytes 1253384 | tf_op jit(solution)/shard_map/cond/branch_1_fun/ppermute | solution.py:25
  32.1 2.4 %collective-permute-start = (f32[16,96,128]{2,1,0:T(8,128)S(1)}, f32[16,96,128]{2,1,0:T(8,128)S(1)}, u32[]{:S(2)}, u32[]{:S(2)}) collective-permute-start(f32[16,96,128]{2,1,0:T(8,128)S(1)} %get-tuple-element.39), channel_id=1, source_target_pairs={{0,1},{1,0},{2,3},{3,2},{4,5},{5,4},{6,7},{7,6},{8,9},{9,8},{10,11... | collective-permute-start | bytes 2359304 | tf_op jit(solution)/shard_map/cond/branch_1_fun/cond/branch_1_fun/ppermute | solution.py:25
  46.6 1.9 %collective-permute-start.4 = (bf16[16,24,128]{2,1,0:T(8,128)(2,1)S(1)}, bf16[16,24,128]{2,1,0:T(8,128)(2,1)S(1)}, u32[]{:S(2)}, u32[]{:S(2)}) collective-permute-start(bf16[16,24,128]{2,1,0:T(8,128)(2,1)S(1)} %get-tuple-element.59), channel_id=1, source_target_pairs={{0,1},{1,0},{2,3},{3,2},{4,5},{5,4},{6,7},{7,6},{8,9},{9,8},{10,11... | collective-permute-start | bytes 294920 | tf_op jit(solution)/shard_map/ppermute | solution.py:25
  46.7 5.7 %collective-permute-start.5 = (bf16[16,24,128]{2,1,0:T(8,128)(2,1)S(1)}, bf16[16,24,128]{2,1,0:T(8,128)(2,1)S(1)}, u32[]{:S(2)}, u32[]{:S(2)}) collective-permute-start(bf16[16,24,128]{2,1,0:T(8,128)(2,1)S(1)} %get-tuple-element.60), channel_id=1, source_target_pairs={{0,2},{1,3},{2,0},{3,1},{4,6},{5,7},{6,4},{7,5},{8,10},{9,11},{10,... | collective-permute-start | bytes 294920 | tf_op jit(solution)/shard_map/ppermute | solution.py:25
  47.4 6.2 %collective-permute-start.6 = (bf16[16,24,128]{2,1,0:T(8,128)(2,1)S(1)}, bf16[16,24,128]{2,1,0:T(8,128)(2,1)S(1)}, u32[]{:S(2)}, u32[]{:S(2)}) collective-permute-start(bf16[16,24,128]{2,1,0:T(8,128)(2,1)S(1)} %get-tuple-element.61), channel_id=1, source_target_pairs={{0,3},{1,2},{2,1},{3,0},{4,7},{5,6},{6,5},{7,4},{8,11},{9,10},{10,... | collective-permute-start | bytes 294920 | tf_op jit(solution)/shard_map/ppermute | solution.py:25
  54.3 7.7 %collective-permute-start.9 = (f16[5,96,128]{2,1,0:T(8,128)(2,1)S(1)}, f16[5,96,128]{2,1,0:T(8,128)(2,1)S(1)}, u32[]{:S(2)}, u32[]{:S(2)}) collective-permute-start(f16[5,96,128]{2,1,0:T(8,128)(2,1)S(1)} %pad_maximum_fusion.3), channel_id=1, source_target_pairs={{0,12},{1,13},{2,14},{3,15},{4,8},{5,9},{6,10},{7,11},{8,4},{9,5},... | collective-permute-start | bytes 368648 | tf_op jit(solution)/shard_map/ppermute | solution.py:25
  57.4 12.2 %collective-permute-start.8 = (f16[5,96,128]{2,1,0:T(8,128)(2,1)S(1)}, f16[5,96,128]{2,1,0:T(8,128)(2,1)S(1)}, u32[]{:S(2)}, u32[]{:S(2)}) collective-permute-start(f16[5,96,128]{2,1,0:T(8,128)(2,1)S(1)} %pad_maximum_fusion.2), channel_id=1, source_target_pairs={{0,8},{1,9},{2,10},{3,11},{4,12},{5,13},{6,14},{7,15},{8,0},{9,1},... | collective-permute-start | bytes 368648 | tf_op jit(solution)/shard_map/ppermute | solution.py:25
  59.8 9.8 %collective-permute-start.7 = (f16[5,96,128]{2,1,0:T(8,128)(2,1)S(1)}, f16[5,96,128]{2,1,0:T(8,128)(2,1)S(1)}, u32[]{:S(2)}, u32[]{:S(2)}) collective-permute-start(f16[5,96,128]{2,1,0:T(8,128)(2,1)S(1)} %pad_maximum_fusion.1), channel_id=1, source_target_pairs={{0,4},{1,5},{2,6},{3,7},{4,0},{5,1},{6,2},{7,3},{8,12},{9,13},{10,... | collective-permute-start | bytes 368648 | tf_op jit(solution)/shard_map/ppermute | solution.py:25

commit v12 on v11

--- a/solution.py
+++ b/solution.py
@@ -14,7 +14,6 @@
 F16_TOP = 14.0
 PLANE = 4
 HELD = 24
-IN_FLIGHT = 4
 
 
 def in_hbm(value):
@@ -91,9 +90,9 @@
 
 
 def pair_sums(hidden, down_matrix, group, order, width):
-    half = group * width // LANES // 4
+    half = group * width // LANES // PLANE
     rows = hidden.shape[0]
-    share = group // 4
+    share = group // PLANE
 
     def first():
         (far,) = column_blocks(hidden, down_matrix, order[:share], width)
@@ -104,35 +103,36 @@
     def first_idle():
         return jnp.zeros((half + 1, rows, LANES), jnp.float16)
 
-    def whole():
-        sent = lax.cond(order[1] >= 0, first, first_idle)
-        pair_in = xor_permute(sent, group, 2)
-        later, _ = lax.optimization_barrier((order, sent))
-
-        def second():
-            far, near = column_blocks(hidden, down_matrix, later[2 * share :], width, groups=2)
-            return near + xor_permute(far, group, 1)
-
-        kept = lax.cond(later[2] >= 0, second, idle)
-        return kept + unpack_scaled(pair_in)
-
-    def idle():
+    sent = lax.cond(order[0] >= 0, first, first_idle)
+    pair_in = xor_permute(sent, group, 2)
+    order, _ = lax.optimization_barrier((order, sent))
+
+    def second():
+        far, near = column_blocks(hidden, down_matrix, order[2 * share :], width, groups=2)
+        return near + xor_permute(far, group, 1)
+
+    def second_idle():
         return jnp.zeros((half, rows, LANES), jnp.float32)
 
-    return lax.cond(order[0] >= 0, whole, idle)
+    kept = lax.cond(order[1] >= 0, second, second_idle)
+    return kept + unpack_scaled(pair_in)
 
 
 def line_sums(pair, group, width):
-    rows = pair.shape[1]
     parts = width // LANES
-    arrived = [
-        xor_permute(pack_scaled(pair[i * parts : (i + 1) * parts]), group, 4 * i)
-        for i in range(1, group // 4)
-    ]
-    total = pair[:parts]
-    for packed in arrived:
-        total = total + unpack_scaled(packed)
-    return jnp.transpose(total, (1, 0, 2)).reshape(rows, width)
+    lines = group // PLANE
+    sent = [pack_scaled(pair[i * parts : (i + 1) * parts]) for i in range(lines)]
+    along = [list(range(first, group, PLANE)) for first in range(PLANE)]
+    arrived = lax.all_to_all(
+        jnp.concatenate(sent, axis=0),
+        "tp",
+        split_axis=0,
+        concat_axis=0,
+        axis_index_groups=along,
+        tiled=True,
+    )
+    size = parts + 1
+    return sum(unpack_scaled(arrived[i * size : (i + 1) * size]) for i in range(lines))
 
 
 def pack_kernel(
@@ -142,31 +142,28 @@
     slot_hbm,
     adapter_hbm,
     hidden_hbm,
-    other_hbm,
     packed_ref,
     pick_ref,
+    spread_ref,
     order_ref,
     kept_ref,
     slot_ref,
     adapter_ref,
     hidden_ref,
-    other_ref,
     sems,
 ):
     rows = hidden_ref.shape[0]
     group = slot_ref.shape[0]
-    chips = group // 2
-    me = me_ref[0]
     copies = [
         pltpu.make_async_copy(slot_hbm, slot_ref, sems.at[0]),
         pltpu.make_async_copy(adapter_hbm, adapter_ref, sems.at[1]),
         pltpu.make_async_copy(hidden_hbm, hidden_ref, sems.at[2]),
-        pltpu.make_async_copy(other_hbm, other_ref, sems.at[3]),
     ]
     for copy in copies:
         copy.start()
-    for i, offset in enumerate(orders):
-        order_ref[i] = me ^ offset
+    me = me_ref[0]
+    for i, (line, k) in enumerate(orders):
+        order_ref[i] = PLANE * line + (me % PLANE ^ k)
     ids = lax.broadcasted_iota(jnp.int32, (group, 1), 0)
     slots = jnp.zeros((group, 1), jnp.int32)
     copies[0].wait()
@@ -176,85 +173,87 @@
     adapter = adapter_ref[...]
     first = jnp.sum((adapter < ids).astype(jnp.int32), axis=1, keepdims=True)
     slot = jnp.sum(jnp.where(adapter == ids, slots, 0), axis=0, keepdims=True)
-    offset = slot ^ me
     first = jnp.sum(jnp.where(adapter == ids, first, 0), axis=0, keepdims=True)
     index = lax.broadcasted_iota(jnp.int32, (1, rows), 1) - first
+    held = blocks * BLOCK
+    spots = lax.broadcasted_iota(jnp.int32, (group * held, rows), 0)
+    pick = jnp.where(spots == slot * held + index, 1.0, 0.0).astype(jnp.bfloat16)
     for k in range(PLANE):
-        line = lax.broadcasted_iota(jnp.int32, (HELD, rows), 0)
-        mine = (offset == k) & (index == line)
+        spots = lax.broadcasted_iota(jnp.int32, (HELD, rows), 0)
+        mine = (slot == me ^ k) & (index == spots)
         pick_ref[k * HELD : (k + 1) * HELD] = jnp.where(mine, 1.0, 0.0).astype(jnp.bfloat16)
-    held = blocks * BLOCK
-    place = jnp.where((offset & 1) == 0, (slot >> 1) * held + index, -1)
-    spots = lax.broadcasted_iota(jnp.int32, (chips * held, rows), 0)
-    pick = jnp.where(spots == place, 1.0, 0.0).astype(jnp.bfloat16)
-    for source, source_ref in enumerate((hidden_ref, other_ref)):
-        copies[2 + source].wait()
-        packed = jnp.dot(pick, source_ref[...], preferred_element_type=jnp.float32)
-        packed = packed.astype(jnp.bfloat16).reshape(chips * blocks, BLOCK, packed.shape[1])
-        for chip in range(chips):
-            start = (2 * chip + source) * blocks
-            packed_ref[start : start + blocks] = packed[chip * blocks : (chip + 1) * blocks]
+    lines = group // PLANE
+    line = slot // PLANE
+    member = (line == lax.broadcasted_iota(jnp.int32, (lines, rows), 0)).astype(jnp.float32)
+    earlier = lax.broadcasted_iota(jnp.int32, (rows, rows), 0) < lax.broadcasted_iota(
+        jnp.int32, (rows, rows), 1
+    )
+    ahead = jnp.dot(
+        member.astype(jnp.bfloat16),
+        jnp.where(earlier, 1.0, 0.0).astype(jnp.bfloat16),
+        preferred_element_type=jnp.float32,
+    )
+    place = jnp.sum(member * ahead, axis=0, keepdims=True).astype(jnp.int32)
+    most = spread_ref.shape[0] // lines
+    spots = lax.broadcasted_iota(jnp.int32, (most, rows), 0)
+    for i in range(lines):
+        mine = (line == (me // PLANE) ^ i) & (place == spots)
+        spread_ref[i * most : (i + 1) * most] = jnp.where(mine, 1.0, 0.0).astype(jnp.bfloat16)
+    copies[2].wait()
+    packed = jnp.dot(pick, hidden_ref[...], preferred_element_type=jnp.float32)
+    packed_ref[...] = packed.astype(jnp.bfloat16).reshape(packed_ref.shape)
     kept_ref[...] = hidden_ref[...]
 
 
-def pack_rows(hidden, other, adapter_of_row, adapter_holder_slot, me, orders):
+def plane_rows(rows, group):
+    return min(PLANE * MOST, rows - (group - PLANE) * BLOCK)
+
+
+def pack_rows(hidden, adapter_of_row, adapter_holder_slot, me, orders):
     rows, depth = hidden.shape
     group = adapter_holder_slot.shape[0]
     blocks = MOST // BLOCK
     vmem = pl.BlockSpec(memory_space=pltpu.VMEM)
     smem = pl.BlockSpec(memory_space=pltpu.SMEM)
-    anywhere = pl.BlockSpec(memory_space=pl.ANY)
+    anywhere = pl.BlockSpec(memory_space=pltpu.HBM)
     return pl.pallas_call(
         functools.partial(pack_kernel, blocks, orders),
-        out_shape=[
+        out_shape=(
             jax.ShapeDtypeStruct((group * blocks, BLOCK, depth), jnp.bfloat16),
             jax.ShapeDtypeStruct((PLANE * HELD, rows), jnp.bfloat16),
+            jax.ShapeDtypeStruct((group // PLANE * plane_rows(rows, group), rows), jnp.bfloat16),
             jax.ShapeDtypeStruct((len(orders),), jnp.int32),
             jax.ShapeDtypeStruct((rows, depth), jnp.bfloat16),
-        ],
-        in_specs=[smem] + [anywhere] * 4,
-        out_specs=[vmem, vmem, smem, vmem],
+        ),
+        in_specs=[smem, anywhere, anywhere, anywhere],
+        out_specs=(vmem, vmem, vmem, smem, vmem),
         scratch_shapes=[
             pltpu.SMEM((group,), jnp.int32),
             pltpu.VMEM((1, rows), jnp.int32),
             pltpu.VMEM((rows, depth), jnp.bfloat16),
-            pltpu.VMEM((rows, depth), jnp.bfloat16),
-            pltpu.SemaphoreType.DMA((4,)),
+            pltpu.SemaphoreType.DMA((3,)),
         ],
         compiler_params=pltpu.CompilerParams(vmem_limit_bytes=24 * 2**20),
-    )(
-        me.reshape(1),
-        in_hbm(adapter_holder_slot),
-        in_hbm(adapter_of_row.reshape(1, rows)),
-        in_hbm(hidden),
-        other,
-    )
-
-
-def adapter_kernel(parts, me_ref, rows_ref, shrink_hbm, expand_hbm, *refs):
+    )(me.reshape(1), in_hbm(adapter_holder_slot), in_hbm(adapter_of_row.reshape(1, rows)), in_hbm(hidden))
+
+
+def adapter_kernel(parts, me_ref, rows_ref, expand_ref, shrink_hbm, *refs):
     out_refs = refs[:PLANE]
-    shrink_ref, expand_ref, total_ref, sems, expand_sem = refs[PLANE:]
+    shrink_ref, total_ref, sems = refs[PLANE:]
     me = me_ref[0]
     group, _, depth = shrink_ref.shape
     blocks = MOST // BLOCK
 
     def copy(source):
-        device = source // 2 * 2 + ((me & 1) ^ (source % 2))
-        start = pl.multiple_of(device * depth, LANES)
         return pltpu.make_async_copy(
-            shrink_hbm.at[:, pl.ds(start, depth)], shrink_ref.at[source], sems.at[source]
+            shrink_hbm.at[:, pl.ds(source * depth, depth)], shrink_ref.at[source], sems.at[source]
         )
 
-    for source in range(IN_FLIGHT):
+    for source in range(group):
         copy(source).start()
-    expand_copy = pltpu.make_async_copy(expand_hbm, expand_ref, expand_sem)
     total = jnp.zeros((MOST, total_ref.shape[1]), jnp.float32)
     for source in range(group):
         copy(source).wait()
-        if source + IN_FLIGHT < group:
-            copy(source + IN_FLIGHT).start()
-        elif source + IN_FLIGHT == group:
-            expand_copy.start()
         own = rows_ref[source * blocks : (source + 1) * blocks].reshape(MOST, depth)
         total += lax.dot_general(
             own, shrink_ref[source], (((1,), (1,)), ((), ())), preferred_element_type=jnp.float32
@@ -262,11 +261,10 @@
     total_ref[...] = jnp.zeros_like(total_ref)
     total_ref[:MOST] = total
     rank_rows = total_ref[...].astype(jnp.bfloat16)
-    expand_copy.wait()
     width = parts * LANES
     for k in range(PLANE):
-        for line in range(out_refs[k].shape[0] // parts):
-            target = me ^ (PLANE * line + k)
+        for line in range(group // PLANE):
+            target = PLANE * line + (me % PLANE ^ k)
             columns = pl.ds(pl.multiple_of(target * width, LANES), width)
             piece = jnp.dot(rank_rows, expand_ref[:, columns], preferred_element_type=jnp.float32)
             piece = piece.astype(jnp.bfloat16)
@@ -281,45 +279,81 @@
     parts = model_width // group // LANES
     held = (model_width // PLANE // LANES, HELD, LANES)
     vmem = pl.BlockSpec(memory_space=pltpu.VMEM)
-    anywhere = pl.BlockSpec(memory_space=pl.ANY)
     return pl.pallas_call(
         functools.partial(adapter_kernel, parts),
         out_shape=[jax.ShapeDtypeStruct(held, jnp.bfloat16)] * PLANE,
-        in_specs=[pl.BlockSpec(memory_space=pltpu.SMEM), vmem, anywhere, anywhere],
+        in_specs=[
+            pl.BlockSpec(memory_space=pltpu.SMEM),
+            vmem,
+            vmem,
+            pl.BlockSpec(memory_space=pl.ANY),
+        ],
         out_specs=[vmem] * PLANE,
         scratch_shapes=[
             pltpu.VMEM((group, rank, depth), jnp.bfloat16),
-            pltpu.VMEM((rank, model_width), jnp.bfloat16),
             pltpu.VMEM((HELD, rank), jnp.float32),
             pltpu.SemaphoreType.DMA((group,)),
-            pltpu.SemaphoreType.DMA,
         ],
         compiler_params=pltpu.CompilerParams(vmem_limit_bytes=24 * 2**20),
-    )(me.reshape(1), gathered, in_hbm(shrink), in_hbm(expand))
-
-
-def merge_kernel(pair_ref, pick_ref, *refs):
-    in_refs, out_ref, held_ref = refs[:PLANE], refs[PLANE], refs[PLANE + 1]
+    )(me.reshape(1), gathered, expand, in_hbm(shrink))
+
+
+def line_kernel(me_ref, pick_ref, spread_ref, *refs):
+    in_refs, out_refs, held_ref = refs[:PLANE], refs[PLANE:-1], refs[-1]
+    lines = len(out_refs)
+    parts, most = out_refs[0].shape[:2]
     for k in range(PLANE):
         held_ref[:, k * HELD : (k + 1) * HELD] = in_refs[k][...]
-    pick = pick_ref[...]
-    for part in range(pair_ref.shape[0]):
-        adapter_rows = lax.dot_general(
-            pick, held_ref[part], (((0,), (0,)), ((), ())), preferred_element_type=jnp.float32
-        )
-        out_ref[part] = pair_ref[part] + ADAPTER_SCALE * adapter_rows
-
-
-def merge_adapters(pair, pick, arrived):
+    pick = lax.dot_general(
+        spread_ref[:most], pick_ref[...], (((1,), (1,)), ((), ())), preferred_element_type=jnp.float32
+    ).astype(jnp.bfloat16)
+    for i in range(lines):
+        line = (me_ref[0] // PLANE) ^ i
+        for part in range(parts):
+            piece = jnp.dot(pick, held_ref[line * parts + part], preferred_element_type=jnp.float32)
+            out_refs[i][part] = piece.astype(jnp.bfloat16)
+
+
+def line_rows(pick, spread, arrived, group, me):
+    lines = group // PLANE
+    blocks = arrived[0].shape[0]
+    most = spread.shape[0] // lines
     vmem = pl.BlockSpec(memory_space=pltpu.VMEM)
     return pl.pallas_call(
-        merge_kernel,
-        out_shape=jax.ShapeDtypeStruct(pair.shape, jnp.float32),
-        in_specs=[vmem] * (2 + PLANE),
+        line_kernel,
+        out_shape=[jax.ShapeDtypeStruct((blocks // lines, most, LANES), jnp.bfloat16)] * lines,
+        in_specs=[pl.BlockSpec(memory_space=pltpu.SMEM)] + [vmem] * (2 + PLANE),
+        out_specs=[vmem] * lines,
+        scratch_shapes=[pltpu.VMEM((blocks, PLANE * HELD, LANES), jnp.bfloat16)],
+        compiler_params=pltpu.CompilerParams(vmem_limit_bytes=24 * 2**20),
+    )(me.reshape(1), pick, spread, *arrived)
+
+
+def final_kernel(base_ref, spread_ref, *refs):
+    in_refs, out_ref = refs[:-1], refs[-1]
+    parts, most = in_refs[0].shape[:2]
+    for part in range(parts):
+        total = base_ref[part]
+        for i, in_ref in enumerate(in_refs):
+            total += ADAPTER_SCALE * lax.dot_general(
+                spread_ref[i * most : (i + 1) * most],
+                in_ref[part],
+                (((0,), (0,)), ((), ())),
+                preferred_element_type=jnp.float32,
+            )
+        out_ref[:, part * LANES : (part + 1) * LANES] = total.astype(out_ref.dtype)
+
+
+def add_adapters(base, spread, arrived):
+    parts, rows, _ = base.shape
+    vmem = pl.BlockSpec(memory_space=pltpu.VMEM)
+    return pl.pallas_call(
+        final_kernel,
+        out_shape=jax.ShapeDtypeStruct((rows, parts * LANES), jnp.bfloat16),
+        in_specs=[vmem] * (2 + len(arrived)),
         out_specs=vmem,
-        scratch_shapes=[pltpu.VMEM((pair.shape[0], PLANE * HELD, LANES), jnp.bfloat16)],
         compiler_params=pltpu.CompilerParams(vmem_limit_bytes=24 * 2**20),
-    )(pair, pick, *arrived)
+    )(base, spread, *arrived)
 
 
 def shards_by_blocks(
@@ -329,24 +363,23 @@
     me = lax.axis_index("tp")
     rows, depth = hidden.shape
     width = down_matrix.shape[1] // group
-    quads = list(range(0, group, 4))
-    orders = [q + k for k in (3, 2, 1, 0) for q in quads]
-    other = xor_permute(hidden, group, 1)
-    packed, pick, order, kept_hidden = pack_rows(
-        hidden, other, adapter_of_row, adapter_holder_slot, me, orders
-    )
-    same_core = [list(range(core, group, 2)) for core in range(2)]
-    gathered = lax.all_to_all(
-        packed, "tp", split_axis=0, concat_axis=0, axis_index_groups=same_core, tiled=True
-    )
+    lines = group // PLANE
+    orders = [(line, k) for k in (3, 2, 1, 0) for line in range(lines)]
+    packed, pick, spread, order, kept_hidden = pack_rows(
+        hidden, adapter_of_row, adapter_holder_slot, me, orders
+    )
+    gathered = lax.all_to_all(packed, "tp", split_axis=0, concat_axis=0, tiled=True)
     pair = pair_sums(kept_hidden, down_matrix, group, order, width)
     gathered, _ = lax.optimization_barrier((gathered, pair))
     shrink = jnp.swapaxes(shrink_matrices, 1, 2)[0]
     expand = jnp.swapaxes(expand_matrices, 1, 2)[0]
     outs = adapter_output(gathered, shrink, expand, group, me)
+    pair, _ = lax.optimization_barrier((pair, outs[0]))
+    base = line_sums(pair, group, width)
     arrived = [outs[0]] + [xor_permute(outs[k], group, k) for k in range(1, PLANE)]
-    merged = merge_adapters(pair, pick, arrived)
-    return line_sums(merged, group, width).astype(jnp.bfloat16)
+    sent = line_rows(pick, spread, arrived, group, me)
+    arrived = [sent[0]] + [xor_permute(sent[i], group, PLANE * i) for i in range(1, lines)]
+    return add_adapters(base, spread, arrived)
 
 
 def shards(

time: 70.8 us -> 73.1 us (1.032)
  waiting for transfers between devices: 22.6 us -> 17.1 us
  starting transfers between devices: 17.3 us -> 21.2 us
  other arithmetic: 3.68 us -> 7.51 us
  local copies, waits for them, and re-layouts: 1.69 us -> 3.61 us
  loops' own time: 1.36 us -> 0.09 us
  Pallas kernels: 23.6 us -> 22.5 us
    ppermute x10 -> x9, waiting for transfers between devices: 22.6 us -> 13.3 us  [xor_permute(): return lax.ppermute(value, 'tp', [(i, i ^ offset) for i in range(group)])]
    all_to_all x1 -> x2, starting transfers between devices: 7.19 us -> 12.5 us  [the longest x1 7.37 us: shards_by_blocks(): lax.all_to_all(packed, 'tp', split_axis=0, concat_axis=0, tiled=True)]
    all_to_all x1 -> x2, waiting for transfers between devices: 0.01 us -> 3.83 us  [the longest x1 3.83 us: line_sums(): lax.all_to_all(jnp.concatenate(sent, axis=0), 'tp', split_axis=0, concat_...]
    unnamed x0 -> x4, other arithmetic: none -> 2.9 us
    unnamed x0 -> x5, local copies, waits for them, and re-layouts: none -> 2.06 us
    pallas_call x1, Pallas kernels: 5.78 us -> 3.83 us  [adapter_output(): pl.pallas_call(functools.partial(adapter_kernel, parts), out_shape=[jax.S...]
    ppermute x10 -> x9, starting transfers between devices: 10.1 us -> 8.66 us  [xor_permute(): return lax.ppermute(value, 'tp', [(i, i ^ offset) for i in range(group)])]
    another operation x3 -> x2, loops' own time: 1.36 us -> 0.09 us  [the longest x1 0.06 us: pair_sums(): sent = lax.cond(order[0] >= 0, first, first_idle)]
  transfers between devices with their start and end apart: 11 -> 11, of which waited for: 7 -> 7; matrix products, arithmetic and copies ran while one was open for 6% -> 7% of each run, Pallas kernels for 21% -> 21%
where the time goes in v12:
time: 73.1 us; the launch traced here: 72.8 us
  Pallas kernels  22.5 us (31%)
  starting transfers between devices  21.2 us (29%)
  waiting for transfers between devices  17.1 us (23%)
  other arithmetic  7.51 us (10%)
  local copies, waits for them, and re-layouts  3.61 us (5%)
  between operations  0.79 us (1%)
    pallas_call x3, Pallas kernels, column_blocks(): pl.pallas_call(functools.partial(column_blocks_kernel, groups), out_shape...  14.8 us
    ppermute x9, waiting for transfers between devices, xor_permute(): return lax.ppermute(value, 'tp', [(i, i ^ offset) for i in range(group)])  13.3 us
    ppermute x9, starting transfers between devices, xor_permute(): return lax.ppermute(value, 'tp', [(i, i ^ offset) for i in range(group)])  8.66 us
    all_to_all x1, starting transfers between devices, shards_by_blocks(): lax.all_to_all(packed, 'tp', split_axis=0, concat_axis=0, tiled=True)  7.37 us
    all_to_all x1, starting transfers between devices, line_sums(): lax.all_to_all(jnp.concatenate(sent, axis=0), 'tp', split_axis=0, concat_...  5.16 us
    pallas_call x1, Pallas kernels, adapter_output(): pl.pallas_call(functools.partial(adapter_kernel, parts), out_shape=[jax.S...  3.83 us
    all_to_all x1, waiting for transfers between devices, line_sums(): lax.all_to_all(jnp.concatenate(sent, axis=0), 'tp', split_axis=0, concat_...  3.83 us
    unnamed x4, other arithmetic  2.9 us
  transfers between devices with their start and end apart: 11, of which 7 were waited for; matrix products, arithmetic and copies ran while one was open for 7% of the time, Pallas kernels for 21%

profile of v12, /device:TPU:0, one launch (start us, length us, event | category | flops | bytes accessed | tf_op | source)
XLA Modules:
  0.0 72.8 jit_solution(14303511308026255626)
XLA Ops:
  0.0 2.5 %shard_map.64 = (bf16[80,4,1792]{2,1,0:T(4,128)(2,1)}, bf16[96,96]{1,0:T(8,128)(2,1)S(1)}, bf16[192,96]{1,0:T(8,128)(2,1)S(1)}, s32[16]{0:T(128)S(1)}, bf16[96,1792]{1,0:T(8,128)(2,1)S(1)}) custom-call(s32[1]{0:T(128)} %bitcast.me_ref, s32[16]{0:T(128)} %slot_hbm.1, s32[1,96]{1,0:T(1,128)} %bitcast.24, bf16[96,1792]{1,0:T(8,128)(2,1)} %hidden_hbm.1), custom_call_target="tpu_custom_call" | custom-call | tf_op jit(solution)/shard_map/pallas_call | solution.py:219
  2.5 7.4 %all-to-all-start = ((bf16[80,4,1792]{2,1,0:T(4,128)(2,1)}), bf16[80,4,1792]{2,1,0:T(4,128)(2,1)S(1)}, u32[]{:S(2)}, u32[]{:S(2)}) async-start(bf16[80,4,1792]{2,1,0:T(4,128)(2,1)} %get-tuple-element.50), calls=%async_computation | async-start | bytes 2293760 | tf_op jit(solution)/shard_map/all_to_all | solution.py:371
  9.9 10.3 %conditional.2 = (f16[17,96,128]{2,1,0:T(8,128)(2,1)}) conditional(s32[]{:T(128)} %bitcast.2, () %tuple.20, (s32[16]{0:T(128)S(1)}, bf16[96,1792]{1,0:T(8,128)(2,1)S(1)}, bf16[1792,8192]{1,0:T(8,128)(2,1)}) %tuple.21), branch_computations={%region_0.0_spmd, %region_1.0_spmd} | conditional | flops 1194416 | bytes 7548864 | solution.py:106
  10.0 0.1 fusion.9
  10.0 4.2 %branch_1_fun.4 = f32[16,96,128]{2,1,0:T(8,128)S(1)} custom-call(s32[4]{0:T(128)S(1)} %get-tuple-element.71.order_ref, bf16[96,1792]{1,0:T(8,128)(2,1)S(1)} %get-tuple-element.24.hidden_ref, bf16[1792,8192]{1,0:T(8,128)(2,1)} %get-tuple-element.25.down_ref), custom_call_target="tpu_custom_call" | custom-call | flops 1000 | bytes 1000 | tf_op jit(solution)/shard_map/cond/branch_1_fun/pallas_call | solution.py:61
  14.2 0.5 collective-permute-start.1
  14.7 4.2 %branch_1_fun.3 = f32[16,96,128]{2,1,0:T(8,128)S(1)} custom-call(s32[4]{0:T(128)S(1)} %get-tuple-element.72.order_ref, bf16[96,1792]{1,0:T(8,128)(2,1)S(1)} %get-tuple-element.24.hidden_ref, bf16[1792,8192]{1,0:T(8,128)(2,1)} %get-tuple-element.25.down_ref), custom_call_target="tpu_custom_call" | custom-call | flops 1000 | bytes 1000 | tf_op jit(solution)/shard_map/cond/branch_1_fun/pallas_call | solution.py:61
  18.9 0.0 collective-permute-done.1
  18.9 0.2 abs_reduce_fusion
  19.1 0.2 multiply_convert_fusion
  19.3 0.1 broadcast_in_dim.3
  19.4 0.9 %pad_maximum_fusion = f16[17,96,128]{2,1,0:T(8,128)(2,1)} fusion(f16[1,96,128]{2,1,0:T(8,128)(2,1)S(1)} %broadcast_in_dim.3, f16[16,96,128]{2,1,0:T(8,128)(2,1)S(1)} %multiply_convert_fusion), kind=kLoop, calls=%fused_computation.2 | loop fusion | flops 208896 | bytes 835584 | tf_op jit(solution)/shard_map/cond/branch_1_fun/concatenate | solution.py:84
  20.3 1.7 %collective-permute-start.2 = (f16[17,96,128]{2,1,0:T(8,128)(2,1)}, f16[17,96,128]{2,1,0:T(8,128)(2,1)}, u32[]{:S(2)}, u32[]{:S(2)}) collective-permute-start(f16[17,96,128]{2,1,0:T(8,128)(2,1)} %get-tuple-element.89), channel_id=1, source_target_pairs={{0,2},{1,3},{2,0},{3,1},{4,6},{5,7},{6,4},{7,5},{8,10},{9,11},{10,... | collective-permute-start | bytes 1253384 | tf_op jit(solution)/shard_map/ppermute | solution.py:24
  21.9 0.6 slice.70
  23.2 0.0 copy-start
  23.2 9.8 %conditional.3 = (f32[16,96,128]{2,1,0:T(8,128)}) conditional(s32[]{:T(128)} %bitcast.3, () %tuple.23, (s32[16]{0:T(128)S(1)}, bf16[96,1792]{1,0:T(8,128)(2,1)S(1)}, bf16[1792,8192]{1,0:T(8,128)(2,1)}) %tuple.24), branch_computations={%region_3.0_spmd, %region_4.0_spmd} | conditional | flops 197608 | bytes 5506136 | solution.py:117
  23.2 0.1 slice.52.order_ref
  23.3 6.4 %branch_1_fun.5 = (f32[16,96,128]{2,1,0:T(8,128)S(1)}, f32[16,96,128]{2,1,0:T(8,128)S(1)}) custom-call(s32[8]{0:T(128)S(1)} %slice.52.order_ref, bf16[96,1792]{1,0:T(8,128)(2,1)S(1)} %get-tuple-element.27.hidden_ref, bf16[1792,8192]{1,0:T(8,128)(2,1)} %get-tuple-element.28.down_ref), custom_call_target="tpu_custom_call" | custom-call | flops 1000 | bytes 1000 | tf_op jit(solution)/shard_map/cond/branch_1_fun/pallas_call | solution.py:61
  29.7 0.1 collective-permute-start
  29.9 2.2 %collective-permute-done = f32[16,96,128]{2,1,0:T(8,128)S(1)} collective-permute-done((f32[16,96,128]{2,1,0:T(8,128)S(1)}, f32[16,96,128]{2,1,0:T(8,128)S(1)}, u32[]{:S(2)}, u32[]{:S(2)}) %collective-permute-start) | collective-permute-done | bytes 786464 | tf_op jit(solution)/shard_map/cond/branch_1_fun/ppermute | solution.py:24
  32.1 1.0 %add.18 = f32[16,96,128]{2,1,0:T(8,128)} add(f32[16,96,128]{2,1,0:T(8,128)S(1)} %get-tuple-element.29, f32[16,96,128]{2,1,0:T(8,128)S(1)} %collective-permute-done) | non-fusion elementwise | flops 196608 | bytes 2359296 | tf_op jit(solution)/shard_map/cond/branch_1_fun/add | solution.py:112
  33.1 4.0 %collective-permute-done.2 = f16[17,96,128]{2,1,0:T(8,128)(2,1)} collective-permute-done((f16[17,96,128]{2,1,0:T(8,128)(2,1)}, f16[17,96,128]{2,1,0:T(8,128)(2,1)}, u32[]{:S(2)}, u32[]{:S(2)}) %collective-permute-start.2) | collective-permute-done | bytes 417824 | tf_op jit(solution)/shard_map/ppermute | solution.py:24
  37.1 0.8 %exponential_bitcast_fusion.4 = f32[96,128]{1,0:T(8,128)S(1)} fusion(f16[17,96,128]{2,1,0:T(8,128)(2,1)} %collective-permute-done.2), kind=kLoop, calls=%fused_computation.24 | loop fusion | flops 36864 | bytes 73728 | tf_op jit(solution)/shard_map/mul | solution.py:89
  37.9 1.3 %multiply_add_fusion = f32[16,96,128]{2,1,0:T(8,128)S(1)} fusion(f32[16,96,128]{2,1,0:T(8,128)} %get-tuple-element.90, f16[17,96,128]{2,1,0:T(8,128)(2,1)} %collective-permute-done.2, f32[96,128]{1,0:T(8,128)S(1)} %exponential_bitcast_fusion.4), kind=kLoop, calls=%fused_computation.6 | loop fusion | flops 589824 | bytes 2015232 | tf_op jit(solution)/shard_map/add | solution.py:118
  39.2 0.0 all-to-all-done.rows_ref
  39.2 0.0 copy-done
  39.2 3.8 %shard_map.65 = (bf16[16,24,128]{2,1,0:T(8,128)(2,1)S(1)}, bf16[16,24,128]{2,1,0:T(8,128)(2,1)S(1)}, bf16[16,24,128]{2,1,0:T(8,128)(2,1)S(1)}, bf16[16,24,128]{2,1,0:T(8,128)(2,1)S(1)}) custom-call(s32[1]{0:T(128)} %bitcast.me_ref, bf16[80,4,1792]{2,1,0:T(4,128)(2,1)S(1)} %all-to-all-done.rows_ref, bf16[64,8192]{1,0:T(8,128)(2,1)S(1)} %bitcast.21, ...), custom_call_target="tpu_custom_call" | custom-call | tf_op jit(solution)/shard_map/pallas_call | solution.py:282
  43.1 0.2 abs_reduce_fusion.1
  43.2 0.7 %fusion.1 = f16[20,96,128]{2,1,0:T(8,128)(2,1)} fusion(f32[16,96,128]{2,1,0:T(8,128)S(1)} %multiply_add_fusion, f32[96]{0:T(128)S(1)} %get-tuple-element.84), kind=kLoop, calls=%fused_computation.16 | loop fusion | flops 98303 | bytes 295296
  44.0 0.7 constant_dynamic-update-slice_fusion.3
  44.7 0.7 fusion.2
  45.4 0.7 constant_dynamic-update-slice_fusion.2
  46.1 0.7 %fusion.3 = f16[20,96,128]{2,1,0:T(8,128)(2,1)} fusion(f16[20,96,128]{2,1,0:T(8,128)(2,1)} %constant_dynamic-update-slice_fusion.2, f32[16,96,128]{2,1,0:T(8,128)S(1)} %multiply_add_fusion, f32[96]{0:T(128)S(1)} %get-tuple-element.80), kind=kLoop, calls=%fused_computation.18 | loop fusion | flops 98304 | bytes 295296
  46.8 0.7 constant_dynamic-update-slice_fusion.1
  47.5 0.7 fusion.4
  48.2 0.7 constant_dynamic-update-slice_fusion
  48.9 5.2 %all-to-all-start.1 = ((f16[20,96,128]{2,1,0:T(8,128)(2,1)}), f16[20,96,128]{2,1,0:T(8,128)(2,1)S(1)}, u32[]{:S(2)}, u32[]{:S(2)}) async-start(f16[20,96,128]{2,1,0:T(8,128)(2,1)} %constant_dynamic-update-slice_fusion), calls=%async_computation.1 | async-start | bytes 983040 | tf_op jit(solution)/shard_map/all_to_all | solution.py:126
  54.1 0.0 collective-permute-start.3
  54.1 0.1 collective-permute-start.4
  54.2 1.7 %collective-permute-start.5 = (bf16[16,24,128]{2,1,0:T(8,128)(2,1)S(1)}, bf16[16,24,128]{2,1,0:T(8,128)(2,1)S(1)}, u32[]{:S(2)}, u32[]{:S(2)}) collective-permute-start(bf16[16,24,128]{2,1,0:T(8,128)(2,1)S(1)} %get-tuple-element.58), channel_id=1, source_target_pairs={{0,3},{1,2},{2,1},{3,0},{4,7},{5,6},{6,5},{7,4},{8,11},{9,10},{10,... | collective-permute-start | bytes 294920 | tf_op jit(solution)/shard_map/ppermute | solution.py:24
  55.9 0.0 collective-permute-done.3.refs_1_
  55.9 3.7 %collective-permute-done.4.refs_2_ = bf16[16,24,128]{2,1,0:T(8,128)(2,1)S(1)} collective-permute-done((bf16[16,24,128]{2,1,0:T(8,128)(2,1)S(1)}, bf16[16,24,128]{2,1,0:T(8,128)(2,1)S(1)}, u32[]{:S(2)}, u32[]{:S(2)}) %collective-permute-start.4) | collective-permute-done | bytes 98336 | tf_op jit(solution)/shard_map/ppermute | solution.py:24
  59.6 1.3 %collective-permute-done.5.refs_3_ = bf16[16,24,128]{2,1,0:T(8,128)(2,1)S(1)} collective-permute-done((bf16[16,24,128]{2,1,0:T(8,128)(2,1)S(1)}, bf16[16,24,128]{2,1,0:T(8,128)(2,1)S(1)}, u32[]{:S(2)}, u32[]{:S(2)}) %collective-permute-start.5) | collective-permute-done | bytes 98336 | tf_op jit(solution)/shard_map/ppermute | solution.py:24
  61.0 0.4 shard_map.66
  61.4 2.1 %collective-permute-start.6 = (bf16[4,48,128]{2,1,0:T(8,128)(2,1)S(1)}, bf16[4,48,128]{2,1,0:T(8,128)(2,1)S(1)}, u32[]{:S(2)}, u32[]{:S(2)}) collective-permute-start(bf16[4,48,128]{2,1,0:T(8,128)(2,1)S(1)} %get-tuple-element.60), channel_id=1, source_target_pairs={{0,4},{1,5},{2,6},{3,7},{4,0},{5,1},{6,2},{7,3},{8,12},{9,13},{10,... | collective-permute-start | bytes 147464 | tf_op jit(solution)/shard_map/ppermute | solution.py:24
  63.5 2.4 %collective-permute-start.7 = (bf16[4,48,128]{2,1,0:T(8,128)(2,1)S(1)}, bf16[4,48,128]{2,1,0:T(8,128)(2,1)S(1)}, u32[]{:S(2)}, u32[]{:S(2)}) collective-permute-start(bf16[4,48,128]{2,1,0:T(8,128)(2,1)S(1)} %get-tuple-element.61), channel_id=1, source_target_pairs={{0,8},{1,9},{2,10},{3,11},{4,12},{5,13},{6,14},{7,15},{8,0},{9,1},... | collective-permute-start | bytes 147464 | tf_op jit(solution)/shard_map/ppermute | solution.py:24
  65.8 0.1 collective-permute-start.8
  65.9 3.8 %all-to-all-done.1 = f16[20,96,128]{2,1,0:T(8,128)(2,1)S(1)} async-done(((f16[20,96,128]{2,1,0:T(8,128)(2,1)}), f16[20,96,128]{2,1,0:T(8,128)(2,1)S(1)}, u32[]{:S(2)}, u32[]{:S(2)}) %all-to-all-start.1) | async-done | bytes 491552 | tf_op jit(solution)/shard_map/all_to_all | solution.py:126
  69.8 0.1 multiply_add_fusion.1.base_ref
  69.9 0.0 collective-permute-done.6.refs_1_
  69.9 1.3 %collective-permute-done.7.refs_2_ = bf16[4,48,128]{2,1,0:T(8,128)(2,1)S(1)} collective-permute-done((bf16[4,48,128]{2,1,0:T(8,128)(2,1)S(1)}, bf16[4,48,128]{2,1,0:T(8,128)(2,1)S(1)}, u32[]{:S(2)}, u32[]{:S(2)}) %collective-permute-start.7) | collective-permute-done | bytes 49184 | tf_op jit(solution)/shard_map/ppermute | solution.py:24
  71.1 0.7 collective-permute-done.8.refs_3_
  71.8 0.9 %shard_map.67 = bf16[96,512]{1,0:T(8,128)(2,1)} custom-call(f32[4,96,128]{2,1,0:T(8,128)S(1)} %multiply_add_fusion.1.base_ref, bf16[192,96]{1,0:T(8,128)(2,1)S(1)} %get-tuple-element.54.spread_ref, bf16[4,48,128]{2,1,0:T(8,128)(2,1)S(1)} %get-tuple-element.59.refs_0_, bf16[4,48,128]{2,1,0:T(8,128)(2,1)S(1)} %collective-permute-done.6.refs_1_, ...), custom_call_target="tpu_custom_call" | custom-call | tf_op jit(solution)/shard_map/pallas_call | solution.py:350
  (4 shorter events, 0.1 us)
Async XLA Ops:
  2.5 36.7 %all-to-all-start = ((bf16[80,4,1792]{2,1,0:T(4,128)(2,1)}), bf16[80,4,1792]{2,1,0:T(4,128)(2,1)S(1)}, u32[]{:S(2)}, u32[]{:S(2)}) async-start(bf16[80,4,1792]{2,1,0:T(4,128)(2,1)} %get-tuple-element.50), calls=%async_computation | async-start | bytes 2293760 | tf_op jit(solution)/shard_map/all_to_all | solution.py:371
  14.2 4.7 %collective-permute-start.1 = (f32[16,96,128]{2,1,0:T(8,128)S(1)}, f32[16,96,128]{2,1,0:T(8,128)S(1)}, u32[]{:S(2)}, u32[]{:S(2)}) collective-permute-start(f32[16,96,128]{2,1,0:T(8,128)S(1)} %branch_1_fun.4), channel_id=1, source_target_pairs={{0,1},{1,0},{2,3},{3,2},{4,5},{5,4},{6,7},{7,6},{8,9},{9,8},{10,11... | collective-permute-start | bytes 2359304 | tf_op jit(solution)/shard_map/cond/branch_1_fun/ppermute | solution.py:24
  20.3 16.8 %collective-permute-start.2 = (f16[17,96,128]{2,1,0:T(8,128)(2,1)}, f16[17,96,128]{2,1,0:T(8,128)(2,1)}, u32[]{:S(2)}, u32[]{:S(2)}) collective-permute-start(f16[17,96,128]{2,1,0:T(8,128)(2,1)} %get-tuple-element.89), channel_id=1, source_target_pairs={{0,2},{1,3},{2,0},{3,1},{4,6},{5,7},{6,4},{7,5},{8,10},{9,11},{10,... | collective-permute-start | bytes 1253384 | tf_op jit(solution)/shard_map/ppermute | solution.py:24
  23.2 16.0 %copy-start = (bf16[1,8192,64]{1,2,0:T(8,128)(2,1)S(1)}, bf16[1,8192,64]{1,2,0:T(8,128)(2,1)}, u32[]{:S(2)}) copy-start(bf16[1,8192,64]{1,2,0:T(8,128)(2,1)} %param.13) | copy-start | bytes 3145732
  29.7 2.4 %collective-permute-start = (f32[16,96,128]{2,1,0:T(8,128)S(1)}, f32[16,96,128]{2,1,0:T(8,128)S(1)}, u32[]{:S(2)}, u32[]{:S(2)}) collective-permute-start(f32[16,96,128]{2,1,0:T(8,128)S(1)} %get-tuple-element.30), channel_id=1, source_target_pairs={{0,1},{1,0},{2,3},{3,2},{4,5},{5,4},{6,7},{7,6},{8,9},{9,8},{10,11... | collective-permute-start | bytes 2359304 | tf_op jit(solution)/shard_map/cond/branch_1_fun/ppermute | solution.py:24
  48.9 20.8 %all-to-all-start.1 = ((f16[20,96,128]{2,1,0:T(8,128)(2,1)}), f16[20,96,128]{2,1,0:T(8,128)(2,1)S(1)}, u32[]{:S(2)}, u32[]{:S(2)}) async-start(f16[20,96,128]{2,1,0:T(8,128)(2,1)} %constant_dynamic-update-slice_fusion), calls=%async_computation.1 | async-start | bytes 983040 | tf_op jit(solution)/shard_map/all_to_all | solution.py:126
  54.1 1.9 %collective-permute-start.3 = (bf16[16,24,128]{2,1,0:T(8,128)(2,1)S(1)}, bf16[16,24,128]{2,1,0:T(8,128)(2,1)S(1)}, u32[]{:S(2)}, u32[]{:S(2)}) collective-permute-start(bf16[16,24,128]{2,1,0:T(8,128)(2,1)S(1)} %get-tuple-element.56), channel_id=1, source_target_pairs={{0,1},{1,0},{2,3},{3,2},{4,5},{5,4},{6,7},{7,6},{8,9},{9,8},{10,11... | collective-permute-start | bytes 294920 | tf_op jit(solution)/shard_map/ppermute | solution.py:24
  54.1 5.6 %collective-permute-start.4 = (bf16[16,24,128]{2,1,0:T(8,128)(2,1)S(1)}, bf16[16,24,128]{2,1,0:T(8,128)(2,1)S(1)}, u32[]{:S(2)}, u32[]{:S(2)}) collective-permute-start(bf16[16,24,128]{2,1,0:T(8,128)(2,1)S(1)} %get-tuple-element.57), channel_id=1, source_target_pairs={{0,2},{1,3},{2,0},{3,1},{4,6},{5,7},{6,4},{7,5},{8,10},{9,11},{10,... | collective-permute-start | bytes 294920 | tf_op jit(solution)/shard_map/ppermute | solution.py:24
  54.2 6.8 %collective-permute-start.5 = (bf16[16,24,128]{2,1,0:T(8,128)(2,1)S(1)}, bf16[16,24,128]{2,1,0:T(8,128)(2,1)S(1)}, u32[]{:S(2)}, u32[]{:S(2)}) collective-permute-start(bf16[16,24,128]{2,1,0:T(8,128)(2,1)S(1)} %get-tuple-element.58), channel_id=1, source_target_pairs={{0,3},{1,2},{2,1},{3,0},{4,7},{5,6},{6,5},{7,4},{8,11},{9,10},{10,... | collective-permute-start | bytes 294920 | tf_op jit(solution)/shard_map/ppermute | solution.py:24
  61.4 8.5 %collective-permute-start.6 = (bf16[4,48,128]{2,1,0:T(8,128)(2,1)S(1)}, bf16[4,48,128]{2,1,0:T(8,128)(2,1)S(1)}, u32[]{:S(2)}, u32[]{:S(2)}) collective-permute-start(bf16[4,48,128]{2,1,0:T(8,128)(2,1)S(1)} %get-tuple-element.60), channel_id=1, source_target_pairs={{0,4},{1,5},{2,6},{3,7},{4,0},{5,1},{6,2},{7,3},{8,12},{9,13},{10,... | collective-permute-start | bytes 147464 | tf_op jit(solution)/shard_map/ppermute | solution.py:24
  63.5 7.7 %collective-permute-start.7 = (bf16[4,48,128]{2,1,0:T(8,128)(2,1)S(1)}, bf16[4,48,128]{2,1,0:T(8,128)(2,1)S(1)}, u32[]{:S(2)}, u32[]{:S(2)}) collective-permute-start(bf16[4,48,128]{2,1,0:T(8,128)(2,1)S(1)} %get-tuple-element.61), channel_id=1, source_target_pairs={{0,8},{1,9},{2,10},{3,11},{4,12},{5,13},{6,14},{7,15},{8,0},{9,1},... | collective-permute-start | bytes 147464 | tf_op jit(solution)/shard_map/ppermute | solution.py:24
  65.8 6.0 %collective-permute-start.8 = (bf16[4,48,128]{2,1,0:T(8,128)(2,1)S(1)}, bf16[4,48,128]{2,1,0:T(8,128)(2,1)S(1)}, u32[]{:S(2)}, u32[]{:S(2)}) collective-permute-start(bf16[4,48,128]{2,1,0:T(8,128)(2,1)S(1)} %get-tuple-element.62), channel_id=1, source_target_pairs={{0,12},{1,13},{2,14},{3,15},{4,8},{5,9},{6,10},{7,11},{8,4},{9,5},... | collective-permute-start | bytes 147464 | tf_op jit(solution)/shard_map/ppermute | solution.py:24

commit v13 on v12

--- a/solution.py
+++ b/solution.py
@@ -120,19 +120,14 @@
 
 def line_sums(pair, group, width):
     parts = width // LANES
-    lines = group // PLANE
-    sent = [pack_scaled(pair[i * parts : (i + 1) * parts]) for i in range(lines)]
-    along = [list(range(first, group, PLANE)) for first in range(PLANE)]
-    arrived = lax.all_to_all(
-        jnp.concatenate(sent, axis=0),
-        "tp",
-        split_axis=0,
-        concat_axis=0,
-        axis_index_groups=along,
-        tiled=True,
-    )
-    size = parts + 1
-    return sum(unpack_scaled(arrived[i * size : (i + 1) * size]) for i in range(lines))
+    arrived = [
+        xor_permute(pack_scaled(pair[i * parts : (i + 1) * parts]), group, PLANE * i)
+        for i in range(1, group // PLANE)
+    ]
+    total = pair[:parts]
+    for packed in arrived:
+        total = total + unpack_scaled(packed)
+    return total
 
 
 def pack_kernel(
@@ -163,7 +158,7 @@
         copy.start()
     me = me_ref[0]
     for i, (line, k) in enumerate(orders):
-        order_ref[i] = PLANE * line + (me % PLANE ^ k)
+        order_ref[i] = me ^ (PLANE * line + k)
     ids = lax.broadcasted_iota(jnp.int32, (group, 1), 0)
     slots = jnp.zeros((group, 1), jnp.int32)
     copies[0].wait()
@@ -264,7 +259,7 @@
     width = parts * LANES
     for k in range(PLANE):
         for line in range(group // PLANE):
-            target = PLANE * line + (me % PLANE ^ k)
+            target = me ^ (PLANE * line + k)
             columns = pl.ds(pl.multiple_of(target * width, LANES), width)
             piece = jnp.dot(rank_rows, expand_ref[:, columns], preferred_element_type=jnp.float32)
             piece = piece.astype(jnp.bfloat16)
@@ -298,7 +293,7 @@
     )(me.reshape(1), gathered, expand, in_hbm(shrink))
 
 
-def line_kernel(me_ref, pick_ref, spread_ref, *refs):
+def line_kernel(pick_ref, spread_ref, *refs):
     in_refs, out_refs, held_ref = refs[:PLANE], refs[PLANE:-1], refs[-1]
     lines = len(out_refs)
     parts, most = out_refs[0].shape[:2]
@@ -308,13 +303,12 @@
         spread_ref[:most], pick_ref[...], (((1,), (1,)), ((), ())), preferred_element_type=jnp.float32
     ).astype(jnp.bfloat16)
     for i in range(lines):
-        line = (me_ref[0] // PLANE) ^ i
         for part in range(parts):
-            piece = jnp.dot(pick, held_ref[line * parts + part], preferred_element_type=jnp.float32)
+            piece = jnp.dot(pick, held_ref[i * parts + part], preferred_element_type=jnp.float32)
             out_refs[i][part] = piece.astype(jnp.bfloat16)
 
 
-def line_rows(pick, spread, arrived, group, me):
+def line_rows(pick, spread, arrived, group):
     lines = group // PLANE
     blocks = arrived[0].shape[0]
     most = spread.shape[0] // lines
@@ -322,11 +316,11 @@
     return pl.pallas_call(
         line_kernel,
         out_shape=[jax.ShapeDtypeStruct((blocks // lines, most, LANES), jnp.bfloat16)] * lines,
-        in_specs=[pl.BlockSpec(memory_space=pltpu.SMEM)] + [vmem] * (2 + PLANE),
+        in_specs=[vmem] * (2 + PLANE),
         out_specs=[vmem] * lines,
         scratch_shapes=[pltpu.VMEM((blocks, PLANE * HELD, LANES), jnp.bfloat16)],
         compiler_params=pltpu.CompilerParams(vmem_limit_bytes=24 * 2**20),
-    )(me.reshape(1), pick, spread, *arrived)
+    )(pick, spread, *arrived)
 
 
 def final_kernel(base_ref, spread_ref, *refs):
@@ -377,7 +371,7 @@
     pair, _ = lax.optimization_barrier((pair, outs[0]))
     base = line_sums(pair, group, width)
     arrived = [outs[0]] + [xor_permute(outs[k], group, k) for k in range(1, PLANE)]
-    sent = line_rows(pick, spread, arrived, group, me)
+    sent = line_rows(pick, spread, arrived, group)
     arrived = [sent[0]] + [xor_permute(sent[i], group, PLANE * i) for i in range(1, lines)]
     return add_adapters(base, spread, arrived)
 

time: 73.1 us -> 65.7 us (0.90)
  other arithmetic: 7.51 us -> 4.93 us
  local copies, waits for them, and re-layouts: 3.61 us -> 1.1 us
  waiting for transfers between devices: 17.1 us -> 15.2 us
    all_to_all x1 -> x0, starting transfers between devices: 5.16 us -> none  [line_sums(): lax.all_to_all(jnp.concatenate(sent, axis=0), 'tp', split_axis=0, concat_...]
    ppermute x9 -> x12, starting transfers between devices: 8.66 us -> 13.4 us  [xor_permute(): return lax.ppermute(value, 'tp', [(i, i ^ offset) for i in range(group)])]
    all_to_all x1 -> x0, waiting for transfers between devices: 3.83 us -> none  [line_sums(): lax.all_to_all(jnp.concatenate(sent, axis=0), 'tp', split_axis=0, concat_...]
    unnamed x4 -> x0, other arithmetic: 2.9 us -> none
    unnamed x5 -> x2, local copies, waits for them, and re-layouts: 2.06 us -> 0.01 us
    ppermute x9 -> x12, waiting for transfers between devices: 13.3 us -> 15.2 us  [xor_permute(): return lax.ppermute(value, 'tp', [(i, i ^ offset) for i in range(group)])]
  transfers between devices with their start and end apart: 11 -> 13, of which waited for: 7 -> 6; matrix products, arithmetic and copies ran while one was open for 7% -> 9% of each run, Pallas kernels for 21% -> 23%
where the time goes in v13:
time: 65.7 us; the launch traced here: 65.4 us
  Pallas kernels  22.5 us (34%)
  starting transfers between devices  20.7 us (32%)
  waiting for transfers between devices  15.2 us (23%)
  other arithmetic  4.93 us (8%)
  local copies, waits for them, and re-layouts  1.1 us (2%)
  between operations  0.86 us (1%)
    ppermute x12, waiting for transfers between devices, xor_permute(): return lax.ppermute(value, 'tp', [(i, i ^ offset) for i in range(group)])  15.2 us
    pallas_call x3, Pallas kernels, column_blocks(): pl.pallas_call(functools.partial(column_blocks_kernel, groups), out_shape...  14.8 us
    ppermute x12, starting transfers between devices, xor_permute(): return lax.ppermute(value, 'tp', [(i, i ^ offset) for i in range(group)])  13.4 us
    all_to_all x1, starting transfers between devices, shards_by_blocks(): lax.all_to_all(packed, 'tp', split_axis=0, concat_axis=0, tiled=True)  7.37 us
    pallas_call x1, Pallas kernels, adapter_output(): pl.pallas_call(functools.partial(adapter_kernel, parts), out_shape=[jax.S...  3.83 us
    pallas_call x1, Pallas kernels, pack_rows(): pl.pallas_call(functools.partial(pack_kernel, blocks, orders), out_shape=...  2.52 us
    add x1, other arithmetic, pair_sums(): return kept + unpack_scaled(pair_in)  1.33 us
  transfers between devices with their start and end apart: 13, of which 6 were waited for; matrix products, arithmetic and copies ran while one was open for 9% of the time, Pallas kernels for 23%

profile of v13, /device:TPU:0, one launch (start us, length us, event | category | flops | bytes accessed | tf_op | source)
XLA Modules:
  0.0 65.4 jit_solution(2859041997440972473)
XLA Ops:
  0.0 2.5 %shard_map.64 = (bf16[80,4,1792]{2,1,0:T(4,128)(2,1)}, bf16[96,96]{1,0:T(8,128)(2,1)S(1)}, bf16[192,96]{1,0:T(8,128)(2,1)S(1)}, s32[16]{0:T(128)S(1)}, bf16[96,1792]{1,0:T(8,128)(2,1)S(1)}) custom-call(s32[1]{0:T(128)} %bitcast.me_ref, s32[16]{0:T(128)} %slot_hbm.1, s32[1,96]{1,0:T(1,128)} %bitcast.22, bf16[96,1792]{1,0:T(8,128)(2,1)} %hidden_hbm.1), custom_call_target="tpu_custom_call" | custom-call | tf_op jit(solution)/shard_map/pallas_call | solution.py:214
  2.5 7.4 %all-to-all-start = ((bf16[80,4,1792]{2,1,0:T(4,128)(2,1)}), bf16[80,4,1792]{2,1,0:T(4,128)(2,1)S(1)}, u32[]{:S(2)}, u32[]{:S(2)}) async-start(bf16[80,4,1792]{2,1,0:T(4,128)(2,1)} %get-tuple-element.50), calls=%async_computation | async-start | bytes 2293760 | tf_op jit(solution)/shard_map/all_to_all | solution.py:365
  9.9 10.3 %conditional.2 = (f16[17,96,128]{2,1,0:T(8,128)(2,1)}) conditional(s32[]{:T(128)} %bitcast.2, () %tuple.20, (s32[16]{0:T(128)S(1)}, bf16[96,1792]{1,0:T(8,128)(2,1)S(1)}, bf16[1792,8192]{1,0:T(8,128)(2,1)}) %tuple.21), branch_computations={%region_0.0_spmd, %region_1.0_spmd} | conditional | flops 1194416 | bytes 7548864 | solution.py:106
  10.0 0.1 fusion.4
  10.0 4.2 %branch_1_fun.4 = f32[16,96,128]{2,1,0:T(8,128)S(1)} custom-call(s32[4]{0:T(128)S(1)} %get-tuple-element.70.order_ref, bf16[96,1792]{1,0:T(8,128)(2,1)S(1)} %get-tuple-element.24.hidden_ref, bf16[1792,8192]{1,0:T(8,128)(2,1)} %get-tuple-element.25.down_ref), custom_call_target="tpu_custom_call" | custom-call | flops 1000 | bytes 1000 | tf_op jit(solution)/shard_map/cond/branch_1_fun/pallas_call | solution.py:61
  14.2 0.5 collective-permute-start.1
  14.7 4.2 %branch_1_fun.3 = f32[16,96,128]{2,1,0:T(8,128)S(1)} custom-call(s32[4]{0:T(128)S(1)} %get-tuple-element.71.order_ref, bf16[96,1792]{1,0:T(8,128)(2,1)S(1)} %get-tuple-element.24.hidden_ref, bf16[1792,8192]{1,0:T(8,128)(2,1)} %get-tuple-element.25.down_ref), custom_call_target="tpu_custom_call" | custom-call | flops 1000 | bytes 1000 | tf_op jit(solution)/shard_map/cond/branch_1_fun/pallas_call | solution.py:61
  18.9 0.0 collective-permute-done.1
  18.9 0.2 abs_reduce_fusion
  19.1 0.2 multiply_convert_fusion
  19.3 0.1 broadcast_in_dim.8
  19.4 0.9 %pad_maximum_fusion = f16[17,96,128]{2,1,0:T(8,128)(2,1)} fusion(f16[1,96,128]{2,1,0:T(8,128)(2,1)S(1)} %broadcast_in_dim.8, f16[16,96,128]{2,1,0:T(8,128)(2,1)S(1)} %multiply_convert_fusion), kind=kLoop, calls=%fused_computation.2 | loop fusion | flops 208896 | bytes 835584 | tf_op jit(solution)/shard_map/cond/branch_1_fun/concatenate | solution.py:84
  20.3 1.7 %collective-permute-start.2 = (f16[17,96,128]{2,1,0:T(8,128)(2,1)}, f16[17,96,128]{2,1,0:T(8,128)(2,1)}, u32[]{:S(2)}, u32[]{:S(2)}) collective-permute-start(f16[17,96,128]{2,1,0:T(8,128)(2,1)} %get-tuple-element.83), channel_id=1, source_target_pairs={{0,2},{1,3},{2,0},{3,1},{4,6},{5,7},{6,4},{7,5},{8,10},{9,11},{10,... | collective-permute-start | bytes 1253384 | tf_op jit(solution)/shard_map/ppermute | solution.py:24
  22.0 0.6 slice.52
  23.3 0.0 copy-start
  23.3 9.9 %conditional.3 = (f32[16,96,128]{2,1,0:T(8,128)}) conditional(s32[]{:T(128)} %bitcast.3, () %tuple.23, (s32[16]{0:T(128)S(1)}, bf16[96,1792]{1,0:T(8,128)(2,1)S(1)}, bf16[1792,8192]{1,0:T(8,128)(2,1)}) %tuple.24), branch_computations={%region_3.0_spmd, %region_4.0_spmd} | conditional | flops 197608 | bytes 5506136 | solution.py:117
  23.3 0.1 slice.36.order_ref
  23.4 6.4 %branch_1_fun.5 = (f32[16,96,128]{2,1,0:T(8,128)S(1)}, f32[16,96,128]{2,1,0:T(8,128)S(1)}) custom-call(s32[8]{0:T(128)S(1)} %slice.36.order_ref, bf16[96,1792]{1,0:T(8,128)(2,1)S(1)} %get-tuple-element.27.hidden_ref, bf16[1792,8192]{1,0:T(8,128)(2,1)} %get-tuple-element.28.down_ref), custom_call_target="tpu_custom_call" | custom-call | flops 1000 | bytes 1000 | tf_op jit(solution)/shard_map/cond/branch_1_fun/pallas_call | solution.py:61
  29.8 0.1 collective-permute-start
  29.9 2.2 %collective-permute-done = f32[16,96,128]{2,1,0:T(8,128)S(1)} collective-permute-done((f32[16,96,128]{2,1,0:T(8,128)S(1)}, f32[16,96,128]{2,1,0:T(8,128)S(1)}, u32[]{:S(2)}, u32[]{:S(2)}) %collective-permute-start) | collective-permute-done | bytes 786464 | tf_op jit(solution)/shard_map/cond/branch_1_fun/ppermute | solution.py:24
  32.1 1.0 %add.17 = f32[16,96,128]{2,1,0:T(8,128)} add(f32[16,96,128]{2,1,0:T(8,128)S(1)} %get-tuple-element.29, f32[16,96,128]{2,1,0:T(8,128)S(1)} %collective-permute-done) | non-fusion elementwise | flops 196608 | bytes 2359296 | tf_op jit(solution)/shard_map/cond/branch_1_fun/add | solution.py:112
  33.1 4.0 %collective-permute-done.2 = f16[17,96,128]{2,1,0:T(8,128)(2,1)} collective-permute-done((f16[17,96,128]{2,1,0:T(8,128)(2,1)}, f16[17,96,128]{2,1,0:T(8,128)(2,1)}, u32[]{:S(2)}, u32[]{:S(2)}) %collective-permute-start.2) | collective-permute-done | bytes 417824 | tf_op jit(solution)/shard_map/ppermute | solution.py:24
  37.1 0.8 %exponential_bitcast_fusion.3 = f32[96,128]{1,0:T(8,128)S(1)} fusion(f16[17,96,128]{2,1,0:T(8,128)(2,1)} %collective-permute-done.2), kind=kLoop, calls=%fused_computation.20 | loop fusion | flops 36864 | bytes 73728 | tf_op jit(solution)/shard_map/mul | solution.py:89
  37.9 1.3 %multiply_add_fusion = f32[16,96,128]{2,1,0:T(8,128)S(1)} fusion(f32[16,96,128]{2,1,0:T(8,128)} %get-tuple-element.84, f16[17,96,128]{2,1,0:T(8,128)(2,1)} %collective-permute-done.2, f32[96,128]{1,0:T(8,128)S(1)} %exponential_bitcast_fusion.3), kind=kLoop, calls=%fused_computation.6 | loop fusion | flops 589824 | bytes 2015232 | tf_op jit(solution)/shard_map/add | solution.py:118
  39.2 0.0 all-to-all-done.rows_ref
  39.2 0.0 copy-done
  39.2 3.8 %shard_map.65 = (bf16[16,24,128]{2,1,0:T(8,128)(2,1)S(1)}, bf16[16,24,128]{2,1,0:T(8,128)(2,1)S(1)}, bf16[16,24,128]{2,1,0:T(8,128)(2,1)S(1)}, bf16[16,24,128]{2,1,0:T(8,128)(2,1)S(1)}) custom-call(s32[1]{0:T(128)} %bitcast.me_ref, bf16[80,4,1792]{2,1,0:T(4,128)(2,1)S(1)} %all-to-all-done.rows_ref, bf16[64,8192]{1,0:T(8,128)(2,1)S(1)} %bitcast.19, ...), custom_call_target="tpu_custom_call" | custom-call | tf_op jit(solution)/shard_map/pallas_call | solution.py:277
  43.1 0.2 abs_reduce_fusion.3
  43.3 0.1 multiply_convert_fusion.3
  43.4 0.1 broadcast_in_dim.14
  43.5 3.2 %collective-permute-start.5 = (f16[5,96,128]{2,1,0:T(8,128)(2,1)S(1)}, f16[5,96,128]{2,1,0:T(8,128)(2,1)S(1)}, u32[]{:S(2)}, u32[]{:S(2)}) collective-permute-start(f16[5,96,128]{2,1,0:T(8,128)(2,1)S(1)} %pad_maximum_fusion.3), channel_id=1, source_target_pairs={{0,12},{1,13},{2,14},{3,15},{4,8},{5,9},{6,10},{7,11},{8,4},{9,5},... | collective-permute-start | bytes 368648 | tf_op jit(solution)/shard_map/ppermute | solution.py:24
  46.7 0.1 broadcast_in_dim.13
  46.8 0.9 %collective-permute-start.4 = (f16[5,96,128]{2,1,0:T(8,128)(2,1)S(1)}, f16[5,96,128]{2,1,0:T(8,128)(2,1)S(1)}, u32[]{:S(2)}, u32[]{:S(2)}) collective-permute-start(f16[5,96,128]{2,1,0:T(8,128)(2,1)S(1)} %pad_maximum_fusion.2), channel_id=1, source_target_pairs={{0,8},{1,9},{2,10},{3,11},{4,12},{5,13},{6,14},{7,15},{8,0},{9,1},... | collective-permute-start | bytes 368648 | tf_op jit(solution)/shard_map/ppermute | solution.py:24
  47.7 0.0 collective-permute-start.6
  47.7 1.4 %collective-permute-start.7 = (bf16[16,24,128]{2,1,0:T(8,128)(2,1)S(1)}, bf16[16,24,128]{2,1,0:T(8,128)(2,1)S(1)}, u32[]{:S(2)}, u32[]{:S(2)}) collective-permute-start(bf16[16,24,128]{2,1,0:T(8,128)(2,1)S(1)} %get-tuple-element.57), channel_id=1, source_target_pairs={{0,2},{1,3},{2,0},{3,1},{4,6},{5,7},{6,4},{7,5},{8,10},{9,11},{10,... | collective-permute-start | bytes 294920 | tf_op jit(solution)/shard_map/ppermute | solution.py:24
  49.1 0.5 collective-permute-start.8
  49.6 0.1 broadcast_in_dim.12
  49.7 0.0 collective-permute-done.6.refs_1_
  49.7 0.7 %collective-permute-start.3 = (f16[5,96,128]{2,1,0:T(8,128)(2,1)S(1)}, f16[5,96,128]{2,1,0:T(8,128)(2,1)S(1)}, u32[]{:S(2)}, u32[]{:S(2)}) collective-permute-start(f16[5,96,128]{2,1,0:T(8,128)(2,1)S(1)} %pad_maximum_fusion.1), channel_id=1, source_target_pairs={{0,4},{1,5},{2,6},{3,7},{4,0},{5,1},{6,2},{7,3},{8,12},{9,13},{10,... | collective-permute-start | bytes 368648 | tf_op jit(solution)/shard_map/ppermute | solution.py:24
  50.4 2.9 %collective-permute-done.7.refs_2_ = bf16[16,24,128]{2,1,0:T(8,128)(2,1)S(1)} collective-permute-done((bf16[16,24,128]{2,1,0:T(8,128)(2,1)S(1)}, bf16[16,24,128]{2,1,0:T(8,128)(2,1)S(1)}, u32[]{:S(2)}, u32[]{:S(2)}) %collective-permute-start.7) | collective-permute-done | bytes 98336 | tf_op jit(solution)/shard_map/ppermute | solution.py:24
  53.3 1.3 %collective-permute-done.8.refs_3_ = bf16[16,24,128]{2,1,0:T(8,128)(2,1)S(1)} collective-permute-done((bf16[16,24,128]{2,1,0:T(8,128)(2,1)S(1)}, bf16[16,24,128]{2,1,0:T(8,128)(2,1)S(1)}, u32[]{:S(2)}, u32[]{:S(2)}) %collective-permute-start.8) | collective-permute-done | bytes 98336 | tf_op jit(solution)/shard_map/ppermute | solution.py:24
  54.6 0.4 shard_map.66
  55.0 0.6 collective-permute-start.9
  55.7 2.9 %collective-permute-start.10 = (bf16[4,48,128]{2,1,0:T(8,128)(2,1)S(1)}, bf16[4,48,128]{2,1,0:T(8,128)(2,1)S(1)}, u32[]{:S(2)}, u32[]{:S(2)}) collective-permute-start(bf16[4,48,128]{2,1,0:T(8,128)(2,1)S(1)} %get-tuple-element.61), channel_id=1, source_target_pairs={{0,8},{1,9},{2,10},{3,11},{4,12},{5,13},{6,14},{7,15},{8,0},{9,1},... | collective-permute-start | bytes 147464 | tf_op jit(solution)/shard_map/ppermute | solution.py:24
  58.6 0.0 collective-permute-done.5
  58.6 0.9 %collective-permute-start.11 = (bf16[4,48,128]{2,1,0:T(8,128)(2,1)S(1)}, bf16[4,48,128]{2,1,0:T(8,128)(2,1)S(1)}, u32[]{:S(2)}, u32[]{:S(2)}) collective-permute-start(bf16[4,48,128]{2,1,0:T(8,128)(2,1)S(1)} %get-tuple-element.62), channel_id=1, source_target_pairs={{0,12},{1,13},{2,14},{3,15},{4,8},{5,9},{6,10},{7,11},{8,4},{9,5},... | collective-permute-start | bytes 147464 | tf_op jit(solution)/shard_map/ppermute | solution.py:24
  59.5 0.0 collective-permute-done.4
  59.5 0.0 collective-permute-done.3
  59.6 0.1 multiply_add_fusion.1.base_ref
  59.7 0.0 collective-permute-done.9.refs_1_
  59.7 1.3 %collective-permute-done.10.refs_2_ = bf16[4,48,128]{2,1,0:T(8,128)(2,1)S(1)} collective-permute-done((bf16[4,48,128]{2,1,0:T(8,128)(2,1)S(1)}, bf16[4,48,128]{2,1,0:T(8,128)(2,1)S(1)}, u32[]{:S(2)}, u32[]{:S(2)}) %collective-permute-start.10) | collective-permute-done | bytes 49184 | tf_op jit(solution)/shard_map/ppermute | solution.py:24
  61.0 3.5 %collective-permute-done.11.refs_3_ = bf16[4,48,128]{2,1,0:T(8,128)(2,1)S(1)} collective-permute-done((bf16[4,48,128]{2,1,0:T(8,128)(2,1)S(1)}, bf16[4,48,128]{2,1,0:T(8,128)(2,1)S(1)}, u32[]{:S(2)}, u32[]{:S(2)}) %collective-permute-start.11) | collective-permute-done | bytes 49184 | tf_op jit(solution)/shard_map/ppermute | solution.py:24
  64.5 0.9 %shard_map.67 = bf16[96,512]{1,0:T(8,128)(2,1)} custom-call(f32[4,96,128]{2,1,0:T(8,128)S(1)} %multiply_add_fusion.1.base_ref, bf16[192,96]{1,0:T(8,128)(2,1)S(1)} %get-tuple-element.54.spread_ref, bf16[4,48,128]{2,1,0:T(8,128)(2,1)S(1)} %get-tuple-element.59.refs_0_, bf16[4,48,128]{2,1,0:T(8,128)(2,1)S(1)} %collective-permute-done.9.refs_1_, ...), custom_call_target="tpu_custom_call" | custom-call | tf_op jit(solution)/shard_map/pallas_call | solution.py:344
  (9 shorter events, 0.2 us)
Async XLA Ops:
  2.5 36.7 %all-to-all-start = ((bf16[80,4,1792]{2,1,0:T(4,128)(2,1)}), bf16[80,4,1792]{2,1,0:T(4,128)(2,1)S(1)}, u32[]{:S(2)}, u32[]{:S(2)}) async-start(bf16[80,4,1792]{2,1,0:T(4,128)(2,1)} %get-tuple-element.50), calls=%async_computation | async-start | bytes 2293760 | tf_op jit(solution)/shard_map/all_to_all | solution.py:365
  14.2 4.7 %collective-permute-start.1 = (f32[16,96,128]{2,1,0:T(8,128)S(1)}, f32[16,96,128]{2,1,0:T(8,128)S(1)}, u32[]{:S(2)}, u32[]{:S(2)}) collective-permute-start(f32[16,96,128]{2,1,0:T(8,128)S(1)} %branch_1_fun.4), channel_id=1, source_target_pairs={{0,1},{1,0},{2,3},{3,2},{4,5},{5,4},{6,7},{7,6},{8,9},{9,8},{10,11... | collective-permute-start | bytes 2359304 | tf_op jit(solution)/shard_map/cond/branch_1_fun/ppermute | solution.py:24
  20.3 16.8 %collective-permute-start.2 = (f16[17,96,128]{2,1,0:T(8,128)(2,1)}, f16[17,96,128]{2,1,0:T(8,128)(2,1)}, u32[]{:S(2)}, u32[]{:S(2)}) collective-permute-start(f16[17,96,128]{2,1,0:T(8,128)(2,1)} %get-tuple-element.83), channel_id=1, source_target_pairs={{0,2},{1,3},{2,0},{3,1},{4,6},{5,7},{6,4},{7,5},{8,10},{9,11},{10,... | collective-permute-start | bytes 1253384 | tf_op jit(solution)/shard_map/ppermute | solution.py:24
  23.3 16.0 %copy-start = (bf16[1,8192,64]{1,2,0:T(8,128)(2,1)S(1)}, bf16[1,8192,64]{1,2,0:T(8,128)(2,1)}, u32[]{:S(2)}) copy-start(bf16[1,8192,64]{1,2,0:T(8,128)(2,1)} %param.13) | copy-start | bytes 3145732
  29.8 2.4 %collective-permute-start = (f32[16,96,128]{2,1,0:T(8,128)S(1)}, f32[16,96,128]{2,1,0:T(8,128)S(1)}, u32[]{:S(2)}, u32[]{:S(2)}) collective-permute-start(f32[16,96,128]{2,1,0:T(8,128)S(1)} %get-tuple-element.30), channel_id=1, source_target_pairs={{0,1},{1,0},{2,3},{3,2},{4,5},{5,4},{6,7},{7,6},{8,9},{9,8},{10,11... | collective-permute-start | bytes 2359304 | tf_op jit(solution)/shard_map/cond/branch_1_fun/ppermute | solution.py:24
  43.5 15.0 %collective-permute-start.5 = (f16[5,96,128]{2,1,0:T(8,128)(2,1)S(1)}, f16[5,96,128]{2,1,0:T(8,128)(2,1)S(1)}, u32[]{:S(2)}, u32[]{:S(2)}) collective-permute-start(f16[5,96,128]{2,1,0:T(8,128)(2,1)S(1)} %pad_maximum_fusion.3), channel_id=1, source_target_pairs={{0,12},{1,13},{2,14},{3,15},{4,8},{5,9},{6,10},{7,11},{8,4},{9,5},... | collective-permute-start | bytes 368648 | tf_op jit(solution)/shard_map/ppermute | solution.py:24
  46.8 12.7 %collective-permute-start.4 = (f16[5,96,128]{2,1,0:T(8,128)(2,1)S(1)}, f16[5,96,128]{2,1,0:T(8,128)(2,1)S(1)}, u32[]{:S(2)}, u32[]{:S(2)}) collective-permute-start(f16[5,96,128]{2,1,0:T(8,128)(2,1)S(1)} %pad_maximum_fusion.2), channel_id=1, source_target_pairs={{0,8},{1,9},{2,10},{3,11},{4,12},{5,13},{6,14},{7,15},{8,0},{9,1},... | collective-permute-start | bytes 368648 | tf_op jit(solution)/shard_map/ppermute | solution.py:24
  47.7 2.0 %collective-permute-start.6 = (bf16[16,24,128]{2,1,0:T(8,128)(2,1)S(1)}, bf16[16,24,128]{2,1,0:T(8,128)(2,1)S(1)}, u32[]{:S(2)}, u32[]{:S(2)}) collective-permute-start(bf16[16,24,128]{2,1,0:T(8,128)(2,1)S(1)} %get-tuple-element.56), channel_id=1, source_target_pairs={{0,1},{1,0},{2,3},{3,2},{4,5},{5,4},{6,7},{7,6},{8,9},{9,8},{10,11... | collective-permute-start | bytes 294920 | tf_op jit(solution)/shard_map/ppermute | solution.py:24
  47.7 5.6 %collective-permute-start.7 = (bf16[16,24,128]{2,1,0:T(8,128)(2,1)S(1)}, bf16[16,24,128]{2,1,0:T(8,128)(2,1)S(1)}, u32[]{:S(2)}, u32[]{:S(2)}) collective-permute-start(bf16[16,24,128]{2,1,0:T(8,128)(2,1)S(1)} %get-tuple-element.57), channel_id=1, source_target_pairs={{0,2},{1,3},{2,0},{3,1},{4,6},{5,7},{6,4},{7,5},{8,10},{9,11},{10,... | collective-permute-start | bytes 294920 | tf_op jit(solution)/shard_map/ppermute | solution.py:24
  49.1 5.5 %collective-permute-start.8 = (bf16[16,24,128]{2,1,0:T(8,128)(2,1)S(1)}, bf16[16,24,128]{2,1,0:T(8,128)(2,1)S(1)}, u32[]{:S(2)}, u32[]{:S(2)}) collective-permute-start(bf16[16,24,128]{2,1,0:T(8,128)(2,1)S(1)} %get-tuple-element.58), channel_id=1, source_target_pairs={{0,3},{1,2},{2,1},{3,0},{4,7},{5,6},{6,5},{7,4},{8,11},{9,10},{10,... | collective-permute-start | bytes 294920 | tf_op jit(solution)/shard_map/ppermute | solution.py:24
  49.7 9.8 %collective-permute-start.3 = (f16[5,96,128]{2,1,0:T(8,128)(2,1)S(1)}, f16[5,96,128]{2,1,0:T(8,128)(2,1)S(1)}, u32[]{:S(2)}, u32[]{:S(2)}) collective-permute-start(f16[5,96,128]{2,1,0:T(8,128)(2,1)S(1)} %pad_maximum_fusion.1), channel_id=1, source_target_pairs={{0,4},{1,5},{2,6},{3,7},{4,0},{5,1},{6,2},{7,3},{8,12},{9,13},{10,... | collective-permute-start | bytes 368648 | tf_op jit(solution)/shard_map/ppermute | solution.py:24
  55.0 4.6 %collective-permute-start.9 = (bf16[4,48,128]{2,1,0:T(8,128)(2,1)S(1)}, bf16[4,48,128]{2,1,0:T(8,128)(2,1)S(1)}, u32[]{:S(2)}, u32[]{:S(2)}) collective-permute-start(bf16[4,48,128]{2,1,0:T(8,128)(2,1)S(1)} %get-tuple-element.60), channel_id=1, source_target_pairs={{0,4},{1,5},{2,6},{3,7},{4,0},{5,1},{6,2},{7,3},{8,12},{9,13},{10,... | collective-permute-start | bytes 147464 | tf_op jit(solution)/shard_map/ppermute | solution.py:24
  55.7 5.3 %collective-permute-start.10 = (bf16[4,48,128]{2,1,0:T(8,128)(2,1)S(1)}, bf16[4,48,128]{2,1,0:T(8,128)(2,1)S(1)}, u32[]{:S(2)}, u32[]{:S(2)}) collective-permute-start(bf16[4,48,128]{2,1,0:T(8,128)(2,1)S(1)} %get-tuple-element.61), channel_id=1, source_target_pairs={{0,8},{1,9},{2,10},{3,11},{4,12},{5,13},{6,14},{7,15},{8,0},{9,1},... | collective-permute-start | bytes 147464 | tf_op jit(solution)/shard_map/ppermute | solution.py:24
  58.6 5.9 %collective-permute-start.11 = (bf16[4,48,128]{2,1,0:T(8,128)(2,1)S(1)}, bf16[4,48,128]{2,1,0:T(8,128)(2,1)S(1)}, u32[]{:S(2)}, u32[]{:S(2)}) collective-permute-start(bf16[4,48,128]{2,1,0:T(8,128)(2,1)S(1)} %get-tuple-element.62), channel_id=1, source_target_pairs={{0,12},{1,13},{2,14},{3,15},{4,8},{5,9},{6,10},{7,11},{8,4},{9,5},... | collective-permute-start | bytes 147464 | tf_op jit(solution)/shard_map/ppermute | solution.py:24

commit v14 on v13

--- a/solution.py
+++ b/solution.py
@@ -232,9 +232,9 @@
     )(me.reshape(1), in_hbm(adapter_holder_slot), in_hbm(adapter_of_row.reshape(1, rows)), in_hbm(hidden))
 
 
-def adapter_kernel(parts, me_ref, rows_ref, expand_ref, shrink_hbm, *refs):
+def adapter_kernel(parts, me_ref, rows_ref, expand_hbm, shrink_hbm, *refs):
     out_refs = refs[:PLANE]
-    shrink_ref, total_ref, sems = refs[PLANE:]
+    shrink_ref, expand_ref, total_ref, sems, expand_sem = refs[PLANE:]
     me = me_ref[0]
     group, _, depth = shrink_ref.shape
     blocks = MOST // BLOCK
@@ -246,6 +246,8 @@
 
     for source in range(group):
         copy(source).start()
+    expand_copy = pltpu.make_async_copy(expand_hbm, expand_ref, expand_sem)
+    expand_copy.start()
     total = jnp.zeros((MOST, total_ref.shape[1]), jnp.float32)
     for source in range(group):
         copy(source).wait()
@@ -256,6 +258,7 @@
     total_ref[...] = jnp.zeros_like(total_ref)
     total_ref[:MOST] = total
     rank_rows = total_ref[...].astype(jnp.bfloat16)
+    expand_copy.wait()
     width = parts * LANES
     for k in range(PLANE):
         for line in range(group // PLANE):
@@ -280,17 +283,19 @@
         in_specs=[
             pl.BlockSpec(memory_space=pltpu.SMEM),
             vmem,
-            vmem,
+            pl.BlockSpec(memory_space=pl.ANY),
             pl.BlockSpec(memory_space=pl.ANY),
         ],
         out_specs=[vmem] * PLANE,
         scratch_shapes=[
             pltpu.VMEM((group, rank, depth), jnp.bfloat16),
+            pltpu.VMEM((rank, model_width), jnp.bfloat16),
             pltpu.VMEM((HELD, rank), jnp.float32),
             pltpu.SemaphoreType.DMA((group,)),
+            pltpu.SemaphoreType.DMA,
         ],
         compiler_params=pltpu.CompilerParams(vmem_limit_bytes=24 * 2**20),
-    )(me.reshape(1), gathered, expand, in_hbm(shrink))
+    )(me.reshape(1), gathered, in_hbm(expand), in_hbm(shrink))
 
 
 def line_kernel(pick_ref, spread_ref, *refs):
@@ -320,6 +325,7 @@
         out_specs=[vmem] * lines,
         scratch_shapes=[pltpu.VMEM((blocks, PLANE * HELD, LANES), jnp.bfloat16)],
         compiler_params=pltpu.CompilerParams(vmem_limit_bytes=24 * 2**20),
+        cost_estimate=pl.CostEstimate(flops=1000, bytes_accessed=4_000_000, transcendentals=0),
     )(pick, spread, *arrived)
 
 

time: 65.7 us -> 64.8 us (0.986)
  other arithmetic: 4.93 us -> 3.01 us
  waiting for transfers between devices: 15.2 us -> 16.1 us
    add x1, other arithmetic: 1 us -> 0.11 us  [second(): return near + xor_permute(far, group, 1)]
    ppermute x12, waiting for transfers between devices: 15.2 us -> 16 us  [xor_permute(): return lax.ppermute(value, 'tp', [(i, i ^ offset) for i in range(group)])]
    concatenate x4, other arithmetic: 1.01 us -> 0.23 us  [pack_scaled(): return jnp.concatenate([scaled, marks], axis=0)]
  transfers between devices with their start and end apart: 13 -> 13, of which waited for: 6 -> 6; matrix products, arithmetic and copies ran while one was open for 9% -> 6% of each run, Pallas kernels for 23% -> 24%
where the time goes in v14:
time: 64.8 us; the launch traced here: 64.5 us
  Pallas kernels  22.5 us (35%)
  starting transfers between devices  20.8 us (32%)
  waiting for transfers between devices  16.1 us (25%)
  other arithmetic  3.01 us (5%)
  local copies, waits for them, and re-layouts  1.11 us (2%)
  between operations  0.91 us (1%)
    ppermute x12, waiting for transfers between devices, xor_permute(): return lax.ppermute(value, 'tp', [(i, i ^ offset) for i in range(group)])  16 us
    pallas_call x3, Pallas kernels, column_blocks(): pl.pallas_call(functools.partial(column_blocks_kernel, groups), out_shape...  14.8 us
    ppermute x12, starting transfers between devices, xor_permute(): return lax.ppermute(value, 'tp', [(i, i ^ offset) for i in range(group)])  13.4 us
    all_to_all x1, starting transfers between devices, shards_by_blocks(): lax.all_to_all(packed, 'tp', split_axis=0, concat_axis=0, tiled=True)  7.37 us
    pallas_call x1, Pallas kernels, adapter_output(): pl.pallas_call(functools.partial(adapter_kernel, parts), out_shape=[jax.S...  3.85 us
    pallas_call x1, Pallas kernels, pack_rows(): pl.pallas_call(functools.partial(pack_kernel, blocks, orders), out_shape=...  2.52 us
  transfers between devices with their start and end apart: 13, of which 6 were waited for; matrix products, arithmetic and copies ran while one was open for 6% of the time, Pallas kernels for 24%

profile of v14, /device:TPU:0, one launch (start us, length us, event | category | flops | bytes accessed | tf_op | source)
XLA Modules:
  0.0 64.5 jit_solution(17176770685752397056)
XLA Ops:
  0.0 2.5 %shard_map.64 = (bf16[80,4,1792]{2,1,0:T(4,128)(2,1)}, bf16[96,96]{1,0:T(8,128)(2,1)S(1)}, bf16[192,96]{1,0:T(8,128)(2,1)S(1)}, s32[16]{0:T(128)S(1)}, bf16[96,1792]{1,0:T(8,128)(2,1)S(1)}) custom-call(s32[1]{0:T(128)} %bitcast.me_ref, s32[16]{0:T(128)} %slot_hbm.1, s32[1,96]{1,0:T(1,128)} %bitcast.22, bf16[96,1792]{1,0:T(8,128)(2,1)} %hidden_hbm.1), custom_call_target="tpu_custom_call" | custom-call | tf_op jit(solution)/shard_map/pallas_call | solution.py:214
  2.5 7.4 %all-to-all-start = ((bf16[80,4,1792]{2,1,0:T(4,128)(2,1)}), bf16[80,4,1792]{2,1,0:T(4,128)(2,1)S(1)}, u32[]{:S(2)}, u32[]{:S(2)}) async-start(bf16[80,4,1792]{2,1,0:T(4,128)(2,1)} %get-tuple-element.50), calls=%async_computation | async-start | bytes 2293760 | tf_op jit(solution)/shard_map/all_to_all | solution.py:371
  9.9 9.5 %conditional.2 = (f16[17,96,128]{2,1,0:T(8,128)(2,1)S(1)}) conditional(s32[]{:T(128)} %bitcast.2, () %tuple.20, (s32[16]{0:T(128)S(1)}, bf16[96,1792]{1,0:T(8,128)(2,1)S(1)}, bf16[1792,8192]{1,0:T(8,128)(2,1)}) %tuple.21), branch_computations={%region_0.0_spmd, %region_1.0_spmd} | conditional | flops 1194416 | bytes 7548864 | solution.py:106
  10.0 0.1 fusion.4
  10.0 4.2 %branch_1_fun.4 = f32[16,96,128]{2,1,0:T(8,128)S(1)} custom-call(s32[4]{0:T(128)S(1)} %get-tuple-element.70.order_ref, bf16[96,1792]{1,0:T(8,128)(2,1)S(1)} %get-tuple-element.24.hidden_ref, bf16[1792,8192]{1,0:T(8,128)(2,1)} %get-tuple-element.25.down_ref), custom_call_target="tpu_custom_call" | custom-call | flops 1000 | bytes 1000 | tf_op jit(solution)/shard_map/cond/branch_1_fun/pallas_call | solution.py:61
  14.2 0.5 collective-permute-start.1
  14.7 4.2 %branch_1_fun.3 = f32[16,96,128]{2,1,0:T(8,128)S(1)} custom-call(s32[4]{0:T(128)S(1)} %get-tuple-element.71.order_ref, bf16[96,1792]{1,0:T(8,128)(2,1)S(1)} %get-tuple-element.24.hidden_ref, bf16[1792,8192]{1,0:T(8,128)(2,1)} %get-tuple-element.25.down_ref), custom_call_target="tpu_custom_call" | custom-call | flops 1000 | bytes 1000 | tf_op jit(solution)/shard_map/cond/branch_1_fun/pallas_call | solution.py:61
  18.9 0.0 collective-permute-done.1
  18.9 0.2 abs_reduce_fusion
  19.1 0.2 multiply_convert_fusion
  19.3 0.1 broadcast_in_dim.8
  19.4 0.1 pad_maximum_fusion
  19.5 1.7 %collective-permute-start.2 = (f16[17,96,128]{2,1,0:T(8,128)(2,1)S(1)}, f16[17,96,128]{2,1,0:T(8,128)(2,1)}, u32[]{:S(2)}, u32[]{:S(2)}) collective-permute-start(f16[17,96,128]{2,1,0:T(8,128)(2,1)S(1)} %get-tuple-element.83), channel_id=1, source_target_pairs={{0,2},{1,3},{2,0},{3,1},{4,6},{5,7},{6,4},{7,5},{8,10},{9,11},{10,... | collective-permute-start | bytes 1253384 | tf_op jit(solution)/shard_map/ppermute | solution.py:24
  21.2 0.7 %slice.52 = s32[1]{0:T(128)} slice(s32[16]{0:T(128)S(1)} %get-tuple-element.49), slice={[1:2]} | slice | bytes 8 | tf_op jit(solution)/shard_map/slice | solution.py:117
  22.6 9.0 %conditional.3 = (f32[16,96,128]{2,1,0:T(8,128)S(1)}) conditional(s32[]{:T(128)} %bitcast.3, () %tuple.23, (s32[16]{0:T(128)S(1)}, bf16[96,1792]{1,0:T(8,128)(2,1)S(1)}, bf16[1792,8192]{1,0:T(8,128)(2,1)}) %tuple.24), branch_computations={%region_3.0_spmd, %region_4.0_spmd} | conditional | flops 197608 | bytes 5506136 | solution.py:117
  22.6 0.1 slice.36.order_ref
  22.7 6.4 %branch_1_fun.5 = (f32[16,96,128]{2,1,0:T(8,128)S(1)}, f32[16,96,128]{2,1,0:T(8,128)S(1)}) custom-call(s32[8]{0:T(128)S(1)} %slice.36.order_ref, bf16[96,1792]{1,0:T(8,128)(2,1)S(1)} %get-tuple-element.27.hidden_ref, bf16[1792,8192]{1,0:T(8,128)(2,1)} %get-tuple-element.28.down_ref), custom_call_target="tpu_custom_call" | custom-call | flops 1000 | bytes 1000 | tf_op jit(solution)/shard_map/cond/branch_1_fun/pallas_call | solution.py:61
  29.1 0.1 collective-permute-start
  29.2 2.2 %collective-permute-done = f32[16,96,128]{2,1,0:T(8,128)S(1)} collective-permute-done((f32[16,96,128]{2,1,0:T(8,128)S(1)}, f32[16,96,128]{2,1,0:T(8,128)S(1)}, u32[]{:S(2)}, u32[]{:S(2)}) %collective-permute-start) | collective-permute-done | bytes 786464 | tf_op jit(solution)/shard_map/cond/branch_1_fun/ppermute | solution.py:24
  31.4 0.1 add.17
  31.6 5.0 %collective-permute-done.2 = f16[17,96,128]{2,1,0:T(8,128)(2,1)} collective-permute-done((f16[17,96,128]{2,1,0:T(8,128)(2,1)S(1)}, f16[17,96,128]{2,1,0:T(8,128)(2,1)}, u32[]{:S(2)}, u32[]{:S(2)}) %collective-permute-start.2) | collective-permute-done | bytes 417824 | tf_op jit(solution)/shard_map/ppermute | solution.py:24
  36.5 0.8 %exponential_bitcast_fusion.3 = f32[96,128]{1,0:T(8,128)S(1)} fusion(f16[17,96,128]{2,1,0:T(8,128)(2,1)} %collective-permute-done.2), kind=kLoop, calls=%fused_computation.20 | loop fusion | flops 36864 | bytes 73728 | tf_op jit(solution)/shard_map/mul | solution.py:89
  37.3 1.1 %multiply_add_fusion = f32[16,96,128]{2,1,0:T(8,128)S(1)} fusion(f32[16,96,128]{2,1,0:T(8,128)S(1)} %get-tuple-element.84, f16[17,96,128]{2,1,0:T(8,128)(2,1)} %collective-permute-done.2, f32[96,128]{1,0:T(8,128)S(1)} %exponential_bitcast_fusion.3), kind=kLoop, calls=%fused_computation.6 | loop fusion | flops 589824 | bytes 2015232 | tf_op jit(solution)/shard_map/add | solution.py:118
  38.4 0.0 all-to-all-done.rows_ref
  38.4 3.9 %shard_map.65 = (bf16[16,24,128]{2,1,0:T(8,128)(2,1)S(1)}, bf16[16,24,128]{2,1,0:T(8,128)(2,1)S(1)}, bf16[16,24,128]{2,1,0:T(8,128)(2,1)S(1)}, bf16[16,24,128]{2,1,0:T(8,128)(2,1)S(1)}) custom-call(s32[1]{0:T(128)} %bitcast.me_ref, bf16[80,4,1792]{2,1,0:T(4,128)(2,1)S(1)} %all-to-all-done.rows_ref, bf16[64,8192]{1,0:T(8,128)(2,1)} %bitcast.20, ...), custom_call_target="tpu_custom_call" | custom-call | tf_op jit(solution)/shard_map/pallas_call | solution.py:280
  42.3 0.2 abs_reduce_fusion.3
  42.5 0.1 multiply_convert_fusion.3
  42.6 0.1 broadcast_in_dim.14
  42.8 2.9 %collective-permute-start.5 = (f16[5,96,128]{2,1,0:T(8,128)(2,1)S(1)}, f16[5,96,128]{2,1,0:T(8,128)(2,1)S(1)}, u32[]{:S(2)}, u32[]{:S(2)}) collective-permute-start(f16[5,96,128]{2,1,0:T(8,128)(2,1)S(1)} %pad_maximum_fusion.3), channel_id=1, source_target_pairs={{0,12},{1,13},{2,14},{3,15},{4,8},{5,9},{6,10},{7,11},{8,4},{9,5},... | collective-permute-start | bytes 368648 | tf_op jit(solution)/shard_map/ppermute | solution.py:24
  45.7 0.1 broadcast_in_dim.13
  45.8 1.0 %collective-permute-start.4 = (f16[5,96,128]{2,1,0:T(8,128)(2,1)S(1)}, f16[5,96,128]{2,1,0:T(8,128)(2,1)S(1)}, u32[]{:S(2)}, u32[]{:S(2)}) collective-permute-start(f16[5,96,128]{2,1,0:T(8,128)(2,1)S(1)} %pad_maximum_fusion.2), channel_id=1, source_target_pairs={{0,8},{1,9},{2,10},{3,11},{4,12},{5,13},{6,14},{7,15},{8,0},{9,1},... | collective-permute-start | bytes 368648 | tf_op jit(solution)/shard_map/ppermute | solution.py:24
  46.8 0.0 collective-permute-start.6
  46.8 0.9 %collective-permute-start.7 = (bf16[16,24,128]{2,1,0:T(8,128)(2,1)S(1)}, bf16[16,24,128]{2,1,0:T(8,128)(2,1)S(1)}, u32[]{:S(2)}, u32[]{:S(2)}) collective-permute-start(bf16[16,24,128]{2,1,0:T(8,128)(2,1)S(1)} %get-tuple-element.57), channel_id=1, source_target_pairs={{0,2},{1,3},{2,0},{3,1},{4,6},{5,7},{6,4},{7,5},{8,10},{9,11},{10,... | collective-permute-start | bytes 294920 | tf_op jit(solution)/shard_map/ppermute | solution.py:24
  47.7 1.0 %collective-permute-start.8 = (bf16[16,24,128]{2,1,0:T(8,128)(2,1)S(1)}, bf16[16,24,128]{2,1,0:T(8,128)(2,1)S(1)}, u32[]{:S(2)}, u32[]{:S(2)}) collective-permute-start(bf16[16,24,128]{2,1,0:T(8,128)(2,1)S(1)} %get-tuple-element.58), channel_id=1, source_target_pairs={{0,3},{1,2},{2,1},{3,0},{4,7},{5,6},{6,5},{7,4},{8,11},{9,10},{10,... | collective-permute-start | bytes 294920 | tf_op jit(solution)/shard_map/ppermute | solution.py:24
  48.6 0.1 broadcast_in_dim.12
  48.8 0.0 collective-permute-done.6.refs_1_
  48.8 0.9 %collective-permute-start.3 = (f16[5,96,128]{2,1,0:T(8,128)(2,1)S(1)}, f16[5,96,128]{2,1,0:T(8,128)(2,1)S(1)}, u32[]{:S(2)}, u32[]{:S(2)}) collective-permute-start(f16[5,96,128]{2,1,0:T(8,128)(2,1)S(1)} %pad_maximum_fusion.1), channel_id=1, source_target_pairs={{0,4},{1,5},{2,6},{3,7},{4,0},{5,1},{6,2},{7,3},{8,12},{9,13},{10,... | collective-permute-start | bytes 368648 | tf_op jit(solution)/shard_map/ppermute | solution.py:24
  49.6 2.7 %collective-permute-done.7.refs_2_ = bf16[16,24,128]{2,1,0:T(8,128)(2,1)S(1)} collective-permute-done((bf16[16,24,128]{2,1,0:T(8,128)(2,1)S(1)}, bf16[16,24,128]{2,1,0:T(8,128)(2,1)S(1)}, u32[]{:S(2)}, u32[]{:S(2)}) %collective-permute-start.7) | collective-permute-done | bytes 98336 | tf_op jit(solution)/shard_map/ppermute | solution.py:24
  52.4 1.3 %collective-permute-done.8.refs_3_ = bf16[16,24,128]{2,1,0:T(8,128)(2,1)S(1)} collective-permute-done((bf16[16,24,128]{2,1,0:T(8,128)(2,1)S(1)}, bf16[16,24,128]{2,1,0:T(8,128)(2,1)S(1)}, u32[]{:S(2)}, u32[]{:S(2)}) %collective-permute-start.8) | collective-permute-done | bytes 98336 | tf_op jit(solution)/shard_map/ppermute | solution.py:24
  53.7 0.4 shard_map.66
  54.1 0.9 %collective-permute-start.9 = (bf16[4,48,128]{2,1,0:T(8,128)(2,1)S(1)}, bf16[4,48,128]{2,1,0:T(8,128)(2,1)S(1)}, u32[]{:S(2)}, u32[]{:S(2)}) collective-permute-start(bf16[4,48,128]{2,1,0:T(8,128)(2,1)S(1)} %get-tuple-element.60), channel_id=1, source_target_pairs={{0,4},{1,5},{2,6},{3,7},{4,0},{5,1},{6,2},{7,3},{8,12},{9,13},{10,... | collective-permute-start | bytes 147464 | tf_op jit(solution)/shard_map/ppermute | solution.py:24
  55.0 2.6 %collective-permute-start.10 = (bf16[4,48,128]{2,1,0:T(8,128)(2,1)S(1)}, bf16[4,48,128]{2,1,0:T(8,128)(2,1)S(1)}, u32[]{:S(2)}, u32[]{:S(2)}) collective-permute-start(bf16[4,48,128]{2,1,0:T(8,128)(2,1)S(1)} %get-tuple-element.61), channel_id=1, source_target_pairs={{0,8},{1,9},{2,10},{3,11},{4,12},{5,13},{6,14},{7,15},{8,0},{9,1},... | collective-permute-start | bytes 147464 | tf_op jit(solution)/shard_map/ppermute | solution.py:24
  57.6 0.0 collective-permute-done.5
  57.6 0.9 %collective-permute-start.11 = (bf16[4,48,128]{2,1,0:T(8,128)(2,1)S(1)}, bf16[4,48,128]{2,1,0:T(8,128)(2,1)S(1)}, u32[]{:S(2)}, u32[]{:S(2)}) collective-permute-start(bf16[4,48,128]{2,1,0:T(8,128)(2,1)S(1)} %get-tuple-element.62), channel_id=1, source_target_pairs={{0,12},{1,13},{2,14},{3,15},{4,8},{5,9},{6,10},{7,11},{8,4},{9,5},... | collective-permute-start | bytes 147464 | tf_op jit(solution)/shard_map/ppermute | solution.py:24
  58.6 0.0 collective-permute-done.4
  58.6 0.0 collective-permute-done.3
  58.7 0.1 multiply_add_fusion.1.base_ref
  58.7 0.0 collective-permute-done.9.refs_1_
  58.8 2.5 %collective-permute-done.10.refs_2_ = bf16[4,48,128]{2,1,0:T(8,128)(2,1)S(1)} collective-permute-done((bf16[4,48,128]{2,1,0:T(8,128)(2,1)S(1)}, bf16[4,48,128]{2,1,0:T(8,128)(2,1)S(1)}, u32[]{:S(2)}, u32[]{:S(2)}) %collective-permute-start.10) | collective-permute-done | bytes 49184 | tf_op jit(solution)/shard_map/ppermute | solution.py:24
  61.2 2.3 %collective-permute-done.11.refs_3_ = bf16[4,48,128]{2,1,0:T(8,128)(2,1)S(1)} collective-permute-done((bf16[4,48,128]{2,1,0:T(8,128)(2,1)S(1)}, bf16[4,48,128]{2,1,0:T(8,128)(2,1)S(1)}, u32[]{:S(2)}, u32[]{:S(2)}) %collective-permute-start.11) | collective-permute-done | bytes 49184 | tf_op jit(solution)/shard_map/ppermute | solution.py:24
  63.5 0.9 %shard_map.67 = bf16[96,512]{1,0:T(8,128)(2,1)} custom-call(f32[4,96,128]{2,1,0:T(8,128)S(1)} %multiply_add_fusion.1.base_ref, bf16[192,96]{1,0:T(8,128)(2,1)S(1)} %get-tuple-element.54.spread_ref, bf16[4,48,128]{2,1,0:T(8,128)(2,1)S(1)} %get-tuple-element.59.refs_0_, bf16[4,48,128]{2,1,0:T(8,128)(2,1)S(1)} %collective-permute-done.9.refs_1_, ...), custom_call_target="tpu_custom_call" | custom-call | tf_op jit(solution)/shard_map/pallas_call | solution.py:350
  (9 shorter events, 0.2 us)
Async XLA Ops:
  2.5 35.9 %all-to-all-start = ((bf16[80,4,1792]{2,1,0:T(4,128)(2,1)}), bf16[80,4,1792]{2,1,0:T(4,128)(2,1)S(1)}, u32[]{:S(2)}, u32[]{:S(2)}) async-start(bf16[80,4,1792]{2,1,0:T(4,128)(2,1)} %get-tuple-element.50), calls=%async_computation | async-start | bytes 2293760 | tf_op jit(solution)/shard_map/all_to_all | solution.py:371
  14.2 4.7 %collective-permute-start.1 = (f32[16,96,128]{2,1,0:T(8,128)S(1)}, f32[16,96,128]{2,1,0:T(8,128)S(1)}, u32[]{:S(2)}, u32[]{:S(2)}) collective-permute-start(f32[16,96,128]{2,1,0:T(8,128)S(1)} %branch_1_fun.4), channel_id=1, source_target_pairs={{0,1},{1,0},{2,3},{3,2},{4,5},{5,4},{6,7},{7,6},{8,9},{9,8},{10,11... | collective-permute-start | bytes 2359304 | tf_op jit(solution)/shard_map/cond/branch_1_fun/ppermute | solution.py:24
  19.5 17.1 %collective-permute-start.2 = (f16[17,96,128]{2,1,0:T(8,128)(2,1)S(1)}, f16[17,96,128]{2,1,0:T(8,128)(2,1)}, u32[]{:S(2)}, u32[]{:S(2)}) collective-permute-start(f16[17,96,128]{2,1,0:T(8,128)(2,1)S(1)} %get-tuple-element.83), channel_id=1, source_target_pairs={{0,2},{1,3},{2,0},{3,1},{4,6},{5,7},{6,4},{7,5},{8,10},{9,11},{10,... | collective-permute-start | bytes 1253384 | tf_op jit(solution)/shard_map/ppermute | solution.py:24
  29.1 2.4 %collective-permute-start = (f32[16,96,128]{2,1,0:T(8,128)S(1)}, f32[16,96,128]{2,1,0:T(8,128)S(1)}, u32[]{:S(2)}, u32[]{:S(2)}) collective-permute-start(f32[16,96,128]{2,1,0:T(8,128)S(1)} %get-tuple-element.30), channel_id=1, source_target_pairs={{0,1},{1,0},{2,3},{3,2},{4,5},{5,4},{6,7},{7,6},{8,9},{9,8},{10,11... | collective-permute-start | bytes 2359304 | tf_op jit(solution)/shard_map/cond/branch_1_fun/ppermute | solution.py:24
  42.8 14.9 %collective-permute-start.5 = (f16[5,96,128]{2,1,0:T(8,128)(2,1)S(1)}, f16[5,96,128]{2,1,0:T(8,128)(2,1)S(1)}, u32[]{:S(2)}, u32[]{:S(2)}) collective-permute-start(f16[5,96,128]{2,1,0:T(8,128)(2,1)S(1)} %pad_maximum_fusion.3), channel_id=1, source_target_pairs={{0,12},{1,13},{2,14},{3,15},{4,8},{5,9},{6,10},{7,11},{8,4},{9,5},... | collective-permute-start | bytes 368648 | tf_op jit(solution)/shard_map/ppermute | solution.py:24
  45.8 12.8 %collective-permute-start.4 = (f16[5,96,128]{2,1,0:T(8,128)(2,1)S(1)}, f16[5,96,128]{2,1,0:T(8,128)(2,1)S(1)}, u32[]{:S(2)}, u32[]{:S(2)}) collective-permute-start(f16[5,96,128]{2,1,0:T(8,128)(2,1)S(1)} %pad_maximum_fusion.2), channel_id=1, source_target_pairs={{0,8},{1,9},{2,10},{3,11},{4,12},{5,13},{6,14},{7,15},{8,0},{9,1},... | collective-permute-start | bytes 368648 | tf_op jit(solution)/shard_map/ppermute | solution.py:24
  46.8 2.0 %collective-permute-start.6 = (bf16[16,24,128]{2,1,0:T(8,128)(2,1)S(1)}, bf16[16,24,128]{2,1,0:T(8,128)(2,1)S(1)}, u32[]{:S(2)}, u32[]{:S(2)}) collective-permute-start(bf16[16,24,128]{2,1,0:T(8,128)(2,1)S(1)} %get-tuple-element.56), channel_id=1, source_target_pairs={{0,1},{1,0},{2,3},{3,2},{4,5},{5,4},{6,7},{7,6},{8,9},{9,8},{10,11... | collective-permute-start | bytes 294920 | tf_op jit(solution)/shard_map/ppermute | solution.py:24
  46.8 5.6 %collective-permute-start.7 = (bf16[16,24,128]{2,1,0:T(8,128)(2,1)S(1)}, bf16[16,24,128]{2,1,0:T(8,128)(2,1)S(1)}, u32[]{:S(2)}, u32[]{:S(2)}) collective-permute-start(bf16[16,24,128]{2,1,0:T(8,128)(2,1)S(1)} %get-tuple-element.57), channel_id=1, source_target_pairs={{0,2},{1,3},{2,0},{3,1},{4,6},{5,7},{6,4},{7,5},{8,10},{9,11},{10,... | collective-permute-start | bytes 294920 | tf_op jit(solution)/shard_map/ppermute | solution.py:24
  47.7 6.0 %collective-permute-start.8 = (bf16[16,24,128]{2,1,0:T(8,128)(2,1)S(1)}, bf16[16,24,128]{2,1,0:T(8,128)(2,1)S(1)}, u32[]{:S(2)}, u32[]{:S(2)}) collective-permute-start(bf16[16,24,128]{2,1,0:T(8,128)(2,1)S(1)} %get-tuple-element.58), channel_id=1, source_target_pairs={{0,3},{1,2},{2,1},{3,0},{4,7},{5,6},{6,5},{7,4},{8,11},{9,10},{10,... | collective-permute-start | bytes 294920 | tf_op jit(solution)/shard_map/ppermute | solution.py:24
  48.8 9.8 %collective-permute-start.3 = (f16[5,96,128]{2,1,0:T(8,128)(2,1)S(1)}, f16[5,96,128]{2,1,0:T(8,128)(2,1)S(1)}, u32[]{:S(2)}, u32[]{:S(2)}) collective-permute-start(f16[5,96,128]{2,1,0:T(8,128)(2,1)S(1)} %pad_maximum_fusion.1), channel_id=1, source_target_pairs={{0,4},{1,5},{2,6},{3,7},{4,0},{5,1},{6,2},{7,3},{8,12},{9,13},{10,... | collective-permute-start | bytes 368648 | tf_op jit(solution)/shard_map/ppermute | solution.py:24
  54.1 4.6 %collective-permute-start.9 = (bf16[4,48,128]{2,1,0:T(8,128)(2,1)S(1)}, bf16[4,48,128]{2,1,0:T(8,128)(2,1)S(1)}, u32[]{:S(2)}, u32[]{:S(2)}) collective-permute-start(bf16[4,48,128]{2,1,0:T(8,128)(2,1)S(1)} %get-tuple-element.60), channel_id=1, source_target_pairs={{0,4},{1,5},{2,6},{3,7},{4,0},{5,1},{6,2},{7,3},{8,12},{9,13},{10,... | collective-permute-start | bytes 147464 | tf_op jit(solution)/shard_map/ppermute | solution.py:24
  55.0 6.2 %collective-permute-start.10 = (bf16[4,48,128]{2,1,0:T(8,128)(2,1)S(1)}, bf16[4,48,128]{2,1,0:T(8,128)(2,1)S(1)}, u32[]{:S(2)}, u32[]{:S(2)}) collective-permute-start(bf16[4,48,128]{2,1,0:T(8,128)(2,1)S(1)} %get-tuple-element.61), channel_id=1, source_target_pairs={{0,8},{1,9},{2,10},{3,11},{4,12},{5,13},{6,14},{7,15},{8,0},{9,1},... | collective-permute-start | bytes 147464 | tf_op jit(solution)/shard_map/ppermute | solution.py:24
  57.6 5.9 %collective-permute-start.11 = (bf16[4,48,128]{2,1,0:T(8,128)(2,1)S(1)}, bf16[4,48,128]{2,1,0:T(8,128)(2,1)S(1)}, u32[]{:S(2)}, u32[]{:S(2)}) collective-permute-start(bf16[4,48,128]{2,1,0:T(8,128)(2,1)S(1)} %get-tuple-element.62), channel_id=1, source_target_pairs={{0,12},{1,13},{2,14},{3,15},{4,8},{5,9},{6,10},{7,11},{8,4},{9,5},... | collective-permute-start | bytes 147464 | tf_op jit(solution)/shard_map/ppermute | solution.py:24

commit v15 on v14

--- a/solution.py
+++ b/solution.py
@@ -325,7 +325,7 @@
         out_specs=[vmem] * lines,
         scratch_shapes=[pltpu.VMEM((blocks, PLANE * HELD, LANES), jnp.bfloat16)],
         compiler_params=pltpu.CompilerParams(vmem_limit_bytes=24 * 2**20),
-        cost_estimate=pl.CostEstimate(flops=1000, bytes_accessed=4_000_000, transcendentals=0),
+        cost_estimate=pl.CostEstimate(flops=1000, bytes_accessed=40_000_000, transcendentals=0),
     )(pick, spread, *arrived)
 
 

time: 64.8 us -> 64.8 us (level)
  no operation moved by 1% of the time
where the time goes in v15:
time: 64.8 us; the launch traced here: 64.5 us
  Pallas kernels  22.5 us (35%)
  starting transfers between devices  20.8 us (32%)
  waiting for transfers between devices  16.1 us (25%)
  other arithmetic  3.01 us (5%)
  local copies, waits for them, and re-layouts  1.11 us (2%)
  between operations  0.91 us (1%)
    ppermute x12, waiting for transfers between devices, xor_permute(): return lax.ppermute(value, 'tp', [(i, i ^ offset) for i in range(group)])  16 us
    pallas_call x3, Pallas kernels, column_blocks(): pl.pallas_call(functools.partial(column_blocks_kernel, groups), out_shape...  14.8 us
    ppermute x12, starting transfers between devices, xor_permute(): return lax.ppermute(value, 'tp', [(i, i ^ offset) for i in range(group)])  13.4 us
    all_to_all x1, starting transfers between devices, shards_by_blocks(): lax.all_to_all(packed, 'tp', split_axis=0, concat_axis=0, tiled=True)  7.37 us
    pallas_call x1, Pallas kernels, adapter_output(): pl.pallas_call(functools.partial(adapter_kernel, parts), out_shape=[jax.S...  3.85 us
    pallas_call x1, Pallas kernels, pack_rows(): pl.pallas_call(functools.partial(pack_kernel, blocks, orders), out_shape=...  2.52 us
  transfers between devices with their start and end apart: 13, of which 6 were waited for; matrix products, arithmetic and copies ran while one was open for 6% of the time, Pallas kernels for 24%

profile of v15, /device:TPU:0, one launch (start us, length us, event | category | flops | bytes accessed | tf_op | source)
XLA Modules:
  0.0 64.5 jit_solution(17176770685752397056)
XLA Ops:
  0.0 2.5 %shard_map.64 = (bf16[80,4,1792]{2,1,0:T(4,128)(2,1)}, bf16[96,96]{1,0:T(8,128)(2,1)S(1)}, bf16[192,96]{1,0:T(8,128)(2,1)S(1)}, s32[16]{0:T(128)S(1)}, bf16[96,1792]{1,0:T(8,128)(2,1)S(1)}) custom-call(s32[1]{0:T(128)} %bitcast.me_ref, s32[16]{0:T(128)} %slot_hbm.1, s32[1,96]{1,0:T(1,128)} %bitcast.22, bf16[96,1792]{1,0:T(8,128)(2,1)} %hidden_hbm.1), custom_call_target="tpu_custom_call" | custom-call | tf_op jit(solution)/shard_map/pallas_call | solution.py:214
  2.5 7.4 %all-to-all-start = ((bf16[80,4,1792]{2,1,0:T(4,128)(2,1)}), bf16[80,4,1792]{2,1,0:T(4,128)(2,1)S(1)}, u32[]{:S(2)}, u32[]{:S(2)}) async-start(bf16[80,4,1792]{2,1,0:T(4,128)(2,1)} %get-tuple-element.50), calls=%async_computation | async-start | bytes 2293760 | tf_op jit(solution)/shard_map/all_to_all | solution.py:371
  9.9 9.5 %conditional.2 = (f16[17,96,128]{2,1,0:T(8,128)(2,1)S(1)}) conditional(s32[]{:T(128)} %bitcast.2, () %tuple.20, (s32[16]{0:T(128)S(1)}, bf16[96,1792]{1,0:T(8,128)(2,1)S(1)}, bf16[1792,8192]{1,0:T(8,128)(2,1)}) %tuple.21), branch_computations={%region_0.0_spmd, %region_1.0_spmd} | conditional | flops 1194416 | bytes 7548864 | solution.py:106
  10.0 0.1 fusion.4
  10.0 4.2 %branch_1_fun.4 = f32[16,96,128]{2,1,0:T(8,128)S(1)} custom-call(s32[4]{0:T(128)S(1)} %get-tuple-element.70.order_ref, bf16[96,1792]{1,0:T(8,128)(2,1)S(1)} %get-tuple-element.24.hidden_ref, bf16[1792,8192]{1,0:T(8,128)(2,1)} %get-tuple-element.25.down_ref), custom_call_target="tpu_custom_call" | custom-call | flops 1000 | bytes 1000 | tf_op jit(solution)/shard_map/cond/branch_1_fun/pallas_call | solution.py:61
  14.2 0.5 collective-permute-start.1
  14.7 4.2 %branch_1_fun.3 = f32[16,96,128]{2,1,0:T(8,128)S(1)} custom-call(s32[4]{0:T(128)S(1)} %get-tuple-element.71.order_ref, bf16[96,1792]{1,0:T(8,128)(2,1)S(1)} %get-tuple-element.24.hidden_ref, bf16[1792,8192]{1,0:T(8,128)(2,1)} %get-tuple-element.25.down_ref), custom_call_target="tpu_custom_call" | custom-call | flops 1000 | bytes 1000 | tf_op jit(solution)/shard_map/cond/branch_1_fun/pallas_call | solution.py:61
  18.9 0.0 collective-permute-done.1
  18.9 0.2 abs_reduce_fusion
  19.1 0.2 multiply_convert_fusion
  19.3 0.1 broadcast_in_dim.8
  19.4 0.1 pad_maximum_fusion
  19.5 1.7 %collective-permute-start.2 = (f16[17,96,128]{2,1,0:T(8,128)(2,1)S(1)}, f16[17,96,128]{2,1,0:T(8,128)(2,1)}, u32[]{:S(2)}, u32[]{:S(2)}) collective-permute-start(f16[17,96,128]{2,1,0:T(8,128)(2,1)S(1)} %get-tuple-element.83), channel_id=1, source_target_pairs={{0,2},{1,3},{2,0},{3,1},{4,6},{5,7},{6,4},{7,5},{8,10},{9,11},{10,... | collective-permute-start | bytes 1253384 | tf_op jit(solution)/shard_map/ppermute | solution.py:24
  21.2 0.7 %slice.52 = s32[1]{0:T(128)} slice(s32[16]{0:T(128)S(1)} %get-tuple-element.49), slice={[1:2]} | slice | bytes 8 | tf_op jit(solution)/shard_map/slice | solution.py:117
  22.6 9.0 %conditional.3 = (f32[16,96,128]{2,1,0:T(8,128)S(1)}) conditional(s32[]{:T(128)} %bitcast.3, () %tuple.23, (s32[16]{0:T(128)S(1)}, bf16[96,1792]{1,0:T(8,128)(2,1)S(1)}, bf16[1792,8192]{1,0:T(8,128)(2,1)}) %tuple.24), branch_computations={%region_3.0_spmd, %region_4.0_spmd} | conditional | flops 197608 | bytes 5506136 | solution.py:117
  22.6 0.1 slice.36.order_ref
  22.7 6.4 %branch_1_fun.5 = (f32[16,96,128]{2,1,0:T(8,128)S(1)}, f32[16,96,128]{2,1,0:T(8,128)S(1)}) custom-call(s32[8]{0:T(128)S(1)} %slice.36.order_ref, bf16[96,1792]{1,0:T(8,128)(2,1)S(1)} %get-tuple-element.27.hidden_ref, bf16[1792,8192]{1,0:T(8,128)(2,1)} %get-tuple-element.28.down_ref), custom_call_target="tpu_custom_call" | custom-call | flops 1000 | bytes 1000 | tf_op jit(solution)/shard_map/cond/branch_1_fun/pallas_call | solution.py:61
  29.1 0.1 collective-permute-start
  29.2 2.2 %collective-permute-done = f32[16,96,128]{2,1,0:T(8,128)S(1)} collective-permute-done((f32[16,96,128]{2,1,0:T(8,128)S(1)}, f32[16,96,128]{2,1,0:T(8,128)S(1)}, u32[]{:S(2)}, u32[]{:S(2)}) %collective-permute-start) | collective-permute-done | bytes 786464 | tf_op jit(solution)/shard_map/cond/branch_1_fun/ppermute | solution.py:24
  31.4 0.1 add.17
  31.6 5.0 %collective-permute-done.2 = f16[17,96,128]{2,1,0:T(8,128)(2,1)} collective-permute-done((f16[17,96,128]{2,1,0:T(8,128)(2,1)S(1)}, f16[17,96,128]{2,1,0:T(8,128)(2,1)}, u32[]{:S(2)}, u32[]{:S(2)}) %collective-permute-start.2) | collective-permute-done | bytes 417824 | tf_op jit(solution)/shard_map/ppermute | solution.py:24
  36.5 0.8 %exponential_bitcast_fusion.3 = f32[96,128]{1,0:T(8,128)S(1)} fusion(f16[17,96,128]{2,1,0:T(8,128)(2,1)} %collective-permute-done.2), kind=kLoop, calls=%fused_computation.20 | loop fusion | flops 36864 | bytes 73728 | tf_op jit(solution)/shard_map/mul | solution.py:89
  37.3 1.1 %multiply_add_fusion = f32[16,96,128]{2,1,0:T(8,128)S(1)} fusion(f32[16,96,128]{2,1,0:T(8,128)S(1)} %get-tuple-element.84, f16[17,96,128]{2,1,0:T(8,128)(2,1)} %collective-permute-done.2, f32[96,128]{1,0:T(8,128)S(1)} %exponential_bitcast_fusion.3), kind=kLoop, calls=%fused_computation.6 | loop fusion | flops 589824 | bytes 2015232 | tf_op jit(solution)/shard_map/add | solution.py:118
  38.4 0.0 all-to-all-done.rows_ref
  38.4 3.9 %shard_map.65 = (bf16[16,24,128]{2,1,0:T(8,128)(2,1)S(1)}, bf16[16,24,128]{2,1,0:T(8,128)(2,1)S(1)}, bf16[16,24,128]{2,1,0:T(8,128)(2,1)S(1)}, bf16[16,24,128]{2,1,0:T(8,128)(2,1)S(1)}) custom-call(s32[1]{0:T(128)} %bitcast.me_ref, bf16[80,4,1792]{2,1,0:T(4,128)(2,1)S(1)} %all-to-all-done.rows_ref, bf16[64,8192]{1,0:T(8,128)(2,1)} %bitcast.20, ...), custom_call_target="tpu_custom_call" | custom-call | tf_op jit(solution)/shard_map/pallas_call | solution.py:280
  42.3 0.2 abs_reduce_fusion.3
  42.5 0.1 multiply_convert_fusion.3
  42.6 0.1 broadcast_in_dim.14
  42.8 2.9 %collective-permute-start.5 = (f16[5,96,128]{2,1,0:T(8,128)(2,1)S(1)}, f16[5,96,128]{2,1,0:T(8,128)(2,1)S(1)}, u32[]{:S(2)}, u32[]{:S(2)}) collective-permute-start(f16[5,96,128]{2,1,0:T(8,128)(2,1)S(1)} %pad_maximum_fusion.3), channel_id=1, source_target_pairs={{0,12},{1,13},{2,14},{3,15},{4,8},{5,9},{6,10},{7,11},{8,4},{9,5},... | collective-permute-start | bytes 368648 | tf_op jit(solution)/shard_map/ppermute | solution.py:24
  45.7 0.1 broadcast_in_dim.13
  45.8 1.0 %collective-permute-start.4 = (f16[5,96,128]{2,1,0:T(8,128)(2,1)S(1)}, f16[5,96,128]{2,1,0:T(8,128)(2,1)S(1)}, u32[]{:S(2)}, u32[]{:S(2)}) collective-permute-start(f16[5,96,128]{2,1,0:T(8,128)(2,1)S(1)} %pad_maximum_fusion.2), channel_id=1, source_target_pairs={{0,8},{1,9},{2,10},{3,11},{4,12},{5,13},{6,14},{7,15},{8,0},{9,1},... | collective-permute-start | bytes 368648 | tf_op jit(solution)/shard_map/ppermute | solution.py:24
  46.8 0.0 collective-permute-start.6
  46.8 0.9 %collective-permute-start.7 = (bf16[16,24,128]{2,1,0:T(8,128)(2,1)S(1)}, bf16[16,24,128]{2,1,0:T(8,128)(2,1)S(1)}, u32[]{:S(2)}, u32[]{:S(2)}) collective-permute-start(bf16[16,24,128]{2,1,0:T(8,128)(2,1)S(1)} %get-tuple-element.57), channel_id=1, source_target_pairs={{0,2},{1,3},{2,0},{3,1},{4,6},{5,7},{6,4},{7,5},{8,10},{9,11},{10,... | collective-permute-start | bytes 294920 | tf_op jit(solution)/shard_map/ppermute | solution.py:24
  47.7 1.0 %collective-permute-start.8 = (bf16[16,24,128]{2,1,0:T(8,128)(2,1)S(1)}, bf16[16,24,128]{2,1,0:T(8,128)(2,1)S(1)}, u32[]{:S(2)}, u32[]{:S(2)}) collective-permute-start(bf16[16,24,128]{2,1,0:T(8,128)(2,1)S(1)} %get-tuple-element.58), channel_id=1, source_target_pairs={{0,3},{1,2},{2,1},{3,0},{4,7},{5,6},{6,5},{7,4},{8,11},{9,10},{10,... | collective-permute-start | bytes 294920 | tf_op jit(solution)/shard_map/ppermute | solution.py:24
  48.6 0.1 broadcast_in_dim.12
  48.8 0.0 collective-permute-done.6.refs_1_
  48.8 0.9 %collective-permute-start.3 = (f16[5,96,128]{2,1,0:T(8,128)(2,1)S(1)}, f16[5,96,128]{2,1,0:T(8,128)(2,1)S(1)}, u32[]{:S(2)}, u32[]{:S(2)}) collective-permute-start(f16[5,96,128]{2,1,0:T(8,128)(2,1)S(1)} %pad_maximum_fusion.1), channel_id=1, source_target_pairs={{0,4},{1,5},{2,6},{3,7},{4,0},{5,1},{6,2},{7,3},{8,12},{9,13},{10,... | collective-permute-start | bytes 368648 | tf_op jit(solution)/shard_map/ppermute | solution.py:24
  49.6 2.7 %collective-permute-done.7.refs_2_ = bf16[16,24,128]{2,1,0:T(8,128)(2,1)S(1)} collective-permute-done((bf16[16,24,128]{2,1,0:T(8,128)(2,1)S(1)}, bf16[16,24,128]{2,1,0:T(8,128)(2,1)S(1)}, u32[]{:S(2)}, u32[]{:S(2)}) %collective-permute-start.7) | collective-permute-done | bytes 98336 | tf_op jit(solution)/shard_map/ppermute | solution.py:24
  52.4 1.3 %collective-permute-done.8.refs_3_ = bf16[16,24,128]{2,1,0:T(8,128)(2,1)S(1)} collective-permute-done((bf16[16,24,128]{2,1,0:T(8,128)(2,1)S(1)}, bf16[16,24,128]{2,1,0:T(8,128)(2,1)S(1)}, u32[]{:S(2)}, u32[]{:S(2)}) %collective-permute-start.8) | collective-permute-done | bytes 98336 | tf_op jit(solution)/shard_map/ppermute | solution.py:24
  53.7 0.4 shard_map.66
  54.1 0.9 %collective-permute-start.9 = (bf16[4,48,128]{2,1,0:T(8,128)(2,1)S(1)}, bf16[4,48,128]{2,1,0:T(8,128)(2,1)S(1)}, u32[]{:S(2)}, u32[]{:S(2)}) collective-permute-start(bf16[4,48,128]{2,1,0:T(8,128)(2,1)S(1)} %get-tuple-element.60), channel_id=1, source_target_pairs={{0,4},{1,5},{2,6},{3,7},{4,0},{5,1},{6,2},{7,3},{8,12},{9,13},{10,... | collective-permute-start | bytes 147464 | tf_op jit(solution)/shard_map/ppermute | solution.py:24
  55.0 2.6 %collective-permute-start.10 = (bf16[4,48,128]{2,1,0:T(8,128)(2,1)S(1)}, bf16[4,48,128]{2,1,0:T(8,128)(2,1)S(1)}, u32[]{:S(2)}, u32[]{:S(2)}) collective-permute-start(bf16[4,48,128]{2,1,0:T(8,128)(2,1)S(1)} %get-tuple-element.61), channel_id=1, source_target_pairs={{0,8},{1,9},{2,10},{3,11},{4,12},{5,13},{6,14},{7,15},{8,0},{9,1},... | collective-permute-start | bytes 147464 | tf_op jit(solution)/shard_map/ppermute | solution.py:24
  57.6 0.0 collective-permute-done.5
  57.6 0.9 %collective-permute-start.11 = (bf16[4,48,128]{2,1,0:T(8,128)(2,1)S(1)}, bf16[4,48,128]{2,1,0:T(8,128)(2,1)S(1)}, u32[]{:S(2)}, u32[]{:S(2)}) collective-permute-start(bf16[4,48,128]{2,1,0:T(8,128)(2,1)S(1)} %get-tuple-element.62), channel_id=1, source_target_pairs={{0,12},{1,13},{2,14},{3,15},{4,8},{5,9},{6,10},{7,11},{8,4},{9,5},... | collective-permute-start | bytes 147464 | tf_op jit(solution)/shard_map/ppermute | solution.py:24
  58.6 0.0 collective-permute-done.4
  58.6 0.0 collective-permute-done.3
  58.7 0.1 multiply_add_fusion.1.base_ref
  58.7 0.0 collective-permute-done.9.refs_1_
  58.8 2.5 %collective-permute-done.10.refs_2_ = bf16[4,48,128]{2,1,0:T(8,128)(2,1)S(1)} collective-permute-done((bf16[4,48,128]{2,1,0:T(8,128)(2,1)S(1)}, bf16[4,48,128]{2,1,0:T(8,128)(2,1)S(1)}, u32[]{:S(2)}, u32[]{:S(2)}) %collective-permute-start.10) | collective-permute-done | bytes 49184 | tf_op jit(solution)/shard_map/ppermute | solution.py:24
  61.2 2.3 %collective-permute-done.11.refs_3_ = bf16[4,48,128]{2,1,0:T(8,128)(2,1)S(1)} collective-permute-done((bf16[4,48,128]{2,1,0:T(8,128)(2,1)S(1)}, bf16[4,48,128]{2,1,0:T(8,128)(2,1)S(1)}, u32[]{:S(2)}, u32[]{:S(2)}) %collective-permute-start.11) | collective-permute-done | bytes 49184 | tf_op jit(solution)/shard_map/ppermute | solution.py:24
  63.5 0.9 %shard_map.67 = bf16[96,512]{1,0:T(8,128)(2,1)} custom-call(f32[4,96,128]{2,1,0:T(8,128)S(1)} %multiply_add_fusion.1.base_ref, bf16[192,96]{1,0:T(8,128)(2,1)S(1)} %get-tuple-element.54.spread_ref, bf16[4,48,128]{2,1,0:T(8,128)(2,1)S(1)} %get-tuple-element.59.refs_0_, bf16[4,48,128]{2,1,0:T(8,128)(2,1)S(1)} %collective-permute-done.9.refs_1_, ...), custom_call_target="tpu_custom_call" | custom-call | tf_op jit(solution)/shard_map/pallas_call | solution.py:350
  (9 shorter events, 0.2 us)
Async XLA Ops:
  2.5 35.9 %all-to-all-start = ((bf16[80,4,1792]{2,1,0:T(4,128)(2,1)}), bf16[80,4,1792]{2,1,0:T(4,128)(2,1)S(1)}, u32[]{:S(2)}, u32[]{:S(2)}) async-start(bf16[80,4,1792]{2,1,0:T(4,128)(2,1)} %get-tuple-element.50), calls=%async_computation | async-start | bytes 2293760 | tf_op jit(solution)/shard_map/all_to_all | solution.py:371
  14.2 4.7 %collective-permute-start.1 = (f32[16,96,128]{2,1,0:T(8,128)S(1)}, f32[16,96,128]{2,1,0:T(8,128)S(1)}, u32[]{:S(2)}, u32[]{:S(2)}) collective-permute-start(f32[16,96,128]{2,1,0:T(8,128)S(1)} %branch_1_fun.4), channel_id=1, source_target_pairs={{0,1},{1,0},{2,3},{3,2},{4,5},{5,4},{6,7},{7,6},{8,9},{9,8},{10,11... | collective-permute-start | bytes 2359304 | tf_op jit(solution)/shard_map/cond/branch_1_fun/ppermute | solution.py:24
  19.5 17.1 %collective-permute-start.2 = (f16[17,96,128]{2,1,0:T(8,128)(2,1)S(1)}, f16[17,96,128]{2,1,0:T(8,128)(2,1)}, u32[]{:S(2)}, u32[]{:S(2)}) collective-permute-start(f16[17,96,128]{2,1,0:T(8,128)(2,1)S(1)} %get-tuple-element.83), channel_id=1, source_target_pairs={{0,2},{1,3},{2,0},{3,1},{4,6},{5,7},{6,4},{7,5},{8,10},{9,11},{10,... | collective-permute-start | bytes 1253384 | tf_op jit(solution)/shard_map/ppermute | solution.py:24
  29.1 2.4 %collective-permute-start = (f32[16,96,128]{2,1,0:T(8,128)S(1)}, f32[16,96,128]{2,1,0:T(8,128)S(1)}, u32[]{:S(2)}, u32[]{:S(2)}) collective-permute-start(f32[16,96,128]{2,1,0:T(8,128)S(1)} %get-tuple-element.30), channel_id=1, source_target_pairs={{0,1},{1,0},{2,3},{3,2},{4,5},{5,4},{6,7},{7,6},{8,9},{9,8},{10,11... | collective-permute-start | bytes 2359304 | tf_op jit(solution)/shard_map/cond/branch_1_fun/ppermute | solution.py:24
  42.8 14.9 %collective-permute-start.5 = (f16[5,96,128]{2,1,0:T(8,128)(2,1)S(1)}, f16[5,96,128]{2,1,0:T(8,128)(2,1)S(1)}, u32[]{:S(2)}, u32[]{:S(2)}) collective-permute-start(f16[5,96,128]{2,1,0:T(8,128)(2,1)S(1)} %pad_maximum_fusion.3), channel_id=1, source_target_pairs={{0,12},{1,13},{2,14},{3,15},{4,8},{5,9},{6,10},{7,11},{8,4},{9,5},... | collective-permute-start | bytes 368648 | tf_op jit(solution)/shard_map/ppermute | solution.py:24
  45.8 12.8 %collective-permute-start.4 = (f16[5,96,128]{2,1,0:T(8,128)(2,1)S(1)}, f16[5,96,128]{2,1,0:T(8,128)(2,1)S(1)}, u32[]{:S(2)}, u32[]{:S(2)}) collective-permute-start(f16[5,96,128]{2,1,0:T(8,128)(2,1)S(1)} %pad_maximum_fusion.2), channel_id=1, source_target_pairs={{0,8},{1,9},{2,10},{3,11},{4,12},{5,13},{6,14},{7,15},{8,0},{9,1},... | collective-permute-start | bytes 368648 | tf_op jit(solution)/shard_map/ppermute | solution.py:24
  46.8 2.0 %collective-permute-start.6 = (bf16[16,24,128]{2,1,0:T(8,128)(2,1)S(1)}, bf16[16,24,128]{2,1,0:T(8,128)(2,1)S(1)}, u32[]{:S(2)}, u32[]{:S(2)}) collective-permute-start(bf16[16,24,128]{2,1,0:T(8,128)(2,1)S(1)} %get-tuple-element.56), channel_id=1, source_target_pairs={{0,1},{1,0},{2,3},{3,2},{4,5},{5,4},{6,7},{7,6},{8,9},{9,8},{10,11... | collective-permute-start | bytes 294920 | tf_op jit(solution)/shard_map/ppermute | solution.py:24
  46.8 5.6 %collective-permute-start.7 = (bf16[16,24,128]{2,1,0:T(8,128)(2,1)S(1)}, bf16[16,24,128]{2,1,0:T(8,128)(2,1)S(1)}, u32[]{:S(2)}, u32[]{:S(2)}) collective-permute-start(bf16[16,24,128]{2,1,0:T(8,128)(2,1)S(1)} %get-tuple-element.57), channel_id=1, source_target_pairs={{0,2},{1,3},{2,0},{3,1},{4,6},{5,7},{6,4},{7,5},{8,10},{9,11},{10,... | collective-permute-start | bytes 294920 | tf_op jit(solution)/shard_map/ppermute | solution.py:24
  47.7 6.0 %collective-permute-start.8 = (bf16[16,24,128]{2,1,0:T(8,128)(2,1)S(1)}, bf16[16,24,128]{2,1,0:T(8,128)(2,1)S(1)}, u32[]{:S(2)}, u32[]{:S(2)}) collective-permute-start(bf16[16,24,128]{2,1,0:T(8,128)(2,1)S(1)} %get-tuple-element.58), channel_id=1, source_target_pairs={{0,3},{1,2},{2,1},{3,0},{4,7},{5,6},{6,5},{7,4},{8,11},{9,10},{10,... | collective-permute-start | bytes 294920 | tf_op jit(solution)/shard_map/ppermute | solution.py:24
  48.8 9.8 %collective-permute-start.3 = (f16[5,96,128]{2,1,0:T(8,128)(2,1)S(1)}, f16[5,96,128]{2,1,0:T(8,128)(2,1)S(1)}, u32[]{:S(2)}, u32[]{:S(2)}) collective-permute-start(f16[5,96,128]{2,1,0:T(8,128)(2,1)S(1)} %pad_maximum_fusion.1), channel_id=1, source_target_pairs={{0,4},{1,5},{2,6},{3,7},{4,0},{5,1},{6,2},{7,3},{8,12},{9,13},{10,... | collective-permute-start | bytes 368648 | tf_op jit(solution)/shard_map/ppermute | solution.py:24
  54.1 4.6 %collective-permute-start.9 = (bf16[4,48,128]{2,1,0:T(8,128)(2,1)S(1)}, bf16[4,48,128]{2,1,0:T(8,128)(2,1)S(1)}, u32[]{:S(2)}, u32[]{:S(2)}) collective-permute-start(bf16[4,48,128]{2,1,0:T(8,128)(2,1)S(1)} %get-tuple-element.60), channel_id=1, source_target_pairs={{0,4},{1,5},{2,6},{3,7},{4,0},{5,1},{6,2},{7,3},{8,12},{9,13},{10,... | collective-permute-start | bytes 147464 | tf_op jit(solution)/shard_map/ppermute | solution.py:24
  55.0 6.2 %collective-permute-start.10 = (bf16[4,48,128]{2,1,0:T(8,128)(2,1)S(1)}, bf16[4,48,128]{2,1,0:T(8,128)(2,1)S(1)}, u32[]{:S(2)}, u32[]{:S(2)}) collective-permute-start(bf16[4,48,128]{2,1,0:T(8,128)(2,1)S(1)} %get-tuple-element.61), channel_id=1, source_target_pairs={{0,8},{1,9},{2,10},{3,11},{4,12},{5,13},{6,14},{7,15},{8,0},{9,1},... | collective-permute-start | bytes 147464 | tf_op jit(solution)/shard_map/ppermute | solution.py:24
  57.6 5.9 %collective-permute-start.11 = (bf16[4,48,128]{2,1,0:T(8,128)(2,1)S(1)}, bf16[4,48,128]{2,1,0:T(8,128)(2,1)S(1)}, u32[]{:S(2)}, u32[]{:S(2)}) collective-permute-start(bf16[4,48,128]{2,1,0:T(8,128)(2,1)S(1)} %get-tuple-element.62), channel_id=1, source_target_pairs={{0,12},{1,13},{2,14},{3,15},{4,8},{5,9},{6,10},{7,11},{8,4},{9,5},... | collective-permute-start | bytes 147464 | tf_op jit(solution)/shard_map/ppermute | solution.py:24

commit v16 on v11

--- a/solution.py
+++ b/solution.py
@@ -14,7 +14,7 @@
 F16_TOP = 14.0
 PLANE = 4
 HELD = 24
-IN_FLIGHT = 4
+MARK_ROWS = 16
 
 
 def in_hbm(value):
@@ -78,22 +78,24 @@
 
 
 def pack_scaled(value):
-    peak = jnp.max(jnp.abs(value), axis=(0, 2), keepdims=True)
+    blocks, rows, lanes = value.shape
+    peak = jnp.max(jnp.abs(value), axis=(0, 2))
     exponent = jnp.ceil(jnp.log2(jnp.maximum(peak, 2.0**-100)))
-    scaled = (value * jnp.exp2(F16_TOP - exponent)).astype(jnp.float16)
-    marks = jnp.broadcast_to(exponent, (1,) + value.shape[1:]).astype(jnp.float16)
-    return jnp.concatenate([scaled, marks], axis=0)
-
-
-def unpack_scaled(packed):
-    exponent = packed[-1:].astype(jnp.float32)
-    return packed[:-1].astype(jnp.float32) * jnp.exp2(exponent - F16_TOP)
+    scaled = (value * jnp.exp2(F16_TOP - exponent)[None, :, None]).astype(jnp.float16)
+    marks = jnp.pad(exponent.astype(jnp.float16)[None], ((0, MARK_ROWS - 1), (0, lanes - rows)))
+    return jnp.concatenate([scaled.reshape(blocks * rows, lanes), marks], axis=0)
+
+
+def unpack_scaled(packed, rows):
+    values, exponent = packed[:-MARK_ROWS], packed[-MARK_ROWS, :rows].astype(jnp.float32)
+    values = values.reshape(-1, rows, packed.shape[1]).astype(jnp.float32)
+    return values * jnp.exp2(exponent - F16_TOP)[None, :, None]
 
 
 def pair_sums(hidden, down_matrix, group, order, width):
-    half = group * width // LANES // 4
+    half = group * width // LANES // PLANE
     rows = hidden.shape[0]
-    share = group // 4
+    share = group // PLANE
 
     def first():
         (far,) = column_blocks(hidden, down_matrix, order[:share], width)
@@ -102,24 +104,21 @@
         return pack_scaled(near + far_in)
 
     def first_idle():
-        return jnp.zeros((half + 1, rows, LANES), jnp.float16)
-
-    def whole():
-        sent = lax.cond(order[1] >= 0, first, first_idle)
-        pair_in = xor_permute(sent, group, 2)
-        later, _ = lax.optimization_barrier((order, sent))
-
-        def second():
-            far, near = column_blocks(hidden, down_matrix, later[2 * share :], width, groups=2)
-            return near + xor_permute(far, group, 1)
-
-        kept = lax.cond(later[2] >= 0, second, idle)
-        return kept + unpack_scaled(pair_in)
-
-    def idle():
+        return jnp.zeros((half * rows + MARK_ROWS, LANES), jnp.float16)
+
+    sent = lax.cond(order[0] >= 0, first, first_idle)
+    pair_in = xor_permute(sent, group, 2)
+    order, _ = lax.optimization_barrier((order, sent))
+
+    def second():
+        far, near = column_blocks(hidden, down_matrix, order[2 * share :], width, groups=2)
+        return near + xor_permute(far, group, 1)
+
+    def second_idle():
         return jnp.zeros((half, rows, LANES), jnp.float32)
 
-    return lax.cond(order[0] >= 0, whole, idle)
+    kept = lax.cond(order[1] >= 0, second, second_idle)
+    return kept + unpack_scaled(pair_in, rows)
 
 
 def line_sums(pair, group, width):
@@ -131,7 +130,7 @@
     ]
     total = pair[:parts]
     for packed in arrived:
-        total = total + unpack_scaled(packed)
+        total = total + unpack_scaled(packed, rows)
     return jnp.transpose(total, (1, 0, 2)).reshape(rows, width)
 
 
@@ -142,7 +141,6 @@
     slot_hbm,
     adapter_hbm,
     hidden_hbm,
-    other_hbm,
     packed_ref,
     pick_ref,
     order_ref,
@@ -150,23 +148,19 @@
     slot_ref,
     adapter_ref,
     hidden_ref,
-    other_ref,
     sems,
 ):
     rows = hidden_ref.shape[0]
     group = slot_ref.shape[0]
-    chips = group // 2
-    me = me_ref[0]
     copies = [
         pltpu.make_async_copy(slot_hbm, slot_ref, sems.at[0]),
         pltpu.make_async_copy(adapter_hbm, adapter_ref, sems.at[1]),
         pltpu.make_async_copy(hidden_hbm, hidden_ref, sems.at[2]),
-        pltpu.make_async_copy(other_hbm, other_ref, sems.at[3]),
     ]
     for copy in copies:
         copy.start()
     for i, offset in enumerate(orders):
-        order_ref[i] = me ^ offset
+        order_ref[i] = me_ref[0] ^ offset
     ids = lax.broadcasted_iota(jnp.int32, (group, 1), 0)
     slots = jnp.zeros((group, 1), jnp.int32)
     copies[0].wait()
@@ -175,63 +169,48 @@
     copies[1].wait()
     adapter = adapter_ref[...]
     first = jnp.sum((adapter < ids).astype(jnp.int32), axis=1, keepdims=True)
-    slot = jnp.sum(jnp.where(adapter == ids, slots, 0), axis=0, keepdims=True)
-    offset = slot ^ me
-    first = jnp.sum(jnp.where(adapter == ids, first, 0), axis=0, keepdims=True)
-    index = lax.broadcasted_iota(jnp.int32, (1, rows), 1) - first
+    shift = jnp.where(adapter == ids, slots * (blocks * BLOCK) - first, 0)
+    place = jnp.sum(shift, axis=0, keepdims=True) + lax.broadcasted_iota(jnp.int32, (1, rows), 1)
+    spots = lax.broadcasted_iota(jnp.int32, (group * blocks * BLOCK, rows), 0)
+    pick = jnp.where(spots == place, 1.0, 0.0).astype(jnp.bfloat16)
     for k in range(PLANE):
         line = lax.broadcasted_iota(jnp.int32, (HELD, rows), 0)
-        mine = (offset == k) & (index == line)
+        mine = (line + (me_ref[0] ^ k) * (blocks * BLOCK) == place) & (line < blocks * BLOCK)
         pick_ref[k * HELD : (k + 1) * HELD] = jnp.where(mine, 1.0, 0.0).astype(jnp.bfloat16)
-    held = blocks * BLOCK
-    place = jnp.where((offset & 1) == 0, (slot >> 1) * held + index, -1)
-    spots = lax.broadcasted_iota(jnp.int32, (chips * held, rows), 0)
-    pick = jnp.where(spots == place, 1.0, 0.0).astype(jnp.bfloat16)
-    for source, source_ref in enumerate((hidden_ref, other_ref)):
-        copies[2 + source].wait()
-        packed = jnp.dot(pick, source_ref[...], preferred_element_type=jnp.float32)
-        packed = packed.astype(jnp.bfloat16).reshape(chips * blocks, BLOCK, packed.shape[1])
-        for chip in range(chips):
-            start = (2 * chip + source) * blocks
-            packed_ref[start : start + blocks] = packed[chip * blocks : (chip + 1) * blocks]
+    copies[2].wait()
+    packed = jnp.dot(pick, hidden_ref[...], preferred_element_type=jnp.float32)
+    packed_ref[...] = packed.astype(jnp.bfloat16).reshape(packed_ref.shape)
     kept_ref[...] = hidden_ref[...]
 
 
-def pack_rows(hidden, other, adapter_of_row, adapter_holder_slot, me, orders):
+def pack_rows(hidden, adapter_of_row, adapter_holder_slot, me, orders):
     rows, depth = hidden.shape
     group = adapter_holder_slot.shape[0]
     blocks = MOST // BLOCK
     vmem = pl.BlockSpec(memory_space=pltpu.VMEM)
     smem = pl.BlockSpec(memory_space=pltpu.SMEM)
-    anywhere = pl.BlockSpec(memory_space=pl.ANY)
+    anywhere = pl.BlockSpec(memory_space=pltpu.HBM)
     return pl.pallas_call(
         functools.partial(pack_kernel, blocks, orders),
-        out_shape=[
+        out_shape=(
             jax.ShapeDtypeStruct((group * blocks, BLOCK, depth), jnp.bfloat16),
             jax.ShapeDtypeStruct((PLANE * HELD, rows), jnp.bfloat16),
             jax.ShapeDtypeStruct((len(orders),), jnp.int32),
             jax.ShapeDtypeStruct((rows, depth), jnp.bfloat16),
-        ],
-        in_specs=[smem] + [anywhere] * 4,
-        out_specs=[vmem, vmem, smem, vmem],
+        ),
+        in_specs=[smem, anywhere, anywhere, anywhere],
+        out_specs=(vmem, vmem, smem, vmem),
         scratch_shapes=[
             pltpu.SMEM((group,), jnp.int32),
             pltpu.VMEM((1, rows), jnp.int32),
             pltpu.VMEM((rows, depth), jnp.bfloat16),
-            pltpu.VMEM((rows, depth), jnp.bfloat16),
-            pltpu.SemaphoreType.DMA((4,)),
+            pltpu.SemaphoreType.DMA((3,)),
         ],
         compiler_params=pltpu.CompilerParams(vmem_limit_bytes=24 * 2**20),
-    )(
-        me.reshape(1),
-        in_hbm(adapter_holder_slot),
-        in_hbm(adapter_of_row.reshape(1, rows)),
-        in_hbm(hidden),
-        other,
-    )
-
-
-def adapter_kernel(parts, me_ref, rows_ref, shrink_hbm, expand_hbm, *refs):
+    )(me.reshape(1), in_hbm(adapter_holder_slot), in_hbm(adapter_of_row.reshape(1, rows)), in_hbm(hidden))
+
+
+def adapter_kernel(parts, me_ref, rows_ref, expand_hbm, shrink_hbm, *refs):
     out_refs = refs[:PLANE]
     shrink_ref, expand_ref, total_ref, sems, expand_sem = refs[PLANE:]
     me = me_ref[0]
@@ -239,22 +218,17 @@
     blocks = MOST // BLOCK
 
     def copy(source):
-        device = source // 2 * 2 + ((me & 1) ^ (source % 2))
-        start = pl.multiple_of(device * depth, LANES)
         return pltpu.make_async_copy(
-            shrink_hbm.at[:, pl.ds(start, depth)], shrink_ref.at[source], sems.at[source]
-        )
-
-    for source in range(IN_FLIGHT):
+            shrink_hbm.at[:, pl.ds(source * depth, depth)], shrink_ref.at[source], sems.at[source]
+        )
+
+    for source in range(group):
         copy(source).start()
     expand_copy = pltpu.make_async_copy(expand_hbm, expand_ref, expand_sem)
+    expand_copy.start()
     total = jnp.zeros((MOST, total_ref.shape[1]), jnp.float32)
     for source in range(group):
         copy(source).wait()
-        if source + IN_FLIGHT < group:
-            copy(source + IN_FLIGHT).start()
-        elif source + IN_FLIGHT == group:
-            expand_copy.start()
         own = rows_ref[source * blocks : (source + 1) * blocks].reshape(MOST, depth)
         total += lax.dot_general(
             own, shrink_ref[source], (((1,), (1,)), ((), ())), preferred_element_type=jnp.float32
@@ -265,7 +239,7 @@
     expand_copy.wait()
     width = parts * LANES
     for k in range(PLANE):
-        for line in range(out_refs[k].shape[0] // parts):
+        for line in range(group // PLANE):
             target = me ^ (PLANE * line + k)
             columns = pl.ds(pl.multiple_of(target * width, LANES), width)
             piece = jnp.dot(rank_rows, expand_ref[:, columns], preferred_element_type=jnp.float32)
@@ -281,11 +255,15 @@
     parts = model_width // group // LANES
     held = (model_width // PLANE // LANES, HELD, LANES)
     vmem = pl.BlockSpec(memory_space=pltpu.VMEM)
-    anywhere = pl.BlockSpec(memory_space=pl.ANY)
     return pl.pallas_call(
         functools.partial(adapter_kernel, parts),
         out_shape=[jax.ShapeDtypeStruct(held, jnp.bfloat16)] * PLANE,
-        in_specs=[pl.BlockSpec(memory_space=pltpu.SMEM), vmem, anywhere, anywhere],
+        in_specs=[
+            pl.BlockSpec(memory_space=pltpu.SMEM),
+            vmem,
+            pl.BlockSpec(memory_space=pl.ANY),
+            pl.BlockSpec(memory_space=pl.ANY),
+        ],
         out_specs=[vmem] * PLANE,
         scratch_shapes=[
             pltpu.VMEM((group, rank, depth), jnp.bfloat16),
@@ -295,7 +273,7 @@
             pltpu.SemaphoreType.DMA,
         ],
         compiler_params=pltpu.CompilerParams(vmem_limit_bytes=24 * 2**20),
-    )(me.reshape(1), gathered, in_hbm(shrink), in_hbm(expand))
+    )(me.reshape(1), gathered, in_hbm(expand), in_hbm(shrink))
 
 
 def merge_kernel(pair_ref, pick_ref, *refs):
@@ -331,17 +309,13 @@
     width = down_matrix.shape[1] // group
     quads = list(range(0, group, 4))
     orders = [q + k for k in (3, 2, 1, 0) for q in quads]
-    other = xor_permute(hidden, group, 1)
     packed, pick, order, kept_hidden = pack_rows(
-        hidden, other, adapter_of_row, adapter_holder_slot, me, orders
+        hidden, adapter_of_row, adapter_holder_slot, me, orders
     )
-    same_core = [list(range(core, group, 2)) for core in range(2)]
-    gathered = lax.all_to_all(
-        packed, "tp", split_axis=0, concat_axis=0, axis_index_groups=same_core, tiled=True
-    )
+    gathered = lax.all_to_all(packed, "tp", split_axis=0, concat_axis=0, tiled=True)
+    shrink = jnp.swapaxes(shrink_matrices, 1, 2)[0]
     pair = pair_sums(kept_hidden, down_matrix, group, order, width)
     gathered, _ = lax.optimization_barrier((gathered, pair))
-    shrink = jnp.swapaxes(shrink_matrices, 1, 2)[0]
     expand = jnp.swapaxes(expand_matrices, 1, 2)[0]
     outs = adapter_output(gathered, shrink, expand, group, me)
     arrived = [outs[0]] + [xor_permute(outs[k], group, k) for k in range(1, PLANE)]
@@ -355,7 +329,7 @@
     group = lax.axis_size("tp")
     rows, depth = hidden.shape
     width = down_matrix.shape[1] // group
-    if width % LANES == 0 and depth % LANES == 0 and group >= PLANE and group & (group - 1) == 0:
+    if width % LANES == 0 and depth % LANES == 0 and rows <= LANES and group >= PLANE and group & (group - 1) == 0:
         return shards_by_blocks(
             hidden, down_matrix, shrink_matrices, expand_matrices, adapter_of_row, adapter_holder_slot
         )

time: 70.8 us -> 61.2 us (0.86)
  waiting for transfers between devices: 22.6 us -> 18.8 us
  Pallas kernels: 23.6 us -> 21.4 us
  other arithmetic: 3.68 us -> 1.95 us
  loops' own time: 1.36 us -> 0.08 us
  local copies, waits for them, and re-layouts: 1.69 us -> 0.9 us
    ppermute x10 -> x9, waiting for transfers between devices: 22.6 us -> 18.8 us  [xor_permute(): return lax.ppermute(value, 'tp', [(i, i ^ offset) for i in range(group)])]
    pallas_call x1, Pallas kernels: 5.78 us -> 3.85 us  [adapter_output(): pl.pallas_call(functools.partial(adapter_kernel, parts), out_shape=[jax.S...]
    another operation x3 -> x2, loops' own time: 1.36 us -> 0.08 us  [the longest x1 0.05 us: pair_sums(): sent = lax.cond(order[0] >= 0, first, first_idle)]
    add x1, other arithmetic: 1.11 us -> 0.18 us  [pair_sums(): return kept + unpack_scaled(pair_in, rows)]
    mul x4 -> x0, other arithmetic: 0.81 us -> none  [unpack_scaled(): return packed[:-1].astype(jnp.float32) * jnp.exp2(exponent - F16_TOP)]
    ppermute x10 -> x9, starting transfers between devices: 10.1 us -> 9.67 us  [xor_permute(): return lax.ppermute(value, 'tp', [(i, i ^ offset) for i in range(group)])]
  transfers between devices with their start and end apart: 11 -> 10, of which waited for: 7 -> 6; matrix products, arithmetic and copies ran while one was open for 6% -> 3% of each run, Pallas kernels for 21% -> 24%
where the time goes in v16:
time: 61.2 us; the launch traced here: 61 us
  Pallas kernels  21.4 us (35%)
  waiting for transfers between devices  18.8 us (31%)
  starting transfers between devices  17 us (28%)
  other arithmetic  1.95 us (3%)
  local copies, waits for them, and re-layouts  0.9 us (1%)
  between operations  0.82 us (1%)
    ppermute x9, waiting for transfers between devices, xor_permute(): return lax.ppermute(value, 'tp', [(i, i ^ offset) for i in range(group)])  18.8 us
    pallas_call x3, Pallas kernels, column_blocks(): pl.pallas_call(functools.partial(column_blocks_kernel, groups), out_shape...  14.8 us
    ppermute x9, starting transfers between devices, xor_permute(): return lax.ppermute(value, 'tp', [(i, i ^ offset) for i in range(group)])  9.67 us
    all_to_all x1, starting transfers between devices, shards_by_blocks(): lax.all_to_all(packed, 'tp', split_axis=0, concat_axis=0, tiled=True)  7.37 us
    pallas_call x1, Pallas kernels, adapter_output(): pl.pallas_call(functools.partial(adapter_kernel, parts), out_shape=[jax.S...  3.85 us
    pallas_call x1, Pallas kernels, pack_rows(): pl.pallas_call(functools.partial(pack_kernel, blocks, orders), out_shape=...  2.49 us
  transfers between devices with their start and end apart: 10, of which 6 were waited for; matrix products, arithmetic and copies ran while one was open for 3% of the time, Pallas kernels for 24%

profile of v16, /device:TPU:0, one launch (start us, length us, event | category | flops | bytes accessed | tf_op | source)
XLA Modules:
  0.0 61.0 jit_solution(13020535900768818039)
XLA Ops:
  0.0 2.5 %shard_map.64 = (bf16[80,4,1792]{2,1,0:T(4,128)(2,1)}, bf16[96,96]{1,0:T(8,128)(2,1)S(1)}, s32[16]{0:T(128)S(1)}, bf16[96,1792]{1,0:T(8,128)(2,1)S(1)}) custom-call(s32[1]{0:T(128)} %bitcast.2.me_ref, s32[16]{0:T(128)} %slot_hbm.1, s32[1,96]{1,0:T(1,128)} %bitcast.56, bf16[96,1792]{1,0:T(8,128)(2,1)} %hidden_hbm.1), custom_call_target="tpu_custom_call" | custom-call | tf_op jit(solution)/shard_map/pallas_call | solution.py:193
  2.5 7.4 %all-to-all-start = ((bf16[80,4,1792]{2,1,0:T(4,128)(2,1)}), bf16[80,4,1792]{2,1,0:T(4,128)(2,1)S(1)}, u32[]{:S(2)}, u32[]{:S(2)}) async-start(bf16[80,4,1792]{2,1,0:T(4,128)(2,1)} %get-tuple-element.45), calls=%async_computation | async-start | bytes 2293760 | tf_op jit(solution)/shard_map/all_to_all | solution.py:315
  9.9 9.4 %conditional.2 = (f16[1552,128]{1,0:T(8,128)(2,1)S(1)}) conditional(s32[]{:T(128)} %bitcast.4, () %tuple.19, (s32[16]{0:T(128)S(1)}, bf16[96,1792]{1,0:T(8,128)(2,1)S(1)}, bf16[1792,8192]{1,0:T(8,128)(2,1)}) %tuple.20), branch_computations={%region_0.0_spmd, %region_1.3_spmd} | conditional | flops 1581488 | bytes 7479232 | solution.py:109
  9.9 0.1 fusion.29
  10.0 4.2 %branch_1_fun.4 = f32[16,96,128]{2,1,0:T(8,128)S(1)} custom-call(s32[4]{0:T(128)S(1)} %get-tuple-element.58.order_ref, bf16[96,1792]{1,0:T(8,128)(2,1)S(1)} %get-tuple-element.24.hidden_ref, bf16[1792,8192]{1,0:T(8,128)(2,1)} %get-tuple-element.25.down_ref), custom_call_target="tpu_custom_call" | custom-call | flops 1000 | bytes 1000 | tf_op jit(solution)/shard_map/cond/branch_1_fun/pallas_call | solution.py:62
  14.2 0.5 collective-permute-start.1
  14.7 4.2 %branch_1_fun.3 = f32[16,96,128]{2,1,0:T(8,128)S(1)} custom-call(s32[4]{0:T(128)S(1)} %get-tuple-element.59.order_ref, bf16[96,1792]{1,0:T(8,128)(2,1)S(1)} %get-tuple-element.24.hidden_ref, bf16[1792,8192]{1,0:T(8,128)(2,1)} %get-tuple-element.25.down_ref), custom_call_target="tpu_custom_call" | custom-call | flops 1000 | bytes 1000 | tf_op jit(solution)/shard_map/cond/branch_1_fun/pallas_call | solution.py:62
  18.9 0.0 collective-permute-done.1
  18.9 0.2 abs_reduce_fusion
  19.1 0.2 multiply_convert_fusion
  19.3 0.1 fusion.1
  19.3 1.7 %collective-permute-start.2 = (f16[1552,128]{1,0:T(8,128)(2,1)S(1)}, f16[1552,128]{1,0:T(8,128)(2,1)S(1)}, u32[]{:S(2)}, u32[]{:S(2)}) collective-permute-start(f16[1552,128]{1,0:T(8,128)(2,1)S(1)} %get-tuple-element.71), channel_id=1, source_target_pairs={{0,2},{1,3},{2,0},{3,1},{4,6},{5,7},{6,4},{7,5},{8,10},{9,11},{10,... | collective-permute-start | bytes 1191944 | tf_op jit(solution)/shard_map/ppermute | solution.py:25
  21.1 0.6 slice.52
  22.3 9.0 %conditional.3 = (f32[16,96,128]{2,1,0:T(8,128)S(1)}) conditional(s32[]{:T(128)} %bitcast.5, () %tuple.22, (s32[16]{0:T(128)S(1)}, bf16[96,1792]{1,0:T(8,128)(2,1)S(1)}, bf16[1792,8192]{1,0:T(8,128)(2,1)}) %tuple.23), branch_computations={%region_3.4_spmd, %region_4.5_spmd} | conditional | flops 197608 | bytes 5506136 | solution.py:120
  22.4 0.1 slice.36.order_ref
  22.4 6.4 %branch_1_fun.5 = (f32[16,96,128]{2,1,0:T(8,128)S(1)}, f32[16,96,128]{2,1,0:T(8,128)S(1)}) custom-call(s32[8]{0:T(128)S(1)} %slice.36.order_ref, bf16[96,1792]{1,0:T(8,128)(2,1)S(1)} %get-tuple-element.27.hidden_ref, bf16[1792,8192]{1,0:T(8,128)(2,1)} %get-tuple-element.28.down_ref), custom_call_target="tpu_custom_call" | custom-call | flops 1000 | bytes 1000 | tf_op jit(solution)/shard_map/cond/branch_1_fun/pallas_call | solution.py:62
  28.8 0.1 collective-permute-start
  29.0 2.2 %collective-permute-done = f32[16,96,128]{2,1,0:T(8,128)S(1)} collective-permute-done((f32[16,96,128]{2,1,0:T(8,128)S(1)}, f32[16,96,128]{2,1,0:T(8,128)S(1)}, u32[]{:S(2)}, u32[]{:S(2)}) %collective-permute-start) | collective-permute-done | bytes 786464 | tf_op jit(solution)/shard_map/cond/branch_1_fun/ppermute | solution.py:25
  31.2 0.1 add.39
  31.3 4.6 %collective-permute-done.2 = f16[1552,128]{1,0:T(8,128)(2,1)S(1)} collective-permute-done((f16[1552,128]{1,0:T(8,128)(2,1)S(1)}, f16[1552,128]{1,0:T(8,128)(2,1)S(1)}, u32[]{:S(2)}, u32[]{:S(2)}) %collective-permute-start.2) | collective-permute-done | bytes 397344 | tf_op jit(solution)/shard_map/ppermute | solution.py:25
  35.9 0.1 slice.65
  36.0 0.2 fusion.2.pair_ref
  36.2 0.0 all-to-all-done.rows_ref
  36.2 3.9 %shard_map.65 = (bf16[16,24,128]{2,1,0:T(8,128)(2,1)S(1)}, bf16[16,24,128]{2,1,0:T(8,128)(2,1)S(1)}, bf16[16,24,128]{2,1,0:T(8,128)(2,1)S(1)}, bf16[16,24,128]{2,1,0:T(8,128)(2,1)S(1)}) custom-call(s32[1]{0:T(128)} %bitcast.2.me_ref, bf16[80,4,1792]{2,1,0:T(4,128)(2,1)S(1)} %all-to-all-done.rows_ref, bf16[64,8192]{1,0:T(8,128)(2,1)} %bitcast.48, ...), custom_call_target="tpu_custom_call" | custom-call | tf_op jit(solution)/shard_map/pallas_call | solution.py:258
  40.0 0.1 collective-permute-start.3
  40.1 2.0 %collective-permute-start.4 = (bf16[16,24,128]{2,1,0:T(8,128)(2,1)S(1)}, bf16[16,24,128]{2,1,0:T(8,128)(2,1)S(1)}, u32[]{:S(2)}, u32[]{:S(2)}) collective-permute-start(bf16[16,24,128]{2,1,0:T(8,128)(2,1)S(1)} %get-tuple-element.49), channel_id=1, source_target_pairs={{0,2},{1,3},{2,0},{3,1},{4,6},{5,7},{6,4},{7,5},{8,10},{9,11},{10,... | collective-permute-start | bytes 294920 | tf_op jit(solution)/shard_map/ppermute | solution.py:25
  42.2 0.1 collective-permute-start.5
  42.2 0.0 collective-permute-done.3.refs_1_
  42.2 3.6 %collective-permute-done.4.refs_2_ = bf16[16,24,128]{2,1,0:T(8,128)(2,1)S(1)} collective-permute-done((bf16[16,24,128]{2,1,0:T(8,128)(2,1)S(1)}, bf16[16,24,128]{2,1,0:T(8,128)(2,1)S(1)}, u32[]{:S(2)}, u32[]{:S(2)}) %collective-permute-start.4) | collective-permute-done | bytes 98336 | tf_op jit(solution)/shard_map/ppermute | solution.py:25
  45.9 1.5 %collective-permute-done.5.refs_3_ = bf16[16,24,128]{2,1,0:T(8,128)(2,1)S(1)} collective-permute-done((bf16[16,24,128]{2,1,0:T(8,128)(2,1)S(1)}, bf16[16,24,128]{2,1,0:T(8,128)(2,1)S(1)}, u32[]{:S(2)}, u32[]{:S(2)}) %collective-permute-start.5) | collective-permute-done | bytes 98336 | tf_op jit(solution)/shard_map/ppermute | solution.py:25
  47.3 0.3 shard_map.66
  47.6 0.2 abs_reduce_fusion.3
  47.8 0.1 multiply_convert_fusion.3
  48.0 3.5 %collective-permute-start.7 = (f16[400,128]{1,0:T(8,128)(2,1)S(1)}, f16[400,128]{1,0:T(8,128)(2,1)S(1)}, u32[]{:S(2)}, u32[]{:S(2)}) collective-permute-start(f16[400,128]{1,0:T(8,128)(2,1)S(1)} %fusion.10), channel_id=1, source_target_pairs={{0,8},{1,9},{2,10},{3,11},{4,12},{5,13},{6,14},{7,15},{8,0},{9,1},... | collective-permute-start | bytes 307208 | tf_op jit(solution)/shard_map/ppermute | solution.py:25
  51.6 0.2 collective-permute-start.6
  51.8 1.4 %collective-permute-start.8 = (f16[400,128]{1,0:T(8,128)(2,1)S(1)}, f16[400,128]{1,0:T(8,128)(2,1)S(1)}, u32[]{:S(2)}, u32[]{:S(2)}) collective-permute-start(f16[400,128]{1,0:T(8,128)(2,1)S(1)} %fusion.11), channel_id=1, source_target_pairs={{0,12},{1,13},{2,14},{3,15},{4,8},{5,9},{6,10},{7,11},{8,4},{9,5},... | collective-permute-start | bytes 307208 | tf_op jit(solution)/shard_map/ppermute | solution.py:25
  53.2 4.7 %collective-permute-done.7 = f16[400,128]{1,0:T(8,128)(2,1)S(1)} collective-permute-done((f16[400,128]{1,0:T(8,128)(2,1)S(1)}, f16[400,128]{1,0:T(8,128)(2,1)S(1)}, u32[]{:S(2)}, u32[]{:S(2)}) %collective-permute-start.7) | collective-permute-done | bytes 102432 | tf_op jit(solution)/shard_map/ppermute | solution.py:25
  57.9 2.2 %collective-permute-done.6 = f16[400,128]{1,0:T(8,128)(2,1)S(1)} collective-permute-done((f16[400,128]{1,0:T(8,128)(2,1)S(1)}, f16[400,128]{1,0:T(8,128)(2,1)S(1)}, u32[]{:S(2)}, u32[]{:S(2)}) %collective-permute-start.6) | collective-permute-done | bytes 102432 | tf_op jit(solution)/shard_map/ppermute | solution.py:25
  60.2 0.0 collective-permute-done.8
  60.2 0.8 %copy_bitcast_fusion = bf16[96,512]{1,0:T(8,128)(2,1)} fusion(f16[4,96,128]{2,1,0:T(8,128)(2,1)S(1)} %bitcast.54, f16[4,96,128]{2,1,0:T(8,128)(2,1)S(1)} %bitcast.51, f16[4,96,128]{2,1,0:T(8,128)(2,1)S(1)} %bitcast.52, f32[16,96,128]{2,1,0:T(8,128)S(1)} %shard_map.66, f32[96]{0:T(128)S(1)} %fusion.16, f32[96]{0:T(128)S(1)} %fusion.20, f32[96]{0:T(128)S(1)} %fusion.24), kind=kLoop, calls=%fused_computation.31 | loop fusion | flops 491520 | bytes 591360 | tf_op jit(solution)/shard_map/convert_element_type | solution.py:323
  (13 shorter events, 0.2 us)
Async XLA Ops:
  2.5 33.7 %all-to-all-start = ((bf16[80,4,1792]{2,1,0:T(4,128)(2,1)}), bf16[80,4,1792]{2,1,0:T(4,128)(2,1)S(1)}, u32[]{:S(2)}, u32[]{:S(2)}) async-start(bf16[80,4,1792]{2,1,0:T(4,128)(2,1)} %get-tuple-element.45), calls=%async_computation | async-start | bytes 2293760 | tf_op jit(solution)/shard_map/all_to_all | solution.py:315
  14.2 4.7 %collective-permute-start.1 = (f32[16,96,128]{2,1,0:T(8,128)S(1)}, f32[16,96,128]{2,1,0:T(8,128)S(1)}, u32[]{:S(2)}, u32[]{:S(2)}) collective-permute-start(f32[16,96,128]{2,1,0:T(8,128)S(1)} %branch_1_fun.4), channel_id=1, source_target_pairs={{0,1},{1,0},{2,3},{3,2},{4,5},{5,4},{6,7},{7,6},{8,9},{9,8},{10,11... | collective-permute-start | bytes 2359304 | tf_op jit(solution)/shard_map/cond/branch_1_fun/ppermute | solution.py:25
  19.3 16.5 %collective-permute-start.2 = (f16[1552,128]{1,0:T(8,128)(2,1)S(1)}, f16[1552,128]{1,0:T(8,128)(2,1)S(1)}, u32[]{:S(2)}, u32[]{:S(2)}) collective-permute-start(f16[1552,128]{1,0:T(8,128)(2,1)S(1)} %get-tuple-element.71), channel_id=1, source_target_pairs={{0,2},{1,3},{2,0},{3,1},{4,6},{5,7},{6,4},{7,5},{8,10},{9,11},{10,... | collective-permute-start | bytes 1191944 | tf_op jit(solution)/shard_map/ppermute | solution.py:25
  28.8 2.4 %collective-permute-start = (f32[16,96,128]{2,1,0:T(8,128)S(1)}, f32[16,96,128]{2,1,0:T(8,128)S(1)}, u32[]{:S(2)}, u32[]{:S(2)}) collective-permute-start(f32[16,96,128]{2,1,0:T(8,128)S(1)} %get-tuple-element.30), channel_id=1, source_target_pairs={{0,1},{1,0},{2,3},{3,2},{4,5},{5,4},{6,7},{7,6},{8,9},{9,8},{10,11... | collective-permute-start | bytes 2359304 | tf_op jit(solution)/shard_map/cond/branch_1_fun/ppermute | solution.py:25
  40.0 2.2 %collective-permute-start.3 = (bf16[16,24,128]{2,1,0:T(8,128)(2,1)S(1)}, bf16[16,24,128]{2,1,0:T(8,128)(2,1)S(1)}, u32[]{:S(2)}, u32[]{:S(2)}) collective-permute-start(bf16[16,24,128]{2,1,0:T(8,128)(2,1)S(1)} %get-tuple-element.48), channel_id=1, source_target_pairs={{0,1},{1,0},{2,3},{3,2},{4,5},{5,4},{6,7},{7,6},{8,9},{9,8},{10,11... | collective-permute-start | bytes 294920 | tf_op jit(solution)/shard_map/ppermute | solution.py:25
  40.1 5.7 %collective-permute-start.4 = (bf16[16,24,128]{2,1,0:T(8,128)(2,1)S(1)}, bf16[16,24,128]{2,1,0:T(8,128)(2,1)S(1)}, u32[]{:S(2)}, u32[]{:S(2)}) collective-permute-start(bf16[16,24,128]{2,1,0:T(8,128)(2,1)S(1)} %get-tuple-element.49), channel_id=1, source_target_pairs={{0,2},{1,3},{2,0},{3,1},{4,6},{5,7},{6,4},{7,5},{8,10},{9,11},{10,... | collective-permute-start | bytes 294920 | tf_op jit(solution)/shard_map/ppermute | solution.py:25
  42.2 5.2 %collective-permute-start.5 = (bf16[16,24,128]{2,1,0:T(8,128)(2,1)S(1)}, bf16[16,24,128]{2,1,0:T(8,128)(2,1)S(1)}, u32[]{:S(2)}, u32[]{:S(2)}) collective-permute-start(bf16[16,24,128]{2,1,0:T(8,128)(2,1)S(1)} %get-tuple-element.50), channel_id=1, source_target_pairs={{0,3},{1,2},{2,1},{3,0},{4,7},{5,6},{6,5},{7,4},{8,11},{9,10},{10,... | collective-permute-start | bytes 294920 | tf_op jit(solution)/shard_map/ppermute | solution.py:25
  48.0 9.9 %collective-permute-start.7 = (f16[400,128]{1,0:T(8,128)(2,1)S(1)}, f16[400,128]{1,0:T(8,128)(2,1)S(1)}, u32[]{:S(2)}, u32[]{:S(2)}) collective-permute-start(f16[400,128]{1,0:T(8,128)(2,1)S(1)} %fusion.10), channel_id=1, source_target_pairs={{0,8},{1,9},{2,10},{3,11},{4,12},{5,13},{6,14},{7,15},{8,0},{9,1},... | collective-permute-start | bytes 307208 | tf_op jit(solution)/shard_map/ppermute | solution.py:25
  51.6 8.5 %collective-permute-start.6 = (f16[400,128]{1,0:T(8,128)(2,1)S(1)}, f16[400,128]{1,0:T(8,128)(2,1)S(1)}, u32[]{:S(2)}, u32[]{:S(2)}) collective-permute-start(f16[400,128]{1,0:T(8,128)(2,1)S(1)} %fusion.9), channel_id=1, source_target_pairs={{0,4},{1,5},{2,6},{3,7},{4,0},{5,1},{6,2},{7,3},{8,12},{9,13},{10,... | collective-permute-start | bytes 307208 | tf_op jit(solution)/shard_map/ppermute | solution.py:25
  51.8 8.4 %collective-permute-start.8 = (f16[400,128]{1,0:T(8,128)(2,1)S(1)}, f16[400,128]{1,0:T(8,128)(2,1)S(1)}, u32[]{:S(2)}, u32[]{:S(2)}) collective-permute-start(f16[400,128]{1,0:T(8,128)(2,1)S(1)} %fusion.11), channel_id=1, source_target_pairs={{0,12},{1,13},{2,14},{3,15},{4,8},{5,9},{6,10},{7,11},{8,4},{9,5},... | collective-permute-start | bytes 307208 | tf_op jit(solution)/shard_map/ppermute | solution.py:25

commit v17 on v16

--- a/solution.py
+++ b/solution.py
@@ -118,7 +118,7 @@
         return jnp.zeros((half, rows, LANES), jnp.float32)
 
     kept = lax.cond(order[1] >= 0, second, second_idle)
-    return kept + unpack_scaled(pair_in, rows)
+    return kept, pair_in
 
 
 def line_sums(pair, group, width):
@@ -314,11 +314,12 @@
     )
     gathered = lax.all_to_all(packed, "tp", split_axis=0, concat_axis=0, tiled=True)
     shrink = jnp.swapaxes(shrink_matrices, 1, 2)[0]
-    pair = pair_sums(kept_hidden, down_matrix, group, order, width)
-    gathered, _ = lax.optimization_barrier((gathered, pair))
+    kept, pair_in = pair_sums(kept_hidden, down_matrix, group, order, width)
+    gathered, _ = lax.optimization_barrier((gathered, kept))
     expand = jnp.swapaxes(expand_matrices, 1, 2)[0]
     outs = adapter_output(gathered, shrink, expand, group, me)
     arrived = [outs[0]] + [xor_permute(outs[k], group, k) for k in range(1, PLANE)]
+    pair = kept + unpack_scaled(pair_in, rows)
     merged = merge_adapters(pair, pick, arrived)
     return line_sums(merged, group, width).astype(jnp.bfloat16)
 

time: 61.2 us -> 61.2 us (level)
  no operation moved by 1% of the time
where the time goes in v17:
time: 61.2 us; the launch traced here: 61 us
  Pallas kernels  21.4 us (35%)
  waiting for transfers between devices  18.6 us (30%)
  starting transfers between devices  17.2 us (28%)
  other arithmetic  1.95 us (3%)
  local copies, waits for them, and re-layouts  0.9 us (1%)
  between operations  0.83 us (1%)
    ppermute x9, waiting for transfers between devices, xor_permute(): return lax.ppermute(value, 'tp', [(i, i ^ offset) for i in range(group)])  18.6 us
    pallas_call x3, Pallas kernels, column_blocks(): pl.pallas_call(functools.partial(column_blocks_kernel, groups), out_shape...  14.8 us
    ppermute x9, starting transfers between devices, xor_permute(): return lax.ppermute(value, 'tp', [(i, i ^ offset) for i in range(group)])  9.85 us
    all_to_all x1, starting transfers between devices, shards_by_blocks(): lax.all_to_all(packed, 'tp', split_axis=0, concat_axis=0, tiled=True)  7.37 us
    pallas_call x1, Pallas kernels, adapter_output(): pl.pallas_call(functools.partial(adapter_kernel, parts), out_shape=[jax.S...  3.86 us
    pallas_call x1, Pallas kernels, pack_rows(): pl.pallas_call(functools.partial(pack_kernel, blocks, orders), out_shape=...  2.49 us
  transfers between devices with their start and end apart: 10, of which 6 were waited for; matrix products, arithmetic and copies ran while one was open for 3% of the time, Pallas kernels for 24%

profile of v17, /device:TPU:0, one launch (start us, length us, event | category | flops | bytes accessed | tf_op | source)
XLA Modules:
  0.0 61.0 jit_solution(16922047571142785843)
XLA Ops:
  0.0 2.5 %shard_map.64 = (bf16[80,4,1792]{2,1,0:T(4,128)(2,1)}, bf16[96,96]{1,0:T(8,128)(2,1)S(1)}, s32[16]{0:T(128)S(1)}, bf16[96,1792]{1,0:T(8,128)(2,1)S(1)}) custom-call(s32[1]{0:T(128)} %bitcast.2.me_ref, s32[16]{0:T(128)} %slot_hbm.1, s32[1,96]{1,0:T(1,128)} %bitcast.56, bf16[96,1792]{1,0:T(8,128)(2,1)} %hidden_hbm.1), custom_call_target="tpu_custom_call" | custom-call | tf_op jit(solution)/shard_map/pallas_call | solution.py:193
  2.5 7.4 %all-to-all-start = ((bf16[80,4,1792]{2,1,0:T(4,128)(2,1)}), bf16[80,4,1792]{2,1,0:T(4,128)(2,1)S(1)}, u32[]{:S(2)}, u32[]{:S(2)}) async-start(bf16[80,4,1792]{2,1,0:T(4,128)(2,1)} %get-tuple-element.45), calls=%async_computation | async-start | bytes 2293760 | tf_op jit(solution)/shard_map/all_to_all | solution.py:315
  9.9 9.5 %conditional.2 = (f16[1552,128]{1,0:T(8,128)(2,1)S(1)}) conditional(s32[]{:T(128)} %bitcast.4, () %tuple.19, (s32[16]{0:T(128)S(1)}, bf16[96,1792]{1,0:T(8,128)(2,1)S(1)}, bf16[1792,8192]{1,0:T(8,128)(2,1)}) %tuple.20), branch_computations={%region_0.0_spmd, %region_1.3_spmd} | conditional | flops 1581488 | bytes 7479232 | solution.py:109
  9.9 0.1 fusion.29
  10.0 4.2 %branch_1_fun.4 = f32[16,96,128]{2,1,0:T(8,128)S(1)} custom-call(s32[4]{0:T(128)S(1)} %get-tuple-element.58.order_ref, bf16[96,1792]{1,0:T(8,128)(2,1)S(1)} %get-tuple-element.24.hidden_ref, bf16[1792,8192]{1,0:T(8,128)(2,1)} %get-tuple-element.25.down_ref), custom_call_target="tpu_custom_call" | custom-call | flops 1000 | bytes 1000 | tf_op jit(solution)/shard_map/cond/branch_1_fun/pallas_call | solution.py:62
  14.2 0.5 collective-permute-start.1
  14.7 4.2 %branch_1_fun.3 = f32[16,96,128]{2,1,0:T(8,128)S(1)} custom-call(s32[4]{0:T(128)S(1)} %get-tuple-element.59.order_ref, bf16[96,1792]{1,0:T(8,128)(2,1)S(1)} %get-tuple-element.24.hidden_ref, bf16[1792,8192]{1,0:T(8,128)(2,1)} %get-tuple-element.25.down_ref), custom_call_target="tpu_custom_call" | custom-call | flops 1000 | bytes 1000 | tf_op jit(solution)/shard_map/cond/branch_1_fun/pallas_call | solution.py:62
  18.9 0.0 collective-permute-done.1
  18.9 0.2 abs_reduce_fusion
  19.1 0.2 multiply_convert_fusion
  19.3 0.1 fusion.1
  19.4 1.7 %collective-permute-start.2 = (f16[1552,128]{1,0:T(8,128)(2,1)S(1)}, f16[1552,128]{1,0:T(8,128)(2,1)S(1)}, u32[]{:S(2)}, u32[]{:S(2)}) collective-permute-start(f16[1552,128]{1,0:T(8,128)(2,1)S(1)} %get-tuple-element.71), channel_id=1, source_target_pairs={{0,2},{1,3},{2,0},{3,1},{4,6},{5,7},{6,4},{7,5},{8,10},{9,11},{10,... | collective-permute-start | bytes 1191944 | tf_op jit(solution)/shard_map/ppermute | solution.py:25
  21.1 0.6 slice.52
  22.4 9.0 %conditional.3 = (f32[16,96,128]{2,1,0:T(8,128)S(1)}) conditional(s32[]{:T(128)} %bitcast.5, () %tuple.22, (s32[16]{0:T(128)S(1)}, bf16[96,1792]{1,0:T(8,128)(2,1)S(1)}, bf16[1792,8192]{1,0:T(8,128)(2,1)}) %tuple.23), branch_computations={%region_3.4_spmd, %region_4.5_spmd} | conditional | flops 197608 | bytes 5506136 | solution.py:120
  22.4 0.1 slice.36.order_ref
  22.5 6.4 %branch_1_fun.5 = (f32[16,96,128]{2,1,0:T(8,128)S(1)}, f32[16,96,128]{2,1,0:T(8,128)S(1)}) custom-call(s32[8]{0:T(128)S(1)} %slice.36.order_ref, bf16[96,1792]{1,0:T(8,128)(2,1)S(1)} %get-tuple-element.27.hidden_ref, bf16[1792,8192]{1,0:T(8,128)(2,1)} %get-tuple-element.28.down_ref), custom_call_target="tpu_custom_call" | custom-call | flops 1000 | bytes 1000 | tf_op jit(solution)/shard_map/cond/branch_1_fun/pallas_call | solution.py:62
  28.9 0.1 collective-permute-start
  29.0 2.2 %collective-permute-done = f32[16,96,128]{2,1,0:T(8,128)S(1)} collective-permute-done((f32[16,96,128]{2,1,0:T(8,128)S(1)}, f32[16,96,128]{2,1,0:T(8,128)S(1)}, u32[]{:S(2)}, u32[]{:S(2)}) %collective-permute-start) | collective-permute-done | bytes 786464 | tf_op jit(solution)/shard_map/cond/branch_1_fun/ppermute | solution.py:25
  31.2 0.1 add.39
  31.3 4.6 %collective-permute-done.2 = f16[1552,128]{1,0:T(8,128)(2,1)S(1)} collective-permute-done((f16[1552,128]{1,0:T(8,128)(2,1)S(1)}, f16[1552,128]{1,0:T(8,128)(2,1)S(1)}, u32[]{:S(2)}, u32[]{:S(2)}) %collective-permute-start.2) | collective-permute-done | bytes 397344 | tf_op jit(solution)/shard_map/ppermute | solution.py:25
  35.9 0.1 slice.65
  36.0 0.0 all-to-all-done.rows_ref
  36.0 3.9 %shard_map.65 = (bf16[16,24,128]{2,1,0:T(8,128)(2,1)S(1)}, bf16[16,24,128]{2,1,0:T(8,128)(2,1)S(1)}, bf16[16,24,128]{2,1,0:T(8,128)(2,1)S(1)}, bf16[16,24,128]{2,1,0:T(8,128)(2,1)S(1)}) custom-call(s32[1]{0:T(128)} %bitcast.2.me_ref, bf16[80,4,1792]{2,1,0:T(4,128)(2,1)S(1)} %all-to-all-done.rows_ref, bf16[64,8192]{1,0:T(8,128)(2,1)} %bitcast.48, ...), custom_call_target="tpu_custom_call" | custom-call | tf_op jit(solution)/shard_map/pallas_call | solution.py:258
  39.9 0.1 collective-permute-start.3
  40.0 2.0 %collective-permute-start.4 = (bf16[16,24,128]{2,1,0:T(8,128)(2,1)S(1)}, bf16[16,24,128]{2,1,0:T(8,128)(2,1)S(1)}, u32[]{:S(2)}, u32[]{:S(2)}) collective-permute-start(bf16[16,24,128]{2,1,0:T(8,128)(2,1)S(1)} %get-tuple-element.49), channel_id=1, source_target_pairs={{0,2},{1,3},{2,0},{3,1},{4,6},{5,7},{6,4},{7,5},{8,10},{9,11},{10,... | collective-permute-start | bytes 294920 | tf_op jit(solution)/shard_map/ppermute | solution.py:25
  42.0 0.1 collective-permute-start.5
  42.0 0.2 fusion.2.pair_ref
  42.2 0.0 collective-permute-done.3.refs_1_
  42.2 3.5 %collective-permute-done.4.refs_2_ = bf16[16,24,128]{2,1,0:T(8,128)(2,1)S(1)} collective-permute-done((bf16[16,24,128]{2,1,0:T(8,128)(2,1)S(1)}, bf16[16,24,128]{2,1,0:T(8,128)(2,1)S(1)}, u32[]{:S(2)}, u32[]{:S(2)}) %collective-permute-start.4) | collective-permute-done | bytes 98336 | tf_op jit(solution)/shard_map/ppermute | solution.py:25
  45.7 1.4 %collective-permute-done.5.refs_3_ = bf16[16,24,128]{2,1,0:T(8,128)(2,1)S(1)} collective-permute-done((bf16[16,24,128]{2,1,0:T(8,128)(2,1)S(1)}, bf16[16,24,128]{2,1,0:T(8,128)(2,1)S(1)}, u32[]{:S(2)}, u32[]{:S(2)}) %collective-permute-start.5) | collective-permute-done | bytes 98336 | tf_op jit(solution)/shard_map/ppermute | solution.py:25
  47.1 0.3 shard_map.66
  47.4 0.2 abs_reduce_fusion.3
  47.6 0.1 multiply_convert_fusion.3
  47.8 3.7 %collective-permute-start.7 = (f16[400,128]{1,0:T(8,128)(2,1)S(1)}, f16[400,128]{1,0:T(8,128)(2,1)S(1)}, u32[]{:S(2)}, u32[]{:S(2)}) collective-permute-start(f16[400,128]{1,0:T(8,128)(2,1)S(1)} %fusion.10), channel_id=1, source_target_pairs={{0,8},{1,9},{2,10},{3,11},{4,12},{5,13},{6,14},{7,15},{8,0},{9,1},... | collective-permute-start | bytes 307208 | tf_op jit(solution)/shard_map/ppermute | solution.py:25
  51.6 0.2 collective-permute-start.6
  51.8 1.4 %collective-permute-start.8 = (f16[400,128]{1,0:T(8,128)(2,1)S(1)}, f16[400,128]{1,0:T(8,128)(2,1)S(1)}, u32[]{:S(2)}, u32[]{:S(2)}) collective-permute-start(f16[400,128]{1,0:T(8,128)(2,1)S(1)} %fusion.11), channel_id=1, source_target_pairs={{0,12},{1,13},{2,14},{3,15},{4,8},{5,9},{6,10},{7,11},{8,4},{9,5},... | collective-permute-start | bytes 307208 | tf_op jit(solution)/shard_map/ppermute | solution.py:25
  53.2 4.7 %collective-permute-done.7 = f16[400,128]{1,0:T(8,128)(2,1)S(1)} collective-permute-done((f16[400,128]{1,0:T(8,128)(2,1)S(1)}, f16[400,128]{1,0:T(8,128)(2,1)S(1)}, u32[]{:S(2)}, u32[]{:S(2)}) %collective-permute-start.7) | collective-permute-done | bytes 102432 | tf_op jit(solution)/shard_map/ppermute | solution.py:25
  57.9 2.2 %collective-permute-done.6 = f16[400,128]{1,0:T(8,128)(2,1)S(1)} collective-permute-done((f16[400,128]{1,0:T(8,128)(2,1)S(1)}, f16[400,128]{1,0:T(8,128)(2,1)S(1)}, u32[]{:S(2)}, u32[]{:S(2)}) %collective-permute-start.6) | collective-permute-done | bytes 102432 | tf_op jit(solution)/shard_map/ppermute | solution.py:25
  60.1 0.0 collective-permute-done.8
  60.2 0.8 %copy_bitcast_fusion = bf16[96,512]{1,0:T(8,128)(2,1)} fusion(f16[4,96,128]{2,1,0:T(8,128)(2,1)S(1)} %bitcast.54, f16[4,96,128]{2,1,0:T(8,128)(2,1)S(1)} %bitcast.51, f16[4,96,128]{2,1,0:T(8,128)(2,1)S(1)} %bitcast.52, f32[16,96,128]{2,1,0:T(8,128)S(1)} %shard_map.66, f32[96]{0:T(128)S(1)} %fusion.16, f32[96]{0:T(128)S(1)} %fusion.20, f32[96]{0:T(128)S(1)} %fusion.24), kind=kLoop, calls=%fused_computation.31 | loop fusion | flops 491520 | bytes 591360 | tf_op jit(solution)/shard_map/convert_element_type | solution.py:324
  (13 shorter events, 0.2 us)
Async XLA Ops:
  2.5 33.5 %all-to-all-start = ((bf16[80,4,1792]{2,1,0:T(4,128)(2,1)}), bf16[80,4,1792]{2,1,0:T(4,128)(2,1)S(1)}, u32[]{:S(2)}, u32[]{:S(2)}) async-start(bf16[80,4,1792]{2,1,0:T(4,128)(2,1)} %get-tuple-element.45), calls=%async_computation | async-start | bytes 2293760 | tf_op jit(solution)/shard_map/all_to_all | solution.py:315
  14.2 4.7 %collective-permute-start.1 = (f32[16,96,128]{2,1,0:T(8,128)S(1)}, f32[16,96,128]{2,1,0:T(8,128)S(1)}, u32[]{:S(2)}, u32[]{:S(2)}) collective-permute-start(f32[16,96,128]{2,1,0:T(8,128)S(1)} %branch_1_fun.4), channel_id=1, source_target_pairs={{0,1},{1,0},{2,3},{3,2},{4,5},{5,4},{6,7},{7,6},{8,9},{9,8},{10,11... | collective-permute-start | bytes 2359304 | tf_op jit(solution)/shard_map/cond/branch_1_fun/ppermute | solution.py:25
  19.4 16.5 %collective-permute-start.2 = (f16[1552,128]{1,0:T(8,128)(2,1)S(1)}, f16[1552,128]{1,0:T(8,128)(2,1)S(1)}, u32[]{:S(2)}, u32[]{:S(2)}) collective-permute-start(f16[1552,128]{1,0:T(8,128)(2,1)S(1)} %get-tuple-element.71), channel_id=1, source_target_pairs={{0,2},{1,3},{2,0},{3,1},{4,6},{5,7},{6,4},{7,5},{8,10},{9,11},{10,... | collective-permute-start | bytes 1191944 | tf_op jit(solution)/shard_map/ppermute | solution.py:25
  28.9 2.4 %collective-permute-start = (f32[16,96,128]{2,1,0:T(8,128)S(1)}, f32[16,96,128]{2,1,0:T(8,128)S(1)}, u32[]{:S(2)}, u32[]{:S(2)}) collective-permute-start(f32[16,96,128]{2,1,0:T(8,128)S(1)} %get-tuple-element.30), channel_id=1, source_target_pairs={{0,1},{1,0},{2,3},{3,2},{4,5},{5,4},{6,7},{7,6},{8,9},{9,8},{10,11... | collective-permute-start | bytes 2359304 | tf_op jit(solution)/shard_map/cond/branch_1_fun/ppermute | solution.py:25
  39.9 2.3 %collective-permute-start.3 = (bf16[16,24,128]{2,1,0:T(8,128)(2,1)S(1)}, bf16[16,24,128]{2,1,0:T(8,128)(2,1)S(1)}, u32[]{:S(2)}, u32[]{:S(2)}) collective-permute-start(bf16[16,24,128]{2,1,0:T(8,128)(2,1)S(1)} %get-tuple-element.48), channel_id=1, source_target_pairs={{0,1},{1,0},{2,3},{3,2},{4,5},{5,4},{6,7},{7,6},{8,9},{9,8},{10,11... | collective-permute-start | bytes 294920 | tf_op jit(solution)/shard_map/ppermute | solution.py:25
  40.0 5.7 %collective-permute-start.4 = (bf16[16,24,128]{2,1,0:T(8,128)(2,1)S(1)}, bf16[16,24,128]{2,1,0:T(8,128)(2,1)S(1)}, u32[]{:S(2)}, u32[]{:S(2)}) collective-permute-start(bf16[16,24,128]{2,1,0:T(8,128)(2,1)S(1)} %get-tuple-element.49), channel_id=1, source_target_pairs={{0,2},{1,3},{2,0},{3,1},{4,6},{5,7},{6,4},{7,5},{8,10},{9,11},{10,... | collective-permute-start | bytes 294920 | tf_op jit(solution)/shard_map/ppermute | solution.py:25
  42.0 5.2 %collective-permute-start.5 = (bf16[16,24,128]{2,1,0:T(8,128)(2,1)S(1)}, bf16[16,24,128]{2,1,0:T(8,128)(2,1)S(1)}, u32[]{:S(2)}, u32[]{:S(2)}) collective-permute-start(bf16[16,24,128]{2,1,0:T(8,128)(2,1)S(1)} %get-tuple-element.50), channel_id=1, source_target_pairs={{0,3},{1,2},{2,1},{3,0},{4,7},{5,6},{6,5},{7,4},{8,11},{9,10},{10,... | collective-permute-start | bytes 294920 | tf_op jit(solution)/shard_map/ppermute | solution.py:25
  47.8 10.1 %collective-permute-start.7 = (f16[400,128]{1,0:T(8,128)(2,1)S(1)}, f16[400,128]{1,0:T(8,128)(2,1)S(1)}, u32[]{:S(2)}, u32[]{:S(2)}) collective-permute-start(f16[400,128]{1,0:T(8,128)(2,1)S(1)} %fusion.10), channel_id=1, source_target_pairs={{0,8},{1,9},{2,10},{3,11},{4,12},{5,13},{6,14},{7,15},{8,0},{9,1},... | collective-permute-start | bytes 307208 | tf_op jit(solution)/shard_map/ppermute | solution.py:25
  51.6 8.5 %collective-permute-start.6 = (f16[400,128]{1,0:T(8,128)(2,1)S(1)}, f16[400,128]{1,0:T(8,128)(2,1)S(1)}, u32[]{:S(2)}, u32[]{:S(2)}) collective-permute-start(f16[400,128]{1,0:T(8,128)(2,1)S(1)} %fusion.9), channel_id=1, source_target_pairs={{0,4},{1,5},{2,6},{3,7},{4,0},{5,1},{6,2},{7,3},{8,12},{9,13},{10,... | collective-permute-start | bytes 307208 | tf_op jit(solution)/shard_map/ppermute | solution.py:25
  51.8 8.4 %collective-permute-start.8 = (f16[400,128]{1,0:T(8,128)(2,1)S(1)}, f16[400,128]{1,0:T(8,128)(2,1)S(1)}, u32[]{:S(2)}, u32[]{:S(2)}) collective-permute-start(f16[400,128]{1,0:T(8,128)(2,1)S(1)} %fusion.11), channel_id=1, source_target_pairs={{0,12},{1,13},{2,14},{3,15},{4,8},{5,9},{6,10},{7,11},{8,4},{9,5},... | collective-permute-start | bytes 307208 | tf_op jit(solution)/shard_map/ppermute | solution.py:25

commit v18 on v17

--- a/solution.py
+++ b/solution.py
@@ -13,7 +13,6 @@
 LANES = 128
 F16_TOP = 14.0
 PLANE = 4
-HELD = 24
 MARK_ROWS = 16
 
 
@@ -121,17 +120,25 @@
     return kept, pair_in
 
 
-def line_sums(pair, group, width):
-    rows = pair.shape[1]
+def line_sums(kept, pair_in, flag, group, width):
+    rows = kept.shape[1]
     parts = width // LANES
-    arrived = [
-        xor_permute(pack_scaled(pair[i * parts : (i + 1) * parts]), group, 4 * i)
-        for i in range(1, group // 4)
-    ]
-    total = pair[:parts]
-    for packed in arrived:
-        total = total + unpack_scaled(packed, rows)
-    return jnp.transpose(total, (1, 0, 2)).reshape(rows, width)
+
+    def work():
+        pair = kept + unpack_scaled(pair_in, rows)
+        arrived = [
+            xor_permute(pack_scaled(pair[i * parts : (i + 1) * parts]), group, PLANE * i)
+            for i in range(1, group // PLANE)
+        ]
+        total = pair[:parts]
+        for packed in arrived:
+            total = total + unpack_scaled(packed, rows)
+        return total
+
+    def idle():
+        return jnp.zeros((parts, rows, LANES), jnp.float32)
+
+    return lax.cond(flag >= 0, work, idle)
 
 
 def pack_kernel(
@@ -173,10 +180,7 @@
     place = jnp.sum(shift, axis=0, keepdims=True) + lax.broadcasted_iota(jnp.int32, (1, rows), 1)
     spots = lax.broadcasted_iota(jnp.int32, (group * blocks * BLOCK, rows), 0)
     pick = jnp.where(spots == place, 1.0, 0.0).astype(jnp.bfloat16)
-    for k in range(PLANE):
-        line = lax.broadcasted_iota(jnp.int32, (HELD, rows), 0)
-        mine = (line + (me_ref[0] ^ k) * (blocks * BLOCK) == place) & (line < blocks * BLOCK)
-        pick_ref[k * HELD : (k + 1) * HELD] = jnp.where(mine, 1.0, 0.0).astype(jnp.bfloat16)
+    pick_ref[...] = pick
     copies[2].wait()
     packed = jnp.dot(pick, hidden_ref[...], preferred_element_type=jnp.float32)
     packed_ref[...] = packed.astype(jnp.bfloat16).reshape(packed_ref.shape)
@@ -194,7 +198,7 @@
         functools.partial(pack_kernel, blocks, orders),
         out_shape=(
             jax.ShapeDtypeStruct((group * blocks, BLOCK, depth), jnp.bfloat16),
-            jax.ShapeDtypeStruct((PLANE * HELD, rows), jnp.bfloat16),
+            jax.ShapeDtypeStruct((group * MOST, rows), jnp.bfloat16),
             jax.ShapeDtypeStruct((len(orders),), jnp.int32),
             jax.ShapeDtypeStruct((rows, depth), jnp.bfloat16),
         ),
@@ -210,12 +214,12 @@
     )(me.reshape(1), in_hbm(adapter_holder_slot), in_hbm(adapter_of_row.reshape(1, rows)), in_hbm(hidden))
 
 
-def adapter_kernel(parts, me_ref, rows_ref, expand_hbm, shrink_hbm, *refs):
-    out_refs = refs[:PLANE]
-    shrink_ref, expand_ref, total_ref, sems, expand_sem = refs[PLANE:]
-    me = me_ref[0]
+def adapter_kernel(rows_ref, expand_hbm, shrink_hbm, out_ref, flag_ref, *refs):
+    shrink_ref, expand_ref, sems, expand_sem = refs
     group, _, depth = shrink_ref.shape
     blocks = MOST // BLOCK
+    width = out_ref.shape[2]
+    flag_ref[0] = group
 
     def copy(source):
         return pltpu.make_async_copy(
@@ -226,78 +230,72 @@
         copy(source).start()
     expand_copy = pltpu.make_async_copy(expand_hbm, expand_ref, expand_sem)
     expand_copy.start()
-    total = jnp.zeros((MOST, total_ref.shape[1]), jnp.float32)
+    total = jnp.zeros((MOST, shrink_ref.shape[1]), jnp.float32)
     for source in range(group):
         copy(source).wait()
         own = rows_ref[source * blocks : (source + 1) * blocks].reshape(MOST, depth)
         total += lax.dot_general(
             own, shrink_ref[source], (((1,), (1,)), ((), ())), preferred_element_type=jnp.float32
         )
-    total_ref[...] = jnp.zeros_like(total_ref)
-    total_ref[:MOST] = total
-    rank_rows = total_ref[...].astype(jnp.bfloat16)
+    rank_rows = total.astype(jnp.bfloat16)
     expand_copy.wait()
-    width = parts * LANES
-    for k in range(PLANE):
-        for line in range(group // PLANE):
-            target = me ^ (PLANE * line + k)
-            columns = pl.ds(pl.multiple_of(target * width, LANES), width)
-            piece = jnp.dot(rank_rows, expand_ref[:, columns], preferred_element_type=jnp.float32)
-            piece = piece.astype(jnp.bfloat16)
-            for part in range(parts):
-                out_refs[k][line * parts + part] = piece[:, part * LANES : (part + 1) * LANES]
-
-
-def adapter_output(gathered, shrink, expand, group, me):
+    for target in range(group):
+        piece = jnp.dot(
+            rank_rows,
+            expand_ref[:, target * width : (target + 1) * width],
+            preferred_element_type=jnp.float32,
+        )
+        out_ref[target * blocks : (target + 1) * blocks] = piece.astype(jnp.bfloat16).reshape(
+            blocks, BLOCK, width
+        )
+
+
+def adapter_output(gathered, shrink, expand, group):
     rank = shrink.shape[0]
     model_width = expand.shape[1]
     depth = gathered.shape[2]
-    parts = model_width // group // LANES
-    held = (model_width // PLANE // LANES, HELD, LANES)
     vmem = pl.BlockSpec(memory_space=pltpu.VMEM)
     return pl.pallas_call(
-        functools.partial(adapter_kernel, parts),
-        out_shape=[jax.ShapeDtypeStruct(held, jnp.bfloat16)] * PLANE,
-        in_specs=[
-            pl.BlockSpec(memory_space=pltpu.SMEM),
-            vmem,
-            pl.BlockSpec(memory_space=pl.ANY),
-            pl.BlockSpec(memory_space=pl.ANY),
-        ],
-        out_specs=[vmem] * PLANE,
+        adapter_kernel,
+        out_shape=[
+            jax.ShapeDtypeStruct((gathered.shape[0], BLOCK, model_width // group), jnp.bfloat16),
+            jax.ShapeDtypeStruct((1,), jnp.int32),
+        ],
+        in_specs=[vmem, pl.BlockSpec(memory_space=pl.ANY), pl.BlockSpec(memory_space=pl.ANY)],
+        out_specs=[vmem, pl.BlockSpec(memory_space=pltpu.SMEM)],
         scratch_shapes=[
             pltpu.VMEM((group, rank, depth), jnp.bfloat16),
             pltpu.VMEM((rank, model_width), jnp.bfloat16),
-            pltpu.VMEM((HELD, rank), jnp.float32),
             pltpu.SemaphoreType.DMA((group,)),
             pltpu.SemaphoreType.DMA,
         ],
         compiler_params=pltpu.CompilerParams(vmem_limit_bytes=24 * 2**20),
-    )(me.reshape(1), gathered, in_hbm(expand), in_hbm(shrink))
-
-
-def merge_kernel(pair_ref, pick_ref, *refs):
-    in_refs, out_ref, held_ref = refs[:PLANE], refs[PLANE], refs[PLANE + 1]
-    for k in range(PLANE):
-        held_ref[:, k * HELD : (k + 1) * HELD] = in_refs[k][...]
-    pick = pick_ref[...]
-    for part in range(pair_ref.shape[0]):
-        adapter_rows = lax.dot_general(
-            pick, held_ref[part], (((0,), (0,)), ((), ())), preferred_element_type=jnp.float32
-        )
-        out_ref[part] = pair_ref[part] + ADAPTER_SCALE * adapter_rows
-
-
-def merge_adapters(pair, pick, arrived):
+    )(gathered, in_hbm(expand), in_hbm(shrink))
+
+
+def final_kernel(base_ref, pick_ref, rows_ref, out_ref):
+    adapter_rows = lax.dot_general(
+        pick_ref[...],
+        rows_ref[...].reshape(pick_ref.shape[0], out_ref.shape[1]),
+        (((0,), (0,)), ((), ())),
+        preferred_element_type=jnp.float32,
+    )
+    for part in range(base_ref.shape[0]):
+        lanes = slice(part * LANES, (part + 1) * LANES)
+        total = base_ref[part] + ADAPTER_SCALE * adapter_rows[:, lanes]
+        out_ref[:, lanes] = total.astype(out_ref.dtype)
+
+
+def add_adapters(base, pick, arrived):
+    parts, rows, _ = base.shape
     vmem = pl.BlockSpec(memory_space=pltpu.VMEM)
     return pl.pallas_call(
-        merge_kernel,
-        out_shape=jax.ShapeDtypeStruct(pair.shape, jnp.float32),
-        in_specs=[vmem] * (2 + PLANE),
+        final_kernel,
+        out_shape=jax.ShapeDtypeStruct((rows, parts * LANES), jnp.bfloat16),
+        in_specs=[vmem] * 3,
         out_specs=vmem,
-        scratch_shapes=[pltpu.VMEM((pair.shape[0], PLANE * HELD, LANES), jnp.bfloat16)],
         compiler_params=pltpu.CompilerParams(vmem_limit_bytes=24 * 2**20),
-    )(pair, pick, *arrived)
+    )(base, pick, arrived)
 
 
 def shards_by_blocks(
@@ -317,11 +315,10 @@
     kept, pair_in = pair_sums(kept_hidden, down_matrix, group, order, width)
     gathered, _ = lax.optimization_barrier((gathered, kept))
     expand = jnp.swapaxes(expand_matrices, 1, 2)[0]
-    outs = adapter_output(gathered, shrink, expand, group, me)
-    arrived = [outs[0]] + [xor_permute(outs[k], group, k) for k in range(1, PLANE)]
-    pair = kept + unpack_scaled(pair_in, rows)
-    merged = merge_adapters(pair, pick, arrived)
-    return line_sums(merged, group, width).astype(jnp.bfloat16)
+    adapter_out, flag = adapter_output(gathered, shrink, expand, group)
+    arrived = lax.all_to_all(adapter_out, "tp", split_axis=0, concat_axis=0, tiled=True)
+    base = line_sums(kept, pair_in, flag[0], group, width)
+    return add_adapters(base, pick, arrived)
 
 
 def shards(

time: 61.2 us -> 75 us (1.23)
  waiting for transfers between devices: 18.6 us -> 26.4 us
  starting transfers between devices: 17.2 us -> 21.9 us
  Pallas kernels: 21.4 us -> 22.7 us
    all_to_all x0 -> x1, starting transfers between devices: none -> 7.36 us  [shards_by_blocks(): lax.all_to_all(adapter_out, 'tp', split_axis=0, concat_axis=0, tiled=True)]
    all_to_all x1, waiting for transfers between devices: 0.01 us -> 4.88 us  [shards_by_blocks(): lax.all_to_all(packed, 'tp', split_axis=0, concat_axis=0, tiled=True)]
    ppermute x9 -> x6, waiting for transfers between devices: 18.6 us -> 21.5 us  [xor_permute(): return lax.ppermute(value, 'tp', [(i, i ^ offset) for i in range(group)])]
    ppermute x9 -> x6, starting transfers between devices: 9.85 us -> 7.14 us  [xor_permute(): return lax.ppermute(value, 'tp', [(i, i ^ offset) for i in range(group)])]
    pallas_call x2, Pallas kernels: 4.15 us -> 5.39 us  [the longest x1 4.52 us: adapter_output(): pl.pallas_call(adapter_kernel, out_shape=[jax.ShapeDtypeStruct((gathered....]
    convert_element_type x1 -> x0, other arithmetic: 0.79 us -> none  [shards_by_blocks(): return line_sums(merged, group, width).astype(jnp.bfloat16)]
  transfers between devices with their start and end apart: 10 -> 8, of which waited for: 6 -> 5; matrix products, arithmetic and copies ran while one was open for 3% -> 3% of each run, Pallas kernels for 24% -> 20%
where the time goes in v18:
time: 75 us; the launch traced here: 74.7 us
  waiting for transfers between devices  26.4 us (35%)
  Pallas kernels  22.7 us (30%)
  starting transfers between devices  21.9 us (29%)
  between operations  1.4 us (2%)
  other arithmetic  1.29 us (2%)
  local copies, waits for them, and re-layouts  0.88 us (1%)
    ppermute x6, waiting for transfers between devices, xor_permute(): return lax.ppermute(value, 'tp', [(i, i ^ offset) for i in range(group)])  21.5 us
    pallas_call x3, Pallas kernels, column_blocks(): pl.pallas_call(functools.partial(column_blocks_kernel, groups), out_shape...  14.8 us
    all_to_all x1, starting transfers between devices, shards_by_blocks(): lax.all_to_all(packed, 'tp', split_axis=0, concat_axis=0, tiled=True)  7.37 us
    all_to_all x1, starting transfers between devices, shards_by_blocks(): lax.all_to_all(adapter_out, 'tp', split_axis=0, concat_axis=0, tiled=True)  7.36 us
    ppermute x6, starting transfers between devices, xor_permute(): return lax.ppermute(value, 'tp', [(i, i ^ offset) for i in range(group)])  7.14 us
    all_to_all x1, waiting for transfers between devices, shards_by_blocks(): lax.all_to_all(packed, 'tp', split_axis=0, concat_axis=0, tiled=True)  4.88 us
    pallas_call x1, Pallas kernels, adapter_output(): pl.pallas_call(adapter_kernel, out_shape=[jax.ShapeDtypeStruct((gathered....  4.52 us
    pallas_call x1, Pallas kernels, pack_rows(): pl.pallas_call(functools.partial(pack_kernel, blocks, orders), out_shape=...  2.51 us
  transfers between devices with their start and end apart: 8, of which 5 were waited for; matrix products, arithmetic and copies ran while one was open for 3% of the time, Pallas kernels for 20%

profile of v18, /device:TPU:0, one launch (start us, length us, event | category | flops | bytes accessed | tf_op | source)
XLA Modules:
  0.0 74.7 jit_solution(3709146444631913557)
XLA Ops:
  0.0 2.5 %shard_map.64 = (bf16[80,4,1792]{2,1,0:T(4,128)(2,1)}, bf16[320,96]{1,0:T(8,128)(2,1)S(1)}, s32[16]{0:T(128)S(1)}, bf16[96,1792]{1,0:T(8,128)(2,1)S(1)}) custom-call(s32[1]{0:T(128)} %bitcast.20.me_ref, s32[16]{0:T(128)} %slot_hbm.1, s32[1,96]{1,0:T(1,128)} %bitcast.51, bf16[96,1792]{1,0:T(8,128)(2,1)} %hidden_hbm.1), custom_call_target="tpu_custom_call" | custom-call | tf_op jit(solution)/shard_map/pallas_call | solution.py:197
  2.5 7.4 %all-to-all-start = ((bf16[80,4,1792]{2,1,0:T(4,128)(2,1)}), bf16[80,4,1792]{2,1,0:T(4,128)(2,1)S(1)}, u32[]{:S(2)}, u32[]{:S(2)}) async-start(bf16[80,4,1792]{2,1,0:T(4,128)(2,1)} %get-tuple-element.48), calls=%async_computation | async-start | bytes 2293760 | tf_op jit(solution)/shard_map/all_to_all | solution.py:313
  9.9 9.4 %conditional.3 = (f16[1552,128]{1,0:T(8,128)(2,1)S(1)}) conditional(s32[]{:T(128)} %bitcast.22, () %tuple.25, (s32[16]{0:T(128)S(1)}, bf16[96,1792]{1,0:T(8,128)(2,1)S(1)}, bf16[1792,8192]{1,0:T(8,128)(2,1)}) %tuple.26), branch_computations={%region_0.0_spmd, %region_1.3_spmd} | conditional | flops 1581488 | bytes 7479232 | solution.py:108
  9.9 0.1 fusion.23
  10.0 4.2 %branch_1_fun.4 = f32[16,96,128]{2,1,0:T(8,128)S(1)} custom-call(s32[4]{0:T(128)S(1)} %get-tuple-element.63.order_ref, bf16[96,1792]{1,0:T(8,128)(2,1)S(1)} %get-tuple-element.30.hidden_ref, bf16[1792,8192]{1,0:T(8,128)(2,1)} %get-tuple-element.32.down_ref), custom_call_target="tpu_custom_call" | custom-call | flops 1000 | bytes 1000 | tf_op jit(solution)/shard_map/cond/branch_1_fun/pallas_call | solution.py:61
  14.2 0.5 collective-permute-start.4
  14.7 4.2 %branch_1_fun.3 = f32[16,96,128]{2,1,0:T(8,128)S(1)} custom-call(s32[4]{0:T(128)S(1)} %get-tuple-element.64.order_ref, bf16[96,1792]{1,0:T(8,128)(2,1)S(1)} %get-tuple-element.30.hidden_ref, bf16[1792,8192]{1,0:T(8,128)(2,1)} %get-tuple-element.32.down_ref), custom_call_target="tpu_custom_call" | custom-call | flops 1000 | bytes 1000 | tf_op jit(solution)/shard_map/cond/branch_1_fun/pallas_call | solution.py:61
  18.9 0.0 collective-permute-done.4
  18.9 0.2 abs_reduce_fusion
  19.1 0.2 multiply_convert_fusion
  19.3 0.1 fusion.1
  19.4 0.6 slice.52
  20.6 9.0 %conditional.4 = (f32[16,96,128]{2,1,0:T(8,128)S(1)}) conditional(s32[]{:T(128)} %bitcast.23, () %tuple.28, (s32[16]{0:T(128)S(1)}, bf16[96,1792]{1,0:T(8,128)(2,1)S(1)}, bf16[1792,8192]{1,0:T(8,128)(2,1)}) %tuple.29), branch_computations={%region_3.4_spmd, %region_4.5_spmd} | conditional | flops 197608 | bytes 5506136 | solution.py:119
  20.6 0.1 slice.36.order_ref
  20.7 6.4 %branch_1_fun.5 = (f32[16,96,128]{2,1,0:T(8,128)S(1)}, f32[16,96,128]{2,1,0:T(8,128)S(1)}) custom-call(s32[8]{0:T(128)S(1)} %slice.36.order_ref, bf16[96,1792]{1,0:T(8,128)(2,1)S(1)} %get-tuple-element.34.hidden_ref, bf16[1792,8192]{1,0:T(8,128)(2,1)} %get-tuple-element.35.down_ref), custom_call_target="tpu_custom_call" | custom-call | flops 1000 | bytes 1000 | tf_op jit(solution)/shard_map/cond/branch_1_fun/pallas_call | solution.py:61
  27.1 0.2 collective-permute-start
  27.3 2.2 %collective-permute-done = f32[16,96,128]{2,1,0:T(8,128)S(1)} collective-permute-done((f32[16,96,128]{2,1,0:T(8,128)S(1)}, f32[16,96,128]{2,1,0:T(8,128)S(1)}, u32[]{:S(2)}, u32[]{:S(2)}) %collective-permute-start) | collective-permute-done | bytes 786464 | tf_op jit(solution)/shard_map/cond/branch_1_fun/ppermute | solution.py:24
  29.5 0.1 add.39
  29.6 4.9 %all-to-all-done.rows_ref = bf16[80,4,1792]{2,1,0:T(4,128)(2,1)S(1)} async-done(((bf16[80,4,1792]{2,1,0:T(4,128)(2,1)}), bf16[80,4,1792]{2,1,0:T(4,128)(2,1)S(1)}, u32[]{:S(2)}, u32[]{:S(2)}) %all-to-all-start) | async-done | bytes 1146912 | tf_op jit(solution)/shard_map/all_to_all | solution.py:313
  34.5 4.5 %shard_map.65 = (bf16[80,4,512]{2,1,0:T(4,128)(2,1)}, s32[1]{0:T(128)}) custom-call(bf16[80,4,1792]{2,1,0:T(4,128)(2,1)S(1)} %all-to-all-done.rows_ref, bf16[64,8192]{1,0:T(8,128)(2,1)} %bitcast.43, bf16[64,28672]{1,0:T(8,128)(2,1)} %bitcast.40), custom_call_target="tpu_custom_call" | custom-call | tf_op jit(solution)/shard_map/pallas_call | solution.py:258
  39.0 7.4 %all-to-all-start.1 = ((bf16[80,4,512]{2,1,0:T(4,128)(2,1)}), bf16[80,4,512]{2,1,0:T(4,128)(2,1)S(1)}, u32[]{:S(2)}, u32[]{:S(2)}) async-start(bf16[80,4,512]{2,1,0:T(4,128)(2,1)} %get-tuple-element.55), calls=%async_computation.1 | async-start | bytes 655360 | tf_op jit(solution)/shard_map/all_to_all | solution.py:319
  46.3 1.9 %collective-permute-start.5 = (f16[1552,128]{1,0:T(8,128)(2,1)S(1)}, f16[1552,128]{1,0:T(8,128)(2,1)S(1)}, u32[]{:S(2)}, u32[]{:S(2)}) collective-permute-start(f16[1552,128]{1,0:T(8,128)(2,1)S(1)} %get-tuple-element.76), channel_id=1, source_target_pairs={{0,2},{1,3},{2,0},{3,1},{4,6},{5,7},{6,4},{7,5},{8,10},{9,11},{10,... | collective-permute-start | bytes 1191944 | tf_op jit(solution)/shard_map/ppermute | solution.py:24
  48.3 13.2 %collective-permute-done.5 = f16[1552,128]{1,0:T(8,128)(2,1)S(1)} collective-permute-done((f16[1552,128]{1,0:T(8,128)(2,1)S(1)}, f16[1552,128]{1,0:T(8,128)(2,1)S(1)}, u32[]{:S(2)}, u32[]{:S(2)}) %collective-permute-start.5) | collective-permute-done | bytes 397344 | tf_op jit(solution)/shard_map/ppermute | solution.py:24
  62.2 11.6 %conditional.5 = (f32[4,96,128]{2,1,0:T(8,128)S(1)}) conditional(s32[]{:T(128)} %bitcast.28, () %tuple.31, (f16[1552,128]{1,0:T(8,128)(2,1)S(1)}, f32[16,96,128]{2,1,0:T(8,128)S(1)}) %tuple.32), branch_computations={%region_5.6_spmd, %region_6.10_spmd} | conditional | flops 2085408 | bytes 7345664 | solution.py:141
  62.2 0.1 slice.37
  62.3 0.2 fusion.2
  62.4 0.2 abs_reduce_fusion.3
  62.6 0.1 multiply_convert_fusion.3
  62.8 2.4 %collective-permute-start.2 = (f16[400,128]{1,0:T(8,128)(2,1)S(1)}, f16[400,128]{1,0:T(8,128)(2,1)S(1)}, u32[]{:S(2)}, u32[]{:S(2)}) collective-permute-start(f16[400,128]{1,0:T(8,128)(2,1)S(1)} %fusion.9), channel_id=1, source_target_pairs={{0,8},{1,9},{2,10},{3,11},{4,12},{5,13},{6,14},{7,15},{8,0},{9,1},... | collective-permute-start | bytes 307208 | tf_op jit(solution)/shard_map/cond/branch_1_fun/ppermute | solution.py:24
  65.3 1.5 %collective-permute-start.1 = (f16[400,128]{1,0:T(8,128)(2,1)S(1)}, f16[400,128]{1,0:T(8,128)(2,1)S(1)}, u32[]{:S(2)}, u32[]{:S(2)}) collective-permute-start(f16[400,128]{1,0:T(8,128)(2,1)S(1)} %fusion.8), channel_id=1, source_target_pairs={{0,4},{1,5},{2,6},{3,7},{4,0},{5,1},{6,2},{7,3},{8,12},{9,13},{10,... | collective-permute-start | bytes 307208 | tf_op jit(solution)/shard_map/cond/branch_1_fun/ppermute | solution.py:24
  66.8 0.6 collective-permute-start.3
  67.5 4.3 %collective-permute-done.2 = f16[400,128]{1,0:T(8,128)(2,1)S(1)} collective-permute-done((f16[400,128]{1,0:T(8,128)(2,1)S(1)}, f16[400,128]{1,0:T(8,128)(2,1)S(1)}, u32[]{:S(2)}, u32[]{:S(2)}) %collective-permute-start.2) | collective-permute-done | bytes 102432 | tf_op jit(solution)/shard_map/cond/branch_1_fun/ppermute | solution.py:24
  71.8 0.0 collective-permute-done.1
  71.9 1.7 %collective-permute-done.3 = f16[400,128]{1,0:T(8,128)(2,1)S(1)} collective-permute-done((f16[400,128]{1,0:T(8,128)(2,1)S(1)}, f16[400,128]{1,0:T(8,128)(2,1)S(1)}, u32[]{:S(2)}, u32[]{:S(2)}) %collective-permute-start.3) | collective-permute-done | bytes 102432 | tf_op jit(solution)/shard_map/cond/branch_1_fun/ppermute | solution.py:24
  73.6 0.1 fusion.7
  73.8 0.0 all-to-all-done.1.rows_ref
  73.8 0.9 %shard_map.66 = bf16[96,512]{1,0:T(8,128)(2,1)} custom-call(f32[4,96,128]{2,1,0:T(8,128)S(1)} %get-tuple-element.78.base_ref, bf16[320,96]{1,0:T(8,128)(2,1)S(1)} %get-tuple-element.54.pick_ref, bf16[80,4,512]{2,1,0:T(4,128)(2,1)S(1)} %all-to-all-done.1.rows_ref), custom_call_target="tpu_custom_call" | custom-call | tf_op jit(solution)/shard_map/pallas_call | solution.py:292
  (13 shorter events, 0.2 us)
Async XLA Ops:
  2.5 31.9 %all-to-all-start = ((bf16[80,4,1792]{2,1,0:T(4,128)(2,1)}), bf16[80,4,1792]{2,1,0:T(4,128)(2,1)S(1)}, u32[]{:S(2)}, u32[]{:S(2)}) async-start(bf16[80,4,1792]{2,1,0:T(4,128)(2,1)} %get-tuple-element.48), calls=%async_computation | async-start | bytes 2293760 | tf_op jit(solution)/shard_map/all_to_all | solution.py:313
  14.2 4.7 %collective-permute-start.4 = (f32[16,96,128]{2,1,0:T(8,128)S(1)}, f32[16,96,128]{2,1,0:T(8,128)S(1)}, u32[]{:S(2)}, u32[]{:S(2)}) collective-permute-start(f32[16,96,128]{2,1,0:T(8,128)S(1)} %branch_1_fun.4), channel_id=1, source_target_pairs={{0,1},{1,0},{2,3},{3,2},{4,5},{5,4},{6,7},{7,6},{8,9},{9,8},{10,11... | collective-permute-start | bytes 2359304 | tf_op jit(solution)/shard_map/cond/branch_1_fun/ppermute | solution.py:24
  27.1 2.4 %collective-permute-start = (f32[16,96,128]{2,1,0:T(8,128)S(1)}, f32[16,96,128]{2,1,0:T(8,128)S(1)}, u32[]{:S(2)}, u32[]{:S(2)}) collective-permute-start(f32[16,96,128]{2,1,0:T(8,128)S(1)} %get-tuple-element.37), channel_id=1, source_target_pairs={{0,1},{1,0},{2,3},{3,2},{4,5},{5,4},{6,7},{7,6},{8,9},{9,8},{10,11... | collective-permute-start | bytes 2359304 | tf_op jit(solution)/shard_map/cond/branch_1_fun/ppermute | solution.py:24
  39.0 34.8 %all-to-all-start.1 = ((bf16[80,4,512]{2,1,0:T(4,128)(2,1)}), bf16[80,4,512]{2,1,0:T(4,128)(2,1)S(1)}, u32[]{:S(2)}, u32[]{:S(2)}) async-start(bf16[80,4,512]{2,1,0:T(4,128)(2,1)} %get-tuple-element.55), calls=%async_computation.1 | async-start | bytes 655360 | tf_op jit(solution)/shard_map/all_to_all | solution.py:319
  46.3 15.2 %collective-permute-start.5 = (f16[1552,128]{1,0:T(8,128)(2,1)S(1)}, f16[1552,128]{1,0:T(8,128)(2,1)S(1)}, u32[]{:S(2)}, u32[]{:S(2)}) collective-permute-start(f16[1552,128]{1,0:T(8,128)(2,1)S(1)} %get-tuple-element.76), channel_id=1, source_target_pairs={{0,2},{1,3},{2,0},{3,1},{4,6},{5,7},{6,4},{7,5},{8,10},{9,11},{10,... | collective-permute-start | bytes 1191944 | tf_op jit(solution)/shard_map/ppermute | solution.py:24
  62.8 9.0 %collective-permute-start.2 = (f16[400,128]{1,0:T(8,128)(2,1)S(1)}, f16[400,128]{1,0:T(8,128)(2,1)S(1)}, u32[]{:S(2)}, u32[]{:S(2)}) collective-permute-start(f16[400,128]{1,0:T(8,128)(2,1)S(1)} %fusion.9), channel_id=1, source_target_pairs={{0,8},{1,9},{2,10},{3,11},{4,12},{5,13},{6,14},{7,15},{8,0},{9,1},... | collective-permute-start | bytes 307208 | tf_op jit(solution)/shard_map/cond/branch_1_fun/ppermute | solution.py:24
  65.3 6.5 %collective-permute-start.1 = (f16[400,128]{1,0:T(8,128)(2,1)S(1)}, f16[400,128]{1,0:T(8,128)(2,1)S(1)}, u32[]{:S(2)}, u32[]{:S(2)}) collective-permute-start(f16[400,128]{1,0:T(8,128)(2,1)S(1)} %fusion.8), channel_id=1, source_target_pairs={{0,4},{1,5},{2,6},{3,7},{4,0},{5,1},{6,2},{7,3},{8,12},{9,13},{10,... | collective-permute-start | bytes 307208 | tf_op jit(solution)/shard_map/cond/branch_1_fun/ppermute | solution.py:24
  66.8 6.8 %collective-permute-start.3 = (f16[400,128]{1,0:T(8,128)(2,1)S(1)}, f16[400,128]{1,0:T(8,128)(2,1)S(1)}, u32[]{:S(2)}, u32[]{:S(2)}) collective-permute-start(f16[400,128]{1,0:T(8,128)(2,1)S(1)} %fusion.10), channel_id=1, source_target_pairs={{0,12},{1,13},{2,14},{3,15},{4,8},{5,9},{6,10},{7,11},{8,4},{9,5},... | collective-permute-start | bytes 307208 | tf_op jit(solution)/shard_map/cond/branch_1_fun/ppermute | solution.py:24

commit v19 on v18

--- a/solution.py
+++ b/solution.py
@@ -313,7 +313,7 @@
     gathered = lax.all_to_all(packed, "tp", split_axis=0, concat_axis=0, tiled=True)
     shrink = jnp.swapaxes(shrink_matrices, 1, 2)[0]
     kept, pair_in = pair_sums(kept_hidden, down_matrix, group, order, width)
-    gathered, _ = lax.optimization_barrier((gathered, kept))
+    gathered, _, pair_in = lax.optimization_barrier((gathered, kept, pair_in))
     expand = jnp.swapaxes(expand_matrices, 1, 2)[0]
     adapter_out, flag = adapter_output(gathered, shrink, expand, group)
     arrived = lax.all_to_all(adapter_out, "tp", split_axis=0, concat_axis=0, tiled=True)

time: 75 us -> 66 us (0.88)
  waiting for transfers between devices: 26.4 us -> 19 us
  starting transfers between devices: 21.9 us -> 20.2 us
    all_to_all x1, waiting for transfers between devices: 4.88 us -> 0.01 us  [shards_by_blocks(): lax.all_to_all(packed, 'tp', split_axis=0, concat_axis=0, tiled=True)]
    ppermute x6, waiting for transfers between devices: 21.5 us -> 19 us  [xor_permute(): return lax.ppermute(value, 'tp', [(i, i ^ offset) for i in range(group)])]
    all_to_all x1, starting transfers between devices: 7.36 us -> 5.89 us  [shards_by_blocks(): lax.all_to_all(adapter_out, 'tp', split_axis=0, concat_axis=0, tiled=True)]
  transfers between devices with their start and end apart: 8 -> 8, of which waited for: 5 -> 3; matrix products, arithmetic and copies ran while one was open for 3% -> 3% of each run, Pallas kernels for 20% -> 23%
where the time goes in v19:
time: 66 us; the launch traced here: 65.6 us
  Pallas kernels  22.7 us (34%)
  starting transfers between devices  20.2 us (31%)
  waiting for transfers between devices  19 us (29%)
  between operations  1.4 us (2%)
  other arithmetic  1.29 us (2%)
  local copies, waits for them, and re-layouts  0.87 us (1%)
    ppermute x6, waiting for transfers between devices, xor_permute(): return lax.ppermute(value, 'tp', [(i, i ^ offset) for i in range(group)])  19 us
    pallas_call x3, Pallas kernels, column_blocks(): pl.pallas_call(functools.partial(column_blocks_kernel, groups), out_shape...  14.8 us
    all_to_all x1, starting transfers between devices, shards_by_blocks(): lax.all_to_all(packed, 'tp', split_axis=0, concat_axis=0, tiled=True)  7.37 us
    ppermute x6, starting transfers between devices, xor_permute(): return lax.ppermute(value, 'tp', [(i, i ^ offset) for i in range(group)])  6.94 us
    all_to_all x1, starting transfers between devices, shards_by_blocks(): lax.all_to_all(adapter_out, 'tp', split_axis=0, concat_axis=0, tiled=True)  5.89 us
    pallas_call x1, Pallas kernels, adapter_output(): pl.pallas_call(adapter_kernel, out_shape=[jax.ShapeDtypeStruct((gathered....  4.52 us
    pallas_call x1, Pallas kernels, pack_rows(): pl.pallas_call(functools.partial(pack_kernel, blocks, orders), out_shape=...  2.51 us
  transfers between devices with their start and end apart: 8, of which 3 were waited for; matrix products, arithmetic and copies ran while one was open for 3% of the time, Pallas kernels for 23%

profile of v19, /device:TPU:0, one launch (start us, length us, event | category | flops | bytes accessed | tf_op | source)
XLA Modules:
  0.0 65.6 jit_solution(1357006513945163404)
XLA Ops:
  0.0 2.5 %shard_map.64 = (bf16[80,4,1792]{2,1,0:T(4,128)(2,1)}, bf16[320,96]{1,0:T(8,128)(2,1)S(1)}, s32[16]{0:T(128)S(1)}, bf16[96,1792]{1,0:T(8,128)(2,1)S(1)}) custom-call(s32[1]{0:T(128)} %bitcast.20.me_ref, s32[16]{0:T(128)} %slot_hbm.1, s32[1,96]{1,0:T(1,128)} %bitcast.51, bf16[96,1792]{1,0:T(8,128)(2,1)} %hidden_hbm.1), custom_call_target="tpu_custom_call" | custom-call | tf_op jit(solution)/shard_map/pallas_call | solution.py:197
  2.5 7.4 %all-to-all-start = ((bf16[80,4,1792]{2,1,0:T(4,128)(2,1)}), bf16[80,4,1792]{2,1,0:T(4,128)(2,1)S(1)}, u32[]{:S(2)}, u32[]{:S(2)}) async-start(bf16[80,4,1792]{2,1,0:T(4,128)(2,1)} %get-tuple-element.49), calls=%async_computation | async-start | bytes 2293760 | tf_op jit(solution)/shard_map/all_to_all | solution.py:313
  9.9 9.4 %conditional.3 = (f16[1552,128]{1,0:T(8,128)(2,1)S(1)}) conditional(s32[]{:T(128)} %bitcast.22, () %tuple.25, (s32[16]{0:T(128)S(1)}, bf16[96,1792]{1,0:T(8,128)(2,1)S(1)}, bf16[1792,8192]{1,0:T(8,128)(2,1)}) %tuple.26), branch_computations={%region_0.0_spmd, %region_1.3_spmd} | conditional | flops 1581488 | bytes 7479232 | solution.py:108
  9.9 0.1 fusion.23
  10.0 4.2 %branch_1_fun.4 = f32[16,96,128]{2,1,0:T(8,128)S(1)} custom-call(s32[4]{0:T(128)S(1)} %get-tuple-element.65.order_ref, bf16[96,1792]{1,0:T(8,128)(2,1)S(1)} %get-tuple-element.30.hidden_ref, bf16[1792,8192]{1,0:T(8,128)(2,1)} %get-tuple-element.32.down_ref), custom_call_target="tpu_custom_call" | custom-call | flops 1000 | bytes 1000 | tf_op jit(solution)/shard_map/cond/branch_1_fun/pallas_call | solution.py:61
  14.2 0.5 collective-permute-start.4
  14.7 4.2 %branch_1_fun.3 = f32[16,96,128]{2,1,0:T(8,128)S(1)} custom-call(s32[4]{0:T(128)S(1)} %get-tuple-element.66.order_ref, bf16[96,1792]{1,0:T(8,128)(2,1)S(1)} %get-tuple-element.30.hidden_ref, bf16[1792,8192]{1,0:T(8,128)(2,1)} %get-tuple-element.32.down_ref), custom_call_target="tpu_custom_call" | custom-call | flops 1000 | bytes 1000 | tf_op jit(solution)/shard_map/cond/branch_1_fun/pallas_call | solution.py:61
  18.9 0.0 collective-permute-done.4
  18.9 0.2 abs_reduce_fusion
  19.1 0.2 multiply_convert_fusion
  19.3 0.1 fusion.1
  19.4 1.7 %collective-permute-start.5 = (f16[1552,128]{1,0:T(8,128)(2,1)S(1)}, f16[1552,128]{1,0:T(8,128)(2,1)S(1)}, u32[]{:S(2)}, u32[]{:S(2)}) collective-permute-start(f16[1552,128]{1,0:T(8,128)(2,1)S(1)} %get-tuple-element.78), channel_id=1, source_target_pairs={{0,2},{1,3},{2,0},{3,1},{4,6},{5,7},{6,4},{7,5},{8,10},{9,11},{10,... | collective-permute-start | bytes 1191944 | tf_op jit(solution)/shard_map/ppermute | solution.py:24
  21.1 0.6 slice.52
  22.4 8.9 %conditional.4 = (f32[16,96,128]{2,1,0:T(8,128)S(1)}) conditional(s32[]{:T(128)} %bitcast.23, () %tuple.28, (s32[16]{0:T(128)S(1)}, bf16[96,1792]{1,0:T(8,128)(2,1)S(1)}, bf16[1792,8192]{1,0:T(8,128)(2,1)}) %tuple.29), branch_computations={%region_3.4_spmd, %region_4.5_spmd} | conditional | flops 197608 | bytes 5506136 | solution.py:119
  22.4 0.1 slice.36.order_ref
  22.5 6.4 %branch_1_fun.5 = (f32[16,96,128]{2,1,0:T(8,128)S(1)}, f32[16,96,128]{2,1,0:T(8,128)S(1)}) custom-call(s32[8]{0:T(128)S(1)} %slice.36.order_ref, bf16[96,1792]{1,0:T(8,128)(2,1)S(1)} %get-tuple-element.34.hidden_ref, bf16[1792,8192]{1,0:T(8,128)(2,1)} %get-tuple-element.35.down_ref), custom_call_target="tpu_custom_call" | custom-call | flops 1000 | bytes 1000 | tf_op jit(solution)/shard_map/cond/branch_1_fun/pallas_call | solution.py:61
  28.9 0.1 collective-permute-start
  29.0 2.2 %collective-permute-done = f32[16,96,128]{2,1,0:T(8,128)S(1)} collective-permute-done((f32[16,96,128]{2,1,0:T(8,128)S(1)}, f32[16,96,128]{2,1,0:T(8,128)S(1)}, u32[]{:S(2)}, u32[]{:S(2)}) %collective-permute-start) | collective-permute-done | bytes 786464 | tf_op jit(solution)/shard_map/cond/branch_1_fun/ppermute | solution.py:24
  31.2 0.1 add.39
  31.3 4.6 %collective-permute-done.5 = f16[1552,128]{1,0:T(8,128)(2,1)S(1)} collective-permute-done((f16[1552,128]{1,0:T(8,128)(2,1)S(1)}, f16[1552,128]{1,0:T(8,128)(2,1)S(1)}, u32[]{:S(2)}, u32[]{:S(2)}) %collective-permute-start.5) | collective-permute-done | bytes 397344 | tf_op jit(solution)/shard_map/ppermute | solution.py:24
  35.9 0.0 all-to-all-done.rows_ref
  35.9 4.5 %shard_map.65 = (bf16[80,4,512]{2,1,0:T(4,128)(2,1)}, s32[1]{0:T(128)}) custom-call(bf16[80,4,1792]{2,1,0:T(4,128)(2,1)S(1)} %all-to-all-done.rows_ref, bf16[64,8192]{1,0:T(8,128)(2,1)} %bitcast.43, bf16[64,28672]{1,0:T(8,128)(2,1)} %bitcast.40), custom_call_target="tpu_custom_call" | custom-call | tf_op jit(solution)/shard_map/pallas_call | solution.py:258
  40.4 5.9 %all-to-all-start.1 = ((bf16[80,4,512]{2,1,0:T(4,128)(2,1)}), bf16[80,4,512]{2,1,0:T(4,128)(2,1)S(1)}, u32[]{:S(2)}, u32[]{:S(2)}) async-start(bf16[80,4,512]{2,1,0:T(4,128)(2,1)} %get-tuple-element.57), calls=%async_computation.1 | async-start | bytes 655360 | tf_op jit(solution)/shard_map/all_to_all | solution.py:319
  47.0 17.7 %conditional.5 = (f32[4,96,128]{2,1,0:T(8,128)S(1)}) conditional(s32[]{:T(128)} %bitcast.28, () %tuple.31, (f16[1552,128]{1,0:T(8,128)(2,1)S(1)}, f32[16,96,128]{2,1,0:T(8,128)S(1)}) %tuple.32), branch_computations={%region_5.6_spmd, %region_6.10_spmd} | conditional | flops 2085408 | bytes 7345664 | solution.py:141
  47.0 0.1 slice.37
  47.1 0.2 fusion.2
  47.3 0.2 abs_reduce_fusion.3
  47.5 0.1 multiply_convert_fusion.3
  47.7 2.9 %collective-permute-start.2 = (f16[400,128]{1,0:T(8,128)(2,1)S(1)}, f16[400,128]{1,0:T(8,128)(2,1)S(1)}, u32[]{:S(2)}, u32[]{:S(2)}) collective-permute-start(f16[400,128]{1,0:T(8,128)(2,1)S(1)} %fusion.9), channel_id=1, source_target_pairs={{0,8},{1,9},{2,10},{3,11},{4,12},{5,13},{6,14},{7,15},{8,0},{9,1},... | collective-permute-start | bytes 307208 | tf_op jit(solution)/shard_map/cond/branch_1_fun/ppermute | solution.py:24
  50.6 1.5 %collective-permute-start.1 = (f16[400,128]{1,0:T(8,128)(2,1)S(1)}, f16[400,128]{1,0:T(8,128)(2,1)S(1)}, u32[]{:S(2)}, u32[]{:S(2)}) collective-permute-start(f16[400,128]{1,0:T(8,128)(2,1)S(1)} %fusion.8), channel_id=1, source_target_pairs={{0,4},{1,5},{2,6},{3,7},{4,0},{5,1},{6,2},{7,3},{8,12},{9,13},{10,... | collective-permute-start | bytes 307208 | tf_op jit(solution)/shard_map/cond/branch_1_fun/ppermute | solution.py:24
  52.1 0.2 collective-permute-start.3
  52.3 12.2 %collective-permute-done.2 = f16[400,128]{1,0:T(8,128)(2,1)S(1)} collective-permute-done((f16[400,128]{1,0:T(8,128)(2,1)S(1)}, f16[400,128]{1,0:T(8,128)(2,1)S(1)}, u32[]{:S(2)}, u32[]{:S(2)}) %collective-permute-start.2) | collective-permute-done | bytes 102432 | tf_op jit(solution)/shard_map/cond/branch_1_fun/ppermute | solution.py:24
  64.5 0.0 collective-permute-done.1
  64.5 0.0 collective-permute-done.3
  64.6 0.1 fusion.7
  64.7 0.0 all-to-all-done.1.rows_ref
  64.8 0.9 %shard_map.66 = bf16[96,512]{1,0:T(8,128)(2,1)} custom-call(f32[4,96,128]{2,1,0:T(8,128)S(1)} %get-tuple-element.80.base_ref, bf16[320,96]{1,0:T(8,128)(2,1)S(1)} %get-tuple-element.56.pick_ref, bf16[80,4,512]{2,1,0:T(4,128)(2,1)S(1)} %all-to-all-done.1.rows_ref), custom_call_target="tpu_custom_call" | custom-call | tf_op jit(solution)/shard_map/pallas_call | solution.py:292
  (13 shorter events, 0.2 us)
Async XLA Ops:
  2.5 33.4 %all-to-all-start = ((bf16[80,4,1792]{2,1,0:T(4,128)(2,1)}), bf16[80,4,1792]{2,1,0:T(4,128)(2,1)S(1)}, u32[]{:S(2)}, u32[]{:S(2)}) async-start(bf16[80,4,1792]{2,1,0:T(4,128)(2,1)} %get-tuple-element.49), calls=%async_computation | async-start | bytes 2293760 | tf_op jit(solution)/shard_map/all_to_all | solution.py:313
  14.2 4.7 %collective-permute-start.4 = (f32[16,96,128]{2,1,0:T(8,128)S(1)}, f32[16,96,128]{2,1,0:T(8,128)S(1)}, u32[]{:S(2)}, u32[]{:S(2)}) collective-permute-start(f32[16,96,128]{2,1,0:T(8,128)S(1)} %branch_1_fun.4), channel_id=1, source_target_pairs={{0,1},{1,0},{2,3},{3,2},{4,5},{5,4},{6,7},{7,6},{8,9},{9,8},{10,11... | collective-permute-start | bytes 2359304 | tf_op jit(solution)/shard_map/cond/branch_1_fun/ppermute | solution.py:24
  19.4 16.5 %collective-permute-start.5 = (f16[1552,128]{1,0:T(8,128)(2,1)S(1)}, f16[1552,128]{1,0:T(8,128)(2,1)S(1)}, u32[]{:S(2)}, u32[]{:S(2)}) collective-permute-start(f16[1552,128]{1,0:T(8,128)(2,1)S(1)} %get-tuple-element.78), channel_id=1, source_target_pairs={{0,2},{1,3},{2,0},{3,1},{4,6},{5,7},{6,4},{7,5},{8,10},{9,11},{10,... | collective-permute-start | bytes 1191944 | tf_op jit(solution)/shard_map/ppermute | solution.py:24
  28.9 2.4 %collective-permute-start = (f32[16,96,128]{2,1,0:T(8,128)S(1)}, f32[16,96,128]{2,1,0:T(8,128)S(1)}, u32[]{:S(2)}, u32[]{:S(2)}) collective-permute-start(f32[16,96,128]{2,1,0:T(8,128)S(1)} %get-tuple-element.37), channel_id=1, source_target_pairs={{0,1},{1,0},{2,3},{3,2},{4,5},{5,4},{6,7},{7,6},{8,9},{9,8},{10,11... | collective-permute-start | bytes 2359304 | tf_op jit(solution)/shard_map/cond/branch_1_fun/ppermute | solution.py:24
  40.4 24.3 %all-to-all-start.1 = ((bf16[80,4,512]{2,1,0:T(4,128)(2,1)}), bf16[80,4,512]{2,1,0:T(4,128)(2,1)S(1)}, u32[]{:S(2)}, u32[]{:S(2)}) async-start(bf16[80,4,512]{2,1,0:T(4,128)(2,1)} %get-tuple-element.57), calls=%async_computation.1 | async-start | bytes 655360 | tf_op jit(solution)/shard_map/all_to_all | solution.py:319
  47.7 16.8 %collective-permute-start.2 = (f16[400,128]{1,0:T(8,128)(2,1)S(1)}, f16[400,128]{1,0:T(8,128)(2,1)S(1)}, u32[]{:S(2)}, u32[]{:S(2)}) collective-permute-start(f16[400,128]{1,0:T(8,128)(2,1)S(1)} %fusion.9), channel_id=1, source_target_pairs={{0,8},{1,9},{2,10},{3,11},{4,12},{5,13},{6,14},{7,15},{8,0},{9,1},... | collective-permute-start | bytes 307208 | tf_op jit(solution)/shard_map/cond/branch_1_fun/ppermute | solution.py:24
  50.6 13.9 %collective-permute-start.1 = (f16[400,128]{1,0:T(8,128)(2,1)S(1)}, f16[400,128]{1,0:T(8,128)(2,1)S(1)}, u32[]{:S(2)}, u32[]{:S(2)}) collective-permute-start(f16[400,128]{1,0:T(8,128)(2,1)S(1)} %fusion.8), channel_id=1, source_target_pairs={{0,4},{1,5},{2,6},{3,7},{4,0},{5,1},{6,2},{7,3},{8,12},{9,13},{10,... | collective-permute-start | bytes 307208 | tf_op jit(solution)/shard_map/cond/branch_1_fun/ppermute | solution.py:24
  52.1 12.4 %collective-permute-start.3 = (f16[400,128]{1,0:T(8,128)(2,1)S(1)}, f16[400,128]{1,0:T(8,128)(2,1)S(1)}, u32[]{:S(2)}, u32[]{:S(2)}) collective-permute-start(f16[400,128]{1,0:T(8,128)(2,1)S(1)} %fusion.10), channel_id=1, source_target_pairs={{0,12},{1,13},{2,14},{3,15},{4,8},{5,9},{6,10},{7,11},{8,4},{9,5},... | collective-permute-start | bytes 307208 | tf_op jit(solution)/shard_map/cond/branch_1_fun/ppermute | solution.py:24

commit v20 on v17

--- a/solution.py
+++ b/solution.py
@@ -169,13 +169,16 @@
     copies[1].wait()
     adapter = adapter_ref[...]
     first = jnp.sum((adapter < ids).astype(jnp.int32), axis=1, keepdims=True)
-    shift = jnp.where(adapter == ids, slots * (blocks * BLOCK) - first, 0)
-    place = jnp.sum(shift, axis=0, keepdims=True) + lax.broadcasted_iota(jnp.int32, (1, rows), 1)
-    spots = lax.broadcasted_iota(jnp.int32, (group * blocks * BLOCK, rows), 0)
-    pick = jnp.where(spots == place, 1.0, 0.0).astype(jnp.bfloat16)
+    slot = jnp.sum(jnp.where(adapter == ids, slots, 0), axis=0, keepdims=True)
+    first = jnp.sum(jnp.where(adapter == ids, first, 0), axis=0, keepdims=True)
+    index = lax.broadcasted_iota(jnp.int32, (1, rows), 1) - first
+    held = blocks * BLOCK
+    rank = lax.rem(slot, PLANE) * (group // PLANE) + lax.div(slot, PLANE)
+    spots = lax.broadcasted_iota(jnp.int32, (group * held, rows), 0)
+    pick = jnp.where(spots == rank * held + index, 1.0, 0.0).astype(jnp.bfloat16)
     for k in range(PLANE):
         line = lax.broadcasted_iota(jnp.int32, (HELD, rows), 0)
-        mine = (line + (me_ref[0] ^ k) * (blocks * BLOCK) == place) & (line < blocks * BLOCK)
+        mine = (slot == me_ref[0] ^ k) & (index == line)
         pick_ref[k * HELD : (k + 1) * HELD] = jnp.where(mine, 1.0, 0.0).astype(jnp.bfloat16)
     copies[2].wait()
     packed = jnp.dot(pick, hidden_ref[...], preferred_element_type=jnp.float32)
@@ -210,7 +213,7 @@
     )(me.reshape(1), in_hbm(adapter_holder_slot), in_hbm(adapter_of_row.reshape(1, rows)), in_hbm(hidden))
 
 
-def adapter_kernel(parts, me_ref, rows_ref, expand_hbm, shrink_hbm, *refs):
+def adapter_kernel(parts, ranks, me_ref, rows_ref, expand_hbm, shrink_hbm, *refs):
     out_refs = refs[:PLANE]
     shrink_ref, expand_ref, total_ref, sems, expand_sem = refs[PLANE:]
     me = me_ref[0]
@@ -219,7 +222,9 @@
 
     def copy(source):
         return pltpu.make_async_copy(
-            shrink_hbm.at[:, pl.ds(source * depth, depth)], shrink_ref.at[source], sems.at[source]
+            shrink_hbm.at[:, pl.ds(ranks[source] * depth, depth)],
+            shrink_ref.at[source],
+            sems.at[source],
         )
 
     for source in range(group):
@@ -248,7 +253,7 @@
                 out_refs[k][line * parts + part] = piece[:, part * LANES : (part + 1) * LANES]
 
 
-def adapter_output(gathered, shrink, expand, group, me):
+def adapter_output(gathered, shrink, expand, group, me, ranks):
     rank = shrink.shape[0]
     model_width = expand.shape[1]
     depth = gathered.shape[2]
@@ -256,7 +261,7 @@
     held = (model_width // PLANE // LANES, HELD, LANES)
     vmem = pl.BlockSpec(memory_space=pltpu.VMEM)
     return pl.pallas_call(
-        functools.partial(adapter_kernel, parts),
+        functools.partial(adapter_kernel, parts, ranks),
         out_shape=[jax.ShapeDtypeStruct(held, jnp.bfloat16)] * PLANE,
         in_specs=[
             pl.BlockSpec(memory_space=pltpu.SMEM),
@@ -309,15 +314,19 @@
     width = down_matrix.shape[1] // group
     quads = list(range(0, group, 4))
     orders = [q + k for k in (3, 2, 1, 0) for q in quads]
+    lines = group // PLANE
+    ranks = [PLANE * (i % lines) + i // lines for i in range(group)]
     packed, pick, order, kept_hidden = pack_rows(
         hidden, adapter_of_row, adapter_holder_slot, me, orders
     )
-    gathered = lax.all_to_all(packed, "tp", split_axis=0, concat_axis=0, tiled=True)
+    gathered = lax.all_to_all(
+        packed, "tp", split_axis=0, concat_axis=0, axis_index_groups=[ranks], tiled=True
+    )
     shrink = jnp.swapaxes(shrink_matrices, 1, 2)[0]
     kept, pair_in = pair_sums(kept_hidden, down_matrix, group, order, width)
     gathered, _ = lax.optimization_barrier((gathered, kept))
     expand = jnp.swapaxes(expand_matrices, 1, 2)[0]
-    outs = adapter_output(gathered, shrink, expand, group, me)
+    outs = adapter_output(gathered, shrink, expand, group, me, ranks)
     arrived = [outs[0]] + [xor_permute(outs[k], group, k) for k in range(1, PLANE)]
     pair = kept + unpack_scaled(pair_in, rows)
     merged = merge_adapters(pair, pick, arrived)

time: 61.2 us -> 61.3 us (level)
  waiting for transfers between devices: 18.6 us -> 19.7 us
  starting transfers between devices: 17.2 us -> 16.2 us
    all_to_all x1, waiting for transfers between devices: 0.01 us -> 4.62 us  [shards_by_blocks(): lax.all_to_all(packed, 'tp', split_axis=0, concat_axis=0, axis_index_grou...]
    ppermute x9, waiting for transfers between devices: 18.6 us -> 15 us  [xor_permute(): return lax.ppermute(value, 'tp', [(i, i ^ offset) for i in range(group)])]
    ppermute x9, starting transfers between devices: 9.85 us -> 8.86 us  [xor_permute(): return lax.ppermute(value, 'tp', [(i, i ^ offset) for i in range(group)])]
  transfers between devices with their start and end apart: 10 -> 10, of which waited for: 6 -> 7; matrix products, arithmetic and copies ran while one was open for 3% -> 3% of each run, Pallas kernels for 24% -> 24%
where the time goes in v20:
time: 61.3 us; the launch traced here: 61.1 us
  Pallas kernels  21.4 us (35%)
  waiting for transfers between devices  19.7 us (32%)
  starting transfers between devices  16.2 us (26%)
  other arithmetic  1.95 us (3%)
  local copies, waits for them, and re-layouts  0.9 us (1%)
  between operations  0.83 us (1%)
    ppermute x9, waiting for transfers between devices, xor_permute(): return lax.ppermute(value, 'tp', [(i, i ^ offset) for i in range(group)])  15 us
    pallas_call x3, Pallas kernels, column_blocks(): pl.pallas_call(functools.partial(column_blocks_kernel, groups), out_shape...  14.8 us
    ppermute x9, starting transfers between devices, xor_permute(): return lax.ppermute(value, 'tp', [(i, i ^ offset) for i in range(group)])  8.86 us
    all_to_all x1, starting transfers between devices, shards_by_blocks(): lax.all_to_all(packed, 'tp', split_axis=0, concat_axis=0, axis_index_grou...  7.37 us
    all_to_all x1, waiting for transfers between devices, shards_by_blocks(): lax.all_to_all(packed, 'tp', split_axis=0, concat_axis=0, axis_index_grou...  4.62 us
    pallas_call x1, Pallas kernels, adapter_output(): pl.pallas_call(functools.partial(adapter_kernel, parts, ranks), out_shape...  3.85 us
    pallas_call x1, Pallas kernels, pack_rows(): pl.pallas_call(functools.partial(pack_kernel, blocks, orders), out_shape=...  2.49 us
  transfers between devices with their start and end apart: 10, of which 7 were waited for; matrix products, arithmetic and copies ran while one was open for 3% of the time, Pallas kernels for 24%

profile of v20, /device:TPU:0, one launch (start us, length us, event | category | flops | bytes accessed | tf_op | source)
XLA Modules:
  0.0 61.1 jit_solution(16367210469442520691)
XLA Ops:
  0.0 2.5 %shard_map.64 = (bf16[80,4,1792]{2,1,0:T(4,128)(2,1)}, bf16[96,96]{1,0:T(8,128)(2,1)S(1)}, s32[16]{0:T(128)S(1)}, bf16[96,1792]{1,0:T(8,128)(2,1)S(1)}) custom-call(s32[1]{0:T(128)} %bitcast.2.me_ref, s32[16]{0:T(128)} %slot_hbm.1, s32[1,96]{1,0:T(1,128)} %bitcast.56, bf16[96,1792]{1,0:T(8,128)(2,1)} %hidden_hbm.1), custom_call_target="tpu_custom_call" | custom-call | tf_op jit(solution)/shard_map/pallas_call | solution.py:196
  2.5 7.4 %all-to-all-start = ((bf16[80,4,1792]{2,1,0:T(4,128)(2,1)}), bf16[80,4,1792]{2,1,0:T(4,128)(2,1)S(1)}, u32[]{:S(2)}, u32[]{:S(2)}) async-start(bf16[80,4,1792]{2,1,0:T(4,128)(2,1)} %get-tuple-element.45), calls=%async_computation | async-start | bytes 2293760 | tf_op jit(solution)/shard_map/all_to_all | solution.py:322
  9.9 9.5 %conditional.2 = (f16[1552,128]{1,0:T(8,128)(2,1)S(1)}) conditional(s32[]{:T(128)} %bitcast.4, () %tuple.19, (s32[16]{0:T(128)S(1)}, bf16[96,1792]{1,0:T(8,128)(2,1)S(1)}, bf16[1792,8192]{1,0:T(8,128)(2,1)}) %tuple.20), branch_computations={%region_0.0_spmd, %region_1.3_spmd} | conditional | flops 1581488 | bytes 7479232 | solution.py:109
  9.9 0.1 fusion.29
  10.0 4.2 %branch_1_fun.4 = f32[16,96,128]{2,1,0:T(8,128)S(1)} custom-call(s32[4]{0:T(128)S(1)} %get-tuple-element.58.order_ref, bf16[96,1792]{1,0:T(8,128)(2,1)S(1)} %get-tuple-element.24.hidden_ref, bf16[1792,8192]{1,0:T(8,128)(2,1)} %get-tuple-element.25.down_ref), custom_call_target="tpu_custom_call" | custom-call | flops 1000 | bytes 1000 | tf_op jit(solution)/shard_map/cond/branch_1_fun/pallas_call | solution.py:62
  14.2 0.5 collective-permute-start.1
  14.7 4.2 %branch_1_fun.3 = f32[16,96,128]{2,1,0:T(8,128)S(1)} custom-call(s32[4]{0:T(128)S(1)} %get-tuple-element.59.order_ref, bf16[96,1792]{1,0:T(8,128)(2,1)S(1)} %get-tuple-element.24.hidden_ref, bf16[1792,8192]{1,0:T(8,128)(2,1)} %get-tuple-element.25.down_ref), custom_call_target="tpu_custom_call" | custom-call | flops 1000 | bytes 1000 | tf_op jit(solution)/shard_map/cond/branch_1_fun/pallas_call | solution.py:62
  18.9 0.0 collective-permute-done.1
  18.9 0.2 abs_reduce_fusion
  19.1 0.2 multiply_convert_fusion
  19.3 0.1 fusion.1
  19.4 1.7 %collective-permute-start.2 = (f16[1552,128]{1,0:T(8,128)(2,1)S(1)}, f16[1552,128]{1,0:T(8,128)(2,1)S(1)}, u32[]{:S(2)}, u32[]{:S(2)}) collective-permute-start(f16[1552,128]{1,0:T(8,128)(2,1)S(1)} %get-tuple-element.71), channel_id=1, source_target_pairs={{0,2},{1,3},{2,0},{3,1},{4,6},{5,7},{6,4},{7,5},{8,10},{9,11},{10,... | collective-permute-start | bytes 1191944 | tf_op jit(solution)/shard_map/ppermute | solution.py:25
  21.1 0.6 slice.52
  22.4 8.9 %conditional.3 = (f32[16,96,128]{2,1,0:T(8,128)S(1)}) conditional(s32[]{:T(128)} %bitcast.5, () %tuple.22, (s32[16]{0:T(128)S(1)}, bf16[96,1792]{1,0:T(8,128)(2,1)S(1)}, bf16[1792,8192]{1,0:T(8,128)(2,1)}) %tuple.23), branch_computations={%region_3.4_spmd, %region_4.5_spmd} | conditional | flops 197608 | bytes 5506136 | solution.py:120
  22.4 0.1 slice.36.order_ref
  22.5 6.4 %branch_1_fun.5 = (f32[16,96,128]{2,1,0:T(8,128)S(1)}, f32[16,96,128]{2,1,0:T(8,128)S(1)}) custom-call(s32[8]{0:T(128)S(1)} %slice.36.order_ref, bf16[96,1792]{1,0:T(8,128)(2,1)S(1)} %get-tuple-element.27.hidden_ref, bf16[1792,8192]{1,0:T(8,128)(2,1)} %get-tuple-element.28.down_ref), custom_call_target="tpu_custom_call" | custom-call | flops 1000 | bytes 1000 | tf_op jit(solution)/shard_map/cond/branch_1_fun/pallas_call | solution.py:62
  28.9 0.1 collective-permute-start
  29.0 2.2 %collective-permute-done = f32[16,96,128]{2,1,0:T(8,128)S(1)} collective-permute-done((f32[16,96,128]{2,1,0:T(8,128)S(1)}, f32[16,96,128]{2,1,0:T(8,128)S(1)}, u32[]{:S(2)}, u32[]{:S(2)}) %collective-permute-start) | collective-permute-done | bytes 786464 | tf_op jit(solution)/shard_map/cond/branch_1_fun/ppermute | solution.py:25
  31.2 0.1 add.39
  31.3 2.9 %collective-permute-done.2 = f16[1552,128]{1,0:T(8,128)(2,1)S(1)} collective-permute-done((f16[1552,128]{1,0:T(8,128)(2,1)S(1)}, f16[1552,128]{1,0:T(8,128)(2,1)S(1)}, u32[]{:S(2)}, u32[]{:S(2)}) %collective-permute-start.2) | collective-permute-done | bytes 397344 | tf_op jit(solution)/shard_map/ppermute | solution.py:25
  34.3 0.1 slice.65
  34.4 4.6 %all-to-all-done.rows_ref = bf16[80,4,1792]{2,1,0:T(4,128)(2,1)S(1)} async-done(((bf16[80,4,1792]{2,1,0:T(4,128)(2,1)}), bf16[80,4,1792]{2,1,0:T(4,128)(2,1)S(1)}, u32[]{:S(2)}, u32[]{:S(2)}) %all-to-all-start) | async-done | bytes 1146912 | tf_op jit(solution)/shard_map/all_to_all | solution.py:322
  39.0 3.9 %shard_map.65 = (bf16[16,24,128]{2,1,0:T(8,128)(2,1)S(1)}, bf16[16,24,128]{2,1,0:T(8,128)(2,1)S(1)}, bf16[16,24,128]{2,1,0:T(8,128)(2,1)S(1)}, bf16[16,24,128]{2,1,0:T(8,128)(2,1)S(1)}) custom-call(s32[1]{0:T(128)} %bitcast.2.me_ref, bf16[80,4,1792]{2,1,0:T(4,128)(2,1)S(1)} %all-to-all-done.rows_ref, bf16[64,8192]{1,0:T(8,128)(2,1)} %bitcast.48, ...), custom_call_target="tpu_custom_call" | custom-call | tf_op jit(solution)/shard_map/pallas_call | solution.py:263
  42.8 0.1 collective-permute-start.3
  42.9 0.8 %collective-permute-start.4 = (bf16[16,24,128]{2,1,0:T(8,128)(2,1)S(1)}, bf16[16,24,128]{2,1,0:T(8,128)(2,1)S(1)}, u32[]{:S(2)}, u32[]{:S(2)}) collective-permute-start(bf16[16,24,128]{2,1,0:T(8,128)(2,1)S(1)} %get-tuple-element.49), channel_id=1, source_target_pairs={{0,2},{1,3},{2,0},{3,1},{4,6},{5,7},{6,4},{7,5},{8,10},{9,11},{10,... | collective-permute-start | bytes 294920 | tf_op jit(solution)/shard_map/ppermute | solution.py:25
  43.8 1.0 %collective-permute-start.5 = (bf16[16,24,128]{2,1,0:T(8,128)(2,1)S(1)}, bf16[16,24,128]{2,1,0:T(8,128)(2,1)S(1)}, u32[]{:S(2)}, u32[]{:S(2)}) collective-permute-start(bf16[16,24,128]{2,1,0:T(8,128)(2,1)S(1)} %get-tuple-element.50), channel_id=1, source_target_pairs={{0,3},{1,2},{2,1},{3,0},{4,7},{5,6},{6,5},{7,4},{8,11},{9,10},{10,... | collective-permute-start | bytes 294920 | tf_op jit(solution)/shard_map/ppermute | solution.py:25
  44.8 0.2 fusion.2.pair_ref
  45.0 0.0 collective-permute-done.3.refs_1_
  45.0 3.6 %collective-permute-done.4.refs_2_ = bf16[16,24,128]{2,1,0:T(8,128)(2,1)S(1)} collective-permute-done((bf16[16,24,128]{2,1,0:T(8,128)(2,1)S(1)}, bf16[16,24,128]{2,1,0:T(8,128)(2,1)S(1)}, u32[]{:S(2)}, u32[]{:S(2)}) %collective-permute-start.4) | collective-permute-done | bytes 98336 | tf_op jit(solution)/shard_map/ppermute | solution.py:25
  48.6 1.2 %collective-permute-done.5.refs_3_ = bf16[16,24,128]{2,1,0:T(8,128)(2,1)S(1)} collective-permute-done((bf16[16,24,128]{2,1,0:T(8,128)(2,1)S(1)}, bf16[16,24,128]{2,1,0:T(8,128)(2,1)S(1)}, u32[]{:S(2)}, u32[]{:S(2)}) %collective-permute-start.5) | collective-permute-done | bytes 98336 | tf_op jit(solution)/shard_map/ppermute | solution.py:25
  49.8 0.3 shard_map.66
  50.1 0.2 abs_reduce_fusion.3
  50.3 0.1 multiply_convert_fusion.3
  50.4 0.1 collective-permute-start.7
  50.6 1.5 %collective-permute-start.6 = (f16[400,128]{1,0:T(8,128)(2,1)S(1)}, f16[400,128]{1,0:T(8,128)(2,1)S(1)}, u32[]{:S(2)}, u32[]{:S(2)}) collective-permute-start(f16[400,128]{1,0:T(8,128)(2,1)S(1)} %fusion.9), channel_id=1, source_target_pairs={{0,4},{1,5},{2,6},{3,7},{4,0},{5,1},{6,2},{7,3},{8,12},{9,13},{10,... | collective-permute-start | bytes 307208 | tf_op jit(solution)/shard_map/ppermute | solution.py:25
  52.1 3.0 %collective-permute-start.8 = (f16[400,128]{1,0:T(8,128)(2,1)S(1)}, f16[400,128]{1,0:T(8,128)(2,1)S(1)}, u32[]{:S(2)}, u32[]{:S(2)}) collective-permute-start(f16[400,128]{1,0:T(8,128)(2,1)S(1)} %fusion.11), channel_id=1, source_target_pairs={{0,12},{1,13},{2,14},{3,15},{4,8},{5,9},{6,10},{7,11},{8,4},{9,5},... | collective-permute-start | bytes 307208 | tf_op jit(solution)/shard_map/ppermute | solution.py:25
  55.1 3.7 %collective-permute-done.7 = f16[400,128]{1,0:T(8,128)(2,1)S(1)} collective-permute-done((f16[400,128]{1,0:T(8,128)(2,1)S(1)}, f16[400,128]{1,0:T(8,128)(2,1)S(1)}, u32[]{:S(2)}, u32[]{:S(2)}) %collective-permute-start.7) | collective-permute-done | bytes 102432 | tf_op jit(solution)/shard_map/ppermute | solution.py:25
  58.8 0.0 collective-permute-done.6
  58.9 1.4 %collective-permute-done.8 = f16[400,128]{1,0:T(8,128)(2,1)S(1)} collective-permute-done((f16[400,128]{1,0:T(8,128)(2,1)S(1)}, f16[400,128]{1,0:T(8,128)(2,1)S(1)}, u32[]{:S(2)}, u32[]{:S(2)}) %collective-permute-start.8) | collective-permute-done | bytes 102432 | tf_op jit(solution)/shard_map/ppermute | solution.py:25
  60.3 0.8 %copy_bitcast_fusion = bf16[96,512]{1,0:T(8,128)(2,1)} fusion(f16[4,96,128]{2,1,0:T(8,128)(2,1)S(1)} %bitcast.54, f16[4,96,128]{2,1,0:T(8,128)(2,1)S(1)} %bitcast.51, f16[4,96,128]{2,1,0:T(8,128)(2,1)S(1)} %bitcast.52, f32[16,96,128]{2,1,0:T(8,128)S(1)} %shard_map.66, f32[96]{0:T(128)S(1)} %fusion.16, f32[96]{0:T(128)S(1)} %fusion.20, f32[96]{0:T(128)S(1)} %fusion.24), kind=kLoop, calls=%fused_computation.31 | loop fusion | flops 491520 | bytes 591360 | tf_op jit(solution)/shard_map/convert_element_type | solution.py:333
  (13 shorter events, 0.2 us)
Async XLA Ops:
  2.5 36.5 %all-to-all-start = ((bf16[80,4,1792]{2,1,0:T(4,128)(2,1)}), bf16[80,4,1792]{2,1,0:T(4,128)(2,1)S(1)}, u32[]{:S(2)}, u32[]{:S(2)}) async-start(bf16[80,4,1792]{2,1,0:T(4,128)(2,1)} %get-tuple-element.45), calls=%async_computation | async-start | bytes 2293760 | tf_op jit(solution)/shard_map/all_to_all | solution.py:322
  14.2 4.7 %collective-permute-start.1 = (f32[16,96,128]{2,1,0:T(8,128)S(1)}, f32[16,96,128]{2,1,0:T(8,128)S(1)}, u32[]{:S(2)}, u32[]{:S(2)}) collective-permute-start(f32[16,96,128]{2,1,0:T(8,128)S(1)} %branch_1_fun.4), channel_id=1, source_target_pairs={{0,1},{1,0},{2,3},{3,2},{4,5},{5,4},{6,7},{7,6},{8,9},{9,8},{10,11... | collective-permute-start | bytes 2359304 | tf_op jit(solution)/shard_map/cond/branch_1_fun/ppermute | solution.py:25
  19.4 14.9 %collective-permute-start.2 = (f16[1552,128]{1,0:T(8,128)(2,1)S(1)}, f16[1552,128]{1,0:T(8,128)(2,1)S(1)}, u32[]{:S(2)}, u32[]{:S(2)}) collective-permute-start(f16[1552,128]{1,0:T(8,128)(2,1)S(1)} %get-tuple-element.71), channel_id=1, source_target_pairs={{0,2},{1,3},{2,0},{3,1},{4,6},{5,7},{6,4},{7,5},{8,10},{9,11},{10,... | collective-permute-start | bytes 1191944 | tf_op jit(solution)/shard_map/ppermute | solution.py:25
  28.9 2.4 %collective-permute-start = (f32[16,96,128]{2,1,0:T(8,128)S(1)}, f32[16,96,128]{2,1,0:T(8,128)S(1)}, u32[]{:S(2)}, u32[]{:S(2)}) collective-permute-start(f32[16,96,128]{2,1,0:T(8,128)S(1)} %get-tuple-element.30), channel_id=1, source_target_pairs={{0,1},{1,0},{2,3},{3,2},{4,5},{5,4},{6,7},{7,6},{8,9},{9,8},{10,11... | collective-permute-start | bytes 2359304 | tf_op jit(solution)/shard_map/cond/branch_1_fun/ppermute | solution.py:25
  42.8 2.1 %collective-permute-start.3 = (bf16[16,24,128]{2,1,0:T(8,128)(2,1)S(1)}, bf16[16,24,128]{2,1,0:T(8,128)(2,1)S(1)}, u32[]{:S(2)}, u32[]{:S(2)}) collective-permute-start(bf16[16,24,128]{2,1,0:T(8,128)(2,1)S(1)} %get-tuple-element.48), channel_id=1, source_target_pairs={{0,1},{1,0},{2,3},{3,2},{4,5},{5,4},{6,7},{7,6},{8,9},{9,8},{10,11... | collective-permute-start | bytes 294920 | tf_op jit(solution)/shard_map/ppermute | solution.py:25
  42.9 5.7 %collective-permute-start.4 = (bf16[16,24,128]{2,1,0:T(8,128)(2,1)S(1)}, bf16[16,24,128]{2,1,0:T(8,128)(2,1)S(1)}, u32[]{:S(2)}, u32[]{:S(2)}) collective-permute-start(bf16[16,24,128]{2,1,0:T(8,128)(2,1)S(1)} %get-tuple-element.49), channel_id=1, source_target_pairs={{0,2},{1,3},{2,0},{3,1},{4,6},{5,7},{6,4},{7,5},{8,10},{9,11},{10,... | collective-permute-start | bytes 294920 | tf_op jit(solution)/shard_map/ppermute | solution.py:25
  43.8 6.0 %collective-permute-start.5 = (bf16[16,24,128]{2,1,0:T(8,128)(2,1)S(1)}, bf16[16,24,128]{2,1,0:T(8,128)(2,1)S(1)}, u32[]{:S(2)}, u32[]{:S(2)}) collective-permute-start(bf16[16,24,128]{2,1,0:T(8,128)(2,1)S(1)} %get-tuple-element.50), channel_id=1, source_target_pairs={{0,3},{1,2},{2,1},{3,0},{4,7},{5,6},{6,5},{7,4},{8,11},{9,10},{10,... | collective-permute-start | bytes 294920 | tf_op jit(solution)/shard_map/ppermute | solution.py:25
  50.4 8.3 %collective-permute-start.7 = (f16[400,128]{1,0:T(8,128)(2,1)S(1)}, f16[400,128]{1,0:T(8,128)(2,1)S(1)}, u32[]{:S(2)}, u32[]{:S(2)}) collective-permute-start(f16[400,128]{1,0:T(8,128)(2,1)S(1)} %fusion.10), channel_id=1, source_target_pairs={{0,8},{1,9},{2,10},{3,11},{4,12},{5,13},{6,14},{7,15},{8,0},{9,1},... | collective-permute-start | bytes 307208 | tf_op jit(solution)/shard_map/ppermute | solution.py:25
  50.6 8.2 %collective-permute-start.6 = (f16[400,128]{1,0:T(8,128)(2,1)S(1)}, f16[400,128]{1,0:T(8,128)(2,1)S(1)}, u32[]{:S(2)}, u32[]{:S(2)}) collective-permute-start(f16[400,128]{1,0:T(8,128)(2,1)S(1)} %fusion.9), channel_id=1, source_target_pairs={{0,4},{1,5},{2,6},{3,7},{4,0},{5,1},{6,2},{7,3},{8,12},{9,13},{10,... | collective-permute-start | bytes 307208 | tf_op jit(solution)/shard_map/ppermute | solution.py:25
  52.1 8.2 %collective-permute-start.8 = (f16[400,128]{1,0:T(8,128)(2,1)S(1)}, f16[400,128]{1,0:T(8,128)(2,1)S(1)}, u32[]{:S(2)}, u32[]{:S(2)}) collective-permute-start(f16[400,128]{1,0:T(8,128)(2,1)S(1)} %fusion.11), channel_id=1, source_target_pairs={{0,12},{1,13},{2,14},{3,15},{4,8},{5,9},{6,10},{7,11},{8,4},{9,5},... | collective-permute-start | bytes 307208 | tf_op jit(solution)/shard_map/ppermute | solution.py:25

commit v21 on v17

--- a/solution.py
+++ b/solution.py
@@ -1,4 +1,5 @@
 import functools
+import math
 
 import jax
 import jax.numpy as jnp
@@ -210,10 +211,7 @@
     )(me.reshape(1), in_hbm(adapter_holder_slot), in_hbm(adapter_of_row.reshape(1, rows)), in_hbm(hidden))
 
 
-def adapter_kernel(parts, me_ref, rows_ref, expand_hbm, shrink_hbm, *refs):
-    out_refs = refs[:PLANE]
-    shrink_ref, expand_ref, total_ref, sems, expand_sem = refs[PLANE:]
-    me = me_ref[0]
+def rank_kernel(rows_ref, shrink_hbm, out_ref, shrink_ref, total_ref, sems):
     group, _, depth = shrink_ref.shape
     blocks = MOST // BLOCK
 
@@ -224,9 +222,7 @@
 
     for source in range(group):
         copy(source).start()
-    expand_copy = pltpu.make_async_copy(expand_hbm, expand_ref, expand_sem)
-    expand_copy.start()
-    total = jnp.zeros((MOST, total_ref.shape[1]), jnp.float32)
+    total = jnp.zeros((MOST, shrink_ref.shape[1]), jnp.float32)
     for source in range(group):
         copy(source).wait()
         own = rows_ref[source * blocks : (source + 1) * blocks].reshape(MOST, depth)
@@ -235,69 +231,97 @@
         )
     total_ref[...] = jnp.zeros_like(total_ref)
     total_ref[:MOST] = total
-    rank_rows = total_ref[...].astype(jnp.bfloat16)
-    expand_copy.wait()
-    width = parts * LANES
-    for k in range(PLANE):
-        for line in range(group // PLANE):
-            target = me ^ (PLANE * line + k)
-            columns = pl.ds(pl.multiple_of(target * width, LANES), width)
-            piece = jnp.dot(rank_rows, expand_ref[:, columns], preferred_element_type=jnp.float32)
-            piece = piece.astype(jnp.bfloat16)
-            for part in range(parts):
-                out_refs[k][line * parts + part] = piece[:, part * LANES : (part + 1) * LANES]
-
-
-def adapter_output(gathered, shrink, expand, group, me):
+    out_ref[...] = total_ref[...].astype(out_ref.dtype)
+
+
+def rank_rows_of(gathered, shrink, group):
     rank = shrink.shape[0]
-    model_width = expand.shape[1]
     depth = gathered.shape[2]
-    parts = model_width // group // LANES
-    held = (model_width // PLANE // LANES, HELD, LANES)
     vmem = pl.BlockSpec(memory_space=pltpu.VMEM)
     return pl.pallas_call(
-        functools.partial(adapter_kernel, parts),
-        out_shape=[jax.ShapeDtypeStruct(held, jnp.bfloat16)] * PLANE,
-        in_specs=[
-            pl.BlockSpec(memory_space=pltpu.SMEM),
-            vmem,
-            pl.BlockSpec(memory_space=pl.ANY),
-            pl.BlockSpec(memory_space=pl.ANY),
-        ],
-        out_specs=[vmem] * PLANE,
+        rank_kernel,
+        out_shape=jax.ShapeDtypeStruct((HELD, rank), jnp.bfloat16),
+        in_specs=[vmem, pl.BlockSpec(memory_space=pl.ANY)],
+        out_specs=vmem,
         scratch_shapes=[
             pltpu.VMEM((group, rank, depth), jnp.bfloat16),
-            pltpu.VMEM((rank, model_width), jnp.bfloat16),
             pltpu.VMEM((HELD, rank), jnp.float32),
             pltpu.SemaphoreType.DMA((group,)),
-            pltpu.SemaphoreType.DMA,
         ],
         compiler_params=pltpu.CompilerParams(vmem_limit_bytes=24 * 2**20),
-    )(me.reshape(1), gathered, in_hbm(expand), in_hbm(shrink))
+    )(gathered, in_hbm(shrink))
+
+
+def columns_kernel(width, me_ref, expand_hbm, *refs):
+    out_refs, sems = refs[:PLANE], refs[PLANE]
+    lines = out_refs[0].shape[1] // width
+    copies = []
+    for k in range(PLANE):
+        for line in range(lines):
+            target = me_ref[0] ^ (PLANE * line + k)
+            columns = pl.ds(pl.multiple_of(target * width, LANES), width)
+            copies.append(
+                pltpu.make_async_copy(
+                    expand_hbm.at[:, columns],
+                    out_refs[k].at[:, pl.ds(line * width, width)],
+                    sems.at[k, line],
+                )
+            )
+    for copy in copies:
+        copy.start()
+    for copy in copies:
+        copy.wait()
+
+
+def plane_columns(expand, group, me):
+    rank, model_width = expand.shape
+    vmem = pl.BlockSpec(memory_space=pltpu.VMEM)
+    return pl.pallas_call(
+        functools.partial(columns_kernel, model_width // group),
+        out_shape=[jax.ShapeDtypeStruct((rank, model_width // PLANE), jnp.bfloat16)] * PLANE,
+        in_specs=[pl.BlockSpec(memory_space=pltpu.SMEM), pl.BlockSpec(memory_space=pl.ANY)],
+        out_specs=[vmem] * PLANE,
+        scratch_shapes=[pltpu.SemaphoreType.DMA((PLANE, group // PLANE))],
+        compiler_params=pltpu.CompilerParams(vmem_limit_bytes=24 * 2**20),
+    )(me.reshape(1), in_hbm(expand))
 
 
 def merge_kernel(pair_ref, pick_ref, *refs):
-    in_refs, out_ref, held_ref = refs[:PLANE], refs[PLANE], refs[PLANE + 1]
-    for k in range(PLANE):
-        held_ref[:, k * HELD : (k + 1) * HELD] = in_refs[k][...]
-    pick = pick_ref[...]
-    for part in range(pair_ref.shape[0]):
-        adapter_rows = lax.dot_general(
-            pick, held_ref[part], (((0,), (0,)), ((), ())), preferred_element_type=jnp.float32
+    rank_refs, column_refs, out_ref = refs[:PLANE], refs[PLANE : 2 * PLANE], refs[2 * PLANE]
+    spread = [
+        lax.dot_general(
+            pick_ref[k * HELD : (k + 1) * HELD],
+            rank_refs[k][...],
+            (((0,), (0,)), ((), ())),
+            preferred_element_type=jnp.float32,
+        ).astype(jnp.bfloat16)
+        for k in range(PLANE)
+    ]
+    blocks = out_ref.shape[0]
+    step = math.gcd(blocks, 4)
+    for first in range(0, blocks, step):
+        columns = slice(first * LANES, (first + step) * LANES)
+        adapter_rows = jnp.dot(
+            spread[0], column_refs[0][:, columns], preferred_element_type=jnp.float32
         )
-        out_ref[part] = pair_ref[part] + ADAPTER_SCALE * adapter_rows
-
-
-def merge_adapters(pair, pick, arrived):
+        for k in range(1, PLANE):
+            adapter_rows += jnp.dot(
+                spread[k], column_refs[k][:, columns], preferred_element_type=jnp.float32
+            )
+        for part in range(step):
+            lanes = slice(part * LANES, (part + 1) * LANES)
+            out_ref[first + part] = pair_ref[first + part] + ADAPTER_SCALE * adapter_rows[:, lanes]
+
+
+def merge_adapters(pair, pick, ranks, columns):
     vmem = pl.BlockSpec(memory_space=pltpu.VMEM)
     return pl.pallas_call(
         merge_kernel,
         out_shape=jax.ShapeDtypeStruct(pair.shape, jnp.float32),
-        in_specs=[vmem] * (2 + PLANE),
+        in_specs=[vmem] * (2 + 2 * PLANE),
         out_specs=vmem,
-        scratch_shapes=[pltpu.VMEM((pair.shape[0], PLANE * HELD, LANES), jnp.bfloat16)],
         compiler_params=pltpu.CompilerParams(vmem_limit_bytes=24 * 2**20),
-    )(pair, pick, *arrived)
+    )(pair, pick, *ranks, *columns)
 
 
 def shards_by_blocks(
@@ -317,10 +341,13 @@
     kept, pair_in = pair_sums(kept_hidden, down_matrix, group, order, width)
     gathered, _ = lax.optimization_barrier((gathered, kept))
     expand = jnp.swapaxes(expand_matrices, 1, 2)[0]
-    outs = adapter_output(gathered, shrink, expand, group, me)
-    arrived = [outs[0]] + [xor_permute(outs[k], group, k) for k in range(1, PLANE)]
+    expand, _ = lax.optimization_barrier((expand, kept))
+    columns = plane_columns(expand, group, me)
+    columns = [columns[0]] + [xor_permute(columns[k], group, k) for k in range(1, PLANE)]
+    rank_rows = rank_rows_of(gathered, shrink, group)
+    ranks = [rank_rows] + [xor_permute(rank_rows, group, k) for k in range(1, PLANE)]
     pair = kept + unpack_scaled(pair_in, rows)
-    merged = merge_adapters(pair, pick, arrived)
+    merged = merge_adapters(pair, pick, ranks, columns)
     return line_sums(merged, group, width).astype(jnp.bfloat16)
 
 

time: 61.2 us -> 62.5 us (1.021)
  waiting for transfers between devices: 18.6 us -> 14.1 us
  local copies, waits for them, and re-layouts: 0.9 us -> 2.83 us
  starting transfers between devices: 17.2 us -> 18.8 us
  Pallas kernels: 21.4 us -> 22.9 us
  other arithmetic: 1.95 us -> 2.58 us
    ppermute x9 -> x12, waiting for transfers between devices: 18.6 us -> 14.1 us  [xor_permute(): return lax.ppermute(value, 'tp', [(i, i ^ offset) for i in range(group)])]
    ppermute x9 -> x12, starting transfers between devices: 9.85 us -> 11.4 us  [xor_permute(): return lax.ppermute(value, 'tp', [(i, i ^ offset) for i in range(group)])]
    pallas_call x1 -> x2, Pallas kernels: 3.86 us -> 4.92 us  [the longest x1 3.54 us: rank_rows_of(): pl.pallas_call(rank_kernel, out_shape=jax.ShapeDtypeStruct((HELD, rank),...]
    slice x4, local copies, waits for them, and re-layouts: 0.15 us -> 1.14 us  [unpack_scaled(): packed[:-MARK_ROWS]]
    unnamed x0 -> x4, local copies, waits for them, and re-layouts: none -> 0.9 us
    exp2 x4, other arithmetic: 0.03 us -> 0.7 us  [unpack_scaled(): return values * jnp.exp2(exponent - F16_TOP)[None, :, None]]
  transfers between devices with their start and end apart: 10 -> 13, of which waited for: 6 -> 7; matrix products, arithmetic and copies ran while one was open for 3% -> 5% of each run, Pallas kernels for 24% -> 32%
where the time goes in v21:
time: 62.5 us; the launch traced here: 62.1 us
  Pallas kernels  22.9 us (37%)
  starting transfers between devices  18.8 us (30%)
  waiting for transfers between devices  14.1 us (23%)
  local copies, waits for them, and re-layouts  2.83 us (5%)
  other arithmetic  2.58 us (4%)
  between operations  0.83 us (1%)
    pallas_call x3, Pallas kernels, column_blocks(): pl.pallas_call(functools.partial(column_blocks_kernel, groups), out_shape...  14.8 us
    ppermute x12, waiting for transfers between devices, xor_permute(): return lax.ppermute(value, 'tp', [(i, i ^ offset) for i in range(group)])  14.1 us
    ppermute x12, starting transfers between devices, xor_permute(): return lax.ppermute(value, 'tp', [(i, i ^ offset) for i in range(group)])  11.4 us
    all_to_all x1, starting transfers between devices, shards_by_blocks(): lax.all_to_all(packed, 'tp', split_axis=0, concat_axis=0, tiled=True)  7.37 us
    pallas_call x1, Pallas kernels, rank_rows_of(): pl.pallas_call(rank_kernel, out_shape=jax.ShapeDtypeStruct((HELD, rank),...  3.54 us
    pallas_call x1, Pallas kernels, pack_rows(): pl.pallas_call(functools.partial(pack_kernel, blocks, orders), out_shape=...  2.5 us
    pallas_call x1, Pallas kernels, plane_columns(): pl.pallas_call(functools.partial(columns_kernel, model_width // group), o...  1.38 us
  transfers between devices with their start and end apart: 13, of which 7 were waited for; matrix products, arithmetic and copies ran while one was open for 5% of the time, Pallas kernels for 32%

profile of v21, /device:TPU:0, one launch (start us, length us, event | category | flops | bytes accessed | tf_op | source)
XLA Modules:
  0.0 62.1 jit_solution(6765592388335228132)
XLA Ops:
  0.0 2.5 %shard_map.64 = (bf16[80,4,1792]{2,1,0:T(4,128)(2,1)}, bf16[96,96]{1,0:T(8,128)(2,1)S(1)}, s32[16]{0:T(128)S(1)}, bf16[96,1792]{1,0:T(8,128)(2,1)S(1)}) custom-call(s32[1]{0:T(128)} %bitcast.2.me_ref, s32[16]{0:T(128)} %slot_hbm.1, s32[1,96]{1,0:T(1,128)} %bitcast.56, bf16[96,1792]{1,0:T(8,128)(2,1)} %hidden_hbm.1), custom_call_target="tpu_custom_call" | custom-call | tf_op jit(solution)/shard_map/pallas_call | solution.py:194
  2.5 7.4 %all-to-all-start = ((bf16[80,4,1792]{2,1,0:T(4,128)(2,1)}), bf16[80,4,1792]{2,1,0:T(4,128)(2,1)S(1)}, u32[]{:S(2)}, u32[]{:S(2)}) async-start(bf16[80,4,1792]{2,1,0:T(4,128)(2,1)} %get-tuple-element.46), calls=%async_computation | async-start | bytes 2293760 | tf_op jit(solution)/shard_map/all_to_all | solution.py:339
  9.9 9.4 %conditional.2 = (f16[1552,128]{1,0:T(8,128)(2,1)S(1)}) conditional(s32[]{:T(128)} %bitcast.4, () %tuple.20, (s32[16]{0:T(128)S(1)}, bf16[96,1792]{1,0:T(8,128)(2,1)S(1)}, bf16[1792,8192]{1,0:T(8,128)(2,1)}) %tuple.21), branch_computations={%region_0.0_spmd, %region_1.3_spmd} | conditional | flops 1581488 | bytes 7479232 | solution.py:110
  9.9 0.1 fusion.29
  10.0 4.2 %branch_1_fun.4 = f32[16,96,128]{2,1,0:T(8,128)S(1)} custom-call(s32[4]{0:T(128)S(1)} %get-tuple-element.60.order_ref, bf16[96,1792]{1,0:T(8,128)(2,1)S(1)} %get-tuple-element.24.hidden_ref, bf16[1792,8192]{1,0:T(8,128)(2,1)} %get-tuple-element.25.down_ref), custom_call_target="tpu_custom_call" | custom-call | flops 1000 | bytes 1000 | tf_op jit(solution)/shard_map/cond/branch_1_fun/pallas_call | solution.py:63
  14.2 0.5 collective-permute-start.1
  14.7 4.2 %branch_1_fun.3 = f32[16,96,128]{2,1,0:T(8,128)S(1)} custom-call(s32[4]{0:T(128)S(1)} %get-tuple-element.61.order_ref, bf16[96,1792]{1,0:T(8,128)(2,1)S(1)} %get-tuple-element.24.hidden_ref, bf16[1792,8192]{1,0:T(8,128)(2,1)} %get-tuple-element.25.down_ref), custom_call_target="tpu_custom_call" | custom-call | flops 1000 | bytes 1000 | tf_op jit(solution)/shard_map/cond/branch_1_fun/pallas_call | solution.py:63
  18.9 0.0 collective-permute-done.1
  18.9 0.2 abs_reduce_fusion
  19.1 0.2 multiply_convert_fusion
  19.3 0.1 fusion.1
  19.4 1.7 %collective-permute-start.2 = (f16[1552,128]{1,0:T(8,128)(2,1)S(1)}, f16[1552,128]{1,0:T(8,128)(2,1)}, u32[]{:S(2)}, u32[]{:S(2)}) collective-permute-start(f16[1552,128]{1,0:T(8,128)(2,1)S(1)} %get-tuple-element.73), channel_id=1, source_target_pairs={{0,2},{1,3},{2,0},{3,1},{4,6},{5,7},{6,4},{7,5},{8,10},{9,11},{10,... | collective-permute-start | bytes 1191944 | tf_op jit(solution)/shard_map/ppermute | solution.py:26
  21.1 0.6 %slice.52 = s32[1]{0:T(128)} slice(s32[16]{0:T(128)S(1)} %get-tuple-element.44), slice={[1:2]} | slice | bytes 8 | tf_op jit(solution)/shard_map/slice | solution.py:121
  22.4 8.9 %conditional.3 = (f32[16,96,128]{2,1,0:T(8,128)S(1)}) conditional(s32[]{:T(128)} %bitcast.5, () %tuple.23, (s32[16]{0:T(128)S(1)}, bf16[96,1792]{1,0:T(8,128)(2,1)S(1)}, bf16[1792,8192]{1,0:T(8,128)(2,1)}) %tuple.24), branch_computations={%region_3.4_spmd, %region_4.5_spmd} | conditional | flops 197608 | bytes 5506136 | solution.py:121
  22.4 0.1 slice.36.order_ref
  22.5 6.4 %branch_1_fun.5 = (f32[16,96,128]{2,1,0:T(8,128)S(1)}, f32[16,96,128]{2,1,0:T(8,128)S(1)}) custom-call(s32[8]{0:T(128)S(1)} %slice.36.order_ref, bf16[96,1792]{1,0:T(8,128)(2,1)S(1)} %get-tuple-element.27.hidden_ref, bf16[1792,8192]{1,0:T(8,128)(2,1)} %get-tuple-element.28.down_ref), custom_call_target="tpu_custom_call" | custom-call | flops 1000 | bytes 1000 | tf_op jit(solution)/shard_map/cond/branch_1_fun/pallas_call | solution.py:63
  28.9 0.1 collective-permute-start
  29.0 2.2 %collective-permute-done = f32[16,96,128]{2,1,0:T(8,128)S(1)} collective-permute-done((f32[16,96,128]{2,1,0:T(8,128)S(1)}, f32[16,96,128]{2,1,0:T(8,128)S(1)}, u32[]{:S(2)}, u32[]{:S(2)}) %collective-permute-start) | collective-permute-done | bytes 786464 | tf_op jit(solution)/shard_map/cond/branch_1_fun/ppermute | solution.py:26
  31.2 0.1 add.39
  31.3 0.0 copy-start
  31.3 0.9 %copy-done = f32[16,96,128]{2,1,0:T(8,128)} copy-done((f32[16,96,128]{2,1,0:T(8,128)}, f32[16,96,128]{2,1,0:T(8,128)S(1)}, u32[]{:S(2)}) %copy-start) | copy-done | bytes 786456
  32.2 1.4 %shard_map.66 = (bf16[64,2048]{1,0:T(8,128)(2,1)S(1)}, bf16[64,2048]{1,0:T(8,128)(2,1)S(1)}, bf16[64,2048]{1,0:T(8,128)(2,1)S(1)}, bf16[64,2048]{1,0:T(8,128)(2,1)S(1)}) custom-call(s32[1]{0:T(128)} %bitcast.2.me_ref, bf16[64,8192]{1,0:T(8,128)(2,1)} %bitcast.48), custom_call_target="tpu_custom_call" | custom-call | tf_op jit(solution)/shard_map/pallas_call | solution.py:279
  33.6 0.2 collective-permute-start.6
  33.8 0.4 collective-permute-start.7
  34.2 1.3 %collective-permute-start.8 = (bf16[64,2048]{1,0:T(8,128)(2,1)S(1)}, bf16[64,2048]{1,0:T(8,128)(2,1)S(1)}, u32[]{:S(2)}, u32[]{:S(2)}) collective-permute-start(bf16[64,2048]{1,0:T(8,128)(2,1)S(1)} %get-tuple-element.52), channel_id=1, source_target_pairs={{0,3},{1,2},{2,1},{3,0},{4,7},{5,6},{6,5},{7,4},{8,11},{9,10},{10,... | collective-permute-start | bytes 786440 | tf_op jit(solution)/shard_map/ppermute | solution.py:26
  35.5 0.5 collective-permute-done.2
  36.0 1.1 %slice.65 = f16[1536,128]{1,0:T(8,128)(2,1)S(1)} slice(f16[1552,128]{1,0:T(8,128)(2,1)} %collective-permute-done.2), slice={[0:1536], [0:128]} | slice | bytes 786432 | tf_op jit(solution)/shard_map/slice | solution.py:91
  37.1 0.7 %fusion.28 = f32[96]{0:T(128)S(1)} fusion(f16[1552,128]{1,0:T(8,128)(2,1)} %collective-permute-done.2), kind=kLoop, calls=%fused_computation.51 | loop fusion | flops 288 | bytes 576 | tf_op jit(solution)/shard_map/exp2 | solution.py:93
  37.8 0.0 all-to-all-done.rows_ref
  37.8 0.0 copy-start.1
  37.8 3.5 %shard_map.65.refs_0_ = bf16[24,64]{1,0:T(8,128)(2,1)S(1)} custom-call(bf16[80,4,1792]{2,1,0:T(4,128)(2,1)S(1)} %all-to-all-done.rows_ref, bf16[64,28672]{1,0:T(8,128)(2,1)} %bitcast.45), custom_call_target="tpu_custom_call" | custom-call | tf_op jit(solution)/shard_map/pallas_call | solution.py:241
  41.3 1.7 %collective-permute-start.5 = (bf16[24,64]{1,0:T(8,128)(2,1)S(1)}, bf16[24,64]{1,0:T(8,128)(2,1)S(1)}, u32[]{:S(2)}, u32[]{:S(2)}) collective-permute-start(bf16[24,64]{1,0:T(8,128)(2,1)S(1)} %shard_map.65.refs_0_), channel_id=1, source_target_pairs={{0,3},{1,2},{2,1},{3,0},{4,7},{5,6},{6,5},{7,4},{8,11},{9,10},{10,... | collective-permute-start | bytes 9224 | tf_op jit(solution)/shard_map/ppermute | solution.py:26
  43.0 0.5 collective-permute-start.4
  43.5 0.0 collective-permute-done.6.refs_5_
  43.5 0.0 collective-permute-start.3
  43.6 0.0 copy-done.1
  43.6 0.2 fusion.2.pair_ref
  43.7 0.0 collective-permute-done.7.refs_6_
  43.7 3.7 %collective-permute-done.8.refs_7_ = bf16[64,2048]{1,0:T(8,128)(2,1)S(1)} collective-permute-done((bf16[64,2048]{1,0:T(8,128)(2,1)S(1)}, bf16[64,2048]{1,0:T(8,128)(2,1)S(1)}, u32[]{:S(2)}, u32[]{:S(2)}) %collective-permute-start.8) | collective-permute-done | bytes 262176 | tf_op jit(solution)/shard_map/ppermute | solution.py:26
  47.5 0.1 collective-permute-done.5.refs_3_
  47.6 0.7 %collective-permute-done.4.refs_2_ = bf16[24,64]{1,0:T(8,128)(2,1)S(1)} collective-permute-done((bf16[24,64]{1,0:T(8,128)(2,1)S(1)}, bf16[24,64]{1,0:T(8,128)(2,1)S(1)}, u32[]{:S(2)}, u32[]{:S(2)}) %collective-permute-start.4) | collective-permute-done | bytes 3104 | tf_op jit(solution)/shard_map/ppermute | solution.py:26
  48.3 0.0 collective-permute-done.3.refs_1_
  48.3 0.7 %shard_map.67 = f32[16,96,128]{2,1,0:T(8,128)S(1)} custom-call(f32[16,96,128]{2,1,0:T(8,128)S(1)} %fusion.2.pair_ref, bf16[96,96]{1,0:T(8,128)(2,1)S(1)} %get-tuple-element.45.pick_ref, bf16[24,64]{1,0:T(8,128)(2,1)S(1)} %shard_map.65.refs_0_, bf16[24,64]{1,0:T(8,128)(2,1)S(1)} %collective-permute-done.3.refs_1_, ...), custom_call_target="tpu_custom_call" | custom-call | tf_op jit(solution)/shard_map/pallas_call | solution.py:318
  49.0 0.2 abs_reduce_fusion.3
  49.2 0.1 multiply_convert_fusion.3
  49.4 3.3 %collective-permute-start.10 = (f16[400,128]{1,0:T(8,128)(2,1)S(1)}, f16[400,128]{1,0:T(8,128)(2,1)S(1)}, u32[]{:S(2)}, u32[]{:S(2)}) collective-permute-start(f16[400,128]{1,0:T(8,128)(2,1)S(1)} %fusion.10), channel_id=1, source_target_pairs={{0,8},{1,9},{2,10},{3,11},{4,12},{5,13},{6,14},{7,15},{8,0},{9,1},... | collective-permute-start | bytes 307208 | tf_op jit(solution)/shard_map/ppermute | solution.py:26
  52.7 0.7 %collective-permute-start.9 = (f16[400,128]{1,0:T(8,128)(2,1)S(1)}, f16[400,128]{1,0:T(8,128)(2,1)S(1)}, u32[]{:S(2)}, u32[]{:S(2)}) collective-permute-start(f16[400,128]{1,0:T(8,128)(2,1)S(1)} %fusion.9), channel_id=1, source_target_pairs={{0,4},{1,5},{2,6},{3,7},{4,0},{5,1},{6,2},{7,3},{8,12},{9,13},{10,... | collective-permute-start | bytes 307208 | tf_op jit(solution)/shard_map/ppermute | solution.py:26
  53.4 0.9 %collective-permute-start.11 = (f16[400,128]{1,0:T(8,128)(2,1)S(1)}, f16[400,128]{1,0:T(8,128)(2,1)S(1)}, u32[]{:S(2)}, u32[]{:S(2)}) collective-permute-start(f16[400,128]{1,0:T(8,128)(2,1)S(1)} %fusion.11), channel_id=1, source_target_pairs={{0,12},{1,13},{2,14},{3,15},{4,8},{5,9},{6,10},{7,11},{8,4},{9,5},... | collective-permute-start | bytes 307208 | tf_op jit(solution)/shard_map/ppermute | solution.py:26
  54.3 5.2 %collective-permute-done.10 = f16[400,128]{1,0:T(8,128)(2,1)S(1)} collective-permute-done((f16[400,128]{1,0:T(8,128)(2,1)S(1)}, f16[400,128]{1,0:T(8,128)(2,1)S(1)}, u32[]{:S(2)}, u32[]{:S(2)}) %collective-permute-start.10) | collective-permute-done | bytes 102432 | tf_op jit(solution)/shard_map/ppermute | solution.py:26
  59.6 1.6 %collective-permute-done.9 = f16[400,128]{1,0:T(8,128)(2,1)S(1)} collective-permute-done((f16[400,128]{1,0:T(8,128)(2,1)S(1)}, f16[400,128]{1,0:T(8,128)(2,1)S(1)}, u32[]{:S(2)}, u32[]{:S(2)}) %collective-permute-start.9) | collective-permute-done | bytes 102432 | tf_op jit(solution)/shard_map/ppermute | solution.py:26
  61.3 0.0 collective-permute-done.11
  61.3 0.8 %copy_bitcast_fusion = bf16[96,512]{1,0:T(8,128)(2,1)} fusion(f16[4,96,128]{2,1,0:T(8,128)(2,1)S(1)} %bitcast.54, f16[4,96,128]{2,1,0:T(8,128)(2,1)S(1)} %bitcast.51, f16[4,96,128]{2,1,0:T(8,128)(2,1)S(1)} %bitcast.52, f32[16,96,128]{2,1,0:T(8,128)S(1)} %shard_map.67, f32[96]{0:T(128)S(1)} %fusion.16, f32[96]{0:T(128)S(1)} %fusion.20, f32[96]{0:T(128)S(1)} %fusion.24), kind=kLoop, calls=%fused_computation.31 | loop fusion | flops 491520 | bytes 591360 | tf_op jit(solution)/shard_map/convert_element_type | solution.py:351
  (12 shorter events, 0.2 us)
Async XLA Ops:
  2.5 35.3 %all-to-all-start = ((bf16[80,4,1792]{2,1,0:T(4,128)(2,1)}), bf16[80,4,1792]{2,1,0:T(4,128)(2,1)S(1)}, u32[]{:S(2)}, u32[]{:S(2)}) async-start(bf16[80,4,1792]{2,1,0:T(4,128)(2,1)} %get-tuple-element.46), calls=%async_computation | async-start | bytes 2293760 | tf_op jit(solution)/shard_map/all_to_all | solution.py:339
  14.2 4.7 %collective-permute-start.1 = (f32[16,96,128]{2,1,0:T(8,128)S(1)}, f32[16,96,128]{2,1,0:T(8,128)S(1)}, u32[]{:S(2)}, u32[]{:S(2)}) collective-permute-start(f32[16,96,128]{2,1,0:T(8,128)S(1)} %branch_1_fun.4), channel_id=1, source_target_pairs={{0,1},{1,0},{2,3},{3,2},{4,5},{5,4},{6,7},{7,6},{8,9},{9,8},{10,11... | collective-permute-start | bytes 2359304 | tf_op jit(solution)/shard_map/cond/branch_1_fun/ppermute | solution.py:26
  19.4 16.6 %collective-permute-start.2 = (f16[1552,128]{1,0:T(8,128)(2,1)S(1)}, f16[1552,128]{1,0:T(8,128)(2,1)}, u32[]{:S(2)}, u32[]{:S(2)}) collective-permute-start(f16[1552,128]{1,0:T(8,128)(2,1)S(1)} %get-tuple-element.73), channel_id=1, source_target_pairs={{0,2},{1,3},{2,0},{3,1},{4,6},{5,7},{6,4},{7,5},{8,10},{9,11},{10,... | collective-permute-start | bytes 1191944 | tf_op jit(solution)/shard_map/ppermute | solution.py:26
  28.9 2.4 %collective-permute-start = (f32[16,96,128]{2,1,0:T(8,128)S(1)}, f32[16,96,128]{2,1,0:T(8,128)S(1)}, u32[]{:S(2)}, u32[]{:S(2)}) collective-permute-start(f32[16,96,128]{2,1,0:T(8,128)S(1)} %get-tuple-element.30), channel_id=1, source_target_pairs={{0,1},{1,0},{2,3},{3,2},{4,5},{5,4},{6,7},{7,6},{8,9},{9,8},{10,11... | collective-permute-start | bytes 2359304 | tf_op jit(solution)/shard_map/cond/branch_1_fun/ppermute | solution.py:26
  31.3 0.9 %copy-start = (f32[16,96,128]{2,1,0:T(8,128)}, f32[16,96,128]{2,1,0:T(8,128)S(1)}, u32[]{:S(2)}) copy-start(f32[16,96,128]{2,1,0:T(8,128)S(1)} %get-tuple-element.74) | copy-start | bytes 2359300
  33.6 9.9 %collective-permute-start.6 = (bf16[64,2048]{1,0:T(8,128)(2,1)S(1)}, bf16[64,2048]{1,0:T(8,128)(2,1)S(1)}, u32[]{:S(2)}, u32[]{:S(2)}) collective-permute-start(bf16[64,2048]{1,0:T(8,128)(2,1)S(1)} %get-tuple-element.50), channel_id=1, source_target_pairs={{0,1},{1,0},{2,3},{3,2},{4,5},{5,4},{6,7},{7,6},{8,9},{9,8},{10,11... | collective-permute-start | bytes 786440 | tf_op jit(solution)/shard_map/ppermute | solution.py:26
  33.8 9.9 %collective-permute-start.7 = (bf16[64,2048]{1,0:T(8,128)(2,1)S(1)}, bf16[64,2048]{1,0:T(8,128)(2,1)S(1)}, u32[]{:S(2)}, u32[]{:S(2)}) collective-permute-start(bf16[64,2048]{1,0:T(8,128)(2,1)S(1)} %get-tuple-element.51), channel_id=1, source_target_pairs={{0,2},{1,3},{2,0},{3,1},{4,6},{5,7},{6,4},{7,5},{8,10},{9,11},{10,... | collective-permute-start | bytes 786440 | tf_op jit(solution)/shard_map/ppermute | solution.py:26
  34.2 13.3 %collective-permute-start.8 = (bf16[64,2048]{1,0:T(8,128)(2,1)S(1)}, bf16[64,2048]{1,0:T(8,128)(2,1)S(1)}, u32[]{:S(2)}, u32[]{:S(2)}) collective-permute-start(bf16[64,2048]{1,0:T(8,128)(2,1)S(1)} %get-tuple-element.52), channel_id=1, source_target_pairs={{0,3},{1,2},{2,1},{3,0},{4,7},{5,6},{6,5},{7,4},{8,11},{9,10},{10,... | collective-permute-start | bytes 786440 | tf_op jit(solution)/shard_map/ppermute | solution.py:26
  37.8 5.8 %copy-start.1 = (f32[16,96,128]{2,1,0:T(8,128)S(1)}, f32[16,96,128]{2,1,0:T(8,128)}, u32[]{:S(2)}) copy-start(f32[16,96,128]{2,1,0:T(8,128)} %copy-done) | copy-start | bytes 2359300
  41.3 6.3 %collective-permute-start.5 = (bf16[24,64]{1,0:T(8,128)(2,1)S(1)}, bf16[24,64]{1,0:T(8,128)(2,1)S(1)}, u32[]{:S(2)}, u32[]{:S(2)}) collective-permute-start(bf16[24,64]{1,0:T(8,128)(2,1)S(1)} %shard_map.65.refs_0_), channel_id=1, source_target_pairs={{0,3},{1,2},{2,1},{3,0},{4,7},{5,6},{6,5},{7,4},{8,11},{9,10},{10,... | collective-permute-start | bytes 9224 | tf_op jit(solution)/shard_map/ppermute | solution.py:26
  43.0 5.3 %collective-permute-start.4 = (bf16[24,64]{1,0:T(8,128)(2,1)S(1)}, bf16[24,64]{1,0:T(8,128)(2,1)S(1)}, u32[]{:S(2)}, u32[]{:S(2)}) collective-permute-start(bf16[24,64]{1,0:T(8,128)(2,1)S(1)} %shard_map.65.refs_0_), channel_id=1, source_target_pairs={{0,2},{1,3},{2,0},{3,1},{4,6},{5,7},{6,4},{7,5},{8,10},{9,11},{10,... | collective-permute-start | bytes 9224 | tf_op jit(solution)/shard_map/ppermute | solution.py:26
  43.5 4.8 %collective-permute-start.3 = (bf16[24,64]{1,0:T(8,128)(2,1)S(1)}, bf16[24,64]{1,0:T(8,128)(2,1)S(1)}, u32[]{:S(2)}, u32[]{:S(2)}) collective-permute-start(bf16[24,64]{1,0:T(8,128)(2,1)S(1)} %shard_map.65.refs_0_), channel_id=1, source_target_pairs={{0,1},{1,0},{2,3},{3,2},{4,5},{5,4},{6,7},{7,6},{8,9},{9,8},{10,11... | collective-permute-start | bytes 9224 | tf_op jit(solution)/shard_map/ppermute | solution.py:26
  49.4 10.2 %collective-permute-start.10 = (f16[400,128]{1,0:T(8,128)(2,1)S(1)}, f16[400,128]{1,0:T(8,128)(2,1)S(1)}, u32[]{:S(2)}, u32[]{:S(2)}) collective-permute-start(f16[400,128]{1,0:T(8,128)(2,1)S(1)} %fusion.10), channel_id=1, source_target_pairs={{0,8},{1,9},{2,10},{3,11},{4,12},{5,13},{6,14},{7,15},{8,0},{9,1},... | collective-permute-start | bytes 307208 | tf_op jit(solution)/shard_map/ppermute | solution.py:26
  52.7 8.5 %collective-permute-start.9 = (f16[400,128]{1,0:T(8,128)(2,1)S(1)}, f16[400,128]{1,0:T(8,128)(2,1)S(1)}, u32[]{:S(2)}, u32[]{:S(2)}) collective-permute-start(f16[400,128]{1,0:T(8,128)(2,1)S(1)} %fusion.9), channel_id=1, source_target_pairs={{0,4},{1,5},{2,6},{3,7},{4,0},{5,1},{6,2},{7,3},{8,12},{9,13},{10,... | collective-permute-start | bytes 307208 | tf_op jit(solution)/shard_map/ppermute | solution.py:26
  53.4 7.8 %collective-permute-start.11 = (f16[400,128]{1,0:T(8,128)(2,1)S(1)}, f16[400,128]{1,0:T(8,128)(2,1)S(1)}, u32[]{:S(2)}, u32[]{:S(2)}) collective-permute-start(f16[400,128]{1,0:T(8,128)(2,1)S(1)} %fusion.11), channel_id=1, source_target_pairs={{0,12},{1,13},{2,14},{3,15},{4,8},{5,9},{6,10},{7,11},{8,4},{9,5},... | collective-permute-start | bytes 307208 | tf_op jit(solution)/shard_map/ppermute | solution.py:26

commit v22 on v17

--- a/solution.py
+++ b/solution.py
@@ -121,17 +121,30 @@
     return kept, pair_in
 
 
-def line_sums(pair, group, width):
-    rows = pair.shape[1]
-    parts = width // LANES
-    arrived = [
-        xor_permute(pack_scaled(pair[i * parts : (i + 1) * parts]), group, 4 * i)
-        for i in range(1, group // 4)
-    ]
-    total = pair[:parts]
-    for packed in arrived:
-        total = total + unpack_scaled(packed, rows)
-    return jnp.transpose(total, (1, 0, 2)).reshape(rows, width)
+def exchange_sum(kept, sent, group, offset):
+    return kept + unpack_scaled(xor_permute(pack_scaled(sent), group, offset), kept.shape[1])
+
+
+def line_sums(merged, group):
+    if group != 4 * PLANE:
+        (whole,) = merged
+        return sum_direct(whole, group)
+    near_kept, near_sent, far_kept, far_sent = merged
+    half = near_kept.shape[0] // 2
+    far = exchange_sum(far_kept, far_sent, group, 2 * PLANE)
+    near = exchange_sum(near_kept, near_sent, group, PLANE)
+    near = exchange_sum(near[:half], near[half:], group, 2 * PLANE)
+    far = exchange_sum(far[:half], far[half:], group, PLANE)
+    return jnp.concatenate([near, far], axis=0)
+
+
+def sum_direct(whole, group):
+    lines = group // PLANE
+    parts = whole.shape[0] // lines
+    total = whole[:parts]
+    for i in range(1, lines):
+        total = exchange_sum(total, whole[i * parts : (i + 1) * parts], group, PLANE * i)
+    return total
 
 
 def pack_kernel(
@@ -276,26 +289,38 @@
     )(me.reshape(1), gathered, in_hbm(expand), in_hbm(shrink))
 
 
-def merge_kernel(pair_ref, pick_ref, *refs):
-    in_refs, out_ref, held_ref = refs[:PLANE], refs[PLANE], refs[PLANE + 1]
+def merge_kernel(places, pair_ref, pick_ref, *refs):
+    in_refs, out_refs, held_ref = refs[:PLANE], refs[PLANE:-1], refs[-1]
     for k in range(PLANE):
         held_ref[:, k * HELD : (k + 1) * HELD] = in_refs[k][...]
     pick = pick_ref[...]
-    for part in range(pair_ref.shape[0]):
-        adapter_rows = lax.dot_general(
-            pick, held_ref[part], (((0,), (0,)), ((), ())), preferred_element_type=jnp.float32
-        )
-        out_ref[part] = pair_ref[part] + ADAPTER_SCALE * adapter_rows
-
-
-def merge_adapters(pair, pick, arrived):
+    for out_ref, blocks in zip(out_refs, places):
+        for i, block in enumerate(blocks):
+            adapter_rows = lax.dot_general(
+                pick, held_ref[block], (((0,), (0,)), ((), ())), preferred_element_type=jnp.float32
+            )
+            out_ref[i] = pair_ref[block] + ADAPTER_SCALE * adapter_rows
+
+
+def merge_adapters(pair, pick, arrived, group):
+    blocks, rows, _ = pair.shape
+    if group == 4 * PLANE:
+        parts = blocks // 4
+        half = parts // 2
+
+        def pieces(first, *lines):
+            return [line * parts + first + i for line in lines for i in range(half)]
+
+        places = [pieces(0, 0, 2), pieces(0, 1, 3), pieces(half, 0, 1), pieces(half, 2, 3)]
+    else:
+        places = [list(range(blocks))]
     vmem = pl.BlockSpec(memory_space=pltpu.VMEM)
     return pl.pallas_call(
-        merge_kernel,
-        out_shape=jax.ShapeDtypeStruct(pair.shape, jnp.float32),
+        functools.partial(merge_kernel, places),
+        out_shape=[jax.ShapeDtypeStruct((len(p), rows, LANES), jnp.float32) for p in places],
         in_specs=[vmem] * (2 + PLANE),
-        out_specs=vmem,
-        scratch_shapes=[pltpu.VMEM((pair.shape[0], PLANE * HELD, LANES), jnp.bfloat16)],
+        out_specs=[vmem] * len(places),
+        scratch_shapes=[pltpu.VMEM((blocks, PLANE * HELD, LANES), jnp.bfloat16)],
         compiler_params=pltpu.CompilerParams(vmem_limit_bytes=24 * 2**20),
     )(pair, pick, *arrived)
 
@@ -320,8 +345,8 @@
     outs = adapter_output(gathered, shrink, expand, group, me)
     arrived = [outs[0]] + [xor_permute(outs[k], group, k) for k in range(1, PLANE)]
     pair = kept + unpack_scaled(pair_in, rows)
-    merged = merge_adapters(pair, pick, arrived)
-    return line_sums(merged, group, width).astype(jnp.bfloat16)
+    total = line_sums(merge_adapters(pair, pick, arrived, group), group)
+    return jnp.transpose(total, (1, 0, 2)).reshape(rows, width).astype(jnp.bfloat16)
 
 
 def shards(
@@ -330,7 +355,7 @@
     group = lax.axis_size("tp")
     rows, depth = hidden.shape
     width = down_matrix.shape[1] // group
-    if width % LANES == 0 and depth % LANES == 0 and rows <= LANES and group >= PLANE and group & (group - 1) == 0:
+    if width % (2 * LANES) == 0 and depth % LANES == 0 and rows <= LANES and group >= PLANE and group & (group - 1) == 0:
         return shards_by_blocks(
             hidden, down_matrix, shrink_matrices, expand_matrices, adapter_of_row, adapter_holder_slot
         )

time: 61.2 us -> 64.6 us (1.056)
  waiting for transfers between devices: 18.6 us -> 20.2 us
  starting transfers between devices: 17.2 us -> 18.2 us
  other arithmetic: 1.95 us -> 2.64 us
    ppermute x9 -> x10, waiting for transfers between devices: 18.6 us -> 20.2 us  [xor_permute(): return lax.ppermute(value, 'tp', [(i, i ^ offset) for i in range(group)])]
    ppermute x9 -> x10, starting transfers between devices: 9.85 us -> 10.8 us  [xor_permute(): return lax.ppermute(value, 'tp', [(i, i ^ offset) for i in range(group)])]
  transfers between devices with their start and end apart: 10 -> 11, of which waited for: 6 -> 8; matrix products, arithmetic and copies ran while one was open for 3% -> 4% of each run, Pallas kernels for 24% -> 23%
where the time goes in v22:
time: 64.6 us; the launch traced here: 64.4 us
  Pallas kernels  21.4 us (33%)
  waiting for transfers between devices  20.2 us (31%)
  starting transfers between devices  18.2 us (28%)
  other arithmetic  2.64 us (4%)
  between operations  0.91 us (1%)
  local copies, waits for them, and re-layouts  0.9 us (1%)
    ppermute x10, waiting for transfers between devices, xor_permute(): return lax.ppermute(value, 'tp', [(i, i ^ offset) for i in range(group)])  20.2 us
    pallas_call x3, Pallas kernels, column_blocks(): pl.pallas_call(functools.partial(column_blocks_kernel, groups), out_shape...  14.8 us
    ppermute x10, starting transfers between devices, xor_permute(): return lax.ppermute(value, 'tp', [(i, i ^ offset) for i in range(group)])  10.8 us
    all_to_all x1, starting transfers between devices, shards_by_blocks(): lax.all_to_all(packed, 'tp', split_axis=0, concat_axis=0, tiled=True)  7.37 us
    pallas_call x1, Pallas kernels, adapter_output(): pl.pallas_call(functools.partial(adapter_kernel, parts), out_shape=[jax.S...  3.85 us
    pallas_call x1, Pallas kernels, pack_rows(): pl.pallas_call(functools.partial(pack_kernel, blocks, orders), out_shape=...  2.49 us
  transfers between devices with their start and end apart: 11, of which 8 were waited for; matrix products, arithmetic and copies ran while one was open for 4% of the time, Pallas kernels for 23%

profile of v22, /device:TPU:0, one launch (start us, length us, event | category | flops | bytes accessed | tf_op | source)
XLA Modules:
  0.0 64.4 jit_solution(18401994438081361996)
XLA Ops:
  0.0 2.5 %shard_map.64 = (bf16[80,4,1792]{2,1,0:T(4,128)(2,1)}, bf16[96,96]{1,0:T(8,128)(2,1)S(1)}, s32[16]{0:T(128)S(1)}, bf16[96,1792]{1,0:T(8,128)(2,1)S(1)}) custom-call(s32[1]{0:T(128)} %bitcast.2.me_ref, s32[16]{0:T(128)} %slot_hbm.1, s32[1,96]{1,0:T(1,128)} %bitcast.65, bf16[96,1792]{1,0:T(8,128)(2,1)} %hidden_hbm.1), custom_call_target="tpu_custom_call" | custom-call | tf_op jit(solution)/shard_map/pallas_call | solution.py:206
  2.5 7.4 %all-to-all-start = ((bf16[80,4,1792]{2,1,0:T(4,128)(2,1)}), bf16[80,4,1792]{2,1,0:T(4,128)(2,1)S(1)}, u32[]{:S(2)}, u32[]{:S(2)}) async-start(bf16[80,4,1792]{2,1,0:T(4,128)(2,1)} %get-tuple-element.49), calls=%async_computation | async-start | bytes 2293760 | tf_op jit(solution)/shard_map/all_to_all | solution.py:340
  9.9 9.4 %conditional.2 = (f16[1552,128]{1,0:T(8,128)(2,1)S(1)}) conditional(s32[]{:T(128)} %bitcast.4, () %tuple.19, (s32[16]{0:T(128)S(1)}, bf16[96,1792]{1,0:T(8,128)(2,1)S(1)}, bf16[1792,8192]{1,0:T(8,128)(2,1)}) %tuple.20), branch_computations={%region_0.0_spmd, %region_1.3_spmd} | conditional | flops 1581488 | bytes 7479232 | solution.py:109
  9.9 0.1 fusion.35
  10.0 4.2 %branch_1_fun.4 = f32[16,96,128]{2,1,0:T(8,128)S(1)} custom-call(s32[4]{0:T(128)S(1)} %get-tuple-element.63.order_ref, bf16[96,1792]{1,0:T(8,128)(2,1)S(1)} %get-tuple-element.24.hidden_ref, bf16[1792,8192]{1,0:T(8,128)(2,1)} %get-tuple-element.25.down_ref), custom_call_target="tpu_custom_call" | custom-call | flops 1000 | bytes 1000 | tf_op jit(solution)/shard_map/cond/branch_1_fun/pallas_call | solution.py:62
  14.2 0.5 collective-permute-start.1
  14.7 4.2 %branch_1_fun.3 = f32[16,96,128]{2,1,0:T(8,128)S(1)} custom-call(s32[4]{0:T(128)S(1)} %get-tuple-element.64.order_ref, bf16[96,1792]{1,0:T(8,128)(2,1)S(1)} %get-tuple-element.24.hidden_ref, bf16[1792,8192]{1,0:T(8,128)(2,1)} %get-tuple-element.25.down_ref), custom_call_target="tpu_custom_call" | custom-call | flops 1000 | bytes 1000 | tf_op jit(solution)/shard_map/cond/branch_1_fun/pallas_call | solution.py:62
  18.9 0.0 collective-permute-done.1
  18.9 0.2 abs_reduce_fusion
  19.1 0.2 multiply_convert_fusion
  19.3 0.1 fusion.1
  19.4 1.7 %collective-permute-start.2 = (f16[1552,128]{1,0:T(8,128)(2,1)S(1)}, f16[1552,128]{1,0:T(8,128)(2,1)S(1)}, u32[]{:S(2)}, u32[]{:S(2)}) collective-permute-start(f16[1552,128]{1,0:T(8,128)(2,1)S(1)} %get-tuple-element.75), channel_id=1, source_target_pairs={{0,2},{1,3},{2,0},{3,1},{4,6},{5,7},{6,4},{7,5},{8,10},{9,11},{10,... | collective-permute-start | bytes 1191944 | tf_op jit(solution)/shard_map/ppermute | solution.py:25
  21.1 0.6 slice.58
  22.4 8.9 %conditional.3 = (f32[16,96,128]{2,1,0:T(8,128)S(1)}) conditional(s32[]{:T(128)} %bitcast.5, () %tuple.22, (s32[16]{0:T(128)S(1)}, bf16[96,1792]{1,0:T(8,128)(2,1)S(1)}, bf16[1792,8192]{1,0:T(8,128)(2,1)}) %tuple.23), branch_computations={%region_3.4_spmd, %region_4.5_spmd} | conditional | flops 197608 | bytes 5506136 | solution.py:120
  22.4 0.1 slice.40.order_ref
  22.5 6.4 %branch_1_fun.5 = (f32[16,96,128]{2,1,0:T(8,128)S(1)}, f32[16,96,128]{2,1,0:T(8,128)S(1)}) custom-call(s32[8]{0:T(128)S(1)} %slice.40.order_ref, bf16[96,1792]{1,0:T(8,128)(2,1)S(1)} %get-tuple-element.27.hidden_ref, bf16[1792,8192]{1,0:T(8,128)(2,1)} %get-tuple-element.28.down_ref), custom_call_target="tpu_custom_call" | custom-call | flops 1000 | bytes 1000 | tf_op jit(solution)/shard_map/cond/branch_1_fun/pallas_call | solution.py:62
  28.9 0.1 collective-permute-start
  29.0 2.2 %collective-permute-done = f32[16,96,128]{2,1,0:T(8,128)S(1)} collective-permute-done((f32[16,96,128]{2,1,0:T(8,128)S(1)}, f32[16,96,128]{2,1,0:T(8,128)S(1)}, u32[]{:S(2)}, u32[]{:S(2)}) %collective-permute-start) | collective-permute-done | bytes 786464 | tf_op jit(solution)/shard_map/cond/branch_1_fun/ppermute | solution.py:25
  31.2 0.1 add.47
  31.3 4.6 %collective-permute-done.2 = f16[1552,128]{1,0:T(8,128)(2,1)S(1)} collective-permute-done((f16[1552,128]{1,0:T(8,128)(2,1)S(1)}, f16[1552,128]{1,0:T(8,128)(2,1)S(1)}, u32[]{:S(2)}, u32[]{:S(2)}) %collective-permute-start.2) | collective-permute-done | bytes 397344 | tf_op jit(solution)/shard_map/ppermute | solution.py:25
  35.9 0.1 slice.73
  36.0 0.0 all-to-all-done.rows_ref
  36.0 3.9 %shard_map.65 = (bf16[16,24,128]{2,1,0:T(8,128)(2,1)S(1)}, bf16[16,24,128]{2,1,0:T(8,128)(2,1)S(1)}, bf16[16,24,128]{2,1,0:T(8,128)(2,1)S(1)}, bf16[16,24,128]{2,1,0:T(8,128)(2,1)S(1)}) custom-call(s32[1]{0:T(128)} %bitcast.2.me_ref, bf16[80,4,1792]{2,1,0:T(4,128)(2,1)S(1)} %all-to-all-done.rows_ref, bf16[64,8192]{1,0:T(8,128)(2,1)} %bitcast.55, ...), custom_call_target="tpu_custom_call" | custom-call | tf_op jit(solution)/shard_map/pallas_call | solution.py:271
  39.9 0.1 collective-permute-start.3
  40.0 2.0 %collective-permute-start.4 = (bf16[16,24,128]{2,1,0:T(8,128)(2,1)S(1)}, bf16[16,24,128]{2,1,0:T(8,128)(2,1)S(1)}, u32[]{:S(2)}, u32[]{:S(2)}) collective-permute-start(bf16[16,24,128]{2,1,0:T(8,128)(2,1)S(1)} %get-tuple-element.53), channel_id=1, source_target_pairs={{0,2},{1,3},{2,0},{3,1},{4,6},{5,7},{6,4},{7,5},{8,10},{9,11},{10,... | collective-permute-start | bytes 294920 | tf_op jit(solution)/shard_map/ppermute | solution.py:25
  42.0 0.1 collective-permute-start.5
  42.0 0.2 fusion.2.pair_ref
  42.2 0.0 collective-permute-done.3.refs_1_
  42.2 3.5 %collective-permute-done.4.refs_2_ = bf16[16,24,128]{2,1,0:T(8,128)(2,1)S(1)} collective-permute-done((bf16[16,24,128]{2,1,0:T(8,128)(2,1)S(1)}, bf16[16,24,128]{2,1,0:T(8,128)(2,1)S(1)}, u32[]{:S(2)}, u32[]{:S(2)}) %collective-permute-start.4) | collective-permute-done | bytes 98336 | tf_op jit(solution)/shard_map/ppermute | solution.py:25
  45.7 1.4 %collective-permute-done.5.refs_3_ = bf16[16,24,128]{2,1,0:T(8,128)(2,1)S(1)} collective-permute-done((bf16[16,24,128]{2,1,0:T(8,128)(2,1)S(1)}, bf16[16,24,128]{2,1,0:T(8,128)(2,1)S(1)}, u32[]{:S(2)}, u32[]{:S(2)}) %collective-permute-start.5) | collective-permute-done | bytes 98336 | tf_op jit(solution)/shard_map/ppermute | solution.py:25
  47.1 0.3 shard_map.66
  47.4 0.1 abs_reduce_fusion.2
  47.6 0.1 abs_reduce_fusion.1
  47.7 0.1 multiply_convert_fusion.1
  47.9 3.7 %collective-permute-start.8 = (f16[400,128]{1,0:T(8,128)(2,1)S(1)}, f16[400,128]{1,0:T(8,128)(2,1)S(1)}, u32[]{:S(2)}, u32[]{:S(2)}) collective-permute-start(f16[400,128]{1,0:T(8,128)(2,1)S(1)} %fusion.10), channel_id=1, source_target_pairs={{0,8},{1,9},{2,10},{3,11},{4,12},{5,13},{6,14},{7,15},{8,0},{9,1},... | collective-permute-start | bytes 307208 | tf_op jit(solution)/shard_map/ppermute | solution.py:25
  51.6 0.2 collective-permute-start.6
  51.8 5.4 %collective-permute-done.8 = f16[400,128]{1,0:T(8,128)(2,1)S(1)} collective-permute-done((f16[400,128]{1,0:T(8,128)(2,1)S(1)}, f16[400,128]{1,0:T(8,128)(2,1)S(1)}, u32[]{:S(2)}, u32[]{:S(2)}) %collective-permute-start.8) | collective-permute-done | bytes 102432 | tf_op jit(solution)/shard_map/ppermute | solution.py:25
  57.3 0.1 fusion.5
  57.3 0.1 abs_reduce_fusion.3
  57.5 0.1 multiply_convert_fusion.3
  57.6 0.1 collective-permute-start.9
  57.7 0.3 collective-permute-done.6
  58.0 0.1 fusion.6
  58.1 0.1 abs_reduce_fusion.4
  58.2 0.1 multiply_convert_fusion.4
  58.3 2.3 %collective-permute-start.7 = (f16[208,128]{1,0:T(8,128)(2,1)S(1)}, f16[208,128]{1,0:T(8,128)(2,1)S(1)}, u32[]{:S(2)}, u32[]{:S(2)}) collective-permute-start(f16[208,128]{1,0:T(8,128)(2,1)S(1)} %fusion.13), channel_id=1, source_target_pairs={{0,8},{1,9},{2,10},{3,11},{4,12},{5,13},{6,14},{7,15},{8,0},{9,1},... | collective-permute-start | bytes 159752 | tf_op jit(solution)/shard_map/ppermute | solution.py:25
  60.6 1.7 %collective-permute-done.9 = f16[208,128]{1,0:T(8,128)(2,1)S(1)} collective-permute-done((f16[208,128]{1,0:T(8,128)(2,1)S(1)}, f16[208,128]{1,0:T(8,128)(2,1)S(1)}, u32[]{:S(2)}, u32[]{:S(2)}) %collective-permute-start.9) | collective-permute-done | bytes 53280 | tf_op jit(solution)/shard_map/ppermute | solution.py:25
  62.4 0.1 fusion.11
  62.5 1.1 %collective-permute-done.7 = f16[208,128]{1,0:T(8,128)(2,1)S(1)} collective-permute-done((f16[208,128]{1,0:T(8,128)(2,1)S(1)}, f16[208,128]{1,0:T(8,128)(2,1)S(1)}, u32[]{:S(2)}, u32[]{:S(2)}) %collective-permute-start.7) | collective-permute-done | bytes 53280 | tf_op jit(solution)/shard_map/ppermute | solution.py:25
  63.7 0.1 fusion.12
  63.7 0.6 %copy_bitcast_fusion = bf16[96,512]{1,0:T(8,128)(2,1)} fusion(bf16[2,96,128]{2,1,0:T(8,128)(2,1)S(1)} %fusion.11, bf16[2,96,128]{2,1,0:T(8,128)(2,1)S(1)} %fusion.12), kind=kLoop, calls=%fused_computation.26 | loop fusion | flops 49152 | bytes 196608 | tf_op jit(solution)/shard_map/convert_element_type | solution.py:349
  (18 shorter events, 0.3 us)
Async XLA Ops:
  2.5 33.5 %all-to-all-start = ((bf16[80,4,1792]{2,1,0:T(4,128)(2,1)}), bf16[80,4,1792]{2,1,0:T(4,128)(2,1)S(1)}, u32[]{:S(2)}, u32[]{:S(2)}) async-start(bf16[80,4,1792]{2,1,0:T(4,128)(2,1)} %get-tuple-element.49), calls=%async_computation | async-start | bytes 2293760 | tf_op jit(solution)/shard_map/all_to_all | solution.py:340
  14.2 4.7 %collective-permute-start.1 = (f32[16,96,128]{2,1,0:T(8,128)S(1)}, f32[16,96,128]{2,1,0:T(8,128)S(1)}, u32[]{:S(2)}, u32[]{:S(2)}) collective-permute-start(f32[16,96,128]{2,1,0:T(8,128)S(1)} %branch_1_fun.4), channel_id=1, source_target_pairs={{0,1},{1,0},{2,3},{3,2},{4,5},{5,4},{6,7},{7,6},{8,9},{9,8},{10,11... | collective-permute-start | bytes 2359304 | tf_op jit(solution)/shard_map/cond/branch_1_fun/ppermute | solution.py:25
  19.4 16.5 %collective-permute-start.2 = (f16[1552,128]{1,0:T(8,128)(2,1)S(1)}, f16[1552,128]{1,0:T(8,128)(2,1)S(1)}, u32[]{:S(2)}, u32[]{:S(2)}) collective-permute-start(f16[1552,128]{1,0:T(8,128)(2,1)S(1)} %get-tuple-element.75), channel_id=1, source_target_pairs={{0,2},{1,3},{2,0},{3,1},{4,6},{5,7},{6,4},{7,5},{8,10},{9,11},{10,... | collective-permute-start | bytes 1191944 | tf_op jit(solution)/shard_map/ppermute | solution.py:25
  28.9 2.4 %collective-permute-start = (f32[16,96,128]{2,1,0:T(8,128)S(1)}, f32[16,96,128]{2,1,0:T(8,128)S(1)}, u32[]{:S(2)}, u32[]{:S(2)}) collective-permute-start(f32[16,96,128]{2,1,0:T(8,128)S(1)} %get-tuple-element.30), channel_id=1, source_target_pairs={{0,1},{1,0},{2,3},{3,2},{4,5},{5,4},{6,7},{7,6},{8,9},{9,8},{10,11... | collective-permute-start | bytes 2359304 | tf_op jit(solution)/shard_map/cond/branch_1_fun/ppermute | solution.py:25
  39.9 2.4 %collective-permute-start.3 = (bf16[16,24,128]{2,1,0:T(8,128)(2,1)S(1)}, bf16[16,24,128]{2,1,0:T(8,128)(2,1)S(1)}, u32[]{:S(2)}, u32[]{:S(2)}) collective-permute-start(bf16[16,24,128]{2,1,0:T(8,128)(2,1)S(1)} %get-tuple-element.52), channel_id=1, source_target_pairs={{0,1},{1,0},{2,3},{3,2},{4,5},{5,4},{6,7},{7,6},{8,9},{9,8},{10,11... | collective-permute-start | bytes 294920 | tf_op jit(solution)/shard_map/ppermute | solution.py:25
  40.0 5.7 %collective-permute-start.4 = (bf16[16,24,128]{2,1,0:T(8,128)(2,1)S(1)}, bf16[16,24,128]{2,1,0:T(8,128)(2,1)S(1)}, u32[]{:S(2)}, u32[]{:S(2)}) collective-permute-start(bf16[16,24,128]{2,1,0:T(8,128)(2,1)S(1)} %get-tuple-element.53), channel_id=1, source_target_pairs={{0,2},{1,3},{2,0},{3,1},{4,6},{5,7},{6,4},{7,5},{8,10},{9,11},{10,... | collective-permute-start | bytes 294920 | tf_op jit(solution)/shard_map/ppermute | solution.py:25
  42.0 5.2 %collective-permute-start.5 = (bf16[16,24,128]{2,1,0:T(8,128)(2,1)S(1)}, bf16[16,24,128]{2,1,0:T(8,128)(2,1)S(1)}, u32[]{:S(2)}, u32[]{:S(2)}) collective-permute-start(bf16[16,24,128]{2,1,0:T(8,128)(2,1)S(1)} %get-tuple-element.54), channel_id=1, source_target_pairs={{0,3},{1,2},{2,1},{3,0},{4,7},{5,6},{6,5},{7,4},{8,11},{9,10},{10,... | collective-permute-start | bytes 294920 | tf_op jit(solution)/shard_map/ppermute | solution.py:25
  47.9 9.3 %collective-permute-start.8 = (f16[400,128]{1,0:T(8,128)(2,1)S(1)}, f16[400,128]{1,0:T(8,128)(2,1)S(1)}, u32[]{:S(2)}, u32[]{:S(2)}) collective-permute-start(f16[400,128]{1,0:T(8,128)(2,1)S(1)} %fusion.10), channel_id=1, source_target_pairs={{0,8},{1,9},{2,10},{3,11},{4,12},{5,13},{6,14},{7,15},{8,0},{9,1},... | collective-permute-start | bytes 307208 | tf_op jit(solution)/shard_map/ppermute | solution.py:25
  51.6 6.3 %collective-permute-start.6 = (f16[400,128]{1,0:T(8,128)(2,1)S(1)}, f16[400,128]{1,0:T(8,128)(2,1)S(1)}, u32[]{:S(2)}, u32[]{:S(2)}) collective-permute-start(f16[400,128]{1,0:T(8,128)(2,1)S(1)} %fusion.9), channel_id=1, source_target_pairs={{0,4},{1,5},{2,6},{3,7},{4,0},{5,1},{6,2},{7,3},{8,12},{9,13},{10,... | collective-permute-start | bytes 307208 | tf_op jit(solution)/shard_map/ppermute | solution.py:25
  57.6 4.8 %collective-permute-start.9 = (f16[208,128]{1,0:T(8,128)(2,1)S(1)}, f16[208,128]{1,0:T(8,128)(2,1)S(1)}, u32[]{:S(2)}, u32[]{:S(2)}) collective-permute-start(f16[208,128]{1,0:T(8,128)(2,1)S(1)} %fusion.14), channel_id=1, source_target_pairs={{0,4},{1,5},{2,6},{3,7},{4,0},{5,1},{6,2},{7,3},{8,12},{9,13},{10,... | collective-permute-start | bytes 159752 | tf_op jit(solution)/shard_map/ppermute | solution.py:25
  58.3 5.3 %collective-permute-start.7 = (f16[208,128]{1,0:T(8,128)(2,1)S(1)}, f16[208,128]{1,0:T(8,128)(2,1)S(1)}, u32[]{:S(2)}, u32[]{:S(2)}) collective-permute-start(f16[208,128]{1,0:T(8,128)(2,1)S(1)} %fusion.13), channel_id=1, source_target_pairs={{0,8},{1,9},{2,10},{3,11},{4,12},{5,13},{6,14},{7,15},{8,0},{9,1},... | collective-permute-start | bytes 159752 | tf_op jit(solution)/shard_map/ppermute | solution.py:25

commit v23 on v17

--- a/solution.py
+++ b/solution.py
@@ -141,14 +141,16 @@
     slot_hbm,
     adapter_hbm,
     hidden_hbm,
-    packed_ref,
+    packed_hbm,
     pick_ref,
     order_ref,
     kept_ref,
     slot_ref,
     adapter_ref,
     hidden_ref,
+    packed_ref,
     sems,
+    out_sems,
 ):
     rows = hidden_ref.shape[0]
     group = slot_ref.shape[0]
@@ -171,16 +173,26 @@
     first = jnp.sum((adapter < ids).astype(jnp.int32), axis=1, keepdims=True)
     shift = jnp.where(adapter == ids, slots * (blocks * BLOCK) - first, 0)
     place = jnp.sum(shift, axis=0, keepdims=True) + lax.broadcasted_iota(jnp.int32, (1, rows), 1)
-    spots = lax.broadcasted_iota(jnp.int32, (group * blocks * BLOCK, rows), 0)
-    pick = jnp.where(spots == place, 1.0, 0.0).astype(jnp.bfloat16)
+    copies[2].wait()
+    pieces = out_sems.shape[0]
+    size = packed_ref.shape[0] // pieces
+    outs = []
+    for piece in range(pieces):
+        spots = lax.broadcasted_iota(jnp.int32, (size * BLOCK, rows), 0) + piece * size * BLOCK
+        pick = jnp.where(spots == place, 1.0, 0.0).astype(jnp.bfloat16)
+        packed = jnp.dot(pick, hidden_ref[...], preferred_element_type=jnp.float32)
+        part = pl.ds(piece * size, size)
+        packed_ref[part] = packed.astype(jnp.bfloat16).reshape(size, BLOCK, packed.shape[1])
+        out = pltpu.make_async_copy(packed_ref.at[part], packed_hbm.at[part], out_sems.at[piece])
+        out.start()
+        outs.append(out)
+    kept_ref[...] = hidden_ref[...]
     for k in range(PLANE):
         line = lax.broadcasted_iota(jnp.int32, (HELD, rows), 0)
         mine = (line + (me_ref[0] ^ k) * (blocks * BLOCK) == place) & (line < blocks * BLOCK)
         pick_ref[k * HELD : (k + 1) * HELD] = jnp.where(mine, 1.0, 0.0).astype(jnp.bfloat16)
-    copies[2].wait()
-    packed = jnp.dot(pick, hidden_ref[...], preferred_element_type=jnp.float32)
-    packed_ref[...] = packed.astype(jnp.bfloat16).reshape(packed_ref.shape)
-    kept_ref[...] = hidden_ref[...]
+    for out in outs:
+        out.wait()
 
 
 def pack_rows(hidden, adapter_of_row, adapter_holder_slot, me, orders):
@@ -199,12 +211,14 @@
             jax.ShapeDtypeStruct((rows, depth), jnp.bfloat16),
         ),
         in_specs=[smem, anywhere, anywhere, anywhere],
-        out_specs=(vmem, vmem, smem, vmem),
+        out_specs=(anywhere, vmem, smem, vmem),
         scratch_shapes=[
             pltpu.SMEM((group,), jnp.int32),
             pltpu.VMEM((1, rows), jnp.int32),
             pltpu.VMEM((rows, depth), jnp.bfloat16),
+            pltpu.VMEM((group * blocks, BLOCK, depth), jnp.bfloat16),
             pltpu.SemaphoreType.DMA((3,)),
+            pltpu.SemaphoreType.DMA((4,)),
         ],
         compiler_params=pltpu.CompilerParams(vmem_limit_bytes=24 * 2**20),
     )(me.reshape(1), in_hbm(adapter_holder_slot), in_hbm(adapter_of_row.reshape(1, rows)), in_hbm(hidden))
@@ -212,7 +226,7 @@
 
 def adapter_kernel(parts, me_ref, rows_ref, expand_hbm, shrink_hbm, *refs):
     out_refs = refs[:PLANE]
-    shrink_ref, expand_ref, total_ref, sems, expand_sem = refs[PLANE:]
+    shrink_ref, expand_ref, total_ref, own_ref, sems, expand_sem = refs[PLANE:]
     me = me_ref[0]
     group, _, depth = shrink_ref.shape
     blocks = MOST // BLOCK
@@ -226,12 +240,14 @@
         copy(source).start()
     expand_copy = pltpu.make_async_copy(expand_hbm, expand_ref, expand_sem)
     expand_copy.start()
+    for source in range(group):
+        own = rows_ref[source * blocks : (source + 1) * blocks]
+        own_ref[source, :MOST] = own.reshape(MOST, depth)
     total = jnp.zeros((MOST, total_ref.shape[1]), jnp.float32)
     for source in range(group):
         copy(source).wait()
-        own = rows_ref[source * blocks : (source + 1) * blocks].reshape(MOST, depth)
         total += lax.dot_general(
-            own, shrink_ref[source], (((1,), (1,)), ((), ())), preferred_element_type=jnp.float32
+            own_ref[source, :MOST], shrink_ref[source], (((1,), (1,)), ((), ())), preferred_element_type=jnp.float32
         )
     total_ref[...] = jnp.zeros_like(total_ref)
     total_ref[:MOST] = total
@@ -269,6 +285,7 @@
             pltpu.VMEM((group, rank, depth), jnp.bfloat16),
             pltpu.VMEM((rank, model_width), jnp.bfloat16),
             pltpu.VMEM((HELD, rank), jnp.float32),
+            pltpu.VMEM((group, 2 * 16, depth), jnp.bfloat16),
             pltpu.SemaphoreType.DMA((group,)),
             pltpu.SemaphoreType.DMA,
         ],

time: 61.2 us -> 61.6 us (level)
  no operation moved by 1% of the time
where the time goes in v23:
time: 61.6 us; the launch traced here: 61.3 us
  Pallas kernels  21.8 us (35%)
  waiting for transfers between devices  18.6 us (30%)
  starting transfers between devices  17.2 us (28%)
  other arithmetic  1.95 us (3%)
  local copies, waits for them, and re-layouts  0.9 us (1%)
  between operations  0.83 us (1%)
    ppermute x9, waiting for transfers between devices, xor_permute(): return lax.ppermute(value, 'tp', [(i, i ^ offset) for i in range(group)])  18.6 us
    pallas_call x3, Pallas kernels, column_blocks(): pl.pallas_call(functools.partial(column_blocks_kernel, groups), out_shape...  14.8 us
    ppermute x9, starting transfers between devices, xor_permute(): return lax.ppermute(value, 'tp', [(i, i ^ offset) for i in range(group)])  9.86 us
    all_to_all x1, starting transfers between devices, shards_by_blocks(): lax.all_to_all(packed, 'tp', split_axis=0, concat_axis=0, tiled=True)  7.37 us
    pallas_call x1, Pallas kernels, adapter_output(): pl.pallas_call(functools.partial(adapter_kernel, parts), out_shape=[jax.S...  3.8 us
    pallas_call x1, Pallas kernels, pack_rows(): pl.pallas_call(functools.partial(pack_kernel, blocks, orders), out_shape=...  2.9 us
  transfers between devices with their start and end apart: 10, of which 6 were waited for; matrix products, arithmetic and copies ran while one was open for 3% of the time, Pallas kernels for 24%

profile of v23, /device:TPU:0, one launch (start us, length us, event | category | flops | bytes accessed | tf_op | source)
XLA Modules:
  0.0 61.3 jit_solution(14124036435690019907)
XLA Ops:
  0.0 2.9 %shard_map.64 = (bf16[80,4,1792]{2,1,0:T(4,128)(2,1)}, bf16[96,96]{1,0:T(8,128)(2,1)S(1)}, s32[16]{0:T(128)S(1)}, bf16[96,1792]{1,0:T(8,128)(2,1)S(1)}) custom-call(s32[1]{0:T(128)} %bitcast.2.me_ref, s32[16]{0:T(128)} %slot_hbm.1, s32[1,96]{1,0:T(1,128)} %bitcast.56, bf16[96,1792]{1,0:T(8,128)(2,1)} %hidden_hbm.1), custom_call_target="tpu_custom_call" | custom-call | tf_op jit(solution)/shard_map/pallas_call | solution.py:205
  2.9 7.4 %all-to-all-start = ((bf16[80,4,1792]{2,1,0:T(4,128)(2,1)}), bf16[80,4,1792]{2,1,0:T(4,128)(2,1)S(1)}, u32[]{:S(2)}, u32[]{:S(2)}) async-start(bf16[80,4,1792]{2,1,0:T(4,128)(2,1)} %get-tuple-element.45), calls=%async_computation | async-start | bytes 2293760 | tf_op jit(solution)/shard_map/all_to_all | solution.py:332
  10.3 9.5 %conditional.2 = (f16[1552,128]{1,0:T(8,128)(2,1)S(1)}) conditional(s32[]{:T(128)} %bitcast.4, () %tuple.19, (s32[16]{0:T(128)S(1)}, bf16[96,1792]{1,0:T(8,128)(2,1)S(1)}, bf16[1792,8192]{1,0:T(8,128)(2,1)}) %tuple.20), branch_computations={%region_0.0_spmd, %region_1.3_spmd} | conditional | flops 1581488 | bytes 7479232 | solution.py:109
  10.3 0.1 fusion.29
  10.4 4.2 %branch_1_fun.4 = f32[16,96,128]{2,1,0:T(8,128)S(1)} custom-call(s32[4]{0:T(128)S(1)} %get-tuple-element.58.order_ref, bf16[96,1792]{1,0:T(8,128)(2,1)S(1)} %get-tuple-element.24.hidden_ref, bf16[1792,8192]{1,0:T(8,128)(2,1)} %get-tuple-element.25.down_ref), custom_call_target="tpu_custom_call" | custom-call | flops 1000 | bytes 1000 | tf_op jit(solution)/shard_map/cond/branch_1_fun/pallas_call | solution.py:62
  14.6 0.5 collective-permute-start.1
  15.1 4.2 %branch_1_fun.3 = f32[16,96,128]{2,1,0:T(8,128)S(1)} custom-call(s32[4]{0:T(128)S(1)} %get-tuple-element.59.order_ref, bf16[96,1792]{1,0:T(8,128)(2,1)S(1)} %get-tuple-element.24.hidden_ref, bf16[1792,8192]{1,0:T(8,128)(2,1)} %get-tuple-element.25.down_ref), custom_call_target="tpu_custom_call" | custom-call | flops 1000 | bytes 1000 | tf_op jit(solution)/shard_map/cond/branch_1_fun/pallas_call | solution.py:62
  19.3 0.0 collective-permute-done.1
  19.3 0.2 abs_reduce_fusion
  19.5 0.2 multiply_convert_fusion
  19.7 0.1 fusion.1
  19.8 1.7 %collective-permute-start.2 = (f16[1552,128]{1,0:T(8,128)(2,1)S(1)}, f16[1552,128]{1,0:T(8,128)(2,1)S(1)}, u32[]{:S(2)}, u32[]{:S(2)}) collective-permute-start(f16[1552,128]{1,0:T(8,128)(2,1)S(1)} %get-tuple-element.71), channel_id=1, source_target_pairs={{0,2},{1,3},{2,0},{3,1},{4,6},{5,7},{6,4},{7,5},{8,10},{9,11},{10,... | collective-permute-start | bytes 1191944 | tf_op jit(solution)/shard_map/ppermute | solution.py:25
  21.5 0.6 slice.52
  22.8 9.0 %conditional.3 = (f32[16,96,128]{2,1,0:T(8,128)S(1)}) conditional(s32[]{:T(128)} %bitcast.5, () %tuple.22, (s32[16]{0:T(128)S(1)}, bf16[96,1792]{1,0:T(8,128)(2,1)S(1)}, bf16[1792,8192]{1,0:T(8,128)(2,1)}) %tuple.23), branch_computations={%region_3.4_spmd, %region_4.5_spmd} | conditional | flops 197608 | bytes 5506136 | solution.py:120
  22.8 0.1 slice.36.order_ref
  22.9 6.4 %branch_1_fun.5 = (f32[16,96,128]{2,1,0:T(8,128)S(1)}, f32[16,96,128]{2,1,0:T(8,128)S(1)}) custom-call(s32[8]{0:T(128)S(1)} %slice.36.order_ref, bf16[96,1792]{1,0:T(8,128)(2,1)S(1)} %get-tuple-element.27.hidden_ref, bf16[1792,8192]{1,0:T(8,128)(2,1)} %get-tuple-element.28.down_ref), custom_call_target="tpu_custom_call" | custom-call | flops 1000 | bytes 1000 | tf_op jit(solution)/shard_map/cond/branch_1_fun/pallas_call | solution.py:62
  29.3 0.1 collective-permute-start
  29.4 2.2 %collective-permute-done = f32[16,96,128]{2,1,0:T(8,128)S(1)} collective-permute-done((f32[16,96,128]{2,1,0:T(8,128)S(1)}, f32[16,96,128]{2,1,0:T(8,128)S(1)}, u32[]{:S(2)}, u32[]{:S(2)}) %collective-permute-start) | collective-permute-done | bytes 786464 | tf_op jit(solution)/shard_map/cond/branch_1_fun/ppermute | solution.py:25
  31.6 0.1 add.39
  31.7 4.6 %collective-permute-done.2 = f16[1552,128]{1,0:T(8,128)(2,1)S(1)} collective-permute-done((f16[1552,128]{1,0:T(8,128)(2,1)S(1)}, f16[1552,128]{1,0:T(8,128)(2,1)S(1)}, u32[]{:S(2)}, u32[]{:S(2)}) %collective-permute-start.2) | collective-permute-done | bytes 397344 | tf_op jit(solution)/shard_map/ppermute | solution.py:25
  36.3 0.1 slice.65
  36.4 0.0 all-to-all-done.rows_ref
  36.4 3.8 %shard_map.65 = (bf16[16,24,128]{2,1,0:T(8,128)(2,1)S(1)}, bf16[16,24,128]{2,1,0:T(8,128)(2,1)S(1)}, bf16[16,24,128]{2,1,0:T(8,128)(2,1)S(1)}, bf16[16,24,128]{2,1,0:T(8,128)(2,1)S(1)}) custom-call(s32[1]{0:T(128)} %bitcast.2.me_ref, bf16[80,4,1792]{2,1,0:T(4,128)(2,1)S(1)} %all-to-all-done.rows_ref, bf16[64,8192]{1,0:T(8,128)(2,1)} %bitcast.48, ...), custom_call_target="tpu_custom_call" | custom-call | tf_op jit(solution)/shard_map/pallas_call | solution.py:274
  40.2 0.1 collective-permute-start.3
  40.3 2.0 %collective-permute-start.4 = (bf16[16,24,128]{2,1,0:T(8,128)(2,1)S(1)}, bf16[16,24,128]{2,1,0:T(8,128)(2,1)S(1)}, u32[]{:S(2)}, u32[]{:S(2)}) collective-permute-start(bf16[16,24,128]{2,1,0:T(8,128)(2,1)S(1)} %get-tuple-element.49), channel_id=1, source_target_pairs={{0,2},{1,3},{2,0},{3,1},{4,6},{5,7},{6,4},{7,5},{8,10},{9,11},{10,... | collective-permute-start | bytes 294920 | tf_op jit(solution)/shard_map/ppermute | solution.py:25
  42.3 0.1 collective-permute-start.5
  42.4 0.2 fusion.2.pair_ref
  42.6 0.0 collective-permute-done.3.refs_1_
  42.6 3.5 %collective-permute-done.4.refs_2_ = bf16[16,24,128]{2,1,0:T(8,128)(2,1)S(1)} collective-permute-done((bf16[16,24,128]{2,1,0:T(8,128)(2,1)S(1)}, bf16[16,24,128]{2,1,0:T(8,128)(2,1)S(1)}, u32[]{:S(2)}, u32[]{:S(2)}) %collective-permute-start.4) | collective-permute-done | bytes 98336 | tf_op jit(solution)/shard_map/ppermute | solution.py:25
  46.0 1.4 %collective-permute-done.5.refs_3_ = bf16[16,24,128]{2,1,0:T(8,128)(2,1)S(1)} collective-permute-done((bf16[16,24,128]{2,1,0:T(8,128)(2,1)S(1)}, bf16[16,24,128]{2,1,0:T(8,128)(2,1)S(1)}, u32[]{:S(2)}, u32[]{:S(2)}) %collective-permute-start.5) | collective-permute-done | bytes 98336 | tf_op jit(solution)/shard_map/ppermute | solution.py:25
  47.5 0.3 shard_map.66
  47.8 0.2 abs_reduce_fusion.3
  48.0 0.1 multiply_convert_fusion.3
  48.1 3.7 %collective-permute-start.7 = (f16[400,128]{1,0:T(8,128)(2,1)S(1)}, f16[400,128]{1,0:T(8,128)(2,1)S(1)}, u32[]{:S(2)}, u32[]{:S(2)}) collective-permute-start(f16[400,128]{1,0:T(8,128)(2,1)S(1)} %fusion.10), channel_id=1, source_target_pairs={{0,8},{1,9},{2,10},{3,11},{4,12},{5,13},{6,14},{7,15},{8,0},{9,1},... | collective-permute-start | bytes 307208 | tf_op jit(solution)/shard_map/ppermute | solution.py:25
  51.9 0.2 collective-permute-start.6
  52.1 1.4 %collective-permute-start.8 = (f16[400,128]{1,0:T(8,128)(2,1)S(1)}, f16[400,128]{1,0:T(8,128)(2,1)S(1)}, u32[]{:S(2)}, u32[]{:S(2)}) collective-permute-start(f16[400,128]{1,0:T(8,128)(2,1)S(1)} %fusion.11), channel_id=1, source_target_pairs={{0,12},{1,13},{2,14},{3,15},{4,8},{5,9},{6,10},{7,11},{8,4},{9,5},... | collective-permute-start | bytes 307208 | tf_op jit(solution)/shard_map/ppermute | solution.py:25
  53.6 4.7 %collective-permute-done.7 = f16[400,128]{1,0:T(8,128)(2,1)S(1)} collective-permute-done((f16[400,128]{1,0:T(8,128)(2,1)S(1)}, f16[400,128]{1,0:T(8,128)(2,1)S(1)}, u32[]{:S(2)}, u32[]{:S(2)}) %collective-permute-start.7) | collective-permute-done | bytes 102432 | tf_op jit(solution)/shard_map/ppermute | solution.py:25
  58.2 2.2 %collective-permute-done.6 = f16[400,128]{1,0:T(8,128)(2,1)S(1)} collective-permute-done((f16[400,128]{1,0:T(8,128)(2,1)S(1)}, f16[400,128]{1,0:T(8,128)(2,1)S(1)}, u32[]{:S(2)}, u32[]{:S(2)}) %collective-permute-start.6) | collective-permute-done | bytes 102432 | tf_op jit(solution)/shard_map/ppermute | solution.py:25
  60.5 0.0 collective-permute-done.8
  60.5 0.8 %copy_bitcast_fusion = bf16[96,512]{1,0:T(8,128)(2,1)} fusion(f16[4,96,128]{2,1,0:T(8,128)(2,1)S(1)} %bitcast.54, f16[4,96,128]{2,1,0:T(8,128)(2,1)S(1)} %bitcast.51, f16[4,96,128]{2,1,0:T(8,128)(2,1)S(1)} %bitcast.52, f32[16,96,128]{2,1,0:T(8,128)S(1)} %shard_map.66, f32[96]{0:T(128)S(1)} %fusion.16, f32[96]{0:T(128)S(1)} %fusion.20, f32[96]{0:T(128)S(1)} %fusion.24), kind=kLoop, calls=%fused_computation.31 | loop fusion | flops 491520 | bytes 591360 | tf_op jit(solution)/shard_map/convert_element_type | solution.py:341
  (13 shorter events, 0.2 us)
Async XLA Ops:
  2.9 33.5 %all-to-all-start = ((bf16[80,4,1792]{2,1,0:T(4,128)(2,1)}), bf16[80,4,1792]{2,1,0:T(4,128)(2,1)S(1)}, u32[]{:S(2)}, u32[]{:S(2)}) async-start(bf16[80,4,1792]{2,1,0:T(4,128)(2,1)} %get-tuple-element.45), calls=%async_computation | async-start | bytes 2293760 | tf_op jit(solution)/shard_map/all_to_all | solution.py:332
  14.6 4.7 %collective-permute-start.1 = (f32[16,96,128]{2,1,0:T(8,128)S(1)}, f32[16,96,128]{2,1,0:T(8,128)S(1)}, u32[]{:S(2)}, u32[]{:S(2)}) collective-permute-start(f32[16,96,128]{2,1,0:T(8,128)S(1)} %branch_1_fun.4), channel_id=1, source_target_pairs={{0,1},{1,0},{2,3},{3,2},{4,5},{5,4},{6,7},{7,6},{8,9},{9,8},{10,11... | collective-permute-start | bytes 2359304 | tf_op jit(solution)/shard_map/cond/branch_1_fun/ppermute | solution.py:25
  19.8 16.5 %collective-permute-start.2 = (f16[1552,128]{1,0:T(8,128)(2,1)S(1)}, f16[1552,128]{1,0:T(8,128)(2,1)S(1)}, u32[]{:S(2)}, u32[]{:S(2)}) collective-permute-start(f16[1552,128]{1,0:T(8,128)(2,1)S(1)} %get-tuple-element.71), channel_id=1, source_target_pairs={{0,2},{1,3},{2,0},{3,1},{4,6},{5,7},{6,4},{7,5},{8,10},{9,11},{10,... | collective-permute-start | bytes 1191944 | tf_op jit(solution)/shard_map/ppermute | solution.py:25
  29.3 2.4 %collective-permute-start = (f32[16,96,128]{2,1,0:T(8,128)S(1)}, f32[16,96,128]{2,1,0:T(8,128)S(1)}, u32[]{:S(2)}, u32[]{:S(2)}) collective-permute-start(f32[16,96,128]{2,1,0:T(8,128)S(1)} %get-tuple-element.30), channel_id=1, source_target_pairs={{0,1},{1,0},{2,3},{3,2},{4,5},{5,4},{6,7},{7,6},{8,9},{9,8},{10,11... | collective-permute-start | bytes 2359304 | tf_op jit(solution)/shard_map/cond/branch_1_fun/ppermute | solution.py:25
  40.2 2.3 %collective-permute-start.3 = (bf16[16,24,128]{2,1,0:T(8,128)(2,1)S(1)}, bf16[16,24,128]{2,1,0:T(8,128)(2,1)S(1)}, u32[]{:S(2)}, u32[]{:S(2)}) collective-permute-start(bf16[16,24,128]{2,1,0:T(8,128)(2,1)S(1)} %get-tuple-element.48), channel_id=1, source_target_pairs={{0,1},{1,0},{2,3},{3,2},{4,5},{5,4},{6,7},{7,6},{8,9},{9,8},{10,11... | collective-permute-start | bytes 294920 | tf_op jit(solution)/shard_map/ppermute | solution.py:25
  40.3 5.7 %collective-permute-start.4 = (bf16[16,24,128]{2,1,0:T(8,128)(2,1)S(1)}, bf16[16,24,128]{2,1,0:T(8,128)(2,1)S(1)}, u32[]{:S(2)}, u32[]{:S(2)}) collective-permute-start(bf16[16,24,128]{2,1,0:T(8,128)(2,1)S(1)} %get-tuple-element.49), channel_id=1, source_target_pairs={{0,2},{1,3},{2,0},{3,1},{4,6},{5,7},{6,4},{7,5},{8,10},{9,11},{10,... | collective-permute-start | bytes 294920 | tf_op jit(solution)/shard_map/ppermute | solution.py:25
  42.3 5.2 %collective-permute-start.5 = (bf16[16,24,128]{2,1,0:T(8,128)(2,1)S(1)}, bf16[16,24,128]{2,1,0:T(8,128)(2,1)S(1)}, u32[]{:S(2)}, u32[]{:S(2)}) collective-permute-start(bf16[16,24,128]{2,1,0:T(8,128)(2,1)S(1)} %get-tuple-element.50), channel_id=1, source_target_pairs={{0,3},{1,2},{2,1},{3,0},{4,7},{5,6},{6,5},{7,4},{8,11},{9,10},{10,... | collective-permute-start | bytes 294920 | tf_op jit(solution)/shard_map/ppermute | solution.py:25
  48.1 10.1 %collective-permute-start.7 = (f16[400,128]{1,0:T(8,128)(2,1)S(1)}, f16[400,128]{1,0:T(8,128)(2,1)S(1)}, u32[]{:S(2)}, u32[]{:S(2)}) collective-permute-start(f16[400,128]{1,0:T(8,128)(2,1)S(1)} %fusion.10), channel_id=1, source_target_pairs={{0,8},{1,9},{2,10},{3,11},{4,12},{5,13},{6,14},{7,15},{8,0},{9,1},... | collective-permute-start | bytes 307208 | tf_op jit(solution)/shard_map/ppermute | solution.py:25
  51.9 8.5 %collective-permute-start.6 = (f16[400,128]{1,0:T(8,128)(2,1)S(1)}, f16[400,128]{1,0:T(8,128)(2,1)S(1)}, u32[]{:S(2)}, u32[]{:S(2)}) collective-permute-start(f16[400,128]{1,0:T(8,128)(2,1)S(1)} %fusion.9), channel_id=1, source_target_pairs={{0,4},{1,5},{2,6},{3,7},{4,0},{5,1},{6,2},{7,3},{8,12},{9,13},{10,... | collective-permute-start | bytes 307208 | tf_op jit(solution)/shard_map/ppermute | solution.py:25
  52.1 8.4 %collective-permute-start.8 = (f16[400,128]{1,0:T(8,128)(2,1)S(1)}, f16[400,128]{1,0:T(8,128)(2,1)S(1)}, u32[]{:S(2)}, u32[]{:S(2)}) collective-permute-start(f16[400,128]{1,0:T(8,128)(2,1)S(1)} %fusion.11), channel_id=1, source_target_pairs={{0,12},{1,13},{2,14},{3,15},{4,8},{5,9},{6,10},{7,11},{8,4},{9,5},... | collective-permute-start | bytes 307208 | tf_op jit(solution)/shard_map/ppermute | solution.py:25

commit v24 on v17

--- a/solution.py
+++ b/solution.py
@@ -212,7 +212,7 @@
 
 def adapter_kernel(parts, me_ref, rows_ref, expand_hbm, shrink_hbm, *refs):
     out_refs = refs[:PLANE]
-    shrink_ref, expand_ref, total_ref, sems, expand_sem = refs[PLANE:]
+    shrink_ref, expand_ref, total_ref, own_ref, sems, expand_sem = refs[PLANE:]
     me = me_ref[0]
     group, _, depth = shrink_ref.shape
     blocks = MOST // BLOCK
@@ -226,12 +226,14 @@
         copy(source).start()
     expand_copy = pltpu.make_async_copy(expand_hbm, expand_ref, expand_sem)
     expand_copy.start()
+    for source in range(group):
+        own = rows_ref[source * blocks : (source + 1) * blocks]
+        own_ref[source, :MOST] = own.reshape(MOST, depth)
     total = jnp.zeros((MOST, total_ref.shape[1]), jnp.float32)
     for source in range(group):
         copy(source).wait()
-        own = rows_ref[source * blocks : (source + 1) * blocks].reshape(MOST, depth)
         total += lax.dot_general(
-            own, shrink_ref[source], (((1,), (1,)), ((), ())), preferred_element_type=jnp.float32
+            own_ref[source, :MOST], shrink_ref[source], (((1,), (1,)), ((), ())), preferred_element_type=jnp.float32
         )
     total_ref[...] = jnp.zeros_like(total_ref)
     total_ref[:MOST] = total
@@ -269,6 +271,7 @@
             pltpu.VMEM((group, rank, depth), jnp.bfloat16),
             pltpu.VMEM((rank, model_width), jnp.bfloat16),
             pltpu.VMEM((HELD, rank), jnp.float32),
+            pltpu.VMEM((group, 2 * 16, depth), jnp.bfloat16),
             pltpu.SemaphoreType.DMA((group,)),
             pltpu.SemaphoreType.DMA,
         ],
@@ -312,6 +315,7 @@
     packed, pick, order, kept_hidden = pack_rows(
         hidden, adapter_of_row, adapter_holder_slot, me, orders
     )
+    packed = pltpu.with_memory_space_constraint(packed, pltpu.VMEM)
     gathered = lax.all_to_all(packed, "tp", split_axis=0, concat_axis=0, tiled=True)
     shrink = jnp.swapaxes(shrink_matrices, 1, 2)[0]
     kept, pair_in = pair_sums(kept_hidden, down_matrix, group, order, width)

time: 61.2 us -> 61.2 us (level)
  no operation moved by 1% of the time
where the time goes in v24:
time: 61.2 us; the launch traced here: 60.9 us
  Pallas kernels  21.4 us (35%)
  waiting for transfers between devices  18.6 us (30%)
  starting transfers between devices  17.2 us (28%)
  other arithmetic  1.95 us (3%)
  local copies, waits for them, and re-layouts  0.9 us (1%)
  between operations  0.83 us (1%)
    ppermute x9, waiting for transfers between devices, xor_permute(): return lax.ppermute(value, 'tp', [(i, i ^ offset) for i in range(group)])  18.6 us
    pallas_call x3, Pallas kernels, column_blocks(): pl.pallas_call(functools.partial(column_blocks_kernel, groups), out_shape...  14.8 us
    ppermute x9, starting transfers between devices, xor_permute(): return lax.ppermute(value, 'tp', [(i, i ^ offset) for i in range(group)])  9.85 us
    all_to_all x1, starting transfers between devices, shards_by_blocks(): lax.all_to_all(packed, 'tp', split_axis=0, concat_axis=0, tiled=True)  7.37 us
    pallas_call x1, Pallas kernels, adapter_output(): pl.pallas_call(functools.partial(adapter_kernel, parts), out_shape=[jax.S...  3.8 us
    pallas_call x1, Pallas kernels, pack_rows(): pl.pallas_call(functools.partial(pack_kernel, blocks, orders), out_shape=...  2.49 us
  transfers between devices with their start and end apart: 10, of which 6 were waited for; matrix products, arithmetic and copies ran while one was open for 3% of the time, Pallas kernels for 24%

profile of v24, /device:TPU:0, one launch (start us, length us, event | category | flops | bytes accessed | tf_op | source)
XLA Modules:
  0.0 60.9 jit_solution(4184878565125016327)
XLA Ops:
  0.0 2.5 %shard_map.64 = (bf16[80,4,1792]{2,1,0:T(4,128)(2,1)}, bf16[96,96]{1,0:T(8,128)(2,1)S(1)}, s32[16]{0:T(128)S(1)}, bf16[96,1792]{1,0:T(8,128)(2,1)S(1)}) custom-call(s32[1]{0:T(128)} %bitcast.2.me_ref, s32[16]{0:T(128)} %slot_hbm.1, s32[1,96]{1,0:T(1,128)} %bitcast.56, bf16[96,1792]{1,0:T(8,128)(2,1)} %hidden_hbm.1), custom_call_target="tpu_custom_call" | custom-call | tf_op jit(solution)/shard_map/pallas_call | solution.py:193
  2.5 7.4 %all-to-all-start = ((bf16[80,4,1792]{2,1,0:T(4,128)(2,1)}), bf16[80,4,1792]{2,1,0:T(4,128)(2,1)S(1)}, u32[]{:S(2)}, u32[]{:S(2)}) async-start(bf16[80,4,1792]{2,1,0:T(4,128)(2,1)} %get-tuple-element.45), calls=%async_computation | async-start | bytes 2293760 | tf_op jit(solution)/shard_map/all_to_all | solution.py:319
  9.9 9.5 %conditional.2 = (f16[1552,128]{1,0:T(8,128)(2,1)S(1)}) conditional(s32[]{:T(128)} %bitcast.4, () %tuple.19, (s32[16]{0:T(128)S(1)}, bf16[96,1792]{1,0:T(8,128)(2,1)S(1)}, bf16[1792,8192]{1,0:T(8,128)(2,1)}) %tuple.20), branch_computations={%region_0.0_spmd, %region_1.3_spmd} | conditional | flops 1581488 | bytes 7479232 | solution.py:109
  9.9 0.1 fusion.29
  10.0 4.2 %branch_1_fun.4 = f32[16,96,128]{2,1,0:T(8,128)S(1)} custom-call(s32[4]{0:T(128)S(1)} %get-tuple-element.58.order_ref, bf16[96,1792]{1,0:T(8,128)(2,1)S(1)} %get-tuple-element.24.hidden_ref, bf16[1792,8192]{1,0:T(8,128)(2,1)} %get-tuple-element.25.down_ref), custom_call_target="tpu_custom_call" | custom-call | flops 1000 | bytes 1000 | tf_op jit(solution)/shard_map/cond/branch_1_fun/pallas_call | solution.py:62
  14.2 0.5 collective-permute-start.1
  14.7 4.2 %branch_1_fun.3 = f32[16,96,128]{2,1,0:T(8,128)S(1)} custom-call(s32[4]{0:T(128)S(1)} %get-tuple-element.59.order_ref, bf16[96,1792]{1,0:T(8,128)(2,1)S(1)} %get-tuple-element.24.hidden_ref, bf16[1792,8192]{1,0:T(8,128)(2,1)} %get-tuple-element.25.down_ref), custom_call_target="tpu_custom_call" | custom-call | flops 1000 | bytes 1000 | tf_op jit(solution)/shard_map/cond/branch_1_fun/pallas_call | solution.py:62
  18.9 0.0 collective-permute-done.1
  18.9 0.2 abs_reduce_fusion
  19.1 0.2 multiply_convert_fusion
  19.3 0.1 fusion.1
  19.4 1.7 %collective-permute-start.2 = (f16[1552,128]{1,0:T(8,128)(2,1)S(1)}, f16[1552,128]{1,0:T(8,128)(2,1)S(1)}, u32[]{:S(2)}, u32[]{:S(2)}) collective-permute-start(f16[1552,128]{1,0:T(8,128)(2,1)S(1)} %get-tuple-element.71), channel_id=1, source_target_pairs={{0,2},{1,3},{2,0},{3,1},{4,6},{5,7},{6,4},{7,5},{8,10},{9,11},{10,... | collective-permute-start | bytes 1191944 | tf_op jit(solution)/shard_map/ppermute | solution.py:25
  21.1 0.6 slice.52
  22.4 9.0 %conditional.3 = (f32[16,96,128]{2,1,0:T(8,128)S(1)}) conditional(s32[]{:T(128)} %bitcast.5, () %tuple.22, (s32[16]{0:T(128)S(1)}, bf16[96,1792]{1,0:T(8,128)(2,1)S(1)}, bf16[1792,8192]{1,0:T(8,128)(2,1)}) %tuple.23), branch_computations={%region_3.4_spmd, %region_4.5_spmd} | conditional | flops 197608 | bytes 5506136 | solution.py:120
  22.4 0.1 slice.36.order_ref
  22.5 6.4 %branch_1_fun.5 = (f32[16,96,128]{2,1,0:T(8,128)S(1)}, f32[16,96,128]{2,1,0:T(8,128)S(1)}) custom-call(s32[8]{0:T(128)S(1)} %slice.36.order_ref, bf16[96,1792]{1,0:T(8,128)(2,1)S(1)} %get-tuple-element.27.hidden_ref, bf16[1792,8192]{1,0:T(8,128)(2,1)} %get-tuple-element.28.down_ref), custom_call_target="tpu_custom_call" | custom-call | flops 1000 | bytes 1000 | tf_op jit(solution)/shard_map/cond/branch_1_fun/pallas_call | solution.py:62
  28.9 0.1 collective-permute-start
  29.0 2.2 %collective-permute-done = f32[16,96,128]{2,1,0:T(8,128)S(1)} collective-permute-done((f32[16,96,128]{2,1,0:T(8,128)S(1)}, f32[16,96,128]{2,1,0:T(8,128)S(1)}, u32[]{:S(2)}, u32[]{:S(2)}) %collective-permute-start) | collective-permute-done | bytes 786464 | tf_op jit(solution)/shard_map/cond/branch_1_fun/ppermute | solution.py:25
  31.2 0.1 add.39
  31.3 4.6 %collective-permute-done.2 = f16[1552,128]{1,0:T(8,128)(2,1)S(1)} collective-permute-done((f16[1552,128]{1,0:T(8,128)(2,1)S(1)}, f16[1552,128]{1,0:T(8,128)(2,1)S(1)}, u32[]{:S(2)}, u32[]{:S(2)}) %collective-permute-start.2) | collective-permute-done | bytes 397344 | tf_op jit(solution)/shard_map/ppermute | solution.py:25
  35.9 0.1 slice.65
  36.0 0.0 all-to-all-done.rows_ref
  36.0 3.8 %shard_map.65 = (bf16[16,24,128]{2,1,0:T(8,128)(2,1)S(1)}, bf16[16,24,128]{2,1,0:T(8,128)(2,1)S(1)}, bf16[16,24,128]{2,1,0:T(8,128)(2,1)S(1)}, bf16[16,24,128]{2,1,0:T(8,128)(2,1)S(1)}) custom-call(s32[1]{0:T(128)} %bitcast.2.me_ref, bf16[80,4,1792]{2,1,0:T(4,128)(2,1)S(1)} %all-to-all-done.rows_ref, bf16[64,8192]{1,0:T(8,128)(2,1)} %bitcast.48, ...), custom_call_target="tpu_custom_call" | custom-call | tf_op jit(solution)/shard_map/pallas_call | solution.py:260
  39.8 0.1 collective-permute-start.3
  39.9 2.0 %collective-permute-start.4 = (bf16[16,24,128]{2,1,0:T(8,128)(2,1)S(1)}, bf16[16,24,128]{2,1,0:T(8,128)(2,1)S(1)}, u32[]{:S(2)}, u32[]{:S(2)}) collective-permute-start(bf16[16,24,128]{2,1,0:T(8,128)(2,1)S(1)} %get-tuple-element.49), channel_id=1, source_target_pairs={{0,2},{1,3},{2,0},{3,1},{4,6},{5,7},{6,4},{7,5},{8,10},{9,11},{10,... | collective-permute-start | bytes 294920 | tf_op jit(solution)/shard_map/ppermute | solution.py:25
  41.9 0.1 collective-permute-start.5
  42.0 0.2 fusion.2.pair_ref
  42.2 0.0 collective-permute-done.3.refs_1_
  42.2 3.5 %collective-permute-done.4.refs_2_ = bf16[16,24,128]{2,1,0:T(8,128)(2,1)S(1)} collective-permute-done((bf16[16,24,128]{2,1,0:T(8,128)(2,1)S(1)}, bf16[16,24,128]{2,1,0:T(8,128)(2,1)S(1)}, u32[]{:S(2)}, u32[]{:S(2)}) %collective-permute-start.4) | collective-permute-done | bytes 98336 | tf_op jit(solution)/shard_map/ppermute | solution.py:25
  45.6 1.4 %collective-permute-done.5.refs_3_ = bf16[16,24,128]{2,1,0:T(8,128)(2,1)S(1)} collective-permute-done((bf16[16,24,128]{2,1,0:T(8,128)(2,1)S(1)}, bf16[16,24,128]{2,1,0:T(8,128)(2,1)S(1)}, u32[]{:S(2)}, u32[]{:S(2)}) %collective-permute-start.5) | collective-permute-done | bytes 98336 | tf_op jit(solution)/shard_map/ppermute | solution.py:25
  47.1 0.3 shard_map.66
  47.4 0.2 abs_reduce_fusion.3
  47.6 0.1 multiply_convert_fusion.3
  47.7 3.7 %collective-permute-start.7 = (f16[400,128]{1,0:T(8,128)(2,1)S(1)}, f16[400,128]{1,0:T(8,128)(2,1)S(1)}, u32[]{:S(2)}, u32[]{:S(2)}) collective-permute-start(f16[400,128]{1,0:T(8,128)(2,1)S(1)} %fusion.10), channel_id=1, source_target_pairs={{0,8},{1,9},{2,10},{3,11},{4,12},{5,13},{6,14},{7,15},{8,0},{9,1},... | collective-permute-start | bytes 307208 | tf_op jit(solution)/shard_map/ppermute | solution.py:25
  51.5 0.2 collective-permute-start.6
  51.7 1.4 %collective-permute-start.8 = (f16[400,128]{1,0:T(8,128)(2,1)S(1)}, f16[400,128]{1,0:T(8,128)(2,1)S(1)}, u32[]{:S(2)}, u32[]{:S(2)}) collective-permute-start(f16[400,128]{1,0:T(8,128)(2,1)S(1)} %fusion.11), channel_id=1, source_target_pairs={{0,12},{1,13},{2,14},{3,15},{4,8},{5,9},{6,10},{7,11},{8,4},{9,5},... | collective-permute-start | bytes 307208 | tf_op jit(solution)/shard_map/ppermute | solution.py:25
  53.1 4.7 %collective-permute-done.7 = f16[400,128]{1,0:T(8,128)(2,1)S(1)} collective-permute-done((f16[400,128]{1,0:T(8,128)(2,1)S(1)}, f16[400,128]{1,0:T(8,128)(2,1)S(1)}, u32[]{:S(2)}, u32[]{:S(2)}) %collective-permute-start.7) | collective-permute-done | bytes 102432 | tf_op jit(solution)/shard_map/ppermute | solution.py:25
  57.8 2.2 %collective-permute-done.6 = f16[400,128]{1,0:T(8,128)(2,1)S(1)} collective-permute-done((f16[400,128]{1,0:T(8,128)(2,1)S(1)}, f16[400,128]{1,0:T(8,128)(2,1)S(1)}, u32[]{:S(2)}, u32[]{:S(2)}) %collective-permute-start.6) | collective-permute-done | bytes 102432 | tf_op jit(solution)/shard_map/ppermute | solution.py:25
  60.1 0.0 collective-permute-done.8
  60.2 0.8 %copy_bitcast_fusion = bf16[96,512]{1,0:T(8,128)(2,1)} fusion(f16[4,96,128]{2,1,0:T(8,128)(2,1)S(1)} %bitcast.54, f16[4,96,128]{2,1,0:T(8,128)(2,1)S(1)} %bitcast.51, f16[4,96,128]{2,1,0:T(8,128)(2,1)S(1)} %bitcast.52, f32[16,96,128]{2,1,0:T(8,128)S(1)} %shard_map.66, f32[96]{0:T(128)S(1)} %fusion.16, f32[96]{0:T(128)S(1)} %fusion.20, f32[96]{0:T(128)S(1)} %fusion.24), kind=kLoop, calls=%fused_computation.31 | loop fusion | flops 491520 | bytes 591360 | tf_op jit(solution)/shard_map/convert_element_type | solution.py:328
  (13 shorter events, 0.2 us)
Async XLA Ops:
  2.5 33.5 %all-to-all-start = ((bf16[80,4,1792]{2,1,0:T(4,128)(2,1)}), bf16[80,4,1792]{2,1,0:T(4,128)(2,1)S(1)}, u32[]{:S(2)}, u32[]{:S(2)}) async-start(bf16[80,4,1792]{2,1,0:T(4,128)(2,1)} %get-tuple-element.45), calls=%async_computation | async-start | bytes 2293760 | tf_op jit(solution)/shard_map/all_to_all | solution.py:319
  14.2 4.7 %collective-permute-start.1 = (f32[16,96,128]{2,1,0:T(8,128)S(1)}, f32[16,96,128]{2,1,0:T(8,128)S(1)}, u32[]{:S(2)}, u32[]{:S(2)}) collective-permute-start(f32[16,96,128]{2,1,0:T(8,128)S(1)} %branch_1_fun.4), channel_id=1, source_target_pairs={{0,1},{1,0},{2,3},{3,2},{4,5},{5,4},{6,7},{7,6},{8,9},{9,8},{10,11... | collective-permute-start | bytes 2359304 | tf_op jit(solution)/shard_map/cond/branch_1_fun/ppermute | solution.py:25
  19.4 16.5 %collective-permute-start.2 = (f16[1552,128]{1,0:T(8,128)(2,1)S(1)}, f16[1552,128]{1,0:T(8,128)(2,1)S(1)}, u32[]{:S(2)}, u32[]{:S(2)}) collective-permute-start(f16[1552,128]{1,0:T(8,128)(2,1)S(1)} %get-tuple-element.71), channel_id=1, source_target_pairs={{0,2},{1,3},{2,0},{3,1},{4,6},{5,7},{6,4},{7,5},{8,10},{9,11},{10,... | collective-permute-start | bytes 1191944 | tf_op jit(solution)/shard_map/ppermute | solution.py:25
  28.9 2.4 %collective-permute-start = (f32[16,96,128]{2,1,0:T(8,128)S(1)}, f32[16,96,128]{2,1,0:T(8,128)S(1)}, u32[]{:S(2)}, u32[]{:S(2)}) collective-permute-start(f32[16,96,128]{2,1,0:T(8,128)S(1)} %get-tuple-element.30), channel_id=1, source_target_pairs={{0,1},{1,0},{2,3},{3,2},{4,5},{5,4},{6,7},{7,6},{8,9},{9,8},{10,11... | collective-permute-start | bytes 2359304 | tf_op jit(solution)/shard_map/cond/branch_1_fun/ppermute | solution.py:25
  39.8 2.3 %collective-permute-start.3 = (bf16[16,24,128]{2,1,0:T(8,128)(2,1)S(1)}, bf16[16,24,128]{2,1,0:T(8,128)(2,1)S(1)}, u32[]{:S(2)}, u32[]{:S(2)}) collective-permute-start(bf16[16,24,128]{2,1,0:T(8,128)(2,1)S(1)} %get-tuple-element.48), channel_id=1, source_target_pairs={{0,1},{1,0},{2,3},{3,2},{4,5},{5,4},{6,7},{7,6},{8,9},{9,8},{10,11... | collective-permute-start | bytes 294920 | tf_op jit(solution)/shard_map/ppermute | solution.py:25
  39.9 5.7 %collective-permute-start.4 = (bf16[16,24,128]{2,1,0:T(8,128)(2,1)S(1)}, bf16[16,24,128]{2,1,0:T(8,128)(2,1)S(1)}, u32[]{:S(2)}, u32[]{:S(2)}) collective-permute-start(bf16[16,24,128]{2,1,0:T(8,128)(2,1)S(1)} %get-tuple-element.49), channel_id=1, source_target_pairs={{0,2},{1,3},{2,0},{3,1},{4,6},{5,7},{6,4},{7,5},{8,10},{9,11},{10,... | collective-permute-start | bytes 294920 | tf_op jit(solution)/shard_map/ppermute | solution.py:25
  41.9 5.2 %collective-permute-start.5 = (bf16[16,24,128]{2,1,0:T(8,128)(2,1)S(1)}, bf16[16,24,128]{2,1,0:T(8,128)(2,1)S(1)}, u32[]{:S(2)}, u32[]{:S(2)}) collective-permute-start(bf16[16,24,128]{2,1,0:T(8,128)(2,1)S(1)} %get-tuple-element.50), channel_id=1, source_target_pairs={{0,3},{1,2},{2,1},{3,0},{4,7},{5,6},{6,5},{7,4},{8,11},{9,10},{10,... | collective-permute-start | bytes 294920 | tf_op jit(solution)/shard_map/ppermute | solution.py:25
  47.7 10.1 %collective-permute-start.7 = (f16[400,128]{1,0:T(8,128)(2,1)S(1)}, f16[400,128]{1,0:T(8,128)(2,1)S(1)}, u32[]{:S(2)}, u32[]{:S(2)}) collective-permute-start(f16[400,128]{1,0:T(8,128)(2,1)S(1)} %fusion.10), channel_id=1, source_target_pairs={{0,8},{1,9},{2,10},{3,11},{4,12},{5,13},{6,14},{7,15},{8,0},{9,1},... | collective-permute-start | bytes 307208 | tf_op jit(solution)/shard_map/ppermute | solution.py:25
  51.5 8.5 %collective-permute-start.6 = (f16[400,128]{1,0:T(8,128)(2,1)S(1)}, f16[400,128]{1,0:T(8,128)(2,1)S(1)}, u32[]{:S(2)}, u32[]{:S(2)}) collective-permute-start(f16[400,128]{1,0:T(8,128)(2,1)S(1)} %fusion.9), channel_id=1, source_target_pairs={{0,4},{1,5},{2,6},{3,7},{4,0},{5,1},{6,2},{7,3},{8,12},{9,13},{10,... | collective-permute-start | bytes 307208 | tf_op jit(solution)/shard_map/ppermute | solution.py:25
  51.7 8.4 %collective-permute-start.8 = (f16[400,128]{1,0:T(8,128)(2,1)S(1)}, f16[400,128]{1,0:T(8,128)(2,1)S(1)}, u32[]{:S(2)}, u32[]{:S(2)}) collective-permute-start(f16[400,128]{1,0:T(8,128)(2,1)S(1)} %fusion.11), channel_id=1, source_target_pairs={{0,12},{1,13},{2,14},{3,15},{4,8},{5,9},{6,10},{7,11},{8,4},{9,5},... | collective-permute-start | bytes 307208 | tf_op jit(solution)/shard_map/ppermute | solution.py:25

commit v25 on v20

--- a/solution.py
+++ b/solution.py
@@ -173,7 +173,8 @@
     first = jnp.sum(jnp.where(adapter == ids, first, 0), axis=0, keepdims=True)
     index = lax.broadcasted_iota(jnp.int32, (1, rows), 1) - first
     held = blocks * BLOCK
-    rank = lax.rem(slot, PLANE) * (group // PLANE) + lax.div(slot, PLANE)
+    far = lax.rem(lax.div(slot, 2), 2)
+    rank = far * (group // 2) + lax.div(slot, PLANE) * 2 + lax.rem(slot, 2)
     spots = lax.broadcasted_iota(jnp.int32, (group * held, rows), 0)
     pick = jnp.where(spots == rank * held + index, 1.0, 0.0).astype(jnp.bfloat16)
     for k in range(PLANE):
@@ -215,7 +216,7 @@
 
 def adapter_kernel(parts, ranks, me_ref, rows_ref, expand_hbm, shrink_hbm, *refs):
     out_refs = refs[:PLANE]
-    shrink_ref, expand_ref, total_ref, sems, expand_sem = refs[PLANE:]
+    shrink_ref, expand_ref, total_ref, own_ref, sems, expand_sem = refs[PLANE:]
     me = me_ref[0]
     group, _, depth = shrink_ref.shape
     blocks = MOST // BLOCK
@@ -231,12 +232,14 @@
         copy(source).start()
     expand_copy = pltpu.make_async_copy(expand_hbm, expand_ref, expand_sem)
     expand_copy.start()
+    for source in range(group):
+        own = rows_ref[source * blocks : (source + 1) * blocks]
+        own_ref[source, :MOST] = own.reshape(MOST, depth)
     total = jnp.zeros((MOST, total_ref.shape[1]), jnp.float32)
     for source in range(group):
         copy(source).wait()
-        own = rows_ref[source * blocks : (source + 1) * blocks].reshape(MOST, depth)
         total += lax.dot_general(
-            own, shrink_ref[source], (((1,), (1,)), ((), ())), preferred_element_type=jnp.float32
+            own_ref[source, :MOST], shrink_ref[source], (((1,), (1,)), ((), ())), preferred_element_type=jnp.float32
         )
     total_ref[...] = jnp.zeros_like(total_ref)
     total_ref[:MOST] = total
@@ -274,6 +277,7 @@
             pltpu.VMEM((group, rank, depth), jnp.bfloat16),
             pltpu.VMEM((rank, model_width), jnp.bfloat16),
             pltpu.VMEM((HELD, rank), jnp.float32),
+            pltpu.VMEM((group, 2 * 16, depth), jnp.bfloat16),
             pltpu.SemaphoreType.DMA((group,)),
             pltpu.SemaphoreType.DMA,
         ],
@@ -314,8 +318,8 @@
     width = down_matrix.shape[1] // group
     quads = list(range(0, group, 4))
     orders = [q + k for k in (3, 2, 1, 0) for q in quads]
-    lines = group // PLANE
-    ranks = [PLANE * (i % lines) + i // lines for i in range(group)]
+    half = group // 2
+    ranks = [i % half // 2 * PLANE + i // half * 2 + i % 2 for i in range(group)]
     packed, pick, order, kept_hidden = pack_rows(
         hidden, adapter_of_row, adapter_holder_slot, me, orders
     )

time: 61.3 us -> 61.1 us (level)
    all_to_all x1, waiting for transfers between devices: 4.62 us -> 0.97 us  [shards_by_blocks(): lax.all_to_all(packed, 'tp', split_axis=0, concat_axis=0, axis_index_grou...]
    ppermute x9, waiting for transfers between devices: 15 us -> 18.1 us  [xor_permute(): return lax.ppermute(value, 'tp', [(i, i ^ offset) for i in range(group)])]
where the time goes in v25:
time: 61.1 us; the launch traced here: 60.9 us
  Pallas kernels  21.4 us (35%)
  waiting for transfers between devices  19.1 us (31%)
  starting transfers between devices  16.6 us (27%)
  other arithmetic  1.95 us (3%)
  local copies, waits for them, and re-layouts  0.9 us (1%)
  between operations  0.81 us (1%)
    ppermute x9, waiting for transfers between devices, xor_permute(): return lax.ppermute(value, 'tp', [(i, i ^ offset) for i in range(group)])  18.1 us
    pallas_call x3, Pallas kernels, column_blocks(): pl.pallas_call(functools.partial(column_blocks_kernel, groups), out_shape...  14.8 us
    ppermute x9, starting transfers between devices, xor_permute(): return lax.ppermute(value, 'tp', [(i, i ^ offset) for i in range(group)])  9.25 us
    all_to_all x1, starting transfers between devices, shards_by_blocks(): lax.all_to_all(packed, 'tp', split_axis=0, concat_axis=0, axis_index_grou...  7.37 us
    pallas_call x1, Pallas kernels, adapter_output(): pl.pallas_call(functools.partial(adapter_kernel, parts, ranks), out_shape...  3.79 us
    pallas_call x1, Pallas kernels, pack_rows(): pl.pallas_call(functools.partial(pack_kernel, blocks, orders), out_shape=...  2.49 us
  transfers between devices with their start and end apart: 10, of which 7 were waited for; matrix products, arithmetic and copies ran while one was open for 3% of the time, Pallas kernels for 24%

profile of v25, /device:TPU:0, one launch (start us, length us, event | category | flops | bytes accessed | tf_op | source)
XLA Modules:
  0.0 60.9 jit_solution(9282936014920188439)
XLA Ops:
  0.0 2.5 %shard_map.64 = (bf16[80,4,1792]{2,1,0:T(4,128)(2,1)}, bf16[96,96]{1,0:T(8,128)(2,1)S(1)}, s32[16]{0:T(128)S(1)}, bf16[96,1792]{1,0:T(8,128)(2,1)S(1)}) custom-call(s32[1]{0:T(128)} %bitcast.2.me_ref, s32[16]{0:T(128)} %slot_hbm.1, s32[1,96]{1,0:T(1,128)} %bitcast.56, bf16[96,1792]{1,0:T(8,128)(2,1)} %hidden_hbm.1), custom_call_target="tpu_custom_call" | custom-call | tf_op jit(solution)/shard_map/pallas_call | solution.py:197
  2.5 7.4 %all-to-all-start = ((bf16[80,4,1792]{2,1,0:T(4,128)(2,1)}), bf16[80,4,1792]{2,1,0:T(4,128)(2,1)S(1)}, u32[]{:S(2)}, u32[]{:S(2)}) async-start(bf16[80,4,1792]{2,1,0:T(4,128)(2,1)} %get-tuple-element.45), calls=%async_computation | async-start | bytes 2293760 | tf_op jit(solution)/shard_map/all_to_all | solution.py:326
  9.9 9.5 %conditional.2 = (f16[1552,128]{1,0:T(8,128)(2,1)S(1)}) conditional(s32[]{:T(128)} %bitcast.4, () %tuple.19, (s32[16]{0:T(128)S(1)}, bf16[96,1792]{1,0:T(8,128)(2,1)S(1)}, bf16[1792,8192]{1,0:T(8,128)(2,1)}) %tuple.20), branch_computations={%region_0.0_spmd, %region_1.3_spmd} | conditional | flops 1581488 | bytes 7479232 | solution.py:109
  9.9 0.1 fusion.29
  10.0 4.2 %branch_1_fun.4 = f32[16,96,128]{2,1,0:T(8,128)S(1)} custom-call(s32[4]{0:T(128)S(1)} %get-tuple-element.58.order_ref, bf16[96,1792]{1,0:T(8,128)(2,1)S(1)} %get-tuple-element.24.hidden_ref, bf16[1792,8192]{1,0:T(8,128)(2,1)} %get-tuple-element.25.down_ref), custom_call_target="tpu_custom_call" | custom-call | flops 1000 | bytes 1000 | tf_op jit(solution)/shard_map/cond/branch_1_fun/pallas_call | solution.py:62
  14.2 0.5 collective-permute-start.1
  14.7 4.2 %branch_1_fun.3 = f32[16,96,128]{2,1,0:T(8,128)S(1)} custom-call(s32[4]{0:T(128)S(1)} %get-tuple-element.59.order_ref, bf16[96,1792]{1,0:T(8,128)(2,1)S(1)} %get-tuple-element.24.hidden_ref, bf16[1792,8192]{1,0:T(8,128)(2,1)} %get-tuple-element.25.down_ref), custom_call_target="tpu_custom_call" | custom-call | flops 1000 | bytes 1000 | tf_op jit(solution)/shard_map/cond/branch_1_fun/pallas_call | solution.py:62
  18.9 0.0 collective-permute-done.1
  18.9 0.2 abs_reduce_fusion
  19.1 0.2 multiply_convert_fusion
  19.3 0.1 fusion.1
  19.4 1.7 %collective-permute-start.2 = (f16[1552,128]{1,0:T(8,128)(2,1)S(1)}, f16[1552,128]{1,0:T(8,128)(2,1)S(1)}, u32[]{:S(2)}, u32[]{:S(2)}) collective-permute-start(f16[1552,128]{1,0:T(8,128)(2,1)S(1)} %get-tuple-element.71), channel_id=1, source_target_pairs={{0,2},{1,3},{2,0},{3,1},{4,6},{5,7},{6,4},{7,5},{8,10},{9,11},{10,... | collective-permute-start | bytes 1191944 | tf_op jit(solution)/shard_map/ppermute | solution.py:25
  21.1 0.6 slice.52
  22.4 8.9 %conditional.3 = (f32[16,96,128]{2,1,0:T(8,128)S(1)}) conditional(s32[]{:T(128)} %bitcast.5, () %tuple.22, (s32[16]{0:T(128)S(1)}, bf16[96,1792]{1,0:T(8,128)(2,1)S(1)}, bf16[1792,8192]{1,0:T(8,128)(2,1)}) %tuple.23), branch_computations={%region_3.4_spmd, %region_4.5_spmd} | conditional | flops 197608 | bytes 5506136 | solution.py:120
  22.4 0.1 slice.36.order_ref
  22.5 6.4 %branch_1_fun.5 = (f32[16,96,128]{2,1,0:T(8,128)S(1)}, f32[16,96,128]{2,1,0:T(8,128)S(1)}) custom-call(s32[8]{0:T(128)S(1)} %slice.36.order_ref, bf16[96,1792]{1,0:T(8,128)(2,1)S(1)} %get-tuple-element.27.hidden_ref, bf16[1792,8192]{1,0:T(8,128)(2,1)} %get-tuple-element.28.down_ref), custom_call_target="tpu_custom_call" | custom-call | flops 1000 | bytes 1000 | tf_op jit(solution)/shard_map/cond/branch_1_fun/pallas_call | solution.py:62
  28.9 0.1 collective-permute-start
  29.0 2.2 %collective-permute-done = f32[16,96,128]{2,1,0:T(8,128)S(1)} collective-permute-done((f32[16,96,128]{2,1,0:T(8,128)S(1)}, f32[16,96,128]{2,1,0:T(8,128)S(1)}, u32[]{:S(2)}, u32[]{:S(2)}) %collective-permute-start) | collective-permute-done | bytes 786464 | tf_op jit(solution)/shard_map/cond/branch_1_fun/ppermute | solution.py:25
  31.2 0.1 add.39
  31.3 4.1 %collective-permute-done.2 = f16[1552,128]{1,0:T(8,128)(2,1)S(1)} collective-permute-done((f16[1552,128]{1,0:T(8,128)(2,1)S(1)}, f16[1552,128]{1,0:T(8,128)(2,1)S(1)}, u32[]{:S(2)}, u32[]{:S(2)}) %collective-permute-start.2) | collective-permute-done | bytes 397344 | tf_op jit(solution)/shard_map/ppermute | solution.py:25
  35.4 0.1 slice.65
  35.5 1.0 %all-to-all-done.rows_ref = bf16[80,4,1792]{2,1,0:T(4,128)(2,1)S(1)} async-done(((bf16[80,4,1792]{2,1,0:T(4,128)(2,1)}), bf16[80,4,1792]{2,1,0:T(4,128)(2,1)S(1)}, u32[]{:S(2)}, u32[]{:S(2)}) %all-to-all-start) | async-done | bytes 1146912 | tf_op jit(solution)/shard_map/all_to_all | solution.py:326
  36.5 3.8 %shard_map.65 = (bf16[16,24,128]{2,1,0:T(8,128)(2,1)S(1)}, bf16[16,24,128]{2,1,0:T(8,128)(2,1)S(1)}, bf16[16,24,128]{2,1,0:T(8,128)(2,1)S(1)}, bf16[16,24,128]{2,1,0:T(8,128)(2,1)S(1)}) custom-call(s32[1]{0:T(128)} %bitcast.2.me_ref, bf16[80,4,1792]{2,1,0:T(4,128)(2,1)S(1)} %all-to-all-done.rows_ref, bf16[64,8192]{1,0:T(8,128)(2,1)} %bitcast.48, ...), custom_call_target="tpu_custom_call" | custom-call | tf_op jit(solution)/shard_map/pallas_call | solution.py:266
  40.3 0.8 %collective-permute-start.3 = (bf16[16,24,128]{2,1,0:T(8,128)(2,1)S(1)}, bf16[16,24,128]{2,1,0:T(8,128)(2,1)S(1)}, u32[]{:S(2)}, u32[]{:S(2)}) collective-permute-start(bf16[16,24,128]{2,1,0:T(8,128)(2,1)S(1)} %get-tuple-element.48), channel_id=1, source_target_pairs={{0,1},{1,0},{2,3},{3,2},{4,5},{5,4},{6,7},{7,6},{8,9},{9,8},{10,11... | collective-permute-start | bytes 294920 | tf_op jit(solution)/shard_map/ppermute | solution.py:25
  41.2 1.5 %collective-permute-start.4 = (bf16[16,24,128]{2,1,0:T(8,128)(2,1)S(1)}, bf16[16,24,128]{2,1,0:T(8,128)(2,1)S(1)}, u32[]{:S(2)}, u32[]{:S(2)}) collective-permute-start(bf16[16,24,128]{2,1,0:T(8,128)(2,1)S(1)} %get-tuple-element.49), channel_id=1, source_target_pairs={{0,2},{1,3},{2,0},{3,1},{4,6},{5,7},{6,4},{7,5},{8,10},{9,11},{10,... | collective-permute-start | bytes 294920 | tf_op jit(solution)/shard_map/ppermute | solution.py:25
  42.6 0.0 collective-permute-start.5
  42.6 0.2 fusion.2.pair_ref
  42.8 0.0 collective-permute-done.3.refs_1_
  42.8 3.4 %collective-permute-done.4.refs_2_ = bf16[16,24,128]{2,1,0:T(8,128)(2,1)S(1)} collective-permute-done((bf16[16,24,128]{2,1,0:T(8,128)(2,1)S(1)}, bf16[16,24,128]{2,1,0:T(8,128)(2,1)S(1)}, u32[]{:S(2)}, u32[]{:S(2)}) %collective-permute-start.4) | collective-permute-done | bytes 98336 | tf_op jit(solution)/shard_map/ppermute | solution.py:25
  46.3 1.4 %collective-permute-done.5.refs_3_ = bf16[16,24,128]{2,1,0:T(8,128)(2,1)S(1)} collective-permute-done((bf16[16,24,128]{2,1,0:T(8,128)(2,1)S(1)}, bf16[16,24,128]{2,1,0:T(8,128)(2,1)S(1)}, u32[]{:S(2)}, u32[]{:S(2)}) %collective-permute-start.5) | collective-permute-done | bytes 98336 | tf_op jit(solution)/shard_map/ppermute | solution.py:25
  47.7 0.3 shard_map.66
  48.0 0.2 abs_reduce_fusion.3
  48.2 0.1 multiply_convert_fusion.3
  48.4 2.1 %collective-permute-start.7 = (f16[400,128]{1,0:T(8,128)(2,1)S(1)}, f16[400,128]{1,0:T(8,128)(2,1)S(1)}, u32[]{:S(2)}, u32[]{:S(2)}) collective-permute-start(f16[400,128]{1,0:T(8,128)(2,1)S(1)} %fusion.10), channel_id=1, source_target_pairs={{0,8},{1,9},{2,10},{3,11},{4,12},{5,13},{6,14},{7,15},{8,0},{9,1},... | collective-permute-start | bytes 307208 | tf_op jit(solution)/shard_map/ppermute | solution.py:25
  50.5 0.9 %collective-permute-start.6 = (f16[400,128]{1,0:T(8,128)(2,1)S(1)}, f16[400,128]{1,0:T(8,128)(2,1)S(1)}, u32[]{:S(2)}, u32[]{:S(2)}) collective-permute-start(f16[400,128]{1,0:T(8,128)(2,1)S(1)} %fusion.9), channel_id=1, source_target_pairs={{0,4},{1,5},{2,6},{3,7},{4,0},{5,1},{6,2},{7,3},{8,12},{9,13},{10,... | collective-permute-start | bytes 307208 | tf_op jit(solution)/shard_map/ppermute | solution.py:25
  51.4 1.6 %collective-permute-start.8 = (f16[400,128]{1,0:T(8,128)(2,1)S(1)}, f16[400,128]{1,0:T(8,128)(2,1)S(1)}, u32[]{:S(2)}, u32[]{:S(2)}) collective-permute-start(f16[400,128]{1,0:T(8,128)(2,1)S(1)} %fusion.11), channel_id=1, source_target_pairs={{0,12},{1,13},{2,14},{3,15},{4,8},{5,9},{6,10},{7,11},{8,4},{9,5},... | collective-permute-start | bytes 307208 | tf_op jit(solution)/shard_map/ppermute | solution.py:25
  53.0 4.4 %collective-permute-done.7 = f16[400,128]{1,0:T(8,128)(2,1)S(1)} collective-permute-done((f16[400,128]{1,0:T(8,128)(2,1)S(1)}, f16[400,128]{1,0:T(8,128)(2,1)S(1)}, u32[]{:S(2)}, u32[]{:S(2)}) %collective-permute-start.7) | collective-permute-done | bytes 102432 | tf_op jit(solution)/shard_map/ppermute | solution.py:25
  57.4 0.0 collective-permute-done.6
  57.5 2.5 %collective-permute-done.8 = f16[400,128]{1,0:T(8,128)(2,1)S(1)} collective-permute-done((f16[400,128]{1,0:T(8,128)(2,1)S(1)}, f16[400,128]{1,0:T(8,128)(2,1)S(1)}, u32[]{:S(2)}, u32[]{:S(2)}) %collective-permute-start.8) | collective-permute-done | bytes 102432 | tf_op jit(solution)/shard_map/ppermute | solution.py:25
  60.1 0.8 %copy_bitcast_fusion = bf16[96,512]{1,0:T(8,128)(2,1)} fusion(f16[4,96,128]{2,1,0:T(8,128)(2,1)S(1)} %bitcast.54, f16[4,96,128]{2,1,0:T(8,128)(2,1)S(1)} %bitcast.51, f16[4,96,128]{2,1,0:T(8,128)(2,1)S(1)} %bitcast.52, f32[16,96,128]{2,1,0:T(8,128)S(1)} %shard_map.66, f32[96]{0:T(128)S(1)} %fusion.16, f32[96]{0:T(128)S(1)} %fusion.20, f32[96]{0:T(128)S(1)} %fusion.24), kind=kLoop, calls=%fused_computation.31 | loop fusion | flops 491520 | bytes 591360 | tf_op jit(solution)/shard_map/convert_element_type | solution.py:337
  (13 shorter events, 0.2 us)
Async XLA Ops:
  2.5 34.0 %all-to-all-start = ((bf16[80,4,1792]{2,1,0:T(4,128)(2,1)}), bf16[80,4,1792]{2,1,0:T(4,128)(2,1)S(1)}, u32[]{:S(2)}, u32[]{:S(2)}) async-start(bf16[80,4,1792]{2,1,0:T(4,128)(2,1)} %get-tuple-element.45), calls=%async_computation | async-start | bytes 2293760 | tf_op jit(solution)/shard_map/all_to_all | solution.py:326
  14.2 4.7 %collective-permute-start.1 = (f32[16,96,128]{2,1,0:T(8,128)S(1)}, f32[16,96,128]{2,1,0:T(8,128)S(1)}, u32[]{:S(2)}, u32[]{:S(2)}) collective-permute-start(f32[16,96,128]{2,1,0:T(8,128)S(1)} %branch_1_fun.4), channel_id=1, source_target_pairs={{0,1},{1,0},{2,3},{3,2},{4,5},{5,4},{6,7},{7,6},{8,9},{9,8},{10,11... | collective-permute-start | bytes 2359304 | tf_op jit(solution)/shard_map/cond/branch_1_fun/ppermute | solution.py:25
  19.4 16.1 %collective-permute-start.2 = (f16[1552,128]{1,0:T(8,128)(2,1)S(1)}, f16[1552,128]{1,0:T(8,128)(2,1)S(1)}, u32[]{:S(2)}, u32[]{:S(2)}) collective-permute-start(f16[1552,128]{1,0:T(8,128)(2,1)S(1)} %get-tuple-element.71), channel_id=1, source_target_pairs={{0,2},{1,3},{2,0},{3,1},{4,6},{5,7},{6,4},{7,5},{8,10},{9,11},{10,... | collective-permute-start | bytes 1191944 | tf_op jit(solution)/shard_map/ppermute | solution.py:25
  28.9 2.4 %collective-permute-start = (f32[16,96,128]{2,1,0:T(8,128)S(1)}, f32[16,96,128]{2,1,0:T(8,128)S(1)}, u32[]{:S(2)}, u32[]{:S(2)}) collective-permute-start(f32[16,96,128]{2,1,0:T(8,128)S(1)} %get-tuple-element.30), channel_id=1, source_target_pairs={{0,1},{1,0},{2,3},{3,2},{4,5},{5,4},{6,7},{7,6},{8,9},{9,8},{10,11... | collective-permute-start | bytes 2359304 | tf_op jit(solution)/shard_map/cond/branch_1_fun/ppermute | solution.py:25
  40.3 2.5 %collective-permute-start.3 = (bf16[16,24,128]{2,1,0:T(8,128)(2,1)S(1)}, bf16[16,24,128]{2,1,0:T(8,128)(2,1)S(1)}, u32[]{:S(2)}, u32[]{:S(2)}) collective-permute-start(bf16[16,24,128]{2,1,0:T(8,128)(2,1)S(1)} %get-tuple-element.48), channel_id=1, source_target_pairs={{0,1},{1,0},{2,3},{3,2},{4,5},{5,4},{6,7},{7,6},{8,9},{9,8},{10,11... | collective-permute-start | bytes 294920 | tf_op jit(solution)/shard_map/ppermute | solution.py:25
  41.2 5.1 %collective-permute-start.4 = (bf16[16,24,128]{2,1,0:T(8,128)(2,1)S(1)}, bf16[16,24,128]{2,1,0:T(8,128)(2,1)S(1)}, u32[]{:S(2)}, u32[]{:S(2)}) collective-permute-start(bf16[16,24,128]{2,1,0:T(8,128)(2,1)S(1)} %get-tuple-element.49), channel_id=1, source_target_pairs={{0,2},{1,3},{2,0},{3,1},{4,6},{5,7},{6,4},{7,5},{8,10},{9,11},{10,... | collective-permute-start | bytes 294920 | tf_op jit(solution)/shard_map/ppermute | solution.py:25
  42.6 5.1 %collective-permute-start.5 = (bf16[16,24,128]{2,1,0:T(8,128)(2,1)S(1)}, bf16[16,24,128]{2,1,0:T(8,128)(2,1)S(1)}, u32[]{:S(2)}, u32[]{:S(2)}) collective-permute-start(bf16[16,24,128]{2,1,0:T(8,128)(2,1)S(1)} %get-tuple-element.50), channel_id=1, source_target_pairs={{0,3},{1,2},{2,1},{3,0},{4,7},{5,6},{6,5},{7,4},{8,11},{9,10},{10,... | collective-permute-start | bytes 294920 | tf_op jit(solution)/shard_map/ppermute | solution.py:25
  48.4 9.0 %collective-permute-start.7 = (f16[400,128]{1,0:T(8,128)(2,1)S(1)}, f16[400,128]{1,0:T(8,128)(2,1)S(1)}, u32[]{:S(2)}, u32[]{:S(2)}) collective-permute-start(f16[400,128]{1,0:T(8,128)(2,1)S(1)} %fusion.10), channel_id=1, source_target_pairs={{0,8},{1,9},{2,10},{3,11},{4,12},{5,13},{6,14},{7,15},{8,0},{9,1},... | collective-permute-start | bytes 307208 | tf_op jit(solution)/shard_map/ppermute | solution.py:25
  50.5 6.9 %collective-permute-start.6 = (f16[400,128]{1,0:T(8,128)(2,1)S(1)}, f16[400,128]{1,0:T(8,128)(2,1)S(1)}, u32[]{:S(2)}, u32[]{:S(2)}) collective-permute-start(f16[400,128]{1,0:T(8,128)(2,1)S(1)} %fusion.9), channel_id=1, source_target_pairs={{0,4},{1,5},{2,6},{3,7},{4,0},{5,1},{6,2},{7,3},{8,12},{9,13},{10,... | collective-permute-start | bytes 307208 | tf_op jit(solution)/shard_map/ppermute | solution.py:25
  51.4 8.6 %collective-permute-start.8 = (f16[400,128]{1,0:T(8,128)(2,1)S(1)}, f16[400,128]{1,0:T(8,128)(2,1)S(1)}, u32[]{:S(2)}, u32[]{:S(2)}) collective-permute-start(f16[400,128]{1,0:T(8,128)(2,1)S(1)} %fusion.11), channel_id=1, source_target_pairs={{0,12},{1,13},{2,14},{3,15},{4,8},{5,9},{6,10},{7,11},{8,4},{9,5},... | collective-permute-start | bytes 307208 | tf_op jit(solution)/shard_map/ppermute | solution.py:25

commit v26 on v25

--- a/solution.py
+++ b/solution.py
@@ -13,7 +13,7 @@
 LANES = 128
 F16_TOP = 14.0
 PLANE = 4
-HELD = 24
+HELD = 32
 MARK_ROWS = 16
 
 
@@ -216,7 +216,7 @@
 
 def adapter_kernel(parts, ranks, me_ref, rows_ref, expand_hbm, shrink_hbm, *refs):
     out_refs = refs[:PLANE]
-    shrink_ref, expand_ref, total_ref, own_ref, sems, expand_sem = refs[PLANE:]
+    shrink_ref, expand_ref, own_ref, sems, expand_sem = refs[PLANE:]
     me = me_ref[0]
     group, _, depth = shrink_ref.shape
     blocks = MOST // BLOCK
@@ -228,22 +228,26 @@
             sems.at[source],
         )
 
-    for source in range(group):
+    for source in range(group // 2):
         copy(source).start()
-    expand_copy = pltpu.make_async_copy(expand_hbm, expand_ref, expand_sem)
-    expand_copy.start()
     for source in range(group):
         own = rows_ref[source * blocks : (source + 1) * blocks]
         own_ref[source, :MOST] = own.reshape(MOST, depth)
-    total = jnp.zeros((MOST, total_ref.shape[1]), jnp.float32)
+        if source == group // 2 - 1:
+            for later in range(group // 2, group):
+                copy(later).start()
+            expand_copy = pltpu.make_async_copy(expand_hbm, expand_ref, expand_sem)
+            expand_copy.start()
+    total = jnp.zeros((MOST, shrink_ref.shape[1]), jnp.float32)
     for source in range(group):
         copy(source).wait()
         total += lax.dot_general(
-            own_ref[source, :MOST], shrink_ref[source], (((1,), (1,)), ((), ())), preferred_element_type=jnp.float32
+            own_ref[source, :MOST],
+            shrink_ref[source],
+            (((1,), (1,)), ((), ())),
+            preferred_element_type=jnp.float32,
         )
-    total_ref[...] = jnp.zeros_like(total_ref)
-    total_ref[:MOST] = total
-    rank_rows = total_ref[...].astype(jnp.bfloat16)
+    rank_rows = total.astype(jnp.bfloat16)
     expand_copy.wait()
     width = parts * LANES
     for k in range(PLANE):
@@ -253,7 +257,9 @@
             piece = jnp.dot(rank_rows, expand_ref[:, columns], preferred_element_type=jnp.float32)
             piece = piece.astype(jnp.bfloat16)
             for part in range(parts):
-                out_refs[k][line * parts + part] = piece[:, part * LANES : (part + 1) * LANES]
+                first = (line * parts + part) * blocks
+                lanes = piece[:, part * LANES : (part + 1) * LANES]
+                out_refs[k][first : first + blocks] = lanes.reshape(blocks, BLOCK, LANES)
 
 
 def adapter_output(gathered, shrink, expand, group, me, ranks):
@@ -261,7 +267,7 @@
     model_width = expand.shape[1]
     depth = gathered.shape[2]
     parts = model_width // group // LANES
-    held = (model_width // PLANE // LANES, HELD, LANES)
+    held = (model_width // PLANE // LANES * (MOST // BLOCK), BLOCK, LANES)
     vmem = pl.BlockSpec(memory_space=pltpu.VMEM)
     return pl.pallas_call(
         functools.partial(adapter_kernel, parts, ranks),
@@ -276,8 +282,7 @@
         scratch_shapes=[
             pltpu.VMEM((group, rank, depth), jnp.bfloat16),
             pltpu.VMEM((rank, model_width), jnp.bfloat16),
-            pltpu.VMEM((HELD, rank), jnp.float32),
-            pltpu.VMEM((group, 2 * 16, depth), jnp.bfloat16),
+            pltpu.VMEM((group, HELD, depth), jnp.bfloat16),
             pltpu.SemaphoreType.DMA((group,)),
             pltpu.SemaphoreType.DMA,
         ],
@@ -287,10 +292,13 @@
 
 def merge_kernel(pair_ref, pick_ref, *refs):
     in_refs, out_ref, held_ref = refs[:PLANE], refs[PLANE], refs[PLANE + 1]
-    for k in range(PLANE):
-        held_ref[:, k * HELD : (k + 1) * HELD] = in_refs[k][...]
+    blocks = MOST // BLOCK
+    held_ref[...] = jnp.zeros_like(held_ref)
     pick = pick_ref[...]
     for part in range(pair_ref.shape[0]):
+        for k in range(PLANE):
+            rows = in_refs[k][part * blocks : (part + 1) * blocks].reshape(MOST, LANES)
+            held_ref[part, k * HELD : k * HELD + MOST] = rows
         adapter_rows = lax.dot_general(
             pick, held_ref[part], (((0,), (0,)), ((), ())), preferred_element_type=jnp.float32
         )

time: 61.1 us -> 60.6 us (level)
  no operation moved by 1% of the time
where the time goes in v26:
time: 60.6 us; the launch traced here: 60.4 us
  Pallas kernels  21.5 us (35%)
  waiting for transfers between devices  18.6 us (31%)
  starting transfers between devices  16.6 us (27%)
  other arithmetic  1.93 us (3%)
  local copies, waits for them, and re-layouts  0.9 us (1%)
  between operations  0.81 us (1%)
    ppermute x9, waiting for transfers between devices, xor_permute(): return lax.ppermute(value, 'tp', [(i, i ^ offset) for i in range(group)])  17.6 us
    pallas_call x3, Pallas kernels, column_blocks(): pl.pallas_call(functools.partial(column_blocks_kernel, groups), out_shape...  14.8 us
    ppermute x9, starting transfers between devices, xor_permute(): return lax.ppermute(value, 'tp', [(i, i ^ offset) for i in range(group)])  9.25 us
    all_to_all x1, starting transfers between devices, shards_by_blocks(): lax.all_to_all(packed, 'tp', split_axis=0, concat_axis=0, axis_index_grou...  7.37 us
    pallas_call x1, Pallas kernels, adapter_output(): pl.pallas_call(functools.partial(adapter_kernel, parts, ranks), out_shape...  3.79 us
    pallas_call x1, Pallas kernels, pack_rows(): pl.pallas_call(functools.partial(pack_kernel, blocks, orders), out_shape=...  2.49 us
  transfers between devices with their start and end apart: 10, of which 7 were waited for; matrix products, arithmetic and copies ran while one was open for 3% of the time, Pallas kernels for 24%

profile of v26, /device:TPU:0, one launch (start us, length us, event | category | flops | bytes accessed | tf_op | source)
XLA Modules:
  0.0 60.4 jit_solution(7362235724094578897)
XLA Ops:
  0.0 2.5 %shard_map.64 = (bf16[80,4,1792]{2,1,0:T(4,128)(2,1)}, bf16[128,96]{1,0:T(8,128)(2,1)S(1)}, s32[16]{0:T(128)S(1)}, bf16[96,1792]{1,0:T(8,128)(2,1)S(1)}) custom-call(s32[1]{0:T(128)} %bitcast.2.me_ref, s32[16]{0:T(128)} %slot_hbm.1, s32[1,96]{1,0:T(1,128)} %bitcast.56, bf16[96,1792]{1,0:T(8,128)(2,1)} %hidden_hbm.1), custom_call_target="tpu_custom_call" | custom-call | tf_op jit(solution)/shard_map/pallas_call | solution.py:197
  2.5 7.4 %all-to-all-start = ((bf16[80,4,1792]{2,1,0:T(4,128)(2,1)}), bf16[80,4,1792]{2,1,0:T(4,128)(2,1)S(1)}, u32[]{:S(2)}, u32[]{:S(2)}) async-start(bf16[80,4,1792]{2,1,0:T(4,128)(2,1)} %get-tuple-element.45), calls=%async_computation | async-start | bytes 2293760 | tf_op jit(solution)/shard_map/all_to_all | solution.py:334
  9.9 9.4 %conditional.2 = (f16[1552,128]{1,0:T(8,128)(2,1)S(1)}) conditional(s32[]{:T(128)} %bitcast.4, () %tuple.19, (s32[16]{0:T(128)S(1)}, bf16[96,1792]{1,0:T(8,128)(2,1)S(1)}, bf16[1792,8192]{1,0:T(8,128)(2,1)}) %tuple.20), branch_computations={%region_0.0_spmd, %region_1.3_spmd} | conditional | flops 1581488 | bytes 7479232 | solution.py:109
  9.9 0.1 fusion.29
  10.0 4.2 %branch_1_fun.4 = f32[16,96,128]{2,1,0:T(8,128)S(1)} custom-call(s32[4]{0:T(128)S(1)} %get-tuple-element.58.order_ref, bf16[96,1792]{1,0:T(8,128)(2,1)S(1)} %get-tuple-element.24.hidden_ref, bf16[1792,8192]{1,0:T(8,128)(2,1)} %get-tuple-element.25.down_ref), custom_call_target="tpu_custom_call" | custom-call | flops 1000 | bytes 1000 | tf_op jit(solution)/shard_map/cond/branch_1_fun/pallas_call | solution.py:62
  14.2 0.5 collective-permute-start.1
  14.7 4.2 %branch_1_fun.3 = f32[16,96,128]{2,1,0:T(8,128)S(1)} custom-call(s32[4]{0:T(128)S(1)} %get-tuple-element.59.order_ref, bf16[96,1792]{1,0:T(8,128)(2,1)S(1)} %get-tuple-element.24.hidden_ref, bf16[1792,8192]{1,0:T(8,128)(2,1)} %get-tuple-element.25.down_ref), custom_call_target="tpu_custom_call" | custom-call | flops 1000 | bytes 1000 | tf_op jit(solution)/shard_map/cond/branch_1_fun/pallas_call | solution.py:62
  18.9 0.0 collective-permute-done.1
  18.9 0.2 abs_reduce_fusion
  19.1 0.2 multiply_convert_fusion
  19.3 0.1 fusion.1
  19.4 1.7 %collective-permute-start.2 = (f16[1552,128]{1,0:T(8,128)(2,1)S(1)}, f16[1552,128]{1,0:T(8,128)(2,1)S(1)}, u32[]{:S(2)}, u32[]{:S(2)}) collective-permute-start(f16[1552,128]{1,0:T(8,128)(2,1)S(1)} %get-tuple-element.71), channel_id=1, source_target_pairs={{0,2},{1,3},{2,0},{3,1},{4,6},{5,7},{6,4},{7,5},{8,10},{9,11},{10,... | collective-permute-start | bytes 1191944 | tf_op jit(solution)/shard_map/ppermute | solution.py:25
  21.1 0.6 %slice.52 = s32[1]{0:T(128)} slice(s32[16]{0:T(128)S(1)} %get-tuple-element.43), slice={[1:2]} | slice | bytes 8 | tf_op jit(solution)/shard_map/slice | solution.py:120
  22.4 9.0 %conditional.3 = (f32[16,96,128]{2,1,0:T(8,128)S(1)}) conditional(s32[]{:T(128)} %bitcast.5, () %tuple.22, (s32[16]{0:T(128)S(1)}, bf16[96,1792]{1,0:T(8,128)(2,1)S(1)}, bf16[1792,8192]{1,0:T(8,128)(2,1)}) %tuple.23), branch_computations={%region_3.4_spmd, %region_4.5_spmd} | conditional | flops 197608 | bytes 5506136 | solution.py:120
  22.4 0.1 slice.36.order_ref
  22.4 6.4 %branch_1_fun.5 = (f32[16,96,128]{2,1,0:T(8,128)S(1)}, f32[16,96,128]{2,1,0:T(8,128)S(1)}) custom-call(s32[8]{0:T(128)S(1)} %slice.36.order_ref, bf16[96,1792]{1,0:T(8,128)(2,1)S(1)} %get-tuple-element.27.hidden_ref, bf16[1792,8192]{1,0:T(8,128)(2,1)} %get-tuple-element.28.down_ref), custom_call_target="tpu_custom_call" | custom-call | flops 1000 | bytes 1000 | tf_op jit(solution)/shard_map/cond/branch_1_fun/pallas_call | solution.py:62
  28.9 0.1 collective-permute-start
  29.0 2.2 %collective-permute-done = f32[16,96,128]{2,1,0:T(8,128)S(1)} collective-permute-done((f32[16,96,128]{2,1,0:T(8,128)S(1)}, f32[16,96,128]{2,1,0:T(8,128)S(1)}, u32[]{:S(2)}, u32[]{:S(2)}) %collective-permute-start) | collective-permute-done | bytes 786464 | tf_op jit(solution)/shard_map/cond/branch_1_fun/ppermute | solution.py:25
  31.2 0.1 add.39
  31.3 4.1 %collective-permute-done.2 = f16[1552,128]{1,0:T(8,128)(2,1)S(1)} collective-permute-done((f16[1552,128]{1,0:T(8,128)(2,1)S(1)}, f16[1552,128]{1,0:T(8,128)(2,1)S(1)}, u32[]{:S(2)}, u32[]{:S(2)}) %collective-permute-start.2) | collective-permute-done | bytes 397344 | tf_op jit(solution)/shard_map/ppermute | solution.py:25
  35.4 0.1 slice.65
  35.5 1.0 %all-to-all-done.rows_ref = bf16[80,4,1792]{2,1,0:T(4,128)(2,1)S(1)} async-done(((bf16[80,4,1792]{2,1,0:T(4,128)(2,1)}), bf16[80,4,1792]{2,1,0:T(4,128)(2,1)S(1)}, u32[]{:S(2)}, u32[]{:S(2)}) %all-to-all-start) | async-done | bytes 1146912 | tf_op jit(solution)/shard_map/all_to_all | solution.py:334
  36.5 3.8 %shard_map.65 = (bf16[80,4,128]{2,1,0:T(4,128)(2,1)S(1)}, bf16[80,4,128]{2,1,0:T(4,128)(2,1)S(1)}, bf16[80,4,128]{2,1,0:T(4,128)(2,1)S(1)}, bf16[80,4,128]{2,1,0:T(4,128)(2,1)S(1)}) custom-call(s32[1]{0:T(128)} %bitcast.2.me_ref, bf16[80,4,1792]{2,1,0:T(4,128)(2,1)S(1)} %all-to-all-done.rows_ref, bf16[64,8192]{1,0:T(8,128)(2,1)} %bitcast.48, ...), custom_call_target="tpu_custom_call" | custom-call | tf_op jit(solution)/shard_map/pallas_call | solution.py:272
  40.3 0.8 %collective-permute-start.3 = (bf16[80,4,128]{2,1,0:T(4,128)(2,1)S(1)}, bf16[80,4,128]{2,1,0:T(4,128)(2,1)S(1)}, u32[]{:S(2)}, u32[]{:S(2)}) collective-permute-start(bf16[80,4,128]{2,1,0:T(4,128)(2,1)S(1)} %get-tuple-element.48), channel_id=1, source_target_pairs={{0,1},{1,0},{2,3},{3,2},{4,5},{5,4},{6,7},{7,6},{8,9},{9,8},{10,11... | collective-permute-start | bytes 245768 | tf_op jit(solution)/shard_map/ppermute | solution.py:25
  41.1 1.5 %collective-permute-start.4 = (bf16[80,4,128]{2,1,0:T(4,128)(2,1)S(1)}, bf16[80,4,128]{2,1,0:T(4,128)(2,1)S(1)}, u32[]{:S(2)}, u32[]{:S(2)}) collective-permute-start(bf16[80,4,128]{2,1,0:T(4,128)(2,1)S(1)} %get-tuple-element.49), channel_id=1, source_target_pairs={{0,2},{1,3},{2,0},{3,1},{4,6},{5,7},{6,4},{7,5},{8,10},{9,11},{10,... | collective-permute-start | bytes 245768 | tf_op jit(solution)/shard_map/ppermute | solution.py:25
  42.6 0.0 collective-permute-start.5
  42.6 0.2 fusion.2.pair_ref
  42.8 0.0 collective-permute-done.3.refs_1_
  42.8 2.8 %collective-permute-done.4.refs_2_ = bf16[80,4,128]{2,1,0:T(4,128)(2,1)S(1)} collective-permute-done((bf16[80,4,128]{2,1,0:T(4,128)(2,1)S(1)}, bf16[80,4,128]{2,1,0:T(4,128)(2,1)S(1)}, u32[]{:S(2)}, u32[]{:S(2)}) %collective-permute-start.4) | collective-permute-done | bytes 81952 | tf_op jit(solution)/shard_map/ppermute | solution.py:25
  45.6 1.8 %collective-permute-done.5.refs_3_ = bf16[80,4,128]{2,1,0:T(4,128)(2,1)S(1)} collective-permute-done((bf16[80,4,128]{2,1,0:T(4,128)(2,1)S(1)}, bf16[80,4,128]{2,1,0:T(4,128)(2,1)S(1)}, u32[]{:S(2)}, u32[]{:S(2)}) %collective-permute-start.5) | collective-permute-done | bytes 81952 | tf_op jit(solution)/shard_map/ppermute | solution.py:25
  47.3 0.4 shard_map.66
  47.8 0.2 abs_reduce_fusion.3
  47.9 0.1 multiply_convert_fusion.3
  48.1 2.0 %collective-permute-start.7 = (f16[400,128]{1,0:T(8,128)(2,1)S(1)}, f16[400,128]{1,0:T(8,128)(2,1)S(1)}, u32[]{:S(2)}, u32[]{:S(2)}) collective-permute-start(f16[400,128]{1,0:T(8,128)(2,1)S(1)} %fusion.10), channel_id=1, source_target_pairs={{0,8},{1,9},{2,10},{3,11},{4,12},{5,13},{6,14},{7,15},{8,0},{9,1},... | collective-permute-start | bytes 307208 | tf_op jit(solution)/shard_map/ppermute | solution.py:25
  50.2 0.6 %collective-permute-start.6 = (f16[400,128]{1,0:T(8,128)(2,1)S(1)}, f16[400,128]{1,0:T(8,128)(2,1)S(1)}, u32[]{:S(2)}, u32[]{:S(2)}) collective-permute-start(f16[400,128]{1,0:T(8,128)(2,1)S(1)} %fusion.9), channel_id=1, source_target_pairs={{0,4},{1,5},{2,6},{3,7},{4,0},{5,1},{6,2},{7,3},{8,12},{9,13},{10,... | collective-permute-start | bytes 307208 | tf_op jit(solution)/shard_map/ppermute | solution.py:25
  50.8 1.9 %collective-permute-start.8 = (f16[400,128]{1,0:T(8,128)(2,1)S(1)}, f16[400,128]{1,0:T(8,128)(2,1)S(1)}, u32[]{:S(2)}, u32[]{:S(2)}) collective-permute-start(f16[400,128]{1,0:T(8,128)(2,1)S(1)} %fusion.11), channel_id=1, source_target_pairs={{0,12},{1,13},{2,14},{3,15},{4,8},{5,9},{6,10},{7,11},{8,4},{9,5},... | collective-permute-start | bytes 307208 | tf_op jit(solution)/shard_map/ppermute | solution.py:25
  52.8 4.8 %collective-permute-done.7 = f16[400,128]{1,0:T(8,128)(2,1)S(1)} collective-permute-done((f16[400,128]{1,0:T(8,128)(2,1)S(1)}, f16[400,128]{1,0:T(8,128)(2,1)S(1)}, u32[]{:S(2)}, u32[]{:S(2)}) %collective-permute-start.7) | collective-permute-done | bytes 102432 | tf_op jit(solution)/shard_map/ppermute | solution.py:25
  57.6 0.0 collective-permute-done.6
  57.6 1.9 %collective-permute-done.8 = f16[400,128]{1,0:T(8,128)(2,1)S(1)} collective-permute-done((f16[400,128]{1,0:T(8,128)(2,1)S(1)}, f16[400,128]{1,0:T(8,128)(2,1)S(1)}, u32[]{:S(2)}, u32[]{:S(2)}) %collective-permute-start.8) | collective-permute-done | bytes 102432 | tf_op jit(solution)/shard_map/ppermute | solution.py:25
  59.6 0.8 %copy_bitcast_fusion = bf16[96,512]{1,0:T(8,128)(2,1)} fusion(f16[4,96,128]{2,1,0:T(8,128)(2,1)S(1)} %bitcast.54, f16[4,96,128]{2,1,0:T(8,128)(2,1)S(1)} %bitcast.51, f16[4,96,128]{2,1,0:T(8,128)(2,1)S(1)} %bitcast.52, f32[16,96,128]{2,1,0:T(8,128)S(1)} %shard_map.66, f32[96]{0:T(128)S(1)} %fusion.16, f32[96]{0:T(128)S(1)} %fusion.20, f32[96]{0:T(128)S(1)} %fusion.24), kind=kLoop, calls=%fused_computation.31 | loop fusion | flops 491520 | bytes 591360 | tf_op jit(solution)/shard_map/convert_element_type | solution.py:345
  (13 shorter events, 0.2 us)
Async XLA Ops:
  2.5 34.0 %all-to-all-start = ((bf16[80,4,1792]{2,1,0:T(4,128)(2,1)}), bf16[80,4,1792]{2,1,0:T(4,128)(2,1)S(1)}, u32[]{:S(2)}, u32[]{:S(2)}) async-start(bf16[80,4,1792]{2,1,0:T(4,128)(2,1)} %get-tuple-element.45), calls=%async_computation | async-start | bytes 2293760 | tf_op jit(solution)/shard_map/all_to_all | solution.py:334
  14.2 4.7 %collective-permute-start.1 = (f32[16,96,128]{2,1,0:T(8,128)S(1)}, f32[16,96,128]{2,1,0:T(8,128)S(1)}, u32[]{:S(2)}, u32[]{:S(2)}) collective-permute-start(f32[16,96,128]{2,1,0:T(8,128)S(1)} %branch_1_fun.4), channel_id=1, source_target_pairs={{0,1},{1,0},{2,3},{3,2},{4,5},{5,4},{6,7},{7,6},{8,9},{9,8},{10,11... | collective-permute-start | bytes 2359304 | tf_op jit(solution)/shard_map/cond/branch_1_fun/ppermute | solution.py:25
  19.4 16.1 %collective-permute-start.2 = (f16[1552,128]{1,0:T(8,128)(2,1)S(1)}, f16[1552,128]{1,0:T(8,128)(2,1)S(1)}, u32[]{:S(2)}, u32[]{:S(2)}) collective-permute-start(f16[1552,128]{1,0:T(8,128)(2,1)S(1)} %get-tuple-element.71), channel_id=1, source_target_pairs={{0,2},{1,3},{2,0},{3,1},{4,6},{5,7},{6,4},{7,5},{8,10},{9,11},{10,... | collective-permute-start | bytes 1191944 | tf_op jit(solution)/shard_map/ppermute | solution.py:25
  28.9 2.4 %collective-permute-start = (f32[16,96,128]{2,1,0:T(8,128)S(1)}, f32[16,96,128]{2,1,0:T(8,128)S(1)}, u32[]{:S(2)}, u32[]{:S(2)}) collective-permute-start(f32[16,96,128]{2,1,0:T(8,128)S(1)} %get-tuple-element.30), channel_id=1, source_target_pairs={{0,1},{1,0},{2,3},{3,2},{4,5},{5,4},{6,7},{7,6},{8,9},{9,8},{10,11... | collective-permute-start | bytes 2359304 | tf_op jit(solution)/shard_map/cond/branch_1_fun/ppermute | solution.py:25
  40.3 2.5 %collective-permute-start.3 = (bf16[80,4,128]{2,1,0:T(4,128)(2,1)S(1)}, bf16[80,4,128]{2,1,0:T(4,128)(2,1)S(1)}, u32[]{:S(2)}, u32[]{:S(2)}) collective-permute-start(bf16[80,4,128]{2,1,0:T(4,128)(2,1)S(1)} %get-tuple-element.48), channel_id=1, source_target_pairs={{0,1},{1,0},{2,3},{3,2},{4,5},{5,4},{6,7},{7,6},{8,9},{9,8},{10,11... | collective-permute-start | bytes 245768 | tf_op jit(solution)/shard_map/ppermute | solution.py:25
  41.1 4.4 %collective-permute-start.4 = (bf16[80,4,128]{2,1,0:T(4,128)(2,1)S(1)}, bf16[80,4,128]{2,1,0:T(4,128)(2,1)S(1)}, u32[]{:S(2)}, u32[]{:S(2)}) collective-permute-start(bf16[80,4,128]{2,1,0:T(4,128)(2,1)S(1)} %get-tuple-element.49), channel_id=1, source_target_pairs={{0,2},{1,3},{2,0},{3,1},{4,6},{5,7},{6,4},{7,5},{8,10},{9,11},{10,... | collective-permute-start | bytes 245768 | tf_op jit(solution)/shard_map/ppermute | solution.py:25
  42.6 4.7 %collective-permute-start.5 = (bf16[80,4,128]{2,1,0:T(4,128)(2,1)S(1)}, bf16[80,4,128]{2,1,0:T(4,128)(2,1)S(1)}, u32[]{:S(2)}, u32[]{:S(2)}) collective-permute-start(bf16[80,4,128]{2,1,0:T(4,128)(2,1)S(1)} %get-tuple-element.50), channel_id=1, source_target_pairs={{0,3},{1,2},{2,1},{3,0},{4,7},{5,6},{6,5},{7,4},{8,11},{9,10},{10,... | collective-permute-start | bytes 245768 | tf_op jit(solution)/shard_map/ppermute | solution.py:25
  48.1 9.4 %collective-permute-start.7 = (f16[400,128]{1,0:T(8,128)(2,1)S(1)}, f16[400,128]{1,0:T(8,128)(2,1)S(1)}, u32[]{:S(2)}, u32[]{:S(2)}) collective-permute-start(f16[400,128]{1,0:T(8,128)(2,1)S(1)} %fusion.10), channel_id=1, source_target_pairs={{0,8},{1,9},{2,10},{3,11},{4,12},{5,13},{6,14},{7,15},{8,0},{9,1},... | collective-permute-start | bytes 307208 | tf_op jit(solution)/shard_map/ppermute | solution.py:25
  50.2 7.4 %collective-permute-start.6 = (f16[400,128]{1,0:T(8,128)(2,1)S(1)}, f16[400,128]{1,0:T(8,128)(2,1)S(1)}, u32[]{:S(2)}, u32[]{:S(2)}) collective-permute-start(f16[400,128]{1,0:T(8,128)(2,1)S(1)} %fusion.9), channel_id=1, source_target_pairs={{0,4},{1,5},{2,6},{3,7},{4,0},{5,1},{6,2},{7,3},{8,12},{9,13},{10,... | collective-permute-start | bytes 307208 | tf_op jit(solution)/shard_map/ppermute | solution.py:25
  50.8 8.8 %collective-permute-start.8 = (f16[400,128]{1,0:T(8,128)(2,1)S(1)}, f16[400,128]{1,0:T(8,128)(2,1)S(1)}, u32[]{:S(2)}, u32[]{:S(2)}) collective-permute-start(f16[400,128]{1,0:T(8,128)(2,1)S(1)} %fusion.11), channel_id=1, source_target_pairs={{0,12},{1,13},{2,14},{3,15},{4,8},{5,9},{6,10},{7,11},{8,4},{9,5},... | collective-permute-start | bytes 307208 | tf_op jit(solution)/shard_map/ppermute | solution.py:25

commit v27 on v26

--- a/solution.py
+++ b/solution.py
@@ -14,7 +14,7 @@
 F16_TOP = 14.0
 PLANE = 4
 HELD = 32
-MARK_ROWS = 16
+MARK_ROWS = 8
 
 
 def in_hbm(value):
@@ -124,14 +124,19 @@
 def line_sums(pair, group, width):
     rows = pair.shape[1]
     parts = width // LANES
+
+    def flat(value):
+        return jnp.transpose(value, (1, 0, 2)).reshape(rows, width)
+
     arrived = [
-        xor_permute(pack_scaled(pair[i * parts : (i + 1) * parts]), group, 4 * i)
-        for i in range(1, group // 4)
+        xor_permute(pack_scaled(pair[i * parts : (i + 1) * parts]), group, PLANE * i)
+        for i in range(1, group // PLANE)
     ]
     total = pair[:parts]
-    for packed in arrived:
+    for packed in arrived[:-1]:
         total = total + unpack_scaled(packed, rows)
-    return jnp.transpose(total, (1, 0, 2)).reshape(rows, width)
+    total = lax.optimization_barrier(flat(total))
+    return total + flat(unpack_scaled(arrived[-1], rows))
 
 
 def pack_kernel(
@@ -157,7 +162,7 @@
         pltpu.make_async_copy(adapter_hbm, adapter_ref, sems.at[1]),
         pltpu.make_async_copy(hidden_hbm, hidden_ref, sems.at[2]),
     ]
-    for copy in copies:
+    for copy in copies[::-1]:
         copy.start()
     for i, offset in enumerate(orders):
         order_ref[i] = me_ref[0] ^ offset
@@ -351,7 +356,7 @@
     group = lax.axis_size("tp")
     rows, depth = hidden.shape
     width = down_matrix.shape[1] // group
-    if width % LANES == 0 and depth % LANES == 0 and rows <= LANES and group >= PLANE and group & (group - 1) == 0:
+    if width % LANES == 0 and depth % LANES == 0 and rows <= LANES and group > PLANE and group & (group - 1) == 0:
         return shards_by_blocks(
             hidden, down_matrix, shrink_matrices, expand_matrices, adapter_of_row, adapter_holder_slot
         )

time: 60.6 us -> 60.9 us (level)
  no operation moved by 1% of the time
where the time goes in v27:
time: 60.9 us; the launch traced here: 60.7 us
  Pallas kernels  21.5 us (35%)
  waiting for transfers between devices  19.2 us (32%)
  starting transfers between devices  16.2 us (27%)
  other arithmetic  1.97 us (3%)
  local copies, waits for them, and re-layouts  0.9 us (1%)
  between operations  0.83 us (1%)
    ppermute x9, waiting for transfers between devices, xor_permute(): return lax.ppermute(value, 'tp', [(i, i ^ offset) for i in range(group)])  18.2 us
    pallas_call x3, Pallas kernels, column_blocks(): pl.pallas_call(functools.partial(column_blocks_kernel, groups), out_shape...  14.8 us
    ppermute x9, starting transfers between devices, xor_permute(): return lax.ppermute(value, 'tp', [(i, i ^ offset) for i in range(group)])  8.85 us
    all_to_all x1, starting transfers between devices, shards_by_blocks(): lax.all_to_all(packed, 'tp', split_axis=0, concat_axis=0, axis_index_grou...  7.37 us
    pallas_call x1, Pallas kernels, adapter_output(): pl.pallas_call(functools.partial(adapter_kernel, parts, ranks), out_shape...  3.79 us
    pallas_call x1, Pallas kernels, pack_rows(): pl.pallas_call(functools.partial(pack_kernel, blocks, orders), out_shape=...  2.48 us
  transfers between devices with their start and end apart: 10, of which 7 were waited for; matrix products, arithmetic and copies ran while one was open for 3% of the time, Pallas kernels for 24%

profile of v27, /device:TPU:0, one launch (start us, length us, event | category | flops | bytes accessed | tf_op | source)
XLA Modules:
  0.0 60.7 jit_solution(15195592122078369370)
XLA Ops:
  0.0 2.5 %shard_map.64 = (bf16[80,4,1792]{2,1,0:T(4,128)(2,1)}, bf16[128,96]{1,0:T(8,128)(2,1)S(1)}, s32[16]{0:T(128)S(1)}, bf16[96,1792]{1,0:T(8,128)(2,1)S(1)}) custom-call(s32[1]{0:T(128)} %bitcast.2.me_ref, s32[16]{0:T(128)} %slot_hbm.1, s32[1,96]{1,0:T(1,128)} %bitcast.64, bf16[96,1792]{1,0:T(8,128)(2,1)} %hidden_hbm.1), custom_call_target="tpu_custom_call" | custom-call | tf_op jit(solution)/shard_map/pallas_call | solution.py:202
  2.5 7.4 %all-to-all-start = ((bf16[80,4,1792]{2,1,0:T(4,128)(2,1)}), bf16[80,4,1792]{2,1,0:T(4,128)(2,1)S(1)}, u32[]{:S(2)}, u32[]{:S(2)}) async-start(bf16[80,4,1792]{2,1,0:T(4,128)(2,1)} %get-tuple-element.45), calls=%async_computation | async-start | bytes 2293760 | tf_op jit(solution)/shard_map/all_to_all | solution.py:339
  9.9 9.4 %conditional.2 = (f16[1544,128]{1,0:T(8,128)(2,1)S(1)}) conditional(s32[]{:T(128)} %bitcast.4, () %tuple.19, (s32[16]{0:T(128)S(1)}, bf16[96,1792]{1,0:T(8,128)(2,1)S(1)}, bf16[1792,8192]{1,0:T(8,128)(2,1)}) %tuple.20), branch_computations={%region_0.0_spmd, %region_1.3_spmd} | conditional | flops 1578416 | bytes 7477184 | solution.py:109
  9.9 0.1 fusion.29
  10.0 4.2 %branch_1_fun.4 = f32[16,96,128]{2,1,0:T(8,128)S(1)} custom-call(s32[4]{0:T(128)S(1)} %get-tuple-element.58.order_ref, bf16[96,1792]{1,0:T(8,128)(2,1)S(1)} %get-tuple-element.24.hidden_ref, bf16[1792,8192]{1,0:T(8,128)(2,1)} %get-tuple-element.25.down_ref), custom_call_target="tpu_custom_call" | custom-call | flops 1000 | bytes 1000 | tf_op jit(solution)/shard_map/cond/branch_1_fun/pallas_call | solution.py:62
  14.2 0.5 collective-permute-start.1
  14.7 4.2 %branch_1_fun.3 = f32[16,96,128]{2,1,0:T(8,128)S(1)} custom-call(s32[4]{0:T(128)S(1)} %get-tuple-element.59.order_ref, bf16[96,1792]{1,0:T(8,128)(2,1)S(1)} %get-tuple-element.24.hidden_ref, bf16[1792,8192]{1,0:T(8,128)(2,1)} %get-tuple-element.25.down_ref), custom_call_target="tpu_custom_call" | custom-call | flops 1000 | bytes 1000 | tf_op jit(solution)/shard_map/cond/branch_1_fun/pallas_call | solution.py:62
  18.9 0.0 collective-permute-done.1
  18.9 0.2 abs_reduce_fusion
  19.1 0.2 multiply_convert_fusion
  19.3 0.1 fusion.1
  19.4 1.7 %collective-permute-start.2 = (f16[1544,128]{1,0:T(8,128)(2,1)S(1)}, f16[1544,128]{1,0:T(8,128)(2,1)S(1)}, u32[]{:S(2)}, u32[]{:S(2)}) collective-permute-start(f16[1544,128]{1,0:T(8,128)(2,1)S(1)} %get-tuple-element.71), channel_id=1, source_target_pairs={{0,2},{1,3},{2,0},{3,1},{4,6},{5,7},{6,4},{7,5},{8,10},{9,11},{10,... | collective-permute-start | bytes 1185800 | tf_op jit(solution)/shard_map/ppermute | solution.py:25
  21.1 0.6 slice.52
  22.3 9.0 %conditional.3 = (f32[16,96,128]{2,1,0:T(8,128)S(1)}) conditional(s32[]{:T(128)} %bitcast.5, () %tuple.22, (s32[16]{0:T(128)S(1)}, bf16[96,1792]{1,0:T(8,128)(2,1)S(1)}, bf16[1792,8192]{1,0:T(8,128)(2,1)}) %tuple.23), branch_computations={%region_3.4_spmd, %region_4.5_spmd} | conditional | flops 197608 | bytes 5506136 | solution.py:120
  22.4 0.1 slice.36.order_ref
  22.4 6.4 %branch_1_fun.5 = (f32[16,96,128]{2,1,0:T(8,128)S(1)}, f32[16,96,128]{2,1,0:T(8,128)S(1)}) custom-call(s32[8]{0:T(128)S(1)} %slice.36.order_ref, bf16[96,1792]{1,0:T(8,128)(2,1)S(1)} %get-tuple-element.27.hidden_ref, bf16[1792,8192]{1,0:T(8,128)(2,1)} %get-tuple-element.28.down_ref), custom_call_target="tpu_custom_call" | custom-call | flops 1000 | bytes 1000 | tf_op jit(solution)/shard_map/cond/branch_1_fun/pallas_call | solution.py:62
  28.8 0.1 collective-permute-start
  29.0 2.2 %collective-permute-done = f32[16,96,128]{2,1,0:T(8,128)S(1)} collective-permute-done((f32[16,96,128]{2,1,0:T(8,128)S(1)}, f32[16,96,128]{2,1,0:T(8,128)S(1)}, u32[]{:S(2)}, u32[]{:S(2)}) %collective-permute-start) | collective-permute-done | bytes 786464 | tf_op jit(solution)/shard_map/cond/branch_1_fun/ppermute | solution.py:25
  31.2 0.1 add.39
  31.3 4.1 %collective-permute-done.2 = f16[1544,128]{1,0:T(8,128)(2,1)S(1)} collective-permute-done((f16[1544,128]{1,0:T(8,128)(2,1)S(1)}, f16[1544,128]{1,0:T(8,128)(2,1)S(1)}, u32[]{:S(2)}, u32[]{:S(2)}) %collective-permute-start.2) | collective-permute-done | bytes 395296 | tf_op jit(solution)/shard_map/ppermute | solution.py:25
  35.4 0.1 slice.65
  35.5 1.0 %all-to-all-done.rows_ref = bf16[80,4,1792]{2,1,0:T(4,128)(2,1)S(1)} async-done(((bf16[80,4,1792]{2,1,0:T(4,128)(2,1)}), bf16[80,4,1792]{2,1,0:T(4,128)(2,1)S(1)}, u32[]{:S(2)}, u32[]{:S(2)}) %all-to-all-start) | async-done | bytes 1146912 | tf_op jit(solution)/shard_map/all_to_all | solution.py:339
  36.5 3.8 %shard_map.65 = (bf16[80,4,128]{2,1,0:T(4,128)(2,1)S(1)}, bf16[80,4,128]{2,1,0:T(4,128)(2,1)S(1)}, bf16[80,4,128]{2,1,0:T(4,128)(2,1)S(1)}, bf16[80,4,128]{2,1,0:T(4,128)(2,1)S(1)}) custom-call(s32[1]{0:T(128)} %bitcast.2.me_ref, bf16[80,4,1792]{2,1,0:T(4,128)(2,1)S(1)} %all-to-all-done.rows_ref, bf16[64,8192]{1,0:T(8,128)(2,1)} %bitcast.56, ...), custom_call_target="tpu_custom_call" | custom-call | tf_op jit(solution)/shard_map/pallas_call | solution.py:277
  40.3 0.8 %collective-permute-start.3 = (bf16[80,4,128]{2,1,0:T(4,128)(2,1)S(1)}, bf16[80,4,128]{2,1,0:T(4,128)(2,1)S(1)}, u32[]{:S(2)}, u32[]{:S(2)}) collective-permute-start(bf16[80,4,128]{2,1,0:T(4,128)(2,1)S(1)} %get-tuple-element.48), channel_id=1, source_target_pairs={{0,1},{1,0},{2,3},{3,2},{4,5},{5,4},{6,7},{7,6},{8,9},{9,8},{10,11... | collective-permute-start | bytes 245768 | tf_op jit(solution)/shard_map/ppermute | solution.py:25
  41.1 1.5 %collective-permute-start.4 = (bf16[80,4,128]{2,1,0:T(4,128)(2,1)S(1)}, bf16[80,4,128]{2,1,0:T(4,128)(2,1)S(1)}, u32[]{:S(2)}, u32[]{:S(2)}) collective-permute-start(bf16[80,4,128]{2,1,0:T(4,128)(2,1)S(1)} %get-tuple-element.49), channel_id=1, source_target_pairs={{0,2},{1,3},{2,0},{3,1},{4,6},{5,7},{6,4},{7,5},{8,10},{9,11},{10,... | collective-permute-start | bytes 245768 | tf_op jit(solution)/shard_map/ppermute | solution.py:25
  42.6 0.0 collective-permute-start.5
  42.6 0.2 fusion.2.pair_ref
  42.8 0.0 collective-permute-done.3.refs_1_
  42.8 2.8 %collective-permute-done.4.refs_2_ = bf16[80,4,128]{2,1,0:T(4,128)(2,1)S(1)} collective-permute-done((bf16[80,4,128]{2,1,0:T(4,128)(2,1)S(1)}, bf16[80,4,128]{2,1,0:T(4,128)(2,1)S(1)}, u32[]{:S(2)}, u32[]{:S(2)}) %collective-permute-start.4) | collective-permute-done | bytes 81952 | tf_op jit(solution)/shard_map/ppermute | solution.py:25
  45.6 1.8 %collective-permute-done.5.refs_3_ = bf16[80,4,128]{2,1,0:T(4,128)(2,1)S(1)} collective-permute-done((bf16[80,4,128]{2,1,0:T(4,128)(2,1)S(1)}, bf16[80,4,128]{2,1,0:T(4,128)(2,1)S(1)}, u32[]{:S(2)}, u32[]{:S(2)}) %collective-permute-start.5) | collective-permute-done | bytes 81952 | tf_op jit(solution)/shard_map/ppermute | solution.py:25
  47.3 0.4 shard_map.66
  47.7 0.2 abs_reduce_fusion.1
  47.9 0.1 multiply_convert_fusion.1
  48.1 2.0 %collective-permute-start.7 = (f16[392,128]{1,0:T(8,128)(2,1)S(1)}, f16[392,128]{1,0:T(8,128)(2,1)S(1)}, u32[]{:S(2)}, u32[]{:S(2)}) collective-permute-start(f16[392,128]{1,0:T(8,128)(2,1)S(1)} %fusion.11), channel_id=1, source_target_pairs={{0,8},{1,9},{2,10},{3,11},{4,12},{5,13},{6,14},{7,15},{8,0},{9,1},... | collective-permute-start | bytes 301064 | tf_op jit(solution)/shard_map/ppermute | solution.py:25
  50.1 2.1 %collective-permute-start.8 = (f16[392,128]{1,0:T(8,128)(2,1)S(1)}, f16[392,128]{1,0:T(8,128)(2,1)S(1)}, u32[]{:S(2)}, u32[]{:S(2)}) collective-permute-start(f16[392,128]{1,0:T(8,128)(2,1)S(1)} %fusion.12), channel_id=1, source_target_pairs={{0,12},{1,13},{2,14},{3,15},{4,8},{5,9},{6,10},{7,11},{8,4},{9,5},... | collective-permute-start | bytes 301064 | tf_op jit(solution)/shard_map/ppermute | solution.py:25
  52.3 0.1 collective-permute-start.6
  52.4 6.7 %collective-permute-done.7 = f16[392,128]{1,0:T(8,128)(2,1)S(1)} collective-permute-done((f16[392,128]{1,0:T(8,128)(2,1)S(1)}, f16[392,128]{1,0:T(8,128)(2,1)S(1)}, u32[]{:S(2)}, u32[]{:S(2)}) %collective-permute-start.7) | collective-permute-done | bytes 100384 | tf_op jit(solution)/shard_map/ppermute | solution.py:25
  59.1 0.7 %collective-permute-done.6 = f16[392,128]{1,0:T(8,128)(2,1)S(1)} collective-permute-done((f16[392,128]{1,0:T(8,128)(2,1)S(1)}, f16[392,128]{1,0:T(8,128)(2,1)S(1)}, u32[]{:S(2)}, u32[]{:S(2)}) %collective-permute-start.6) | collective-permute-done | bytes 100384 | tf_op jit(solution)/shard_map/ppermute | solution.py:25
  59.8 0.1 copy_bitcast_fusion
  59.9 0.0 collective-permute-done.8
  60.0 0.7 %fusion.6 = bf16[96,512]{1,0:T(8,128)(2,1)} fusion(f32[96,512]{1,0:T(8,128)S(1)} %copy_bitcast_fusion, f16[4,96,128]{2,1,0:T(8,128)(2,1)S(1)} %bitcast.59, f32[96]{0:T(128)S(1)} %fusion.16), kind=kLoop, calls=%fused_computation.15 | loop fusion | flops 196608 | bytes 393600 | tf_op jit(solution)/shard_map/convert_element_type | solution.py:350
  (13 shorter events, 0.2 us)
Async XLA Ops:
  2.5 34.0 %all-to-all-start = ((bf16[80,4,1792]{2,1,0:T(4,128)(2,1)}), bf16[80,4,1792]{2,1,0:T(4,128)(2,1)S(1)}, u32[]{:S(2)}, u32[]{:S(2)}) async-start(bf16[80,4,1792]{2,1,0:T(4,128)(2,1)} %get-tuple-element.45), calls=%async_computation | async-start | bytes 2293760 | tf_op jit(solution)/shard_map/all_to_all | solution.py:339
  14.2 4.7 %collective-permute-start.1 = (f32[16,96,128]{2,1,0:T(8,128)S(1)}, f32[16,96,128]{2,1,0:T(8,128)S(1)}, u32[]{:S(2)}, u32[]{:S(2)}) collective-permute-start(f32[16,96,128]{2,1,0:T(8,128)S(1)} %branch_1_fun.4), channel_id=1, source_target_pairs={{0,1},{1,0},{2,3},{3,2},{4,5},{5,4},{6,7},{7,6},{8,9},{9,8},{10,11... | collective-permute-start | bytes 2359304 | tf_op jit(solution)/shard_map/cond/branch_1_fun/ppermute | solution.py:25
  19.4 16.0 %collective-permute-start.2 = (f16[1544,128]{1,0:T(8,128)(2,1)S(1)}, f16[1544,128]{1,0:T(8,128)(2,1)S(1)}, u32[]{:S(2)}, u32[]{:S(2)}) collective-permute-start(f16[1544,128]{1,0:T(8,128)(2,1)S(1)} %get-tuple-element.71), channel_id=1, source_target_pairs={{0,2},{1,3},{2,0},{3,1},{4,6},{5,7},{6,4},{7,5},{8,10},{9,11},{10,... | collective-permute-start | bytes 1185800 | tf_op jit(solution)/shard_map/ppermute | solution.py:25
  28.8 2.4 %collective-permute-start = (f32[16,96,128]{2,1,0:T(8,128)S(1)}, f32[16,96,128]{2,1,0:T(8,128)S(1)}, u32[]{:S(2)}, u32[]{:S(2)}) collective-permute-start(f32[16,96,128]{2,1,0:T(8,128)S(1)} %get-tuple-element.30), channel_id=1, source_target_pairs={{0,1},{1,0},{2,3},{3,2},{4,5},{5,4},{6,7},{7,6},{8,9},{9,8},{10,11... | collective-permute-start | bytes 2359304 | tf_op jit(solution)/shard_map/cond/branch_1_fun/ppermute | solution.py:25
  40.3 2.5 %collective-permute-start.3 = (bf16[80,4,128]{2,1,0:T(4,128)(2,1)S(1)}, bf16[80,4,128]{2,1,0:T(4,128)(2,1)S(1)}, u32[]{:S(2)}, u32[]{:S(2)}) collective-permute-start(bf16[80,4,128]{2,1,0:T(4,128)(2,1)S(1)} %get-tuple-element.48), channel_id=1, source_target_pairs={{0,1},{1,0},{2,3},{3,2},{4,5},{5,4},{6,7},{7,6},{8,9},{9,8},{10,11... | collective-permute-start | bytes 245768 | tf_op jit(solution)/shard_map/ppermute | solution.py:25
  41.1 4.4 %collective-permute-start.4 = (bf16[80,4,128]{2,1,0:T(4,128)(2,1)S(1)}, bf16[80,4,128]{2,1,0:T(4,128)(2,1)S(1)}, u32[]{:S(2)}, u32[]{:S(2)}) collective-permute-start(bf16[80,4,128]{2,1,0:T(4,128)(2,1)S(1)} %get-tuple-element.49), channel_id=1, source_target_pairs={{0,2},{1,3},{2,0},{3,1},{4,6},{5,7},{6,4},{7,5},{8,10},{9,11},{10,... | collective-permute-start | bytes 245768 | tf_op jit(solution)/shard_map/ppermute | solution.py:25
  42.6 4.7 %collective-permute-start.5 = (bf16[80,4,128]{2,1,0:T(4,128)(2,1)S(1)}, bf16[80,4,128]{2,1,0:T(4,128)(2,1)S(1)}, u32[]{:S(2)}, u32[]{:S(2)}) collective-permute-start(bf16[80,4,128]{2,1,0:T(4,128)(2,1)S(1)} %get-tuple-element.50), channel_id=1, source_target_pairs={{0,3},{1,2},{2,1},{3,0},{4,7},{5,6},{6,5},{7,4},{8,11},{9,10},{10,... | collective-permute-start | bytes 245768 | tf_op jit(solution)/shard_map/ppermute | solution.py:25
  48.1 11.0 %collective-permute-start.7 = (f16[392,128]{1,0:T(8,128)(2,1)S(1)}, f16[392,128]{1,0:T(8,128)(2,1)S(1)}, u32[]{:S(2)}, u32[]{:S(2)}) collective-permute-start(f16[392,128]{1,0:T(8,128)(2,1)S(1)} %fusion.11), channel_id=1, source_target_pairs={{0,8},{1,9},{2,10},{3,11},{4,12},{5,13},{6,14},{7,15},{8,0},{9,1},... | collective-permute-start | bytes 301064 | tf_op jit(solution)/shard_map/ppermute | solution.py:25
  50.1 9.8 %collective-permute-start.8 = (f16[392,128]{1,0:T(8,128)(2,1)S(1)}, f16[392,128]{1,0:T(8,128)(2,1)S(1)}, u32[]{:S(2)}, u32[]{:S(2)}) collective-permute-start(f16[392,128]{1,0:T(8,128)(2,1)S(1)} %fusion.12), channel_id=1, source_target_pairs={{0,12},{1,13},{2,14},{3,15},{4,8},{5,9},{6,10},{7,11},{8,4},{9,5},... | collective-permute-start | bytes 301064 | tf_op jit(solution)/shard_map/ppermute | solution.py:25
  52.3 7.5 %collective-permute-start.6 = (f16[392,128]{1,0:T(8,128)(2,1)S(1)}, f16[392,128]{1,0:T(8,128)(2,1)S(1)}, u32[]{:S(2)}, u32[]{:S(2)}) collective-permute-start(f16[392,128]{1,0:T(8,128)(2,1)S(1)} %fusion.10), channel_id=1, source_target_pairs={{0,4},{1,5},{2,6},{3,7},{4,0},{5,1},{6,2},{7,3},{8,12},{9,13},{10,... | collective-permute-start | bytes 301064 | tf_op jit(solution)/shard_map/ppermute | solution.py:25

commit v28 on v26

--- a/solution.py
+++ b/solution.py
@@ -107,7 +107,6 @@
         return jnp.zeros((half * rows + MARK_ROWS, LANES), jnp.float16)
 
     sent = lax.cond(order[0] >= 0, first, first_idle)
-    pair_in = xor_permute(sent, group, 2)
     order, _ = lax.optimization_barrier((order, sent))
 
     def second():
@@ -118,6 +117,8 @@
         return jnp.zeros((half, rows, LANES), jnp.float32)
 
     kept = lax.cond(order[1] >= 0, second, second_idle)
+    sent, _ = lax.optimization_barrier((sent, kept))
+    pair_in = xor_permute(sent, group, 2)
     return kept, pair_in
 
 

time: 60.6 us -> 66.2 us (1.092)
  waiting for transfers between devices: 18.6 us -> 24.5 us
    ppermute x9, waiting for transfers between devices: 17.6 us -> 24.5 us  [xor_permute(): return lax.ppermute(value, 'tp', [(i, i ^ offset) for i in range(group)])]
    all_to_all x1, waiting for transfers between devices: 0.98 us -> 0.01 us  [shards_by_blocks(): lax.all_to_all(packed, 'tp', split_axis=0, concat_axis=0, axis_index_grou...]
  transfers between devices with their start and end apart: 10 -> 10, of which waited for: 7 -> 6; matrix products, arithmetic and copies ran while one was open for 3% -> 3% of each run, Pallas kernels for 24% -> 22%
where the time goes in v28:
time: 66.2 us; the launch traced here: 66 us
  waiting for transfers between devices  24.5 us (37%)
  Pallas kernels  21.5 us (32%)
  starting transfers between devices  16.3 us (25%)
  other arithmetic  1.93 us (3%)
  local copies, waits for them, and re-layouts  0.9 us (1%)
  between operations  0.82 us (1%)
    ppermute x9, waiting for transfers between devices, xor_permute(): return lax.ppermute(value, 'tp', [(i, i ^ offset) for i in range(group)])  24.5 us
    pallas_call x3, Pallas kernels, column_blocks(): pl.pallas_call(functools.partial(column_blocks_kernel, groups), out_shape...  14.8 us
    ppermute x9, starting transfers between devices, xor_permute(): return lax.ppermute(value, 'tp', [(i, i ^ offset) for i in range(group)])  8.91 us
    all_to_all x1, starting transfers between devices, shards_by_blocks(): lax.all_to_all(packed, 'tp', split_axis=0, concat_axis=0, axis_index_grou...  7.37 us
    pallas_call x1, Pallas kernels, adapter_output(): pl.pallas_call(functools.partial(adapter_kernel, parts, ranks), out_shape...  3.79 us
    pallas_call x1, Pallas kernels, pack_rows(): pl.pallas_call(functools.partial(pack_kernel, blocks, orders), out_shape=...  2.49 us
  transfers between devices with their start and end apart: 10, of which 6 were waited for; matrix products, arithmetic and copies ran while one was open for 3% of the time, Pallas kernels for 22%

profile of v28, /device:TPU:0, one launch (start us, length us, event | category | flops | bytes accessed | tf_op | source)
XLA Modules:
  0.0 66.0 jit_solution(18135919095644142916)
XLA Ops:
  0.0 2.5 %shard_map.64 = (bf16[80,4,1792]{2,1,0:T(4,128)(2,1)}, bf16[128,96]{1,0:T(8,128)(2,1)S(1)}, s32[16]{0:T(128)S(1)}, bf16[96,1792]{1,0:T(8,128)(2,1)S(1)}) custom-call(s32[1]{0:T(128)} %bitcast.2.me_ref, s32[16]{0:T(128)} %slot_hbm.1, s32[1,96]{1,0:T(1,128)} %bitcast.56, bf16[96,1792]{1,0:T(8,128)(2,1)} %hidden_hbm.1), custom_call_target="tpu_custom_call" | custom-call | tf_op jit(solution)/shard_map/pallas_call | solution.py:198
  2.5 7.4 %all-to-all-start = ((bf16[80,4,1792]{2,1,0:T(4,128)(2,1)}), bf16[80,4,1792]{2,1,0:T(4,128)(2,1)S(1)}, u32[]{:S(2)}, u32[]{:S(2)}) async-start(bf16[80,4,1792]{2,1,0:T(4,128)(2,1)} %get-tuple-element.47), calls=%async_computation | async-start | bytes 2293760 | tf_op jit(solution)/shard_map/all_to_all | solution.py:335
  9.9 9.4 %conditional.2 = (f16[1552,128]{1,0:T(8,128)(2,1)S(1)}) conditional(s32[]{:T(128)} %bitcast.4, () %tuple.20, (s32[16]{0:T(128)S(1)}, bf16[96,1792]{1,0:T(8,128)(2,1)S(1)}, bf16[1792,8192]{1,0:T(8,128)(2,1)}) %tuple.21), branch_computations={%region_0.0_spmd, %region_1.3_spmd} | conditional | flops 1581488 | bytes 7479232 | solution.py:109
  9.9 0.1 fusion.29
  10.0 4.2 %branch_1_fun.4 = f32[16,96,128]{2,1,0:T(8,128)S(1)} custom-call(s32[4]{0:T(128)S(1)} %get-tuple-element.60.order_ref, bf16[96,1792]{1,0:T(8,128)(2,1)S(1)} %get-tuple-element.24.hidden_ref, bf16[1792,8192]{1,0:T(8,128)(2,1)} %get-tuple-element.25.down_ref), custom_call_target="tpu_custom_call" | custom-call | flops 1000 | bytes 1000 | tf_op jit(solution)/shard_map/cond/branch_1_fun/pallas_call | solution.py:62
  14.2 0.5 collective-permute-start.1
  14.7 4.2 %branch_1_fun.3 = f32[16,96,128]{2,1,0:T(8,128)S(1)} custom-call(s32[4]{0:T(128)S(1)} %get-tuple-element.61.order_ref, bf16[96,1792]{1,0:T(8,128)(2,1)S(1)} %get-tuple-element.24.hidden_ref, bf16[1792,8192]{1,0:T(8,128)(2,1)} %get-tuple-element.25.down_ref), custom_call_target="tpu_custom_call" | custom-call | flops 1000 | bytes 1000 | tf_op jit(solution)/shard_map/cond/branch_1_fun/pallas_call | solution.py:62
  18.9 0.0 collective-permute-done.1
  18.9 0.2 abs_reduce_fusion
  19.1 0.2 multiply_convert_fusion
  19.3 0.1 fusion.1
  19.4 0.6 slice.52
  20.6 8.9 %conditional.3 = (f32[16,96,128]{2,1,0:T(8,128)S(1)}) conditional(s32[]{:T(128)} %bitcast.5, () %tuple.23, (s32[16]{0:T(128)S(1)}, bf16[96,1792]{1,0:T(8,128)(2,1)S(1)}, bf16[1792,8192]{1,0:T(8,128)(2,1)}) %tuple.24), branch_computations={%region_3.4_spmd, %region_4.5_spmd} | conditional | flops 197608 | bytes 5506136 | solution.py:119
  20.6 0.1 slice.36.order_ref
  20.7 6.4 %branch_1_fun.5 = (f32[16,96,128]{2,1,0:T(8,128)S(1)}, f32[16,96,128]{2,1,0:T(8,128)S(1)}) custom-call(s32[8]{0:T(128)S(1)} %slice.36.order_ref, bf16[96,1792]{1,0:T(8,128)(2,1)S(1)} %get-tuple-element.27.hidden_ref, bf16[1792,8192]{1,0:T(8,128)(2,1)} %get-tuple-element.28.down_ref), custom_call_target="tpu_custom_call" | custom-call | flops 1000 | bytes 1000 | tf_op jit(solution)/shard_map/cond/branch_1_fun/pallas_call | solution.py:62
  27.1 0.2 collective-permute-start
  27.3 2.2 %collective-permute-done = f32[16,96,128]{2,1,0:T(8,128)S(1)} collective-permute-done((f32[16,96,128]{2,1,0:T(8,128)S(1)}, f32[16,96,128]{2,1,0:T(8,128)S(1)}, u32[]{:S(2)}, u32[]{:S(2)}) %collective-permute-start) | collective-permute-done | bytes 786464 | tf_op jit(solution)/shard_map/cond/branch_1_fun/ppermute | solution.py:25
  29.5 0.1 add.39
  29.6 1.7 %collective-permute-start.2 = (f16[1552,128]{1,0:T(8,128)(2,1)S(1)}, f16[1552,128]{1,0:T(8,128)(2,1)S(1)}, u32[]{:S(2)}, u32[]{:S(2)}) collective-permute-start(f16[1552,128]{1,0:T(8,128)(2,1)S(1)} %get-tuple-element.73), channel_id=1, source_target_pairs={{0,2},{1,3},{2,0},{3,1},{4,6},{5,7},{6,4},{7,5},{8,10},{9,11},{10,... | collective-permute-start | bytes 1191944 | tf_op jit(solution)/shard_map/ppermute | solution.py:25
  31.3 12.0 %collective-permute-done.2 = f16[1552,128]{1,0:T(8,128)(2,1)S(1)} collective-permute-done((f16[1552,128]{1,0:T(8,128)(2,1)S(1)}, f16[1552,128]{1,0:T(8,128)(2,1)S(1)}, u32[]{:S(2)}, u32[]{:S(2)}) %collective-permute-start.2) | collective-permute-done | bytes 397344 | tf_op jit(solution)/shard_map/ppermute | solution.py:25
  43.3 0.1 slice.65
  43.4 0.0 all-to-all-done.rows_ref
  43.4 3.8 %shard_map.65 = (bf16[80,4,128]{2,1,0:T(4,128)(2,1)S(1)}, bf16[80,4,128]{2,1,0:T(4,128)(2,1)S(1)}, bf16[80,4,128]{2,1,0:T(4,128)(2,1)S(1)}, bf16[80,4,128]{2,1,0:T(4,128)(2,1)S(1)}) custom-call(s32[1]{0:T(128)} %bitcast.2.me_ref, bf16[80,4,1792]{2,1,0:T(4,128)(2,1)S(1)} %all-to-all-done.rows_ref, bf16[64,8192]{1,0:T(8,128)(2,1)} %bitcast.48, ...), custom_call_target="tpu_custom_call" | custom-call | tf_op jit(solution)/shard_map/pallas_call | solution.py:273
  47.2 0.1 collective-permute-start.3
  47.4 0.6 collective-permute-start.4
  48.0 1.2 %collective-permute-start.5 = (bf16[80,4,128]{2,1,0:T(4,128)(2,1)S(1)}, bf16[80,4,128]{2,1,0:T(4,128)(2,1)S(1)}, u32[]{:S(2)}, u32[]{:S(2)}) collective-permute-start(bf16[80,4,128]{2,1,0:T(4,128)(2,1)S(1)} %get-tuple-element.52), channel_id=1, source_target_pairs={{0,3},{1,2},{2,1},{3,0},{4,7},{5,6},{6,5},{7,4},{8,11},{9,10},{10,... | collective-permute-start | bytes 245768 | tf_op jit(solution)/shard_map/ppermute | solution.py:25
  49.2 0.2 fusion.2.pair_ref
  49.4 0.0 collective-permute-done.3.refs_1_
  49.4 3.3 %collective-permute-done.4.refs_2_ = bf16[80,4,128]{2,1,0:T(4,128)(2,1)S(1)} collective-permute-done((bf16[80,4,128]{2,1,0:T(4,128)(2,1)S(1)}, bf16[80,4,128]{2,1,0:T(4,128)(2,1)S(1)}, u32[]{:S(2)}, u32[]{:S(2)}) %collective-permute-start.4) | collective-permute-done | bytes 81952 | tf_op jit(solution)/shard_map/ppermute | solution.py:25
  52.6 0.8 %collective-permute-done.5.refs_3_ = bf16[80,4,128]{2,1,0:T(4,128)(2,1)S(1)} collective-permute-done((bf16[80,4,128]{2,1,0:T(4,128)(2,1)S(1)}, bf16[80,4,128]{2,1,0:T(4,128)(2,1)S(1)}, u32[]{:S(2)}, u32[]{:S(2)}) %collective-permute-start.5) | collective-permute-done | bytes 81952 | tf_op jit(solution)/shard_map/ppermute | solution.py:25
  53.5 0.4 shard_map.66
  53.9 0.2 abs_reduce_fusion.3
  54.1 0.1 multiply_convert_fusion.3
  54.3 1.9 %collective-permute-start.7 = (f16[400,128]{1,0:T(8,128)(2,1)S(1)}, f16[400,128]{1,0:T(8,128)(2,1)S(1)}, u32[]{:S(2)}, u32[]{:S(2)}) collective-permute-start(f16[400,128]{1,0:T(8,128)(2,1)S(1)} %fusion.10), channel_id=1, source_target_pairs={{0,8},{1,9},{2,10},{3,11},{4,12},{5,13},{6,14},{7,15},{8,0},{9,1},... | collective-permute-start | bytes 307208 | tf_op jit(solution)/shard_map/ppermute | solution.py:25
  56.2 1.6 %collective-permute-start.6 = (f16[400,128]{1,0:T(8,128)(2,1)S(1)}, f16[400,128]{1,0:T(8,128)(2,1)S(1)}, u32[]{:S(2)}, u32[]{:S(2)}) collective-permute-start(f16[400,128]{1,0:T(8,128)(2,1)S(1)} %fusion.9), channel_id=1, source_target_pairs={{0,4},{1,5},{2,6},{3,7},{4,0},{5,1},{6,2},{7,3},{8,12},{9,13},{10,... | collective-permute-start | bytes 307208 | tf_op jit(solution)/shard_map/ppermute | solution.py:25
  57.9 1.0 %collective-permute-start.8 = (f16[400,128]{1,0:T(8,128)(2,1)S(1)}, f16[400,128]{1,0:T(8,128)(2,1)S(1)}, u32[]{:S(2)}, u32[]{:S(2)}) collective-permute-start(f16[400,128]{1,0:T(8,128)(2,1)S(1)} %fusion.11), channel_id=1, source_target_pairs={{0,12},{1,13},{2,14},{3,15},{4,8},{5,9},{6,10},{7,11},{8,4},{9,5},... | collective-permute-start | bytes 307208 | tf_op jit(solution)/shard_map/ppermute | solution.py:25
  58.9 4.7 %collective-permute-done.7 = f16[400,128]{1,0:T(8,128)(2,1)S(1)} collective-permute-done((f16[400,128]{1,0:T(8,128)(2,1)S(1)}, f16[400,128]{1,0:T(8,128)(2,1)S(1)}, u32[]{:S(2)}, u32[]{:S(2)}) %collective-permute-start.7) | collective-permute-done | bytes 102432 | tf_op jit(solution)/shard_map/ppermute | solution.py:25
  63.6 0.0 collective-permute-done.6
  63.6 1.5 %collective-permute-done.8 = f16[400,128]{1,0:T(8,128)(2,1)S(1)} collective-permute-done((f16[400,128]{1,0:T(8,128)(2,1)S(1)}, f16[400,128]{1,0:T(8,128)(2,1)S(1)}, u32[]{:S(2)}, u32[]{:S(2)}) %collective-permute-start.8) | collective-permute-done | bytes 102432 | tf_op jit(solution)/shard_map/ppermute | solution.py:25
  65.2 0.8 %copy_bitcast_fusion = bf16[96,512]{1,0:T(8,128)(2,1)} fusion(f16[4,96,128]{2,1,0:T(8,128)(2,1)S(1)} %bitcast.54, f16[4,96,128]{2,1,0:T(8,128)(2,1)S(1)} %bitcast.51, f16[4,96,128]{2,1,0:T(8,128)(2,1)S(1)} %bitcast.52, f32[16,96,128]{2,1,0:T(8,128)S(1)} %shard_map.66, f32[96]{0:T(128)S(1)} %fusion.16, f32[96]{0:T(128)S(1)} %fusion.20, f32[96]{0:T(128)S(1)} %fusion.24), kind=kLoop, calls=%fused_computation.31 | loop fusion | flops 491520 | bytes 591360 | tf_op jit(solution)/shard_map/convert_element_type | solution.py:346
  (13 shorter events, 0.2 us)
Async XLA Ops:
  2.5 40.9 %all-to-all-start = ((bf16[80,4,1792]{2,1,0:T(4,128)(2,1)}), bf16[80,4,1792]{2,1,0:T(4,128)(2,1)S(1)}, u32[]{:S(2)}, u32[]{:S(2)}) async-start(bf16[80,4,1792]{2,1,0:T(4,128)(2,1)} %get-tuple-element.47), calls=%async_computation | async-start | bytes 2293760 | tf_op jit(solution)/shard_map/all_to_all | solution.py:335
  14.2 4.7 %collective-permute-start.1 = (f32[16,96,128]{2,1,0:T(8,128)S(1)}, f32[16,96,128]{2,1,0:T(8,128)S(1)}, u32[]{:S(2)}, u32[]{:S(2)}) collective-permute-start(f32[16,96,128]{2,1,0:T(8,128)S(1)} %branch_1_fun.4), channel_id=1, source_target_pairs={{0,1},{1,0},{2,3},{3,2},{4,5},{5,4},{6,7},{7,6},{8,9},{9,8},{10,11... | collective-permute-start | bytes 2359304 | tf_op jit(solution)/shard_map/cond/branch_1_fun/ppermute | solution.py:25
  27.1 2.4 %collective-permute-start = (f32[16,96,128]{2,1,0:T(8,128)S(1)}, f32[16,96,128]{2,1,0:T(8,128)S(1)}, u32[]{:S(2)}, u32[]{:S(2)}) collective-permute-start(f32[16,96,128]{2,1,0:T(8,128)S(1)} %get-tuple-element.30), channel_id=1, source_target_pairs={{0,1},{1,0},{2,3},{3,2},{4,5},{5,4},{6,7},{7,6},{8,9},{9,8},{10,11... | collective-permute-start | bytes 2359304 | tf_op jit(solution)/shard_map/cond/branch_1_fun/ppermute | solution.py:25
  29.6 13.8 %collective-permute-start.2 = (f16[1552,128]{1,0:T(8,128)(2,1)S(1)}, f16[1552,128]{1,0:T(8,128)(2,1)S(1)}, u32[]{:S(2)}, u32[]{:S(2)}) collective-permute-start(f16[1552,128]{1,0:T(8,128)(2,1)S(1)} %get-tuple-element.73), channel_id=1, source_target_pairs={{0,2},{1,3},{2,0},{3,1},{4,6},{5,7},{6,4},{7,5},{8,10},{9,11},{10,... | collective-permute-start | bytes 1191944 | tf_op jit(solution)/shard_map/ppermute | solution.py:25
  47.2 2.1 %collective-permute-start.3 = (bf16[80,4,128]{2,1,0:T(4,128)(2,1)S(1)}, bf16[80,4,128]{2,1,0:T(4,128)(2,1)S(1)}, u32[]{:S(2)}, u32[]{:S(2)}) collective-permute-start(bf16[80,4,128]{2,1,0:T(4,128)(2,1)S(1)} %get-tuple-element.50), channel_id=1, source_target_pairs={{0,1},{1,0},{2,3},{3,2},{4,5},{5,4},{6,7},{7,6},{8,9},{9,8},{10,11... | collective-permute-start | bytes 245768 | tf_op jit(solution)/shard_map/ppermute | solution.py:25
  47.4 5.3 %collective-permute-start.4 = (bf16[80,4,128]{2,1,0:T(4,128)(2,1)S(1)}, bf16[80,4,128]{2,1,0:T(4,128)(2,1)S(1)}, u32[]{:S(2)}, u32[]{:S(2)}) collective-permute-start(bf16[80,4,128]{2,1,0:T(4,128)(2,1)S(1)} %get-tuple-element.51), channel_id=1, source_target_pairs={{0,2},{1,3},{2,0},{3,1},{4,6},{5,7},{6,4},{7,5},{8,10},{9,11},{10,... | collective-permute-start | bytes 245768 | tf_op jit(solution)/shard_map/ppermute | solution.py:25
  48.0 5.5 %collective-permute-start.5 = (bf16[80,4,128]{2,1,0:T(4,128)(2,1)S(1)}, bf16[80,4,128]{2,1,0:T(4,128)(2,1)S(1)}, u32[]{:S(2)}, u32[]{:S(2)}) collective-permute-start(bf16[80,4,128]{2,1,0:T(4,128)(2,1)S(1)} %get-tuple-element.52), channel_id=1, source_target_pairs={{0,3},{1,2},{2,1},{3,0},{4,7},{5,6},{6,5},{7,4},{8,11},{9,10},{10,... | collective-permute-start | bytes 245768 | tf_op jit(solution)/shard_map/ppermute | solution.py:25
  54.3 9.3 %collective-permute-start.7 = (f16[400,128]{1,0:T(8,128)(2,1)S(1)}, f16[400,128]{1,0:T(8,128)(2,1)S(1)}, u32[]{:S(2)}, u32[]{:S(2)}) collective-permute-start(f16[400,128]{1,0:T(8,128)(2,1)S(1)} %fusion.10), channel_id=1, source_target_pairs={{0,8},{1,9},{2,10},{3,11},{4,12},{5,13},{6,14},{7,15},{8,0},{9,1},... | collective-permute-start | bytes 307208 | tf_op jit(solution)/shard_map/ppermute | solution.py:25
  56.2 7.3 %collective-permute-start.6 = (f16[400,128]{1,0:T(8,128)(2,1)S(1)}, f16[400,128]{1,0:T(8,128)(2,1)S(1)}, u32[]{:S(2)}, u32[]{:S(2)}) collective-permute-start(f16[400,128]{1,0:T(8,128)(2,1)S(1)} %fusion.9), channel_id=1, source_target_pairs={{0,4},{1,5},{2,6},{3,7},{4,0},{5,1},{6,2},{7,3},{8,12},{9,13},{10,... | collective-permute-start | bytes 307208 | tf_op jit(solution)/shard_map/ppermute | solution.py:25
  57.9 7.3 %collective-permute-start.8 = (f16[400,128]{1,0:T(8,128)(2,1)S(1)}, f16[400,128]{1,0:T(8,128)(2,1)S(1)}, u32[]{:S(2)}, u32[]{:S(2)}) collective-permute-start(f16[400,128]{1,0:T(8,128)(2,1)S(1)} %fusion.11), channel_id=1, source_target_pairs={{0,12},{1,13},{2,14},{3,15},{4,8},{5,9},{6,10},{7,11},{8,4},{9,5},... | collective-permute-start | bytes 307208 | tf_op jit(solution)/shard_map/ppermute | solution.py:25

commit v29 on v26

--- a/solution.py
+++ b/solution.py
@@ -218,32 +218,34 @@
     out_refs = refs[:PLANE]
     shrink_ref, expand_ref, own_ref, sems, expand_sem = refs[PLANE:]
     me = me_ref[0]
-    group, _, depth = shrink_ref.shape
+    chips = shrink_ref.shape[0]
+    group, depth = 2 * chips, shrink_ref.shape[2] // 2
     blocks = MOST // BLOCK
 
-    def copy(source):
+    def copy(pair):
         return pltpu.make_async_copy(
-            shrink_hbm.at[:, pl.ds(ranks[source] * depth, depth)],
-            shrink_ref.at[source],
-            sems.at[source],
+            shrink_hbm.at[:, pl.ds(ranks[2 * pair] * depth, 2 * depth)],
+            shrink_ref.at[pair],
+            sems.at[pair],
         )
 
-    for source in range(group // 2):
-        copy(source).start()
+    for pair in range(chips // 2):
+        copy(pair).start()
     for source in range(group):
         own = rows_ref[source * blocks : (source + 1) * blocks]
-        own_ref[source, :MOST] = own.reshape(MOST, depth)
+        first = source % 2 * depth
+        own_ref[source // 2, :MOST, first : first + depth] = own.reshape(MOST, depth)
         if source == group // 2 - 1:
-            for later in range(group // 2, group):
+            for later in range(chips // 2, chips):
                 copy(later).start()
             expand_copy = pltpu.make_async_copy(expand_hbm, expand_ref, expand_sem)
             expand_copy.start()
     total = jnp.zeros((MOST, shrink_ref.shape[1]), jnp.float32)
-    for source in range(group):
-        copy(source).wait()
+    for pair in range(chips):
+        copy(pair).wait()
         total += lax.dot_general(
-            own_ref[source, :MOST],
-            shrink_ref[source],
+            own_ref[pair, :MOST],
+            shrink_ref[pair],
             (((1,), (1,)), ((), ())),
             preferred_element_type=jnp.float32,
         )
@@ -280,10 +282,10 @@
         ],
         out_specs=[vmem] * PLANE,
         scratch_shapes=[
-            pltpu.VMEM((group, rank, depth), jnp.bfloat16),
+            pltpu.VMEM((group // 2, rank, 2 * depth), jnp.bfloat16),
             pltpu.VMEM((rank, model_width), jnp.bfloat16),
-            pltpu.VMEM((group, HELD, depth), jnp.bfloat16),
-            pltpu.SemaphoreType.DMA((group,)),
+            pltpu.VMEM((group // 2, HELD, 2 * depth), jnp.bfloat16),
+            pltpu.SemaphoreType.DMA((group // 2,)),
             pltpu.SemaphoreType.DMA,
         ],
         compiler_params=pltpu.CompilerParams(vmem_limit_bytes=24 * 2**20),

time: 60.6 us -> 60.5 us (level)
  transfers between devices with their start and end apart: 10 -> 10, of which waited for: 7 -> 7; matrix products, arithmetic and copies ran while one was open for 3% -> 3% of each run, Pallas kernels for 24% -> 25%
where the time goes in v29:
time: 60.5 us; the launch traced here: 60.3 us
  Pallas kernels  21.3 us (35%)
  waiting for transfers between devices  18.6 us (31%)
  starting transfers between devices  16.6 us (27%)
  other arithmetic  1.93 us (3%)
  local copies, waits for them, and re-layouts  0.9 us (1%)
  between operations  0.81 us (1%)
    ppermute x9, waiting for transfers between devices, xor_permute(): return lax.ppermute(value, 'tp', [(i, i ^ offset) for i in range(group)])  17.6 us
    pallas_call x3, Pallas kernels, column_blocks(): pl.pallas_call(functools.partial(column_blocks_kernel, groups), out_shape...  14.8 us
    ppermute x9, starting transfers between devices, xor_permute(): return lax.ppermute(value, 'tp', [(i, i ^ offset) for i in range(group)])  9.25 us
    all_to_all x1, starting transfers between devices, shards_by_blocks(): lax.all_to_all(packed, 'tp', split_axis=0, concat_axis=0, axis_index_grou...  7.37 us
    pallas_call x1, Pallas kernels, adapter_output(): pl.pallas_call(functools.partial(adapter_kernel, parts, ranks), out_shape...  3.66 us
    pallas_call x1, Pallas kernels, pack_rows(): pl.pallas_call(functools.partial(pack_kernel, blocks, orders), out_shape=...  2.49 us
  transfers between devices with their start and end apart: 10, of which 7 were waited for; matrix products, arithmetic and copies ran while one was open for 3% of the time, Pallas kernels for 25%

profile of v29, /device:TPU:0, one launch (start us, length us, event | category | flops | bytes accessed | tf_op | source)
XLA Modules:
  0.0 60.3 jit_solution(13858876604895289759)
XLA Ops:
  0.0 2.5 %shard_map.64 = (bf16[80,4,1792]{2,1,0:T(4,128)(2,1)}, bf16[128,96]{1,0:T(8,128)(2,1)S(1)}, s32[16]{0:T(128)S(1)}, bf16[96,1792]{1,0:T(8,128)(2,1)S(1)}) custom-call(s32[1]{0:T(128)} %bitcast.2.me_ref, s32[16]{0:T(128)} %slot_hbm.1, s32[1,96]{1,0:T(1,128)} %bitcast.56, bf16[96,1792]{1,0:T(8,128)(2,1)} %hidden_hbm.1), custom_call_target="tpu_custom_call" | custom-call | tf_op jit(solution)/shard_map/pallas_call | solution.py:197
  2.5 7.4 %all-to-all-start = ((bf16[80,4,1792]{2,1,0:T(4,128)(2,1)}), bf16[80,4,1792]{2,1,0:T(4,128)(2,1)S(1)}, u32[]{:S(2)}, u32[]{:S(2)}) async-start(bf16[80,4,1792]{2,1,0:T(4,128)(2,1)} %get-tuple-element.45), calls=%async_computation | async-start | bytes 2293760 | tf_op jit(solution)/shard_map/all_to_all | solution.py:336
  9.9 9.4 %conditional.2 = (f16[1552,128]{1,0:T(8,128)(2,1)S(1)}) conditional(s32[]{:T(128)} %bitcast.4, () %tuple.19, (s32[16]{0:T(128)S(1)}, bf16[96,1792]{1,0:T(8,128)(2,1)S(1)}, bf16[1792,8192]{1,0:T(8,128)(2,1)}) %tuple.20), branch_computations={%region_0.0_spmd, %region_1.3_spmd} | conditional | flops 1581488 | bytes 7479232 | solution.py:109
  9.9 0.1 fusion.29
  10.0 4.2 %branch_1_fun.4 = f32[16,96,128]{2,1,0:T(8,128)S(1)} custom-call(s32[4]{0:T(128)S(1)} %get-tuple-element.58.order_ref, bf16[96,1792]{1,0:T(8,128)(2,1)S(1)} %get-tuple-element.24.hidden_ref, bf16[1792,8192]{1,0:T(8,128)(2,1)} %get-tuple-element.25.down_ref), custom_call_target="tpu_custom_call" | custom-call | flops 1000 | bytes 1000 | tf_op jit(solution)/shard_map/cond/branch_1_fun/pallas_call | solution.py:62
  14.2 0.5 collective-permute-start.1
  14.7 4.2 %branch_1_fun.3 = f32[16,96,128]{2,1,0:T(8,128)S(1)} custom-call(s32[4]{0:T(128)S(1)} %get-tuple-element.59.order_ref, bf16[96,1792]{1,0:T(8,128)(2,1)S(1)} %get-tuple-element.24.hidden_ref, bf16[1792,8192]{1,0:T(8,128)(2,1)} %get-tuple-element.25.down_ref), custom_call_target="tpu_custom_call" | custom-call | flops 1000 | bytes 1000 | tf_op jit(solution)/shard_map/cond/branch_1_fun/pallas_call | solution.py:62
  18.9 0.0 collective-permute-done.1
  18.9 0.2 abs_reduce_fusion
  19.1 0.2 multiply_convert_fusion
  19.3 0.1 fusion.1
  19.4 1.7 %collective-permute-start.2 = (f16[1552,128]{1,0:T(8,128)(2,1)S(1)}, f16[1552,128]{1,0:T(8,128)(2,1)S(1)}, u32[]{:S(2)}, u32[]{:S(2)}) collective-permute-start(f16[1552,128]{1,0:T(8,128)(2,1)S(1)} %get-tuple-element.71), channel_id=1, source_target_pairs={{0,2},{1,3},{2,0},{3,1},{4,6},{5,7},{6,4},{7,5},{8,10},{9,11},{10,... | collective-permute-start | bytes 1191944 | tf_op jit(solution)/shard_map/ppermute | solution.py:25
  21.1 0.6 %slice.52 = s32[1]{0:T(128)} slice(s32[16]{0:T(128)S(1)} %get-tuple-element.43), slice={[1:2]} | slice | bytes 8 | tf_op jit(solution)/shard_map/slice | solution.py:120
  22.4 9.0 %conditional.3 = (f32[16,96,128]{2,1,0:T(8,128)S(1)}) conditional(s32[]{:T(128)} %bitcast.5, () %tuple.22, (s32[16]{0:T(128)S(1)}, bf16[96,1792]{1,0:T(8,128)(2,1)S(1)}, bf16[1792,8192]{1,0:T(8,128)(2,1)}) %tuple.23), branch_computations={%region_3.4_spmd, %region_4.5_spmd} | conditional | flops 197608 | bytes 5506136 | solution.py:120
  22.4 0.1 slice.36.order_ref
  22.4 6.4 %branch_1_fun.5 = (f32[16,96,128]{2,1,0:T(8,128)S(1)}, f32[16,96,128]{2,1,0:T(8,128)S(1)}) custom-call(s32[8]{0:T(128)S(1)} %slice.36.order_ref, bf16[96,1792]{1,0:T(8,128)(2,1)S(1)} %get-tuple-element.27.hidden_ref, bf16[1792,8192]{1,0:T(8,128)(2,1)} %get-tuple-element.28.down_ref), custom_call_target="tpu_custom_call" | custom-call | flops 1000 | bytes 1000 | tf_op jit(solution)/shard_map/cond/branch_1_fun/pallas_call | solution.py:62
  28.9 0.1 collective-permute-start
  29.0 2.2 %collective-permute-done = f32[16,96,128]{2,1,0:T(8,128)S(1)} collective-permute-done((f32[16,96,128]{2,1,0:T(8,128)S(1)}, f32[16,96,128]{2,1,0:T(8,128)S(1)}, u32[]{:S(2)}, u32[]{:S(2)}) %collective-permute-start) | collective-permute-done | bytes 786464 | tf_op jit(solution)/shard_map/cond/branch_1_fun/ppermute | solution.py:25
  31.2 0.1 add.39
  31.3 4.1 %collective-permute-done.2 = f16[1552,128]{1,0:T(8,128)(2,1)S(1)} collective-permute-done((f16[1552,128]{1,0:T(8,128)(2,1)S(1)}, f16[1552,128]{1,0:T(8,128)(2,1)S(1)}, u32[]{:S(2)}, u32[]{:S(2)}) %collective-permute-start.2) | collective-permute-done | bytes 397344 | tf_op jit(solution)/shard_map/ppermute | solution.py:25
  35.4 0.1 slice.65
  35.5 1.0 %all-to-all-done.rows_ref = bf16[80,4,1792]{2,1,0:T(4,128)(2,1)S(1)} async-done(((bf16[80,4,1792]{2,1,0:T(4,128)(2,1)}), bf16[80,4,1792]{2,1,0:T(4,128)(2,1)S(1)}, u32[]{:S(2)}, u32[]{:S(2)}) %all-to-all-start) | async-done | bytes 1146912 | tf_op jit(solution)/shard_map/all_to_all | solution.py:336
  36.5 3.7 %shard_map.65 = (bf16[80,4,128]{2,1,0:T(4,128)(2,1)S(1)}, bf16[80,4,128]{2,1,0:T(4,128)(2,1)S(1)}, bf16[80,4,128]{2,1,0:T(4,128)(2,1)S(1)}, bf16[80,4,128]{2,1,0:T(4,128)(2,1)S(1)}) custom-call(s32[1]{0:T(128)} %bitcast.2.me_ref, bf16[80,4,1792]{2,1,0:T(4,128)(2,1)S(1)} %all-to-all-done.rows_ref, bf16[64,8192]{1,0:T(8,128)(2,1)} %bitcast.48, ...), custom_call_target="tpu_custom_call" | custom-call | tf_op jit(solution)/shard_map/pallas_call | solution.py:274
  40.2 0.8 %collective-permute-start.3 = (bf16[80,4,128]{2,1,0:T(4,128)(2,1)S(1)}, bf16[80,4,128]{2,1,0:T(4,128)(2,1)S(1)}, u32[]{:S(2)}, u32[]{:S(2)}) collective-permute-start(bf16[80,4,128]{2,1,0:T(4,128)(2,1)S(1)} %get-tuple-element.48), channel_id=1, source_target_pairs={{0,1},{1,0},{2,3},{3,2},{4,5},{5,4},{6,7},{7,6},{8,9},{9,8},{10,11... | collective-permute-start | bytes 245768 | tf_op jit(solution)/shard_map/ppermute | solution.py:25
  41.0 1.5 %collective-permute-start.4 = (bf16[80,4,128]{2,1,0:T(4,128)(2,1)S(1)}, bf16[80,4,128]{2,1,0:T(4,128)(2,1)S(1)}, u32[]{:S(2)}, u32[]{:S(2)}) collective-permute-start(bf16[80,4,128]{2,1,0:T(4,128)(2,1)S(1)} %get-tuple-element.49), channel_id=1, source_target_pairs={{0,2},{1,3},{2,0},{3,1},{4,6},{5,7},{6,4},{7,5},{8,10},{9,11},{10,... | collective-permute-start | bytes 245768 | tf_op jit(solution)/shard_map/ppermute | solution.py:25
  42.5 0.0 collective-permute-start.5
  42.5 0.2 fusion.2.pair_ref
  42.7 0.0 collective-permute-done.3.refs_1_
  42.7 2.8 %collective-permute-done.4.refs_2_ = bf16[80,4,128]{2,1,0:T(4,128)(2,1)S(1)} collective-permute-done((bf16[80,4,128]{2,1,0:T(4,128)(2,1)S(1)}, bf16[80,4,128]{2,1,0:T(4,128)(2,1)S(1)}, u32[]{:S(2)}, u32[]{:S(2)}) %collective-permute-start.4) | collective-permute-done | bytes 81952 | tf_op jit(solution)/shard_map/ppermute | solution.py:25
  45.5 1.8 %collective-permute-done.5.refs_3_ = bf16[80,4,128]{2,1,0:T(4,128)(2,1)S(1)} collective-permute-done((bf16[80,4,128]{2,1,0:T(4,128)(2,1)S(1)}, bf16[80,4,128]{2,1,0:T(4,128)(2,1)S(1)}, u32[]{:S(2)}, u32[]{:S(2)}) %collective-permute-start.5) | collective-permute-done | bytes 81952 | tf_op jit(solution)/shard_map/ppermute | solution.py:25
  47.2 0.4 shard_map.66
  47.6 0.2 abs_reduce_fusion.3
  47.8 0.1 multiply_convert_fusion.3
  48.0 2.0 %collective-permute-start.7 = (f16[400,128]{1,0:T(8,128)(2,1)S(1)}, f16[400,128]{1,0:T(8,128)(2,1)S(1)}, u32[]{:S(2)}, u32[]{:S(2)}) collective-permute-start(f16[400,128]{1,0:T(8,128)(2,1)S(1)} %fusion.10), channel_id=1, source_target_pairs={{0,8},{1,9},{2,10},{3,11},{4,12},{5,13},{6,14},{7,15},{8,0},{9,1},... | collective-permute-start | bytes 307208 | tf_op jit(solution)/shard_map/ppermute | solution.py:25
  50.0 0.6 %collective-permute-start.6 = (f16[400,128]{1,0:T(8,128)(2,1)S(1)}, f16[400,128]{1,0:T(8,128)(2,1)S(1)}, u32[]{:S(2)}, u32[]{:S(2)}) collective-permute-start(f16[400,128]{1,0:T(8,128)(2,1)S(1)} %fusion.9), channel_id=1, source_target_pairs={{0,4},{1,5},{2,6},{3,7},{4,0},{5,1},{6,2},{7,3},{8,12},{9,13},{10,... | collective-permute-start | bytes 307208 | tf_op jit(solution)/shard_map/ppermute | solution.py:25
  50.7 1.9 %collective-permute-start.8 = (f16[400,128]{1,0:T(8,128)(2,1)S(1)}, f16[400,128]{1,0:T(8,128)(2,1)S(1)}, u32[]{:S(2)}, u32[]{:S(2)}) collective-permute-start(f16[400,128]{1,0:T(8,128)(2,1)S(1)} %fusion.11), channel_id=1, source_target_pairs={{0,12},{1,13},{2,14},{3,15},{4,8},{5,9},{6,10},{7,11},{8,4},{9,5},... | collective-permute-start | bytes 307208 | tf_op jit(solution)/shard_map/ppermute | solution.py:25
  52.6 4.8 %collective-permute-done.7 = f16[400,128]{1,0:T(8,128)(2,1)S(1)} collective-permute-done((f16[400,128]{1,0:T(8,128)(2,1)S(1)}, f16[400,128]{1,0:T(8,128)(2,1)S(1)}, u32[]{:S(2)}, u32[]{:S(2)}) %collective-permute-start.7) | collective-permute-done | bytes 102432 | tf_op jit(solution)/shard_map/ppermute | solution.py:25
  57.4 0.0 collective-permute-done.6
  57.5 1.9 %collective-permute-done.8 = f16[400,128]{1,0:T(8,128)(2,1)S(1)} collective-permute-done((f16[400,128]{1,0:T(8,128)(2,1)S(1)}, f16[400,128]{1,0:T(8,128)(2,1)S(1)}, u32[]{:S(2)}, u32[]{:S(2)}) %collective-permute-start.8) | collective-permute-done | bytes 102432 | tf_op jit(solution)/shard_map/ppermute | solution.py:25
  59.5 0.8 %copy_bitcast_fusion = bf16[96,512]{1,0:T(8,128)(2,1)} fusion(f16[4,96,128]{2,1,0:T(8,128)(2,1)S(1)} %bitcast.54, f16[4,96,128]{2,1,0:T(8,128)(2,1)S(1)} %bitcast.51, f16[4,96,128]{2,1,0:T(8,128)(2,1)S(1)} %bitcast.52, f32[16,96,128]{2,1,0:T(8,128)S(1)} %shard_map.66, f32[96]{0:T(128)S(1)} %fusion.16, f32[96]{0:T(128)S(1)} %fusion.20, f32[96]{0:T(128)S(1)} %fusion.24), kind=kLoop, calls=%fused_computation.31 | loop fusion | flops 491520 | bytes 591360 | tf_op jit(solution)/shard_map/convert_element_type | solution.py:347
  (13 shorter events, 0.2 us)
Async XLA Ops:
  2.5 34.0 %all-to-all-start = ((bf16[80,4,1792]{2,1,0:T(4,128)(2,1)}), bf16[80,4,1792]{2,1,0:T(4,128)(2,1)S(1)}, u32[]{:S(2)}, u32[]{:S(2)}) async-start(bf16[80,4,1792]{2,1,0:T(4,128)(2,1)} %get-tuple-element.45), calls=%async_computation | async-start | bytes 2293760 | tf_op jit(solution)/shard_map/all_to_all | solution.py:336
  14.2 4.7 %collective-permute-start.1 = (f32[16,96,128]{2,1,0:T(8,128)S(1)}, f32[16,96,128]{2,1,0:T(8,128)S(1)}, u32[]{:S(2)}, u32[]{:S(2)}) collective-permute-start(f32[16,96,128]{2,1,0:T(8,128)S(1)} %branch_1_fun.4), channel_id=1, source_target_pairs={{0,1},{1,0},{2,3},{3,2},{4,5},{5,4},{6,7},{7,6},{8,9},{9,8},{10,11... | collective-permute-start | bytes 2359304 | tf_op jit(solution)/shard_map/cond/branch_1_fun/ppermute | solution.py:25
  19.4 16.1 %collective-permute-start.2 = (f16[1552,128]{1,0:T(8,128)(2,1)S(1)}, f16[1552,128]{1,0:T(8,128)(2,1)S(1)}, u32[]{:S(2)}, u32[]{:S(2)}) collective-permute-start(f16[1552,128]{1,0:T(8,128)(2,1)S(1)} %get-tuple-element.71), channel_id=1, source_target_pairs={{0,2},{1,3},{2,0},{3,1},{4,6},{5,7},{6,4},{7,5},{8,10},{9,11},{10,... | collective-permute-start | bytes 1191944 | tf_op jit(solution)/shard_map/ppermute | solution.py:25
  28.9 2.4 %collective-permute-start = (f32[16,96,128]{2,1,0:T(8,128)S(1)}, f32[16,96,128]{2,1,0:T(8,128)S(1)}, u32[]{:S(2)}, u32[]{:S(2)}) collective-permute-start(f32[16,96,128]{2,1,0:T(8,128)S(1)} %get-tuple-element.30), channel_id=1, source_target_pairs={{0,1},{1,0},{2,3},{3,2},{4,5},{5,4},{6,7},{7,6},{8,9},{9,8},{10,11... | collective-permute-start | bytes 2359304 | tf_op jit(solution)/shard_map/cond/branch_1_fun/ppermute | solution.py:25
  40.2 2.5 %collective-permute-start.3 = (bf16[80,4,128]{2,1,0:T(4,128)(2,1)S(1)}, bf16[80,4,128]{2,1,0:T(4,128)(2,1)S(1)}, u32[]{:S(2)}, u32[]{:S(2)}) collective-permute-start(bf16[80,4,128]{2,1,0:T(4,128)(2,1)S(1)} %get-tuple-element.48), channel_id=1, source_target_pairs={{0,1},{1,0},{2,3},{3,2},{4,5},{5,4},{6,7},{7,6},{8,9},{9,8},{10,11... | collective-permute-start | bytes 245768 | tf_op jit(solution)/shard_map/ppermute | solution.py:25
  41.0 4.4 %collective-permute-start.4 = (bf16[80,4,128]{2,1,0:T(4,128)(2,1)S(1)}, bf16[80,4,128]{2,1,0:T(4,128)(2,1)S(1)}, u32[]{:S(2)}, u32[]{:S(2)}) collective-permute-start(bf16[80,4,128]{2,1,0:T(4,128)(2,1)S(1)} %get-tuple-element.49), channel_id=1, source_target_pairs={{0,2},{1,3},{2,0},{3,1},{4,6},{5,7},{6,4},{7,5},{8,10},{9,11},{10,... | collective-permute-start | bytes 245768 | tf_op jit(solution)/shard_map/ppermute | solution.py:25
  42.5 4.7 %collective-permute-start.5 = (bf16[80,4,128]{2,1,0:T(4,128)(2,1)S(1)}, bf16[80,4,128]{2,1,0:T(4,128)(2,1)S(1)}, u32[]{:S(2)}, u32[]{:S(2)}) collective-permute-start(bf16[80,4,128]{2,1,0:T(4,128)(2,1)S(1)} %get-tuple-element.50), channel_id=1, source_target_pairs={{0,3},{1,2},{2,1},{3,0},{4,7},{5,6},{6,5},{7,4},{8,11},{9,10},{10,... | collective-permute-start | bytes 245768 | tf_op jit(solution)/shard_map/ppermute | solution.py:25
  48.0 9.4 %collective-permute-start.7 = (f16[400,128]{1,0:T(8,128)(2,1)S(1)}, f16[400,128]{1,0:T(8,128)(2,1)S(1)}, u32[]{:S(2)}, u32[]{:S(2)}) collective-permute-start(f16[400,128]{1,0:T(8,128)(2,1)S(1)} %fusion.10), channel_id=1, source_target_pairs={{0,8},{1,9},{2,10},{3,11},{4,12},{5,13},{6,14},{7,15},{8,0},{9,1},... | collective-permute-start | bytes 307208 | tf_op jit(solution)/shard_map/ppermute | solution.py:25
  50.0 7.4 %collective-permute-start.6 = (f16[400,128]{1,0:T(8,128)(2,1)S(1)}, f16[400,128]{1,0:T(8,128)(2,1)S(1)}, u32[]{:S(2)}, u32[]{:S(2)}) collective-permute-start(f16[400,128]{1,0:T(8,128)(2,1)S(1)} %fusion.9), channel_id=1, source_target_pairs={{0,4},{1,5},{2,6},{3,7},{4,0},{5,1},{6,2},{7,3},{8,12},{9,13},{10,... | collective-permute-start | bytes 307208 | tf_op jit(solution)/shard_map/ppermute | solution.py:25
  50.7 8.8 %collective-permute-start.8 = (f16[400,128]{1,0:T(8,128)(2,1)S(1)}, f16[400,128]{1,0:T(8,128)(2,1)S(1)}, u32[]{:S(2)}, u32[]{:S(2)}) collective-permute-start(f16[400,128]{1,0:T(8,128)(2,1)S(1)} %fusion.11), channel_id=1, source_target_pairs={{0,12},{1,13},{2,14},{3,15},{4,8},{5,9},{6,10},{7,11},{8,4},{9,5},... | collective-permute-start | bytes 307208 | tf_op jit(solution)/shard_map/ppermute | solution.py:25

commit v30 on v29

--- a/solution.py
+++ b/solution.py
@@ -341,7 +341,9 @@
     gathered, _ = lax.optimization_barrier((gathered, kept))
     expand = jnp.swapaxes(expand_matrices, 1, 2)[0]
     outs = adapter_output(gathered, shrink, expand, group, me, ranks)
-    arrived = [outs[0]] + [xor_permute(outs[k], group, k) for k in range(1, PLANE)]
+    across = [xor_permute(outs[k], group, k) for k in range(2, PLANE)]
+    beside, _ = lax.optimization_barrier((outs[1], across[0]))
+    arrived = [outs[0], xor_permute(beside, group, 1)] + across
     pair = kept + unpack_scaled(pair_in, rows)
     merged = merge_adapters(pair, pick, arrived)
     return line_sums(merged, group, width).astype(jnp.bfloat16)

time: 60.5 us -> 60.2 us (level)
    ppermute x9, waiting for transfers between devices: 17.6 us -> 13.2 us  [xor_permute(): return lax.ppermute(value, 'tp', [(i, i ^ offset) for i in range(group)])]
    all_to_all x1, waiting for transfers between devices: 0.98 us -> 5.2 us  [shards_by_blocks(): lax.all_to_all(packed, 'tp', split_axis=0, concat_axis=0, axis_index_grou...]
  transfers between devices with their start and end apart: 10 -> 10, of which waited for: 7 -> 6; matrix products, arithmetic and copies ran while one was open for 3% -> 3% of each run, Pallas kernels for 25% -> 31%
where the time goes in v30:
time: 60.2 us; the launch traced here: 60 us
  Pallas kernels  21.3 us (35%)
  waiting for transfers between devices  18.4 us (31%)
  starting transfers between devices  16.6 us (28%)
  other arithmetic  1.93 us (3%)
  local copies, waits for them, and re-layouts  0.9 us (1%)
  between operations  0.8 us (1%)
    pallas_call x3, Pallas kernels, column_blocks(): pl.pallas_call(functools.partial(column_blocks_kernel, groups), out_shape...  14.8 us
    ppermute x9, waiting for transfers between devices, xor_permute(): return lax.ppermute(value, 'tp', [(i, i ^ offset) for i in range(group)])  13.2 us
    ppermute x9, starting transfers between devices, xor_permute(): return lax.ppermute(value, 'tp', [(i, i ^ offset) for i in range(group)])  9.19 us
    all_to_all x1, starting transfers between devices, shards_by_blocks(): lax.all_to_all(packed, 'tp', split_axis=0, concat_axis=0, axis_index_grou...  7.37 us
    all_to_all x1, waiting for transfers between devices, shards_by_blocks(): lax.all_to_all(packed, 'tp', split_axis=0, concat_axis=0, axis_index_grou...  5.2 us
    pallas_call x1, Pallas kernels, adapter_output(): pl.pallas_call(functools.partial(adapter_kernel, parts, ranks), out_shape...  3.66 us
    pallas_call x1, Pallas kernels, pack_rows(): pl.pallas_call(functools.partial(pack_kernel, blocks, orders), out_shape=...  2.49 us
  transfers between devices with their start and end apart: 10, of which 6 were waited for; matrix products, arithmetic and copies ran while one was open for 3% of the time, Pallas kernels for 31%

profile of v30, /device:TPU:0, one launch (start us, length us, event | category | flops | bytes accessed | tf_op | source)
XLA Modules:
  0.0 60.0 jit_solution(6921238437309345851)
XLA Ops:
  0.0 2.5 %shard_map.64 = (bf16[80,4,1792]{2,1,0:T(4,128)(2,1)}, bf16[128,96]{1,0:T(8,128)(2,1)S(1)}, s32[16]{0:T(128)S(1)}, bf16[96,1792]{1,0:T(8,128)(2,1)S(1)}) custom-call(s32[1]{0:T(128)} %bitcast.2.me_ref, s32[16]{0:T(128)} %slot_hbm.1, s32[1,96]{1,0:T(1,128)} %bitcast.56, bf16[96,1792]{1,0:T(8,128)(2,1)} %hidden_hbm.1), custom_call_target="tpu_custom_call" | custom-call | tf_op jit(solution)/shard_map/pallas_call | solution.py:197
  2.5 7.4 %all-to-all-start = ((bf16[80,4,1792]{2,1,0:T(4,128)(2,1)}), bf16[80,4,1792]{2,1,0:T(4,128)(2,1)S(1)}, u32[]{:S(2)}, u32[]{:S(2)}) async-start(bf16[80,4,1792]{2,1,0:T(4,128)(2,1)} %get-tuple-element.46), calls=%async_computation | async-start | bytes 2293760 | tf_op jit(solution)/shard_map/all_to_all | solution.py:336
  9.9 9.4 %conditional.2 = (f16[1552,128]{1,0:T(8,128)(2,1)S(1)}) conditional(s32[]{:T(128)} %bitcast.4, () %tuple.20, (s32[16]{0:T(128)S(1)}, bf16[96,1792]{1,0:T(8,128)(2,1)S(1)}, bf16[1792,8192]{1,0:T(8,128)(2,1)}) %tuple.21), branch_computations={%region_0.0_spmd, %region_1.3_spmd} | conditional | flops 1581488 | bytes 7479232 | solution.py:109
  9.9 0.1 fusion.29
  10.0 4.2 %branch_1_fun.4 = f32[16,96,128]{2,1,0:T(8,128)S(1)} custom-call(s32[4]{0:T(128)S(1)} %get-tuple-element.60.order_ref, bf16[96,1792]{1,0:T(8,128)(2,1)S(1)} %get-tuple-element.24.hidden_ref, bf16[1792,8192]{1,0:T(8,128)(2,1)} %get-tuple-element.25.down_ref), custom_call_target="tpu_custom_call" | custom-call | flops 1000 | bytes 1000 | tf_op jit(solution)/shard_map/cond/branch_1_fun/pallas_call | solution.py:62
  14.2 0.5 collective-permute-start.1
  14.7 4.2 %branch_1_fun.3 = f32[16,96,128]{2,1,0:T(8,128)S(1)} custom-call(s32[4]{0:T(128)S(1)} %get-tuple-element.61.order_ref, bf16[96,1792]{1,0:T(8,128)(2,1)S(1)} %get-tuple-element.24.hidden_ref, bf16[1792,8192]{1,0:T(8,128)(2,1)} %get-tuple-element.25.down_ref), custom_call_target="tpu_custom_call" | custom-call | flops 1000 | bytes 1000 | tf_op jit(solution)/shard_map/cond/branch_1_fun/pallas_call | solution.py:62
  18.9 0.0 collective-permute-done.1
  18.9 0.2 abs_reduce_fusion
  19.1 0.2 multiply_convert_fusion
  19.3 0.1 fusion.1
  19.4 1.7 %collective-permute-start.2 = (f16[1552,128]{1,0:T(8,128)(2,1)S(1)}, f16[1552,128]{1,0:T(8,128)(2,1)S(1)}, u32[]{:S(2)}, u32[]{:S(2)}) collective-permute-start(f16[1552,128]{1,0:T(8,128)(2,1)S(1)} %get-tuple-element.73), channel_id=1, source_target_pairs={{0,2},{1,3},{2,0},{3,1},{4,6},{5,7},{6,4},{7,5},{8,10},{9,11},{10,... | collective-permute-start | bytes 1191944 | tf_op jit(solution)/shard_map/ppermute | solution.py:25
  21.1 0.6 %slice.52 = s32[1]{0:T(128)} slice(s32[16]{0:T(128)S(1)} %get-tuple-element.44), slice={[1:2]} | slice | bytes 8 | tf_op jit(solution)/shard_map/slice | solution.py:120
  22.4 9.0 %conditional.3 = (f32[16,96,128]{2,1,0:T(8,128)S(1)}) conditional(s32[]{:T(128)} %bitcast.5, () %tuple.23, (s32[16]{0:T(128)S(1)}, bf16[96,1792]{1,0:T(8,128)(2,1)S(1)}, bf16[1792,8192]{1,0:T(8,128)(2,1)}) %tuple.24), branch_computations={%region_3.4_spmd, %region_4.5_spmd} | conditional | flops 197608 | bytes 5506136 | solution.py:120
  22.4 0.1 slice.36.order_ref
  22.4 6.4 %branch_1_fun.5 = (f32[16,96,128]{2,1,0:T(8,128)S(1)}, f32[16,96,128]{2,1,0:T(8,128)S(1)}) custom-call(s32[8]{0:T(128)S(1)} %slice.36.order_ref, bf16[96,1792]{1,0:T(8,128)(2,1)S(1)} %get-tuple-element.27.hidden_ref, bf16[1792,8192]{1,0:T(8,128)(2,1)} %get-tuple-element.28.down_ref), custom_call_target="tpu_custom_call" | custom-call | flops 1000 | bytes 1000 | tf_op jit(solution)/shard_map/cond/branch_1_fun/pallas_call | solution.py:62
  28.9 0.1 collective-permute-start
  29.0 2.2 %collective-permute-done = f32[16,96,128]{2,1,0:T(8,128)S(1)} collective-permute-done((f32[16,96,128]{2,1,0:T(8,128)S(1)}, f32[16,96,128]{2,1,0:T(8,128)S(1)}, u32[]{:S(2)}, u32[]{:S(2)}) %collective-permute-start) | collective-permute-done | bytes 786464 | tf_op jit(solution)/shard_map/cond/branch_1_fun/ppermute | solution.py:25
  31.2 0.1 add.39
  31.3 5.2 %all-to-all-done.rows_ref = bf16[80,4,1792]{2,1,0:T(4,128)(2,1)S(1)} async-done(((bf16[80,4,1792]{2,1,0:T(4,128)(2,1)}), bf16[80,4,1792]{2,1,0:T(4,128)(2,1)S(1)}, u32[]{:S(2)}, u32[]{:S(2)}) %all-to-all-start) | async-done | bytes 1146912 | tf_op jit(solution)/shard_map/all_to_all | solution.py:336
  36.5 3.7 %shard_map.65 = (bf16[80,4,128]{2,1,0:T(4,128)(2,1)S(1)}, bf16[80,4,128]{2,1,0:T(4,128)(2,1)S(1)}, bf16[80,4,128]{2,1,0:T(4,128)(2,1)S(1)}, bf16[80,4,128]{2,1,0:T(4,128)(2,1)S(1)}) custom-call(s32[1]{0:T(128)} %bitcast.2.me_ref, bf16[80,4,1792]{2,1,0:T(4,128)(2,1)S(1)} %all-to-all-done.rows_ref, bf16[64,8192]{1,0:T(8,128)(2,1)} %bitcast.48, ...), custom_call_target="tpu_custom_call" | custom-call | tf_op jit(solution)/shard_map/pallas_call | solution.py:274
  40.2 1.5 %collective-permute-start.3 = (bf16[80,4,128]{2,1,0:T(4,128)(2,1)S(1)}, bf16[80,4,128]{2,1,0:T(4,128)(2,1)S(1)}, u32[]{:S(2)}, u32[]{:S(2)}) collective-permute-start(bf16[80,4,128]{2,1,0:T(4,128)(2,1)S(1)} %get-tuple-element.50), channel_id=1, source_target_pairs={{0,2},{1,3},{2,0},{3,1},{4,6},{5,7},{6,4},{7,5},{8,10},{9,11},{10,... | collective-permute-start | bytes 245768 | tf_op jit(solution)/shard_map/ppermute | solution.py:25
  41.7 0.0 collective-permute-done.2
  41.7 0.1 slice.65
  41.8 0.7 %collective-permute-start.5 = (bf16[80,4,128]{2,1,0:T(4,128)(2,1)S(1)}, bf16[80,4,128]{2,1,0:T(4,128)(2,1)S(1)}, u32[]{:S(2)}, u32[]{:S(2)}) collective-permute-start(bf16[80,4,128]{2,1,0:T(4,128)(2,1)S(1)} %get-tuple-element.52), channel_id=1, source_target_pairs={{0,3},{1,2},{2,1},{3,0},{4,7},{5,6},{6,5},{7,4},{8,11},{9,10},{10,... | collective-permute-start | bytes 245768 | tf_op jit(solution)/shard_map/ppermute | solution.py:25
  42.5 3.0 %collective-permute-done.3.refs_2_ = bf16[80,4,128]{2,1,0:T(4,128)(2,1)S(1)} collective-permute-done((bf16[80,4,128]{2,1,0:T(4,128)(2,1)S(1)}, bf16[80,4,128]{2,1,0:T(4,128)(2,1)S(1)}, u32[]{:S(2)}, u32[]{:S(2)}) %collective-permute-start.3) | collective-permute-done | bytes 81952 | tf_op jit(solution)/shard_map/ppermute | solution.py:25
  45.6 0.0 collective-permute-start.4
  45.6 0.2 fusion.2.pair_ref
  45.7 1.2 %collective-permute-done.5.refs_3_ = bf16[80,4,128]{2,1,0:T(4,128)(2,1)S(1)} collective-permute-done((bf16[80,4,128]{2,1,0:T(4,128)(2,1)S(1)}, bf16[80,4,128]{2,1,0:T(4,128)(2,1)S(1)}, u32[]{:S(2)}, u32[]{:S(2)}) %collective-permute-start.5) | collective-permute-done | bytes 81952 | tf_op jit(solution)/shard_map/ppermute | solution.py:25
  46.9 0.0 collective-permute-done.4.refs_1_
  46.9 0.4 shard_map.66
  47.3 0.2 abs_reduce_fusion.3
  47.5 0.1 multiply_convert_fusion.3
  47.7 2.4 %collective-permute-start.7 = (f16[400,128]{1,0:T(8,128)(2,1)S(1)}, f16[400,128]{1,0:T(8,128)(2,1)S(1)}, u32[]{:S(2)}, u32[]{:S(2)}) collective-permute-start(f16[400,128]{1,0:T(8,128)(2,1)S(1)} %fusion.10), channel_id=1, source_target_pairs={{0,8},{1,9},{2,10},{3,11},{4,12},{5,13},{6,14},{7,15},{8,0},{9,1},... | collective-permute-start | bytes 307208 | tf_op jit(solution)/shard_map/ppermute | solution.py:25
  50.1 1.1 %collective-permute-start.6 = (f16[400,128]{1,0:T(8,128)(2,1)S(1)}, f16[400,128]{1,0:T(8,128)(2,1)S(1)}, u32[]{:S(2)}, u32[]{:S(2)}) collective-permute-start(f16[400,128]{1,0:T(8,128)(2,1)S(1)} %fusion.9), channel_id=1, source_target_pairs={{0,4},{1,5},{2,6},{3,7},{4,0},{5,1},{6,2},{7,3},{8,12},{9,13},{10,... | collective-permute-start | bytes 307208 | tf_op jit(solution)/shard_map/ppermute | solution.py:25
  51.2 1.2 %collective-permute-start.8 = (f16[400,128]{1,0:T(8,128)(2,1)S(1)}, f16[400,128]{1,0:T(8,128)(2,1)S(1)}, u32[]{:S(2)}, u32[]{:S(2)}) collective-permute-start(f16[400,128]{1,0:T(8,128)(2,1)S(1)} %fusion.11), channel_id=1, source_target_pairs={{0,12},{1,13},{2,14},{3,15},{4,8},{5,9},{6,10},{7,11},{8,4},{9,5},... | collective-permute-start | bytes 307208 | tf_op jit(solution)/shard_map/ppermute | solution.py:25
  52.3 4.8 %collective-permute-done.7 = f16[400,128]{1,0:T(8,128)(2,1)S(1)} collective-permute-done((f16[400,128]{1,0:T(8,128)(2,1)S(1)}, f16[400,128]{1,0:T(8,128)(2,1)S(1)}, u32[]{:S(2)}, u32[]{:S(2)}) %collective-permute-start.7) | collective-permute-done | bytes 102432 | tf_op jit(solution)/shard_map/ppermute | solution.py:25
  57.1 0.0 collective-permute-done.6
  57.2 2.0 %collective-permute-done.8 = f16[400,128]{1,0:T(8,128)(2,1)S(1)} collective-permute-done((f16[400,128]{1,0:T(8,128)(2,1)S(1)}, f16[400,128]{1,0:T(8,128)(2,1)S(1)}, u32[]{:S(2)}, u32[]{:S(2)}) %collective-permute-start.8) | collective-permute-done | bytes 102432 | tf_op jit(solution)/shard_map/ppermute | solution.py:25
  59.2 0.8 %copy_bitcast_fusion = bf16[96,512]{1,0:T(8,128)(2,1)} fusion(f16[4,96,128]{2,1,0:T(8,128)(2,1)S(1)} %bitcast.54, f16[4,96,128]{2,1,0:T(8,128)(2,1)S(1)} %bitcast.51, f16[4,96,128]{2,1,0:T(8,128)(2,1)S(1)} %bitcast.52, f32[16,96,128]{2,1,0:T(8,128)S(1)} %shard_map.66, f32[96]{0:T(128)S(1)} %fusion.16, f32[96]{0:T(128)S(1)} %fusion.20, f32[96]{0:T(128)S(1)} %fusion.24), kind=kLoop, calls=%fused_computation.31 | loop fusion | flops 491520 | bytes 591360 | tf_op jit(solution)/shard_map/convert_element_type | solution.py:349
  (13 shorter events, 0.2 us)
Async XLA Ops:
  2.5 34.0 %all-to-all-start = ((bf16[80,4,1792]{2,1,0:T(4,128)(2,1)}), bf16[80,4,1792]{2,1,0:T(4,128)(2,1)S(1)}, u32[]{:S(2)}, u32[]{:S(2)}) async-start(bf16[80,4,1792]{2,1,0:T(4,128)(2,1)} %get-tuple-element.46), calls=%async_computation | async-start | bytes 2293760 | tf_op jit(solution)/shard_map/all_to_all | solution.py:336
  14.2 4.7 %collective-permute-start.1 = (f32[16,96,128]{2,1,0:T(8,128)S(1)}, f32[16,96,128]{2,1,0:T(8,128)S(1)}, u32[]{:S(2)}, u32[]{:S(2)}) collective-permute-start(f32[16,96,128]{2,1,0:T(8,128)S(1)} %branch_1_fun.4), channel_id=1, source_target_pairs={{0,1},{1,0},{2,3},{3,2},{4,5},{5,4},{6,7},{7,6},{8,9},{9,8},{10,11... | collective-permute-start | bytes 2359304 | tf_op jit(solution)/shard_map/cond/branch_1_fun/ppermute | solution.py:25
  19.4 22.4 %collective-permute-start.2 = (f16[1552,128]{1,0:T(8,128)(2,1)S(1)}, f16[1552,128]{1,0:T(8,128)(2,1)S(1)}, u32[]{:S(2)}, u32[]{:S(2)}) collective-permute-start(f16[1552,128]{1,0:T(8,128)(2,1)S(1)} %get-tuple-element.73), channel_id=1, source_target_pairs={{0,2},{1,3},{2,0},{3,1},{4,6},{5,7},{6,4},{7,5},{8,10},{9,11},{10,... | collective-permute-start | bytes 1191944 | tf_op jit(solution)/shard_map/ppermute | solution.py:25
  28.9 2.4 %collective-permute-start = (f32[16,96,128]{2,1,0:T(8,128)S(1)}, f32[16,96,128]{2,1,0:T(8,128)S(1)}, u32[]{:S(2)}, u32[]{:S(2)}) collective-permute-start(f32[16,96,128]{2,1,0:T(8,128)S(1)} %get-tuple-element.30), channel_id=1, source_target_pairs={{0,1},{1,0},{2,3},{3,2},{4,5},{5,4},{6,7},{7,6},{8,9},{9,8},{10,11... | collective-permute-start | bytes 2359304 | tf_op jit(solution)/shard_map/cond/branch_1_fun/ppermute | solution.py:25
  40.2 5.4 %collective-permute-start.3 = (bf16[80,4,128]{2,1,0:T(4,128)(2,1)S(1)}, bf16[80,4,128]{2,1,0:T(4,128)(2,1)S(1)}, u32[]{:S(2)}, u32[]{:S(2)}) collective-permute-start(bf16[80,4,128]{2,1,0:T(4,128)(2,1)S(1)} %get-tuple-element.50), channel_id=1, source_target_pairs={{0,2},{1,3},{2,0},{3,1},{4,6},{5,7},{6,4},{7,5},{8,10},{9,11},{10,... | collective-permute-start | bytes 245768 | tf_op jit(solution)/shard_map/ppermute | solution.py:25
  41.8 5.1 %collective-permute-start.5 = (bf16[80,4,128]{2,1,0:T(4,128)(2,1)S(1)}, bf16[80,4,128]{2,1,0:T(4,128)(2,1)S(1)}, u32[]{:S(2)}, u32[]{:S(2)}) collective-permute-start(bf16[80,4,128]{2,1,0:T(4,128)(2,1)S(1)} %get-tuple-element.52), channel_id=1, source_target_pairs={{0,3},{1,2},{2,1},{3,0},{4,7},{5,6},{6,5},{7,4},{8,11},{9,10},{10,... | collective-permute-start | bytes 245768 | tf_op jit(solution)/shard_map/ppermute | solution.py:25
  45.6 1.4 %collective-permute-start.4 = (bf16[80,4,128]{2,1,0:T(4,128)(2,1)S(1)}, bf16[80,4,128]{2,1,0:T(4,128)(2,1)S(1)}, u32[]{:S(2)}, u32[]{:S(2)}) collective-permute-start(bf16[80,4,128]{2,1,0:T(4,128)(2,1)S(1)} %get-tuple-element.51), channel_id=1, source_target_pairs={{0,1},{1,0},{2,3},{3,2},{4,5},{5,4},{6,7},{7,6},{8,9},{9,8},{10,11... | collective-permute-start | bytes 245768 | tf_op jit(solution)/shard_map/ppermute | solution.py:25
  47.7 9.4 %collective-permute-start.7 = (f16[400,128]{1,0:T(8,128)(2,1)S(1)}, f16[400,128]{1,0:T(8,128)(2,1)S(1)}, u32[]{:S(2)}, u32[]{:S(2)}) collective-permute-start(f16[400,128]{1,0:T(8,128)(2,1)S(1)} %fusion.10), channel_id=1, source_target_pairs={{0,8},{1,9},{2,10},{3,11},{4,12},{5,13},{6,14},{7,15},{8,0},{9,1},... | collective-permute-start | bytes 307208 | tf_op jit(solution)/shard_map/ppermute | solution.py:25
  50.1 7.0 %collective-permute-start.6 = (f16[400,128]{1,0:T(8,128)(2,1)S(1)}, f16[400,128]{1,0:T(8,128)(2,1)S(1)}, u32[]{:S(2)}, u32[]{:S(2)}) collective-permute-start(f16[400,128]{1,0:T(8,128)(2,1)S(1)} %fusion.9), channel_id=1, source_target_pairs={{0,4},{1,5},{2,6},{3,7},{4,0},{5,1},{6,2},{7,3},{8,12},{9,13},{10,... | collective-permute-start | bytes 307208 | tf_op jit(solution)/shard_map/ppermute | solution.py:25
  51.2 8.0 %collective-permute-start.8 = (f16[400,128]{1,0:T(8,128)(2,1)S(1)}, f16[400,128]{1,0:T(8,128)(2,1)S(1)}, u32[]{:S(2)}, u32[]{:S(2)}) collective-permute-start(f16[400,128]{1,0:T(8,128)(2,1)S(1)} %fusion.11), channel_id=1, source_target_pairs={{0,12},{1,13},{2,14},{3,15},{4,8},{5,9},{6,10},{7,11},{8,4},{9,5},... | collective-permute-start | bytes 307208 | tf_op jit(solution)/shard_map/ppermute | solution.py:25

commit v31 on v30

--- a/solution.py
+++ b/solution.py
@@ -144,7 +144,6 @@
     packed_ref,
     pick_ref,
     order_ref,
-    kept_ref,
     slot_ref,
     adapter_ref,
     hidden_ref,
@@ -184,7 +183,6 @@
     copies[2].wait()
     packed = jnp.dot(pick, hidden_ref[...], preferred_element_type=jnp.float32)
     packed_ref[...] = packed.astype(jnp.bfloat16).reshape(packed_ref.shape)
-    kept_ref[...] = hidden_ref[...]
 
 
 def pack_rows(hidden, adapter_of_row, adapter_holder_slot, me, orders):
@@ -200,10 +198,9 @@
             jax.ShapeDtypeStruct((group * blocks, BLOCK, depth), jnp.bfloat16),
             jax.ShapeDtypeStruct((PLANE * HELD, rows), jnp.bfloat16),
             jax.ShapeDtypeStruct((len(orders),), jnp.int32),
-            jax.ShapeDtypeStruct((rows, depth), jnp.bfloat16),
         ),
         in_specs=[smem, anywhere, anywhere, anywhere],
-        out_specs=(vmem, vmem, smem, vmem),
+        out_specs=(vmem, vmem, smem),
         scratch_shapes=[
             pltpu.SMEM((group,), jnp.int32),
             pltpu.VMEM((1, rows), jnp.int32),
@@ -330,14 +327,14 @@
     orders = [q + k for k in (3, 2, 1, 0) for q in quads]
     half = group // 2
     ranks = [i % half // 2 * PLANE + i // half * 2 + i % 2 for i in range(group)]
-    packed, pick, order, kept_hidden = pack_rows(
+    packed, pick, order = pack_rows(
         hidden, adapter_of_row, adapter_holder_slot, me, orders
     )
     gathered = lax.all_to_all(
         packed, "tp", split_axis=0, concat_axis=0, axis_index_groups=[ranks], tiled=True
     )
     shrink = jnp.swapaxes(shrink_matrices, 1, 2)[0]
-    kept, pair_in = pair_sums(kept_hidden, down_matrix, group, order, width)
+    kept, pair_in = pair_sums(hidden, down_matrix, group, order, width)
     gathered, _ = lax.optimization_barrier((gathered, kept))
     expand = jnp.swapaxes(expand_matrices, 1, 2)[0]
     outs = adapter_output(gathered, shrink, expand, group, me, ranks)

time: 60.2 us -> 60.3 us (level)
  Pallas kernels: 21.3 us -> 22.3 us
  waiting for transfers between devices: 18.4 us -> 17.4 us
    all_to_all x1, waiting for transfers between devices: 5.2 us -> 4.21 us  [shards_by_blocks(): lax.all_to_all(packed, 'tp', split_axis=0, concat_axis=0, axis_index_grou...]
    pallas_call x3, Pallas kernels: 14.8 us -> 15.8 us  [column_blocks(): pl.pallas_call(functools.partial(column_blocks_kernel, groups), out_shape...]
  transfers between devices with their start and end apart: 10 -> 10, of which waited for: 6 -> 6; matrix products, arithmetic and copies ran while one was open for 3% -> 3% of each run, Pallas kernels for 31% -> 32%
where the time goes in v31:
time: 60.3 us; the launch traced here: 60 us
  Pallas kernels  22.3 us (37%)
  waiting for transfers between devices  17.4 us (29%)
  starting transfers between devices  16.6 us (28%)
  other arithmetic  1.91 us (3%)
  local copies, waits for them, and re-layouts  0.95 us (2%)
  between operations  0.8 us (1%)
    pallas_call x3, Pallas kernels, column_blocks(): pl.pallas_call(functools.partial(column_blocks_kernel, groups), out_shape...  15.8 us
    ppermute x9, waiting for transfers between devices, xor_permute(): return lax.ppermute(value, 'tp', [(i, i ^ offset) for i in range(group)])  13.2 us
    ppermute x9, starting transfers between devices, xor_permute(): return lax.ppermute(value, 'tp', [(i, i ^ offset) for i in range(group)])  9.21 us
    all_to_all x1, starting transfers between devices, shards_by_blocks(): lax.all_to_all(packed, 'tp', split_axis=0, concat_axis=0, axis_index_grou...  7.37 us
    all_to_all x1, waiting for transfers between devices, shards_by_blocks(): lax.all_to_all(packed, 'tp', split_axis=0, concat_axis=0, axis_index_grou...  4.21 us
    pallas_call x1, Pallas kernels, adapter_output(): pl.pallas_call(functools.partial(adapter_kernel, parts, ranks), out_shape...  3.66 us
    pallas_call x1, Pallas kernels, pack_rows(): pl.pallas_call(functools.partial(pack_kernel, blocks, orders), out_shape=...  2.49 us
  transfers between devices with their start and end apart: 10, of which 6 were waited for; matrix products, arithmetic and copies ran while one was open for 3% of the time, Pallas kernels for 32%

profile of v31, /device:TPU:0, one launch (start us, length us, event | category | flops | bytes accessed | tf_op | source)
XLA Modules:
  0.0 60.0 jit_solution(2766012342325896684)
XLA Ops:
  0.0 2.5 %shard_map.64 = (bf16[80,4,1792]{2,1,0:T(4,128)(2,1)}, bf16[128,96]{1,0:T(8,128)(2,1)S(1)}, s32[16]{0:T(128)S(1)}) custom-call(s32[1]{0:T(128)} %bitcast.2.me_ref, s32[16]{0:T(128)} %slot_hbm.1, s32[1,96]{1,0:T(1,128)} %bitcast.56, bf16[96,1792]{1,0:T(8,128)(2,1)} %hidden_hbm.1), custom_call_target="tpu_custom_call" | custom-call | tf_op jit(solution)/shard_map/pallas_call | solution.py:195
  2.5 7.4 %all-to-all-start = ((bf16[80,4,1792]{2,1,0:T(4,128)(2,1)}), bf16[80,4,1792]{2,1,0:T(4,128)(2,1)S(1)}, u32[]{:S(2)}, u32[]{:S(2)}) async-start(bf16[80,4,1792]{2,1,0:T(4,128)(2,1)} %get-tuple-element.44), calls=%async_computation | async-start | bytes 2293760 | tf_op jit(solution)/shard_map/all_to_all | solution.py:333
  9.9 9.9 %conditional.2 = (f16[1552,128]{1,0:T(8,128)(2,1)S(1)}) conditional(s32[]{:T(128)} %bitcast.4, () %tuple.20, (s32[16]{0:T(128)S(1)}, bf16[96,1792]{1,0:T(8,128)(2,1)}, bf16[1792,8192]{1,0:T(8,128)(2,1)}) %tuple.21), branch_computations={%region_0.0_spmd, %region_1.3_spmd} | conditional | flops 1581488 | bytes 8855516 | solution.py:109
  9.9 0.1 fusion.29
  10.0 0.0 copy-start
  10.0 4.7 %branch_1_fun.4 = f32[16,96,128]{2,1,0:T(8,128)S(1)} custom-call(s32[4]{0:T(128)S(1)} %get-tuple-element.58.order_ref, bf16[96,1792]{1,0:T(8,128)(2,1)} %get-tuple-element.24.hidden_ref, bf16[1792,8192]{1,0:T(8,128)(2,1)} %get-tuple-element.25.down_ref), custom_call_target="tpu_custom_call" | custom-call | flops 1000 | bytes 1000 | tf_op jit(solution)/shard_map/cond/branch_1_fun/pallas_call | solution.py:62
  14.7 0.5 collective-permute-start.1
  15.2 0.0 copy-done
  15.2 4.2 %branch_1_fun.3 = f32[16,96,128]{2,1,0:T(8,128)S(1)} custom-call(s32[4]{0:T(128)S(1)} %get-tuple-element.59.order_ref, bf16[96,1792]{1,0:T(8,128)(2,1)S(1)} %copy-done, bf16[1792,8192]{1,0:T(8,128)(2,1)} %get-tuple-element.25.down_ref), custom_call_target="tpu_custom_call" | custom-call | flops 1000 | bytes 1000 | tf_op jit(solution)/shard_map/cond/branch_1_fun/pallas_call | solution.py:62
  19.4 0.0 collective-permute-done.1
  19.4 0.2 abs_reduce_fusion
  19.6 0.2 multiply_convert_fusion
  19.8 0.1 fusion.1
  19.9 1.7 %collective-permute-start.2 = (f16[1552,128]{1,0:T(8,128)(2,1)S(1)}, f16[1552,128]{1,0:T(8,128)(2,1)S(1)}, u32[]{:S(2)}, u32[]{:S(2)}) collective-permute-start(f16[1552,128]{1,0:T(8,128)(2,1)S(1)} %get-tuple-element.71), channel_id=1, source_target_pairs={{0,2},{1,3},{2,0},{3,1},{4,6},{5,7},{6,4},{7,5},{8,10},{9,11},{10,... | collective-permute-start | bytes 1191944 | tf_op jit(solution)/shard_map/ppermute | solution.py:25
  21.6 0.6 %slice.52 = s32[1]{0:T(128)} slice(s32[16]{0:T(128)S(1)} %get-tuple-element.42), slice={[1:2]} | slice | bytes 8 | tf_op jit(solution)/shard_map/slice | solution.py:120
  22.9 9.4 %conditional.3 = (f32[16,96,128]{2,1,0:T(8,128)S(1)}) conditional(s32[]{:T(128)} %bitcast.5, () %tuple.23, (s32[16]{0:T(128)S(1)}, bf16[96,1792]{1,0:T(8,128)(2,1)}, bf16[1792,8192]{1,0:T(8,128)(2,1)}) %tuple.24), branch_computations={%region_3.4_spmd, %region_4.5_spmd} | conditional | flops 197608 | bytes 5506136 | solution.py:120
  22.9 0.1 slice.36.order_ref
  23.0 6.9 %branch_1_fun.5 = (f32[16,96,128]{2,1,0:T(8,128)S(1)}, f32[16,96,128]{2,1,0:T(8,128)S(1)}) custom-call(s32[8]{0:T(128)S(1)} %slice.36.order_ref, bf16[96,1792]{1,0:T(8,128)(2,1)} %get-tuple-element.27.hidden_ref, bf16[1792,8192]{1,0:T(8,128)(2,1)} %get-tuple-element.28.down_ref), custom_call_target="tpu_custom_call" | custom-call | flops 1000 | bytes 1000 | tf_op jit(solution)/shard_map/cond/branch_1_fun/pallas_call | solution.py:62
  29.9 0.1 collective-permute-start
  30.0 2.2 %collective-permute-done = f32[16,96,128]{2,1,0:T(8,128)S(1)} collective-permute-done((f32[16,96,128]{2,1,0:T(8,128)S(1)}, f32[16,96,128]{2,1,0:T(8,128)S(1)}, u32[]{:S(2)}, u32[]{:S(2)}) %collective-permute-start) | collective-permute-done | bytes 786464 | tf_op jit(solution)/shard_map/cond/branch_1_fun/ppermute | solution.py:25
  32.2 0.1 add.39
  32.3 4.2 %all-to-all-done.rows_ref = bf16[80,4,1792]{2,1,0:T(4,128)(2,1)S(1)} async-done(((bf16[80,4,1792]{2,1,0:T(4,128)(2,1)}), bf16[80,4,1792]{2,1,0:T(4,128)(2,1)S(1)}, u32[]{:S(2)}, u32[]{:S(2)}) %all-to-all-start) | async-done | bytes 1146912 | tf_op jit(solution)/shard_map/all_to_all | solution.py:333
  36.5 3.7 %shard_map.65 = (bf16[80,4,128]{2,1,0:T(4,128)(2,1)S(1)}, bf16[80,4,128]{2,1,0:T(4,128)(2,1)S(1)}, bf16[80,4,128]{2,1,0:T(4,128)(2,1)S(1)}, bf16[80,4,128]{2,1,0:T(4,128)(2,1)S(1)}) custom-call(s32[1]{0:T(128)} %bitcast.2.me_ref, bf16[80,4,1792]{2,1,0:T(4,128)(2,1)S(1)} %all-to-all-done.rows_ref, bf16[64,8192]{1,0:T(8,128)(2,1)} %bitcast.48, ...), custom_call_target="tpu_custom_call" | custom-call | tf_op jit(solution)/shard_map/pallas_call | solution.py:271
  40.2 1.5 %collective-permute-start.3 = (bf16[80,4,128]{2,1,0:T(4,128)(2,1)S(1)}, bf16[80,4,128]{2,1,0:T(4,128)(2,1)S(1)}, u32[]{:S(2)}, u32[]{:S(2)}) collective-permute-start(bf16[80,4,128]{2,1,0:T(4,128)(2,1)S(1)} %get-tuple-element.48), channel_id=1, source_target_pairs={{0,2},{1,3},{2,0},{3,1},{4,6},{5,7},{6,4},{7,5},{8,10},{9,11},{10,... | collective-permute-start | bytes 245768 | tf_op jit(solution)/shard_map/ppermute | solution.py:25
  41.7 0.0 collective-permute-done.2
  41.7 0.1 slice.65
  41.8 0.7 %collective-permute-start.5 = (bf16[80,4,128]{2,1,0:T(4,128)(2,1)S(1)}, bf16[80,4,128]{2,1,0:T(4,128)(2,1)S(1)}, u32[]{:S(2)}, u32[]{:S(2)}) collective-permute-start(bf16[80,4,128]{2,1,0:T(4,128)(2,1)S(1)} %get-tuple-element.50), channel_id=1, source_target_pairs={{0,3},{1,2},{2,1},{3,0},{4,7},{5,6},{6,5},{7,4},{8,11},{9,10},{10,... | collective-permute-start | bytes 245768 | tf_op jit(solution)/shard_map/ppermute | solution.py:25
  42.5 3.0 %collective-permute-done.3.refs_2_ = bf16[80,4,128]{2,1,0:T(4,128)(2,1)S(1)} collective-permute-done((bf16[80,4,128]{2,1,0:T(4,128)(2,1)S(1)}, bf16[80,4,128]{2,1,0:T(4,128)(2,1)S(1)}, u32[]{:S(2)}, u32[]{:S(2)}) %collective-permute-start.3) | collective-permute-done | bytes 81952 | tf_op jit(solution)/shard_map/ppermute | solution.py:25
  45.6 0.0 collective-permute-start.4
  45.6 0.2 fusion.2.pair_ref
  45.7 1.2 %collective-permute-done.5.refs_3_ = bf16[80,4,128]{2,1,0:T(4,128)(2,1)S(1)} collective-permute-done((bf16[80,4,128]{2,1,0:T(4,128)(2,1)S(1)}, bf16[80,4,128]{2,1,0:T(4,128)(2,1)S(1)}, u32[]{:S(2)}, u32[]{:S(2)}) %collective-permute-start.5) | collective-permute-done | bytes 81952 | tf_op jit(solution)/shard_map/ppermute | solution.py:25
  46.9 0.0 collective-permute-done.4.refs_1_
  46.9 0.4 shard_map.66
  47.3 0.2 abs_reduce_fusion.3
  47.5 0.1 multiply_convert_fusion.3
  47.7 2.4 %collective-permute-start.7 = (f16[400,128]{1,0:T(8,128)(2,1)S(1)}, f16[400,128]{1,0:T(8,128)(2,1)S(1)}, u32[]{:S(2)}, u32[]{:S(2)}) collective-permute-start(f16[400,128]{1,0:T(8,128)(2,1)S(1)} %fusion.10), channel_id=1, source_target_pairs={{0,8},{1,9},{2,10},{3,11},{4,12},{5,13},{6,14},{7,15},{8,0},{9,1},... | collective-permute-start | bytes 307208 | tf_op jit(solution)/shard_map/ppermute | solution.py:25
  50.1 1.0 %collective-permute-start.6 = (f16[400,128]{1,0:T(8,128)(2,1)S(1)}, f16[400,128]{1,0:T(8,128)(2,1)S(1)}, u32[]{:S(2)}, u32[]{:S(2)}) collective-permute-start(f16[400,128]{1,0:T(8,128)(2,1)S(1)} %fusion.9), channel_id=1, source_target_pairs={{0,4},{1,5},{2,6},{3,7},{4,0},{5,1},{6,2},{7,3},{8,12},{9,13},{10,... | collective-permute-start | bytes 307208 | tf_op jit(solution)/shard_map/ppermute | solution.py:25
  51.2 1.2 %collective-permute-start.8 = (f16[400,128]{1,0:T(8,128)(2,1)S(1)}, f16[400,128]{1,0:T(8,128)(2,1)S(1)}, u32[]{:S(2)}, u32[]{:S(2)}) collective-permute-start(f16[400,128]{1,0:T(8,128)(2,1)S(1)} %fusion.11), channel_id=1, source_target_pairs={{0,12},{1,13},{2,14},{3,15},{4,8},{5,9},{6,10},{7,11},{8,4},{9,5},... | collective-permute-start | bytes 307208 | tf_op jit(solution)/shard_map/ppermute | solution.py:25
  52.3 4.8 %collective-permute-done.7 = f16[400,128]{1,0:T(8,128)(2,1)S(1)} collective-permute-done((f16[400,128]{1,0:T(8,128)(2,1)S(1)}, f16[400,128]{1,0:T(8,128)(2,1)S(1)}, u32[]{:S(2)}, u32[]{:S(2)}) %collective-permute-start.7) | collective-permute-done | bytes 102432 | tf_op jit(solution)/shard_map/ppermute | solution.py:25
  57.1 0.0 collective-permute-done.6
  57.2 2.0 %collective-permute-done.8 = f16[400,128]{1,0:T(8,128)(2,1)S(1)} collective-permute-done((f16[400,128]{1,0:T(8,128)(2,1)S(1)}, f16[400,128]{1,0:T(8,128)(2,1)S(1)}, u32[]{:S(2)}, u32[]{:S(2)}) %collective-permute-start.8) | collective-permute-done | bytes 102432 | tf_op jit(solution)/shard_map/ppermute | solution.py:25
  59.2 0.8 %copy_bitcast_fusion = bf16[96,512]{1,0:T(8,128)(2,1)} fusion(f16[4,96,128]{2,1,0:T(8,128)(2,1)S(1)} %bitcast.54, f16[4,96,128]{2,1,0:T(8,128)(2,1)S(1)} %bitcast.51, f16[4,96,128]{2,1,0:T(8,128)(2,1)S(1)} %bitcast.52, f32[16,96,128]{2,1,0:T(8,128)S(1)} %shard_map.66, f32[96]{0:T(128)S(1)} %fusion.16, f32[96]{0:T(128)S(1)} %fusion.20, f32[96]{0:T(128)S(1)} %fusion.24), kind=kLoop, calls=%fused_computation.31 | loop fusion | flops 491520 | bytes 591360 | tf_op jit(solution)/shard_map/convert_element_type | solution.py:346
  (13 shorter events, 0.2 us)
Async XLA Ops:
  2.5 34.0 %all-to-all-start = ((bf16[80,4,1792]{2,1,0:T(4,128)(2,1)}), bf16[80,4,1792]{2,1,0:T(4,128)(2,1)S(1)}, u32[]{:S(2)}, u32[]{:S(2)}) async-start(bf16[80,4,1792]{2,1,0:T(4,128)(2,1)} %get-tuple-element.44), calls=%async_computation | async-start | bytes 2293760 | tf_op jit(solution)/shard_map/all_to_all | solution.py:333
  10.0 5.2 %copy-start = (bf16[96,1792]{1,0:T(8,128)(2,1)S(1)}, bf16[96,1792]{1,0:T(8,128)(2,1)}, u32[]{:S(2)}) copy-start(bf16[96,1792]{1,0:T(8,128)(2,1)} %get-tuple-element.24.hidden_ref) | copy-start | bytes 1032196 | tf_op jit(solution)/shard_map/cond
  14.7 4.7 %collective-permute-start.1 = (f32[16,96,128]{2,1,0:T(8,128)S(1)}, f32[16,96,128]{2,1,0:T(8,128)S(1)}, u32[]{:S(2)}, u32[]{:S(2)}) collective-permute-start(f32[16,96,128]{2,1,0:T(8,128)S(1)} %branch_1_fun.4), channel_id=1, source_target_pairs={{0,1},{1,0},{2,3},{3,2},{4,5},{5,4},{6,7},{7,6},{8,9},{9,8},{10,11... | collective-permute-start | bytes 2359304 | tf_op jit(solution)/shard_map/cond/branch_1_fun/ppermute | solution.py:25
  19.9 21.9 %collective-permute-start.2 = (f16[1552,128]{1,0:T(8,128)(2,1)S(1)}, f16[1552,128]{1,0:T(8,128)(2,1)S(1)}, u32[]{:S(2)}, u32[]{:S(2)}) collective-permute-start(f16[1552,128]{1,0:T(8,128)(2,1)S(1)} %get-tuple-element.71), channel_id=1, source_target_pairs={{0,2},{1,3},{2,0},{3,1},{4,6},{5,7},{6,4},{7,5},{8,10},{9,11},{10,... | collective-permute-start | bytes 1191944 | tf_op jit(solution)/shard_map/ppermute | solution.py:25
  29.9 2.4 %collective-permute-start = (f32[16,96,128]{2,1,0:T(8,128)S(1)}, f32[16,96,128]{2,1,0:T(8,128)S(1)}, u32[]{:S(2)}, u32[]{:S(2)}) collective-permute-start(f32[16,96,128]{2,1,0:T(8,128)S(1)} %get-tuple-element.30), channel_id=1, source_target_pairs={{0,1},{1,0},{2,3},{3,2},{4,5},{5,4},{6,7},{7,6},{8,9},{9,8},{10,11... | collective-permute-start | bytes 2359304 | tf_op jit(solution)/shard_map/cond/branch_1_fun/ppermute | solution.py:25
  40.2 5.4 %collective-permute-start.3 = (bf16[80,4,128]{2,1,0:T(4,128)(2,1)S(1)}, bf16[80,4,128]{2,1,0:T(4,128)(2,1)S(1)}, u32[]{:S(2)}, u32[]{:S(2)}) collective-permute-start(bf16[80,4,128]{2,1,0:T(4,128)(2,1)S(1)} %get-tuple-element.48), channel_id=1, source_target_pairs={{0,2},{1,3},{2,0},{3,1},{4,6},{5,7},{6,4},{7,5},{8,10},{9,11},{10,... | collective-permute-start | bytes 245768 | tf_op jit(solution)/shard_map/ppermute | solution.py:25
  41.8 5.1 %collective-permute-start.5 = (bf16[80,4,128]{2,1,0:T(4,128)(2,1)S(1)}, bf16[80,4,128]{2,1,0:T(4,128)(2,1)S(1)}, u32[]{:S(2)}, u32[]{:S(2)}) collective-permute-start(bf16[80,4,128]{2,1,0:T(4,128)(2,1)S(1)} %get-tuple-element.50), channel_id=1, source_target_pairs={{0,3},{1,2},{2,1},{3,0},{4,7},{5,6},{6,5},{7,4},{8,11},{9,10},{10,... | collective-permute-start | bytes 245768 | tf_op jit(solution)/shard_map/ppermute | solution.py:25
  45.6 1.4 %collective-permute-start.4 = (bf16[80,4,128]{2,1,0:T(4,128)(2,1)S(1)}, bf16[80,4,128]{2,1,0:T(4,128)(2,1)S(1)}, u32[]{:S(2)}, u32[]{:S(2)}) collective-permute-start(bf16[80,4,128]{2,1,0:T(4,128)(2,1)S(1)} %get-tuple-element.49), channel_id=1, source_target_pairs={{0,1},{1,0},{2,3},{3,2},{4,5},{5,4},{6,7},{7,6},{8,9},{9,8},{10,11... | collective-permute-start | bytes 245768 | tf_op jit(solution)/shard_map/ppermute | solution.py:25
  47.7 9.4 %collective-permute-start.7 = (f16[400,128]{1,0:T(8,128)(2,1)S(1)}, f16[400,128]{1,0:T(8,128)(2,1)S(1)}, u32[]{:S(2)}, u32[]{:S(2)}) collective-permute-start(f16[400,128]{1,0:T(8,128)(2,1)S(1)} %fusion.10), channel_id=1, source_target_pairs={{0,8},{1,9},{2,10},{3,11},{4,12},{5,13},{6,14},{7,15},{8,0},{9,1},... | collective-permute-start | bytes 307208 | tf_op jit(solution)/shard_map/ppermute | solution.py:25
  50.1 7.0 %collective-permute-start.6 = (f16[400,128]{1,0:T(8,128)(2,1)S(1)}, f16[400,128]{1,0:T(8,128)(2,1)S(1)}, u32[]{:S(2)}, u32[]{:S(2)}) collective-permute-start(f16[400,128]{1,0:T(8,128)(2,1)S(1)} %fusion.9), channel_id=1, source_target_pairs={{0,4},{1,5},{2,6},{3,7},{4,0},{5,1},{6,2},{7,3},{8,12},{9,13},{10,... | collective-permute-start | bytes 307208 | tf_op jit(solution)/shard_map/ppermute | solution.py:25
  51.2 8.0 %collective-permute-start.8 = (f16[400,128]{1,0:T(8,128)(2,1)S(1)}, f16[400,128]{1,0:T(8,128)(2,1)S(1)}, u32[]{:S(2)}, u32[]{:S(2)}) collective-permute-start(f16[400,128]{1,0:T(8,128)(2,1)S(1)} %fusion.11), channel_id=1, source_target_pairs={{0,12},{1,13},{2,14},{3,15},{4,8},{5,9},{6,10},{7,11},{8,4},{9,5},... | collective-permute-start | bytes 307208 | tf_op jit(solution)/shard_map/ppermute | solution.py:25
